TPU v7x, 32 devices: a whole 2x2x4 slice. The times are simulated.
32 devices in a mesh: groups: 2 (over x), ctx: 16 (over z, y, core).
Axes of the slice: x: 2, y: 2, z: 4, core: 2. Of those that a mesh axis runs over, the one named last changes fastest.
Arguments:
- q_heads: bfloat16 [4096, 12288], P(('groups', 'ctx')), parts along dimension 0, may hold values from -12 to 12
- kv_latent: bfloat16 [4096, 576], P(('groups', 'ctx')), parts along dimension 0, may hold values from -12 to 12
- latent_gain: float32 [512], replicated, may hold values from 0.1 to 1.9
- w_up: bfloat16 [512, 16384], P('ctx'), may hold values from -0.25 to 0.25
- page_ranks: int32 [4096, 1], P(('groups', 'ctx')), parts along dimension 0, may hold values from 0 to 15; in each aligned block of 128 rows (0 to 127, 128 to 255, ...) at most 16 rows name the same one
- lengths: int32 [16], P('groups'), parts along dimension 0, may hold values from 1 to 1024, 2048 in all
Outputs:
- attn_out: bfloat16 [4096, 8192], P(('groups', 'ctx')), parts along dimension 0
- decode_cache: bfloat16 [8192, 576], P(('groups', 'ctx')), parts along dimension 0
There are 2 independent parts, one for each index of `groups`. A program takes and returns all parts, laid end to end along the dimension named above; an argument that names none is the same for every part. Nothing has to cross between parts.
Inputs may be any that keep to these rules, and one draw needn't show every extreme that they name: `page_ranks`: the 128 positions of one device name one decode rank at most 16 times. The 8 lengths add up to 2048; the longest is 1024.
All inputs are finite; a program needn't handle non-finite values.
Results may differ from a plain program's by a relative error of at most 0.012.
The roundings to bfloat16 on the way count: a program that leaves them out, or rounds other values in their place, can miss the bound.
Values may be sent and summed in bfloat16 or wider, within the bound.
No kernel may reach another device: no remote copies, remote signals or barrier semaphores. Data moves between devices by JAX's collectives and lax.ppermute only.
A program may use at most 128 MiB of HBM per device.

v0:
```python
import math

import jax
import jax.numpy as jnp
from jax import lax
from jax.sharding import PartitionSpec as P

H = 64
NOPE = 128
ROPE = 64
VDIM = 128
LAT = 512
REACH = 3


def from_behind(array, axis, by):
    length = lax.axis_size(axis)
    pairs = [(i, i + by) for i in range(length) if 0 <= i + by < length]
    return lax.ppermute(array, axis, pairs)


def locate(positions, starts):
    inside = positions[:, None] >= starts[None, :]
    request = jnp.sum(inside.astype(jnp.int32), axis=1)
    own_start = jnp.max(jnp.where(inside, starts[None, :], 0), axis=1)
    return (request, positions - own_start)


def rope_tables(offset, width):
    half_width = width // 2
    frequency = jnp.exp(
        -jnp.arange(half_width, dtype=jnp.float32) * (2.0 * math.log(10000.0) / width)
    )
    angles = offset.astype(jnp.float32)[:, None] * frequency[None, :]
    return (jnp.cos(angles), jnp.sin(angles))


def rotate(values, cosine, sine_table):
    half_width = values.shape[-1] // 2
    view_shape = (cosine.shape[0],) + (1,) * (values.ndim - 2) + (half_width,)
    cosine = cosine.reshape(view_shape)
    sine_table = sine_table.reshape(view_shape)
    front_half = values[..., :half_width]
    back_half = values[..., half_width:]
    return jnp.concatenate(
        [
            front_half * cosine - back_half * sine_table,
            back_half * cosine + front_half * sine_table,
        ],
        axis=-1,
    )


def cache_rows_of(kv_latent, latent_gain, cosine, sine_table):
    raw_values = kv_latent.astype(jnp.float32)
    latent_part = raw_values[:, :LAT]
    inverse_rms = lax.rsqrt(jnp.mean(latent_part * latent_part, axis=1, keepdims=True) + 1e-06)
    latent = latent_part * inverse_rms * latent_gain[None, :]
    key_rope = rotate(raw_values[:, LAT:], cosine, sine_table)
    return jnp.concatenate([latent, key_rope], axis=1).astype(jnp.bfloat16)


def attend(query_nope, query_rope, key_nope, key_rope, value_heads, allowed):
    softmax_scale = (query_nope.shape[-1] + query_rope.shape[-1]) ** (-0.5)
    scores = jnp.einsum("thd,uhd->htu", query_nope, key_nope, preferred_element_type=jnp.float32)
    scores = scores + jnp.einsum(
        "thr,ur->htu", query_rope, key_rope, preferred_element_type=jnp.float32
    )
    scores = jnp.where(allowed[None], scores * softmax_scale, -1e30)
    row_max = jnp.max(scores, axis=2, keepdims=True)
    exponent = jnp.where(allowed[None], jnp.exp(scores - row_max), 0.0)
    totals = jnp.sum(exponent, axis=2)
    weights = exponent.astype(jnp.bfloat16)
    mixed_values = jnp.einsum(
        "htu,uhv->thv", weights, value_heads, preferred_element_type=jnp.float32
    )
    return (mixed_values / jnp.transpose(totals)[:, :, None]).astype(jnp.bfloat16)


def body(q_heads, kv_latent, latent_gain, w_up, page_ranks, lengths):
    tok_count = q_heads.shape[0]
    loop_size = lax.axis_size("ctx")
    my_index = lax.axis_index("ctx")
    slot_count = max(2, 2 * tok_count // loop_size)
    full_weight = lax.all_gather(w_up, "ctx", axis=0, tiled=True)
    starts = jnp.cumsum(lengths) - lengths
    local_rows = jnp.arange(tok_count, dtype=jnp.int32)
    query_spots = my_index * tok_count + local_rows
    query_request, offset = locate(query_spots, starts)
    cosine, sine_table = rope_tables(offset, ROPE)
    cache_rows = cache_rows_of(kv_latent, latent_gain, cosine, sine_table)
    query = q_heads.reshape(tok_count, H, NOPE + ROPE)
    query_nope = query[:, :, :NOPE]
    query_rope = rotate(query[:, :, NOPE:].astype(jnp.float32), cosine, sine_table).astype(
        jnp.bfloat16
    )
    dest_rank = page_ranks[:, 0]
    onehot = (dest_rank[:, None] == jnp.arange(loop_size, dtype=jnp.int32)[None, :]).astype(
        jnp.int32
    )
    running = jnp.cumsum(onehot, axis=0)
    slot_index = jnp.sum((running - 1) * onehot, axis=1)
    target = dest_rank * slot_count + slot_index
    selector = (
        target[None, :] == jnp.arange(loop_size * slot_count, dtype=jnp.int32)[:, None]
    ).astype(jnp.bfloat16)
    outgoing = jnp.dot(selector, cache_rows, preferred_element_type=jnp.float32).astype(
        jnp.bfloat16
    )
    outgoing = outgoing.reshape(loop_size, slot_count, LAT + ROPE)
    arrived = lax.all_to_all(outgoing, "ctx", split_axis=0, concat_axis=0, tiled=True)
    decode_cache = arrived.reshape(loop_size * slot_count, LAT + ROPE)

    def expand(block_rows):
        return jnp.dot(block_rows[:, :LAT], full_weight, preferred_element_type=jnp.float32).astype(
            jnp.bfloat16
        )

    def allowed_for(age_index):
        key_spots = (my_index - age_index) * tok_count + local_rows
        key_request, unused = locate(key_spots, starts)
        return (
            (key_spots[None, :] >= 0)
            & (key_spots[None, :] <= query_spots[:, None])
            & (key_request[None, :] == query_request[:, None])
        )

    masks = [allowed_for(age_index) for age_index in range(REACH + 1)]
    carried = cache_rows
    arrived_rows = [cache_rows]
    for age_index in range(REACH):
        carried = from_behind(carried, "ctx", 1)
        arrived_rows.append(carried)
    rope_list = [rows_here[:, LAT:] for rows_here in arrived_rows]
    kv_list = [expand(rows_here) for rows_here in arrived_rows]
    window = (REACH + 1) * tok_count
    key_kv = jnp.concatenate(kv_list[::-1], axis=0).reshape(window, H, NOPE + VDIM)
    key_rope = jnp.concatenate(rope_list[::-1], axis=0)
    allowed = jnp.concatenate(masks[::-1], axis=1)
    attn_out = attend(
        query_nope, query_rope, key_kv[:, :, :NOPE], key_rope, key_kv[:, :, NOPE:], allowed
    )
    return (attn_out.reshape(tok_count, H * VDIM), decode_cache)


def solution(mesh):
    return jax.shard_map(
        body,
        mesh=mesh,
        in_specs=(
            P(("groups", "ctx"), None),
            P(("groups", "ctx"), None),
            P(),
            P("ctx", None),
            P(("groups", "ctx"), None),
            P("groups"),
        ),
        out_specs=(P(("groups", "ctx"), None), P(("groups", "ctx"), None)),
        check_vma=False,
    )
```

profile of v0, /device:TPU:0, one launch (start us, length us, event | category | flops | bytes accessed | tf_op | source)
XLA Modules:
  0.0 258.3 jit_solution(2751288510454173216)
XLA Ops:
  7.2 0.0 all-gather.2.cloned.1.call-start
  7.2 0.7 all-gather.2.cloned.1.call-update
  7.9 0.9 convert_element_type.53
  8.8 0.8 reduce-window.9
  9.7 0.7 bitcast_subtract_fusion
  10.4 0.1 convert_reduce_fusion.2
  10.4 0.1 multiply_reduce_fusion
  10.5 0.1 multiply_cosine_fusion
  10.7 0.8 multiply_convert_fusion
  11.5 0.0 copy-start.3
  11.5 0.7 pad_maximum_fusion.1
  12.2 3.0 %collective-permute-start = (bf16[128,576]{0,1:T(8,128)(2,1)}, bf16[128,576]{0,1:T(8,128)(2,1)}, u32[]{:S(2)}, u32[]{:S(2)}) collective-permute-start(bf16[128,576]{0,1:T(8,128)(2,1)} %pad_maximum_fusion.1), channel_id=1, source_target_pairs={{0,1},{1,2},{2,3},{3,4},{4,5},{5,6},{6,7},{7,8},{8,9},{9,10},{10,1... | collective-permute-start | bytes 442376 | tf_op jit(solution)/shard_map/ppermute | solution.py:19
  15.2 0.7 fusion.29
  16.0 0.2 reduce_window_sum.18
  16.1 0.8 select_reduce_fusion
  17.0 0.7 multiply_add_fusion
  17.6 0.2 convolution_convert_fusion.4
  17.9 0.9 copy.28
  18.8 0.0 copy-done.3
  18.8 6.6 %all-to-all-start = ((bf16[16,16,576]{2,1,0:T(8,128)(2,1)}), bf16[16,16,576]{2,1,0:T(8,128)(2,1)S(1)}, u32[]{:S(2)}, u32[]{:S(2)}) async-start(bf16[16,16,576]{2,1,0:T(8,128)(2,1)} %bitcast.10), calls=%async_computation | async-start | bytes 655360 | tf_op jit(solution)/shard_map/all_to_all | solution.py:111
  25.4 3.5 %copy.25 = bf16[128,12288]{0,1:T(8,128)(2,1)S(1)} copy(bf16[128,12288]{1,0:T(8,128)(2,1)} %param.6) | data formatting | bytes 6291456 | tf_op args[0]
  28.9 0.0 copy-start.1
  28.9 0.2 slice_convert_fusion
  29.1 1.7 subtract_convert_fusion
  30.8 0.0 collective-permute-done
  30.8 2.3 collective-permute-start.1
  33.2 1.2 collective-permute-done.1
  34.3 0.0 copy-start.7
  34.3 5.6 %collective-permute-start.2 = (bf16[128,576]{0,1:T(8,128)(2,1)S(1)}, bf16[128,576]{0,1:T(8,128)(2,1)S(1)}, u32[]{:S(2)}, u32[]{:S(2)}) collective-permute-start(bf16[128,576]{0,1:T(8,128)(2,1)S(1)} %collective-permute-done.1), channel_id=1, source_target_pairs={{0,1},{1,2},{2,3},{3,4},{4,5},{5,6},{6,7},{7,8},{8,9},{9,10},{10,1... | collective-permute-start | bytes 442376 | tf_op jit(solution)/shard_map/ppermute | solution.py:19
  40.0 0.3 compare_and_fusion.3
  40.3 1.3 slice.80
  41.6 0.6 slice.79
  42.2 0.0 collective-permute-done.2
  42.2 0.0 copy-done.7
  42.2 0.0 copy-start.9
  42.2 0.7 copy-done.9
  42.9 0.0 all-to-all-done
  42.9 0.9 copy.30
  43.7 0.0 copy-done.1
  43.7 106.0 %all-gather.2.cloned.1.call-done = bf16[512,16384]{1,0:T(8,128)(2,1)} async-done(((bf16[32,16384]{1,0:T(8,128)(2,1)}), bf16[512,16384]{1,0:T(8,128)(2,1)}) %all-gather.2.cloned.1.call-update) | async-done | bytes 16777232 | tf_op jit(solution)/shard_map/all_gather | solution.py:85
  149.8 8.4 %convolution_convert_fusion.3 = bf16[128,16384]{1,0:T(8,128)(2,1)S(1)} fusion(bf16[512,16384]{1,0:T(8,128)(2,1)} %all-gather.2.cloned.1.call-done, bf16[128,576]{0,1:T(8,128)(2,1)} %copy-done.9), kind=kOutput, calls=%fused_computation.4 | convolution fusion | flops 2149580800 | bytes 21102592 | tf_op jit(solution)/shard_map/dot_general | solution.py:115
  158.2 0.0 copy-done.8
  158.2 2.2 copy-done
  160.4 4.6 %convolution_convert_fusion.2 = bf16[128,16384]{1,0:T(8,128)(2,1)} fusion(bf16[512,16384]{1,0:T(8,128)(2,1)S(1)} %copy-done, bf16[128,576]{0,1:T(8,128)(2,1)S(1)} %copy-done.8), kind=kOutput, calls=%fused_computation.3 | convolution fusion | flops 2149580800 | bytes 21102592 | tf_op jit(solution)/shard_map/dot_general | solution.py:115
  165.0 5.5 %convolution_convert_fusion.1 = bf16[128,16384]{1,0:T(8,128)(2,1)} fusion(bf16[512,16384]{1,0:T(8,128)(2,1)S(1)} %copy-done, bf16[128,576]{0,1:T(8,128)(2,1)} %collective-permute-done), kind=kOutput, calls=%fused_computation.2 | convolution fusion | flops 2149580800 | bytes 21102592 | tf_op jit(solution)/shard_map/dot_general | solution.py:115
  170.5 0.0 copy-done.4
  170.5 4.6 %convolution_convert_fusion = bf16[128,16384]{1,0:T(8,128)(2,1)} fusion(bf16[128,512]{0,1:T(8,128)(2,1)S(1)} %copy-done.4, bf16[512,16384]{1,0:T(8,128)(2,1)S(1)} %copy-done), kind=kOutput, calls=%fused_computation.1 | convolution fusion | flops 2149580800 | bytes 21102592 | tf_op jit(solution)/shard_map/dot_general | solution.py:115
  175.2 7.4 %pad_maximum_fusion = bf16[512,16384]{1,0:T(8,128)(2,1)S(1)} fusion(bf16[128,16384]{1,0:T(8,128)(2,1)} %convolution_convert_fusion, bf16[128,16384]{1,0:T(8,128)(2,1)} %convolution_convert_fusion.1, bf16[128,16384]{1,0:T(8,128)(2,1)} %convolution_convert_fusion.2, bf16[128,16384]{1,0:T(8,128)(2,1)S(1)} %convolution_convert_fusion.3), kind=kLoop, calls=%fused_computation.5 | loop fusion | flops 67108864 | bytes 33554432 | tf_op jit(solution)/shard_map/concatenate | solution.py:137
  182.6 4.0 %copy.35 = bf16[64,8,64,256]{3,2,1,0:T(8,128)(2,1)S(1)} copy(bf16[64,8,64,256]{3,1,2,0:T(8,128)(2,1)S(1)} %bitcast.39) | data formatting | bytes 33554432
  186.6 0.0 copy-start.2
  186.6 7.3 %fusion.33 = (bf16[512,64,128]{2,1,0:T(8,128)(2,1)}, bf16[512,64,128]{2,1,0:T(8,128)(2,1)}) fusion(bf16[512,64,256]{2,1,0:T(8,128)(2,1)S(1)} %bitcast.40), kind=kLoop, calls=%fused_computation.75 | loop fusion | bytes 33554432 | tf_op jit(solution)/shard_map/slice | solution.py:141
  193.9 0.0 copy-done.2
  193.9 0.0 slice-start
  193.9 0.0 copy-start.10
  193.9 0.0 copy-start.11
  193.9 17.6 %fusion.3 = f32[64,512,128]{2,1,0:T(8,128)} fusion(bf16[512,64,128]{2,1,0:T(8,128)(2,1)} %get-tuple-element.16, bf16[128,64,192]{0,2,1:T(8,128)(2,1)S(1)} %bitcast.42), kind=kOutput, calls=%fused_computation.10 | convolution fusion | flops 1073741824 | bytes 27262976 | tf_op jit(solution)/shard_map/thd,uhd->htu/dot_general | solution.py:65
  211.6 0.0 copy-done.5
  211.6 0.0 copy-done.6
  211.6 0.0 slice-done
  211.6 0.0 copy-done.10
  211.6 0.0 copy-done.11
  211.6 13.0 %fusion.34 = (f32[64,128]{1,0:T(8,128)S(1)}, bf16[64,128,512]{1,2,0:T(8,128)(2,1)}) fusion(pred[128,512]{0,1:T(8,128)(4,1)S(1)} %pad_add_fusion, f32[64,512,128]{2,1,0:T(8,128)} %fusion.3, bf16[128,64,32]{0,2,1:T(8,128)(2,1)S(1)} %copy-done.6, bf16[128,64,32]{0,2,1:T(8,128)(2,1)S(1)} %copy-done.5, bf16[128,32]{0,1:T(8,128)(2,1)S(1)} %get-tuple-element.23, ...), kind=kOutput, calls=%fused_computation.76 | convolution fusion | flops 568656384 | bytes 26378240 | tf_op jit(solution)/shard_map/sub | solution.py:71
  224.6 23.7 %fusion.8 = bf16[128,64,128]{0,2,1:T(8,128)(2,1)S(1)} fusion(bf16[64,128,512]{1,2,0:T(8,128)(2,1)} %get-tuple-element.30, bf16[512,64,128]{2,1,0:T(8,128)(2,1)} %get-tuple-element.15, f32[128,64]{0,1:T(8,128)S(1)} %bitcast.48), kind=kOutput, calls=%fused_computation.16 | convolution fusion | flops 1075838976 | bytes 18907136 | tf_op jit(solution)/shard_map/htu,uhv->thv/dot_general | solution.py:74
  248.4 2.9 %copy.29 = bf16[128,8192]{1,0:T(8,128)(2,1)} copy(bf16[128,8192]{0,1:T(8,128)(2,1)S(1)} %bitcast.43) | data formatting | bytes 4194304
  (13 shorter events, 0.1 us)
Async XLA Ops:
  7.2 142.6 %all-gather.2.cloned.1.call-start = ((), (), s32[]{:S(2)}) async-start(), calls=%async_computation.1 | async-start | bytes 17825792 | tf_op jit(solution)/shard_map/all_gather | solution.py:85
  11.5 7.3 %copy-start.3 = (bf16[128,512]{0,1:T(8,128)(2,1)}, bf16[128,512]{0,1:T(8,128)(2,1)S(1)}, u32[]{:S(2)}) copy-start(bf16[128,512]{0,1:T(8,128)(2,1)S(1)} %multiply_convert_fusion) | copy-start | bytes 393220
  12.2 18.6 %collective-permute-start = (bf16[128,576]{0,1:T(8,128)(2,1)}, bf16[128,576]{0,1:T(8,128)(2,1)}, u32[]{:S(2)}, u32[]{:S(2)}) collective-permute-start(bf16[128,576]{0,1:T(8,128)(2,1)} %pad_maximum_fusion.1), channel_id=1, source_target_pairs={{0,1},{1,2},{2,3},{3,4},{4,5},{5,6},{6,7},{7,8},{8,9},{9,10},{10,1... | collective-permute-start | bytes 442376 | tf_op jit(solution)/shard_map/ppermute | solution.py:19
  18.8 24.1 %all-to-all-start = ((bf16[16,16,576]{2,1,0:T(8,128)(2,1)}), bf16[16,16,576]{2,1,0:T(8,128)(2,1)S(1)}, u32[]{:S(2)}, u32[]{:S(2)}) async-start(bf16[16,16,576]{2,1,0:T(8,128)(2,1)} %bitcast.10), calls=%async_computation | async-start | bytes 655360 | tf_op jit(solution)/shard_map/all_to_all | solution.py:111
  28.9 14.9 %copy-start.1 = (bf16[128,12288]{0,1:T(8,128)(2,1)}, bf16[128,12288]{0,1:T(8,128)(2,1)S(1)}, u32[]{:S(2)}) copy-start(bf16[128,12288]{0,1:T(8,128)(2,1)S(1)} %copy.25) | copy-start | bytes 9437188
  30.8 3.5 %collective-permute-start.1 = (bf16[128,576]{0,1:T(8,128)(2,1)}, bf16[128,576]{0,1:T(8,128)(2,1)S(1)}, u32[]{:S(2)}, u32[]{:S(2)}) collective-permute-start(bf16[128,576]{0,1:T(8,128)(2,1)} %collective-permute-done), channel_id=1, source_target_pairs={{0,1},{1,2},{2,3},{3,4},{4,5},{5,6},{6,7},{7,8},{8,9},{9,10},{10,1... | collective-permute-start | bytes 442376 | tf_op jit(solution)/shard_map/ppermute | solution.py:19
  34.3 7.9 %copy-start.7 = (bf16[128,576]{0,1:T(8,128)(2,1)}, bf16[128,576]{0,1:T(8,128)(2,1)S(1)}, u32[]{:S(2)}) copy-start(bf16[128,576]{0,1:T(8,128)(2,1)S(1)} %collective-permute-done.1) | copy-start | bytes 442372
  34.3 7.9 %collective-permute-start.2 = (bf16[128,576]{0,1:T(8,128)(2,1)S(1)}, bf16[128,576]{0,1:T(8,128)(2,1)S(1)}, u32[]{:S(2)}, u32[]{:S(2)}) collective-permute-start(bf16[128,576]{0,1:T(8,128)(2,1)S(1)} %collective-permute-done.1), channel_id=1, source_target_pairs={{0,1},{1,2},{2,3},{3,4},{4,5},{5,6},{6,7},{7,8},{8,9},{9,10},{10,1... | collective-permute-start | bytes 442376 | tf_op jit(solution)/shard_map/ppermute | solution.py:19
  42.2 0.7 copy-start.9
  43.7 114.4 %copy-start.8 = (bf16[128,576]{0,1:T(8,128)(2,1)S(1)}, bf16[128,576]{0,1:T(8,128)(2,1)}, u32[]{:S(2)}) copy-start(bf16[128,576]{0,1:T(8,128)(2,1)} %copy-done.7) | copy-start | bytes 442372
  149.8 10.6 %copy-start = (bf16[512,16384]{1,0:T(8,128)(2,1)S(1)}, bf16[512,16384]{1,0:T(8,128)(2,1)}, u32[]{:S(2)}) copy-start(bf16[512,16384]{1,0:T(8,128)(2,1)} %all-gather.2.cloned.1.call-done) | copy-start | bytes 50331652
  165.0 5.5 %copy-start.4 = (bf16[128,512]{0,1:T(8,128)(2,1)S(1)}, bf16[128,512]{0,1:T(8,128)(2,1)}, u32[]{:S(2)}) copy-start(bf16[128,512]{0,1:T(8,128)(2,1)} %copy-done.3) | copy-start | bytes 393220
  186.6 7.3 %copy-start.2 = (bf16[128,12288]{0,1:T(8,128)(2,1)S(1)}, bf16[128,12288]{0,1:T(8,128)(2,1)}, u32[]{:S(2)}) copy-start(bf16[128,12288]{0,1:T(8,128)(2,1)} %copy-done.1) | copy-start | bytes 9437188
  193.9 17.7 %copy-start.5 = (bf16[128,64,32]{0,2,1:T(8,128)(2,1)S(1)}, bf16[128,64,32]{0,2,1:T(8,128)(2,1)}, u32[]{:S(2)}) copy-start(bf16[128,64,32]{0,2,1:T(8,128)(2,1)} %get-tuple-element.17) | copy-start | bytes 1572868
  193.9 17.7 %copy-start.6 = (bf16[128,64,32]{0,2,1:T(8,128)(2,1)S(1)}, bf16[128,64,32]{0,2,1:T(8,128)(2,1)}, u32[]{:S(2)}) copy-start(bf16[128,64,32]{0,2,1:T(8,128)(2,1)} %get-tuple-element.18) | copy-start | bytes 1572868
  193.9 17.7 %slice-start = ((bf16[128,576]{0,1:T(8,128)(2,1)}), bf16[128,64]{0,1:T(8,128)(2,1)S(1)}, s32[]{:S(2)}) async-start(bf16[128,576]{0,1:T(8,128)(2,1)} %copy-done.9), calls=%async_computation.2 | async-start | bytes 32768 | tf_op jit(solution)/shard_map/slice | solution.py:134
  193.9 17.7 %copy-start.10 = (bf16[128,64]{0,1:T(8,128)(2,1)S(1)}, bf16[128,64]{0,1:T(8,128)(2,1)}, u32[]{:S(2)}) copy-start(bf16[128,64]{0,1:T(8,128)(2,1)} %slice.80) | copy-start | bytes 49156
  193.9 17.7 %copy-start.11 = (bf16[128,64]{0,1:T(8,128)(2,1)S(1)}, bf16[128,64]{0,1:T(8,128)(2,1)}, u32[]{:S(2)}) copy-start(bf16[128,64]{0,1:T(8,128)(2,1)} %slice.79) | copy-start | bytes 49156
Sparse Core Ops, SparseCore 0:
  10.2 139.5 all-gather.1
where the time goes:
time: 261 us; the launch traced here: 258 us
  waiting for transfers between devices  108 us (41%)
  matrix products  77.9 us (30%)
  local copies, waits for them, and re-layouts  24.3 us (9%)
  starting transfers between devices  17.6 us (7%)
  other arithmetic  16.3 us (6%)
  between operations  14.5 us (6%)
    all_gather x1, waiting for transfers between devices, body(): full_weight = lax.all_gather(w_up, 'ctx', axis=0, tiled=True)  106 us
    dot_general x1, matrix products, attend(): jnp.einsum('htu,uhv->thv', weights, value_heads, preferred_element_type=j...  23.7 us
    dot_general x4, matrix products, expand(): jnp.dot(block_rows[:, :LAT], full_weight, preferred_element_type=jnp.floa...  23.2 us
    dot_general x1, matrix products, attend(): jnp.einsum('thd,uhd->htu', query_nope, key_nope, preferred_element_type=j...  17.6 us
    unnamed x28, local copies, waits for them, and re-layouts  14.2 us
    sub x1, matrix products, attend(): exponent = jnp.where(allowed[None], jnp.exp(scores - row_max), 0.0)  13 us
    ppermute x3, starting transfers between devices, from_behind(): return lax.ppermute(array, axis, pairs)  11 us
    concatenate x1, other arithmetic, body(): jnp.concatenate(kv_list[::-1], axis=0).reshape(window, H, NOPE + VDIM)  7.36 us
  transfers between devices with their start and end apart: 5, of which 2 were waited for; matrix products, arithmetic and copies ran while one was open for 6% of the time, Pallas kernels for 0%

commit v1 on v0

v1 whole, which is shorter than its diff:
```python
import functools
import math

import jax
import jax.numpy as jnp
import numpy as np
from jax import lax
from jax.experimental import pallas as pl
from jax.experimental.pallas import tpu as pltpu
from jax.sharding import PartitionSpec as P

H = 64
NOPE = 128
ROPE = 64
VDIM = 128
LAT = 512
REACH = 3
QUAD = 4
HQ = H // QUAD
CHUNKS = 2
HC = HQ // CHUNKS
ROW = LAT + ROPE
EXT = 640
VMEM_LIMIT = 48 * 1024 * 1024
SMEM = pltpu.SMEM
VMEM = pltpu.VMEM


def rows_kernel(slot_count, info, kv, gain, ranks, freq, rows_out, cos_out, sin_out, outgoing_out):
    tok = kv.shape[0]
    base = info[0] * tok
    spots = base + lax.broadcasted_iota(jnp.int32, (tok, 128), 0)
    lane = lax.broadcasted_iota(jnp.int32, (tok, 128), 1)
    begin = jnp.int32(0)
    own_start = jnp.zeros((tok, 128), jnp.int32)
    for r in range(info.shape[0] - 1):
        own_start = jnp.where(spots >= begin, begin, own_start)
        begin = begin + info[1 + r]
    offset = spots - own_start
    angles = offset.astype(jnp.float32) * freq[...]
    cosine = jnp.cos(angles)
    sine = jnp.where((lane & 32) == 0, -jnp.sin(angles), jnp.sin(angles))
    cos_out[...] = cosine
    sin_out[...] = sine
    raw = kv[...].astype(jnp.float32)
    latent = raw[:, :LAT]
    mean = jnp.sum(latent * latent, axis=1, keepdims=True) * (1.0 / LAT)
    latent = latent * lax.rsqrt(mean + 1e-06) * gain[...]
    key = raw[:, LAT:]
    swapped = jnp.concatenate([key[:, ROPE // 2 :], key[:, : ROPE // 2]], axis=1)
    turned = key * cosine[:, :ROPE] + swapped * sine[:, :ROPE]
    high = (offset >> 8).astype(jnp.float32)
    low = (offset & 255).astype(jnp.float32)
    meta = jnp.where(lane == 0, high, jnp.where(lane == 1, low, 0.0))
    tail = jnp.concatenate([turned, meta[:, :ROPE]], axis=1)
    rows_out[:, :LAT] = latent.astype(jnp.bfloat16)
    rows_out[:, LAT:] = tail.astype(jnp.bfloat16)

    rank_col = jnp.broadcast_to(ranks[...], (tok, tok)).astype(jnp.float32)
    rank_row = rank_col.T
    earlier = lax.broadcasted_iota(jnp.int32, (tok, tok), 0) < lax.broadcasted_iota(
        jnp.int32, (tok, tok), 1
    )
    same = jnp.where((rank_col == rank_row) & earlier, 1.0, 0.0)
    slot = jnp.sum(same, axis=0, keepdims=True)
    target = (rank_row[:1] * slot_count + slot).astype(jnp.int32)
    spots_out = lax.broadcasted_iota(jnp.int32, (outgoing_out.shape[0], tok), 0)
    selector = jnp.where(spots_out == target, 1.0, 0.0).astype(jnp.bfloat16)
    picked = jnp.dot(selector, rows_out[:, :ROW], preferred_element_type=jnp.float32)
    outgoing_out[...] = picked.astype(jnp.bfloat16)


def query_kernel(info, query, cosine, sine, *outs):
    tok = query.shape[0]
    lane = lax.broadcasted_iota(jnp.int32, (tok, 128), 1)
    low_half = lane < 64
    first_quarter = (lane & 32) == 0
    cos_table = cosine[...]
    sin_table = sine[...]
    for r in range(QUAD):
        first = (info[0] ^ r) * (HQ * (NOPE + ROPE))
        for pair in range(HQ // 2):
            out = outs[r * CHUNKS + pair // (HC // 2)]
            at = pair % (HC // 2)
            begin = pl.multiple_of(first + pair * 2 * (NOPE + ROPE), 128)
            both = query[:, pl.ds(begin, 2 * (NOPE + ROPE))]
            mid = both[:, 128:256].astype(jnp.float32)
            end = both[:, 256:384].astype(jnp.float32)
            turned = jnp.where(low_half, mid, end)
            odd_nope = pltpu.roll(jnp.where(low_half, end, mid), 64, 1)
            swapped = jnp.where(
                first_quarter, pltpu.roll(turned, 96, 1), pltpu.roll(turned, 32, 1)
            )
            turned = turned * cos_table + swapped * sin_table
            out[:, at * 256 : at * 256 + 128] = both[:, :128]
            out[:, at * 256 + 128 : at * 256 + 256] = odd_nope.astype(jnp.bfloat16)
            out[:, HC * NOPE + at * 128 : HC * NOPE + at * 128 + 128] = turned.astype(
                jnp.bfloat16
            )


def attend_kernel(info, own, other, weight, *refs):
    nope = refs[0:QUAD]
    rope = refs[QUAD : 2 * QUAD]
    outs = refs[2 * QUAD : 3 * QUAD]
    latent, rope_even, rope_odd, bias = refs[3 * QUAD :]
    tok = nope[0].shape[0]
    blocks = REACH + 2
    mine = info[0]
    partner = mine ^ 1
    scale = (NOPE + ROPE) ** (-0.5) * math.log2(math.e)

    @pl.when(pl.program_id(0) == 0)
    def _():
        has_last = (mine & 1) == 1
        starts = [mine, partner, mine - 2, partner - 2, (mine >> 1) * 2 - 3]
        blank = jnp.zeros((tok, ROPE), jnp.bfloat16)
        lane = lax.broadcasted_iota(jnp.int32, (tok, tok), 1)
        row = lax.broadcasted_iota(jnp.int32, (tok, tok), 0)
        for g in range(2):
            pieces = [
                own[g * tok : (g + 1) * tok],
                other[g * tok : (g + 1) * tok],
                own[(2 + g) * tok : (3 + g) * tok],
                other[(2 + g) * tok : (3 + g) * tok],
                jnp.where(
                    has_last,
                    own[(4 + g) * tok : (5 + g) * tok],
                    other[(4 + g) * tok : (5 + g) * tok],
                ),
            ]
            for b, piece in enumerate(pieces):
                here = slice(b * tok, (b + 1) * tok)
                latent[g, here] = piece[:, :LAT]
                turned = piece[:, LAT : LAT + ROPE]
                rope_even[g, here] = jnp.concatenate([turned, blank], axis=1)
                rope_odd[g, here] = jnp.concatenate([blank, turned], axis=1)
            for half in range(2):
                meta = pieces[half][:, LAT:].astype(jnp.float32)
                offset = (meta[:, ROPE : ROPE + 1] * 256.0 + meta[:, ROPE + 1 : ROPE + 2]).astype(
                    jnp.int32
                )
                spots = starts[half] * tok + row
                lowest = jnp.maximum(spots - offset, (starts[half] - REACH) * tok)
                for b in range(blocks):
                    keys = starts[b] * tok + lane
                    allowed = (keys >= lowest) & (keys <= spots)
                    bias[g, half * tok : (half + 1) * tok, b * tok : (b + 1) * tok] = jnp.where(
                        allowed, 0.0, -1e30
                    )

    for g in range(2):
        expanded = jnp.dot(latent[g], weight[...], preferred_element_type=jnp.float32).astype(
            jnp.bfloat16
        )
        query_rope = jnp.concatenate([rope[2 * g][...], rope[2 * g + 1][...]], axis=0)
        for b in range(2):
            at = slice(b * 128, (b + 1) * 128)
            key_rope = (rope_even, rope_odd)[b][g]
            key = jnp.concatenate([expanded[:, b * 256 : b * 256 + 128], key_rope], axis=1)
            value = expanded[:, b * 256 + 128 : b * 256 + 256]
            query = jnp.concatenate([nope[2 * g][:, at], nope[2 * g + 1][:, at]], axis=0)
            query = jnp.concatenate([query, query_rope], axis=1)
            scores = lax.dot_general(
                query, key, (((1,), (1,)), ((), ())), preferred_element_type=jnp.float32
            )
            scores = scores * scale + bias[g]
            largest = jnp.max(scores, axis=1, keepdims=True)
            expo = jnp.exp2(scores - largest)
            total = jnp.sum(expo, axis=1, keepdims=True)
            mixed = jnp.dot(expo.astype(jnp.bfloat16), value, preferred_element_type=jnp.float32)
            mixed = (mixed / total).astype(jnp.bfloat16)
            outs[2 * g][:, at] = mixed[:tok]
            outs[2 * g + 1][:, at] = mixed[tok:]


def gather_kernel(info, *refs):
    pieces, out, sems = refs[:-2], refs[-2], refs[-1]
    copies = []
    for i, piece in enumerate(pieces):
        r, j = i // CHUNKS, i % CHUNKS
        begin = (info[0] ^ r) * (HQ * VDIM) + j * HC * VDIM
        begin = pl.multiple_of(begin, 128)
        copies.append(
            pltpu.make_async_copy(piece, out.at[:, pl.ds(begin, HC * VDIM)], sems.at[i])
        )
    for copy in copies:
        copy.start()
    for copy in copies:
        copy.wait()


def shape(dims, kind=jnp.bfloat16):
    return jax.ShapeDtypeStruct(dims, kind)


def body(q_heads, kv_latent, latent_gain, w_up, page_ranks, lengths):
    tok = q_heads.shape[0]
    size = lax.axis_size("ctx")
    groups = lax.axis_size("groups")
    mine = lax.axis_index("ctx")
    quarter = lax.axis_index("groups") * 2 + mine % 2
    slot_count = max(2, 2 * tok // size)
    smem = pl.BlockSpec(memory_space=SMEM)
    whole = pl.BlockSpec(memory_space=VMEM)
    params = pltpu.CompilerParams(vmem_limit_bytes=VMEM_LIMIT)

    def quad_swap(array, r):
        dx, dc = r // 2, r % 2
        pairs = [
            (g * size + i, (g ^ dx) * size + (i ^ dc)) for g in range(groups) for i in range(size)
        ]
        return lax.ppermute(array, ("groups", "ctx"), pairs)

    def from_behind(array, by, odd_only):
        first = 1 if odd_only else 0
        step = 2 if odd_only else 1
        pairs = [(i, i + by) for i in range(first, size - by, step)]
        return lax.ppermute(array, "ctx", pairs)

    width = HQ * (NOPE + VDIM)
    keep = lax.dynamic_slice_in_dim(w_up, quarter * width, width, 1)
    give = lax.dynamic_slice_in_dim(w_up, (quarter ^ 1) * width, width, 1)
    got = quad_swap(give, 1)
    even = mine % 2 == 0
    pair_rows = jnp.concatenate(
        [jnp.where(even, keep, got), jnp.where(even, got, keep)], axis=0
    )
    same_core = [list(range(c, size, 2)) for c in range(2)]
    part = width // CHUNKS
    weights = [
        lax.all_gather(
            pair_rows[:, j * part : (j + 1) * part],
            "ctx",
            axis=0,
            tiled=True,
            axis_index_groups=same_core,
        )
        for j in range(CHUNKS)
    ]

    frequency = np.exp(-np.arange(ROPE // 2) * (2.0 * math.log(10000.0) / ROPE))
    frequency = jnp.asarray(np.tile(frequency, 4)[None, :], jnp.float32)
    info = jnp.concatenate([mine[None].astype(jnp.int32), lengths.astype(jnp.int32)])
    rows, cosine, sine, outgoing = pl.pallas_call(
        functools.partial(rows_kernel, slot_count),
        out_shape=(
            shape((tok, EXT)),
            shape((tok, 128), jnp.float32),
            shape((tok, 128), jnp.float32),
            shape((size * slot_count, ROW)),
        ),
        in_specs=[smem] + [whole] * 4,
        out_specs=[whole] * 4,
        compiler_params=params,
        name="rows",
    )(info, kv_latent, latent_gain[None, :], page_ranks, frequency)

    quarter_info = quarter[None].astype(jnp.int32)
    queries = pl.pallas_call(
        query_kernel,
        out_shape=[shape((tok, HC * (NOPE + ROPE)))] * (QUAD * CHUNKS),
        in_specs=[smem] + [whole] * 3,
        out_specs=[whole] * (QUAD * CHUNKS),
        compiler_params=params,
        name="queries",
    )(quarter_info, q_heads, cosine, sine)

    both_groups = jnp.concatenate([rows, quad_swap(rows, 2)], axis=0)
    behind = from_behind(both_groups, 2, False)
    far_behind = from_behind(both_groups, 4, True)
    own_rows = jnp.concatenate([both_groups, behind, far_behind], axis=0)
    other_rows = quad_swap(own_rows, 1)

    moved = [
        [
            queries[r * CHUNKS + j] if r == 0 else quad_swap(queries[r * CHUNKS + j], r)
            for r in range(QUAD)
        ]
        for j in range(CHUNKS)
    ]

    arrived = lax.all_to_all(
        outgoing.reshape(size, slot_count, ROW), "ctx", split_axis=0, concat_axis=0, tiled=True
    )
    decode_cache = arrived.reshape(size * slot_count, ROW)

    mine_info = mine[None].astype(jnp.int32)
    window = (REACH + 2) * tok
    flops = 2 * HC * 2 * (window * LAT * 256 + 2 * tok * window * (NOPE + ROPE + VDIM))
    attend = pl.pallas_call(
        attend_kernel,
        grid=(HC // 2,),
        out_shape=[shape((tok, HC * VDIM))] * QUAD,
        in_specs=[
            smem,
            pl.BlockSpec((6 * tok, EXT), lambda i: (0, 0)),
            pl.BlockSpec((6 * tok, EXT), lambda i: (0, 0)),
            pl.BlockSpec((LAT, 512), lambda i: (0, i)),
        ]
        + [pl.BlockSpec((tok, 256), lambda i: (0, i))] * QUAD
        + [pl.BlockSpec((tok, 128), lambda i: (0, HC + i))] * QUAD,
        out_specs=[pl.BlockSpec((tok, 256), lambda i: (0, i))] * QUAD,
        scratch_shapes=[
            VMEM((2, window, LAT), jnp.bfloat16),
            VMEM((2, window, 128), jnp.bfloat16),
            VMEM((2, window, 128), jnp.bfloat16),
            VMEM((2, 2 * tok, window), jnp.float32),
        ],
        compiler_params=params,
        cost_estimate=pl.CostEstimate(
            flops=flops, bytes_accessed=8 << 20, transcendentals=HC * 4 * tok * window
        ),
        name="attend",
    )
    results = [
        attend(mine_info, own_rows, other_rows, weights[j], *moved[j], *moved[j])
        for j in range(CHUNKS)
    ]
    pieces = [
        results[j][r] if r == 0 else quad_swap(results[j][r], r)
        for r in range(QUAD)
        for j in range(CHUNKS)
    ]
    anywhere = pl.BlockSpec(memory_space=pl.ANY)
    attn_out = pl.pallas_call(
        gather_kernel,
        out_shape=shape((tok, H * VDIM)),
        in_specs=[smem] + [anywhere] * len(pieces),
        out_specs=anywhere,
        scratch_shapes=[pltpu.SemaphoreType.DMA((len(pieces),))],
        compiler_params=params,
        name="place",
    )(quarter_info, *pieces)
    return (attn_out, decode_cache)


def solution(mesh):
    return jax.shard_map(
        body,
        mesh=mesh,
        in_specs=(
            P(("groups", "ctx"), None),
            P(("groups", "ctx"), None),
            P(),
            P("ctx", None),
            P(("groups", "ctx"), None),
            P("groups"),
        ),
        out_specs=(P(("groups", "ctx"), None), P(("groups", "ctx"), None)),
        check_vma=False,
    )
```

time: 261 us -> 161 us (0.62)
  matrix products: 77.9 us -> 0 us
  waiting for transfers between devices: 108 us -> 72.9 us
  Pallas kernels: 0 us -> 33.1 us
  local copies, waits for them, and re-layouts: 24.3 us -> 6.76 us
  other arithmetic: 16.3 us -> 1.96 us
  starting transfers between devices: 17.6 us -> 31.6 us
    dot_general x7 -> x0, matrix products: 64.8 us -> none  [the longest x1 23.7 us: attend(): jnp.einsum('htu,uhv->thv', weights, value_heads, preferred_element_type=j...]
    all_gather x1 -> x2, waiting for transfers between devices: 106 us -> 46 us  [body(): lax.all_gather(pair_rows[:, j * part:(j + 1) * part], 'ctx', axis=0, tile...]
    pallas_call x0 -> x5, Pallas kernels: none -> 33.1 us  [the longest x2 25.1 us: body(): attend(mine_info, own_rows, other_rows, weights[j], *moved[j], *moved[j])]
    ppermute x3 -> x17, waiting for transfers between devices: 1.17 us -> 26.2 us  [the longest x15 19.9 us: quad_swap(): return lax.ppermute(array, ('groups', 'ctx'), pairs)]
    sub x1 -> x0, matrix products: 13 us -> none  [attend(): exponent = jnp.where(allowed[None], jnp.exp(scores - row_max), 0.0)]
    slice x5 -> x0, local copies, waits for them, and re-layouts: 9.19 us -> none  [the longest x1 7.27 us: body(): key_kv[:, :, NOPE:]]
    unnamed x28 -> x23, local copies, waits for them, and re-layouts: 14.2 us -> 5.7 us
    ppermute x3 -> x17, starting transfers between devices: 11 us -> 19 us  [the longest x15 14.6 us: quad_swap(): return lax.ppermute(array, ('groups', 'ctx'), pairs)]
  transfers between devices with their start and end apart: 5 -> 20, of which waited for: 2 -> 8; matrix products, arithmetic and copies ran while one was open for 6% -> 1% of each run, Pallas kernels for 0% -> 20%
where the time goes in v1:
time: 161 us
  waiting for transfers between devices  72.9 us (45%)
  Pallas kernels  33.1 us (21%)
  starting transfers between devices  31.6 us (20%)
  between operations  14.2 us (9%)
  local copies, waits for them, and re-layouts  6.76 us (4%)
  other arithmetic  1.96 us (1%)
    all_gather x2, waiting for transfers between devices, body(): lax.all_gather(pair_rows[:, j * part:(j + 1) * part], 'ctx', axis=0, tile...  46 us
    pallas_call x2, Pallas kernels, body(): attend(mine_info, own_rows, other_rows, weights[j], *moved[j], *moved[j])  25.1 us
    ppermute x15, waiting for transfers between devices, quad_swap(): return lax.ppermute(array, ('groups', 'ctx'), pairs)  19.9 us
    ppermute x15, starting transfers between devices, quad_swap(): return lax.ppermute(array, ('groups', 'ctx'), pairs)  14.6 us
    all_to_all x1, starting transfers between devices, body(): lax.all_to_all(outgoing.reshape(size, slot_count, ROW), 'ctx', split_axis...  12.5 us
    ppermute x2, waiting for transfers between devices, from_behind(): return lax.ppermute(array, 'ctx', pairs)  6.25 us
    unnamed x23, local copies, waits for them, and re-layouts  5.7 us
    pallas_call x1, Pallas kernels, body(): pl.pallas_call(query_kernel, out_shape=[shape((tok, HC * (NOPE + ROPE)))]...  4.64 us
  transfers between devices with their start and end apart: 20, of which 8 were waited for; matrix products, arithmetic and copies ran while one was open for 1% of the time, Pallas kernels for 20%

profile of v1, /device:TPU:0, one launch (start us, length us, event | category | flops | bytes accessed | tf_op | source)
XLA Modules:
  0.0 160.5 jit_solution(10499266306122266704)
XLA Ops:
  7.2 0.0 copy-start.1
  7.2 0.0 copy-start.6
  7.2 0.0 copy-start.7
  7.2 0.0 all-gather.5.cloned.1.call-start
  7.3 1.0 constant_dynamic-slice_fusion
  8.3 0.5 collective-permute-start.4
  8.8 1.2 collective-permute-done.4
  9.9 1.0 broadcast_select_fusion
  11.0 0.8 pad_maximum_fusion
  11.8 0.0 all-gather.5.cloned.1.call-update
  11.9 0.0 all-gather.3.cloned.1.call-start
  11.9 0.7 all-gather.3.cloned.1.call-update
  12.6 0.2 copy.12.kv
  12.8 0.0 copy-done.7
  12.8 0.1 copy.13.ranks
  12.9 0.0 copy-done.8
  12.9 0.1 pad_add_fusion.info
  13.0 0.0 copy-done.1
  13.0 1.9 %rows.1 = (bf16[128,640]{1,0:T(8,128)(2,1)S(1)}, f32[128,128]{1,0:T(8,128)S(1)}, f32[128,128]{1,0:T(8,128)S(1)}, bf16[256,576]{1,0:T(8,128)(2,1)}) custom-call(s32[9]{0:T(128)S(1)} %pad_add_fusion.info, bf16[128,576]{1,0:T(8,128)(2,1)S(1)} %copy.12.kv, f32[1,512]{1,0:T(1,128)S(1)} %bitcast.5, s32[128,1]{1,0:T(8,128)S(1)} %copy.13.ranks, f32[1,128]{1,0:T(1,128)S(1)} %copy-done.1), custom_call_target="tpu_custom_call" | custom-call | tf_op jit(solution)/shard_map/rows/pallas_call | solution.py:245
  14.9 2.9 %collective-permute-start = (bf16[128,640]{1,0:T(8,128)(2,1)S(1)}, bf16[128,640]{1,0:T(8,128)(2,1)S(1)}, u32[]{:S(2)}, u32[]{:S(2)}) collective-permute-start(bf16[128,640]{1,0:T(8,128)(2,1)S(1)} %get-tuple-element.22), channel_id=1, source_target_pairs={{0,16},{1,17},{2,18},{3,19},{4,20},{5,21},{6,22},{7,23},{8,24},{9,... | collective-permute-start | bytes 491528 | tf_op jit(solution)/shard_map/ppermute | solution.py:213
  17.8 4.5 %collective-permute-done = bf16[128,640]{1,0:T(8,128)(2,1)S(1)} collective-permute-done((bf16[128,640]{1,0:T(8,128)(2,1)S(1)}, bf16[128,640]{1,0:T(8,128)(2,1)S(1)}, u32[]{:S(2)}, u32[]{:S(2)}) %collective-permute-start) | collective-permute-done | bytes 163872 | tf_op jit(solution)/shard_map/ppermute | solution.py:213
  22.3 3.7 %collective-permute-start.1 = (bf16[256,640]{1,0:T(8,128)(2,1)S(1)}, bf16[256,640]{1,0:T(8,128)(2,1)S(1)}, u32[]{:S(2)}, u32[]{:S(2)}) collective-permute-start(bf16[256,640]{1,0:T(8,128)(2,1)S(1)} %get-tuple-element.48), channel_id=1, source_target_pairs={{0,2},{1,3},{2,4},{3,5},{4,6},{5,7},{6,8},{7,9},{8,10},{9,11},{10,... | collective-permute-start | bytes 983048 | tf_op jit(solution)/shard_map/ppermute | solution.py:219
  26.0 0.7 collective-permute-start.2
  26.7 6.2 %collective-permute-done.1 = bf16[256,640]{1,0:T(8,128)(2,1)S(1)} collective-permute-done((bf16[256,640]{1,0:T(8,128)(2,1)S(1)}, bf16[256,640]{1,0:T(8,128)(2,1)S(1)}, u32[]{:S(2)}, u32[]{:S(2)}) %collective-permute-start.1) | collective-permute-done | bytes 327712 | tf_op jit(solution)/shard_map/ppermute | solution.py:219
  33.0 0.0 collective-permute-done.2
  33.0 3.6 %collective-permute-start.3 = (bf16[768,640]{1,0:T(8,128)(2,1)S(1)}, bf16[768,640]{1,0:T(8,128)(2,1)S(1)}, u32[]{:S(2)}, u32[]{:S(2)}) collective-permute-start(bf16[768,640]{1,0:T(8,128)(2,1)S(1)} %constant_dynamic-update-slice_fusion.2.own), channel_id=1, source_target_pairs={{0,1},{1,0},{2,3},{3,2},{4,5},{5,4},{6,7},{7,6},{8,9},{9,8},{10,11... | collective-permute-start | bytes 2949128 | tf_op jit(solution)/shard_map/ppermute | solution.py:213
  36.6 4.6 %queries.1 = (bf16[128,1536]{1,0:T(8,128)(2,1)S(1)}, bf16[128,1536]{1,0:T(8,128)(2,1)S(1)}, bf16[128,1536]{1,0:T(8,128)(2,1)}, bf16[128,1536]{1,0:T(8,128)(2,1)}...) custom-call(s32[1]{0:T(128)} %bitcast.info, ...), custom_call_target="tpu_custom_call" | custom-call | tf_op jit(solution)/shard_map/queries/pallas_call | solution.py:260
  41.3 0.8 copy-done.2
  42.0 1.1 collective-permute-start.10
  43.1 0.5 collective-permute-start.8
  43.6 0.6 collective-permute-start.9
  44.2 0.0 collective-permute-start.5
  44.2 12.5 %all-to-all-start = ((bf16[16,16,576]{2,1,0:T(8,128)(2,1)}), bf16[16,16,576]{2,1,0:T(8,128)(2,1)}, u32[]{:S(2)}, u32[]{:S(2)}) async-start(bf16[16,16,576]{2,1,0:T(8,128)(2,1)} %bitcast.3), calls=%async_computation | async-start | bytes 655360 | tf_op jit(solution)/shard_map/all_to_all | solution.py:283
  56.7 0.0 collective-permute-done.10.refs_3_.refs_7_
  56.7 1.5 collective-permute-start.6
  58.3 0.0 collective-permute-done.8.refs_1_.refs_5_
  58.3 0.2 collective-permute-start.7
  58.5 3.9 %collective-permute-done.9.refs_2_.refs_6_ = bf16[128,1536]{1,0:T(8,128)(2,1)} collective-permute-done((bf16[128,1536]{1,0:T(8,128)(2,1)}, bf16[128,1536]{1,0:T(8,128)(2,1)}, u32[]{:S(2)}, u32[]{:S(2)}) %collective-permute-start.9) | collective-permute-done | bytes 393248 | tf_op jit(solution)/shard_map/ppermute | solution.py:213
  62.4 0.0 collective-permute-done.3.other
  62.4 11.6 %all-gather.5.cloned.1.call-done.weight = bf16[512,2048]{1,0:T(8,128)(2,1)} async-done(((bf16[64,2048]{1,0:T(8,128)(2,1)}), bf16[512,2048]{1,0:T(8,128)(2,1)}) %all-gather.5.cloned.1.call-update) | async-done | bytes 2097168 | tf_op jit(solution)/shard_map/all_gather | solution.py:232
  74.0 12.6 %attend.3 = (bf16[128,1024]{1,0:T(8,128)(2,1)S(1)}, bf16[128,1024]{1,0:T(8,128)(2,1)}, bf16[128,1024]{1,0:T(8,128)(2,1)}, bf16[128,1024]{1,0:T(8,128)(2,1)S(1)}) custom-call(s32[1]{0:T(128)} %bitcast.1.info, bf16[768,640]{1,0:T(8,128)(2,1)S(1)} %constant_dynamic-update-slice_fusion.2.own, bf16[768,640]{1,0:T(8,128)(2,1)S(1)} %collective-permute-done.3.other, ...), custom_call_target="tpu_custom_call" | custom-call | flops 4362076160 | bytes 8388608 | tf_op jit(solution)/shard_map/attend/pallas_call | solution.py:317
  86.6 0.1 collective-permute-start.12
  86.7 1.5 collective-permute-start.14
  88.1 0.0 collective-permute-done.5.refs_1_.refs_5_
  88.2 0.7 copy-done.4
  88.9 0.3 collective-permute-start.16
  89.2 0.0 collective-permute-done.6.refs_2_.refs_6_
  89.2 0.0 collective-permute-done.7.refs_3_.refs_7_
  89.2 34.4 %all-gather.3.cloned.1.call-done.weight = bf16[512,2048]{1,0:T(8,128)(2,1)} async-done(((bf16[64,2048]{1,0:T(8,128)(2,1)}), bf16[512,2048]{1,0:T(8,128)(2,1)}) %all-gather.3.cloned.1.call-update) | async-done | bytes 2097168 | tf_op jit(solution)/shard_map/all_gather | solution.py:232
  123.6 1.0 copy-done.3
  124.6 1.0 copy-done.5
  125.6 12.6 %attend.2 = (bf16[128,1024]{1,0:T(8,128)(2,1)S(1)}, bf16[128,1024]{1,0:T(8,128)(2,1)}, bf16[128,1024]{1,0:T(8,128)(2,1)}, bf16[128,1024]{1,0:T(8,128)(2,1)}) custom-call(s32[1]{0:T(128)} %bitcast.1.info, bf16[768,640]{1,0:T(8,128)(2,1)S(1)} %constant_dynamic-update-slice_fusion.2.own, bf16[768,640]{1,0:T(8,128)(2,1)S(1)} %collective-permute-done.3.other, ...), custom_call_target="tpu_custom_call" | custom-call | flops 4362076160 | bytes 8388608 | tf_op jit(solution)/shard_map/attend/pallas_call | solution.py:317
  138.2 0.0 collective-permute-start.11
  138.2 1.5 collective-permute-start.13
  139.7 0.0 collective-permute-done.12.refs_3_
  139.7 0.3 collective-permute-start.15
  140.0 0.0 all-to-all-done
  140.0 1.8 %copy.14 = bf16[256,576]{0,1:T(8,128)(2,1)} copy(bf16[256,576]{1,0:T(8,128)(2,1)} %bitcast.4) | data formatting | bytes 589824
  141.9 0.0 collective-permute-done.14.refs_5_
  141.9 0.0 collective-permute-done.16.refs_7_
  141.9 0.0 collective-permute-done.11.refs_2_
  141.9 5.7 %collective-permute-done.13.refs_4_ = bf16[128,1024]{1,0:T(8,128)(2,1)S(1)} collective-permute-done((bf16[128,1024]{1,0:T(8,128)(2,1)}, bf16[128,1024]{1,0:T(8,128)(2,1)S(1)}, u32[]{:S(2)}, u32[]{:S(2)}) %collective-permute-start.13) | collective-permute-done | bytes 262176 | tf_op jit(solution)/shard_map/ppermute | solution.py:213
  147.6 4.7 %collective-permute-done.15.refs_6_ = bf16[128,1024]{1,0:T(8,128)(2,1)S(1)} collective-permute-done((bf16[128,1024]{1,0:T(8,128)(2,1)}, bf16[128,1024]{1,0:T(8,128)(2,1)S(1)}, u32[]{:S(2)}, u32[]{:S(2)}) %collective-permute-start.15) | collective-permute-done | bytes 262176 | tf_op jit(solution)/shard_map/ppermute | solution.py:213
  152.3 1.4 place.1
  (12 shorter events, 0.2 us)
Async XLA Ops:
  7.2 5.8 %copy-start.1 = (f32[1,128]{1,0:T(1,128)S(1)}, f32[1,128]{1,0:T(1,128)}, u32[]{:S(2)}) copy-start(f32[1,128]{1,0:T(1,128)} %constant.32.clone.freq) | copy-start | bytes 1540
  7.2 5.4 %copy-start.6 = (bf16[128,576]{0,1:T(8,128)(2,1)S(1)}, bf16[128,576]{0,1:T(8,128)(2,1)}, u32[]{:S(2)}) copy-start(bf16[128,576]{0,1:T(8,128)(2,1)} %param.8) | copy-start | bytes 442372
  7.2 5.6 %copy-start.7 = (s32[128,1]{0,1:T(1,128)S(1)}, s32[128,1]{0,1:T(1,128)}, u32[]{:S(2)}) copy-start(s32[128,1]{0,1:T(1,128)} %param.11) | copy-start | bytes 1540
  7.2 5.7 %copy-start.8 = (s32[8]{0:T(128)S(1)}, s32[8]{0:T(128)}, u32[]{:S(2)}) copy-start(s32[8]{0:T(128)} %param.12) | copy-start | bytes 100
  7.2 5.8 %copy-start = (f32[512]{0:T(512)S(1)}, f32[512]{0:T(512)}, u32[]{:S(2)}) copy-start(f32[512]{0:T(512)} %param.9) | copy-start | bytes 6148
  7.2 66.8 %all-gather.5.cloned.1.call-start = ((), (), s32[]{:S(2)}) async-start(), calls=%async_computation.2 | async-start | bytes 2359296 | tf_op jit(solution)/shard_map/all_gather | solution.py:232
  8.3 1.7 %collective-permute-start.4 = (bf16[32,4096]{1,0:T(8,128)(2,1)S(1)}, bf16[32,4096]{1,0:T(8,128)(2,1)S(1)}, u32[]{:S(2)}, u32[]{:S(2)}) collective-permute-start(bf16[32,4096]{1,0:T(8,128)(2,1)S(1)} %constant_dynamic-slice_fusion), channel_id=1, source_target_pairs={{0,1},{1,0},{2,3},{3,2},{4,5},{5,4},{6,7},{7,6},{8,9},{9,8},{10,11... | collective-permute-start | bytes 786440 | tf_op jit(solution)/shard_map/ppermute | solution.py:213
  11.9 111.8 %all-gather.3.cloned.1.call-start = ((), (), s32[]{:S(2)}) async-start(), calls=%async_computation.1 | async-start | bytes 2359296 | tf_op jit(solution)/shard_map/all_gather | solution.py:232
  14.9 7.4 %collective-permute-start = (bf16[128,640]{1,0:T(8,128)(2,1)S(1)}, bf16[128,640]{1,0:T(8,128)(2,1)S(1)}, u32[]{:S(2)}, u32[]{:S(2)}) collective-permute-start(bf16[128,640]{1,0:T(8,128)(2,1)S(1)} %get-tuple-element.22), channel_id=1, source_target_pairs={{0,16},{1,17},{2,18},{3,19},{4,20},{5,21},{6,22},{7,23},{8,24},{9,... | collective-permute-start | bytes 491528 | tf_op jit(solution)/shard_map/ppermute | solution.py:213
  22.3 10.6 %collective-permute-start.1 = (bf16[256,640]{1,0:T(8,128)(2,1)S(1)}, bf16[256,640]{1,0:T(8,128)(2,1)S(1)}, u32[]{:S(2)}, u32[]{:S(2)}) collective-permute-start(bf16[256,640]{1,0:T(8,128)(2,1)S(1)} %get-tuple-element.48), channel_id=1, source_target_pairs={{0,2},{1,3},{2,4},{3,5},{4,6},{5,7},{6,8},{7,9},{8,10},{9,11},{10,... | collective-permute-start | bytes 983048 | tf_op jit(solution)/shard_map/ppermute | solution.py:219
  26.0 7.0 %collective-permute-start.2 = (bf16[256,640]{1,0:T(8,128)(2,1)S(1)}, bf16[256,640]{1,0:T(8,128)(2,1)S(1)}, u32[]{:S(2)}, u32[]{:S(2)}) collective-permute-start(bf16[256,640]{1,0:T(8,128)(2,1)S(1)} %get-tuple-element.48), channel_id=1, source_target_pairs={{1,5},{3,7},{5,9},{7,11},{9,13},{11,15},{17,21},{19,23},{21,25},{2... | collective-permute-start | bytes 983048 | tf_op jit(solution)/shard_map/ppermute | solution.py:219
  33.0 29.3 %collective-permute-start.3 = (bf16[768,640]{1,0:T(8,128)(2,1)S(1)}, bf16[768,640]{1,0:T(8,128)(2,1)S(1)}, u32[]{:S(2)}, u32[]{:S(2)}) collective-permute-start(bf16[768,640]{1,0:T(8,128)(2,1)S(1)} %constant_dynamic-update-slice_fusion.2.own), channel_id=1, source_target_pairs={{0,1},{1,0},{2,3},{3,2},{4,5},{5,4},{6,7},{7,6},{8,9},{9,8},{10,11... | collective-permute-start | bytes 2949128 | tf_op jit(solution)/shard_map/ppermute | solution.py:213
  41.3 0.8 copy-start.2
  42.0 14.7 %collective-permute-start.10 = (bf16[128,1536]{1,0:T(8,128)(2,1)}, bf16[128,1536]{1,0:T(8,128)(2,1)}, u32[]{:S(2)}, u32[]{:S(2)}) collective-permute-start(bf16[128,1536]{1,0:T(8,128)(2,1)} %get-tuple-element.33), channel_id=1, source_target_pairs={{0,17},{1,16},{2,19},{3,18},{4,21},{5,20},{6,23},{7,22},{8,25},{9,... | collective-permute-start | bytes 1179656 | tf_op jit(solution)/shard_map/ppermute | solution.py:213
  43.1 15.2 %collective-permute-start.8 = (bf16[128,1536]{1,0:T(8,128)(2,1)}, bf16[128,1536]{1,0:T(8,128)(2,1)}, u32[]{:S(2)}, u32[]{:S(2)}) collective-permute-start(bf16[128,1536]{1,0:T(8,128)(2,1)} %get-tuple-element.31), channel_id=1, source_target_pairs={{0,1},{1,0},{2,3},{3,2},{4,5},{5,4},{6,7},{7,6},{8,9},{9,8},{10,11... | collective-permute-start | bytes 1179656 | tf_op jit(solution)/shard_map/ppermute | solution.py:213
  43.6 18.8 %collective-permute-start.9 = (bf16[128,1536]{1,0:T(8,128)(2,1)}, bf16[128,1536]{1,0:T(8,128)(2,1)}, u32[]{:S(2)}, u32[]{:S(2)}) collective-permute-start(bf16[128,1536]{1,0:T(8,128)(2,1)} %get-tuple-element.32), channel_id=1, source_target_pairs={{0,16},{1,17},{2,18},{3,19},{4,20},{5,21},{6,22},{7,23},{8,24},{9,... | collective-permute-start | bytes 1179656 | tf_op jit(solution)/shard_map/ppermute | solution.py:213
  44.2 44.0 %collective-permute-start.5 = (bf16[128,1536]{1,0:T(8,128)(2,1)}, bf16[128,1536]{1,0:T(8,128)(2,1)S(1)}, u32[]{:S(2)}, u32[]{:S(2)}) collective-permute-start(bf16[128,1536]{1,0:T(8,128)(2,1)} %get-tuple-element.26), channel_id=1, source_target_pairs={{0,1},{1,0},{2,3},{3,2},{4,5},{5,4},{6,7},{7,6},{8,9},{9,8},{10,11... | collective-permute-start | bytes 1179656 | tf_op jit(solution)/shard_map/ppermute | solution.py:213
  44.2 95.9 %all-to-all-start = ((bf16[16,16,576]{2,1,0:T(8,128)(2,1)}), bf16[16,16,576]{2,1,0:T(8,128)(2,1)}, u32[]{:S(2)}, u32[]{:S(2)}) async-start(bf16[16,16,576]{2,1,0:T(8,128)(2,1)} %bitcast.3), calls=%async_computation | async-start | bytes 655360 | tf_op jit(solution)/shard_map/all_to_all | solution.py:283
  56.7 32.5 %collective-permute-start.6 = (bf16[128,1536]{1,0:T(8,128)(2,1)}, bf16[128,1536]{1,0:T(8,128)(2,1)}, u32[]{:S(2)}, u32[]{:S(2)}) collective-permute-start(bf16[128,1536]{1,0:T(8,128)(2,1)} %get-tuple-element.27), channel_id=1, source_target_pairs={{0,16},{1,17},{2,18},{3,19},{4,20},{5,21},{6,22},{7,23},{8,24},{9,... | collective-permute-start | bytes 1179656 | tf_op jit(solution)/shard_map/ppermute | solution.py:213
  58.3 31.0 %collective-permute-start.7 = (bf16[128,1536]{1,0:T(8,128)(2,1)}, bf16[128,1536]{1,0:T(8,128)(2,1)}, u32[]{:S(2)}, u32[]{:S(2)}) collective-permute-start(bf16[128,1536]{1,0:T(8,128)(2,1)} %get-tuple-element.28), channel_id=1, source_target_pairs={{0,17},{1,16},{2,19},{3,18},{4,21},{5,20},{6,23},{7,22},{8,25},{9,... | collective-permute-start | bytes 1179656 | tf_op jit(solution)/shard_map/ppermute | solution.py:213
  86.6 53.1 %collective-permute-start.12 = (bf16[128,1024]{1,0:T(8,128)(2,1)}, bf16[128,1024]{1,0:T(8,128)(2,1)S(1)}, u32[]{:S(2)}, u32[]{:S(2)}) collective-permute-start(bf16[128,1024]{1,0:T(8,128)(2,1)} %get-tuple-element.36), channel_id=1, source_target_pairs={{0,1},{1,0},{2,3},{3,2},{4,5},{5,4},{6,7},{7,6},{8,9},{9,8},{10,11... | collective-permute-start | bytes 786440 | tf_op jit(solution)/shard_map/ppermute | solution.py:213
  86.7 55.2 %collective-permute-start.14 = (bf16[128,1024]{1,0:T(8,128)(2,1)}, bf16[128,1024]{1,0:T(8,128)(2,1)S(1)}, u32[]{:S(2)}, u32[]{:S(2)}) collective-permute-start(bf16[128,1024]{1,0:T(8,128)(2,1)} %get-tuple-element.38), channel_id=1, source_target_pairs={{0,16},{1,17},{2,18},{3,19},{4,20},{5,21},{6,22},{7,23},{8,24},{9,... | collective-permute-start | bytes 786440 | tf_op jit(solution)/shard_map/ppermute | solution.py:213
  88.1 0.7 copy-start.4
  88.9 53.0 %collective-permute-start.16 = (bf16[128,1024]{1,0:T(8,128)(2,1)S(1)}, bf16[128,1024]{1,0:T(8,128)(2,1)S(1)}, u32[]{:S(2)}, u32[]{:S(2)}) collective-permute-start(bf16[128,1024]{1,0:T(8,128)(2,1)S(1)} %get-tuple-element.40), channel_id=1, source_target_pairs={{0,17},{1,16},{2,19},{3,18},{4,21},{5,20},{6,23},{7,22},{8,25},{9,... | collective-permute-start | bytes 786440 | tf_op jit(solution)/shard_map/ppermute | solution.py:213
  123.6 1.0 copy-start.3
  124.6 1.0 copy-start.5
  138.2 3.7 %collective-permute-start.11 = (bf16[128,1024]{1,0:T(8,128)(2,1)}, bf16[128,1024]{1,0:T(8,128)(2,1)S(1)}, u32[]{:S(2)}, u32[]{:S(2)}) collective-permute-start(bf16[128,1024]{1,0:T(8,128)(2,1)} %get-tuple-element.35), channel_id=1, source_target_pairs={{0,1},{1,0},{2,3},{3,2},{4,5},{5,4},{6,7},{7,6},{8,9},{9,8},{10,11... | collective-permute-start | bytes 786440 | tf_op jit(solution)/shard_map/ppermute | solution.py:213
  138.2 9.4 %collective-permute-start.13 = (bf16[128,1024]{1,0:T(8,128)(2,1)}, bf16[128,1024]{1,0:T(8,128)(2,1)S(1)}, u32[]{:S(2)}, u32[]{:S(2)}) collective-permute-start(bf16[128,1024]{1,0:T(8,128)(2,1)} %get-tuple-element.37), channel_id=1, source_target_pairs={{0,16},{1,17},{2,18},{3,19},{4,20},{5,21},{6,22},{7,23},{8,24},{9,... | collective-permute-start | bytes 786440 | tf_op jit(solution)/shard_map/ppermute | solution.py:213
  139.7 12.6 %collective-permute-start.15 = (bf16[128,1024]{1,0:T(8,128)(2,1)}, bf16[128,1024]{1,0:T(8,128)(2,1)S(1)}, u32[]{:S(2)}, u32[]{:S(2)}) collective-permute-start(bf16[128,1024]{1,0:T(8,128)(2,1)} %get-tuple-element.39), channel_id=1, source_target_pairs={{0,17},{1,16},{2,19},{3,18},{4,21},{5,20},{6,23},{7,22},{8,25},{9,... | collective-permute-start | bytes 786440 | tf_op jit(solution)/shard_map/ppermute | solution.py:213
Sparse Core Ops, SparseCore 0:
  12.0 61.9 all-gather.4
  76.1 47.4 all-gather.2

commit v2 on v1

--- a/solution.py
+++ b/solution.py
@@ -17,8 +17,9 @@
 REACH = 3
 QUAD = 4
 HQ = H // QUAD
-CHUNKS = 2
-HC = HQ // CHUNKS
+CHUNK_HEADS = (8, 4, 4)
+CHUNKS = len(CHUNK_HEADS)
+FIRST_HEAD = tuple(sum(CHUNK_HEADS[:j]) for j in range(CHUNKS))
 ROW = LAT + ROPE
 EXT = 640
 VMEM_LIMIT = 48 * 1024 * 1024
@@ -80,8 +81,10 @@
     for r in range(QUAD):
         first = (info[0] ^ r) * (HQ * (NOPE + ROPE))
         for pair in range(HQ // 2):
-            out = outs[r * CHUNKS + pair // (HC // 2)]
-            at = pair % (HC // 2)
+            j = max(j for j in range(CHUNKS) if FIRST_HEAD[j] <= 2 * pair)
+            out = outs[r * CHUNKS + j]
+            at = pair - FIRST_HEAD[j] // 2
+            rope_at = CHUNK_HEADS[j] * NOPE + at * 128
             begin = pl.multiple_of(first + pair * 2 * (NOPE + ROPE), 128)
             both = query[:, pl.ds(begin, 2 * (NOPE + ROPE))]
             mid = both[:, 128:256].astype(jnp.float32)
@@ -94,16 +97,40 @@
             turned = turned * cos_table + swapped * sin_table
             out[:, at * 256 : at * 256 + 128] = both[:, :128]
             out[:, at * 256 + 128 : at * 256 + 256] = odd_nope.astype(jnp.bfloat16)
-            out[:, HC * NOPE + at * 128 : HC * NOPE + at * 128 + 128] = turned.astype(
-                jnp.bfloat16
+            out[:, rope_at : rope_at + 128] = turned.astype(jnp.bfloat16)
+
+
+def pair_kernel(info, w_up, got, *refs):
+    outs, sems = refs[:-1], refs[-1]
+    rows = got.shape[0]
+    copies = []
+    for j, out in enumerate(outs):
+        width = out.shape[1]
+        first = FIRST_HEAD[j] * (NOPE + VDIM)
+        begin = pl.multiple_of(info[0] * (HQ * (NOPE + VDIM)) + first, 128)
+        copies.append(
+            pltpu.make_async_copy(
+                w_up.at[:, pl.ds(begin, width)], out.at[pl.ds(0, rows)], sems.at[2 * j]
             )
-
-
-def attend_kernel(info, own, other, weight, *refs):
+        )
+        copies.append(
+            pltpu.make_async_copy(
+                got.at[:, pl.ds(first, width)], out.at[pl.ds(rows, rows)], sems.at[2 * j + 1]
+            )
+        )
+    for copy in copies:
+        copy.start()
+    for copy in copies:
+        copy.wait()
+
+
+def attend_kernel(outer, info, own, other, *refs):
+    pieces_count = 2 * outer if outer else 1
+    pieces_of_weight, refs = refs[:pieces_count], refs[pieces_count:]
     nope = refs[0:QUAD]
     rope = refs[QUAD : 2 * QUAD]
     outs = refs[2 * QUAD : 3 * QUAD]
-    latent, rope_even, rope_odd, bias = refs[3 * QUAD :]
+    latent, rope_even, rope_odd, bias, held = refs[3 * QUAD :]
     tok = nope[0].shape[0]
     blocks = REACH + 2
     mine = info[0]
@@ -149,6 +176,18 @@
                         allowed, 0.0, -1e30
                     )
 
+    if outer:
+        weight = held
+        for i, piece in enumerate(pieces_of_weight):
+            side, behind = i // outer, i % outer
+            chip = ((mine >> 2) + outer - behind) % outer * 2 + (((mine >> 1) & 1) ^ side)
+            rows = piece.shape[0] // 2
+            for core in range(2):
+                begin = pl.multiple_of(chip * 2 * rows + ((mine & 1) ^ core) * rows, rows)
+                held[pl.ds(begin, rows)] = piece[core * rows : (core + 1) * rows]
+    else:
+        weight = pieces_of_weight[0]
+
     for g in range(2):
         expanded = jnp.dot(latent[g], weight[...], preferred_element_type=jnp.float32).astype(
             jnp.bfloat16
@@ -179,15 +218,30 @@
     copies = []
     for i, piece in enumerate(pieces):
         r, j = i // CHUNKS, i % CHUNKS
-        begin = (info[0] ^ r) * (HQ * VDIM) + j * HC * VDIM
+        begin = (info[0] ^ r) * (HQ * VDIM) + FIRST_HEAD[j] * VDIM
         begin = pl.multiple_of(begin, 128)
         copies.append(
-            pltpu.make_async_copy(piece, out.at[:, pl.ds(begin, HC * VDIM)], sems.at[i])
+            pltpu.make_async_copy(piece, out.at[:, pl.ds(begin, piece.shape[1])], sems.at[i])
         )
     for copy in copies:
         copy.start()
     for copy in copies:
         copy.wait()
+
+
+class Stream:
+    def __init__(self, window):
+        self.window = window
+        self.arrived = []
+
+    def after(self, array):
+        if len(self.arrived) < self.window:
+            return array
+        return lax.optimization_barrier((array, self.arrived[-self.window]))[0]
+
+    def send(self, permute, array, *args):
+        self.arrived.append(permute(self.after(array), *args))
+        return self.arrived[-1]
 
 
 def shape(dims, kind=jnp.bfloat16):
@@ -212,32 +266,63 @@
         ]
         return lax.ppermute(array, ("groups", "ctx"), pairs)
 
+    def send_in_quad(array, r):
+        return quad_swap(array, r) if r == 1 else group_stream.send(quad_swap, array, r)
+
+    def around(array, by):
+        return lax.ppermute(array, "ctx", [(i, (i + by) % size) for i in range(size)])
+
+    def inner_swap(array):
+        return lax.ppermute(array, "ctx", [(i, i ^ 2) for i in range(size)])
+
     def from_behind(array, by, odd_only):
         first = 1 if odd_only else 0
         step = 2 if odd_only else 1
         pairs = [(i, i + by) for i in range(first, size - by, step)]
         return lax.ppermute(array, "ctx", pairs)
 
+    outer_stream, inner_stream, group_stream = Stream(3), Stream(2), Stream(2)
+
     width = HQ * (NOPE + VDIM)
-    keep = lax.dynamic_slice_in_dim(w_up, quarter * width, width, 1)
+    quarter_info = quarter[None].astype(jnp.int32)
+    anywhere = pl.BlockSpec(memory_space=pl.ANY)
     give = lax.dynamic_slice_in_dim(w_up, (quarter ^ 1) * width, width, 1)
     got = quad_swap(give, 1)
-    even = mine % 2 == 0
-    pair_rows = jnp.concatenate(
-        [jnp.where(even, keep, got), jnp.where(even, got, keep)], axis=0
-    )
-    same_core = [list(range(c, size, 2)) for c in range(2)]
-    part = width // CHUNKS
-    weights = [
-        lax.all_gather(
-            pair_rows[:, j * part : (j + 1) * part],
-            "ctx",
-            axis=0,
-            tiled=True,
-            axis_index_groups=same_core,
+    widths = [heads * (NOPE + VDIM) for heads in CHUNK_HEADS]
+    outer = size // 4 if size % 4 == 0 and size // 4 <= 4 else 0
+    if outer:
+        pairs_of_rows = pl.pallas_call(
+            pair_kernel,
+            out_shape=[shape((2 * w_up.shape[0], w)) for w in widths],
+            in_specs=[smem, anywhere, anywhere],
+            out_specs=[anywhere] * CHUNKS,
+            scratch_shapes=[pltpu.SemaphoreType.DMA((2 * CHUNKS,))],
+            compiler_params=params,
+            name="pair",
+        )(quarter_info, w_up, got)
+        weights = []
+        for piece in pairs_of_rows:
+            line = [piece] + [outer_stream.send(around, piece, 4 * k) for k in range(1, outer)]
+            weights.append(line + [inner_stream.send(inner_swap, one) for one in line])
+    else:
+        keep = lax.dynamic_slice_in_dim(w_up, quarter * width, width, 1)
+        even = mine % 2 == 0
+        both = jnp.concatenate(
+            [jnp.where(even, keep, got), jnp.where(even, got, keep)], axis=0
         )
-        for j in range(CHUNKS)
-    ]
+        same_core = [list(range(c, size, 2)) for c in range(2)]
+        weights = [
+            [
+                lax.all_gather(
+                    both[:, FIRST_HEAD[j] * 256 : FIRST_HEAD[j] * 256 + widths[j]],
+                    "ctx",
+                    axis=0,
+                    tiled=True,
+                    axis_index_groups=same_core,
+                )
+            ]
+            for j in range(CHUNKS)
+        ]
 
     frequency = np.exp(-np.arange(ROPE // 2) * (2.0 * math.log(10000.0) / ROPE))
     frequency = jnp.asarray(np.tile(frequency, 4)[None, :], jnp.float32)
@@ -256,17 +341,16 @@
         name="rows",
     )(info, kv_latent, latent_gain[None, :], page_ranks, frequency)
 
-    quarter_info = quarter[None].astype(jnp.int32)
     queries = pl.pallas_call(
         query_kernel,
-        out_shape=[shape((tok, HC * (NOPE + ROPE)))] * (QUAD * CHUNKS),
+        out_shape=[shape((tok, h * (NOPE + ROPE))) for h in CHUNK_HEADS] * QUAD,
         in_specs=[smem] + [whole] * 3,
         out_specs=[whole] * (QUAD * CHUNKS),
         compiler_params=params,
         name="queries",
     )(quarter_info, q_heads, cosine, sine)
 
-    both_groups = jnp.concatenate([rows, quad_swap(rows, 2)], axis=0)
+    both_groups = jnp.concatenate([rows, group_stream.send(quad_swap, rows, 2)], axis=0)
     behind = from_behind(both_groups, 2, False)
     far_behind = from_behind(both_groups, 4, True)
     own_rows = jnp.concatenate([both_groups, behind, far_behind], axis=0)
@@ -274,55 +358,60 @@
 
     moved = [
         [
-            queries[r * CHUNKS + j] if r == 0 else quad_swap(queries[r * CHUNKS + j], r)
+            queries[r * CHUNKS + j] if r == 0 else send_in_quad(queries[r * CHUNKS + j], r)
             for r in range(QUAD)
         ]
         for j in range(CHUNKS)
     ]
 
+    outgoing = lax.optimization_barrier((outgoing, moved[0][2]))[0]
     arrived = lax.all_to_all(
         outgoing.reshape(size, slot_count, ROW), "ctx", split_axis=0, concat_axis=0, tiled=True
     )
     decode_cache = arrived.reshape(size * slot_count, ROW)
 
     mine_info = mine[None].astype(jnp.int32)
+    mine_info, decode_cache = lax.optimization_barrier((mine_info, decode_cache))
     window = (REACH + 2) * tok
-    flops = 2 * HC * 2 * (window * LAT * 256 + 2 * tok * window * (NOPE + ROPE + VDIM))
-    attend = pl.pallas_call(
-        attend_kernel,
-        grid=(HC // 2,),
-        out_shape=[shape((tok, HC * VDIM))] * QUAD,
-        in_specs=[
-            smem,
-            pl.BlockSpec((6 * tok, EXT), lambda i: (0, 0)),
-            pl.BlockSpec((6 * tok, EXT), lambda i: (0, 0)),
-            pl.BlockSpec((LAT, 512), lambda i: (0, i)),
-        ]
-        + [pl.BlockSpec((tok, 256), lambda i: (0, i))] * QUAD
-        + [pl.BlockSpec((tok, 128), lambda i: (0, HC + i))] * QUAD,
-        out_specs=[pl.BlockSpec((tok, 256), lambda i: (0, i))] * QUAD,
-        scratch_shapes=[
-            VMEM((2, window, LAT), jnp.bfloat16),
-            VMEM((2, window, 128), jnp.bfloat16),
-            VMEM((2, window, 128), jnp.bfloat16),
-            VMEM((2, 2 * tok, window), jnp.float32),
-        ],
-        compiler_params=params,
-        cost_estimate=pl.CostEstimate(
-            flops=flops, bytes_accessed=8 << 20, transcendentals=HC * 4 * tok * window
-        ),
-        name="attend",
-    )
-    results = [
-        attend(mine_info, own_rows, other_rows, weights[j], *moved[j], *moved[j])
-        for j in range(CHUNKS)
-    ]
-    pieces = [
-        results[j][r] if r == 0 else quad_swap(results[j][r], r)
-        for r in range(QUAD)
-        for j in range(CHUNKS)
-    ]
-    anywhere = pl.BlockSpec(memory_space=pl.ANY)
+
+    def attend(j):
+        heads = CHUNK_HEADS[j]
+        steps = heads // 2
+        flops = 2 * heads * 2 * (window * LAT * 256 + 2 * tok * window * (NOPE + ROPE + VDIM))
+        return pl.pallas_call(
+            functools.partial(attend_kernel, outer),
+            grid=(steps,),
+            out_shape=[shape((tok, heads * VDIM))] * QUAD,
+            in_specs=[
+                smem,
+                pl.BlockSpec((6 * tok, EXT), lambda i: (0, 0)),
+                pl.BlockSpec((6 * tok, EXT), lambda i: (0, 0)),
+            ]
+            + [pl.BlockSpec((piece.shape[0], 512), lambda i: (0, i)) for piece in weights[j]]
+            + [pl.BlockSpec((tok, 256), lambda i: (0, i))] * QUAD
+            + [pl.BlockSpec((tok, 128), lambda i: (0, heads + i))] * QUAD,
+            out_specs=[pl.BlockSpec((tok, 256), lambda i: (0, i))] * QUAD,
+            scratch_shapes=[
+                VMEM((2, window, LAT), jnp.bfloat16),
+                VMEM((2, window, 128), jnp.bfloat16),
+                VMEM((2, window, 128), jnp.bfloat16),
+                VMEM((2, 2 * tok, window), jnp.float32),
+                VMEM((LAT, 512), jnp.bfloat16),
+            ],
+            compiler_params=params,
+            cost_estimate=pl.CostEstimate(
+                flops=flops,
+                bytes_accessed=heads << 20,
+                transcendentals=heads * 4 * tok * window,
+            ),
+            name="attend",
+        )(mine_info, own_rows, other_rows, *weights[j], *moved[j], *moved[j])
+
+    results = []
+    for j in range(CHUNKS):
+        parts = attend(j)
+        results.append([parts[0]] + [send_in_quad(parts[r], r) for r in range(1, QUAD)])
+    pieces = [results[j][r] for r in range(QUAD) for j in range(CHUNKS)]
     attn_out = pl.pallas_call(
         gather_kernel,
         out_shape=shape((tok, H * VDIM)),

time: 161 us -> 162 us (level)
  starting transfers between devices: 31.6 us -> 56.3 us
  waiting for transfers between devices: 72.9 us -> 48.9 us
  between operations: 14.2 us -> 1.14 us
  local copies, waits for them, and re-layouts: 6.76 us -> 18.9 us
  Pallas kernels: 33.1 us -> 35.1 us
    all_gather x2 -> x0, waiting for transfers between devices: 46 us -> none  [body(): lax.all_gather(pair_rows[:, j * part:(j + 1) * part], 'ctx', axis=0, tile...]
    ppermute x0 -> x21, waiting for transfers between devices: none -> 34.9 us  [the longest x9 24.3 us: around(): lax.ppermute(array, 'ctx', [(i, (i + by) % size) for i in range(size)])]
    ppermute x0 -> x21, starting transfers between devices: none -> 29.3 us  [the longest x9 16.7 us: around(): lax.ppermute(array, 'ctx', [(i, (i + by) % size) for i in range(size)])]
    unnamed x23 -> x79, local copies, waits for them, and re-layouts: 5.7 us -> 17.8 us
    all_to_all x1, starting transfers between devices: 12.5 us -> 5.09 us  [body(): lax.all_to_all(outgoing.reshape(size, slot_count, ROW), 'ctx', split_axis...]
    ppermute x2, waiting for transfers between devices: 6.25 us -> 0.01 us  [from_behind(): return lax.ppermute(array, 'ctx', pairs)]
    ppermute x15 -> x21, waiting for transfers between devices: 19.9 us -> 14 us  [quad_swap(): return lax.ppermute(array, ('groups', 'ctx'), pairs)]
    ppermute x15 -> x21, starting transfers between devices: 14.6 us -> 17.5 us  [quad_swap(): return lax.ppermute(array, ('groups', 'ctx'), pairs)]
  transfers between devices with their start and end apart: 20 -> 45, of which waited for: 8 -> 11; matrix products, arithmetic and copies ran while one was open for 1% -> 2% of each run, Pallas kernels for 20% -> 20%
where the time goes in v2:
time: 162 us; the launch traced here: 161 us
  starting transfers between devices  56.3 us (35%)
  waiting for transfers between devices  48.9 us (30%)
  Pallas kernels  35.1 us (22%)
  local copies, waits for them, and re-layouts  18.9 us (12%)
    pallas_call x3, Pallas kernels, attend(): pl.pallas_call(functools.partial(attend_kernel, outer), grid=(steps,), ou...  27.7 us
    ppermute x9, waiting for transfers between devices, around(): lax.ppermute(array, 'ctx', [(i, (i + by) % size) for i in range(size)])  24.3 us
    unnamed x79, local copies, waits for them, and re-layouts  17.8 us
    ppermute x21, starting transfers between devices, quad_swap(): return lax.ppermute(array, ('groups', 'ctx'), pairs)  17.5 us
    ppermute x9, starting transfers between devices, around(): lax.ppermute(array, 'ctx', [(i, (i + by) % size) for i in range(size)])  16.7 us
    ppermute x21, waiting for transfers between devices, quad_swap(): return lax.ppermute(array, ('groups', 'ctx'), pairs)  14 us
    ppermute x12, starting transfers between devices, inner_swap(): return lax.ppermute(array, 'ctx', [(i, i ^ 2) for i in range(size)])  12.6 us
    ppermute x12, waiting for transfers between devices, inner_swap(): return lax.ppermute(array, 'ctx', [(i, i ^ 2) for i in range(size)])  10.6 us
  transfers between devices with their start and end apart: 45, of which 11 were waited for; matrix products, arithmetic and copies ran while one was open for 2% of the time, Pallas kernels for 20%

profile of v2, /device:TPU:0, one launch (start us, length us, event | category | flops | bytes accessed | tf_op | source)
XLA Modules:
  0.0 161.1 jit_solution(16387592093425771461)
XLA Ops:
  0.6 1.1 copy.12.kv
  1.8 0.8 copy.13.ranks
  2.6 0.7 pad_add_fusion.info
  3.3 0.7 copy-done.1
  4.0 0.7 copy-done.2
  4.6 1.9 %rows.1 = (bf16[128,640]{1,0:T(8,128)(2,1)S(1)}, f32[128,128]{1,0:T(8,128)S(1)}, f32[128,128]{1,0:T(8,128)S(1)}, bf16[256,576]{1,0:T(8,128)(2,1)}) custom-call(s32[9]{0:T(128)S(1)} %pad_add_fusion.info, bf16[128,576]{1,0:T(8,128)(2,1)S(1)} %copy.12.kv, f32[1,512]{1,0:T(1,128)S(1)} %bitcast.5, s32[128,1]{1,0:T(8,128)S(1)} %copy.13.ranks, f32[1,128]{1,0:T(1,128)S(1)} %copy-done.2), custom_call_target="tpu_custom_call" | custom-call | tf_op jit(solution)/shard_map/rows/pallas_call | solution.py:330
  6.5 2.9 %collective-permute-start.1 = (bf16[128,640]{1,0:T(8,128)(2,1)S(1)}, bf16[128,640]{1,0:T(8,128)(2,1)S(1)}, u32[]{:S(2)}, u32[]{:S(2)}) collective-permute-start(bf16[128,640]{1,0:T(8,128)(2,1)S(1)} %get-tuple-element.69), channel_id=1, source_target_pairs={{0,16},{1,17},{2,18},{3,19},{4,20},{5,21},{6,22},{7,23},{8,24},{9,... | collective-permute-start | bytes 491528 | tf_op jit(solution)/shard_map/ppermute | solution.py:267
  9.5 4.2 %collective-permute-done.1 = bf16[128,640]{1,0:T(8,128)(2,1)S(1)} collective-permute-done((bf16[128,640]{1,0:T(8,128)(2,1)S(1)}, bf16[128,640]{1,0:T(8,128)(2,1)S(1)}, u32[]{:S(2)}, u32[]{:S(2)}) %collective-permute-start.1) | collective-permute-done | bytes 163872 | tf_op jit(solution)/shard_map/ppermute | solution.py:267
  13.7 3.7 %collective-permute-start.2 = (bf16[256,640]{1,0:T(8,128)(2,1)S(1)}, bf16[256,640]{1,0:T(8,128)(2,1)S(1)}, u32[]{:S(2)}, u32[]{:S(2)}) collective-permute-start(bf16[256,640]{1,0:T(8,128)(2,1)S(1)} %get-tuple-element.126), channel_id=1, source_target_pairs={{0,2},{1,3},{2,4},{3,5},{4,6},{5,7},{6,8},{7,9},{8,10},{9,11},{10,... | collective-permute-start | bytes 983048 | tf_op jit(solution)/shard_map/ppermute | solution.py:282
  17.4 1.0 constant_dynamic-slice_fusion
  18.4 3.3 %queries.1 = (bf16[128,1536]{1,0:T(8,128)(2,1)S(1)}, bf16[128,768]{1,0:T(8,128)(2,1)S(1)}, bf16[128,768]{1,0:T(8,128)(2,1)S(1)}, bf16[128,1536]{1,0:T(8,128)(2,1...) custom-call(s32[1]{0:T(128)} %bitcast.info, ...), custom_call_target="tpu_custom_call" | custom-call | tf_op jit(solution)/shard_map/queries/pallas_call | solution.py:344
  21.8 0.7 copy-done.17
  22.5 1.6 collective-permute-start
  24.0 0.7 collective-permute-start.3
  24.7 0.8 pair.1
  26.2 1.6 collective-permute-start.6
  27.8 2.6 %collective-permute-start.14 = (bf16[128,1536]{1,0:T(8,128)(2,1)S(1)}, bf16[128,1536]{1,0:T(8,128)(2,1)S(1)}, u32[]{:S(2)}, u32[]{:S(2)}) collective-permute-start(bf16[128,1536]{1,0:T(8,128)(2,1)S(1)} %get-tuple-element.76), channel_id=1, source_target_pairs={{0,17},{1,16},{2,19},{3,18},{4,21},{5,20},{6,23},{7,22},{8,25},{9,... | collective-permute-start | bytes 1179656 | tf_op jit(solution)/shard_map/ppermute | solution.py:267
  30.4 1.3 collective-permute-start.7
  31.7 2.7 %collective-permute-done.refs_10_.refs_14_ = bf16[128,1536]{1,0:T(8,128)(2,1)S(1)} collective-permute-done((bf16[128,1536]{1,0:T(8,128)(2,1)S(1)}, bf16[128,1536]{1,0:T(8,128)(2,1)S(1)}, u32[]{:S(2)}, u32[]{:S(2)}) %collective-permute-start) | collective-permute-done | bytes 393248 | tf_op jit(solution)/shard_map/ppermute | solution.py:267
  34.4 3.6 %collective-permute-start.8 = (bf16[64,2048]{1,0:T(8,128)(2,1)S(1)}, bf16[64,2048]{1,0:T(8,128)(2,1)}, u32[]{:S(2)}, u32[]{:S(2)}) collective-permute-start(bf16[64,2048]{1,0:T(8,128)(2,1)S(1)} %get-tuple-element.70.refs_0_), channel_id=1, source_target_pairs={{0,12},{1,13},{2,14},{3,15},{4,0},{5,1},{6,2},{7,3},{8,4},{9,5},{1... | collective-permute-start | bytes 786440 | tf_op jit(solution)/shard_map/ppermute | solution.py:273
  38.1 1.4 collective-permute-start.4
  39.5 9.2 %collective-permute-done.7.refs_2_ = bf16[64,2048]{1,0:T(8,128)(2,1)} collective-permute-done((bf16[64,2048]{1,0:T(8,128)(2,1)S(1)}, bf16[64,2048]{1,0:T(8,128)(2,1)}, u32[]{:S(2)}, u32[]{:S(2)}) %collective-permute-start.7) | collective-permute-done | bytes 262176 | tf_op jit(solution)/shard_map/ppermute | solution.py:273
  48.7 1.5 collective-permute-start.10
  50.2 0.7 copy-done.7
  50.9 0.7 copy-done.9
  52.6 5.2 %collective-permute-done.10.refs_5_ = bf16[64,2048]{1,0:T(8,128)(2,1)S(1)} collective-permute-done((bf16[64,2048]{1,0:T(8,128)(2,1)S(1)}, bf16[64,2048]{1,0:T(8,128)(2,1)S(1)}, u32[]{:S(2)}, u32[]{:S(2)}) %collective-permute-start.10) | collective-permute-done | bytes 262176 | tf_op jit(solution)/shard_map/ppermute | solution.py:276
  57.8 0.7 copy-done.11
  58.5 1.5 collective-permute-start.12
  60.1 2.6 %collective-permute-start.15 = (bf16[64,1024]{1,0:T(8,128)(2,1)}, bf16[64,1024]{1,0:T(8,128)(2,1)}, u32[]{:S(2)}, u32[]{:S(2)}) collective-permute-start(bf16[64,1024]{1,0:T(8,128)(2,1)} %get-tuple-element.82.refs_0_), channel_id=1, source_target_pairs={{0,4},{1,5},{2,6},{3,7},{4,8},{5,9},{6,10},{7,11},{8,12},{9,13},{1... | collective-permute-start | bytes 393224 | tf_op jit(solution)/shard_map/ppermute | solution.py:273
  62.7 0.7 copy-done.22
  63.3 3.3 %collective-permute-start.17 = (bf16[64,1024]{1,0:T(8,128)(2,1)}, bf16[64,1024]{1,0:T(8,128)(2,1)}, u32[]{:S(2)}, u32[]{:S(2)}) collective-permute-start(bf16[64,1024]{1,0:T(8,128)(2,1)} %get-tuple-element.82.refs_0_), channel_id=1, source_target_pairs={{0,12},{1,13},{2,14},{3,15},{4,0},{5,1},{6,2},{7,3},{8,4},{9,5},{1... | collective-permute-start | bytes 393224 | tf_op jit(solution)/shard_map/ppermute | solution.py:273
  66.6 5.1 %all-to-all-start = ((bf16[16,16,576]{2,1,0:T(8,128)(2,1)}), bf16[16,16,576]{2,1,0:T(8,128)(2,1)}, u32[]{:S(2)}, u32[]{:S(2)}) async-start(bf16[16,16,576]{2,1,0:T(8,128)(2,1)} %bitcast.3), calls=%async_computation | async-start | bytes 655360 | tf_op jit(solution)/shard_map/all_to_all | solution.py:368
  71.7 1.5 collective-permute-start.24
  73.3 1.6 collective-permute-start.16
  74.9 1.5 collective-permute-start.18
  76.3 12.0 %collective-permute-done.16.refs_2_ = bf16[64,1024]{1,0:T(8,128)(2,1)S(1)} collective-permute-done((bf16[64,1024]{1,0:T(8,128)(2,1)}, bf16[64,1024]{1,0:T(8,128)(2,1)S(1)}, u32[]{:S(2)}, u32[]{:S(2)}) %collective-permute-start.16) | collective-permute-done | bytes 131104 | tf_op jit(solution)/shard_map/ppermute | solution.py:273
  88.3 0.7 copy-done.31
  89.0 1.5 collective-permute-start.19
  90.5 0.7 copy-done.24
  92.4 3.1 %collective-permute-done.25.refs_1_ = bf16[64,1024]{1,0:T(8,128)(2,1)} collective-permute-done((bf16[64,1024]{1,0:T(8,128)(2,1)}, bf16[64,1024]{1,0:T(8,128)(2,1)}, u32[]{:S(2)}, u32[]{:S(2)}) %collective-permute-start.25) | collective-permute-done | bytes 131104 | tf_op jit(solution)/shard_map/ppermute | solution.py:273
  97.1 0.7 copy-done.35
  97.7 1.5 collective-permute-start.21
  99.2 5.0 %collective-permute-done.21.refs_7_ = bf16[64,1024]{1,0:T(8,128)(2,1)} collective-permute-done((bf16[64,1024]{1,0:T(8,128)(2,1)}, bf16[64,1024]{1,0:T(8,128)(2,1)}, u32[]{:S(2)}, u32[]{:S(2)}) %collective-permute-start.21) | collective-permute-done | bytes 131104 | tf_op jit(solution)/shard_map/ppermute | solution.py:276
  104.3 2.8 %collective-permute-start.27 = (bf16[64,1024]{1,0:T(8,128)(2,1)}, bf16[64,1024]{1,0:T(8,128)(2,1)S(1)}, u32[]{:S(2)}, u32[]{:S(2)}) collective-permute-start(bf16[64,1024]{1,0:T(8,128)(2,1)} %copy-done.27), channel_id=1, source_target_pairs={{0,12},{1,13},{2,14},{3,15},{4,0},{5,1},{6,2},{7,3},{8,4},{9,5},{1... | collective-permute-start | bytes 393224 | tf_op jit(solution)/shard_map/ppermute | solution.py:273
  107.0 1.4 collective-permute-start.28
  108.4 0.7 collective-permute-start.29
  109.4 0.9 copy-done.6
  110.3 0.9 copy-done.8
  111.3 0.9 copy-done.10
  112.2 0.9 copy-done.12
  113.2 13.5 %attend.3 = (bf16[128,1024]{1,0:T(8,128)(2,1)S(1)}, bf16[128,1024]{1,0:T(8,128)(2,1)}, bf16[128,1024]{1,0:T(8,128)(2,1)S(1)}, bf16[128,1024]{1,0:T(8,128)(2,1)S(1)}) custom-call(s32[1]{0:T(128)} %bitcast.1.info, bf16[768,640]{1,0:T(8,128)(2,1)S(1)} %constant_dynamic-update-slice_fusion.2.own, bf16[768,640]{1,0:T(8,128)(2,1)} %copy-done.3, ...), custom_call_target="tpu_custom_call" | custom-call | flops 4362076160 | bytes 8388608 | tf_op jit(solution)/shard_map/attend/pallas_call | solution.py:381
  126.8 1.1 collective-permute-start.41
  128.7 1.1 collective-permute-start.30
  129.8 0.9 collective-permute-start.31
  130.8 1.2 copy-done.4
  132.0 6.8 %attend.4 = (bf16[128,512]{1,0:T(8,128)(2,1)S(1)}, bf16[128,512]{1,0:T(8,128)(2,1)S(1)}, bf16[128,512]{1,0:T(8,128)(2,1)S(1)}, bf16[128,512]{1,0:T(8,128)(2,1)S(1)}) custom-call(s32[1]{0:T(128)} %bitcast.1.info, bf16[768,640]{1,0:T(8,128)(2,1)S(1)} %constant_dynamic-update-slice_fusion.2.own, bf16[768,640]{1,0:T(8,128)(2,1)S(1)} %copy-done.4, ...), custom_call_target="tpu_custom_call" | custom-call | flops 2181038080 | bytes 4194304 | tf_op jit(solution)/shard_map/attend/pallas_call | solution.py:381
  138.8 2.2 %collective-permute-done.38.refs_6_ = bf16[128,1024]{1,0:T(8,128)(2,1)S(1)} collective-permute-done((bf16[128,1024]{1,0:T(8,128)(2,1)S(1)}, bf16[128,1024]{1,0:T(8,128)(2,1)S(1)}, u32[]{:S(2)}, u32[]{:S(2)}) %collective-permute-start.38) | collective-permute-done | bytes 262176 | tf_op jit(solution)/shard_map/ppermute | solution.py:267
  141.1 1.6 collective-permute-start.42
  143.2 7.4 %attend.5 = (bf16[128,512]{1,0:T(8,128)(2,1)S(1)}, bf16[128,512]{1,0:T(8,128)(2,1)}, bf16[128,512]{1,0:T(8,128)(2,1)S(1)}, bf16[128,512]{1,0:T(8,128)(2,1)}) custom-call(s32[1]{0:T(128)} %bitcast.1.info, bf16[768,640]{1,0:T(8,128)(2,1)S(1)} %constant_dynamic-update-slice_fusion.2.own, bf16[768,640]{1,0:T(8,128)(2,1)S(1)} %copy-done.4, ...), custom_call_target="tpu_custom_call" | custom-call | flops 2181038080 | bytes 4194304 | tf_op jit(solution)/shard_map/attend/pallas_call | solution.py:381
  150.6 1.6 collective-permute-start.43
  152.8 1.8 %copy.14 = bf16[256,576]{0,1:T(8,128)(2,1)} copy(bf16[256,576]{1,0:T(8,128)(2,1)} %bitcast.4) | data formatting | bytes 589824
  154.6 1.8 %collective-permute-done.43.refs_11_ = bf16[128,512]{1,0:T(8,128)(2,1)S(1)} collective-permute-done((bf16[128,512]{1,0:T(8,128)(2,1)}, bf16[128,512]{1,0:T(8,128)(2,1)S(1)}, u32[]{:S(2)}, u32[]{:S(2)}) %collective-permute-start.43) | collective-permute-done | bytes 131104 | tf_op jit(solution)/shard_map/ppermute | solution.py:267
  156.4 3.1 %collective-permute-done.40.refs_8_ = bf16[128,512]{1,0:T(8,128)(2,1)S(1)} collective-permute-done((bf16[128,512]{1,0:T(8,128)(2,1)S(1)}, bf16[128,512]{1,0:T(8,128)(2,1)S(1)}, u32[]{:S(2)}, u32[]{:S(2)}) %collective-permute-start.40) | collective-permute-done | bytes 131104 | tf_op jit(solution)/shard_map/ppermute | solution.py:267
  159.5 1.4 place.1
  (116 shorter events, 7.2 us)
Async XLA Ops:
  0.6 24.1 %copy-start = (bf16[32,16384]{1,0:T(8,128)(2,1)S(1)}, bf16[32,16384]{1,0:T(8,128)(2,1)}, u32[]{:S(2)}) copy-start(bf16[32,16384]{1,0:T(8,128)(2,1)} %w_up.1) | copy-start | bytes 3145732
  6.5 7.1 %collective-permute-start.1 = (bf16[128,640]{1,0:T(8,128)(2,1)S(1)}, bf16[128,640]{1,0:T(8,128)(2,1)S(1)}, u32[]{:S(2)}, u32[]{:S(2)}) collective-permute-start(bf16[128,640]{1,0:T(8,128)(2,1)S(1)} %get-tuple-element.69), channel_id=1, source_target_pairs={{0,16},{1,17},{2,18},{3,19},{4,20},{5,21},{6,22},{7,23},{8,24},{9,... | collective-permute-start | bytes 491528 | tf_op jit(solution)/shard_map/ppermute | solution.py:267
  13.7 16.7 %collective-permute-start.2 = (bf16[256,640]{1,0:T(8,128)(2,1)S(1)}, bf16[256,640]{1,0:T(8,128)(2,1)S(1)}, u32[]{:S(2)}, u32[]{:S(2)}) collective-permute-start(bf16[256,640]{1,0:T(8,128)(2,1)S(1)} %get-tuple-element.126), channel_id=1, source_target_pairs={{0,2},{1,3},{2,4},{3,5},{4,6},{5,7},{6,8},{7,9},{8,10},{9,11},{10,... | collective-permute-start | bytes 983048 | tf_op jit(solution)/shard_map/ppermute | solution.py:282
  18.4 6.3 %collective-permute-start.5 = (bf16[32,4096]{1,0:T(8,128)(2,1)S(1)}, bf16[32,4096]{1,0:T(8,128)(2,1)S(1)}, u32[]{:S(2)}, u32[]{:S(2)}) collective-permute-start(bf16[32,4096]{1,0:T(8,128)(2,1)S(1)} %constant_dynamic-slice_fusion), channel_id=1, source_target_pairs={{0,1},{1,0},{2,3},{3,2},{4,5},{5,4},{6,7},{7,6},{8,9},{9,8},{10,11... | collective-permute-start | bytes 786440 | tf_op jit(solution)/shard_map/ppermute | solution.py:267
  22.4 2.3 %copy-start.19 = (bf16[128,768]{1,0:T(8,128)(2,1)}, bf16[128,768]{1,0:T(8,128)(2,1)S(1)}, u32[]{:S(2)}) copy-start(bf16[128,768]{1,0:T(8,128)(2,1)S(1)} %get-tuple-element.87) | copy-start | bytes 589828
  22.4 15.6 %copy-start.13 = (bf16[128,768]{1,0:T(8,128)(2,1)}, bf16[128,768]{1,0:T(8,128)(2,1)S(1)}, u32[]{:S(2)}) copy-start(bf16[128,768]{1,0:T(8,128)(2,1)S(1)} %get-tuple-element.101.refs_8_.refs_12_) | copy-start | bytes 589828
  22.4 40.2 %copy-start.15 = (bf16[128,768]{1,0:T(8,128)(2,1)}, bf16[128,768]{1,0:T(8,128)(2,1)S(1)}, u32[]{:S(2)}) copy-start(bf16[128,768]{1,0:T(8,128)(2,1)S(1)} %get-tuple-element.102) | copy-start | bytes 589828
  22.4 40.2 %copy-start.20 = (bf16[128,768]{1,0:T(8,128)(2,1)}, bf16[128,768]{1,0:T(8,128)(2,1)S(1)}, u32[]{:S(2)}) copy-start(bf16[128,768]{1,0:T(8,128)(2,1)S(1)} %get-tuple-element.106) | copy-start | bytes 589828
  22.4 44.2 %copy-start.21 = (bf16[128,768]{1,0:T(8,128)(2,1)}, bf16[128,768]{1,0:T(8,128)(2,1)S(1)}, u32[]{:S(2)}) copy-start(bf16[128,768]{1,0:T(8,128)(2,1)S(1)} %get-tuple-element.104) | copy-start | bytes 589828
  22.4 44.2 %copy-start.26 = (bf16[128,768]{1,0:T(8,128)(2,1)}, bf16[128,768]{1,0:T(8,128)(2,1)S(1)}, u32[]{:S(2)}) copy-start(bf16[128,768]{1,0:T(8,128)(2,1)S(1)} %get-tuple-element.91) | copy-start | bytes 589828
  22.5 12.0 %collective-permute-start = (bf16[128,1536]{1,0:T(8,128)(2,1)S(1)}, bf16[128,1536]{1,0:T(8,128)(2,1)S(1)}, u32[]{:S(2)}, u32[]{:S(2)}) collective-permute-start(bf16[128,1536]{1,0:T(8,128)(2,1)S(1)} %get-tuple-element.66), channel_id=1, source_target_pairs={{0,16},{1,17},{2,18},{3,19},{4,20},{5,21},{6,22},{7,23},{8,24},{9,... | collective-permute-start | bytes 1179656 | tf_op jit(solution)/shard_map/ppermute | solution.py:267
  24.0 14.0 %collective-permute-start.3 = (bf16[256,640]{1,0:T(8,128)(2,1)S(1)}, bf16[256,640]{1,0:T(8,128)(2,1)S(1)}, u32[]{:S(2)}, u32[]{:S(2)}) collective-permute-start(bf16[256,640]{1,0:T(8,128)(2,1)S(1)} %get-tuple-element.126), channel_id=1, source_target_pairs={{1,5},{3,7},{5,9},{7,11},{9,13},{11,15},{17,21},{19,23},{21,25},{2... | collective-permute-start | bytes 983048 | tf_op jit(solution)/shard_map/ppermute | solution.py:282
  26.2 33.9 %copy-start.5 = (bf16[64,2048]{1,0:T(8,128)(2,1)}, bf16[64,2048]{1,0:T(8,128)(2,1)S(1)}, u32[]{:S(2)}) copy-start(bf16[64,2048]{1,0:T(8,128)(2,1)S(1)} %get-tuple-element.70.refs_0_) | copy-start | bytes 786436
  26.2 11.9 %collective-permute-start.6 = (bf16[64,2048]{1,0:T(8,128)(2,1)S(1)}, bf16[64,2048]{1,0:T(8,128)(2,1)S(1)}, u32[]{:S(2)}, u32[]{:S(2)}) collective-permute-start(bf16[64,2048]{1,0:T(8,128)(2,1)S(1)} %get-tuple-element.70.refs_0_), channel_id=1, source_target_pairs={{0,4},{1,5},{2,6},{3,7},{4,8},{5,9},{6,10},{7,11},{8,12},{9,13},{1... | collective-permute-start | bytes 786440 | tf_op jit(solution)/shard_map/ppermute | solution.py:273
  27.8 32.3 %collective-permute-start.14 = (bf16[128,1536]{1,0:T(8,128)(2,1)S(1)}, bf16[128,1536]{1,0:T(8,128)(2,1)S(1)}, u32[]{:S(2)}, u32[]{:S(2)}) collective-permute-start(bf16[128,1536]{1,0:T(8,128)(2,1)S(1)} %get-tuple-element.76), channel_id=1, source_target_pairs={{0,17},{1,16},{2,19},{3,18},{4,21},{5,20},{6,23},{7,22},{8,25},{9,... | collective-permute-start | bytes 1179656 | tf_op jit(solution)/shard_map/ppermute | solution.py:267
  30.4 18.3 %collective-permute-start.7 = (bf16[64,2048]{1,0:T(8,128)(2,1)S(1)}, bf16[64,2048]{1,0:T(8,128)(2,1)}, u32[]{:S(2)}, u32[]{:S(2)}) collective-permute-start(bf16[64,2048]{1,0:T(8,128)(2,1)S(1)} %get-tuple-element.70.refs_0_), channel_id=1, source_target_pairs={{0,8},{1,9},{2,10},{3,11},{4,12},{5,13},{6,14},{7,15},{8,0},{9,1},... | collective-permute-start | bytes 786440 | tf_op jit(solution)/shard_map/ppermute | solution.py:273
  34.4 17.7 %collective-permute-start.8 = (bf16[64,2048]{1,0:T(8,128)(2,1)S(1)}, bf16[64,2048]{1,0:T(8,128)(2,1)}, u32[]{:S(2)}, u32[]{:S(2)}) collective-permute-start(bf16[64,2048]{1,0:T(8,128)(2,1)S(1)} %get-tuple-element.70.refs_0_), channel_id=1, source_target_pairs={{0,12},{1,13},{2,14},{3,15},{4,0},{5,1},{6,2},{7,3},{8,4},{9,5},{1... | collective-permute-start | bytes 786440 | tf_op jit(solution)/shard_map/ppermute | solution.py:273
  38.0 12.8 %collective-permute-start.9 = (bf16[64,2048]{1,0:T(8,128)(2,1)S(1)}, bf16[64,2048]{1,0:T(8,128)(2,1)S(1)}, u32[]{:S(2)}, u32[]{:S(2)}) collective-permute-start(bf16[64,2048]{1,0:T(8,128)(2,1)S(1)} %get-tuple-element.70.refs_0_), channel_id=1, source_target_pairs={{0,2},{1,3},{2,0},{3,1},{4,6},{5,7},{6,4},{7,5},{8,10},{9,11},{10,... | collective-permute-start | bytes 786440 | tf_op jit(solution)/shard_map/ppermute | solution.py:276
  38.1 70.3 %collective-permute-start.4 = (bf16[768,640]{1,0:T(8,128)(2,1)S(1)}, bf16[768,640]{1,0:T(8,128)(2,1)S(1)}, u32[]{:S(2)}, u32[]{:S(2)}) collective-permute-start(bf16[768,640]{1,0:T(8,128)(2,1)S(1)} %constant_dynamic-update-slice_fusion.2.own), channel_id=1, source_target_pairs={{0,1},{1,0},{2,3},{3,2},{4,5},{5,4},{6,7},{7,6},{8,9},{9,8},{10,11... | collective-permute-start | bytes 2949128 | tf_op jit(solution)/shard_map/ppermute | solution.py:267
  48.7 9.2 %collective-permute-start.10 = (bf16[64,2048]{1,0:T(8,128)(2,1)S(1)}, bf16[64,2048]{1,0:T(8,128)(2,1)S(1)}, u32[]{:S(2)}, u32[]{:S(2)}) collective-permute-start(bf16[64,2048]{1,0:T(8,128)(2,1)S(1)} %collective-permute-done.6.refs_1_), channel_id=1, source_target_pairs={{0,2},{1,3},{2,0},{3,1},{4,6},{5,7},{6,4},{7,5},{8,10},{9,11},{10,... | collective-permute-start | bytes 786440 | tf_op jit(solution)/shard_map/ppermute | solution.py:276
  51.6 11.1 %collective-permute-start.23 = (bf16[128,768]{1,0:T(8,128)(2,1)S(1)}, bf16[128,768]{1,0:T(8,128)(2,1)S(1)}, u32[]{:S(2)}, u32[]{:S(2)}) collective-permute-start(bf16[128,768]{1,0:T(8,128)(2,1)S(1)} %get-tuple-element.89), channel_id=1, source_target_pairs={{0,16},{1,17},{2,18},{3,19},{4,20},{5,21},{6,22},{7,23},{8,24},{9,... | collective-permute-start | bytes 589832 | tf_op jit(solution)/shard_map/ppermute | solution.py:267
  52.1 19.6 %collective-permute-start.11 = (bf16[64,2048]{1,0:T(8,128)(2,1)}, bf16[64,2048]{1,0:T(8,128)(2,1)}, u32[]{:S(2)}, u32[]{:S(2)}) collective-permute-start(bf16[64,2048]{1,0:T(8,128)(2,1)} %collective-permute-done.7.refs_2_), channel_id=1, source_target_pairs={{0,2},{1,3},{2,0},{3,1},{4,6},{5,7},{6,4},{7,5},{8,10},{9,11},{10,... | collective-permute-start | bytes 786440 | tf_op jit(solution)/shard_map/ppermute | solution.py:276
  58.5 17.8 %collective-permute-start.12 = (bf16[64,2048]{1,0:T(8,128)(2,1)}, bf16[64,2048]{1,0:T(8,128)(2,1)}, u32[]{:S(2)}, u32[]{:S(2)}) collective-permute-start(bf16[64,2048]{1,0:T(8,128)(2,1)} %collective-permute-done.8.refs_3_), channel_id=1, source_target_pairs={{0,2},{1,3},{2,0},{3,1},{4,6},{5,7},{6,4},{7,5},{8,10},{9,11},{10,... | collective-permute-start | bytes 786440 | tf_op jit(solution)/shard_map/ppermute | solution.py:276
  60.1 13.2 %collective-permute-start.15 = (bf16[64,1024]{1,0:T(8,128)(2,1)}, bf16[64,1024]{1,0:T(8,128)(2,1)}, u32[]{:S(2)}, u32[]{:S(2)}) collective-permute-start(bf16[64,1024]{1,0:T(8,128)(2,1)} %get-tuple-element.82.refs_0_), channel_id=1, source_target_pairs={{0,4},{1,5},{2,6},{3,7},{4,8},{5,9},{6,10},{7,11},{8,12},{9,13},{1... | collective-permute-start | bytes 393224 | tf_op jit(solution)/shard_map/ppermute | solution.py:273
  63.3 11.5 %collective-permute-start.17 = (bf16[64,1024]{1,0:T(8,128)(2,1)}, bf16[64,1024]{1,0:T(8,128)(2,1)}, u32[]{:S(2)}, u32[]{:S(2)}) collective-permute-start(bf16[64,1024]{1,0:T(8,128)(2,1)} %get-tuple-element.82.refs_0_), channel_id=1, source_target_pairs={{0,12},{1,13},{2,14},{3,15},{4,0},{5,1},{6,2},{7,3},{8,4},{9,5},{1... | collective-permute-start | bytes 393224 | tf_op jit(solution)/shard_map/ppermute | solution.py:273
  66.6 32.6 %all-to-all-start = ((bf16[16,16,576]{2,1,0:T(8,128)(2,1)}), bf16[16,16,576]{2,1,0:T(8,128)(2,1)}, u32[]{:S(2)}, u32[]{:S(2)}) async-start(bf16[16,16,576]{2,1,0:T(8,128)(2,1)} %bitcast.3), calls=%async_computation | async-start | bytes 655360 | tf_op jit(solution)/shard_map/all_to_all | solution.py:368
  71.7 18.7 %collective-permute-start.24 = (bf16[128,768]{1,0:T(8,128)(2,1)}, bf16[128,768]{1,0:T(8,128)(2,1)S(1)}, u32[]{:S(2)}, u32[]{:S(2)}) collective-permute-start(bf16[128,768]{1,0:T(8,128)(2,1)} %copy-done.26), channel_id=1, source_target_pairs={{0,17},{1,16},{2,19},{3,18},{4,21},{5,20},{6,23},{7,22},{8,25},{9,... | collective-permute-start | bytes 589832 | tf_op jit(solution)/shard_map/ppermute | solution.py:267
  73.3 15.1 %collective-permute-start.16 = (bf16[64,1024]{1,0:T(8,128)(2,1)}, bf16[64,1024]{1,0:T(8,128)(2,1)S(1)}, u32[]{:S(2)}, u32[]{:S(2)}) collective-permute-start(bf16[64,1024]{1,0:T(8,128)(2,1)} %get-tuple-element.82.refs_0_), channel_id=1, source_target_pairs={{0,8},{1,9},{2,10},{3,11},{4,12},{5,13},{6,14},{7,15},{8,0},{9,1},... | collective-permute-start | bytes 393224 | tf_op jit(solution)/shard_map/ppermute | solution.py:273
  74.9 13.5 %collective-permute-start.18 = (bf16[64,1024]{1,0:T(8,128)(2,1)}, bf16[64,1024]{1,0:T(8,128)(2,1)S(1)}, u32[]{:S(2)}, u32[]{:S(2)}) collective-permute-start(bf16[64,1024]{1,0:T(8,128)(2,1)} %get-tuple-element.82.refs_0_), channel_id=1, source_target_pairs={{0,2},{1,3},{2,0},{3,1},{4,6},{5,7},{6,4},{7,5},{8,10},{9,11},{10,... | collective-permute-start | bytes 393224 | tf_op jit(solution)/shard_map/ppermute | solution.py:276
  76.3 27.9 %collective-permute-start.13 = (bf16[128,1536]{1,0:T(8,128)(2,1)S(1)}, bf16[128,1536]{1,0:T(8,128)(2,1)}, u32[]{:S(2)}, u32[]{:S(2)}) collective-permute-start(bf16[128,1536]{1,0:T(8,128)(2,1)S(1)} %get-tuple-element.74), channel_id=1, source_target_pairs={{0,1},{1,0},{2,3},{3,2},{4,5},{5,4},{6,7},{7,6},{8,9},{9,8},{10,11... | collective-permute-start | bytes 1179656 | tf_op jit(solution)/shard_map/ppermute | solution.py:267
  88.3 7.2 %collective-permute-start.25 = (bf16[64,1024]{1,0:T(8,128)(2,1)}, bf16[64,1024]{1,0:T(8,128)(2,1)}, u32[]{:S(2)}, u32[]{:S(2)}) collective-permute-start(bf16[64,1024]{1,0:T(8,128)(2,1)} %copy-done.27), channel_id=1, source_target_pairs={{0,4},{1,5},{2,6},{3,7},{4,8},{5,9},{6,10},{7,11},{8,12},{9,13},{1... | collective-permute-start | bytes 393224 | tf_op jit(solution)/shard_map/ppermute | solution.py:273
  89.0 7.0 %collective-permute-start.19 = (bf16[64,1024]{1,0:T(8,128)(2,1)}, bf16[64,1024]{1,0:T(8,128)(2,1)S(1)}, u32[]{:S(2)}, u32[]{:S(2)}) collective-permute-start(bf16[64,1024]{1,0:T(8,128)(2,1)} %collective-permute-done.15.refs_1_), channel_id=1, source_target_pairs={{0,2},{1,3},{2,0},{3,1},{4,6},{5,7},{6,4},{7,5},{8,10},{9,11},{10,... | collective-permute-start | bytes 393224 | tf_op jit(solution)/shard_map/ppermute | solution.py:276
  91.2 5.9 %collective-permute-start.20 = (bf16[64,1024]{1,0:T(8,128)(2,1)S(1)}, bf16[64,1024]{1,0:T(8,128)(2,1)S(1)}, u32[]{:S(2)}, u32[]{:S(2)}) collective-permute-start(bf16[64,1024]{1,0:T(8,128)(2,1)S(1)} %collective-permute-done.16.refs_2_), channel_id=1, source_target_pairs={{0,2},{1,3},{2,0},{3,1},{4,6},{5,7},{6,4},{7,5},{8,10},{9,11},{10,... | collective-permute-start | bytes 393224 | tf_op jit(solution)/shard_map/ppermute | solution.py:276
  95.5 11.5 %collective-permute-start.33 = (bf16[128,768]{1,0:T(8,128)(2,1)}, bf16[128,768]{1,0:T(8,128)(2,1)}, u32[]{:S(2)}, u32[]{:S(2)}) collective-permute-start(bf16[128,768]{1,0:T(8,128)(2,1)} %copy-done.21), channel_id=1, source_target_pairs={{0,16},{1,17},{2,18},{3,19},{4,20},{5,21},{6,22},{7,23},{8,24},{9,... | collective-permute-start | bytes 589832 | tf_op jit(solution)/shard_map/ppermute | solution.py:267
  96.7 10.4 %collective-permute-start.34 = (bf16[128,768]{1,0:T(8,128)(2,1)}, bf16[128,768]{1,0:T(8,128)(2,1)}, u32[]{:S(2)}, u32[]{:S(2)}) collective-permute-start(bf16[128,768]{1,0:T(8,128)(2,1)} %copy-done.20), channel_id=1, source_target_pairs={{0,17},{1,16},{2,19},{3,18},{4,21},{5,20},{6,23},{7,22},{8,25},{9,... | collective-permute-start | bytes 589832 | tf_op jit(solution)/shard_map/ppermute | solution.py:267
  97.7 6.4 %collective-permute-start.21 = (bf16[64,1024]{1,0:T(8,128)(2,1)}, bf16[64,1024]{1,0:T(8,128)(2,1)}, u32[]{:S(2)}, u32[]{:S(2)}) collective-permute-start(bf16[64,1024]{1,0:T(8,128)(2,1)} %collective-permute-done.17.refs_3_), channel_id=1, source_target_pairs={{0,2},{1,3},{2,0},{3,1},{4,6},{5,7},{6,4},{7,5},{8,10},{9,11},{10,... | collective-permute-start | bytes 393224 | tf_op jit(solution)/shard_map/ppermute | solution.py:276
  104.1 25.6 %collective-permute-start.22 = (bf16[128,768]{1,0:T(8,128)(2,1)}, bf16[128,768]{1,0:T(8,128)(2,1)S(1)}, u32[]{:S(2)}, u32[]{:S(2)}) collective-permute-start(bf16[128,768]{1,0:T(8,128)(2,1)} %copy-done.19), channel_id=1, source_target_pairs={{0,1},{1,0},{2,3},{3,2},{4,5},{5,4},{6,7},{7,6},{8,9},{9,8},{10,11... | collective-permute-start | bytes 589832 | tf_op jit(solution)/shard_map/ppermute | solution.py:267
  104.3 24.1 %collective-permute-start.27 = (bf16[64,1024]{1,0:T(8,128)(2,1)}, bf16[64,1024]{1,0:T(8,128)(2,1)S(1)}, u32[]{:S(2)}, u32[]{:S(2)}) collective-permute-start(bf16[64,1024]{1,0:T(8,128)(2,1)} %copy-done.27), channel_id=1, source_target_pairs={{0,12},{1,13},{2,14},{3,15},{4,0},{5,1},{6,2},{7,3},{8,4},{9,5},{1... | collective-permute-start | bytes 393224 | tf_op jit(solution)/shard_map/ppermute | solution.py:273
  107.0 19.7 %collective-permute-start.26 = (bf16[64,1024]{1,0:T(8,128)(2,1)}, bf16[64,1024]{1,0:T(8,128)(2,1)S(1)}, u32[]{:S(2)}, u32[]{:S(2)}) collective-permute-start(bf16[64,1024]{1,0:T(8,128)(2,1)} %copy-done.27), channel_id=1, source_target_pairs={{0,8},{1,9},{2,10},{3,11},{4,12},{5,13},{6,14},{7,15},{8,0},{9,1},... | collective-permute-start | bytes 393224 | tf_op jit(solution)/shard_map/ppermute | solution.py:273
  107.0 20.8 %collective-permute-start.28 = (bf16[64,1024]{1,0:T(8,128)(2,1)}, bf16[64,1024]{1,0:T(8,128)(2,1)S(1)}, u32[]{:S(2)}, u32[]{:S(2)}) collective-permute-start(bf16[64,1024]{1,0:T(8,128)(2,1)} %copy-done.27), channel_id=1, source_target_pairs={{0,2},{1,3},{2,0},{3,1},{4,6},{5,7},{6,4},{7,5},{8,10},{9,11},{10,... | collective-permute-start | bytes 393224 | tf_op jit(solution)/shard_map/ppermute | solution.py:276
  108.4 20.3 %collective-permute-start.29 = (bf16[64,1024]{1,0:T(8,128)(2,1)}, bf16[64,1024]{1,0:T(8,128)(2,1)S(1)}, u32[]{:S(2)}, u32[]{:S(2)}) collective-permute-start(bf16[64,1024]{1,0:T(8,128)(2,1)} %collective-permute-done.25.refs_1_), channel_id=1, source_target_pairs={{0,2},{1,3},{2,0},{3,1},{4,6},{5,7},{6,4},{7,5},{8,10},{9,11},{10,... | collective-permute-start | bytes 393224 | tf_op jit(solution)/shard_map/ppermute | solution.py:276
  113.2 15.2 %copy-start.16 = (bf16[128,768]{1,0:T(8,128)(2,1)S(1)}, bf16[128,768]{1,0:T(8,128)(2,1)}, u32[]{:S(2)}) copy-start(bf16[128,768]{1,0:T(8,128)(2,1)} %copy-done.15) | copy-start | bytes 589828
  113.2 17.6 %copy-start.18 = (bf16[128,768]{1,0:T(8,128)(2,1)S(1)}, bf16[128,768]{1,0:T(8,128)(2,1)}, u32[]{:S(2)}) copy-start(bf16[128,768]{1,0:T(8,128)(2,1)} %copy-done.17) | copy-start | bytes 589828
  113.2 17.6 %copy-start.23 = (bf16[128,768]{1,0:T(8,128)(2,1)S(1)}, bf16[128,768]{1,0:T(8,128)(2,1)}, u32[]{:S(2)}) copy-start(bf16[128,768]{1,0:T(8,128)(2,1)} %copy-done.22) | copy-start | bytes 589828
  113.2 17.6 %copy-start.25 = (bf16[128,768]{1,0:T(8,128)(2,1)S(1)}, bf16[128,768]{1,0:T(8,128)(2,1)}, u32[]{:S(2)}) copy-start(bf16[128,768]{1,0:T(8,128)(2,1)} %copy-done.24) | copy-start | bytes 589828
  113.2 17.6 %copy-start.30 = (bf16[64,1024]{1,0:T(8,128)(2,1)S(1)}, bf16[64,1024]{1,0:T(8,128)(2,1)}, u32[]{:S(2)}) copy-start(bf16[64,1024]{1,0:T(8,128)(2,1)} %copy-done.29) | copy-start | bytes 393220
  113.2 17.6 %copy-start.32 = (bf16[64,1024]{1,0:T(8,128)(2,1)S(1)}, bf16[64,1024]{1,0:T(8,128)(2,1)}, u32[]{:S(2)}) copy-start(bf16[64,1024]{1,0:T(8,128)(2,1)} %copy-done.31) | copy-start | bytes 393220
  113.2 17.6 %copy-start.34 = (bf16[64,1024]{1,0:T(8,128)(2,1)S(1)}, bf16[64,1024]{1,0:T(8,128)(2,1)}, u32[]{:S(2)}) copy-start(bf16[64,1024]{1,0:T(8,128)(2,1)} %copy-done.33) | copy-start | bytes 393220
  113.2 17.6 %copy-start.36 = (bf16[64,1024]{1,0:T(8,128)(2,1)S(1)}, bf16[64,1024]{1,0:T(8,128)(2,1)}, u32[]{:S(2)}) copy-start(bf16[64,1024]{1,0:T(8,128)(2,1)} %copy-done.35) | copy-start | bytes 393220
  126.8 12.0 %collective-permute-start.41 = (bf16[128,1024]{1,0:T(8,128)(2,1)S(1)}, bf16[128,1024]{1,0:T(8,128)(2,1)S(1)}, u32[]{:S(2)}, u32[]{:S(2)}) collective-permute-start(bf16[128,1024]{1,0:T(8,128)(2,1)S(1)} %get-tuple-element.118), channel_id=1, source_target_pairs={{0,17},{1,16},{2,19},{3,18},{4,21},{5,20},{6,23},{7,22},{8,25},{9,... | collective-permute-start | bytes 786440 | tf_op jit(solution)/shard_map/ppermute | solution.py:267
  127.9 13.2 %collective-permute-start.38 = (bf16[128,1024]{1,0:T(8,128)(2,1)S(1)}, bf16[128,1024]{1,0:T(8,128)(2,1)S(1)}, u32[]{:S(2)}, u32[]{:S(2)}) collective-permute-start(bf16[128,1024]{1,0:T(8,128)(2,1)S(1)} %get-tuple-element.112), channel_id=1, source_target_pairs={{0,16},{1,17},{2,18},{3,19},{4,20},{5,21},{6,22},{7,23},{8,24},{9,... | collective-permute-start | bytes 786440 | tf_op jit(solution)/shard_map/ppermute | solution.py:267
  128.4 12.6 %collective-permute-start.32 = (bf16[128,768]{1,0:T(8,128)(2,1)S(1)}, bf16[128,768]{1,0:T(8,128)(2,1)S(1)}, u32[]{:S(2)}, u32[]{:S(2)}) collective-permute-start(bf16[128,768]{1,0:T(8,128)(2,1)S(1)} %copy-done.16), channel_id=1, source_target_pairs={{0,1},{1,0},{2,3},{3,2},{4,5},{5,4},{6,7},{7,6},{8,9},{9,8},{10,11... | collective-permute-start | bytes 589832 | tf_op jit(solution)/shard_map/ppermute | solution.py:267
  128.7 14.0 %collective-permute-start.30 = (bf16[64,1024]{1,0:T(8,128)(2,1)S(1)}, bf16[64,1024]{1,0:T(8,128)(2,1)S(1)}, u32[]{:S(2)}, u32[]{:S(2)}) collective-permute-start(bf16[64,1024]{1,0:T(8,128)(2,1)S(1)} %collective-permute-done.26.refs_2_), channel_id=1, source_target_pairs={{0,2},{1,3},{2,0},{3,1},{4,6},{5,7},{6,4},{7,5},{8,10},{9,11},{10,... | collective-permute-start | bytes 393224 | tf_op jit(solution)/shard_map/ppermute | solution.py:276
  129.8 13.4 %collective-permute-start.31 = (bf16[64,1024]{1,0:T(8,128)(2,1)S(1)}, bf16[64,1024]{1,0:T(8,128)(2,1)S(1)}, u32[]{:S(2)}, u32[]{:S(2)}) collective-permute-start(bf16[64,1024]{1,0:T(8,128)(2,1)S(1)} %collective-permute-done.27.refs_3_), channel_id=1, source_target_pairs={{0,2},{1,3},{2,0},{3,1},{4,6},{5,7},{6,4},{7,5},{8,10},{9,11},{10,... | collective-permute-start | bytes 393224 | tf_op jit(solution)/shard_map/ppermute | solution.py:276
  130.8 1.2 copy-start.4
  132.0 11.2 %copy-start.14 = (bf16[128,768]{1,0:T(8,128)(2,1)S(1)}, bf16[128,768]{1,0:T(8,128)(2,1)}, u32[]{:S(2)}) copy-start(bf16[128,768]{1,0:T(8,128)(2,1)} %copy-done.13) | copy-start | bytes 589828
  132.0 11.2 %copy-start.28 = (bf16[64,1024]{1,0:T(8,128)(2,1)S(1)}, bf16[64,1024]{1,0:T(8,128)(2,1)}, u32[]{:S(2)}) copy-start(bf16[64,1024]{1,0:T(8,128)(2,1)} %copy-done.27) | copy-start | bytes 393220
  138.8 15.8 %collective-permute-start.36 = (bf16[128,512]{1,0:T(8,128)(2,1)S(1)}, bf16[128,512]{1,0:T(8,128)(2,1)S(1)}, u32[]{:S(2)}, u32[]{:S(2)}) collective-permute-start(bf16[128,512]{1,0:T(8,128)(2,1)S(1)} %get-tuple-element.109), channel_id=1, source_target_pairs={{0,1},{1,0},{2,3},{3,2},{4,5},{5,4},{6,7},{7,6},{8,9},{9,8},{10,11... | collective-permute-start | bytes 393224 | tf_op jit(solution)/shard_map/ppermute | solution.py:267
  141.0 13.6 %collective-permute-start.35 = (bf16[128,1024]{1,0:T(8,128)(2,1)}, bf16[128,1024]{1,0:T(8,128)(2,1)S(1)}, u32[]{:S(2)}, u32[]{:S(2)}) collective-permute-start(bf16[128,1024]{1,0:T(8,128)(2,1)} %get-tuple-element.108), channel_id=1, source_target_pairs={{0,1},{1,0},{2,3},{3,2},{4,5},{5,4},{6,7},{7,6},{8,9},{9,8},{10,11... | collective-permute-start | bytes 786440 | tf_op jit(solution)/shard_map/ppermute | solution.py:267
  141.1 9.6 %collective-permute-start.42 = (bf16[128,512]{1,0:T(8,128)(2,1)S(1)}, bf16[128,512]{1,0:T(8,128)(2,1)S(1)}, u32[]{:S(2)}, u32[]{:S(2)}) collective-permute-start(bf16[128,512]{1,0:T(8,128)(2,1)S(1)} %get-tuple-element.120), channel_id=1, source_target_pairs={{0,17},{1,16},{2,19},{3,18},{4,21},{5,20},{6,23},{7,22},{8,25},{9,... | collective-permute-start | bytes 393224 | tf_op jit(solution)/shard_map/ppermute | solution.py:267
  142.7 9.5 %collective-permute-start.39 = (bf16[128,512]{1,0:T(8,128)(2,1)S(1)}, bf16[128,512]{1,0:T(8,128)(2,1)S(1)}, u32[]{:S(2)}, u32[]{:S(2)}) collective-permute-start(bf16[128,512]{1,0:T(8,128)(2,1)S(1)} %get-tuple-element.114), channel_id=1, source_target_pairs={{0,16},{1,17},{2,18},{3,19},{4,20},{5,21},{6,22},{7,23},{8,24},{9,... | collective-permute-start | bytes 393224 | tf_op jit(solution)/shard_map/ppermute | solution.py:267
  150.6 4.0 %collective-permute-start.37 = (bf16[128,512]{1,0:T(8,128)(2,1)}, bf16[128,512]{1,0:T(8,128)(2,1)S(1)}, u32[]{:S(2)}, u32[]{:S(2)}) collective-permute-start(bf16[128,512]{1,0:T(8,128)(2,1)} %get-tuple-element.110), channel_id=1, source_target_pairs={{0,1},{1,0},{2,3},{3,2},{4,5},{5,4},{6,7},{7,6},{8,9},{9,8},{10,11... | collective-permute-start | bytes 393224 | tf_op jit(solution)/shard_map/ppermute | solution.py:267
  150.6 5.7 %collective-permute-start.43 = (bf16[128,512]{1,0:T(8,128)(2,1)}, bf16[128,512]{1,0:T(8,128)(2,1)S(1)}, u32[]{:S(2)}, u32[]{:S(2)}) collective-permute-start(bf16[128,512]{1,0:T(8,128)(2,1)} %get-tuple-element.122), channel_id=1, source_target_pairs={{0,17},{1,16},{2,19},{3,18},{4,21},{5,20},{6,23},{7,22},{8,25},{9,... | collective-permute-start | bytes 393224 | tf_op jit(solution)/shard_map/ppermute | solution.py:267
  152.2 7.3 %collective-permute-start.40 = (bf16[128,512]{1,0:T(8,128)(2,1)S(1)}, bf16[128,512]{1,0:T(8,128)(2,1)S(1)}, u32[]{:S(2)}, u32[]{:S(2)}) collective-permute-start(bf16[128,512]{1,0:T(8,128)(2,1)S(1)} %get-tuple-element.116), channel_id=1, source_target_pairs={{0,16},{1,17},{2,18},{3,19},{4,20},{5,21},{6,22},{7,23},{8,24},{9,... | collective-permute-start | bytes 393224 | tf_op jit(solution)/shard_map/ppermute | solution.py:267
  (18 other events, 13.5 us)

commit v3 on v2

v3 whole, which is shorter than its diff:
```python
import functools
import math

import jax
import jax.numpy as jnp
import numpy as np
from jax import lax
from jax.experimental import pallas as pl
from jax.experimental.pallas import tpu as pltpu
from jax.sharding import PartitionSpec as P

H = 64
NOPE = 128
ROPE = 64
VDIM = 128
LAT = 512
REACH = 3
QUAD = 4
HQ = H // QUAD
CHUNK_HEADS = (4, 4, 4, 4)
CHUNKS = len(CHUNK_HEADS)
FIRST_HEAD = tuple(sum(CHUNK_HEADS[:j]) for j in range(CHUNKS))
ROW = LAT + ROPE
EXT = 640
VMEM_LIMIT = 48 * 1024 * 1024
SMEM = pltpu.SMEM
VMEM = pltpu.VMEM


def rows_kernel(slot_count, info, kv, gain, ranks, freq, rows_out, cos_out, sin_out, outgoing_out):
    tok = kv.shape[0]
    base = info[0] * tok
    spots = base + lax.broadcasted_iota(jnp.int32, (tok, 128), 0)
    lane = lax.broadcasted_iota(jnp.int32, (tok, 128), 1)
    begin = jnp.int32(0)
    own_start = jnp.zeros((tok, 128), jnp.int32)
    for r in range(info.shape[0] - 1):
        own_start = jnp.where(spots >= begin, begin, own_start)
        begin = begin + info[1 + r]
    offset = spots - own_start
    angles = offset.astype(jnp.float32) * freq[...]
    cosine = jnp.cos(angles)
    sine = jnp.where((lane & 32) == 0, -jnp.sin(angles), jnp.sin(angles))
    cos_out[...] = cosine
    sin_out[...] = sine
    raw = kv[...].astype(jnp.float32)
    latent = raw[:, :LAT]
    mean = jnp.sum(latent * latent, axis=1, keepdims=True) * (1.0 / LAT)
    latent = latent * lax.rsqrt(mean + 1e-06) * gain[...]
    key = raw[:, LAT:]
    swapped = jnp.concatenate([key[:, ROPE // 2 :], key[:, : ROPE // 2]], axis=1)
    turned = key * cosine[:, :ROPE] + swapped * sine[:, :ROPE]
    high = (offset >> 8).astype(jnp.float32)
    low = (offset & 255).astype(jnp.float32)
    meta = jnp.where(lane == 0, high, jnp.where(lane == 1, low, 0.0))
    tail = jnp.concatenate([turned, meta[:, :ROPE]], axis=1)
    rows_out[:, :LAT] = latent.astype(jnp.bfloat16)
    rows_out[:, LAT:] = tail.astype(jnp.bfloat16)

    rank_col = jnp.broadcast_to(ranks[...], (tok, tok)).astype(jnp.float32)
    rank_row = rank_col.T
    earlier = lax.broadcasted_iota(jnp.int32, (tok, tok), 0) < lax.broadcasted_iota(
        jnp.int32, (tok, tok), 1
    )
    same = jnp.where((rank_col == rank_row) & earlier, 1.0, 0.0)
    slot = jnp.sum(same, axis=0, keepdims=True)
    target = (rank_row[:1] * slot_count + slot).astype(jnp.int32)
    spots_out = lax.broadcasted_iota(jnp.int32, (outgoing_out.shape[0], tok), 0)
    selector = jnp.where(spots_out == target, 1.0, 0.0).astype(jnp.bfloat16)
    picked = jnp.dot(selector, rows_out[:, :ROW], preferred_element_type=jnp.float32)
    outgoing_out[...] = picked.astype(jnp.bfloat16)


def query_kernel(query, cosine, sine, *outs):
    tok = query.shape[0]
    lane = lax.broadcasted_iota(jnp.int32, (tok, 128), 1)
    low_half = lane < 64
    first_quarter = (lane & 32) == 0
    cos_table = cosine[...]
    sin_table = sine[...]
    for member in range(QUAD):
        for pair in range(HQ // 2):
            j = max(j for j in range(CHUNKS) if FIRST_HEAD[j] <= 2 * pair)
            out = outs[j]
            at = pair - FIRST_HEAD[j] // 2
            rope_at = CHUNK_HEADS[j] * NOPE + at * 128
            begin = (member * HQ + pair * 2) * (NOPE + ROPE)
            both = query[:, begin : begin + 2 * (NOPE + ROPE)]
            mid = both[:, 128:256].astype(jnp.float32)
            end = both[:, 256:384].astype(jnp.float32)
            turned = jnp.where(low_half, mid, end)
            odd_nope = pltpu.roll(jnp.where(low_half, end, mid), 64, 1)
            swapped = jnp.where(
                first_quarter, pltpu.roll(turned, 96, 1), pltpu.roll(turned, 32, 1)
            )
            turned = turned * cos_table + swapped * sin_table
            out[member, :, at * 256 : at * 256 + 128] = both[:, :128]
            out[member, :, at * 256 + 128 : at * 256 + 256] = odd_nope.astype(jnp.bfloat16)
            out[member, :, rope_at : rope_at + 128] = turned.astype(jnp.bfloat16)


def spread_kernel(outer, info, w_up, *refs):
    outs, sem = refs[:-1], refs[-1]
    rows = w_up.shape[0]
    copies = []
    for j, out in enumerate(outs):
        width = out.shape[1]
        for core in range(2):
            begin = (info[1] * 2 + core) * (HQ * (NOPE + VDIM)) + FIRST_HEAD[j] * (NOPE + VDIM)
            begin = pl.multiple_of(begin, 128)
            for place in range(outer):
                copies.append(
                    pltpu.make_async_copy(
                        w_up.at[:, pl.ds(begin, width)],
                        out.at[pl.ds((place * 2 + core) * rows, rows)],
                        sem.at[len(copies)],
                    )
                )
    for copy in copies:
        copy.start()
    for copy in copies:
        copy.wait()


def attend_kernel(outer, info, own, other, *refs):
    count = 2 if outer else 1
    pieces_of_weight, refs = refs[:count], refs[count:]
    nope, rope, out, latent, rope_even, rope_odd, bias, held = refs
    tok = nope.shape[1]
    blocks = REACH + 2
    mine = info[0]
    group = info[1]
    partner = mine ^ 1
    scale = (NOPE + ROPE) ** (-0.5) * math.log2(math.e)

    @pl.when(pl.program_id(0) == 0)
    def _():
        has_last = (mine & 1) == 1
        starts = [mine, partner, mine - 2, partner - 2, (mine >> 1) * 2 - 3]
        blank = jnp.zeros((tok, ROPE), jnp.bfloat16)
        lane = lax.broadcasted_iota(jnp.int32, (tok, tok), 1)
        row = lax.broadcasted_iota(jnp.int32, (tok, tok), 0)
        for g in range(2):
            pieces = [
                own[g * tok : (g + 1) * tok],
                other[g * tok : (g + 1) * tok],
                own[(2 + g) * tok : (3 + g) * tok],
                other[(2 + g) * tok : (3 + g) * tok],
                jnp.where(
                    has_last,
                    own[(4 + g) * tok : (5 + g) * tok],
                    other[(4 + g) * tok : (5 + g) * tok],
                ),
            ]
            for b, piece in enumerate(pieces):
                here = slice(b * tok, (b + 1) * tok)
                latent[g, here] = piece[:, :LAT]
                turned = piece[:, LAT : LAT + ROPE]
                rope_even[g, here] = jnp.concatenate([turned, blank], axis=1)
                rope_odd[g, here] = jnp.concatenate([blank, turned], axis=1)
            for half in range(2):
                meta = jnp.where((mine & 1) == half, pieces[0][:, LAT:], pieces[1][:, LAT:])
                meta = meta.astype(jnp.float32)
                block = (mine >> 1) * 2 + half
                offset = (meta[:, ROPE : ROPE + 1] * 256.0 + meta[:, ROPE + 1 : ROPE + 2]).astype(
                    jnp.int32
                )
                spots = block * tok + row
                lowest = jnp.maximum(spots - offset, (block - REACH) * tok)
                for b in range(blocks):
                    keys = starts[b] * tok + lane
                    allowed = (keys >= lowest) & (keys <= spots)
                    bias[g, half * tok : (half + 1) * tok, b * tok : (b + 1) * tok] = jnp.where(
                        allowed, 0.0, -1e30
                    )

    if outer:
        weight = held
        for side, piece in enumerate(pieces_of_weight):
            rows = piece.shape[0] // outer
            for place in range(outer):
                chip = place * 2 + (((mine >> 1) & 1) ^ side)
                begin = pl.multiple_of(chip * rows, rows)
                held[pl.ds(begin, rows)] = piece[place * rows : (place + 1) * rows]
    else:
        weight = pieces_of_weight[0]

    for g in range(2):
        expanded = jnp.dot(latent[g], weight[...], preferred_element_type=jnp.float32).astype(
            jnp.bfloat16
        )
        first = (group ^ g) * 2
        query_rope = jnp.concatenate([rope[first], rope[first + 1]], axis=0)
        for b in range(2):
            at = slice(b * 128, (b + 1) * 128)
            key_rope = (rope_even, rope_odd)[b][g]
            key = jnp.concatenate([expanded[:, b * 256 : b * 256 + 128], key_rope], axis=1)
            value = expanded[:, b * 256 + 128 : b * 256 + 256]
            query = jnp.concatenate([nope[first, :, at], nope[first + 1, :, at]], axis=0)
            query = jnp.concatenate([query, query_rope], axis=1)
            scores = lax.dot_general(
                query, key, (((1,), (1,)), ((), ())), preferred_element_type=jnp.float32
            )
            scores = scores * scale + bias[g]
            largest = jnp.max(scores, axis=1, keepdims=True)
            expo = jnp.exp2(scores - largest)
            total = jnp.sum(expo, axis=1, keepdims=True)
            mixed = jnp.dot(expo.astype(jnp.bfloat16), value, preferred_element_type=jnp.float32)
            mixed = (mixed / total).astype(jnp.bfloat16)
            out[first, :, at] = mixed[:tok]
            out[first + 1, :, at] = mixed[tok:]


def place_kernel(*refs):
    pieces, out, sem = refs[:-2], refs[-2], refs[-1]
    copies = []
    for j, piece in enumerate(pieces):
        for member in range(QUAD):
            begin = (member * HQ + FIRST_HEAD[j]) * VDIM
            copies.append(
                pltpu.make_async_copy(
                    piece.at[member],
                    out.at[:, pl.ds(begin, piece.shape[2])],
                    sem.at[len(copies)],
                )
            )
    for copy in copies:
        copy.start()
    for copy in copies:
        copy.wait()


class Stream:
    def __init__(self, window):
        self.window = window
        self.arrived = []

    def after(self, array):
        if len(self.arrived) < self.window:
            return array
        return lax.optimization_barrier((array, self.arrived[-self.window]))[0]

    def send(self, permute, array, *args):
        self.arrived.append(permute(self.after(array), *args))
        return self.arrived[-1]


def shape(dims, kind=jnp.bfloat16):
    return jax.ShapeDtypeStruct(dims, kind)


def body(q_heads, kv_latent, latent_gain, w_up, page_ranks, lengths):
    tok = q_heads.shape[0]
    size = lax.axis_size("ctx")
    groups = lax.axis_size("groups")
    mine = lax.axis_index("ctx")
    group = lax.axis_index("groups")
    slot_count = max(2, 2 * tok // size)
    smem = pl.BlockSpec(memory_space=SMEM)
    whole = pl.BlockSpec(memory_space=VMEM)
    params = pltpu.CompilerParams(vmem_limit_bytes=VMEM_LIMIT)

    def quad_swap(array, r):
        dx, dc = r // 2, r % 2
        pairs = [
            (g * size + i, (g ^ dx) * size + (i ^ dc)) for g in range(groups) for i in range(size)
        ]
        return lax.ppermute(array, ("groups", "ctx"), pairs)

    quads = [
        [g * size + chip * 2 + c for g in range(groups) for c in range(2)]
        for chip in range(size // 2)
    ]

    def deal(array):
        return lax.all_to_all(
            array, ("groups", "ctx"), 0, 0, axis_index_groups=quads, tiled=True
        )

    def inner_swap(array):
        return lax.ppermute(array, "ctx", [(i, i ^ 2) for i in range(size)])

    def from_behind(array, by, odd_only):
        first = 1 if odd_only else 0
        step = 2 if odd_only else 1
        pairs = [(i, i + by) for i in range(first, size - by, step)]
        return lax.ppermute(array, "ctx", pairs)

    outer_stream, inner_stream, group_stream = Stream(2), Stream(2), Stream(2)
    anywhere = pl.BlockSpec(memory_space=pl.ANY)
    place_info = jnp.stack([mine, group]).astype(jnp.int32)

    width = HQ * (NOPE + VDIM)
    widths = [heads * (NOPE + VDIM) for heads in CHUNK_HEADS]
    outer = size // 4 if size % 4 == 0 and size // 4 <= 4 else 0
    weights = []
    if outer:
        lines = [
            [(z * 2 + y) * 2 + c for z in range(outer) for c in range(2)] for y in range(2)
        ]

        def along(array):
            return lax.all_to_all(array, "ctx", 0, 0, axis_index_groups=lines, tiled=True)

        spread = pl.pallas_call(
            functools.partial(spread_kernel, outer),
            out_shape=[shape((2 * outer * w_up.shape[0], w)) for w in widths],
            in_specs=[smem, anywhere],
            out_specs=[anywhere] * CHUNKS,
            scratch_shapes=[pltpu.SemaphoreType.DMA((2 * outer * CHUNKS,))],
            compiler_params=params,
            name="spread",
        )(place_info, w_up)
        for part in spread:
            line = outer_stream.send(along, part)
            weights.append([line, inner_stream.send(inner_swap, line)])
    else:
        quarter = group * 2 + mine % 2
        keep = lax.dynamic_slice_in_dim(w_up, quarter * width, width, 1)
        got = quad_swap(lax.dynamic_slice_in_dim(w_up, (quarter ^ 1) * width, width, 1), 1)
        even = mine % 2 == 0
        both = jnp.concatenate(
            [jnp.where(even, keep, got), jnp.where(even, got, keep)], axis=0
        )
        same_core = [list(range(c, size, 2)) for c in range(2)]
        for j in range(CHUNKS):
            part = both[:, FIRST_HEAD[j] * 256 : FIRST_HEAD[j] * 256 + widths[j]]
            weights.append(
                [lax.all_gather(part, "ctx", axis=0, tiled=True, axis_index_groups=same_core)]
            )

    frequency = np.exp(-np.arange(ROPE // 2) * (2.0 * math.log(10000.0) / ROPE))
    frequency = jnp.asarray(np.tile(frequency, 4)[None, :], jnp.float32)
    info = jnp.concatenate([mine[None].astype(jnp.int32), lengths.astype(jnp.int32)])
    rows, cosine, sine, outgoing = pl.pallas_call(
        functools.partial(rows_kernel, slot_count),
        out_shape=(
            shape((tok, EXT)),
            shape((tok, 128), jnp.float32),
            shape((tok, 128), jnp.float32),
            shape((size * slot_count, ROW)),
        ),
        in_specs=[smem] + [whole] * 4,
        out_specs=[whole] * 4,
        compiler_params=params,
        name="rows",
    )(info, kv_latent, latent_gain[None, :], page_ranks, frequency)

    queries = pl.pallas_call(
        query_kernel,
        out_shape=[shape((QUAD, tok, h * (NOPE + ROPE))) for h in CHUNK_HEADS],
        in_specs=[whole] * 3,
        out_specs=[whole] * CHUNKS,
        compiler_params=params,
        name="queries",
    )(q_heads, cosine, sine)

    both_groups = jnp.concatenate([rows, quad_swap(rows, 2)], axis=0)
    behind = from_behind(both_groups, 2, False)
    far_behind = from_behind(both_groups, 4, True)
    own_rows = jnp.concatenate([both_groups, behind, far_behind], axis=0)
    other_rows = quad_swap(own_rows, 1)

    moved = [group_stream.send(deal, one) for one in queries]

    outgoing = lax.optimization_barrier((outgoing, moved[0]))[0]
    arrived = lax.all_to_all(
        outgoing.reshape(size, slot_count, ROW), "ctx", split_axis=0, concat_axis=0, tiled=True
    )
    decode_cache = arrived.reshape(size * slot_count, ROW)

    place_info, decode_cache = lax.optimization_barrier((place_info, decode_cache))
    window = (REACH + 2) * tok

    def attend(j):
        heads = CHUNK_HEADS[j]
        steps = heads // 2
        flops = 2 * heads * 2 * (window * LAT * 256 + 2 * tok * window * (NOPE + ROPE + VDIM))
        return pl.pallas_call(
            functools.partial(attend_kernel, outer),
            grid=(steps,),
            out_shape=shape((QUAD, tok, heads * VDIM)),
            in_specs=[
                smem,
                pl.BlockSpec((6 * tok, EXT), lambda i: (0, 0)),
                pl.BlockSpec((6 * tok, EXT), lambda i: (0, 0)),
            ]
            + [pl.BlockSpec((piece.shape[0], 512), lambda i: (0, i)) for piece in weights[j]]
            + [
                pl.BlockSpec((QUAD, tok, 256), lambda i: (0, 0, i)),
                pl.BlockSpec((QUAD, tok, 128), lambda i: (0, 0, heads + i)),
            ],
            out_specs=pl.BlockSpec((QUAD, tok, 256), lambda i: (0, 0, i)),
            scratch_shapes=[
                VMEM((2, window, LAT), jnp.bfloat16),
                VMEM((2, window, 128), jnp.bfloat16),
                VMEM((2, window, 128), jnp.bfloat16),
                VMEM((2, 2 * tok, window), jnp.float32),
                VMEM((LAT, 512), jnp.bfloat16),
            ],
            compiler_params=params,
            cost_estimate=pl.CostEstimate(
                flops=flops,
                bytes_accessed=heads << 20,
                transcendentals=heads * 4 * tok * window,
            ),
            name="attend",
        )(place_info, own_rows, other_rows, *weights[j], moved[j], moved[j])

    pieces = [group_stream.send(deal, attend(j)) for j in range(CHUNKS)]
    attn_out = pl.pallas_call(
        place_kernel,
        out_shape=shape((tok, H * VDIM)),
        in_specs=[anywhere] * CHUNKS,
        out_specs=anywhere,
        scratch_shapes=[pltpu.SemaphoreType.DMA((QUAD * CHUNKS,))],
        compiler_params=params,
        name="place",
    )(*pieces)
    return (attn_out, decode_cache)


def solution(mesh):
    return jax.shard_map(
        body,
        mesh=mesh,
        in_specs=(
            P(("groups", "ctx"), None),
            P(("groups", "ctx"), None),
            P(),
            P("ctx", None),
            P(("groups", "ctx"), None),
            P("groups"),
        ),
        out_specs=(P(("groups", "ctx"), None), P(("groups", "ctx"), None)),
        check_vma=False,
    )
```

time: 162 us -> 241 us (1.49)
  blocking collectives: 0 us -> 36 us
  waiting for transfers between devices: 48.9 us -> 84.8 us
  local copies, waits for them, and re-layouts: 18.9 us -> 23 us
    all_to_all x0 -> x10, waiting for transfers between devices: none -> 52.1 us  [the longest x7 35.4 us: deal(): lax.all_to_all(array, ('groups', 'ctx'), 0, 0, axis_index_groups=quads, t...]
    all_to_all x0 -> x10, starting transfers between devices: none -> 41.8 us  [the longest x7 24.5 us: deal(): lax.all_to_all(array, ('groups', 'ctx'), 0, 0, axis_index_groups=quads, t...]
    all_to_all x0 -> x2, blocking collectives: none -> 36 us  [the longest x1 20.3 us: along(): lax.all_to_all(array, 'ctx', 0, 0, axis_index_groups=lines, tiled=True)]
    ppermute x9 -> x0, waiting for transfers between devices: 24.3 us -> none  [around(): lax.ppermute(array, 'ctx', [(i, (i + by) % size) for i in range(size)])]
    ppermute x9 -> x0, starting transfers between devices: 16.7 us -> none  [around(): lax.ppermute(array, 'ctx', [(i, (i + by) % size) for i in range(size)])]
    ppermute x21 -> x2, waiting for transfers between devices: 14 us -> 0.01 us  [quad_swap(): return lax.ppermute(array, ('groups', 'ctx'), pairs)]
    ppermute x21 -> x2, starting transfers between devices: 17.5 us -> 4.04 us  [quad_swap(): return lax.ppermute(array, ('groups', 'ctx'), pairs)]
    all_to_all x1, waiting for transfers between devices: 0.01 us -> 11.1 us  [body(): lax.all_to_all(outgoing.reshape(size, slot_count, ROW), 'ctx', split_axis...]
  transfers between devices with their start and end apart: 45 -> 19, of which waited for: 11 -> 10; matrix products, arithmetic and copies ran while one was open for 2% -> 2% of each run, Pallas kernels for 20% -> 12%
where the time goes in v3:
time: 241 us; the launch traced here: 239 us
  waiting for transfers between devices  84.8 us (35%)
  starting transfers between devices  57.2 us (24%)
  Pallas kernels  36.5 us (15%)
  blocking collectives  36 us (15%)
  local copies, waits for them, and re-layouts  23 us (10%)
    all_to_all x7, waiting for transfers between devices, deal(): lax.all_to_all(array, ('groups', 'ctx'), 0, 0, axis_index_groups=quads, t...  35.4 us
    pallas_call x4, Pallas kernels, attend(): pl.pallas_call(functools.partial(attend_kernel, outer), grid=(steps,), ou...  28.3 us
    all_to_all x7, starting transfers between devices, deal(): lax.all_to_all(array, ('groups', 'ctx'), 0, 0, axis_index_groups=quads, t...  24.5 us
    unnamed x51, local copies, waits for them, and re-layouts  21.5 us
    all_to_all x1, blocking collectives, along(): lax.all_to_all(array, 'ctx', 0, 0, axis_index_groups=lines, tiled=True)  20.3 us
    all_to_all x3, starting transfers between devices, along(): lax.all_to_all(array, 'ctx', 0, 0, axis_index_groups=lines, tiled=True)  17.2 us
    all_to_all x3, waiting for transfers between devices, along(): lax.all_to_all(array, 'ctx', 0, 0, axis_index_groups=lines, tiled=True)  16.7 us
    all_to_all x1, blocking collectives, deal(): lax.all_to_all(array, ('groups', 'ctx'), 0, 0, axis_index_groups=quads, t...  15.7 us
  transfers between devices with their start and end apart: 19, of which 10 were waited for; matrix products, arithmetic and copies ran while one was open for 2% of the time, Pallas kernels for 12%

profile of v3, /device:TPU:0, one launch (start us, length us, event | category | flops | bytes accessed | tf_op | source)
XLA Modules:
  0.0 239.4 jit_solution(15280336456830137575)
XLA Ops:
  0.6 1.1 copy.12.kv
  1.7 0.8 copy.13.ranks
  2.5 0.7 pad_add_fusion.1.info
  3.2 0.7 copy-done.20
  3.9 0.7 copy-done.21
  4.5 1.9 rows.1
  6.4 3.3 %queries.1 = (bf16[4,128,768]{2,1,0:T(8,128)(2,1)S(1)}, bf16[4,128,768]{2,1,0:T(8,128)(2,1)S(1)}, bf16[4,128,768]{2,1,0:T(8,128)(2,1)S(1)}, bf16[4,128,768]{2,1,0:T(8,128)(2,1)S(1)}) custom-call(bf16[128,12288]{1,0:T(8,128)(2,1)} %query.1, f32[128,128]{1,0:T(8,128)S(1)} %get-tuple-element.28.cosine, f32[128,128]{1,0:T(8,128)S(1)} %get-tuple-element.29.sine), custom_call_target="tpu_custom_call" | custom-call | tf_op jit(solution)/shard_map/queries/pallas_call | solution.py:349
  9.7 0.9 copy-done.3
  10.6 0.9 copy-done.4
  11.5 15.7 %all_to_all.89.refs_2_.refs_3_ = bf16[4,128,768]{2,1,0:T(8,128)(2,1)S(1)} all-to-all(bf16[4,128,768]{2,1,0:T(8,128)(2,1)S(1)} %get-tuple-element.39), channel_id=1, replica_groups={{0,1,16,17},{2,3,18,19},{4,5,20,21},{6,7,22,23},{8,9,24,25},{10,11,26,2..., dimensions={0} | all-to-all | bytes 1572864 | tf_op jit(solution)/shard_map/all_to_all | solution.py:276
  27.2 3.5 %all-to-all-start = ((bf16[4,128,768]{2,1,0:T(8,128)(2,1)}), bf16[4,128,768]{2,1,0:T(8,128)(2,1)S(1)}, u32[]{:S(2)}, u32[]{:S(2)}) async-start(bf16[4,128,768]{2,1,0:T(8,128)(2,1)} %copy-done.5), calls=%async_computation | async-start | bytes 1572864 | tf_op jit(solution)/shard_map/all_to_all | solution.py:276
  30.8 1.7 spread.1
  32.4 0.8 copy-done.8
  33.2 0.8 copy-done.10
  34.0 0.8 copy-done.15
  34.8 7.5 %all-to-all-done.refs_2_.refs_3_ = bf16[4,128,768]{2,1,0:T(8,128)(2,1)S(1)} async-done(((bf16[4,128,768]{2,1,0:T(8,128)(2,1)}), bf16[4,128,768]{2,1,0:T(8,128)(2,1)S(1)}, u32[]{:S(2)}, u32[]{:S(2)}) %all-to-all-start) | async-done | bytes 786464 | tf_op jit(solution)/shard_map/all_to_all | solution.py:276
  42.3 20.3 %all_to_all.90 = bf16[8,32,1024]{2,1,0:T(8,128)(2,1)} all-to-all(bf16[8,32,1024]{2,1,0:T(8,128)(2,1)} %bitcast.19), channel_id=1, replica_groups={{0,1,4,5,8,9,12,13},{2,3,6,7,10,11,14,15},{16,17,20,21,24,25,28,29},{18..., dimensions={0} | all-to-all | bytes 1048576 | tf_op jit(solution)/shard_map/all_to_all | solution.py:303
  62.6 3.5 %all-to-all-start.2 = ((bf16[8,32,1024]{2,1,0:T(8,128)(2,1)}), bf16[8,32,1024]{2,1,0:T(8,128)(2,1)S(1)}, u32[]{:S(2)}, u32[]{:S(2)}) async-start(bf16[8,32,1024]{2,1,0:T(8,128)(2,1)} %bitcast.5), calls=%async_computation.2 | async-start | bytes 1048576 | tf_op jit(solution)/shard_map/all_to_all | solution.py:303
  66.1 15.3 %all-to-all-done.2 = bf16[8,32,1024]{2,1,0:T(8,128)(2,1)S(1)} async-done(((bf16[8,32,1024]{2,1,0:T(8,128)(2,1)}), bf16[8,32,1024]{2,1,0:T(8,128)(2,1)S(1)}, u32[]{:S(2)}, u32[]{:S(2)}) %all-to-all-start.2) | async-done | bytes 524320 | tf_op jit(solution)/shard_map/all_to_all | solution.py:303
  81.4 3.6 %all-to-all-start.1 = ((bf16[16,16,576]{2,1,0:T(8,128)(2,1)}), bf16[16,16,576]{2,1,0:T(8,128)(2,1)S(1)}, u32[]{:S(2)}, u32[]{:S(2)}) async-start(bf16[16,16,576]{2,1,0:T(8,128)(2,1)} %bitcast.3), calls=%async_computation.1 | async-start | bytes 655360 | tf_op jit(solution)/shard_map/all_to_all | solution.py:367
  85.0 11.1 %all-to-all-done.1 = bf16[16,16,576]{2,1,0:T(8,128)(2,1)S(1)} async-done(((bf16[16,16,576]{2,1,0:T(8,128)(2,1)}), bf16[16,16,576]{2,1,0:T(8,128)(2,1)S(1)}, u32[]{:S(2)}, u32[]{:S(2)}) %all-to-all-start.1) | async-done | bytes 294944 | tf_op jit(solution)/shard_map/all_to_all | solution.py:367
  96.1 0.7 copy-done.22
  96.8 3.5 %all-to-all-start.7 = ((bf16[4,128,768]{2,1,0:T(8,128)(2,1)}), bf16[4,128,768]{2,1,0:T(8,128)(2,1)S(1)}, u32[]{:S(2)}, u32[]{:S(2)}) async-start(bf16[4,128,768]{2,1,0:T(8,128)(2,1)} %copy-done.4), calls=%async_computation.7 | async-start | bytes 1572864 | tf_op jit(solution)/shard_map/all_to_all | solution.py:276
  100.3 11.6 %all-to-all-done.7.refs_2_.refs_3_ = bf16[4,128,768]{2,1,0:T(8,128)(2,1)S(1)} async-done(((bf16[4,128,768]{2,1,0:T(8,128)(2,1)}), bf16[4,128,768]{2,1,0:T(8,128)(2,1)S(1)}, u32[]{:S(2)}, u32[]{:S(2)}) %all-to-all-start.7) | async-done | bytes 786464 | tf_op jit(solution)/shard_map/all_to_all | solution.py:276
  112.0 3.5 %all-to-all-start.3 = ((bf16[4,128,768]{2,1,0:T(8,128)(2,1)}), bf16[4,128,768]{2,1,0:T(8,128)(2,1)S(1)}, u32[]{:S(2)}, u32[]{:S(2)}) async-start(bf16[4,128,768]{2,1,0:T(8,128)(2,1)} %copy-done.3), calls=%async_computation.3 | async-start | bytes 1572864 | tf_op jit(solution)/shard_map/all_to_all | solution.py:276
  115.5 2.0 collective-permute-start
  117.4 0.7 constant_dynamic-update-slice_fusion.1
  118.2 9.4 %all-to-all-done.3.refs_2_.refs_3_ = bf16[4,128,768]{2,1,0:T(8,128)(2,1)S(1)} async-done(((bf16[4,128,768]{2,1,0:T(8,128)(2,1)}), bf16[4,128,768]{2,1,0:T(8,128)(2,1)S(1)}, u32[]{:S(2)}, u32[]{:S(2)}) %all-to-all-start.3) | async-done | bytes 786464 | tf_op jit(solution)/shard_map/all_to_all | solution.py:276
  127.5 4.1 %all-to-all-start.11 = ((bf16[8,32,1024]{2,1,0:T(8,128)(2,1)}), bf16[8,32,1024]{2,1,0:T(8,128)(2,1)}, u32[]{:S(2)}, u32[]{:S(2)}) async-start(bf16[8,32,1024]{2,1,0:T(8,128)(2,1)} %bitcast.18), calls=%async_computation.11 | async-start | bytes 1048576 | tf_op jit(solution)/shard_map/all_to_all | solution.py:303
  131.7 0.8 constant_dynamic-update-slice_fusion
  132.5 1.8 collective-permute-start.1
  134.3 0.7 collective-permute-start.2
  135.0 7.1 %collective-permute-done.1 = bf16[256,640]{1,0:T(8,128)(2,1)S(1)} collective-permute-done((bf16[256,640]{1,0:T(8,128)(2,1)}, bf16[256,640]{1,0:T(8,128)(2,1)S(1)}, u32[]{:S(2)}, u32[]{:S(2)}) %collective-permute-start.1) | collective-permute-done | bytes 327712 | tf_op jit(solution)/shard_map/ppermute | solution.py:287
  142.1 0.8 constant_dynamic-update-slice_fusion.3
  142.8 0.8 constant_dynamic-update-slice_fusion.2.own
  143.6 2.1 collective-permute-start.3
  145.6 1.4 all-to-all-done.11
  147.1 9.6 %all-to-all-start.9 = ((bf16[8,32,1024]{2,1,0:T(8,128)(2,1)}), bf16[8,32,1024]{2,1,0:T(8,128)(2,1)}, u32[]{:S(2)}, u32[]{:S(2)}) async-start(bf16[8,32,1024]{2,1,0:T(8,128)(2,1)} %bitcast.15), calls=%async_computation.9 | async-start | bytes 1048576 | tf_op jit(solution)/shard_map/all_to_all | solution.py:303
  156.7 3.0 %collective-permute-start.5 = (bf16[256,1024]{1,0:T(8,128)(2,1)}, bf16[256,1024]{1,0:T(8,128)(2,1)S(1)}, u32[]{:S(2)}, u32[]{:S(2)}) collective-permute-start(bf16[256,1024]{1,0:T(8,128)(2,1)} %bitcast.16), channel_id=1, source_target_pairs={{0,2},{1,3},{2,0},{3,1},{4,6},{5,7},{6,4},{7,5},{8,10},{9,11},{10,... | collective-permute-start | bytes 1572872 | tf_op jit(solution)/shard_map/ppermute | solution.py:281
  159.7 12.9 %collective-permute-done.5.refs_1_ = bf16[256,1024]{1,0:T(8,128)(2,1)S(1)} collective-permute-done((bf16[256,1024]{1,0:T(8,128)(2,1)}, bf16[256,1024]{1,0:T(8,128)(2,1)S(1)}, u32[]{:S(2)}, u32[]{:S(2)}) %collective-permute-start.5) | collective-permute-done | bytes 524320 | tf_op jit(solution)/shard_map/ppermute | solution.py:281
  172.6 1.0 copy-done.9
  173.7 1.2 copy-done.16
  174.9 7.0 %attend.5 = bf16[4,128,512]{2,1,0:T(8,128)(2,1)S(1)} custom-call(s32[2]{0:T(128)S(1)} %pad_add_fusion.info, bf16[768,640]{1,0:T(8,128)(2,1)S(1)} %copy-done.16, bf16[768,640]{1,0:T(8,128)(2,1)} %collective-permute-done.3.other, bf16[256,1024]{1,0:T(8,128)(2,1)S(1)} %bitcast.17, bf16[256,1024]{1,0:T(8,128)(2,1)S(1)} %collective-permute-done.5.refs_1_, ...), custom_call_target="tpu_custom_call" | custom-call | flops 2181038080 | bytes 4194304 | tf_op jit(solution)/shard_map/attend/pallas_call | solution.py:379
  181.9 0.8 copy-done.11
  182.7 3.5 %all-to-all-start.8 = ((bf16[4,128,512]{2,1,0:T(8,128)(2,1)}), bf16[4,128,512]{2,1,0:T(8,128)(2,1)S(1)}, u32[]{:S(2)}, u32[]{:S(2)}) async-start(bf16[4,128,512]{2,1,0:T(8,128)(2,1)} %copy-done.11), calls=%async_computation.8 | async-start | bytes 1048576 | tf_op jit(solution)/shard_map/all_to_all | solution.py:276
  186.2 2.0 collective-permute-start.7
  188.2 1.0 copy-done.7
  189.2 1.2 copy-done.17
  190.4 7.0 %attend.4 = bf16[4,128,512]{2,1,0:T(8,128)(2,1)S(1)} custom-call(s32[2]{0:T(128)S(1)} %pad_add_fusion.info, bf16[768,640]{1,0:T(8,128)(2,1)S(1)} %copy-done.17, bf16[768,640]{1,0:T(8,128)(2,1)} %collective-permute-done.3.other, bf16[256,1024]{1,0:T(8,128)(2,1)S(1)} %bitcast.14, bf16[256,1024]{1,0:T(8,128)(2,1)} %collective-permute-done.4.refs_1_, ...), custom_call_target="tpu_custom_call" | custom-call | flops 2181038080 | bytes 4194304 | tf_op jit(solution)/shard_map/attend/pallas_call | solution.py:379
  197.5 0.8 copy-done.12
  198.3 3.7 %all-to-all-start.4 = ((bf16[4,128,512]{2,1,0:T(8,128)(2,1)}), bf16[4,128,512]{2,1,0:T(8,128)(2,1)S(1)}, u32[]{:S(2)}, u32[]{:S(2)}) async-start(bf16[4,128,512]{2,1,0:T(8,128)(2,1)} %copy-done.12), calls=%async_computation.4 | async-start | bytes 1048576 | tf_op jit(solution)/shard_map/all_to_all | solution.py:276
  201.9 0.2 collective-permute-start.6
  202.2 1.2 copy-done.18
  203.4 7.1 %attend.7 = bf16[4,128,512]{2,1,0:T(8,128)(2,1)S(1)} custom-call(s32[2]{0:T(128)S(1)} %pad_add_fusion.info, bf16[768,640]{1,0:T(8,128)(2,1)S(1)} %copy-done.18, bf16[768,640]{1,0:T(8,128)(2,1)} %collective-permute-done.3.other, bf16[256,1024]{1,0:T(8,128)(2,1)} %bitcast.12.refs_0_, bf16[256,1024]{1,0:T(8,128)(2,1)} %collective-permute-done.7.refs_1_, ...), custom_call_target="tpu_custom_call" | custom-call | flops 2181038080 | bytes 4194304 | tf_op jit(solution)/shard_map/attend/pallas_call | solution.py:379
  210.5 0.8 copy-done.13
  211.3 3.5 %all-to-all-start.12 = ((bf16[4,128,512]{2,1,0:T(8,128)(2,1)}), bf16[4,128,512]{2,1,0:T(8,128)(2,1)S(1)}, u32[]{:S(2)}, u32[]{:S(2)}) async-start(bf16[4,128,512]{2,1,0:T(8,128)(2,1)} %copy-done.13), calls=%async_computation.12 | async-start | bytes 1048576 | tf_op jit(solution)/shard_map/all_to_all | solution.py:276
  214.8 1.6 collective-permute-done.6.refs_1_
  216.4 1.2 copy-done.19
  217.6 7.1 %attend.6 = bf16[4,128,512]{2,1,0:T(8,128)(2,1)S(1)} custom-call(s32[2]{0:T(128)S(1)} %pad_add_fusion.info, bf16[768,640]{1,0:T(8,128)(2,1)S(1)} %copy-done.19, bf16[768,640]{1,0:T(8,128)(2,1)} %collective-permute-done.3.other, bf16[256,1024]{1,0:T(8,128)(2,1)} %bitcast.10.refs_0_, bf16[256,1024]{1,0:T(8,128)(2,1)} %collective-permute-done.6.refs_1_, ...), custom_call_target="tpu_custom_call" | custom-call | flops 2181038080 | bytes 4194304 | tf_op jit(solution)/shard_map/attend/pallas_call | solution.py:379
  224.7 0.8 copy-done.14
  225.5 3.5 %all-to-all-start.10 = ((bf16[4,128,512]{2,1,0:T(8,128)(2,1)}), bf16[4,128,512]{2,1,0:T(8,128)(2,1)S(1)}, u32[]{:S(2)}, u32[]{:S(2)}) async-start(bf16[4,128,512]{2,1,0:T(8,128)(2,1)} %copy-done.14), calls=%async_computation.10 | async-start | bytes 1048576 | tf_op jit(solution)/shard_map/all_to_all | solution.py:276
  229.0 1.8 copy.14
  230.8 7.0 %all-to-all-done.10.refs_2_ = bf16[4,128,512]{2,1,0:T(8,128)(2,1)S(1)} async-done(((bf16[4,128,512]{2,1,0:T(8,128)(2,1)}), bf16[4,128,512]{2,1,0:T(8,128)(2,1)S(1)}, u32[]{:S(2)}, u32[]{:S(2)}) %all-to-all-start.10) | async-done | bytes 524320 | tf_op jit(solution)/shard_map/all_to_all | solution.py:276
  237.8 1.4 place.1
  (39 shorter events, 0.2 us)
Async XLA Ops:
  3.2 0.7 copy-start.20
  3.9 0.7 copy-start.21
  6.4 24.3 %copy-start = (bf16[32,16384]{1,0:T(8,128)(2,1)S(1)}, bf16[32,16384]{1,0:T(8,128)(2,1)}, u32[]{:S(2)}) copy-start(bf16[32,16384]{1,0:T(8,128)(2,1)} %w_up.1) | copy-start | bytes 3145732
  9.7 0.9 copy-start.3
  10.6 0.9 copy-start.4
  11.5 15.7 %copy-start.5 = (bf16[4,128,768]{2,1,0:T(8,128)(2,1)}, bf16[4,128,768]{2,1,0:T(8,128)(2,1)S(1)}, u32[]{:S(2)}) copy-start(bf16[4,128,768]{2,1,0:T(8,128)(2,1)S(1)} %get-tuple-element.30) | copy-start | bytes 2359300
  27.2 15.1 %all-to-all-start = ((bf16[4,128,768]{2,1,0:T(8,128)(2,1)}), bf16[4,128,768]{2,1,0:T(8,128)(2,1)S(1)}, u32[]{:S(2)}, u32[]{:S(2)}) async-start(bf16[4,128,768]{2,1,0:T(8,128)(2,1)} %copy-done.5), calls=%async_computation | async-start | bytes 1572864 | tf_op jit(solution)/shard_map/all_to_all | solution.py:276
  32.4 0.8 copy-start.8
  33.2 0.8 copy-start.10
  34.0 0.8 copy-start.15
  62.6 18.8 %all-to-all-start.2 = ((bf16[8,32,1024]{2,1,0:T(8,128)(2,1)}), bf16[8,32,1024]{2,1,0:T(8,128)(2,1)S(1)}, u32[]{:S(2)}, u32[]{:S(2)}) async-start(bf16[8,32,1024]{2,1,0:T(8,128)(2,1)} %bitcast.5), calls=%async_computation.2 | async-start | bytes 1048576 | tf_op jit(solution)/shard_map/all_to_all | solution.py:303
  81.4 30.5 %copy-start.6 = (bf16[8,32,1024]{2,1,0:T(8,128)(2,1)}, bf16[8,32,1024]{2,1,0:T(8,128)(2,1)S(1)}, u32[]{:S(2)}) copy-start(bf16[8,32,1024]{2,1,0:T(8,128)(2,1)S(1)} %all-to-all-done.2) | copy-start | bytes 1572868
  81.4 14.7 %all-to-all-start.1 = ((bf16[16,16,576]{2,1,0:T(8,128)(2,1)}), bf16[16,16,576]{2,1,0:T(8,128)(2,1)S(1)}, u32[]{:S(2)}, u32[]{:S(2)}) async-start(bf16[16,16,576]{2,1,0:T(8,128)(2,1)} %bitcast.3), calls=%async_computation.1 | async-start | bytes 655360 | tf_op jit(solution)/shard_map/all_to_all | solution.py:367
  96.1 0.7 copy-start.22
  96.8 15.1 %all-to-all-start.7 = ((bf16[4,128,768]{2,1,0:T(8,128)(2,1)}), bf16[4,128,768]{2,1,0:T(8,128)(2,1)S(1)}, u32[]{:S(2)}, u32[]{:S(2)}) async-start(bf16[4,128,768]{2,1,0:T(8,128)(2,1)} %copy-done.4), calls=%async_computation.7 | async-start | bytes 1572864 | tf_op jit(solution)/shard_map/all_to_all | solution.py:276
  111.9 69.9 %copy-start.1 = (bf16[4,128,768]{2,1,0:T(8,128)(2,1)}, bf16[4,128,768]{2,1,0:T(8,128)(2,1)S(1)}, u32[]{:S(2)}) copy-start(bf16[4,128,768]{2,1,0:T(8,128)(2,1)S(1)} %all-to-all-done.7.refs_2_.refs_3_) | copy-start | bytes 2359300
  112.0 15.6 %all-to-all-start.3 = ((bf16[4,128,768]{2,1,0:T(8,128)(2,1)}), bf16[4,128,768]{2,1,0:T(8,128)(2,1)S(1)}, u32[]{:S(2)}, u32[]{:S(2)}) async-start(bf16[4,128,768]{2,1,0:T(8,128)(2,1)} %copy-done.3), calls=%async_computation.3 | async-start | bytes 1572864 | tf_op jit(solution)/shard_map/all_to_all | solution.py:276
  115.5 16.2 %collective-permute-start = (bf16[128,640]{1,0:T(8,128)(2,1)S(1)}, bf16[128,640]{1,0:T(8,128)(2,1)S(1)}, u32[]{:S(2)}, u32[]{:S(2)}) collective-permute-start(bf16[128,640]{1,0:T(8,128)(2,1)S(1)} %get-tuple-element.33), channel_id=1, source_target_pairs={{0,16},{1,17},{2,18},{3,19},{4,20},{5,21},{6,22},{7,23},{8,24},{9,... | collective-permute-start | bytes 491528 | tf_op jit(solution)/shard_map/ppermute | solution.py:268
  127.5 19.5 %all-to-all-start.11 = ((bf16[8,32,1024]{2,1,0:T(8,128)(2,1)}), bf16[8,32,1024]{2,1,0:T(8,128)(2,1)}, u32[]{:S(2)}, u32[]{:S(2)}) async-start(bf16[8,32,1024]{2,1,0:T(8,128)(2,1)} %bitcast.18), calls=%async_computation.11 | async-start | bytes 1048576 | tf_op jit(solution)/shard_map/all_to_all | solution.py:303
  132.5 9.6 %collective-permute-start.1 = (bf16[256,640]{1,0:T(8,128)(2,1)}, bf16[256,640]{1,0:T(8,128)(2,1)S(1)}, u32[]{:S(2)}, u32[]{:S(2)}) collective-permute-start(bf16[256,640]{1,0:T(8,128)(2,1)} %get-tuple-element.54), channel_id=1, source_target_pairs={{0,2},{1,3},{2,4},{3,5},{4,6},{5,7},{6,8},{7,9},{8,10},{9,11},{10,... | collective-permute-start | bytes 983048 | tf_op jit(solution)/shard_map/ppermute | solution.py:287
  134.3 8.5 %collective-permute-start.2 = (bf16[256,640]{1,0:T(8,128)(2,1)}, bf16[256,640]{1,0:T(8,128)(2,1)S(1)}, u32[]{:S(2)}, u32[]{:S(2)}) collective-permute-start(bf16[256,640]{1,0:T(8,128)(2,1)} %get-tuple-element.54), channel_id=1, source_target_pairs={{1,5},{3,7},{5,9},{7,11},{9,13},{11,15},{17,21},{19,23},{21,25},{2... | collective-permute-start | bytes 983048 | tf_op jit(solution)/shard_map/ppermute | solution.py:287
  143.6 29.0 %collective-permute-start.3 = (bf16[768,640]{1,0:T(8,128)(2,1)}, bf16[768,640]{1,0:T(8,128)(2,1)}, u32[]{:S(2)}, u32[]{:S(2)}) collective-permute-start(bf16[768,640]{1,0:T(8,128)(2,1)} %constant_dynamic-update-slice_fusion.2.own), channel_id=1, source_target_pairs={{0,1},{1,0},{2,3},{3,2},{4,5},{5,4},{6,7},{7,6},{8,9},{9,8},{10,11... | collective-permute-start | bytes 2949128 | tf_op jit(solution)/shard_map/ppermute | solution.py:268
  147.1 35.7 %all-to-all-start.9 = ((bf16[8,32,1024]{2,1,0:T(8,128)(2,1)}), bf16[8,32,1024]{2,1,0:T(8,128)(2,1)}, u32[]{:S(2)}, u32[]{:S(2)}) async-start(bf16[8,32,1024]{2,1,0:T(8,128)(2,1)} %bitcast.15), calls=%async_computation.9 | async-start | bytes 1048576 | tf_op jit(solution)/shard_map/all_to_all | solution.py:303
  156.7 16.0 %collective-permute-start.5 = (bf16[256,1024]{1,0:T(8,128)(2,1)}, bf16[256,1024]{1,0:T(8,128)(2,1)S(1)}, u32[]{:S(2)}, u32[]{:S(2)}) collective-permute-start(bf16[256,1024]{1,0:T(8,128)(2,1)} %bitcast.16), channel_id=1, source_target_pairs={{0,2},{1,3},{2,0},{3,1},{4,6},{5,7},{6,4},{7,5},{8,10},{9,11},{10,... | collective-permute-start | bytes 1572872 | tf_op jit(solution)/shard_map/ppermute | solution.py:281
  159.6 28.6 %collective-permute-start.4 = (bf16[256,1024]{1,0:T(8,128)(2,1)}, bf16[256,1024]{1,0:T(8,128)(2,1)}, u32[]{:S(2)}, u32[]{:S(2)}) collective-permute-start(bf16[256,1024]{1,0:T(8,128)(2,1)} %bitcast.13), channel_id=1, source_target_pairs={{0,2},{1,3},{2,0},{3,1},{4,6},{5,7},{6,4},{7,5},{8,10},{9,11},{10,... | collective-permute-start | bytes 1572872 | tf_op jit(solution)/shard_map/ppermute | solution.py:281
  172.6 1.0 copy-start.9
  173.7 1.2 copy-start.16
  181.9 0.8 copy-start.11
  182.7 15.6 %all-to-all-start.8 = ((bf16[4,128,512]{2,1,0:T(8,128)(2,1)}), bf16[4,128,512]{2,1,0:T(8,128)(2,1)S(1)}, u32[]{:S(2)}, u32[]{:S(2)}) async-start(bf16[4,128,512]{2,1,0:T(8,128)(2,1)} %copy-done.11), calls=%async_computation.8 | async-start | bytes 1048576 | tf_op jit(solution)/shard_map/all_to_all | solution.py:276
  186.2 16.0 %copy-start.2 = (bf16[4,128,768]{2,1,0:T(8,128)(2,1)S(1)}, bf16[4,128,768]{2,1,0:T(8,128)(2,1)}, u32[]{:S(2)}) copy-start(bf16[4,128,768]{2,1,0:T(8,128)(2,1)} %copy-done.1) | copy-start | bytes 2359300
  186.2 16.0 %collective-permute-start.7 = (bf16[256,1024]{1,0:T(8,128)(2,1)}, bf16[256,1024]{1,0:T(8,128)(2,1)}, u32[]{:S(2)}, u32[]{:S(2)}) collective-permute-start(bf16[256,1024]{1,0:T(8,128)(2,1)} %bitcast.12.refs_0_), channel_id=1, source_target_pairs={{0,2},{1,3},{2,0},{3,1},{4,6},{5,7},{6,4},{7,5},{8,10},{9,11},{10,... | collective-permute-start | bytes 1572872 | tf_op jit(solution)/shard_map/ppermute | solution.py:281
  188.2 1.0 copy-start.7
  189.2 1.2 copy-start.17
  197.5 0.8 copy-start.12
  198.3 13.0 %all-to-all-start.4 = ((bf16[4,128,512]{2,1,0:T(8,128)(2,1)}), bf16[4,128,512]{2,1,0:T(8,128)(2,1)S(1)}, u32[]{:S(2)}, u32[]{:S(2)}) async-start(bf16[4,128,512]{2,1,0:T(8,128)(2,1)} %copy-done.12), calls=%async_computation.4 | async-start | bytes 1048576 | tf_op jit(solution)/shard_map/all_to_all | solution.py:276
  201.9 14.4 %collective-permute-start.6 = (bf16[256,1024]{1,0:T(8,128)(2,1)}, bf16[256,1024]{1,0:T(8,128)(2,1)}, u32[]{:S(2)}, u32[]{:S(2)}) collective-permute-start(bf16[256,1024]{1,0:T(8,128)(2,1)} %bitcast.10.refs_0_), channel_id=1, source_target_pairs={{0,2},{1,3},{2,0},{3,1},{4,6},{5,7},{6,4},{7,5},{8,10},{9,11},{10,... | collective-permute-start | bytes 1572872 | tf_op jit(solution)/shard_map/ppermute | solution.py:281
  202.2 1.2 copy-start.18
  210.5 0.8 copy-start.13
  211.3 14.2 %all-to-all-start.12 = ((bf16[4,128,512]{2,1,0:T(8,128)(2,1)}), bf16[4,128,512]{2,1,0:T(8,128)(2,1)S(1)}, u32[]{:S(2)}, u32[]{:S(2)}) async-start(bf16[4,128,512]{2,1,0:T(8,128)(2,1)} %copy-done.13), calls=%async_computation.12 | async-start | bytes 1048576 | tf_op jit(solution)/shard_map/all_to_all | solution.py:276
  216.4 1.2 copy-start.19
  224.7 0.8 copy-start.14
  225.5 12.3 %all-to-all-start.10 = ((bf16[4,128,512]{2,1,0:T(8,128)(2,1)}), bf16[4,128,512]{2,1,0:T(8,128)(2,1)S(1)}, u32[]{:S(2)}, u32[]{:S(2)}) async-start(bf16[4,128,512]{2,1,0:T(8,128)(2,1)} %copy-done.14), calls=%async_computation.10 | async-start | bytes 1048576 | tf_op jit(solution)/shard_map/all_to_all | solution.py:276

commit v4 on v2

--- a/solution.py
+++ b/solution.py
@@ -17,33 +17,36 @@
 REACH = 3
 QUAD = 4
 HQ = H // QUAD
-CHUNK_HEADS = (8, 4, 4)
+CHUNK_HEADS = (8, 8)
 CHUNKS = len(CHUNK_HEADS)
 FIRST_HEAD = tuple(sum(CHUNK_HEADS[:j]) for j in range(CHUNKS))
 ROW = LAT + ROPE
 EXT = 640
-VMEM_LIMIT = 48 * 1024 * 1024
+VMEM_LIMIT = 20 * 1024 * 1024
+CALLS = ((0, 0, 2), (0, 2, 2), (1, 0, 2), (1, 2, 2))
 SMEM = pltpu.SMEM
 VMEM = pltpu.VMEM
 
 
-def rows_kernel(slot_count, info, kv, gain, ranks, freq, rows_out, cos_out, sin_out, outgoing_out):
-    tok = kv.shape[0]
+def rows_kernel(
+    slot_count, info, lengths, kv, gain, ranks, freq, rows_out, cos_out, sin_out, outgoing_out
+):
+    tok = kv.shape[1]
     base = info[0] * tok
     spots = base + lax.broadcasted_iota(jnp.int32, (tok, 128), 0)
     lane = lax.broadcasted_iota(jnp.int32, (tok, 128), 1)
     begin = jnp.int32(0)
     own_start = jnp.zeros((tok, 128), jnp.int32)
-    for r in range(info.shape[0] - 1):
+    for r in range(lengths.shape[0]):
         own_start = jnp.where(spots >= begin, begin, own_start)
-        begin = begin + info[1 + r]
+        begin = begin + lengths[r]
     offset = spots - own_start
     angles = offset.astype(jnp.float32) * freq[...]
     cosine = jnp.cos(angles)
     sine = jnp.where((lane & 32) == 0, -jnp.sin(angles), jnp.sin(angles))
     cos_out[...] = cosine
     sin_out[...] = sine
-    raw = kv[...].astype(jnp.float32)
+    raw = kv[...].astype(jnp.float32).T
     latent = raw[:, :LAT]
     mean = jnp.sum(latent * latent, axis=1, keepdims=True) * (1.0 / LAT)
     latent = latent * lax.rsqrt(mean + 1e-06) * gain[...]
@@ -57,8 +60,8 @@
     rows_out[:, :LAT] = latent.astype(jnp.bfloat16)
     rows_out[:, LAT:] = tail.astype(jnp.bfloat16)
 
-    rank_col = jnp.broadcast_to(ranks[...], (tok, tok)).astype(jnp.float32)
-    rank_row = rank_col.T
+    rank_row = jnp.broadcast_to(ranks[...], (tok, tok)).astype(jnp.float32)
+    rank_col = rank_row.T
     earlier = lax.broadcasted_iota(jnp.int32, (tok, tok), 0) < lax.broadcasted_iota(
         jnp.int32, (tok, tok), 1
     )
@@ -217,8 +220,8 @@
     pieces, out, sems = refs[:-2], refs[-2], refs[-1]
     copies = []
     for i, piece in enumerate(pieces):
-        r, j = i // CHUNKS, i % CHUNKS
-        begin = (info[0] ^ r) * (HQ * VDIM) + FIRST_HEAD[j] * VDIM
+        r, (j, first, steps) = i // len(CALLS), CALLS[i % len(CALLS)]
+        begin = ((info[0] ^ r) * HQ + FIRST_HEAD[j] + 2 * first) * VDIM
         begin = pl.multiple_of(begin, 128)
         copies.append(
             pltpu.make_async_copy(piece, out.at[:, pl.ds(begin, piece.shape[1])], sems.at[i])
@@ -229,6 +232,10 @@
         copy.wait()
 
 
+def tie(array, *others):
+    return lax.optimization_barrier((array,) + others)[0]
+
+
 class Stream:
     def __init__(self, window):
         self.window = window
@@ -237,7 +244,7 @@
     def after(self, array):
         if len(self.arrived) < self.window:
             return array
-        return lax.optimization_barrier((array, self.arrived[-self.window]))[0]
+        return tie(array, self.arrived[-self.window])
 
     def send(self, permute, array, *args):
         self.arrived.append(permute(self.after(array), *args))
@@ -256,8 +263,8 @@
     quarter = lax.axis_index("groups") * 2 + mine % 2
     slot_count = max(2, 2 * tok // size)
     smem = pl.BlockSpec(memory_space=SMEM)
-    whole = pl.BlockSpec(memory_space=VMEM)
     params = pltpu.CompilerParams(vmem_limit_bytes=VMEM_LIMIT)
+    alone = pltpu.CompilerParams(vmem_limit_bytes=3 * VMEM_LIMIT)
 
     def quad_swap(array, r):
         dx, dc = r // 2, r % 2
@@ -267,6 +274,8 @@
         return lax.ppermute(array, ("groups", "ctx"), pairs)
 
     def send_in_quad(array, r):
+        if r == 1 and len(group_stream.arrived) < 4:
+            array = tie(array, weights[0][outer if outer else 0])
         return quad_swap(array, r) if r == 1 else group_stream.send(quad_swap, array, r)
 
     def around(array, by):
@@ -274,6 +283,24 @@
 
     def inner_swap(array):
         return lax.ppermute(array, "ctx", [(i, i ^ 2) for i in range(size)])
+
+    def along_and_across(pieces):
+        count = len(pieces)
+        turns = [(k - j, j) for k in range(outer + count) for j in range(count)]
+        lines = [[piece] for piece in pieces]
+        sides = [[] for piece in pieces]
+        outer_done, inner_done = [], []
+        for k, j in turns:
+            if not 0 <= k < outer:
+                continue
+            if k:
+                at = len(outer_done)
+                before = outer_done[-2:-1] + ([inner_done[max(0, at - 2)]] if at else [])
+                outer_done.append(around(tie(lines[j][-1], *before), 4))
+                lines[j].append(outer_done[-1])
+            sides[j].append(inner_swap(tie(lines[j][k], *inner_done[-2:-1])))
+            inner_done.append(sides[j][-1])
+        return [line + side for line, side in zip(lines, sides)]
 
     def from_behind(array, by, odd_only):
         first = 1 if odd_only else 0
@@ -281,12 +308,13 @@
         pairs = [(i, i + by) for i in range(first, size - by, step)]
         return lax.ppermute(array, "ctx", pairs)
 
-    outer_stream, inner_stream, group_stream = Stream(3), Stream(2), Stream(2)
+    group_stream = Stream(2)
 
     width = HQ * (NOPE + VDIM)
     quarter_info = quarter[None].astype(jnp.int32)
     anywhere = pl.BlockSpec(memory_space=pl.ANY)
     give = lax.dynamic_slice_in_dim(w_up, (quarter ^ 1) * width, width, 1)
+    give, lengths = lax.optimization_barrier((give, lengths))
     got = quad_swap(give, 1)
     widths = [heads * (NOPE + VDIM) for heads in CHUNK_HEADS]
     outer = size // 4 if size % 4 == 0 and size // 4 <= 4 else 0
@@ -294,16 +322,13 @@
         pairs_of_rows = pl.pallas_call(
             pair_kernel,
             out_shape=[shape((2 * w_up.shape[0], w)) for w in widths],
-            in_specs=[smem, anywhere, anywhere],
+            in_specs=[smem, pl.BlockSpec(memory_space=pltpu.HBM), anywhere],
             out_specs=[anywhere] * CHUNKS,
             scratch_shapes=[pltpu.SemaphoreType.DMA((2 * CHUNKS,))],
             compiler_params=params,
             name="pair",
         )(quarter_info, w_up, got)
-        weights = []
-        for piece in pairs_of_rows:
-            line = [piece] + [outer_stream.send(around, piece, 4 * k) for k in range(1, outer)]
-            weights.append(line + [inner_stream.send(inner_swap, one) for one in line])
+        weights = along_and_across(pairs_of_rows)
     else:
         keep = lax.dynamic_slice_in_dim(w_up, quarter * width, width, 1)
         even = mine % 2 == 0
@@ -326,26 +351,37 @@
 
     frequency = np.exp(-np.arange(ROPE // 2) * (2.0 * math.log(10000.0) / ROPE))
     frequency = jnp.asarray(np.tile(frequency, 4)[None, :], jnp.float32)
-    info = jnp.concatenate([mine[None].astype(jnp.int32), lengths.astype(jnp.int32)])
+    mine_info = mine[None].astype(jnp.int32)
+
+    def block(*dims):
+        return pl.BlockSpec(dims, lambda i: (0,) * len(dims))
+
     rows, cosine, sine, outgoing = pl.pallas_call(
         functools.partial(rows_kernel, slot_count),
+        grid=(1,),
         out_shape=(
             shape((tok, EXT)),
             shape((tok, 128), jnp.float32),
             shape((tok, 128), jnp.float32),
             shape((size * slot_count, ROW)),
         ),
-        in_specs=[smem] + [whole] * 4,
-        out_specs=[whole] * 4,
-        compiler_params=params,
+        in_specs=[smem, smem, block(ROW, tok), block(1, LAT), block(1, tok), block(1, 128)],
+        out_specs=[
+            block(tok, EXT),
+            block(tok, 128),
+            block(tok, 128),
+            block(size * slot_count, ROW),
+        ],
+        compiler_params=alone,
         name="rows",
-    )(info, kv_latent, latent_gain[None, :], page_ranks, frequency)
+    )(mine_info, lengths, kv_latent.T, latent_gain[None, :], page_ranks.T, frequency)
 
     queries = pl.pallas_call(
         query_kernel,
         out_shape=[shape((tok, h * (NOPE + ROPE))) for h in CHUNK_HEADS] * QUAD,
-        in_specs=[smem] + [whole] * 3,
-        out_specs=[whole] * (QUAD * CHUNKS),
+        grid=(1,),
+        in_specs=[smem, block(*q_heads.shape), block(tok, 128), block(tok, 128)],
+        out_specs=[block(tok, h * (NOPE + ROPE)) for h in CHUNK_HEADS] * QUAD,
         compiler_params=params,
         name="queries",
     )(quarter_info, q_heads, cosine, sine)
@@ -364,32 +400,29 @@
         for j in range(CHUNKS)
     ]
 
-    outgoing = lax.optimization_barrier((outgoing, moved[0][2]))[0]
+    outgoing = tie(outgoing, moved[0][2])
     arrived = lax.all_to_all(
         outgoing.reshape(size, slot_count, ROW), "ctx", split_axis=0, concat_axis=0, tiled=True
     )
     decode_cache = arrived.reshape(size * slot_count, ROW)
 
-    mine_info = mine[None].astype(jnp.int32)
     mine_info, decode_cache = lax.optimization_barrier((mine_info, decode_cache))
     window = (REACH + 2) * tok
 
-    def attend(j):
-        heads = CHUNK_HEADS[j]
-        steps = heads // 2
+    def attend(j, first, steps):
+        heads = 2 * steps
         flops = 2 * heads * 2 * (window * LAT * 256 + 2 * tok * window * (NOPE + ROPE + VDIM))
         return pl.pallas_call(
             functools.partial(attend_kernel, outer),
             grid=(steps,),
             out_shape=[shape((tok, heads * VDIM))] * QUAD,
-            in_specs=[
-                smem,
-                pl.BlockSpec((6 * tok, EXT), lambda i: (0, 0)),
-                pl.BlockSpec((6 * tok, EXT), lambda i: (0, 0)),
+            in_specs=[smem, block(6 * tok, EXT), block(6 * tok, EXT)]
+            + [
+                pl.BlockSpec((piece.shape[0], 512), lambda i: (0, first + i))
+                for piece in weights[j]
             ]
-            + [pl.BlockSpec((piece.shape[0], 512), lambda i: (0, i)) for piece in weights[j]]
-            + [pl.BlockSpec((tok, 256), lambda i: (0, i))] * QUAD
-            + [pl.BlockSpec((tok, 128), lambda i: (0, heads + i))] * QUAD,
+            + [pl.BlockSpec((tok, 256), lambda i: (0, first + i))] * QUAD
+            + [pl.BlockSpec((tok, 128), lambda i: (0, CHUNK_HEADS[j] + first + i))] * QUAD,
             out_specs=[pl.BlockSpec((tok, 256), lambda i: (0, i))] * QUAD,
             scratch_shapes=[
                 VMEM((2, window, LAT), jnp.bfloat16),
@@ -408,10 +441,10 @@
         )(mine_info, own_rows, other_rows, *weights[j], *moved[j], *moved[j])
 
     results = []
-    for j in range(CHUNKS):
-        parts = attend(j)
+    for call in CALLS:
+        parts = attend(*call)
         results.append([parts[0]] + [send_in_quad(parts[r], r) for r in range(1, QUAD)])
-    pieces = [results[j][r] for r in range(QUAD) for j in range(CHUNKS)]
+    pieces = [one[r] for r in range(QUAD) for one in results]
     attn_out = pl.pallas_call(
         gather_kernel,
         out_shape=shape((tok, H * VDIM)),

time: 162 us -> 133 us (0.82)
  waiting for transfers between devices: 48.9 us -> 29.8 us
  starting transfers between devices: 56.3 us -> 44.8 us
  local copies, waits for them, and re-layouts: 18.9 us -> 20.8 us
    ppermute x9 -> x6, waiting for transfers between devices: 24.3 us -> 6.95 us  [around(): lax.ppermute(array, 'ctx', [(i, (i + by) % size) for i in range(size)])]
    ppermute x9 -> x6, starting transfers between devices: 16.7 us -> 9.84 us  [around(): lax.ppermute(array, 'ctx', [(i, (i + by) % size) for i in range(size)])]
    ppermute x21, waiting for transfers between devices: 14 us -> 8.48 us  [quad_swap(): return lax.ppermute(array, ('groups', 'ctx'), pairs)]
    ppermute x21, starting transfers between devices: 17.5 us -> 13.7 us  [quad_swap(): return lax.ppermute(array, ('groups', 'ctx'), pairs)]
    ppermute x12 -> x8, waiting for transfers between devices: 10.6 us -> 14.4 us  [inner_swap(): return lax.ppermute(array, 'ctx', [(i, i ^ 2) for i in range(size)])]
    ppermute x12 -> x8, starting transfers between devices: 12.6 us -> 10.2 us  [inner_swap(): return lax.ppermute(array, 'ctx', [(i, i ^ 2) for i in range(size)])]
    unnamed x79 -> x65, local copies, waits for them, and re-layouts: 17.8 us -> 19.7 us
    pallas_call x3 -> x4, Pallas kernels: 27.7 us -> 29.4 us  [attend(): pl.pallas_call(functools.partial(attend_kernel, outer), grid=(steps,), ou...]
  transfers between devices with their start and end apart: 45 -> 38, of which waited for: 11 -> 9; matrix products, arithmetic and copies ran while one was open for 2% -> 2% of each run, Pallas kernels for 20% -> 24%
where the time goes in v4:
time: 133 us; the launch traced here: 132 us
  starting transfers between devices  44.8 us (34%)
  Pallas kernels  35.6 us (27%)
  waiting for transfers between devices  29.8 us (22%)
  local copies, waits for them, and re-layouts  20.8 us (16%)
    pallas_call x4, Pallas kernels, attend(): pl.pallas_call(functools.partial(attend_kernel, outer), grid=(steps,), ou...  29.4 us
    unnamed x65, local copies, waits for them, and re-layouts  19.7 us
    ppermute x8, waiting for transfers between devices, inner_swap(): return lax.ppermute(array, 'ctx', [(i, i ^ 2) for i in range(size)])  14.4 us
    ppermute x21, starting transfers between devices, quad_swap(): return lax.ppermute(array, ('groups', 'ctx'), pairs)  13.7 us
    ppermute x8, starting transfers between devices, inner_swap(): return lax.ppermute(array, 'ctx', [(i, i ^ 2) for i in range(size)])  10.2 us
    ppermute x6, starting transfers between devices, around(): lax.ppermute(array, 'ctx', [(i, (i + by) % size) for i in range(size)])  9.84 us
    ppermute x21, waiting for transfers between devices, quad_swap(): return lax.ppermute(array, ('groups', 'ctx'), pairs)  8.48 us
    ppermute x6, waiting for transfers between devices, around(): lax.ppermute(array, 'ctx', [(i, (i + by) % size) for i in range(size)])  6.95 us
  transfers between devices with their start and end apart: 38, of which 9 were waited for; matrix products, arithmetic and copies ran while one was open for 2% of the time, Pallas kernels for 24%

profile of v4, /device:TPU:0, one launch (start us, length us, event | category | flops | bytes accessed | tf_op | source)
XLA Modules:
  0.0 132.1 jit_solution(6129324820241166970)
XLA Ops:
  0.6 1.0 constant_dynamic-slice_fusion
  1.6 2.3 %rows.1 = (bf16[128,640]{1,0:T(8,128)(2,1)}, f32[128,128]{1,0:T(8,128)}, f32[128,128]{1,0:T(8,128)}, bf16[256,576]{1,0:T(8,128)(2,1)}) custom-call(s32[1]{0:T(128)} %bitcast.1.info, s32[8]{0:T(128)} %lengths, bf16[576,128]{1,0:T(8,128)(2,1)} %bitcast.8, f32[1,512]{1,0:T(1,128)} %bitcast.9, s32[1,128]{1,0:T(1,128)} %bitcast.10, f32[1,128]{1,0:T(1,128)} %constant.30.clone.freq), custom_call_target="tpu_custom_call" | custom-call | tf_op jit(solution)/shard_map/rows/pallas_call | solution.py:359
  4.0 2.9 %collective-permute-start.1 = (bf16[128,640]{1,0:T(8,128)(2,1)}, bf16[128,640]{1,0:T(8,128)(2,1)S(1)}, u32[]{:S(2)}, u32[]{:S(2)}) collective-permute-start(bf16[128,640]{1,0:T(8,128)(2,1)} %get-tuple-element.68), channel_id=1, source_target_pairs={{0,16},{1,17},{2,18},{3,19},{4,20},{5,21},{6,22},{7,23},{8,24},{9,... | collective-permute-start | bytes 491528 | tf_op jit(solution)/shard_map/ppermute | solution.py:274
  6.9 1.0 constant_dynamic-update-slice_fusion.1
  7.9 3.4 %collective-permute-done.1 = bf16[128,640]{1,0:T(8,128)(2,1)S(1)} collective-permute-done((bf16[128,640]{1,0:T(8,128)(2,1)}, bf16[128,640]{1,0:T(8,128)(2,1)S(1)}, u32[]{:S(2)}, u32[]{:S(2)}) %collective-permute-start.1) | collective-permute-done | bytes 163872 | tf_op jit(solution)/shard_map/ppermute | solution.py:274
  11.3 3.7 %collective-permute-start.2 = (bf16[256,640]{1,0:T(8,128)(2,1)S(1)}, bf16[256,640]{1,0:T(8,128)(2,1)S(1)}, u32[]{:S(2)}, u32[]{:S(2)}) collective-permute-start(bf16[256,640]{1,0:T(8,128)(2,1)S(1)} %get-tuple-element.122), channel_id=1, source_target_pairs={{0,2},{1,3},{2,4},{3,5},{4,6},{5,7},{6,8},{7,9},{8,10},{9,11},{10,... | collective-permute-start | bytes 983048 | tf_op jit(solution)/shard_map/ppermute | solution.py:309
  15.1 1.2 copy-done.1
  16.5 1.6 %collective-permute-start.6 = (bf16[64,2048]{1,0:T(8,128)(2,1)S(1)}, bf16[64,2048]{1,0:T(8,128)(2,1)S(1)}, u32[]{:S(2)}, u32[]{:S(2)}) collective-permute-start(bf16[64,2048]{1,0:T(8,128)(2,1)S(1)} %get-tuple-element.70.refs_0_), channel_id=1, source_target_pairs={{0,4},{1,5},{2,6},{3,7},{4,8},{5,9},{6,10},{7,11},{8,12},{9,13},{1... | collective-permute-start | bytes 786440 | tf_op jit(solution)/shard_map/ppermute | solution.py:282
  18.1 1.5 %collective-permute-start.7 = (bf16[64,2048]{1,0:T(8,128)(2,1)S(1)}, bf16[64,2048]{1,0:T(8,128)(2,1)S(1)}, u32[]{:S(2)}, u32[]{:S(2)}) collective-permute-start(bf16[64,2048]{1,0:T(8,128)(2,1)S(1)} %get-tuple-element.70.refs_0_), channel_id=1, source_target_pairs={{0,2},{1,3},{2,0},{3,1},{4,6},{5,7},{6,4},{7,5},{8,10},{9,11},{10,... | collective-permute-start | bytes 786440 | tf_op jit(solution)/shard_map/ppermute | solution.py:285
  19.7 0.7 collective-permute-start.3
  20.3 1.9 %copy-done = bf16[128,12288]{1,0:T(8,128)(2,1)S(1)} copy-done((bf16[128,12288]{1,0:T(8,128)(2,1)S(1)}, bf16[128,12288]{1,0:T(8,128)(2,1)}, u32[]{:S(2)}) %copy-start) | copy-done | bytes 3145752
  22.2 0.8 copy-done.2
  23.1 0.8 copy-done.3
  23.9 2.2 %queries.1 = (bf16[128,1536]{1,0:T(8,128)(2,1)S(1)}, bf16[128,1536]{1,0:T(8,128)(2,1)S(1)}, bf16[128,1536]{1,0:T(8,128)(2,1)S(1)}, bf16[128,1536]{1,0:T(8,128)(2...) custom-call(s32[1]{0:T(128)} %bitcast.info, ...), custom_call_target="tpu_custom_call" | custom-call | tf_op jit(solution)/shard_map/queries/pallas_call | solution.py:379
  26.2 1.5 %collective-permute-start = (bf16[128,1536]{1,0:T(8,128)(2,1)S(1)}, bf16[128,1536]{1,0:T(8,128)(2,1)S(1)}, u32[]{:S(2)}, u32[]{:S(2)}) collective-permute-start(bf16[128,1536]{1,0:T(8,128)(2,1)S(1)} %get-tuple-element.65), channel_id=1, source_target_pairs={{0,16},{1,17},{2,18},{3,19},{4,20},{5,21},{6,22},{7,23},{8,24},{9,... | collective-permute-start | bytes 1179656 | tf_op jit(solution)/shard_map/ppermute | solution.py:274
  27.7 0.7 copy-done.20
  28.4 2.5 %collective-permute-start.8 = (bf16[64,2048]{1,0:T(8,128)(2,1)S(1)}, bf16[64,2048]{1,0:T(8,128)(2,1)}, u32[]{:S(2)}, u32[]{:S(2)}) collective-permute-start(bf16[64,2048]{1,0:T(8,128)(2,1)S(1)} %collective-permute-done.6.refs_1_), channel_id=1, source_target_pairs={{0,4},{1,5},{2,6},{3,7},{4,8},{5,9},{6,10},{7,11},{8,12},{9,13},{1... | collective-permute-start | bytes 786440 | tf_op jit(solution)/shard_map/ppermute | solution.py:282
  31.1 2.8 %collective-permute-start.9 = (bf16[64,2048]{1,0:T(8,128)(2,1)S(1)}, bf16[64,2048]{1,0:T(8,128)(2,1)S(1)}, u32[]{:S(2)}, u32[]{:S(2)}) collective-permute-start(bf16[64,2048]{1,0:T(8,128)(2,1)S(1)} %collective-permute-done.6.refs_1_), channel_id=1, source_target_pairs={{0,2},{1,3},{2,0},{3,1},{4,6},{5,7},{6,4},{7,5},{8,10},{9,11},{10,... | collective-permute-start | bytes 786440 | tf_op jit(solution)/shard_map/ppermute | solution.py:285
  33.8 1.6 %collective-permute-start.15 = (bf16[64,2048]{1,0:T(8,128)(2,1)S(1)}, bf16[64,2048]{1,0:T(8,128)(2,1)}, u32[]{:S(2)}, u32[]{:S(2)}) collective-permute-start(bf16[64,2048]{1,0:T(8,128)(2,1)S(1)} %get-tuple-element.84.refs_0_), channel_id=1, source_target_pairs={{0,4},{1,5},{2,6},{3,7},{4,8},{5,9},{6,10},{7,11},{8,12},{9,13},{1... | collective-permute-start | bytes 786440 | tf_op jit(solution)/shard_map/ppermute | solution.py:282
  35.4 4.7 %collective-permute-done.8.refs_2_ = bf16[64,2048]{1,0:T(8,128)(2,1)} collective-permute-done((bf16[64,2048]{1,0:T(8,128)(2,1)S(1)}, bf16[64,2048]{1,0:T(8,128)(2,1)}, u32[]{:S(2)}, u32[]{:S(2)}) %collective-permute-start.8) | collective-permute-done | bytes 262176 | tf_op jit(solution)/shard_map/ppermute | solution.py:282
  40.1 1.2 collective-permute-start.16
  41.3 0.7 copy-done.25
  42.0 1.3 collective-permute-start.10
  43.3 1.8 %collective-permute-done.15.refs_1_ = bf16[64,2048]{1,0:T(8,128)(2,1)} collective-permute-done((bf16[64,2048]{1,0:T(8,128)(2,1)S(1)}, bf16[64,2048]{1,0:T(8,128)(2,1)}, u32[]{:S(2)}, u32[]{:S(2)}) %collective-permute-start.15) | collective-permute-done | bytes 262176 | tf_op jit(solution)/shard_map/ppermute | solution.py:282
  45.1 0.6 collective-permute-start.11
  45.7 1.5 %collective-permute-done.16.refs_4_ = bf16[64,2048]{1,0:T(8,128)(2,1)S(1)} collective-permute-done((bf16[64,2048]{1,0:T(8,128)(2,1)S(1)}, bf16[64,2048]{1,0:T(8,128)(2,1)S(1)}, u32[]{:S(2)}, u32[]{:S(2)}) %collective-permute-start.16) | collective-permute-done | bytes 262176 | tf_op jit(solution)/shard_map/ppermute | solution.py:285
  47.2 0.7 copy-done.12
  47.9 0.7 copy-done.8
  48.6 1.5 %collective-permute-start.17 = (bf16[64,2048]{1,0:T(8,128)(2,1)}, bf16[64,2048]{1,0:T(8,128)(2,1)}, u32[]{:S(2)}, u32[]{:S(2)}) collective-permute-start(bf16[64,2048]{1,0:T(8,128)(2,1)} %collective-permute-done.15.refs_1_), channel_id=1, source_target_pairs={{0,4},{1,5},{2,6},{3,7},{4,8},{5,9},{6,10},{7,11},{8,12},{9,13},{1... | collective-permute-start | bytes 786440 | tf_op jit(solution)/shard_map/ppermute | solution.py:282
  50.2 6.6 %all-to-all-start = ((bf16[16,16,576]{2,1,0:T(8,128)(2,1)}), bf16[16,16,576]{2,1,0:T(8,128)(2,1)}, u32[]{:S(2)}, u32[]{:S(2)}) async-start(bf16[16,16,576]{2,1,0:T(8,128)(2,1)} %bitcast.7), calls=%async_computation | async-start | bytes 655360 | tf_op jit(solution)/shard_map/all_to_all | solution.py:404
  56.8 1.9 %collective-permute-start.19 = (bf16[64,2048]{1,0:T(8,128)(2,1)}, bf16[64,2048]{1,0:T(8,128)(2,1)S(1)}, u32[]{:S(2)}, u32[]{:S(2)}) collective-permute-start(bf16[64,2048]{1,0:T(8,128)(2,1)} %collective-permute-done.15.refs_1_), channel_id=1, source_target_pairs={{0,2},{1,3},{2,0},{3,1},{4,6},{5,7},{6,4},{7,5},{8,10},{9,11},{10,... | collective-permute-start | bytes 786440 | tf_op jit(solution)/shard_map/ppermute | solution.py:285
  58.9 0.4 collective-permute-done.17.refs_2_
  59.7 1.4 %collective-permute-start.18 = (bf16[64,2048]{1,0:T(8,128)(2,1)}, bf16[64,2048]{1,0:T(8,128)(2,1)}, u32[]{:S(2)}, u32[]{:S(2)}) collective-permute-start(bf16[64,2048]{1,0:T(8,128)(2,1)} %collective-permute-done.17.refs_2_), channel_id=1, source_target_pairs={{0,4},{1,5},{2,6},{3,7},{4,8},{5,9},{6,10},{7,11},{8,12},{9,13},{1... | collective-permute-start | bytes 786440 | tf_op jit(solution)/shard_map/ppermute | solution.py:282
  61.1 8.4 %collective-permute-done.19.refs_5_ = bf16[64,2048]{1,0:T(8,128)(2,1)S(1)} collective-permute-done((bf16[64,2048]{1,0:T(8,128)(2,1)}, bf16[64,2048]{1,0:T(8,128)(2,1)S(1)}, u32[]{:S(2)}, u32[]{:S(2)}) %collective-permute-start.19) | collective-permute-done | bytes 262176 | tf_op jit(solution)/shard_map/ppermute | solution.py:285
  69.5 0.7 copy-done.23
  70.2 4.4 %collective-permute-done.12.refs_7_ = bf16[64,2048]{1,0:T(8,128)(2,1)S(1)} collective-permute-done((bf16[64,2048]{1,0:T(8,128)(2,1)}, bf16[64,2048]{1,0:T(8,128)(2,1)S(1)}, u32[]{:S(2)}, u32[]{:S(2)}) %collective-permute-start.12) | collective-permute-done | bytes 262176 | tf_op jit(solution)/shard_map/ppermute | solution.py:285
  74.6 0.7 copy-done.28
  75.4 0.6 collective-permute-start.23
  76.0 1.0 collective-permute-start.20
  77.0 1.1 collective-permute-start.21
  78.1 1.0 copy-done.9
  79.1 0.9 copy-done.15
  80.0 0.9 copy-done.18
  81.0 0.9 copy-done.21
  81.9 0.9 copy-done.26
  82.9 0.9 copy-done.29
  83.9 7.7 %attend.4 = (bf16[128,512]{1,0:T(8,128)(2,1)S(1)}, bf16[128,512]{1,0:T(8,128)(2,1)}, bf16[128,512]{1,0:T(8,128)(2,1)S(1)}, bf16[128,512]{1,0:T(8,128)(2,1)S(1)}) custom-call(s32[1]{0:T(128)} %bitcast.1.info, bf16[768,640]{1,0:T(8,128)(2,1)S(1)} %constant_dynamic-update-slice_fusion.2.own, bf16[768,640]{1,0:T(8,128)(2,1)S(1)} %collective-permute-done.4.other, ...), custom_call_target="tpu_custom_call" | custom-call | flops 2181038080 | bytes 4194304 | tf_op jit(solution)/shard_map/attend/pallas_call | solution.py:415
  91.6 1.0 collective-permute-start.33
  92.6 0.6 collective-permute-start.29
  93.2 1.0 copy-done.7
  94.2 6.9 %attend.5 = (bf16[128,512]{1,0:T(8,128)(2,1)S(1)}, bf16[128,512]{1,0:T(8,128)(2,1)S(1)}, bf16[128,512]{1,0:T(8,128)(2,1)S(1)}, bf16[128,512]{1,0:T(8,128)(2,1)S(1)}) custom-call(s32[1]{0:T(128)} %bitcast.1.info, bf16[768,640]{1,0:T(8,128)(2,1)S(1)} %constant_dynamic-update-slice_fusion.2.own, bf16[768,640]{1,0:T(8,128)(2,1)S(1)} %collective-permute-done.4.other, ...), custom_call_target="tpu_custom_call" | custom-call | flops 2181038080 | bytes 4194304 | tf_op jit(solution)/shard_map/attend/pallas_call | solution.py:415
  101.7 1.4 %collective-permute-start.34 = (bf16[128,512]{1,0:T(8,128)(2,1)S(1)}, bf16[128,512]{1,0:T(8,128)(2,1)S(1)}, u32[]{:S(2)}, u32[]{:S(2)}) collective-permute-start(bf16[128,512]{1,0:T(8,128)(2,1)S(1)} %get-tuple-element.114), channel_id=1, source_target_pairs={{0,17},{1,16},{2,19},{3,18},{4,21},{5,20},{6,23},{7,22},{8,25},{9,... | collective-permute-start | bytes 393224 | tf_op jit(solution)/shard_map/ppermute | solution.py:274
  103.1 0.6 collective-permute-start.30
  103.7 7.4 %attend.6 = (bf16[128,512]{1,0:T(8,128)(2,1)S(1)}, bf16[128,512]{1,0:T(8,128)(2,1)}, bf16[128,512]{1,0:T(8,128)(2,1)S(1)}, bf16[128,512]{1,0:T(8,128)(2,1)S(1)}) custom-call(s32[1]{0:T(128)} %bitcast.1.info, bf16[768,640]{1,0:T(8,128)(2,1)S(1)} %constant_dynamic-update-slice_fusion.2.own, bf16[768,640]{1,0:T(8,128)(2,1)S(1)} %collective-permute-done.4.other, ...), custom_call_target="tpu_custom_call" | custom-call | flops 2181038080 | bytes 4194304 | tf_op jit(solution)/shard_map/attend/pallas_call | solution.py:415
  111.1 1.0 collective-permute-start.35
  112.1 0.6 collective-permute-start.31
  112.7 1.0 copy-done.5
  113.7 7.4 %attend.7 = (bf16[128,512]{1,0:T(8,128)(2,1)S(1)}, bf16[128,512]{1,0:T(8,128)(2,1)}, bf16[128,512]{1,0:T(8,128)(2,1)}, bf16[128,512]{1,0:T(8,128)(2,1)}) custom-call(s32[1]{0:T(128)} %bitcast.1.info, bf16[768,640]{1,0:T(8,128)(2,1)S(1)} %constant_dynamic-update-slice_fusion.2.own, bf16[768,640]{1,0:T(8,128)(2,1)S(1)} %collective-permute-done.4.other, ...), custom_call_target="tpu_custom_call" | custom-call | flops 2181038080 | bytes 4194304 | tf_op jit(solution)/shard_map/attend/pallas_call | solution.py:415
  121.7 1.4 %collective-permute-start.36 = (bf16[128,512]{1,0:T(8,128)(2,1)}, bf16[128,512]{1,0:T(8,128)(2,1)S(1)}, u32[]{:S(2)}, u32[]{:S(2)}) collective-permute-start(bf16[128,512]{1,0:T(8,128)(2,1)} %get-tuple-element.118), channel_id=1, source_target_pairs={{0,17},{1,16},{2,19},{3,18},{4,21},{5,20},{6,23},{7,22},{8,25},{9,... | collective-permute-start | bytes 393224 | tf_op jit(solution)/shard_map/ppermute | solution.py:274
  123.0 0.6 collective-permute-start.32
  123.6 1.8 %copy.10 = bf16[256,576]{0,1:T(8,128)(2,1)} copy(bf16[256,576]{1,0:T(8,128)(2,1)} %bitcast.6) | data formatting | bytes 589824
  125.5 1.8 %collective-permute-done.36.refs_15_ = bf16[128,512]{1,0:T(8,128)(2,1)S(1)} collective-permute-done((bf16[128,512]{1,0:T(8,128)(2,1)}, bf16[128,512]{1,0:T(8,128)(2,1)S(1)}, u32[]{:S(2)}, u32[]{:S(2)}) %collective-permute-start.36) | collective-permute-done | bytes 131104 | tf_op jit(solution)/shard_map/ppermute | solution.py:274
  127.2 3.2 %collective-permute-done.32.refs_11_ = bf16[128,512]{1,0:T(8,128)(2,1)S(1)} collective-permute-done((bf16[128,512]{1,0:T(8,128)(2,1)}, bf16[128,512]{1,0:T(8,128)(2,1)S(1)}, u32[]{:S(2)}, u32[]{:S(2)}) %collective-permute-start.32) | collective-permute-done | bytes 131104 | tf_op jit(solution)/shard_map/ppermute | solution.py:274
  130.5 1.4 %place.1 = bf16[128,8192]{1,0:T(8,128)(2,1)} custom-call(s32[1]{0:T(128)} %bitcast.info, bf16[128,512]{1,0:T(8,128)(2,1)S(1)} %get-tuple-element.80.refs_0_, bf16[128,512]{1,0:T(8,128)(2,1)S(1)} %get-tuple-element.81.refs_1_, bf16[128,512]{1,0:T(8,128)(2,1)S(1)} %get-tuple-element.97.refs_2_, bf16[128,512]{1,0:T(8,128)(2,1)S(1)} %get-tuple-element.98.refs_3_, ...), custom_call_target="tpu_custom_call" | custom-call | tf_op jit(solution)/shard_map/place/pallas_call | solution.py:448
  (88 shorter events, 2.3 us)
Async XLA Ops:
  4.0 7.3 %collective-permute-start.1 = (bf16[128,640]{1,0:T(8,128)(2,1)}, bf16[128,640]{1,0:T(8,128)(2,1)S(1)}, u32[]{:S(2)}, u32[]{:S(2)}) collective-permute-start(bf16[128,640]{1,0:T(8,128)(2,1)} %get-tuple-element.68), channel_id=1, source_target_pairs={{0,16},{1,17},{2,18},{3,19},{4,20},{5,21},{6,22},{7,23},{8,24},{9,... | collective-permute-start | bytes 491528 | tf_op jit(solution)/shard_map/ppermute | solution.py:274
  6.9 8.2 %collective-permute-start.5 = (bf16[32,4096]{1,0:T(8,128)(2,1)S(1)}, bf16[32,4096]{1,0:T(8,128)(2,1)S(1)}, u32[]{:S(2)}, u32[]{:S(2)}) collective-permute-start(bf16[32,4096]{1,0:T(8,128)(2,1)S(1)} %constant_dynamic-slice_fusion), channel_id=1, source_target_pairs={{0,1},{1,0},{2,3},{3,2},{4,5},{5,4},{6,7},{7,6},{8,9},{9,8},{10,11... | collective-permute-start | bytes 786440 | tf_op jit(solution)/shard_map/ppermute | solution.py:274
  11.3 19.5 %collective-permute-start.2 = (bf16[256,640]{1,0:T(8,128)(2,1)S(1)}, bf16[256,640]{1,0:T(8,128)(2,1)S(1)}, u32[]{:S(2)}, u32[]{:S(2)}) collective-permute-start(bf16[256,640]{1,0:T(8,128)(2,1)S(1)} %get-tuple-element.122), channel_id=1, source_target_pairs={{0,2},{1,3},{2,4},{3,5},{4,6},{5,7},{6,8},{7,9},{8,10},{9,11},{10,... | collective-permute-start | bytes 983048 | tf_op jit(solution)/shard_map/ppermute | solution.py:309
  15.1 1.2 copy-start.1
  16.5 14.4 %copy-start.14 = (bf16[64,2048]{1,0:T(8,128)(2,1)}, bf16[64,2048]{1,0:T(8,128)(2,1)S(1)}, u32[]{:S(2)}) copy-start(bf16[64,2048]{1,0:T(8,128)(2,1)S(1)} %get-tuple-element.70.refs_0_) | copy-start | bytes 786436
  16.5 31.4 %copy-start.10 = (bf16[64,2048]{1,0:T(8,128)(2,1)}, bf16[64,2048]{1,0:T(8,128)(2,1)S(1)}, u32[]{:S(2)}) copy-start(bf16[64,2048]{1,0:T(8,128)(2,1)S(1)} %get-tuple-element.84.refs_0_) | copy-start | bytes 786436
  16.5 11.1 %collective-permute-start.6 = (bf16[64,2048]{1,0:T(8,128)(2,1)S(1)}, bf16[64,2048]{1,0:T(8,128)(2,1)S(1)}, u32[]{:S(2)}, u32[]{:S(2)}) collective-permute-start(bf16[64,2048]{1,0:T(8,128)(2,1)S(1)} %get-tuple-element.70.refs_0_), channel_id=1, source_target_pairs={{0,4},{1,5},{2,6},{3,7},{4,8},{5,9},{6,10},{7,11},{8,12},{9,13},{1... | collective-permute-start | bytes 786440 | tf_op jit(solution)/shard_map/ppermute | solution.py:282
  18.1 9.5 %collective-permute-start.7 = (bf16[64,2048]{1,0:T(8,128)(2,1)S(1)}, bf16[64,2048]{1,0:T(8,128)(2,1)S(1)}, u32[]{:S(2)}, u32[]{:S(2)}) collective-permute-start(bf16[64,2048]{1,0:T(8,128)(2,1)S(1)} %get-tuple-element.70.refs_0_), channel_id=1, source_target_pairs={{0,2},{1,3},{2,0},{3,1},{4,6},{5,7},{6,4},{7,5},{8,10},{9,11},{10,... | collective-permute-start | bytes 786440 | tf_op jit(solution)/shard_map/ppermute | solution.py:285
  19.7 11.3 %collective-permute-start.3 = (bf16[256,640]{1,0:T(8,128)(2,1)S(1)}, bf16[256,640]{1,0:T(8,128)(2,1)S(1)}, u32[]{:S(2)}, u32[]{:S(2)}) collective-permute-start(bf16[256,640]{1,0:T(8,128)(2,1)S(1)} %get-tuple-element.122), channel_id=1, source_target_pairs={{1,5},{3,7},{5,9},{7,11},{9,13},{11,15},{17,21},{19,23},{21,25},{2... | collective-permute-start | bytes 983048 | tf_op jit(solution)/shard_map/ppermute | solution.py:309
  20.3 1.9 %copy-start = (bf16[128,12288]{1,0:T(8,128)(2,1)S(1)}, bf16[128,12288]{1,0:T(8,128)(2,1)}, u32[]{:S(2)}) copy-start(bf16[128,12288]{1,0:T(8,128)(2,1)} %query.1) | copy-start | bytes 9437188
  22.2 0.8 copy-start.2
  23.1 0.8 copy-start.3
  26.2 65.4 %copy-start.6 = (bf16[128,1536]{1,0:T(8,128)(2,1)}, bf16[128,1536]{1,0:T(8,128)(2,1)S(1)}, u32[]{:S(2)}) copy-start(bf16[128,1536]{1,0:T(8,128)(2,1)S(1)} %get-tuple-element.75.refs_8_.refs_12_) | copy-start | bytes 1179652
  26.2 77.5 %copy-start.4 = (bf16[128,1536]{1,0:T(8,128)(2,1)}, bf16[128,1536]{1,0:T(8,128)(2,1)S(1)}, u32[]{:S(2)}) copy-start(bf16[128,1536]{1,0:T(8,128)(2,1)S(1)} %get-tuple-element.90.refs_8_.refs_12_) | copy-start | bytes 1179652
  26.2 21.7 %collective-permute-start = (bf16[128,1536]{1,0:T(8,128)(2,1)S(1)}, bf16[128,1536]{1,0:T(8,128)(2,1)S(1)}, u32[]{:S(2)}, u32[]{:S(2)}) collective-permute-start(bf16[128,1536]{1,0:T(8,128)(2,1)S(1)} %get-tuple-element.65), channel_id=1, source_target_pairs={{0,16},{1,17},{2,18},{3,19},{4,20},{5,21},{6,22},{7,23},{8,24},{9,... | collective-permute-start | bytes 1179656 | tf_op jit(solution)/shard_map/ppermute | solution.py:274
  27.7 22.5 %copy-start.17 = (bf16[64,2048]{1,0:T(8,128)(2,1)}, bf16[64,2048]{1,0:T(8,128)(2,1)S(1)}, u32[]{:S(2)}) copy-start(bf16[64,2048]{1,0:T(8,128)(2,1)S(1)} %collective-permute-done.6.refs_1_) | copy-start | bytes 786436
  28.4 11.7 %collective-permute-start.8 = (bf16[64,2048]{1,0:T(8,128)(2,1)S(1)}, bf16[64,2048]{1,0:T(8,128)(2,1)}, u32[]{:S(2)}, u32[]{:S(2)}) collective-permute-start(bf16[64,2048]{1,0:T(8,128)(2,1)S(1)} %collective-permute-done.6.refs_1_), channel_id=1, source_target_pairs={{0,4},{1,5},{2,6},{3,7},{4,8},{5,9},{6,10},{7,11},{8,12},{9,13},{1... | collective-permute-start | bytes 786440 | tf_op jit(solution)/shard_map/ppermute | solution.py:282
  31.0 46.0 %collective-permute-start.4 = (bf16[768,640]{1,0:T(8,128)(2,1)S(1)}, bf16[768,640]{1,0:T(8,128)(2,1)S(1)}, u32[]{:S(2)}, u32[]{:S(2)}) collective-permute-start(bf16[768,640]{1,0:T(8,128)(2,1)S(1)} %constant_dynamic-update-slice_fusion.2.own), channel_id=1, source_target_pairs={{0,1},{1,0},{2,3},{3,2},{4,5},{5,4},{6,7},{7,6},{8,9},{9,8},{10,11... | collective-permute-start | bytes 2949128 | tf_op jit(solution)/shard_map/ppermute | solution.py:274
  31.1 10.2 %collective-permute-start.9 = (bf16[64,2048]{1,0:T(8,128)(2,1)S(1)}, bf16[64,2048]{1,0:T(8,128)(2,1)S(1)}, u32[]{:S(2)}, u32[]{:S(2)}) collective-permute-start(bf16[64,2048]{1,0:T(8,128)(2,1)S(1)} %collective-permute-done.6.refs_1_), channel_id=1, source_target_pairs={{0,2},{1,3},{2,0},{3,1},{4,6},{5,7},{6,4},{7,5},{8,10},{9,11},{10,... | collective-permute-start | bytes 786440 | tf_op jit(solution)/shard_map/ppermute | solution.py:285
  33.8 11.3 %collective-permute-start.15 = (bf16[64,2048]{1,0:T(8,128)(2,1)S(1)}, bf16[64,2048]{1,0:T(8,128)(2,1)}, u32[]{:S(2)}, u32[]{:S(2)}) collective-permute-start(bf16[64,2048]{1,0:T(8,128)(2,1)S(1)} %get-tuple-element.84.refs_0_), channel_id=1, source_target_pairs={{0,4},{1,5},{2,6},{3,7},{4,8},{5,9},{6,10},{7,11},{8,12},{9,13},{1... | collective-permute-start | bytes 786440 | tf_op jit(solution)/shard_map/ppermute | solution.py:282
  40.1 7.1 %collective-permute-start.16 = (bf16[64,2048]{1,0:T(8,128)(2,1)S(1)}, bf16[64,2048]{1,0:T(8,128)(2,1)S(1)}, u32[]{:S(2)}, u32[]{:S(2)}) collective-permute-start(bf16[64,2048]{1,0:T(8,128)(2,1)S(1)} %get-tuple-element.84.refs_0_), channel_id=1, source_target_pairs={{0,2},{1,3},{2,0},{3,1},{4,6},{5,7},{6,4},{7,5},{8,10},{9,11},{10,... | collective-permute-start | bytes 786440 | tf_op jit(solution)/shard_map/ppermute | solution.py:285
  42.0 14.8 %collective-permute-start.10 = (bf16[64,2048]{1,0:T(8,128)(2,1)}, bf16[64,2048]{1,0:T(8,128)(2,1)}, u32[]{:S(2)}, u32[]{:S(2)}) collective-permute-start(bf16[64,2048]{1,0:T(8,128)(2,1)} %collective-permute-done.8.refs_2_), channel_id=1, source_target_pairs={{0,4},{1,5},{2,6},{3,7},{4,8},{5,9},{6,10},{7,11},{8,12},{9,13},{1... | collective-permute-start | bytes 786440 | tf_op jit(solution)/shard_map/ppermute | solution.py:282
  45.1 13.7 %collective-permute-start.11 = (bf16[64,2048]{1,0:T(8,128)(2,1)}, bf16[64,2048]{1,0:T(8,128)(2,1)}, u32[]{:S(2)}, u32[]{:S(2)}) collective-permute-start(bf16[64,2048]{1,0:T(8,128)(2,1)} %collective-permute-done.8.refs_2_), channel_id=1, source_target_pairs={{0,2},{1,3},{2,0},{3,1},{4,6},{5,7},{6,4},{7,5},{8,10},{9,11},{10,... | collective-permute-start | bytes 786440 | tf_op jit(solution)/shard_map/ppermute | solution.py:285
  47.9 11.9 %collective-permute-start.14 = (bf16[128,1536]{1,0:T(8,128)(2,1)}, bf16[128,1536]{1,0:T(8,128)(2,1)}, u32[]{:S(2)}, u32[]{:S(2)}) collective-permute-start(bf16[128,1536]{1,0:T(8,128)(2,1)} %get-tuple-element.79), channel_id=1, source_target_pairs={{0,17},{1,16},{2,19},{3,18},{4,21},{5,20},{6,23},{7,22},{8,25},{9,... | collective-permute-start | bytes 1179656 | tf_op jit(solution)/shard_map/ppermute | solution.py:274
  48.6 10.7 %collective-permute-start.17 = (bf16[64,2048]{1,0:T(8,128)(2,1)}, bf16[64,2048]{1,0:T(8,128)(2,1)}, u32[]{:S(2)}, u32[]{:S(2)}) collective-permute-start(bf16[64,2048]{1,0:T(8,128)(2,1)} %collective-permute-done.15.refs_1_), channel_id=1, source_target_pairs={{0,4},{1,5},{2,6},{3,7},{4,8},{5,9},{6,10},{7,11},{8,12},{9,13},{1... | collective-permute-start | bytes 786440 | tf_op jit(solution)/shard_map/ppermute | solution.py:282
  50.2 25.8 %all-to-all-start = ((bf16[16,16,576]{2,1,0:T(8,128)(2,1)}), bf16[16,16,576]{2,1,0:T(8,128)(2,1)}, u32[]{:S(2)}, u32[]{:S(2)}) async-start(bf16[16,16,576]{2,1,0:T(8,128)(2,1)} %bitcast.7), calls=%async_computation | async-start | bytes 655360 | tf_op jit(solution)/shard_map/all_to_all | solution.py:404
  56.8 12.7 %collective-permute-start.19 = (bf16[64,2048]{1,0:T(8,128)(2,1)}, bf16[64,2048]{1,0:T(8,128)(2,1)S(1)}, u32[]{:S(2)}, u32[]{:S(2)}) collective-permute-start(bf16[64,2048]{1,0:T(8,128)(2,1)} %collective-permute-done.15.refs_1_), channel_id=1, source_target_pairs={{0,2},{1,3},{2,0},{3,1},{4,6},{5,7},{6,4},{7,5},{8,10},{9,11},{10,... | collective-permute-start | bytes 786440 | tf_op jit(solution)/shard_map/ppermute | solution.py:285
  58.8 15.9 %collective-permute-start.12 = (bf16[64,2048]{1,0:T(8,128)(2,1)}, bf16[64,2048]{1,0:T(8,128)(2,1)S(1)}, u32[]{:S(2)}, u32[]{:S(2)}) collective-permute-start(bf16[64,2048]{1,0:T(8,128)(2,1)} %collective-permute-done.10.refs_3_), channel_id=1, source_target_pairs={{0,2},{1,3},{2,0},{3,1},{4,6},{5,7},{6,4},{7,5},{8,10},{9,11},{10,... | collective-permute-start | bytes 786440 | tf_op jit(solution)/shard_map/ppermute | solution.py:285
  59.3 16.7 %collective-permute-start.13 = (bf16[128,1536]{1,0:T(8,128)(2,1)S(1)}, bf16[128,1536]{1,0:T(8,128)(2,1)}, u32[]{:S(2)}, u32[]{:S(2)}) collective-permute-start(bf16[128,1536]{1,0:T(8,128)(2,1)S(1)} %get-tuple-element.77), channel_id=1, source_target_pairs={{0,1},{1,0},{2,3},{3,2},{4,5},{5,4},{6,7},{7,6},{8,9},{9,8},{10,11... | collective-permute-start | bytes 1179656 | tf_op jit(solution)/shard_map/ppermute | solution.py:274
  59.7 16.2 %collective-permute-start.18 = (bf16[64,2048]{1,0:T(8,128)(2,1)}, bf16[64,2048]{1,0:T(8,128)(2,1)}, u32[]{:S(2)}, u32[]{:S(2)}) collective-permute-start(bf16[64,2048]{1,0:T(8,128)(2,1)} %collective-permute-done.17.refs_2_), channel_id=1, source_target_pairs={{0,4},{1,5},{2,6},{3,7},{4,8},{5,9},{6,10},{7,11},{8,12},{9,13},{1... | collective-permute-start | bytes 786440 | tf_op jit(solution)/shard_map/ppermute | solution.py:282
  70.2 21.4 %collective-permute-start.24 = (bf16[128,1536]{1,0:T(8,128)(2,1)}, bf16[128,1536]{1,0:T(8,128)(2,1)}, u32[]{:S(2)}, u32[]{:S(2)}) collective-permute-start(bf16[128,1536]{1,0:T(8,128)(2,1)} %get-tuple-element.96), channel_id=1, source_target_pairs={{0,17},{1,16},{2,19},{3,18},{4,21},{5,20},{6,23},{7,22},{8,25},{9,... | collective-permute-start | bytes 1179656 | tf_op jit(solution)/shard_map/ppermute | solution.py:274
  74.6 0.8 copy-start.28
  75.4 17.2 %collective-permute-start.23 = (bf16[128,1536]{1,0:T(8,128)(2,1)}, bf16[128,1536]{1,0:T(8,128)(2,1)}, u32[]{:S(2)}, u32[]{:S(2)}) collective-permute-start(bf16[128,1536]{1,0:T(8,128)(2,1)} %get-tuple-element.94), channel_id=1, source_target_pairs={{0,16},{1,17},{2,18},{3,19},{4,20},{5,21},{6,22},{7,23},{8,24},{9,... | collective-permute-start | bytes 1179656 | tf_op jit(solution)/shard_map/ppermute | solution.py:274
  76.0 25.7 %collective-permute-start.22 = (bf16[128,1536]{1,0:T(8,128)(2,1)S(1)}, bf16[128,1536]{1,0:T(8,128)(2,1)S(1)}, u32[]{:S(2)}, u32[]{:S(2)}) collective-permute-start(bf16[128,1536]{1,0:T(8,128)(2,1)S(1)} %get-tuple-element.92), channel_id=1, source_target_pairs={{0,1},{1,0},{2,3},{3,2},{4,5},{5,4},{6,7},{7,6},{8,9},{9,8},{10,11... | collective-permute-start | bytes 1179656 | tf_op jit(solution)/shard_map/ppermute | solution.py:274
  76.0 27.1 %collective-permute-start.20 = (bf16[64,2048]{1,0:T(8,128)(2,1)}, bf16[64,2048]{1,0:T(8,128)(2,1)S(1)}, u32[]{:S(2)}, u32[]{:S(2)}) collective-permute-start(bf16[64,2048]{1,0:T(8,128)(2,1)} %collective-permute-done.17.refs_2_), channel_id=1, source_target_pairs={{0,2},{1,3},{2,0},{3,1},{4,6},{5,7},{6,4},{7,5},{8,10},{9,11},{10,... | collective-permute-start | bytes 786440 | tf_op jit(solution)/shard_map/ppermute | solution.py:285
  77.0 26.6 %collective-permute-start.21 = (bf16[64,2048]{1,0:T(8,128)(2,1)}, bf16[64,2048]{1,0:T(8,128)(2,1)S(1)}, u32[]{:S(2)}, u32[]{:S(2)}) collective-permute-start(bf16[64,2048]{1,0:T(8,128)(2,1)} %collective-permute-done.18.refs_3_), channel_id=1, source_target_pairs={{0,2},{1,3},{2,0},{3,1},{4,6},{5,7},{6,4},{7,5},{8,10},{9,11},{10,... | collective-permute-start | bytes 786440 | tf_op jit(solution)/shard_map/ppermute | solution.py:285
  78.1 1.0 copy-start.9
  79.1 0.9 copy-start.15
  80.0 0.9 copy-start.18
  81.0 0.9 copy-start.21
  81.9 0.9 copy-start.26
  82.9 0.9 copy-start.29
  83.8 9.3 %copy-start.16 = (bf16[64,2048]{1,0:T(8,128)(2,1)S(1)}, bf16[64,2048]{1,0:T(8,128)(2,1)}, u32[]{:S(2)}) copy-start(bf16[64,2048]{1,0:T(8,128)(2,1)} %copy-done.14) | copy-start | bytes 786436
  83.8 9.3 %copy-start.19 = (bf16[64,2048]{1,0:T(8,128)(2,1)S(1)}, bf16[64,2048]{1,0:T(8,128)(2,1)}, u32[]{:S(2)}) copy-start(bf16[64,2048]{1,0:T(8,128)(2,1)} %copy-done.17) | copy-start | bytes 786436
  83.9 9.3 %copy-start.22 = (bf16[64,2048]{1,0:T(8,128)(2,1)S(1)}, bf16[64,2048]{1,0:T(8,128)(2,1)}, u32[]{:S(2)}) copy-start(bf16[64,2048]{1,0:T(8,128)(2,1)} %copy-done.20) | copy-start | bytes 786436
  83.9 9.3 %copy-start.27 = (bf16[64,2048]{1,0:T(8,128)(2,1)S(1)}, bf16[64,2048]{1,0:T(8,128)(2,1)}, u32[]{:S(2)}) copy-start(bf16[64,2048]{1,0:T(8,128)(2,1)} %copy-done.25) | copy-start | bytes 786436
  83.9 9.3 %copy-start.30 = (bf16[64,2048]{1,0:T(8,128)(2,1)S(1)}, bf16[64,2048]{1,0:T(8,128)(2,1)}, u32[]{:S(2)}) copy-start(bf16[64,2048]{1,0:T(8,128)(2,1)} %copy-done.28) | copy-start | bytes 786436
  91.6 9.5 %collective-permute-start.33 = (bf16[128,512]{1,0:T(8,128)(2,1)S(1)}, bf16[128,512]{1,0:T(8,128)(2,1)S(1)}, u32[]{:S(2)}, u32[]{:S(2)}) collective-permute-start(bf16[128,512]{1,0:T(8,128)(2,1)S(1)} %get-tuple-element.112), channel_id=1, source_target_pairs={{0,17},{1,16},{2,19},{3,18},{4,21},{5,20},{6,23},{7,22},{8,25},{9,... | collective-permute-start | bytes 393224 | tf_op jit(solution)/shard_map/ppermute | solution.py:274
  92.6 8.9 %collective-permute-start.29 = (bf16[128,512]{1,0:T(8,128)(2,1)S(1)}, bf16[128,512]{1,0:T(8,128)(2,1)S(1)}, u32[]{:S(2)}, u32[]{:S(2)}) collective-permute-start(bf16[128,512]{1,0:T(8,128)(2,1)S(1)} %get-tuple-element.104), channel_id=1, source_target_pairs={{0,16},{1,17},{2,18},{3,19},{4,20},{5,21},{6,22},{7,23},{8,24},{9,... | collective-permute-start | bytes 393224 | tf_op jit(solution)/shard_map/ppermute | solution.py:274
  93.2 1.0 copy-start.7
  94.2 9.4 %copy-start.11 = (bf16[64,2048]{1,0:T(8,128)(2,1)S(1)}, bf16[64,2048]{1,0:T(8,128)(2,1)}, u32[]{:S(2)}) copy-start(bf16[64,2048]{1,0:T(8,128)(2,1)} %copy-done.10) | copy-start | bytes 786436
  94.2 9.5 %copy-start.13 = (bf16[64,2048]{1,0:T(8,128)(2,1)S(1)}, bf16[64,2048]{1,0:T(8,128)(2,1)}, u32[]{:S(2)}) copy-start(bf16[64,2048]{1,0:T(8,128)(2,1)} %copy-done.12) | copy-start | bytes 786436
  94.2 9.5 %copy-start.24 = (bf16[64,2048]{1,0:T(8,128)(2,1)S(1)}, bf16[64,2048]{1,0:T(8,128)(2,1)}, u32[]{:S(2)}) copy-start(bf16[64,2048]{1,0:T(8,128)(2,1)} %copy-done.23) | copy-start | bytes 786436
  101.1 21.9 %collective-permute-start.26 = (bf16[128,512]{1,0:T(8,128)(2,1)S(1)}, bf16[128,512]{1,0:T(8,128)(2,1)S(1)}, u32[]{:S(2)}, u32[]{:S(2)}) collective-permute-start(bf16[128,512]{1,0:T(8,128)(2,1)S(1)} %get-tuple-element.100), channel_id=1, source_target_pairs={{0,1},{1,0},{2,3},{3,2},{4,5},{5,4},{6,7},{7,6},{8,9},{9,8},{10,11... | collective-permute-start | bytes 393224 | tf_op jit(solution)/shard_map/ppermute | solution.py:274
  101.5 24.0 %collective-permute-start.25 = (bf16[128,512]{1,0:T(8,128)(2,1)}, bf16[128,512]{1,0:T(8,128)(2,1)S(1)}, u32[]{:S(2)}, u32[]{:S(2)}) collective-permute-start(bf16[128,512]{1,0:T(8,128)(2,1)} %get-tuple-element.99), channel_id=1, source_target_pairs={{0,1},{1,0},{2,3},{3,2},{4,5},{5,4},{6,7},{7,6},{8,9},{9,8},{10,11... | collective-permute-start | bytes 393224 | tf_op jit(solution)/shard_map/ppermute | solution.py:274
  101.7 9.4 %collective-permute-start.34 = (bf16[128,512]{1,0:T(8,128)(2,1)S(1)}, bf16[128,512]{1,0:T(8,128)(2,1)S(1)}, u32[]{:S(2)}, u32[]{:S(2)}) collective-permute-start(bf16[128,512]{1,0:T(8,128)(2,1)S(1)} %get-tuple-element.114), channel_id=1, source_target_pairs={{0,17},{1,16},{2,19},{3,18},{4,21},{5,20},{6,23},{7,22},{8,25},{9,... | collective-permute-start | bytes 393224 | tf_op jit(solution)/shard_map/ppermute | solution.py:274
  103.1 9.0 %collective-permute-start.30 = (bf16[128,512]{1,0:T(8,128)(2,1)S(1)}, bf16[128,512]{1,0:T(8,128)(2,1)S(1)}, u32[]{:S(2)}, u32[]{:S(2)}) collective-permute-start(bf16[128,512]{1,0:T(8,128)(2,1)S(1)} %get-tuple-element.106), channel_id=1, source_target_pairs={{0,16},{1,17},{2,18},{3,19},{4,20},{5,21},{6,22},{7,23},{8,24},{9,... | collective-permute-start | bytes 393224 | tf_op jit(solution)/shard_map/ppermute | solution.py:274
  111.1 10.4 %collective-permute-start.35 = (bf16[128,512]{1,0:T(8,128)(2,1)S(1)}, bf16[128,512]{1,0:T(8,128)(2,1)S(1)}, u32[]{:S(2)}, u32[]{:S(2)}) collective-permute-start(bf16[128,512]{1,0:T(8,128)(2,1)S(1)} %get-tuple-element.116), channel_id=1, source_target_pairs={{0,17},{1,16},{2,19},{3,18},{4,21},{5,20},{6,23},{7,22},{8,25},{9,... | collective-permute-start | bytes 393224 | tf_op jit(solution)/shard_map/ppermute | solution.py:274
  112.1 9.6 %collective-permute-start.31 = (bf16[128,512]{1,0:T(8,128)(2,1)S(1)}, bf16[128,512]{1,0:T(8,128)(2,1)S(1)}, u32[]{:S(2)}, u32[]{:S(2)}) collective-permute-start(bf16[128,512]{1,0:T(8,128)(2,1)S(1)} %get-tuple-element.108), channel_id=1, source_target_pairs={{0,16},{1,17},{2,18},{3,19},{4,20},{5,21},{6,22},{7,23},{8,24},{9,... | collective-permute-start | bytes 393224 | tf_op jit(solution)/shard_map/ppermute | solution.py:274
  112.7 1.0 copy-start.5
  121.1 4.4 %collective-permute-start.28 = (bf16[128,512]{1,0:T(8,128)(2,1)}, bf16[128,512]{1,0:T(8,128)(2,1)S(1)}, u32[]{:S(2)}, u32[]{:S(2)}) collective-permute-start(bf16[128,512]{1,0:T(8,128)(2,1)} %get-tuple-element.102), channel_id=1, source_target_pairs={{0,1},{1,0},{2,3},{3,2},{4,5},{5,4},{6,7},{7,6},{8,9},{9,8},{10,11... | collective-permute-start | bytes 393224 | tf_op jit(solution)/shard_map/ppermute | solution.py:274
  121.5 4.0 %collective-permute-start.27 = (bf16[128,512]{1,0:T(8,128)(2,1)}, bf16[128,512]{1,0:T(8,128)(2,1)S(1)}, u32[]{:S(2)}, u32[]{:S(2)}) collective-permute-start(bf16[128,512]{1,0:T(8,128)(2,1)} %get-tuple-element.101), channel_id=1, source_target_pairs={{0,1},{1,0},{2,3},{3,2},{4,5},{5,4},{6,7},{7,6},{8,9},{9,8},{10,11... | collective-permute-start | bytes 393224 | tf_op jit(solution)/shard_map/ppermute | solution.py:274
  121.7 5.6 %collective-permute-start.36 = (bf16[128,512]{1,0:T(8,128)(2,1)}, bf16[128,512]{1,0:T(8,128)(2,1)S(1)}, u32[]{:S(2)}, u32[]{:S(2)}) collective-permute-start(bf16[128,512]{1,0:T(8,128)(2,1)} %get-tuple-element.118), channel_id=1, source_target_pairs={{0,17},{1,16},{2,19},{3,18},{4,21},{5,20},{6,23},{7,22},{8,25},{9,... | collective-permute-start | bytes 393224 | tf_op jit(solution)/shard_map/ppermute | solution.py:274
  123.0 7.4 %collective-permute-start.32 = (bf16[128,512]{1,0:T(8,128)(2,1)}, bf16[128,512]{1,0:T(8,128)(2,1)S(1)}, u32[]{:S(2)}, u32[]{:S(2)}) collective-permute-start(bf16[128,512]{1,0:T(8,128)(2,1)} %get-tuple-element.110), channel_id=1, source_target_pairs={{0,16},{1,17},{2,18},{3,19},{4,20},{5,21},{6,22},{7,23},{8,24},{9,... | collective-permute-start | bytes 393224 | tf_op jit(solution)/shard_map/ppermute | solution.py:274
  (5 other events, 3.6 us)

commit v5 on v4

--- a/solution.py
+++ b/solution.py
@@ -23,7 +23,7 @@
 ROW = LAT + ROPE
 EXT = 640
 VMEM_LIMIT = 20 * 1024 * 1024
-CALLS = ((0, 0, 2), (0, 2, 2), (1, 0, 2), (1, 2, 2))
+CALLS = ((0, 0, 4), (1, 0, 2), (1, 2, 2))
 SMEM = pltpu.SMEM
 VMEM = pltpu.VMEM
 
@@ -255,6 +255,10 @@
     return jax.ShapeDtypeStruct(dims, kind)
 
 
+def in_hbm(*arrays):
+    return [pltpu.with_memory_space_constraint(array, pltpu.HBM) for array in arrays]
+
+
 def body(q_heads, kv_latent, latent_gain, w_up, page_ranks, lengths):
     tok = q_heads.shape[0]
     size = lax.axis_size("ctx")
@@ -274,8 +278,6 @@
         return lax.ppermute(array, ("groups", "ctx"), pairs)
 
     def send_in_quad(array, r):
-        if r == 1 and len(group_stream.arrived) < 4:
-            array = tie(array, weights[0][outer if outer else 0])
         return quad_swap(array, r) if r == 1 else group_stream.send(quad_swap, array, r)
 
     def around(array, by):
@@ -284,7 +286,7 @@
     def inner_swap(array):
         return lax.ppermute(array, "ctx", [(i, i ^ 2) for i in range(size)])
 
-    def along_and_across(pieces):
+    def along_and_across(pieces, share_rows, gates):
         count = len(pieces)
         turns = [(k - j, j) for k in range(outer + count) for j in range(count)]
         lines = [[piece] for piece in pieces]
@@ -296,8 +298,11 @@
             if k:
                 at = len(outer_done)
                 before = outer_done[-2:-1] + ([inner_done[max(0, at - 2)]] if at else [])
+                before += gates.get(at, [])
                 outer_done.append(around(tie(lines[j][-1], *before), 4))
                 lines[j].append(outer_done[-1])
+                if not at:
+                    share_rows(inner_done[0], outer_done[0])
             sides[j].append(inner_swap(tie(lines[j][k], *inner_done[-2:-1])))
             inner_done.append(sides[j][-1])
         return [line + side for line, side in zip(lines, sides)]
@@ -327,8 +332,7 @@
             scratch_shapes=[pltpu.SemaphoreType.DMA((2 * CHUNKS,))],
             compiler_params=params,
             name="pair",
-        )(quarter_info, w_up, got)
-        weights = along_and_across(pairs_of_rows)
+        )(quarter_info, *in_hbm(w_up), got)
     else:
         keep = lax.dynamic_slice_in_dim(w_up, quarter * width, width, 1)
         even = mine % 2 == 0
@@ -374,7 +378,11 @@
         ],
         compiler_params=alone,
         name="rows",
-    )(mine_info, lengths, kv_latent.T, latent_gain[None, :], page_ranks.T, frequency)
+    )(
+        mine_info,
+        lengths,
+        *in_hbm(kv_latent.T, latent_gain[None, :], page_ranks.T, frequency),
+    )
 
     queries = pl.pallas_call(
         query_kernel,
@@ -383,30 +391,37 @@
         in_specs=[smem, block(*q_heads.shape), block(tok, 128), block(tok, 128)],
         out_specs=[block(tok, h * (NOPE + ROPE)) for h in CHUNK_HEADS] * QUAD,
         compiler_params=params,
+        cost_estimate=pl.CostEstimate(
+            flops=0, bytes_accessed=4 * q_heads.size, transcendentals=0
+        ),
         name="queries",
-    )(quarter_info, q_heads, cosine, sine)
-
-    both_groups = jnp.concatenate([rows, group_stream.send(quad_swap, rows, 2)], axis=0)
-    behind = from_behind(both_groups, 2, False)
-    far_behind = from_behind(both_groups, 4, True)
-    own_rows = jnp.concatenate([both_groups, behind, far_behind], axis=0)
-    other_rows = quad_swap(own_rows, 1)
-
-    moved = [
-        [
-            queries[r * CHUNKS + j] if r == 0 else send_in_quad(queries[r * CHUNKS + j], r)
-            for r in range(QUAD)
-        ]
+    )(quarter_info, *in_hbm(q_heads), tie(cosine, pairs_of_rows[0] if outer else got), sine)
+
+    shared = []
+
+    def share_rows(*others):
+        swapped = quad_swap(tie(rows, queries[0], *others), 2)
+        both_groups = jnp.concatenate([rows, swapped], axis=0)
+        behind = from_behind(both_groups, 2, False)
+        far_behind = from_behind(both_groups, 4, True)
+        own_rows = jnp.concatenate([both_groups, behind, far_behind], axis=0)
+        shared.extend([own_rows, quad_swap(own_rows, 1)])
+
+    across = [
+        [group_stream.send(quad_swap, queries[r * CHUNKS + j], r) for r in (2, 3)]
         for j in range(CHUNKS)
     ]
-
-    outgoing = tie(outgoing, moved[0][2])
-    arrived = lax.all_to_all(
-        outgoing.reshape(size, slot_count, ROW), "ctx", split_axis=0, concat_axis=0, tiled=True
-    )
-    decode_cache = arrived.reshape(size * slot_count, ROW)
-
-    mine_info, decode_cache = lax.optimization_barrier((mine_info, decode_cache))
+    if outer:
+        gates = {3: [across[0][0]], 4: [across[0][1]], 5: [across[1][0]]}
+        weights = along_and_across(pairs_of_rows, share_rows, gates)
+    else:
+        share_rows()
+    own_rows, other_rows = shared
+    moved = [
+        [queries[j], quad_swap(tie(queries[CHUNKS + j], across[j][0]), 1)] + across[j]
+        for j in range(CHUNKS)
+    ]
+
     window = (REACH + 2) * tok
 
     def attend(j, first, steps):
@@ -445,6 +460,14 @@
         parts = attend(*call)
         results.append([parts[0]] + [send_in_quad(parts[r], r) for r in range(1, QUAD)])
     pieces = [one[r] for r in range(QUAD) for one in results]
+    arrived = lax.all_to_all(
+        tie(outgoing, pieces[len(CALLS) - 1]).reshape(size, slot_count, ROW),
+        "ctx",
+        split_axis=0,
+        concat_axis=0,
+        tiled=True,
+    )
+    decode_cache = arrived.reshape(size * slot_count, ROW)
     attn_out = pl.pallas_call(
         gather_kernel,
         out_shape=shape((tok, H * VDIM)),

time: 133 us -> 144 us (1.083)
  waiting for transfers between devices: 29.8 us -> 42.4 us
  Pallas kernels: 35.6 us -> 32.7 us
  starting transfers between devices: 44.8 us -> 47.4 us
    ppermute x21 -> x18, waiting for transfers between devices: 8.48 us -> 20.5 us  [quad_swap(): return lax.ppermute(array, ('groups', 'ctx'), pairs)]
    ppermute x6, starting transfers between devices: 9.84 us -> 17.4 us  [around(): lax.ppermute(array, 'ctx', [(i, (i + by) % size) for i in range(size)])]
    pallas_call x4 -> x3, Pallas kernels: 29.4 us -> 24.6 us  [attend(): pl.pallas_call(functools.partial(attend_kernel, outer), grid=(steps,), ou...]
    ppermute x8, waiting for transfers between devices: 14.4 us -> 19.1 us  [inner_swap(): return lax.ppermute(array, 'ctx', [(i, i ^ 2) for i in range(size)])]
    ppermute x6, waiting for transfers between devices: 6.95 us -> 2.69 us  [around(): lax.ppermute(array, 'ctx', [(i, (i + by) % size) for i in range(size)])]
    ppermute x21 -> x18, starting transfers between devices: 13.7 us -> 9.95 us  [quad_swap(): return lax.ppermute(array, ('groups', 'ctx'), pairs)]
    ppermute x8, starting transfers between devices: 10.2 us -> 12.2 us  [inner_swap(): return lax.ppermute(array, 'ctx', [(i, i ^ 2) for i in range(size)])]
    all_to_all x1, starting transfers between devices: 6.63 us -> 4.65 us  [body(): lax.all_to_all(tie(outgoing, pieces[len(CALLS) - 1]).reshape(size, slot_c...]
  transfers between devices with their start and end apart: 38 -> 35, of which waited for: 9 -> 16; matrix products, arithmetic and copies ran while one was open for 2% -> 0% of each run, Pallas kernels for 24% -> 22%
where the time goes in v5:
time: 144 us; the launch traced here: 143 us
  starting transfers between devices  47.4 us (33%)
  waiting for transfers between devices  42.4 us (29%)
  Pallas kernels  32.7 us (23%)
  local copies, waits for them, and re-layouts  19.7 us (14%)
    pallas_call x3, Pallas kernels, attend(): pl.pallas_call(functools.partial(attend_kernel, outer), grid=(steps,), ou...  24.6 us
    ppermute x18, waiting for transfers between devices, quad_swap(): return lax.ppermute(array, ('groups', 'ctx'), pairs)  20.5 us
    ppermute x8, waiting for transfers between devices, inner_swap(): return lax.ppermute(array, 'ctx', [(i, i ^ 2) for i in range(size)])  19.1 us
    unnamed x97, local copies, waits for them, and re-layouts  18.6 us
    ppermute x6, starting transfers between devices, around(): lax.ppermute(array, 'ctx', [(i, (i + by) % size) for i in range(size)])  17.4 us
    ppermute x8, starting transfers between devices, inner_swap(): return lax.ppermute(array, 'ctx', [(i, i ^ 2) for i in range(size)])  12.2 us
    ppermute x18, starting transfers between devices, quad_swap(): return lax.ppermute(array, ('groups', 'ctx'), pairs)  9.95 us
    all_to_all x1, starting transfers between devices, body(): lax.all_to_all(tie(outgoing, pieces[len(CALLS) - 1]).reshape(size, slot_c...  4.65 us
  transfers between devices with their start and end apart: 35, of which 16 were waited for; matrix products, arithmetic and copies ran while one was open for 0% of the time, Pallas kernels for 22%

profile of v5, /device:TPU:0, one launch (start us, length us, event | category | flops | bytes accessed | tf_op | source)
XLA Modules:
  0.0 143.3 jit_solution(12800613969563444659)
XLA Ops:
  0.6 1.0 constant_dynamic-slice_fusion
  2.1 1.2 collective-permute-done.got
  3.3 1.0 pair.1
  4.3 3.0 %collective-permute-start.1 = (bf16[64,2048]{1,0:T(8,128)(2,1)S(1)}, bf16[64,2048]{1,0:T(8,128)(2,1)S(1)}, u32[]{:S(2)}, u32[]{:S(2)}) collective-permute-start(bf16[64,2048]{1,0:T(8,128)(2,1)S(1)} %get-tuple-element.58.refs_0_), channel_id=1, source_target_pairs={{0,2},{1,3},{2,0},{3,1},{4,6},{5,7},{6,4},{7,5},{8,10},{9,11},{10,... | collective-permute-start | bytes 786440 | tf_op jit(solution)/shard_map/ppermute | solution.py:287
  7.3 1.6 %collective-permute-start.2 = (bf16[64,2048]{1,0:T(8,128)(2,1)S(1)}, bf16[64,2048]{1,0:T(8,128)(2,1)}, u32[]{:S(2)}, u32[]{:S(2)}) collective-permute-start(bf16[64,2048]{1,0:T(8,128)(2,1)S(1)} %get-tuple-element.58.refs_0_), channel_id=1, source_target_pairs={{0,4},{1,5},{2,6},{3,7},{4,8},{5,9},{6,10},{7,11},{8,12},{9,13},{1... | collective-permute-start | bytes 786440 | tf_op jit(solution)/shard_map/ppermute | solution.py:284
  8.9 2.3 %rows.1 = (bf16[128,640]{1,0:T(8,128)(2,1)}, f32[128,128]{1,0:T(8,128)}, f32[128,128]{1,0:T(8,128)}, bf16[256,576]{1,0:T(8,128)(2,1)}) custom-call(s32[1]{0:T(128)} %bitcast.1.info, s32[8]{0:T(128)} %lengths, bf16[576,128]{1,0:T(8,128)(2,1)} %bitcast.8, f32[1,512]{1,0:T(1,128)} %bitcast.9, s32[1,128]{1,0:T(1,128)} %bitcast.10, f32[1,128]{1,0:T(1,128)} %constant.30.clone.freq), custom_call_target="tpu_custom_call" | custom-call | tf_op jit(solution)/shard_map/rows/pallas_call | solution.py:363
  11.2 0.8 copy-done
  12.0 0.8 copy-done.1
  12.9 3.3 %queries.1 = (bf16[128,1536]{1,0:T(8,128)(2,1)S(1)}, bf16[128,1536]{1,0:T(8,128)(2,1)S(1)}, bf16[128,1536]{1,0:T(8,128)(2,1)S(1)}, bf16[128,1536]{1,0:T(8,128)(2...) custom-call(s32[1]{0:T(128)} %bitcast.info, ...), custom_call_target="tpu_custom_call" | custom-call | bytes 6291456 | tf_op jit(solution)/shard_map/queries/pallas_call | solution.py:387
  16.2 1.1 collective-permute-done.2.refs_1_
  17.3 1.5 %collective-permute-start.3 = (bf16[128,640]{1,0:T(8,128)(2,1)S(1)}, bf16[128,640]{1,0:T(8,128)(2,1)S(1)}, u32[]{:S(2)}, u32[]{:S(2)}) collective-permute-start(bf16[128,640]{1,0:T(8,128)(2,1)S(1)} %copy-done.46), channel_id=1, source_target_pairs={{0,16},{1,17},{2,18},{3,19},{4,20},{5,21},{6,22},{7,23},{8,24},{9,... | collective-permute-start | bytes 491528 | tf_op jit(solution)/shard_map/ppermute | solution.py:278
  19.5 5.0 %collective-permute-done.3 = bf16[128,640]{1,0:T(8,128)(2,1)S(1)} collective-permute-done((bf16[128,640]{1,0:T(8,128)(2,1)S(1)}, bf16[128,640]{1,0:T(8,128)(2,1)S(1)}, u32[]{:S(2)}, u32[]{:S(2)}) %collective-permute-start.3) | collective-permute-done | bytes 163872 | tf_op jit(solution)/shard_map/ppermute | solution.py:278
  24.5 2.4 %collective-permute-start.4 = (bf16[256,640]{1,0:T(8,128)(2,1)S(1)}, bf16[256,640]{1,0:T(8,128)(2,1)S(1)}, u32[]{:S(2)}, u32[]{:S(2)}) collective-permute-start(bf16[256,640]{1,0:T(8,128)(2,1)S(1)} %get-tuple-element.108), channel_id=1, source_target_pairs={{0,2},{1,3},{2,4},{3,5},{4,6},{5,7},{6,8},{7,9},{8,10},{9,11},{10,... | collective-permute-start | bytes 983048 | tf_op jit(solution)/shard_map/ppermute | solution.py:314
  27.0 0.7 collective-permute-start.5
  27.7 1.1 collective-permute-start.7
  28.8 2.2 %collective-permute-done.9.refs_10_.refs_14_ = bf16[128,1536]{1,0:T(8,128)(2,1)S(1)} collective-permute-done((bf16[128,1536]{1,0:T(8,128)(2,1)S(1)}, bf16[128,1536]{1,0:T(8,128)(2,1)S(1)}, u32[]{:S(2)}, u32[]{:S(2)}) %collective-permute-start.9) | collective-permute-done | bytes 393248 | tf_op jit(solution)/shard_map/ppermute | solution.py:278
  31.7 6.8 %collective-permute-start.15 = (bf16[64,2048]{1,0:T(8,128)(2,1)S(1)}, bf16[64,2048]{1,0:T(8,128)(2,1)S(1)}, u32[]{:S(2)}, u32[]{:S(2)}) collective-permute-start(bf16[64,2048]{1,0:T(8,128)(2,1)S(1)} %get-tuple-element.74.refs_0_), channel_id=1, source_target_pairs={{0,4},{1,5},{2,6},{3,7},{4,8},{5,9},{6,10},{7,11},{8,12},{9,13},{1... | collective-permute-start | bytes 786440 | tf_op jit(solution)/shard_map/ppermute | solution.py:284
  38.8 1.7 %collective-permute-done.8.refs_5_ = bf16[64,2048]{1,0:T(8,128)(2,1)S(1)} collective-permute-done((bf16[64,2048]{1,0:T(8,128)(2,1)}, bf16[64,2048]{1,0:T(8,128)(2,1)S(1)}, u32[]{:S(2)}, u32[]{:S(2)}) %collective-permute-start.8) | collective-permute-done | bytes 262176 | tf_op jit(solution)/shard_map/ppermute | solution.py:287
  40.5 0.7 copy-done.22
  41.2 0.8 copy-done.4
  42.0 4.2 %collective-permute-start.10 = (bf16[64,2048]{1,0:T(8,128)(2,1)S(1)}, bf16[64,2048]{1,0:T(8,128)(2,1)S(1)}, u32[]{:S(2)}, u32[]{:S(2)}) collective-permute-start(bf16[64,2048]{1,0:T(8,128)(2,1)S(1)} %collective-permute-done.7.refs_2_), channel_id=1, source_target_pairs={{0,4},{1,5},{2,6},{3,7},{4,8},{5,9},{6,10},{7,11},{8,12},{9,13},{1... | collective-permute-start | bytes 786440 | tf_op jit(solution)/shard_map/ppermute | solution.py:284
  46.2 1.5 %collective-permute-start.11 = (bf16[64,2048]{1,0:T(8,128)(2,1)S(1)}, bf16[64,2048]{1,0:T(8,128)(2,1)S(1)}, u32[]{:S(2)}, u32[]{:S(2)}) collective-permute-start(bf16[64,2048]{1,0:T(8,128)(2,1)S(1)} %collective-permute-done.7.refs_2_), channel_id=1, source_target_pairs={{0,2},{1,3},{2,0},{3,1},{4,6},{5,7},{6,4},{7,5},{8,10},{9,11},{10,... | collective-permute-start | bytes 786440 | tf_op jit(solution)/shard_map/ppermute | solution.py:287
  47.7 0.7 copy-done.18
  48.4 2.3 %collective-permute-start.17 = (bf16[64,2048]{1,0:T(8,128)(2,1)S(1)}, bf16[64,2048]{1,0:T(8,128)(2,1)S(1)}, u32[]{:S(2)}, u32[]{:S(2)}) collective-permute-start(bf16[64,2048]{1,0:T(8,128)(2,1)S(1)} %collective-permute-done.15.refs_1_), channel_id=1, source_target_pairs={{0,4},{1,5},{2,6},{3,7},{4,8},{5,9},{6,10},{7,11},{8,12},{9,13},{1... | collective-permute-start | bytes 786440 | tf_op jit(solution)/shard_map/ppermute | solution.py:284
  50.7 1.4 collective-permute-done.10.refs_3_
  52.1 4.1 %collective-permute-start.20 = (bf16[64,2048]{1,0:T(8,128)(2,1)S(1)}, bf16[64,2048]{1,0:T(8,128)(2,1)S(1)}, u32[]{:S(2)}, u32[]{:S(2)}) collective-permute-start(bf16[64,2048]{1,0:T(8,128)(2,1)S(1)} %collective-permute-done.15.refs_1_), channel_id=1, source_target_pairs={{0,2},{1,3},{2,0},{3,1},{4,6},{5,7},{6,4},{7,5},{8,10},{9,11},{10,... | collective-permute-start | bytes 786440 | tf_op jit(solution)/shard_map/ppermute | solution.py:287
  56.2 0.7 copy-done.30
  57.0 0.8 copy-done.28
  58.1 1.5 %collective-permute-start.19 = (bf16[64,2048]{1,0:T(8,128)(2,1)S(1)}, bf16[64,2048]{1,0:T(8,128)(2,1)S(1)}, u32[]{:S(2)}, u32[]{:S(2)}) collective-permute-start(bf16[64,2048]{1,0:T(8,128)(2,1)S(1)} %collective-permute-done.17.refs_2_), channel_id=1, source_target_pairs={{0,4},{1,5},{2,6},{3,7},{4,8},{5,9},{6,10},{7,11},{8,12},{9,13},{1... | collective-permute-start | bytes 786440 | tf_op jit(solution)/shard_map/ppermute | solution.py:284
  59.5 3.5 %collective-permute-done.20.refs_5_ = bf16[64,2048]{1,0:T(8,128)(2,1)S(1)} collective-permute-done((bf16[64,2048]{1,0:T(8,128)(2,1)S(1)}, bf16[64,2048]{1,0:T(8,128)(2,1)S(1)}, u32[]{:S(2)}, u32[]{:S(2)}) %collective-permute-start.20) | collective-permute-done | bytes 262176 | tf_op jit(solution)/shard_map/ppermute | solution.py:287
  63.0 4.1 %collective-permute-done.12.refs_7_ = bf16[64,2048]{1,0:T(8,128)(2,1)S(1)} collective-permute-done((bf16[64,2048]{1,0:T(8,128)(2,1)S(1)}, bf16[64,2048]{1,0:T(8,128)(2,1)S(1)}, u32[]{:S(2)}, u32[]{:S(2)}) %collective-permute-start.12) | collective-permute-done | bytes 262176 | tf_op jit(solution)/shard_map/ppermute | solution.py:287
  67.1 0.7 copy-done.38
  67.8 1.7 %collective-permute-start.21 = (bf16[64,2048]{1,0:T(8,128)(2,1)S(1)}, bf16[64,2048]{1,0:T(8,128)(2,1)S(1)}, u32[]{:S(2)}, u32[]{:S(2)}) collective-permute-start(bf16[64,2048]{1,0:T(8,128)(2,1)S(1)} %collective-permute-done.17.refs_2_), channel_id=1, source_target_pairs={{0,2},{1,3},{2,0},{3,1},{4,6},{5,7},{6,4},{7,5},{8,10},{9,11},{10,... | collective-permute-start | bytes 786440 | tf_op jit(solution)/shard_map/ppermute | solution.py:287
  69.5 1.1 collective-permute-start.22
  70.6 6.4 %collective-permute-done.21.refs_6_ = bf16[64,2048]{1,0:T(8,128)(2,1)S(1)} collective-permute-done((bf16[64,2048]{1,0:T(8,128)(2,1)S(1)}, bf16[64,2048]{1,0:T(8,128)(2,1)S(1)}, u32[]{:S(2)}, u32[]{:S(2)}) %collective-permute-start.21) | collective-permute-done | bytes 262176 | tf_op jit(solution)/shard_map/ppermute | solution.py:287
  77.0 3.5 %collective-permute-done.22.refs_7_ = bf16[64,2048]{1,0:T(8,128)(2,1)S(1)} collective-permute-done((bf16[64,2048]{1,0:T(8,128)(2,1)S(1)}, bf16[64,2048]{1,0:T(8,128)(2,1)S(1)}, u32[]{:S(2)}, u32[]{:S(2)}) %collective-permute-start.22) | collective-permute-done | bytes 262176 | tf_op jit(solution)/shard_map/ppermute | solution.py:287
  80.5 6.1 %attend.5 = (bf16[128,512]{1,0:T(8,128)(2,1)S(1)}, bf16[128,512]{1,0:T(8,128)(2,1)S(1)}, bf16[128,512]{1,0:T(8,128)(2,1)S(1)}, bf16[128,512]{1,0:T(8,128)(2,1)S(1)}) custom-call(s32[1]{0:T(128)} %bitcast.1.info, bf16[768,640]{1,0:T(8,128)(2,1)S(1)} %constant_dynamic-update-slice_fusion.2.own, bf16[768,640]{1,0:T(8,128)(2,1)S(1)} %collective-permute-done.6.other, ...), custom_call_target="tpu_custom_call" | custom-call | flops 2181038080 | bytes 4194304 | tf_op jit(solution)/shard_map/attend/pallas_call | solution.py:430
  86.8 0.6 copy-done.40
  87.4 0.7 copy-done.42
  88.1 0.7 copy-done.44
  88.7 4.7 %all-to-all-start = ((bf16[16,16,576]{2,1,0:T(8,128)(2,1)}), bf16[16,16,576]{2,1,0:T(8,128)(2,1)}, u32[]{:S(2)}, u32[]{:S(2)}) async-start(bf16[16,16,576]{2,1,0:T(8,128)(2,1)} %bitcast.7), calls=%async_computation | async-start | bytes 655360 | tf_op jit(solution)/shard_map/all_to_all | solution.py:463
  93.4 1.0 copy-done.3
  94.4 1.0 copy-done.5
  95.4 0.9 copy-done.13
  96.3 0.9 copy-done.15
  97.3 0.9 copy-done.19
  98.2 0.9 copy-done.23
  99.2 0.9 copy-done.29
  100.1 0.9 copy-done.31
  101.1 0.9 copy-done.39
  102.1 12.3 %attend.3 = (bf16[128,1024]{1,0:T(8,128)(2,1)S(1)}, bf16[128,1024]{1,0:T(8,128)(2,1)S(1)}, bf16[128,1024]{1,0:T(8,128)(2,1)S(1)}, bf16[128,1024]{1,0:T(8,128)(2,1)S(1)}) custom-call(s32[1]{0:T(128)} %bitcast.1.info, bf16[768,640]{1,0:T(8,128)(2,1)S(1)} %constant_dynamic-update-slice_fusion.2.own, bf16[768,640]{1,0:T(8,128)(2,1)S(1)} %collective-permute-done.6.other, ...), custom_call_target="tpu_custom_call" | custom-call | flops 4362076160 | bytes 8388608 | tf_op jit(solution)/shard_map/attend/pallas_call | solution.py:430
  114.5 1.0 collective-permute-start.31
  115.4 1.1 collective-permute-start.28
  116.6 6.2 %attend.4 = (bf16[128,512]{1,0:T(8,128)(2,1)S(1)}, bf16[128,512]{1,0:T(8,128)(2,1)S(1)}, bf16[128,512]{1,0:T(8,128)(2,1)S(1)}, bf16[128,512]{1,0:T(8,128)(2,1)S(1)}) custom-call(s32[1]{0:T(128)} %bitcast.1.info, bf16[768,640]{1,0:T(8,128)(2,1)S(1)} %constant_dynamic-update-slice_fusion.2.own, bf16[768,640]{1,0:T(8,128)(2,1)S(1)} %collective-permute-done.6.other, ...), custom_call_target="tpu_custom_call" | custom-call | flops 2181038080 | bytes 4194304 | tf_op jit(solution)/shard_map/attend/pallas_call | solution.py:430
  122.8 1.3 collective-permute-start.32
  124.0 5.2 %collective-permute-done.28.refs_6_ = bf16[128,1024]{1,0:T(8,128)(2,1)S(1)} collective-permute-done((bf16[128,1024]{1,0:T(8,128)(2,1)S(1)}, bf16[128,1024]{1,0:T(8,128)(2,1)S(1)}, u32[]{:S(2)}, u32[]{:S(2)}) %collective-permute-start.28) | collective-permute-done | bytes 262176 | tf_op jit(solution)/shard_map/ppermute | solution.py:278
  129.2 1.0 collective-permute-start.29
  131.1 1.4 collective-permute-start.33
  132.5 2.2 %collective-permute-done.29.refs_7_ = bf16[128,512]{1,0:T(8,128)(2,1)S(1)} collective-permute-done((bf16[128,512]{1,0:T(8,128)(2,1)S(1)}, bf16[128,512]{1,0:T(8,128)(2,1)S(1)}, u32[]{:S(2)}, u32[]{:S(2)}) %collective-permute-start.29) | collective-permute-done | bytes 131104 | tf_op jit(solution)/shard_map/ppermute | solution.py:278
  134.6 1.0 collective-permute-start.30
  135.6 0.9 collective-permute-done.33.refs_11_
  136.5 3.4 %collective-permute-done.30.refs_8_ = bf16[128,512]{1,0:T(8,128)(2,1)S(1)} collective-permute-done((bf16[128,512]{1,0:T(8,128)(2,1)S(1)}, bf16[128,512]{1,0:T(8,128)(2,1)S(1)}, u32[]{:S(2)}, u32[]{:S(2)}) %collective-permute-start.30) | collective-permute-done | bytes 131104 | tf_op jit(solution)/shard_map/ppermute | solution.py:278
  140.0 1.4 place.1
  141.4 1.8 %copy.10 = bf16[256,576]{0,1:T(8,128)(2,1)} copy(bf16[256,576]{1,0:T(8,128)(2,1)} %bitcast.6) | data formatting | bytes 589824
  (113 shorter events, 3.5 us)
Async XLA Ops:
  1.6 1.7 %collective-permute-start = (bf16[32,4096]{1,0:T(8,128)(2,1)S(1)}, bf16[32,4096]{1,0:T(8,128)(2,1)S(1)}, u32[]{:S(2)}, u32[]{:S(2)}) collective-permute-start(bf16[32,4096]{1,0:T(8,128)(2,1)S(1)} %constant_dynamic-slice_fusion), channel_id=1, source_target_pairs={{0,1},{1,0},{2,3},{3,2},{4,5},{5,4},{6,7},{7,6},{8,9},{9,8},{10,11... | collective-permute-start | bytes 786440 | tf_op jit(solution)/shard_map/ppermute | solution.py:278
  4.3 82.3 %copy-start.12 = (bf16[64,2048]{1,0:T(8,128)(2,1)}, bf16[64,2048]{1,0:T(8,128)(2,1)S(1)}, u32[]{:S(2)}) copy-start(bf16[64,2048]{1,0:T(8,128)(2,1)S(1)} %get-tuple-element.58.refs_0_) | copy-start | bytes 786436
  4.3 11.9 %collective-permute-start.1 = (bf16[64,2048]{1,0:T(8,128)(2,1)S(1)}, bf16[64,2048]{1,0:T(8,128)(2,1)S(1)}, u32[]{:S(2)}, u32[]{:S(2)}) collective-permute-start(bf16[64,2048]{1,0:T(8,128)(2,1)S(1)} %get-tuple-element.58.refs_0_), channel_id=1, source_target_pairs={{0,2},{1,3},{2,0},{3,1},{4,6},{5,7},{6,4},{7,5},{8,10},{9,11},{10,... | collective-permute-start | bytes 786440 | tf_op jit(solution)/shard_map/ppermute | solution.py:287
  7.3 10.0 %collective-permute-start.2 = (bf16[64,2048]{1,0:T(8,128)(2,1)S(1)}, bf16[64,2048]{1,0:T(8,128)(2,1)}, u32[]{:S(2)}, u32[]{:S(2)}) collective-permute-start(bf16[64,2048]{1,0:T(8,128)(2,1)S(1)} %get-tuple-element.58.refs_0_), channel_id=1, source_target_pairs={{0,4},{1,5},{2,6},{3,7},{4,8},{5,9},{6,10},{7,11},{8,12},{9,13},{1... | collective-permute-start | bytes 786440 | tf_op jit(solution)/shard_map/ppermute | solution.py:284
  12.9 4.5 %copy-start.46 = (bf16[128,640]{1,0:T(8,128)(2,1)S(1)}, bf16[128,640]{1,0:T(8,128)(2,1)}, u32[]{:S(2)}) copy-start(bf16[128,640]{1,0:T(8,128)(2,1)} %get-tuple-element.62) | copy-start | bytes 491524
  16.2 70.4 %copy-start.14 = (bf16[64,2048]{1,0:T(8,128)(2,1)}, bf16[64,2048]{1,0:T(8,128)(2,1)S(1)}, u32[]{:S(2)}) copy-start(bf16[64,2048]{1,0:T(8,128)(2,1)S(1)} %collective-permute-done.1.refs_4_) | copy-start | bytes 786436
  17.3 7.2 %collective-permute-start.3 = (bf16[128,640]{1,0:T(8,128)(2,1)S(1)}, bf16[128,640]{1,0:T(8,128)(2,1)S(1)}, u32[]{:S(2)}, u32[]{:S(2)}) collective-permute-start(bf16[128,640]{1,0:T(8,128)(2,1)S(1)} %copy-done.46), channel_id=1, source_target_pairs={{0,16},{1,17},{2,18},{3,19},{4,20},{5,21},{6,22},{7,23},{8,24},{9,... | collective-permute-start | bytes 491528 | tf_op jit(solution)/shard_map/ppermute | solution.py:278
  18.8 12.2 %collective-permute-start.9 = (bf16[128,1536]{1,0:T(8,128)(2,1)S(1)}, bf16[128,1536]{1,0:T(8,128)(2,1)S(1)}, u32[]{:S(2)}, u32[]{:S(2)}) collective-permute-start(bf16[128,1536]{1,0:T(8,128)(2,1)S(1)} %get-tuple-element.64), channel_id=1, source_target_pairs={{0,16},{1,17},{2,18},{3,19},{4,20},{5,21},{6,22},{7,23},{8,24},{9,... | collective-permute-start | bytes 1179656 | tf_op jit(solution)/shard_map/ppermute | solution.py:278
  24.5 7.2 %collective-permute-start.4 = (bf16[256,640]{1,0:T(8,128)(2,1)S(1)}, bf16[256,640]{1,0:T(8,128)(2,1)S(1)}, u32[]{:S(2)}, u32[]{:S(2)}) collective-permute-start(bf16[256,640]{1,0:T(8,128)(2,1)S(1)} %get-tuple-element.108), channel_id=1, source_target_pairs={{0,2},{1,3},{2,4},{3,5},{4,6},{5,7},{6,8},{7,9},{8,10},{9,11},{10,... | collective-permute-start | bytes 983048 | tf_op jit(solution)/shard_map/ppermute | solution.py:314
  27.0 11.6 %collective-permute-start.5 = (bf16[256,640]{1,0:T(8,128)(2,1)S(1)}, bf16[256,640]{1,0:T(8,128)(2,1)S(1)}, u32[]{:S(2)}, u32[]{:S(2)}) collective-permute-start(bf16[256,640]{1,0:T(8,128)(2,1)S(1)} %get-tuple-element.108), channel_id=1, source_target_pairs={{1,5},{3,7},{5,9},{7,11},{9,13},{11,15},{17,21},{19,23},{21,25},{2... | collective-permute-start | bytes 983048 | tf_op jit(solution)/shard_map/ppermute | solution.py:314
  27.6 13.6 %collective-permute-start.14 = (bf16[128,1536]{1,0:T(8,128)(2,1)S(1)}, bf16[128,1536]{1,0:T(8,128)(2,1)S(1)}, u32[]{:S(2)}, u32[]{:S(2)}) collective-permute-start(bf16[128,1536]{1,0:T(8,128)(2,1)S(1)} %get-tuple-element.70), channel_id=1, source_target_pairs={{0,17},{1,16},{2,19},{3,18},{4,21},{5,20},{6,23},{7,22},{8,25},{9,... | collective-permute-start | bytes 1179656 | tf_op jit(solution)/shard_map/ppermute | solution.py:278
  27.7 11.0 %collective-permute-start.7 = (bf16[64,2048]{1,0:T(8,128)(2,1)}, bf16[64,2048]{1,0:T(8,128)(2,1)S(1)}, u32[]{:S(2)}, u32[]{:S(2)}) collective-permute-start(bf16[64,2048]{1,0:T(8,128)(2,1)} %collective-permute-done.2.refs_1_), channel_id=1, source_target_pairs={{0,4},{1,5},{2,6},{3,7},{4,8},{5,9},{6,10},{7,11},{8,12},{9,13},{1... | collective-permute-start | bytes 786440 | tf_op jit(solution)/shard_map/ppermute | solution.py:284
  31.1 7.6 %copy-start.2 = (bf16[128,1536]{1,0:T(8,128)(2,1)}, bf16[128,1536]{1,0:T(8,128)(2,1)S(1)}, u32[]{:S(2)}) copy-start(bf16[128,1536]{1,0:T(8,128)(2,1)S(1)} %collective-permute-done.9.refs_10_.refs_14_) | copy-start | bytes 1179652
  31.1 9.5 %collective-permute-start.8 = (bf16[64,2048]{1,0:T(8,128)(2,1)}, bf16[64,2048]{1,0:T(8,128)(2,1)S(1)}, u32[]{:S(2)}, u32[]{:S(2)}) collective-permute-start(bf16[64,2048]{1,0:T(8,128)(2,1)} %collective-permute-done.2.refs_1_), channel_id=1, source_target_pairs={{0,2},{1,3},{2,0},{3,1},{4,6},{5,7},{6,4},{7,5},{8,10},{9,11},{10,... | collective-permute-start | bytes 786440 | tf_op jit(solution)/shard_map/ppermute | solution.py:287
  31.7 14.5 %collective-permute-start.15 = (bf16[64,2048]{1,0:T(8,128)(2,1)S(1)}, bf16[64,2048]{1,0:T(8,128)(2,1)S(1)}, u32[]{:S(2)}, u32[]{:S(2)}) collective-permute-start(bf16[64,2048]{1,0:T(8,128)(2,1)S(1)} %get-tuple-element.74.refs_0_), channel_id=1, source_target_pairs={{0,4},{1,5},{2,6},{3,7},{4,8},{5,9},{6,10},{7,11},{8,12},{9,13},{1... | collective-permute-start | bytes 786440 | tf_op jit(solution)/shard_map/ppermute | solution.py:284
  38.6 9.8 %collective-permute-start.16 = (bf16[64,2048]{1,0:T(8,128)(2,1)S(1)}, bf16[64,2048]{1,0:T(8,128)(2,1)S(1)}, u32[]{:S(2)}, u32[]{:S(2)}) collective-permute-start(bf16[64,2048]{1,0:T(8,128)(2,1)S(1)} %get-tuple-element.74.refs_0_), channel_id=1, source_target_pairs={{0,2},{1,3},{2,0},{3,1},{4,6},{5,7},{6,4},{7,5},{8,10},{9,11},{10,... | collective-permute-start | bytes 786440 | tf_op jit(solution)/shard_map/ppermute | solution.py:287
  38.7 41.8 %collective-permute-start.6 = (bf16[768,640]{1,0:T(8,128)(2,1)S(1)}, bf16[768,640]{1,0:T(8,128)(2,1)S(1)}, u32[]{:S(2)}, u32[]{:S(2)}) collective-permute-start(bf16[768,640]{1,0:T(8,128)(2,1)S(1)} %constant_dynamic-update-slice_fusion.2.own), channel_id=1, source_target_pairs={{0,1},{1,0},{2,3},{3,2},{4,5},{5,4},{6,7},{7,6},{8,9},{9,8},{10,11... | collective-permute-start | bytes 2949128 | tf_op jit(solution)/shard_map/ppermute | solution.py:278
  41.2 15.7 %collective-permute-start.18 = (bf16[128,1536]{1,0:T(8,128)(2,1)S(1)}, bf16[128,1536]{1,0:T(8,128)(2,1)S(1)}, u32[]{:S(2)}, u32[]{:S(2)}) collective-permute-start(bf16[128,1536]{1,0:T(8,128)(2,1)S(1)} %get-tuple-element.77), channel_id=1, source_target_pairs={{0,16},{1,17},{2,18},{3,19},{4,20},{5,21},{6,22},{7,23},{8,24},{9,... | collective-permute-start | bytes 1179656 | tf_op jit(solution)/shard_map/ppermute | solution.py:278
  42.0 10.1 %collective-permute-start.10 = (bf16[64,2048]{1,0:T(8,128)(2,1)S(1)}, bf16[64,2048]{1,0:T(8,128)(2,1)S(1)}, u32[]{:S(2)}, u32[]{:S(2)}) collective-permute-start(bf16[64,2048]{1,0:T(8,128)(2,1)S(1)} %collective-permute-done.7.refs_2_), channel_id=1, source_target_pairs={{0,4},{1,5},{2,6},{3,7},{4,8},{5,9},{6,10},{7,11},{8,12},{9,13},{1... | collective-permute-start | bytes 786440 | tf_op jit(solution)/shard_map/ppermute | solution.py:284
  46.2 40.5 %copy-start.16 = (bf16[64,2048]{1,0:T(8,128)(2,1)}, bf16[64,2048]{1,0:T(8,128)(2,1)S(1)}, u32[]{:S(2)}) copy-start(bf16[64,2048]{1,0:T(8,128)(2,1)S(1)} %collective-permute-done.15.refs_1_) | copy-start | bytes 786436
  46.2 10.1 %collective-permute-start.11 = (bf16[64,2048]{1,0:T(8,128)(2,1)S(1)}, bf16[64,2048]{1,0:T(8,128)(2,1)S(1)}, u32[]{:S(2)}, u32[]{:S(2)}) collective-permute-start(bf16[64,2048]{1,0:T(8,128)(2,1)S(1)} %collective-permute-done.7.refs_2_), channel_id=1, source_target_pairs={{0,2},{1,3},{2,0},{3,1},{4,6},{5,7},{6,4},{7,5},{8,10},{9,11},{10,... | collective-permute-start | bytes 786440 | tf_op jit(solution)/shard_map/ppermute | solution.py:287
  48.4 38.3 %copy-start.20 = (bf16[64,2048]{1,0:T(8,128)(2,1)}, bf16[64,2048]{1,0:T(8,128)(2,1)S(1)}, u32[]{:S(2)}) copy-start(bf16[64,2048]{1,0:T(8,128)(2,1)S(1)} %collective-permute-done.16.refs_4_) | copy-start | bytes 786436
  48.4 9.7 %collective-permute-start.17 = (bf16[64,2048]{1,0:T(8,128)(2,1)S(1)}, bf16[64,2048]{1,0:T(8,128)(2,1)S(1)}, u32[]{:S(2)}, u32[]{:S(2)}) collective-permute-start(bf16[64,2048]{1,0:T(8,128)(2,1)S(1)} %collective-permute-done.15.refs_1_), channel_id=1, source_target_pairs={{0,4},{1,5},{2,6},{3,7},{4,8},{5,9},{6,10},{7,11},{8,12},{9,13},{1... | collective-permute-start | bytes 786440 | tf_op jit(solution)/shard_map/ppermute | solution.py:284
  52.1 10.9 %collective-permute-start.20 = (bf16[64,2048]{1,0:T(8,128)(2,1)S(1)}, bf16[64,2048]{1,0:T(8,128)(2,1)S(1)}, u32[]{:S(2)}, u32[]{:S(2)}) collective-permute-start(bf16[64,2048]{1,0:T(8,128)(2,1)S(1)} %collective-permute-done.15.refs_1_), channel_id=1, source_target_pairs={{0,2},{1,3},{2,0},{3,1},{4,6},{5,7},{6,4},{7,5},{8,10},{9,11},{10,... | collective-permute-start | bytes 786440 | tf_op jit(solution)/shard_map/ppermute | solution.py:287
  56.9 13.7 %collective-permute-start.24 = (bf16[128,1536]{1,0:T(8,128)(2,1)S(1)}, bf16[128,1536]{1,0:T(8,128)(2,1)S(1)}, u32[]{:S(2)}, u32[]{:S(2)}) collective-permute-start(bf16[128,1536]{1,0:T(8,128)(2,1)S(1)} %get-tuple-element.86), channel_id=1, source_target_pairs={{0,17},{1,16},{2,19},{3,18},{4,21},{5,20},{6,23},{7,22},{8,25},{9,... | collective-permute-start | bytes 1179656 | tf_op jit(solution)/shard_map/ppermute | solution.py:278
  56.9 29.7 %copy-start.6 = (bf16[128,1536]{1,0:T(8,128)(2,1)}, bf16[128,1536]{1,0:T(8,128)(2,1)S(1)}, u32[]{:S(2)}) copy-start(bf16[128,1536]{1,0:T(8,128)(2,1)S(1)} %collective-permute-done.18.refs_10_.refs_14_) | copy-start | bytes 1179652
  57.0 10.1 %collective-permute-start.12 = (bf16[64,2048]{1,0:T(8,128)(2,1)S(1)}, bf16[64,2048]{1,0:T(8,128)(2,1)S(1)}, u32[]{:S(2)}, u32[]{:S(2)}) collective-permute-start(bf16[64,2048]{1,0:T(8,128)(2,1)S(1)} %collective-permute-done.10.refs_3_), channel_id=1, source_target_pairs={{0,2},{1,3},{2,0},{3,1},{4,6},{5,7},{6,4},{7,5},{8,10},{9,11},{10,... | collective-permute-start | bytes 786440 | tf_op jit(solution)/shard_map/ppermute | solution.py:287
  58.1 28.6 %copy-start.24 = (bf16[64,2048]{1,0:T(8,128)(2,1)}, bf16[64,2048]{1,0:T(8,128)(2,1)S(1)}, u32[]{:S(2)}) copy-start(bf16[64,2048]{1,0:T(8,128)(2,1)S(1)} %collective-permute-done.17.refs_2_) | copy-start | bytes 786436
  58.1 11.5 %collective-permute-start.19 = (bf16[64,2048]{1,0:T(8,128)(2,1)S(1)}, bf16[64,2048]{1,0:T(8,128)(2,1)S(1)}, u32[]{:S(2)}, u32[]{:S(2)}) collective-permute-start(bf16[64,2048]{1,0:T(8,128)(2,1)S(1)} %collective-permute-done.17.refs_2_), channel_id=1, source_target_pairs={{0,4},{1,5},{2,6},{3,7},{4,8},{5,9},{6,10},{7,11},{8,12},{9,13},{1... | collective-permute-start | bytes 786440 | tf_op jit(solution)/shard_map/ppermute | solution.py:284
  63.0 23.7 %copy-start.26 = (bf16[64,2048]{1,0:T(8,128)(2,1)}, bf16[64,2048]{1,0:T(8,128)(2,1)S(1)}, u32[]{:S(2)}) copy-start(bf16[64,2048]{1,0:T(8,128)(2,1)S(1)} %collective-permute-done.20.refs_5_) | copy-start | bytes 786436
  63.0 14.0 %collective-permute-start.23 = (bf16[128,1536]{1,0:T(8,128)(2,1)S(1)}, bf16[128,1536]{1,0:T(8,128)(2,1)S(1)}, u32[]{:S(2)}, u32[]{:S(2)}) collective-permute-start(bf16[128,1536]{1,0:T(8,128)(2,1)S(1)} %get-tuple-element.84), channel_id=1, source_target_pairs={{0,1},{1,0},{2,3},{3,2},{4,5},{5,4},{6,7},{7,6},{8,9},{9,8},{10,11... | collective-permute-start | bytes 1179656 | tf_op jit(solution)/shard_map/ppermute | solution.py:278
  67.8 9.2 %collective-permute-start.21 = (bf16[64,2048]{1,0:T(8,128)(2,1)S(1)}, bf16[64,2048]{1,0:T(8,128)(2,1)S(1)}, u32[]{:S(2)}, u32[]{:S(2)}) collective-permute-start(bf16[64,2048]{1,0:T(8,128)(2,1)S(1)} %collective-permute-done.17.refs_2_), channel_id=1, source_target_pairs={{0,2},{1,3},{2,0},{3,1},{4,6},{5,7},{6,4},{7,5},{8,10},{9,11},{10,... | collective-permute-start | bytes 786440 | tf_op jit(solution)/shard_map/ppermute | solution.py:287
  69.5 17.2 %copy-start.32 = (bf16[64,2048]{1,0:T(8,128)(2,1)}, bf16[64,2048]{1,0:T(8,128)(2,1)S(1)}, u32[]{:S(2)}) copy-start(bf16[64,2048]{1,0:T(8,128)(2,1)S(1)} %collective-permute-done.19.refs_3_) | copy-start | bytes 786436
  69.5 11.0 %collective-permute-start.22 = (bf16[64,2048]{1,0:T(8,128)(2,1)S(1)}, bf16[64,2048]{1,0:T(8,128)(2,1)S(1)}, u32[]{:S(2)}, u32[]{:S(2)}) collective-permute-start(bf16[64,2048]{1,0:T(8,128)(2,1)S(1)} %collective-permute-done.19.refs_3_), channel_id=1, source_target_pairs={{0,2},{1,3},{2,0},{3,1},{4,6},{5,7},{6,4},{7,5},{8,10},{9,11},{10,... | collective-permute-start | bytes 786440 | tf_op jit(solution)/shard_map/ppermute | solution.py:287
  70.6 16.1 %copy-start.8 = (bf16[128,1536]{1,0:T(8,128)(2,1)}, bf16[128,1536]{1,0:T(8,128)(2,1)S(1)}, u32[]{:S(2)}) copy-start(bf16[128,1536]{1,0:T(8,128)(2,1)S(1)} %collective-permute-done.24.refs_11_.refs_15_) | copy-start | bytes 1179652
  70.6 22.8 %collective-permute-start.13 = (bf16[128,1536]{1,0:T(8,128)(2,1)S(1)}, bf16[128,1536]{1,0:T(8,128)(2,1)}, u32[]{:S(2)}, u32[]{:S(2)}) collective-permute-start(bf16[128,1536]{1,0:T(8,128)(2,1)S(1)} %get-tuple-element.69), channel_id=1, source_target_pairs={{0,1},{1,0},{2,3},{3,2},{4,5},{5,4},{6,7},{7,6},{8,9},{9,8},{10,11... | collective-permute-start | bytes 1179656 | tf_op jit(solution)/shard_map/ppermute | solution.py:278
  77.0 9.7 %copy-start.34 = (bf16[64,2048]{1,0:T(8,128)(2,1)}, bf16[64,2048]{1,0:T(8,128)(2,1)S(1)}, u32[]{:S(2)}) copy-start(bf16[64,2048]{1,0:T(8,128)(2,1)S(1)} %collective-permute-done.21.refs_6_) | copy-start | bytes 786436
  77.0 9.7 %copy-start.10 = (bf16[128,1536]{1,0:T(8,128)(2,1)}, bf16[128,1536]{1,0:T(8,128)(2,1)S(1)}, u32[]{:S(2)}) copy-start(bf16[128,1536]{1,0:T(8,128)(2,1)S(1)} %collective-permute-done.23.refs_9_.refs_13_) | copy-start | bytes 1179652
  80.5 6.2 %copy-start.36 = (bf16[64,2048]{1,0:T(8,128)(2,1)}, bf16[64,2048]{1,0:T(8,128)(2,1)S(1)}, u32[]{:S(2)}) copy-start(bf16[64,2048]{1,0:T(8,128)(2,1)S(1)} %collective-permute-done.22.refs_7_) | copy-start | bytes 786436
  88.7 52.7 %all-to-all-start = ((bf16[16,16,576]{2,1,0:T(8,128)(2,1)}), bf16[16,16,576]{2,1,0:T(8,128)(2,1)}, u32[]{:S(2)}, u32[]{:S(2)}) async-start(bf16[16,16,576]{2,1,0:T(8,128)(2,1)} %bitcast.7), calls=%async_computation | async-start | bytes 655360 | tf_op jit(solution)/shard_map/all_to_all | solution.py:463
  93.4 1.0 copy-start.3
  94.4 1.0 copy-start.5
  102.0 14.5 %copy-start.7 = (bf16[128,1536]{1,0:T(8,128)(2,1)S(1)}, bf16[128,1536]{1,0:T(8,128)(2,1)}, u32[]{:S(2)}) copy-start(bf16[128,1536]{1,0:T(8,128)(2,1)} %copy-done.6) | copy-start | bytes 1179652
  102.0 14.5 %copy-start.9 = (bf16[128,1536]{1,0:T(8,128)(2,1)S(1)}, bf16[128,1536]{1,0:T(8,128)(2,1)}, u32[]{:S(2)}) copy-start(bf16[128,1536]{1,0:T(8,128)(2,1)} %copy-done.8) | copy-start | bytes 1179652
  102.1 14.5 %copy-start.11 = (bf16[128,1536]{1,0:T(8,128)(2,1)S(1)}, bf16[128,1536]{1,0:T(8,128)(2,1)}, u32[]{:S(2)}) copy-start(bf16[128,1536]{1,0:T(8,128)(2,1)} %copy-done.10) | copy-start | bytes 1179652
  102.1 14.5 %copy-start.17 = (bf16[64,2048]{1,0:T(8,128)(2,1)S(1)}, bf16[64,2048]{1,0:T(8,128)(2,1)}, u32[]{:S(2)}) copy-start(bf16[64,2048]{1,0:T(8,128)(2,1)} %copy-done.16) | copy-start | bytes 786436
  102.1 14.5 %copy-start.21 = (bf16[64,2048]{1,0:T(8,128)(2,1)S(1)}, bf16[64,2048]{1,0:T(8,128)(2,1)}, u32[]{:S(2)}) copy-start(bf16[64,2048]{1,0:T(8,128)(2,1)} %copy-done.20) | copy-start | bytes 786436
  102.1 14.5 %copy-start.25 = (bf16[64,2048]{1,0:T(8,128)(2,1)S(1)}, bf16[64,2048]{1,0:T(8,128)(2,1)}, u32[]{:S(2)}) copy-start(bf16[64,2048]{1,0:T(8,128)(2,1)} %copy-done.24) | copy-start | bytes 786436
  102.1 14.5 %copy-start.27 = (bf16[64,2048]{1,0:T(8,128)(2,1)S(1)}, bf16[64,2048]{1,0:T(8,128)(2,1)}, u32[]{:S(2)}) copy-start(bf16[64,2048]{1,0:T(8,128)(2,1)} %copy-done.26) | copy-start | bytes 786436
  102.1 14.5 %copy-start.33 = (bf16[64,2048]{1,0:T(8,128)(2,1)S(1)}, bf16[64,2048]{1,0:T(8,128)(2,1)}, u32[]{:S(2)}) copy-start(bf16[64,2048]{1,0:T(8,128)(2,1)} %copy-done.32) | copy-start | bytes 786436
  102.1 14.5 %copy-start.35 = (bf16[64,2048]{1,0:T(8,128)(2,1)S(1)}, bf16[64,2048]{1,0:T(8,128)(2,1)}, u32[]{:S(2)}) copy-start(bf16[64,2048]{1,0:T(8,128)(2,1)} %copy-done.34) | copy-start | bytes 786436
  102.1 14.5 %copy-start.37 = (bf16[64,2048]{1,0:T(8,128)(2,1)S(1)}, bf16[64,2048]{1,0:T(8,128)(2,1)}, u32[]{:S(2)}) copy-start(bf16[64,2048]{1,0:T(8,128)(2,1)} %copy-done.36) | copy-start | bytes 786436
  114.5 8.3 %collective-permute-start.31 = (bf16[128,1024]{1,0:T(8,128)(2,1)S(1)}, bf16[128,1024]{1,0:T(8,128)(2,1)S(1)}, u32[]{:S(2)}, u32[]{:S(2)}) collective-permute-start(bf16[128,1024]{1,0:T(8,128)(2,1)S(1)} %get-tuple-element.99), channel_id=1, source_target_pairs={{0,17},{1,16},{2,19},{3,18},{4,21},{5,20},{6,23},{7,22},{8,25},{9,... | collective-permute-start | bytes 786440 | tf_op jit(solution)/shard_map/ppermute | solution.py:278
  115.4 14.8 %copy-start.45 = (bf16[128,512]{1,0:T(8,128)(2,1)S(1)}, bf16[128,512]{1,0:T(8,128)(2,1)}, u32[]{:S(2)}) copy-start(bf16[128,512]{1,0:T(8,128)(2,1)} %copy-done.44) | copy-start | bytes 393220
  115.4 15.7 %copy-start.43 = (bf16[128,512]{1,0:T(8,128)(2,1)S(1)}, bf16[128,512]{1,0:T(8,128)(2,1)}, u32[]{:S(2)}) copy-start(bf16[128,512]{1,0:T(8,128)(2,1)} %copy-done.42) | copy-start | bytes 393220
  115.4 19.2 %copy-start.41 = (bf16[128,512]{1,0:T(8,128)(2,1)S(1)}, bf16[128,512]{1,0:T(8,128)(2,1)}, u32[]{:S(2)}) copy-start(bf16[128,512]{1,0:T(8,128)(2,1)} %copy-done.40) | copy-start | bytes 393220
  115.4 13.8 %collective-permute-start.28 = (bf16[128,1024]{1,0:T(8,128)(2,1)S(1)}, bf16[128,1024]{1,0:T(8,128)(2,1)S(1)}, u32[]{:S(2)}, u32[]{:S(2)}) collective-permute-start(bf16[128,1024]{1,0:T(8,128)(2,1)S(1)} %get-tuple-element.93), channel_id=1, source_target_pairs={{0,16},{1,17},{2,18},{3,19},{4,20},{5,21},{6,22},{7,23},{8,24},{9,... | collective-permute-start | bytes 786440 | tf_op jit(solution)/shard_map/ppermute | solution.py:278
  122.8 8.3 %collective-permute-start.32 = (bf16[128,512]{1,0:T(8,128)(2,1)S(1)}, bf16[128,512]{1,0:T(8,128)(2,1)S(1)}, u32[]{:S(2)}, u32[]{:S(2)}) collective-permute-start(bf16[128,512]{1,0:T(8,128)(2,1)S(1)} %get-tuple-element.101), channel_id=1, source_target_pairs={{0,17},{1,16},{2,19},{3,18},{4,21},{5,20},{6,23},{7,22},{8,25},{9,... | collective-permute-start | bytes 393224 | tf_op jit(solution)/shard_map/ppermute | solution.py:278
  129.2 5.4 %collective-permute-start.29 = (bf16[128,512]{1,0:T(8,128)(2,1)S(1)}, bf16[128,512]{1,0:T(8,128)(2,1)S(1)}, u32[]{:S(2)}, u32[]{:S(2)}) collective-permute-start(bf16[128,512]{1,0:T(8,128)(2,1)S(1)} %get-tuple-element.95), channel_id=1, source_target_pairs={{0,16},{1,17},{2,18},{3,19},{4,20},{5,21},{6,22},{7,23},{8,24},{9,... | collective-permute-start | bytes 393224 | tf_op jit(solution)/shard_map/ppermute | solution.py:278
  130.2 5.4 %collective-permute-start.25 = (bf16[128,1024]{1,0:T(8,128)(2,1)S(1)}, bf16[128,1024]{1,0:T(8,128)(2,1)S(1)}, u32[]{:S(2)}, u32[]{:S(2)}) collective-permute-start(bf16[128,1024]{1,0:T(8,128)(2,1)S(1)} %get-tuple-element.89), channel_id=1, source_target_pairs={{0,1},{1,0},{2,3},{3,2},{4,5},{5,4},{6,7},{7,6},{8,9},{9,8},{10,11... | collective-permute-start | bytes 786440 | tf_op jit(solution)/shard_map/ppermute | solution.py:278
  130.2 5.4 %collective-permute-start.27 = (bf16[128,512]{1,0:T(8,128)(2,1)S(1)}, bf16[128,512]{1,0:T(8,128)(2,1)S(1)}, u32[]{:S(2)}, u32[]{:S(2)}) collective-permute-start(bf16[128,512]{1,0:T(8,128)(2,1)S(1)} %copy-done.45), channel_id=1, source_target_pairs={{0,1},{1,0},{2,3},{3,2},{4,5},{5,4},{6,7},{7,6},{8,9},{9,8},{10,11... | collective-permute-start | bytes 393224 | tf_op jit(solution)/shard_map/ppermute | solution.py:278
  130.7 4.9 %collective-permute-start.26 = (bf16[128,512]{1,0:T(8,128)(2,1)S(1)}, bf16[128,512]{1,0:T(8,128)(2,1)S(1)}, u32[]{:S(2)}, u32[]{:S(2)}) collective-permute-start(bf16[128,512]{1,0:T(8,128)(2,1)S(1)} %get-tuple-element.90), channel_id=1, source_target_pairs={{0,1},{1,0},{2,3},{3,2},{4,5},{5,4},{6,7},{7,6},{8,9},{9,8},{10,11... | collective-permute-start | bytes 393224 | tf_op jit(solution)/shard_map/ppermute | solution.py:278
  131.1 5.4 %collective-permute-start.33 = (bf16[128,512]{1,0:T(8,128)(2,1)S(1)}, bf16[128,512]{1,0:T(8,128)(2,1)S(1)}, u32[]{:S(2)}, u32[]{:S(2)}) collective-permute-start(bf16[128,512]{1,0:T(8,128)(2,1)S(1)} %copy-done.43), channel_id=1, source_target_pairs={{0,17},{1,16},{2,19},{3,18},{4,21},{5,20},{6,23},{7,22},{8,25},{9,... | collective-permute-start | bytes 393224 | tf_op jit(solution)/shard_map/ppermute | solution.py:278
  134.6 5.4 %collective-permute-start.30 = (bf16[128,512]{1,0:T(8,128)(2,1)S(1)}, bf16[128,512]{1,0:T(8,128)(2,1)S(1)}, u32[]{:S(2)}, u32[]{:S(2)}) collective-permute-start(bf16[128,512]{1,0:T(8,128)(2,1)S(1)} %copy-done.41), channel_id=1, source_target_pairs={{0,16},{1,17},{2,18},{3,19},{4,20},{5,21},{6,22},{7,23},{8,24},{9,... | collective-permute-start | bytes 393224 | tf_op jit(solution)/shard_map/ppermute | solution.py:278
  (18 other events, 14.7 us)

commit v6 on v5

--- a/solution.py
+++ b/solution.py
@@ -18,6 +18,7 @@
 QUAD = 4
 HQ = H // QUAD
 CHUNK_HEADS = (8, 8)
+PHASES = "z y0 b~ f~ q02 | z y1 k q01 | z y2 p q03 q12~ | y3 q13~ q11"
 CHUNKS = len(CHUNK_HEADS)
 FIRST_HEAD = tuple(sum(CHUNK_HEADS[:j]) for j in range(CHUNKS))
 ROW = LAT + ROPE
@@ -103,24 +104,13 @@
             out[:, rope_at : rope_at + 128] = turned.astype(jnp.bfloat16)
 
 
-def pair_kernel(info, w_up, got, *refs):
-    outs, sems = refs[:-1], refs[-1]
-    rows = got.shape[0]
-    copies = []
-    for j, out in enumerate(outs):
-        width = out.shape[1]
-        first = FIRST_HEAD[j] * (NOPE + VDIM)
-        begin = pl.multiple_of(info[0] * (HQ * (NOPE + VDIM)) + first, 128)
-        copies.append(
-            pltpu.make_async_copy(
-                w_up.at[:, pl.ds(begin, width)], out.at[pl.ds(0, rows)], sems.at[2 * j]
-            )
-        )
-        copies.append(
-            pltpu.make_async_copy(
-                got.at[:, pl.ds(first, width)], out.at[pl.ds(rows, rows)], sems.at[2 * j + 1]
-            )
-        )
+def pair_kernel(info, w_up, got, out, sem):
+    rows, width = got.shape
+    begin = pl.multiple_of(info[0] * width, 128)
+    copies = [
+        pltpu.make_async_copy(w_up.at[:, pl.ds(begin, width)], out.at[pl.ds(0, rows)], sem.at[0]),
+        pltpu.make_async_copy(got, out.at[pl.ds(rows, rows)], sem.at[1]),
+    ]
     for copy in copies:
         copy.start()
     for copy in copies:
@@ -148,16 +138,16 @@
         lane = lax.broadcasted_iota(jnp.int32, (tok, tok), 1)
         row = lax.broadcasted_iota(jnp.int32, (tok, tok), 0)
         for g in range(2):
+            mine_of, other_of = [
+                [ref[(3 * g + n) * tok : (3 * g + n + 1) * tok] for n in range(3)]
+                for ref in (own, other)
+            ]
             pieces = [
-                own[g * tok : (g + 1) * tok],
-                other[g * tok : (g + 1) * tok],
-                own[(2 + g) * tok : (3 + g) * tok],
-                other[(2 + g) * tok : (3 + g) * tok],
-                jnp.where(
-                    has_last,
-                    own[(4 + g) * tok : (5 + g) * tok],
-                    other[(4 + g) * tok : (5 + g) * tok],
-                ),
+                mine_of[0],
+                other_of[0],
+                mine_of[1],
+                other_of[1],
+                jnp.where(has_last, mine_of[2], other_of[2]),
             ]
             for b, piece in enumerate(pieces):
                 here = slice(b * tok, (b + 1) * tok)
@@ -236,19 +226,18 @@
     return lax.optimization_barrier((array,) + others)[0]
 
 
-class Stream:
-    def __init__(self, window):
-        self.window = window
-        self.arrived = []
-
-    def after(self, array):
-        if len(self.arrived) < self.window:
-            return array
-        return tie(array, self.arrived[-self.window])
-
-    def send(self, permute, array, *args):
-        self.arrived.append(permute(self.after(array), *args))
-        return self.arrived[-1]
+class Phases:
+    def __init__(self):
+        self.before, self.before_late, self.now, self.late = [], [], [], []
+
+    def turn(self):
+        self.before = self.now + self.before_late
+        self.before_late, self.now, self.late = self.late, [], []
+
+    def send(self, late, permute, array, *args):
+        arrived = permute(tie(array, *self.before) if self.before else array, *args)
+        (self.late if late else self.now).append(arrived)
+        return arrived
 
 
 def shape(dims, kind=jnp.bfloat16):
@@ -277,43 +266,17 @@
         ]
         return lax.ppermute(array, ("groups", "ctx"), pairs)
 
-    def send_in_quad(array, r):
-        return quad_swap(array, r) if r == 1 else group_stream.send(quad_swap, array, r)
-
     def around(array, by):
         return lax.ppermute(array, "ctx", [(i, (i + by) % size) for i in range(size)])
 
     def inner_swap(array):
         return lax.ppermute(array, "ctx", [(i, i ^ 2) for i in range(size)])
-
-    def along_and_across(pieces, share_rows, gates):
-        count = len(pieces)
-        turns = [(k - j, j) for k in range(outer + count) for j in range(count)]
-        lines = [[piece] for piece in pieces]
-        sides = [[] for piece in pieces]
-        outer_done, inner_done = [], []
-        for k, j in turns:
-            if not 0 <= k < outer:
-                continue
-            if k:
-                at = len(outer_done)
-                before = outer_done[-2:-1] + ([inner_done[max(0, at - 2)]] if at else [])
-                before += gates.get(at, [])
-                outer_done.append(around(tie(lines[j][-1], *before), 4))
-                lines[j].append(outer_done[-1])
-                if not at:
-                    share_rows(inner_done[0], outer_done[0])
-            sides[j].append(inner_swap(tie(lines[j][k], *inner_done[-2:-1])))
-            inner_done.append(sides[j][-1])
-        return [line + side for line, side in zip(lines, sides)]
 
     def from_behind(array, by, odd_only):
         first = 1 if odd_only else 0
         step = 2 if odd_only else 1
         pairs = [(i, i + by) for i in range(first, size - by, step)]
         return lax.ppermute(array, "ctx", pairs)
-
-    group_stream = Stream(2)
 
     width = HQ * (NOPE + VDIM)
     quarter_info = quarter[None].astype(jnp.int32)
@@ -321,15 +284,14 @@
     give = lax.dynamic_slice_in_dim(w_up, (quarter ^ 1) * width, width, 1)
     give, lengths = lax.optimization_barrier((give, lengths))
     got = quad_swap(give, 1)
-    widths = [heads * (NOPE + VDIM) for heads in CHUNK_HEADS]
     outer = size // 4 if size % 4 == 0 and size // 4 <= 4 else 0
     if outer:
-        pairs_of_rows = pl.pallas_call(
+        pair_rows = pl.pallas_call(
             pair_kernel,
-            out_shape=[shape((2 * w_up.shape[0], w)) for w in widths],
+            out_shape=shape((2 * w_up.shape[0], width)),
             in_specs=[smem, pl.BlockSpec(memory_space=pltpu.HBM), anywhere],
-            out_specs=[anywhere] * CHUNKS,
-            scratch_shapes=[pltpu.SemaphoreType.DMA((2 * CHUNKS,))],
+            out_specs=anywhere,
+            scratch_shapes=[pltpu.SemaphoreType.DMA((2,))],
             compiler_params=params,
             name="pair",
         )(quarter_info, *in_hbm(w_up), got)
@@ -340,18 +302,7 @@
             [jnp.where(even, keep, got), jnp.where(even, got, keep)], axis=0
         )
         same_core = [list(range(c, size, 2)) for c in range(2)]
-        weights = [
-            [
-                lax.all_gather(
-                    both[:, FIRST_HEAD[j] * 256 : FIRST_HEAD[j] * 256 + widths[j]],
-                    "ctx",
-                    axis=0,
-                    tiled=True,
-                    axis_index_groups=same_core,
-                )
-            ]
-            for j in range(CHUNKS)
-        ]
+        gathered = lax.all_gather(both, "ctx", axis=0, tiled=True, axis_index_groups=same_core)
 
     frequency = np.exp(-np.arange(ROPE // 2) * (2.0 * math.log(10000.0) / ROPE))
     frequency = jnp.asarray(np.tile(frequency, 4)[None, :], jnp.float32)
@@ -395,37 +346,54 @@
             flops=0, bytes_accessed=4 * q_heads.size, transcendentals=0
         ),
         name="queries",
-    )(quarter_info, *in_hbm(q_heads), tie(cosine, pairs_of_rows[0] if outer else got), sine)
-
-    shared = []
-
-    def share_rows(*others):
-        swapped = quad_swap(tie(rows, queries[0], *others), 2)
-        both_groups = jnp.concatenate([rows, swapped], axis=0)
-        behind = from_behind(both_groups, 2, False)
-        far_behind = from_behind(both_groups, 4, True)
-        own_rows = jnp.concatenate([both_groups, behind, far_behind], axis=0)
-        shared.extend([own_rows, quad_swap(own_rows, 1)])
-
-    across = [
-        [group_stream.send(quad_swap, queries[r * CHUNKS + j], r) for r in (2, 3)]
-        for j in range(CHUNKS)
-    ]
-    if outer:
-        gates = {3: [across[0][0]], 4: [across[0][1]], 5: [across[1][0]]}
-        weights = along_and_across(pairs_of_rows, share_rows, gates)
-    else:
-        share_rows()
-    own_rows, other_rows = shared
-    moved = [
-        [queries[j], quad_swap(tie(queries[CHUNKS + j], across[j][0]), 1)] + across[j]
-        for j in range(CHUNKS)
-    ]
+    )(quarter_info, *in_hbm(q_heads, tie(cosine, pair_rows if outer else got), sine))
+
+    phases = Phases()
+    line = [pair_rows] if outer else []
+    side = []
+    halves = []
+    moved = [[queries[j]] + [None] * (QUAD - 1) for j in range(CHUNKS)]
+    parts = {"r": tie(rows, pair_rows if outer else got)}
+    for name in PHASES.split():
+        kind, late = name[0], name[-1] == "~"
+        if kind == "|":
+            phases.turn()
+        elif kind == "z" and outer:
+            line.append(phases.send(late, around, line[-1], 4))
+        elif kind == "y" and outer:
+            step = int(name[1])
+            if step < outer - 1:
+                side.append(phases.send(late, inner_swap, line[step]))
+            else:
+                half = line[step].shape[1] // CHUNKS
+                halves = [
+                    phases.send(late, inner_swap, line[step][:, j * half : (j + 1) * half])
+                    for j in range(CHUNKS)
+                ]
+        elif kind == "b":
+            parts["b"] = phases.send(late, from_behind, parts["r"], 2, False)
+        elif kind == "f":
+            parts["f"] = phases.send(late, from_behind, parts["r"], 4, True)
+        elif kind == "k":
+            have = jnp.concatenate([parts["r"], parts["b"], parts["f"]], axis=0)
+            swapped = phases.send(late, quad_swap, have, 2)
+        elif kind == "p":
+            own_rows = jnp.concatenate([have, swapped], axis=0)
+            other_rows = phases.send(late, quad_swap, own_rows, 1)
+        elif kind == "q":
+            j, r = int(name[1]), int(name[2])
+            moved[j][r] = phases.send(late, quad_swap, queries[r * CHUNKS + j], r)
+
+    def weights_for(j):
+        if not outer:
+            return [(gathered, FIRST_HEAD[j] // 2)]
+        return [(piece, FIRST_HEAD[j] // 2) for piece in line + side] + [(halves[j], 0)]
 
     window = (REACH + 2) * tok
 
     def attend(j, first, steps):
         heads = 2 * steps
+        pieces_of_weight = [piece for piece, begin in weights_for(j)]
         flops = 2 * heads * 2 * (window * LAT * 256 + 2 * tok * window * (NOPE + ROPE + VDIM))
         return pl.pallas_call(
             functools.partial(attend_kernel, outer),
@@ -433,8 +401,8 @@
             out_shape=[shape((tok, heads * VDIM))] * QUAD,
             in_specs=[smem, block(6 * tok, EXT), block(6 * tok, EXT)]
             + [
-                pl.BlockSpec((piece.shape[0], 512), lambda i: (0, first + i))
-                for piece in weights[j]
+                pl.BlockSpec((piece.shape[0], 512), lambda i, begin=begin: (0, begin + first + i))
+                for piece, begin in weights_for(j)
             ]
             + [pl.BlockSpec((tok, 256), lambda i: (0, first + i))] * QUAD
             + [pl.BlockSpec((tok, 128), lambda i: (0, CHUNK_HEADS[j] + first + i))] * QUAD,
@@ -453,15 +421,18 @@
                 transcendentals=heads * 4 * tok * window,
             ),
             name="attend",
-        )(mine_info, own_rows, other_rows, *weights[j], *moved[j], *moved[j])
+        )(mine_info, own_rows, other_rows, *pieces_of_weight, *moved[j], *moved[j])
 
     results = []
     for call in CALLS:
-        parts = attend(*call)
-        results.append([parts[0]] + [send_in_quad(parts[r], r) for r in range(1, QUAD)])
+        if len(results) > 1:
+            mine_info = tie(mine_info, results[-2][2])
+        pieces = attend(*call)
+        mine_info = tie(mine_info, pieces[0])
+        results.append([pieces[0]] + [quad_swap(pieces[r], r) for r in range(1, QUAD)])
     pieces = [one[r] for r in range(QUAD) for one in results]
     arrived = lax.all_to_all(
-        tie(outgoing, pieces[len(CALLS) - 1]).reshape(size, slot_count, ROW),
+        tie(outgoing, results[-1][0]).reshape(size, slot_count, ROW),
         "ctx",
         split_axis=0,
         concat_axis=0,

time: 144 us -> 118 us (0.82)
  local copies, waits for them, and re-layouts: 19.7 us -> 2.01 us
  starting transfers between devices: 47.4 us -> 32.2 us
  waiting for transfers between devices: 42.4 us -> 50.3 us
    unnamed x97 -> x6, local copies, waits for them, and re-layouts: 18.6 us -> 0.94 us
    ppermute x6 -> x3, starting transfers between devices: 17.4 us -> 4.72 us  [around(): lax.ppermute(array, 'ctx', [(i, (i + by) % size) for i in range(size)])]
    ppermute x8 -> x5, waiting for transfers between devices: 19.1 us -> 6.44 us  [inner_swap(): return lax.ppermute(array, 'ctx', [(i, i ^ 2) for i in range(size)])]
    ppermute x18, waiting for transfers between devices: 20.5 us -> 31.7 us  [quad_swap(): return lax.ppermute(array, ('groups', 'ctx'), pairs)]
    ppermute x6 -> x3, waiting for transfers between devices: 2.69 us -> 12.2 us  [around(): lax.ppermute(array, 'ctx', [(i, (i + by) % size) for i in range(size)])]
    ppermute x8 -> x5, starting transfers between devices: 12.2 us -> 5.53 us  [inner_swap(): return lax.ppermute(array, 'ctx', [(i, i ^ 2) for i in range(size)])]
    ppermute x18, starting transfers between devices: 9.95 us -> 13.7 us  [quad_swap(): return lax.ppermute(array, ('groups', 'ctx'), pairs)]
  transfers between devices with their start and end apart: 35 -> 29, of which waited for: 16 -> 13; matrix products, arithmetic and copies ran while one was open for 0% -> 0% of each run, Pallas kernels for 22% -> 21%
where the time goes in v6:
time: 118 us; the launch traced here: 117 us
  waiting for transfers between devices  50.3 us (43%)
  starting transfers between devices  32.2 us (27%)
  Pallas kernels  32.1 us (27%)
  local copies, waits for them, and re-layouts  2.01 us (2%)
    ppermute x18, waiting for transfers between devices, quad_swap(): return lax.ppermute(array, ('groups', 'ctx'), pairs)  31.7 us
    pallas_call x3, Pallas kernels, attend(): pl.pallas_call(functools.partial(attend_kernel, outer), grid=(steps,), ou...  24 us
    ppermute x18, starting transfers between devices, quad_swap(): return lax.ppermute(array, ('groups', 'ctx'), pairs)  13.7 us
    ppermute x3, waiting for transfers between devices, around(): lax.ppermute(array, 'ctx', [(i, (i + by) % size) for i in range(size)])  12.2 us
    ppermute x5, waiting for transfers between devices, inner_swap(): return lax.ppermute(array, 'ctx', [(i, i ^ 2) for i in range(size)])  6.44 us
    ppermute x5, starting transfers between devices, inner_swap(): return lax.ppermute(array, 'ctx', [(i, i ^ 2) for i in range(size)])  5.53 us
    all_to_all x1, starting transfers between devices, body(): lax.all_to_all(tie(outgoing, results[-1][0]).reshape(size, slot_count, RO...  5.1 us
    ppermute x3, starting transfers between devices, around(): lax.ppermute(array, 'ctx', [(i, (i + by) % size) for i in range(size)])  4.72 us
  transfers between devices with their start and end apart: 29, of which 13 were waited for; matrix products, arithmetic and copies ran while one was open for 0% of the time, Pallas kernels for 21%

profile of v6, /device:TPU:0, one launch (start us, length us, event | category | flops | bytes accessed | tf_op | source)
XLA Modules:
  0.0 117.4 jit_solution(5681830507679230916)
XLA Ops:
  0.6 1.0 constant_dynamic-slice_fusion
  1.6 0.5 collective-permute-start
  2.1 1.2 collective-permute-done.got
  3.3 1.0 pair.1.refs_0_
  4.3 3.0 %collective-permute-start.4 = (bf16[64,4096]{1,0:T(8,128)(2,1)S(1)}, bf16[64,4096]{1,0:T(8,128)(2,1)S(1)}, u32[]{:S(2)}, u32[]{:S(2)}) collective-permute-start(bf16[64,4096]{1,0:T(8,128)(2,1)S(1)} %pair.1.refs_0_), channel_id=1, source_target_pairs={{0,2},{1,3},{2,0},{3,1},{4,6},{5,7},{6,4},{7,5},{8,10},{9,11},{10,... | collective-permute-start | bytes 1572872 | tf_op jit(solution)/shard_map/ppermute | solution.py:273
  7.2 1.6 %collective-permute-start.3 = (bf16[64,4096]{1,0:T(8,128)(2,1)S(1)}, bf16[64,4096]{1,0:T(8,128)(2,1)S(1)}, u32[]{:S(2)}, u32[]{:S(2)}) collective-permute-start(bf16[64,4096]{1,0:T(8,128)(2,1)S(1)} %pair.1.refs_0_), channel_id=1, source_target_pairs={{0,4},{1,5},{2,6},{3,7},{4,8},{5,9},{6,10},{7,11},{8,12},{9,13},{1... | collective-permute-start | bytes 1572872 | tf_op jit(solution)/shard_map/ppermute | solution.py:270
  8.8 2.3 %rows.1 = (bf16[128,640]{1,0:T(8,128)(2,1)}, f32[128,128]{1,0:T(8,128)}, f32[128,128]{1,0:T(8,128)}, bf16[256,576]{1,0:T(8,128)(2,1)}) custom-call(s32[1]{0:T(128)} %bitcast.1.info, s32[8]{0:T(128)} %lengths, bf16[576,128]{1,0:T(8,128)(2,1)} %bitcast.8, f32[1,512]{1,0:T(1,128)} %bitcast.9, s32[1,128]{1,0:T(1,128)} %bitcast.10, f32[1,128]{1,0:T(1,128)} %constant.30.clone.freq), custom_call_target="tpu_custom_call" | custom-call | tf_op jit(solution)/shard_map/rows/pallas_call | solution.py:314
  11.1 3.4 %queries.1 = (bf16[128,1536]{1,0:T(8,128)(2,1)S(1)}, bf16[128,1536]{1,0:T(8,128)(2,1)S(1)}, bf16[128,1536]{1,0:T(8,128)(2,1)S(1)}, bf16[128,1536]{1,0:T(8,128)(2...) custom-call(s32[1]{0:T(128)} %bitcast.info, ...), custom_call_target="tpu_custom_call" | custom-call | bytes 6291456 | tf_op jit(solution)/shard_map/queries/pallas_call | solution.py:338
  14.5 1.6 %collective-permute-start.5 = (bf16[128,1536]{1,0:T(8,128)(2,1)S(1)}, bf16[128,1536]{1,0:T(8,128)(2,1)S(1)}, u32[]{:S(2)}, u32[]{:S(2)}) collective-permute-start(bf16[128,1536]{1,0:T(8,128)(2,1)S(1)} %get-tuple-element.52), channel_id=1, source_target_pairs={{0,16},{1,17},{2,18},{3,19},{4,20},{5,21},{6,22},{7,23},{8,24},{9,... | collective-permute-start | bytes 1179656 | tf_op jit(solution)/shard_map/ppermute | solution.py:267
  16.1 0.7 collective-permute-start.2
  16.7 2.4 %collective-permute-start.1 = (bf16[128,640]{1,0:T(8,128)(2,1)S(1)}, bf16[128,640]{1,0:T(8,128)(2,1)S(1)}, u32[]{:S(2)}, u32[]{:S(2)}) collective-permute-start(bf16[128,640]{1,0:T(8,128)(2,1)S(1)} %copy-done), channel_id=1, source_target_pairs={{0,2},{1,3},{2,4},{3,5},{4,6},{5,7},{6,8},{7,9},{8,10},{9,11},{10,... | collective-permute-start | bytes 491528 | tf_op jit(solution)/shard_map/ppermute | solution.py:279
  19.2 6.0 %collective-permute-done.5.refs_10_.refs_14_ = bf16[128,1536]{1,0:T(8,128)(2,1)S(1)} collective-permute-done((bf16[128,1536]{1,0:T(8,128)(2,1)S(1)}, bf16[128,1536]{1,0:T(8,128)(2,1)S(1)}, u32[]{:S(2)}, u32[]{:S(2)}) %collective-permute-start.5) | collective-permute-done | bytes 393248 | tf_op jit(solution)/shard_map/ppermute | solution.py:267
  25.2 0.0 collective-permute-done.4.refs_4_
  25.2 0.0 collective-permute-done.3.refs_1_
  25.2 0.5 collective-permute-start.8
  25.7 1.6 %collective-permute-start.7 = (bf16[64,4096]{1,0:T(8,128)(2,1)S(1)}, bf16[64,4096]{1,0:T(8,128)(2,1)S(1)}, u32[]{:S(2)}, u32[]{:S(2)}) collective-permute-start(bf16[64,4096]{1,0:T(8,128)(2,1)S(1)} %collective-permute-done.3.refs_1_), channel_id=1, source_target_pairs={{0,4},{1,5},{2,6},{3,7},{4,8},{5,9},{6,10},{7,11},{8,12},{9,13},{1... | collective-permute-start | bytes 1572872 | tf_op jit(solution)/shard_map/ppermute | solution.py:270
  27.3 0.0 collective-permute-done.2
  27.3 1.6 %collective-permute-start.6 = (bf16[384,640]{1,0:T(8,128)(2,1)S(1)}, bf16[384,640]{1,0:T(8,128)(2,1)S(1)}, u32[]{:S(2)}, u32[]{:S(2)}) collective-permute-start(bf16[384,640]{1,0:T(8,128)(2,1)S(1)} %pad_maximum_fusion), channel_id=1, source_target_pairs={{0,16},{1,17},{2,18},{3,19},{4,20},{5,21},{6,22},{7,23},{8,24},{9,... | collective-permute-start | bytes 1474568 | tf_op jit(solution)/shard_map/ppermute | solution.py:267
  28.9 1.6 %collective-permute-done.9.refs_9_.refs_13_ = bf16[128,1536]{1,0:T(8,128)(2,1)S(1)} collective-permute-done((bf16[128,1536]{1,0:T(8,128)(2,1)S(1)}, bf16[128,1536]{1,0:T(8,128)(2,1)S(1)}, u32[]{:S(2)}, u32[]{:S(2)}) %collective-permute-start.9) | collective-permute-done | bytes 393248 | tf_op jit(solution)/shard_map/ppermute | solution.py:267
  30.6 8.0 %collective-permute-done.6 = bf16[384,640]{1,0:T(8,128)(2,1)S(1)} collective-permute-done((bf16[384,640]{1,0:T(8,128)(2,1)S(1)}, bf16[384,640]{1,0:T(8,128)(2,1)S(1)}, u32[]{:S(2)}, u32[]{:S(2)}) %collective-permute-start.6) | collective-permute-done | bytes 491552 | tf_op jit(solution)/shard_map/ppermute | solution.py:267
  38.6 0.0 collective-permute-done.8.refs_5_
  38.6 1.1 collective-permute-done.7.refs_2_
  39.7 1.6 %collective-permute-start.11 = (bf16[64,4096]{1,0:T(8,128)(2,1)S(1)}, bf16[64,4096]{1,0:T(8,128)(2,1)S(1)}, u32[]{:S(2)}, u32[]{:S(2)}) collective-permute-start(bf16[64,4096]{1,0:T(8,128)(2,1)S(1)} %collective-permute-done.7.refs_2_), channel_id=1, source_target_pairs={{0,4},{1,5},{2,6},{3,7},{4,8},{5,9},{6,10},{7,11},{8,12},{9,13},{1... | collective-permute-start | bytes 1572872 | tf_op jit(solution)/shard_map/ppermute | solution.py:270
  41.3 0.1 constant_dynamic-update-slice_fusion.own
  41.3 0.1 collective-permute-start.10
  41.4 0.5 collective-permute-start.12
  41.9 1.3 %collective-permute-start.13 = (bf16[128,1536]{1,0:T(8,128)(2,1)S(1)}, bf16[128,1536]{1,0:T(8,128)(2,1)S(1)}, u32[]{:S(2)}, u32[]{:S(2)}) collective-permute-start(bf16[128,1536]{1,0:T(8,128)(2,1)S(1)} %get-tuple-element.60), channel_id=1, source_target_pairs={{0,17},{1,16},{2,19},{3,18},{4,21},{5,20},{6,23},{7,22},{8,25},{9,... | collective-permute-start | bytes 1179656 | tf_op jit(solution)/shard_map/ppermute | solution.py:267
  43.2 11.1 %collective-permute-done.11.refs_3_ = bf16[64,4096]{1,0:T(8,128)(2,1)S(1)} collective-permute-done((bf16[64,4096]{1,0:T(8,128)(2,1)S(1)}, bf16[64,4096]{1,0:T(8,128)(2,1)S(1)}, u32[]{:S(2)}, u32[]{:S(2)}) %collective-permute-start.11) | collective-permute-done | bytes 524320 | tf_op jit(solution)/shard_map/ppermute | solution.py:270
  54.3 0.0 collective-permute-done.13.refs_11_.refs_15_
  54.4 1.4 %collective-permute-done.12.refs_6_ = bf16[64,4096]{1,0:T(8,128)(2,1)S(1)} collective-permute-done((bf16[64,4096]{1,0:T(8,128)(2,1)S(1)}, bf16[64,4096]{1,0:T(8,128)(2,1)S(1)}, u32[]{:S(2)}, u32[]{:S(2)}) %collective-permute-start.12) | collective-permute-done | bytes 524320 | tf_op jit(solution)/shard_map/ppermute | solution.py:273
  55.7 0.0 collective-permute-done.10.other
  55.7 0.5 collective-permute-start.14
  56.2 1.5 %collective-permute-start.17 = (bf16[128,1536]{1,0:T(8,128)(2,1)S(1)}, bf16[128,1536]{1,0:T(8,128)(2,1)S(1)}, u32[]{:S(2)}, u32[]{:S(2)}) collective-permute-start(bf16[128,1536]{1,0:T(8,128)(2,1)S(1)} %get-tuple-element.70), channel_id=1, source_target_pairs={{0,16},{1,17},{2,18},{3,19},{4,20},{5,21},{6,22},{7,23},{8,24},{9,... | collective-permute-start | bytes 1179656 | tf_op jit(solution)/shard_map/ppermute | solution.py:267
  57.7 1.1 collective-permute-start.15
  58.8 0.0 collective-permute-start.16
  58.8 1.1 collective-permute-start.18
  59.9 5.0 %collective-permute-done.14.refs_7_ = bf16[64,2048]{1,0:T(8,128)(2,1)S(1)} collective-permute-done((bf16[64,2048]{1,0:T(8,128)(2,1)S(1)}, bf16[64,2048]{1,0:T(8,128)(2,1)S(1)}, u32[]{:S(2)}, u32[]{:S(2)}) %collective-permute-start.14) | collective-permute-done | bytes 262176 | tf_op jit(solution)/shard_map/ppermute | solution.py:273
  65.0 11.6 %attend.3 = (bf16[128,1024]{1,0:T(8,128)(2,1)S(1)}, bf16[128,1024]{1,0:T(8,128)(2,1)S(1)}, bf16[128,1024]{1,0:T(8,128)(2,1)S(1)}, bf16[128,1024]{1,0:T(8,128)(2,1)S(1)}) custom-call(s32[1]{0:T(128)} %bitcast.1.info, bf16[768,640]{1,0:T(8,128)(2,1)S(1)} %constant_dynamic-update-slice_fusion.own, bf16[768,640]{1,0:T(8,128)(2,1)S(1)} %collective-permute-done.10.other, ...), custom_call_target="tpu_custom_call" | custom-call | flops 4362076160 | bytes 8388608 | tf_op jit(solution)/shard_map/attend/pallas_call | solution.py:398
  76.6 1.1 collective-permute-start.19
  77.7 0.0 collective-permute-done.16.refs_9_.refs_13_
  77.7 0.0 collective-permute-done.18.refs_11_.refs_15_
  77.7 6.2 %attend.4 = (bf16[128,512]{1,0:T(8,128)(2,1)S(1)}, bf16[128,512]{1,0:T(8,128)(2,1)S(1)}, bf16[128,512]{1,0:T(8,128)(2,1)S(1)}, bf16[128,512]{1,0:T(8,128)(2,1)S(1)}) custom-call(s32[1]{0:T(128)} %bitcast.1.info, bf16[768,640]{1,0:T(8,128)(2,1)S(1)} %constant_dynamic-update-slice_fusion.own, bf16[768,640]{1,0:T(8,128)(2,1)S(1)} %collective-permute-done.10.other, ...), custom_call_target="tpu_custom_call" | custom-call | flops 2181038080 | bytes 4194304 | tf_op jit(solution)/shard_map/attend/pallas_call | solution.py:398
  83.9 0.0 collective-permute-done.19.refs_6_
  83.9 6.2 %attend.5 = (bf16[128,512]{1,0:T(8,128)(2,1)S(1)}, bf16[128,512]{1,0:T(8,128)(2,1)S(1)}, bf16[128,512]{1,0:T(8,128)(2,1)S(1)}, bf16[128,512]{1,0:T(8,128)(2,1)S(1)}) custom-call(s32[1]{0:T(128)} %bitcast.1.info, bf16[768,640]{1,0:T(8,128)(2,1)S(1)} %constant_dynamic-update-slice_fusion.own, bf16[768,640]{1,0:T(8,128)(2,1)S(1)} %collective-permute-done.10.other, ...), custom_call_target="tpu_custom_call" | custom-call | flops 2181038080 | bytes 4194304 | tf_op jit(solution)/shard_map/attend/pallas_call | solution.py:398
  90.1 5.1 %all-to-all-start = ((bf16[16,16,576]{2,1,0:T(8,128)(2,1)}), bf16[16,16,576]{2,1,0:T(8,128)(2,1)S(1)}, u32[]{:S(2)}, u32[]{:S(2)}) async-start(bf16[16,16,576]{2,1,0:T(8,128)(2,1)} %bitcast.5), calls=%async_computation | async-start | bytes 655360 | tf_op jit(solution)/shard_map/all_to_all | solution.py:434
  95.2 0.4 collective-permute-start.20
  95.6 0.3 collective-permute-start.25
  95.9 0.3 collective-permute-start.21
  96.3 1.5 %collective-permute-start.23 = (bf16[128,512]{1,0:T(8,128)(2,1)S(1)}, bf16[128,512]{1,0:T(8,128)(2,1)S(1)}, u32[]{:S(2)}, u32[]{:S(2)}) collective-permute-start(bf16[128,512]{1,0:T(8,128)(2,1)S(1)} %get-tuple-element.81), channel_id=1, source_target_pairs={{0,16},{1,17},{2,18},{3,19},{4,20},{5,21},{6,22},{7,23},{8,24},{9,... | collective-permute-start | bytes 393224 | tf_op jit(solution)/shard_map/ppermute | solution.py:267
  97.8 0.0 collective-permute-start.26
  97.8 0.0 collective-permute-done.20.refs_3_
  97.8 0.6 collective-permute-start.22
  98.4 5.5 %collective-permute-done.25.refs_9_ = bf16[128,1024]{1,0:T(8,128)(2,1)S(1)} collective-permute-done((bf16[128,1024]{1,0:T(8,128)(2,1)S(1)}, bf16[128,1024]{1,0:T(8,128)(2,1)S(1)}, u32[]{:S(2)}, u32[]{:S(2)}) %collective-permute-start.25) | collective-permute-done | bytes 262176 | tf_op jit(solution)/shard_map/ppermute | solution.py:267
  103.9 0.5 collective-permute-start.24
  104.4 0.0 collective-permute-done.21.refs_4_
  104.4 1.3 %collective-permute-start.27 = (bf16[128,512]{1,0:T(8,128)(2,1)S(1)}, bf16[128,512]{1,0:T(8,128)(2,1)S(1)}, u32[]{:S(2)}, u32[]{:S(2)}) collective-permute-start(bf16[128,512]{1,0:T(8,128)(2,1)S(1)} %get-tuple-element.85), channel_id=1, source_target_pairs={{0,17},{1,16},{2,19},{3,18},{4,21},{5,20},{6,23},{7,22},{8,25},{9,... | collective-permute-start | bytes 393224 | tf_op jit(solution)/shard_map/ppermute | solution.py:267
  105.8 1.6 %collective-permute-done.23.refs_7_ = bf16[128,512]{1,0:T(8,128)(2,1)S(1)} collective-permute-done((bf16[128,512]{1,0:T(8,128)(2,1)S(1)}, bf16[128,512]{1,0:T(8,128)(2,1)S(1)}, u32[]{:S(2)}, u32[]{:S(2)}) %collective-permute-start.23) | collective-permute-done | bytes 131104 | tf_op jit(solution)/shard_map/ppermute | solution.py:267
  107.4 2.1 %collective-permute-done.26.refs_10_ = bf16[128,512]{1,0:T(8,128)(2,1)S(1)} collective-permute-done((bf16[128,512]{1,0:T(8,128)(2,1)S(1)}, bf16[128,512]{1,0:T(8,128)(2,1)S(1)}, u32[]{:S(2)}, u32[]{:S(2)}) %collective-permute-start.26) | collective-permute-done | bytes 131104 | tf_op jit(solution)/shard_map/ppermute | solution.py:267
  109.5 0.0 collective-permute-done.22.refs_5_
  109.5 3.5 %collective-permute-done.24.refs_8_ = bf16[128,512]{1,0:T(8,128)(2,1)S(1)} collective-permute-done((bf16[128,512]{1,0:T(8,128)(2,1)S(1)}, bf16[128,512]{1,0:T(8,128)(2,1)S(1)}, u32[]{:S(2)}, u32[]{:S(2)}) %collective-permute-start.24) | collective-permute-done | bytes 131104 | tf_op jit(solution)/shard_map/ppermute | solution.py:267
  113.0 2.1 %collective-permute-done.27.refs_11_ = bf16[128,512]{1,0:T(8,128)(2,1)S(1)} collective-permute-done((bf16[128,512]{1,0:T(8,128)(2,1)S(1)}, bf16[128,512]{1,0:T(8,128)(2,1)S(1)}, u32[]{:S(2)}, u32[]{:S(2)}) %collective-permute-start.27) | collective-permute-done | bytes 131104 | tf_op jit(solution)/shard_map/ppermute | solution.py:267
  115.1 1.4 %place.1 = bf16[128,8192]{1,0:T(8,128)(2,1)} custom-call(s32[1]{0:T(128)} %bitcast.info, bf16[128,1024]{1,0:T(8,128)(2,1)S(1)} %get-tuple-element.63.refs_0_, bf16[128,512]{1,0:T(8,128)(2,1)S(1)} %get-tuple-element.73.refs_1_, bf16[128,512]{1,0:T(8,128)(2,1)S(1)} %get-tuple-element.77.refs_2_, bf16[128,1024]{1,0:T(8,128)(2,1)S(1)} %collective-permute-done.20.refs_3_, ...), custom_call_target="tpu_custom_call" | custom-call | tf_op jit(solution)/shard_map/place/pallas_call | solution.py:442
  116.5 0.0 all-to-all-done
  116.6 0.9 copy.10
  (11 shorter events, 0.2 us)
Async XLA Ops:
  1.6 1.7 %collective-permute-start = (bf16[32,4096]{1,0:T(8,128)(2,1)S(1)}, bf16[32,4096]{1,0:T(8,128)(2,1)S(1)}, u32[]{:S(2)}, u32[]{:S(2)}) collective-permute-start(bf16[32,4096]{1,0:T(8,128)(2,1)S(1)} %constant_dynamic-slice_fusion), channel_id=1, source_target_pairs={{0,1},{1,0},{2,3},{3,2},{4,5},{5,4},{6,7},{7,6},{8,9},{9,8},{10,11... | collective-permute-start | bytes 786440 | tf_op jit(solution)/shard_map/ppermute | solution.py:267
  4.3 20.9 %collective-permute-start.4 = (bf16[64,4096]{1,0:T(8,128)(2,1)S(1)}, bf16[64,4096]{1,0:T(8,128)(2,1)S(1)}, u32[]{:S(2)}, u32[]{:S(2)}) collective-permute-start(bf16[64,4096]{1,0:T(8,128)(2,1)S(1)} %pair.1.refs_0_), channel_id=1, source_target_pairs={{0,2},{1,3},{2,0},{3,1},{4,6},{5,7},{6,4},{7,5},{8,10},{9,11},{10,... | collective-permute-start | bytes 1572872 | tf_op jit(solution)/shard_map/ppermute | solution.py:273
  7.2 17.9 %collective-permute-start.3 = (bf16[64,4096]{1,0:T(8,128)(2,1)S(1)}, bf16[64,4096]{1,0:T(8,128)(2,1)S(1)}, u32[]{:S(2)}, u32[]{:S(2)}) collective-permute-start(bf16[64,4096]{1,0:T(8,128)(2,1)S(1)} %pair.1.refs_0_), channel_id=1, source_target_pairs={{0,4},{1,5},{2,6},{3,7},{4,8},{5,9},{6,10},{7,11},{8,12},{9,13},{1... | collective-permute-start | bytes 1572872 | tf_op jit(solution)/shard_map/ppermute | solution.py:270
  11.1 4.9 %copy-start = (bf16[128,640]{1,0:T(8,128)(2,1)S(1)}, bf16[128,640]{1,0:T(8,128)(2,1)}, u32[]{:S(2)}) copy-start(bf16[128,640]{1,0:T(8,128)(2,1)} %get-tuple-element.48) | copy-start | bytes 491524
  14.5 10.7 %collective-permute-start.5 = (bf16[128,1536]{1,0:T(8,128)(2,1)S(1)}, bf16[128,1536]{1,0:T(8,128)(2,1)S(1)}, u32[]{:S(2)}, u32[]{:S(2)}) collective-permute-start(bf16[128,1536]{1,0:T(8,128)(2,1)S(1)} %get-tuple-element.52), channel_id=1, source_target_pairs={{0,16},{1,17},{2,18},{3,19},{4,20},{5,21},{6,22},{7,23},{8,24},{9,... | collective-permute-start | bytes 1179656 | tf_op jit(solution)/shard_map/ppermute | solution.py:267
  16.1 11.2 %collective-permute-start.2 = (bf16[128,640]{1,0:T(8,128)(2,1)S(1)}, bf16[128,640]{1,0:T(8,128)(2,1)S(1)}, u32[]{:S(2)}, u32[]{:S(2)}) collective-permute-start(bf16[128,640]{1,0:T(8,128)(2,1)S(1)} %copy-done), channel_id=1, source_target_pairs={{1,5},{3,7},{5,9},{7,11},{9,13},{11,15},{17,21},{19,23},{21,25},{2... | collective-permute-start | bytes 491528 | tf_op jit(solution)/shard_map/ppermute | solution.py:279
  16.7 10.5 %collective-permute-start.1 = (bf16[128,640]{1,0:T(8,128)(2,1)S(1)}, bf16[128,640]{1,0:T(8,128)(2,1)S(1)}, u32[]{:S(2)}, u32[]{:S(2)}) collective-permute-start(bf16[128,640]{1,0:T(8,128)(2,1)S(1)} %copy-done), channel_id=1, source_target_pairs={{0,2},{1,3},{2,4},{3,5},{4,6},{5,7},{6,8},{7,9},{8,10},{9,11},{10,... | collective-permute-start | bytes 491528 | tf_op jit(solution)/shard_map/ppermute | solution.py:279
  25.2 13.4 %collective-permute-start.8 = (bf16[64,4096]{1,0:T(8,128)(2,1)S(1)}, bf16[64,4096]{1,0:T(8,128)(2,1)S(1)}, u32[]{:S(2)}, u32[]{:S(2)}) collective-permute-start(bf16[64,4096]{1,0:T(8,128)(2,1)S(1)} %collective-permute-done.3.refs_1_), channel_id=1, source_target_pairs={{0,2},{1,3},{2,0},{3,1},{4,6},{5,7},{6,4},{7,5},{8,10},{9,11},{10,... | collective-permute-start | bytes 1572872 | tf_op jit(solution)/shard_map/ppermute | solution.py:273
  25.7 14.0 %collective-permute-start.7 = (bf16[64,4096]{1,0:T(8,128)(2,1)S(1)}, bf16[64,4096]{1,0:T(8,128)(2,1)S(1)}, u32[]{:S(2)}, u32[]{:S(2)}) collective-permute-start(bf16[64,4096]{1,0:T(8,128)(2,1)S(1)} %collective-permute-done.3.refs_1_), channel_id=1, source_target_pairs={{0,4},{1,5},{2,6},{3,7},{4,8},{5,9},{6,10},{7,11},{8,12},{9,13},{1... | collective-permute-start | bytes 1572872 | tf_op jit(solution)/shard_map/ppermute | solution.py:270
  27.3 11.3 %collective-permute-start.6 = (bf16[384,640]{1,0:T(8,128)(2,1)S(1)}, bf16[384,640]{1,0:T(8,128)(2,1)S(1)}, u32[]{:S(2)}, u32[]{:S(2)}) collective-permute-start(bf16[384,640]{1,0:T(8,128)(2,1)S(1)} %pad_maximum_fusion), channel_id=1, source_target_pairs={{0,16},{1,17},{2,18},{3,19},{4,20},{5,21},{6,22},{7,23},{8,24},{9,... | collective-permute-start | bytes 1474568 | tf_op jit(solution)/shard_map/ppermute | solution.py:267
  28.9 1.7 %collective-permute-start.9 = (bf16[128,1536]{1,0:T(8,128)(2,1)S(1)}, bf16[128,1536]{1,0:T(8,128)(2,1)S(1)}, u32[]{:S(2)}, u32[]{:S(2)}) collective-permute-start(bf16[128,1536]{1,0:T(8,128)(2,1)S(1)} %get-tuple-element.56), channel_id=1, source_target_pairs={{0,1},{1,0},{2,3},{3,2},{4,5},{5,4},{6,7},{7,6},{8,9},{9,8},{10,11... | collective-permute-start | bytes 1179656 | tf_op jit(solution)/shard_map/ppermute | solution.py:267
  39.7 14.6 %collective-permute-start.11 = (bf16[64,4096]{1,0:T(8,128)(2,1)S(1)}, bf16[64,4096]{1,0:T(8,128)(2,1)S(1)}, u32[]{:S(2)}, u32[]{:S(2)}) collective-permute-start(bf16[64,4096]{1,0:T(8,128)(2,1)S(1)} %collective-permute-done.7.refs_2_), channel_id=1, source_target_pairs={{0,4},{1,5},{2,6},{3,7},{4,8},{5,9},{6,10},{7,11},{8,12},{9,13},{1... | collective-permute-start | bytes 1572872 | tf_op jit(solution)/shard_map/ppermute | solution.py:270
  41.3 14.4 %collective-permute-start.10 = (bf16[768,640]{1,0:T(8,128)(2,1)S(1)}, bf16[768,640]{1,0:T(8,128)(2,1)S(1)}, u32[]{:S(2)}, u32[]{:S(2)}) collective-permute-start(bf16[768,640]{1,0:T(8,128)(2,1)S(1)} %constant_dynamic-update-slice_fusion.own), channel_id=1, source_target_pairs={{0,1},{1,0},{2,3},{3,2},{4,5},{5,4},{6,7},{7,6},{8,9},{9,8},{10,11... | collective-permute-start | bytes 2949128 | tf_op jit(solution)/shard_map/ppermute | solution.py:267
  41.4 14.3 %collective-permute-start.12 = (bf16[64,4096]{1,0:T(8,128)(2,1)S(1)}, bf16[64,4096]{1,0:T(8,128)(2,1)S(1)}, u32[]{:S(2)}, u32[]{:S(2)}) collective-permute-start(bf16[64,4096]{1,0:T(8,128)(2,1)S(1)} %collective-permute-done.7.refs_2_), channel_id=1, source_target_pairs={{0,2},{1,3},{2,0},{3,1},{4,6},{5,7},{6,4},{7,5},{8,10},{9,11},{10,... | collective-permute-start | bytes 1572872 | tf_op jit(solution)/shard_map/ppermute | solution.py:273
  41.9 12.4 %collective-permute-start.13 = (bf16[128,1536]{1,0:T(8,128)(2,1)S(1)}, bf16[128,1536]{1,0:T(8,128)(2,1)S(1)}, u32[]{:S(2)}, u32[]{:S(2)}) collective-permute-start(bf16[128,1536]{1,0:T(8,128)(2,1)S(1)} %get-tuple-element.60), channel_id=1, source_target_pairs={{0,17},{1,16},{2,19},{3,18},{4,21},{5,20},{6,23},{7,22},{8,25},{9,... | collective-permute-start | bytes 1179656 | tf_op jit(solution)/shard_map/ppermute | solution.py:267
  55.7 9.2 %collective-permute-start.14 = (bf16[64,2048]{1,0:T(8,128)(2,1)S(1)}, bf16[64,2048]{1,0:T(8,128)(2,1)S(1)}, u32[]{:S(2)}, u32[]{:S(2)}) collective-permute-start(bf16[64,2048]{1,0:T(8,128)(2,1)S(1)} %get-tuple-element.61), channel_id=1, source_target_pairs={{0,2},{1,3},{2,0},{3,1},{4,6},{5,7},{6,4},{7,5},{8,10},{9,11},{10,... | collective-permute-start | bytes 786440 | tf_op jit(solution)/shard_map/ppermute | solution.py:273
  56.2 21.5 %collective-permute-start.17 = (bf16[128,1536]{1,0:T(8,128)(2,1)S(1)}, bf16[128,1536]{1,0:T(8,128)(2,1)S(1)}, u32[]{:S(2)}, u32[]{:S(2)}) collective-permute-start(bf16[128,1536]{1,0:T(8,128)(2,1)S(1)} %get-tuple-element.70), channel_id=1, source_target_pairs={{0,16},{1,17},{2,18},{3,19},{4,20},{5,21},{6,22},{7,23},{8,24},{9,... | collective-permute-start | bytes 1179656 | tf_op jit(solution)/shard_map/ppermute | solution.py:267
  57.7 20.0 %collective-permute-start.15 = (bf16[64,2048]{1,0:T(8,128)(2,1)S(1)}, bf16[64,2048]{1,0:T(8,128)(2,1)S(1)}, u32[]{:S(2)}, u32[]{:S(2)}) collective-permute-start(bf16[64,2048]{1,0:T(8,128)(2,1)S(1)} %get-tuple-element.65), channel_id=1, source_target_pairs={{0,2},{1,3},{2,0},{3,1},{4,6},{5,7},{6,4},{7,5},{8,10},{9,11},{10,... | collective-permute-start | bytes 786440 | tf_op jit(solution)/shard_map/ppermute | solution.py:273
  58.8 18.9 %collective-permute-start.16 = (bf16[128,1536]{1,0:T(8,128)(2,1)S(1)}, bf16[128,1536]{1,0:T(8,128)(2,1)S(1)}, u32[]{:S(2)}, u32[]{:S(2)}) collective-permute-start(bf16[128,1536]{1,0:T(8,128)(2,1)S(1)} %get-tuple-element.68), channel_id=1, source_target_pairs={{0,1},{1,0},{2,3},{3,2},{4,5},{5,4},{6,7},{7,6},{8,9},{9,8},{10,11... | collective-permute-start | bytes 1179656 | tf_op jit(solution)/shard_map/ppermute | solution.py:267
  58.8 18.9 %collective-permute-start.18 = (bf16[128,1536]{1,0:T(8,128)(2,1)S(1)}, bf16[128,1536]{1,0:T(8,128)(2,1)S(1)}, u32[]{:S(2)}, u32[]{:S(2)}) collective-permute-start(bf16[128,1536]{1,0:T(8,128)(2,1)S(1)} %get-tuple-element.72), channel_id=1, source_target_pairs={{0,17},{1,16},{2,19},{3,18},{4,21},{5,20},{6,23},{7,22},{8,25},{9,... | collective-permute-start | bytes 1179656 | tf_op jit(solution)/shard_map/ppermute | solution.py:267
  76.6 7.3 %collective-permute-start.19 = (bf16[128,1024]{1,0:T(8,128)(2,1)S(1)}, bf16[128,1024]{1,0:T(8,128)(2,1)S(1)}, u32[]{:S(2)}, u32[]{:S(2)}) collective-permute-start(bf16[128,1024]{1,0:T(8,128)(2,1)S(1)} %get-tuple-element.75), channel_id=1, source_target_pairs={{0,16},{1,17},{2,18},{3,19},{4,20},{5,21},{6,22},{7,23},{8,24},{9,... | collective-permute-start | bytes 786440 | tf_op jit(solution)/shard_map/ppermute | solution.py:267
  90.1 26.4 %all-to-all-start = ((bf16[16,16,576]{2,1,0:T(8,128)(2,1)}), bf16[16,16,576]{2,1,0:T(8,128)(2,1)S(1)}, u32[]{:S(2)}, u32[]{:S(2)}) async-start(bf16[16,16,576]{2,1,0:T(8,128)(2,1)} %bitcast.5), calls=%async_computation | async-start | bytes 655360 | tf_op jit(solution)/shard_map/all_to_all | solution.py:434
  95.2 2.6 %collective-permute-start.20 = (bf16[128,1024]{1,0:T(8,128)(2,1)S(1)}, bf16[128,1024]{1,0:T(8,128)(2,1)S(1)}, u32[]{:S(2)}, u32[]{:S(2)}) collective-permute-start(bf16[128,1024]{1,0:T(8,128)(2,1)S(1)} %get-tuple-element.78), channel_id=1, source_target_pairs={{0,1},{1,0},{2,3},{3,2},{4,5},{5,4},{6,7},{7,6},{8,9},{9,8},{10,11... | collective-permute-start | bytes 786440 | tf_op jit(solution)/shard_map/ppermute | solution.py:267
  95.6 8.3 %collective-permute-start.25 = (bf16[128,1024]{1,0:T(8,128)(2,1)S(1)}, bf16[128,1024]{1,0:T(8,128)(2,1)S(1)}, u32[]{:S(2)}, u32[]{:S(2)}) collective-permute-start(bf16[128,1024]{1,0:T(8,128)(2,1)S(1)} %get-tuple-element.83), channel_id=1, source_target_pairs={{0,17},{1,16},{2,19},{3,18},{4,21},{5,20},{6,23},{7,22},{8,25},{9,... | collective-permute-start | bytes 786440 | tf_op jit(solution)/shard_map/ppermute | solution.py:267
  95.9 8.5 %collective-permute-start.21 = (bf16[128,512]{1,0:T(8,128)(2,1)S(1)}, bf16[128,512]{1,0:T(8,128)(2,1)S(1)}, u32[]{:S(2)}, u32[]{:S(2)}) collective-permute-start(bf16[128,512]{1,0:T(8,128)(2,1)S(1)} %get-tuple-element.79), channel_id=1, source_target_pairs={{0,1},{1,0},{2,3},{3,2},{4,5},{5,4},{6,7},{7,6},{8,9},{9,8},{10,11... | collective-permute-start | bytes 393224 | tf_op jit(solution)/shard_map/ppermute | solution.py:267
  96.3 11.1 %collective-permute-start.23 = (bf16[128,512]{1,0:T(8,128)(2,1)S(1)}, bf16[128,512]{1,0:T(8,128)(2,1)S(1)}, u32[]{:S(2)}, u32[]{:S(2)}) collective-permute-start(bf16[128,512]{1,0:T(8,128)(2,1)S(1)} %get-tuple-element.81), channel_id=1, source_target_pairs={{0,16},{1,17},{2,18},{3,19},{4,20},{5,21},{6,22},{7,23},{8,24},{9,... | collective-permute-start | bytes 393224 | tf_op jit(solution)/shard_map/ppermute | solution.py:267
  97.8 11.7 %collective-permute-start.26 = (bf16[128,512]{1,0:T(8,128)(2,1)S(1)}, bf16[128,512]{1,0:T(8,128)(2,1)S(1)}, u32[]{:S(2)}, u32[]{:S(2)}) collective-permute-start(bf16[128,512]{1,0:T(8,128)(2,1)S(1)} %get-tuple-element.84), channel_id=1, source_target_pairs={{0,17},{1,16},{2,19},{3,18},{4,21},{5,20},{6,23},{7,22},{8,25},{9,... | collective-permute-start | bytes 393224 | tf_op jit(solution)/shard_map/ppermute | solution.py:267
  97.8 11.7 %collective-permute-start.22 = (bf16[128,512]{1,0:T(8,128)(2,1)S(1)}, bf16[128,512]{1,0:T(8,128)(2,1)S(1)}, u32[]{:S(2)}, u32[]{:S(2)}) collective-permute-start(bf16[128,512]{1,0:T(8,128)(2,1)S(1)} %get-tuple-element.80), channel_id=1, source_target_pairs={{0,1},{1,0},{2,3},{3,2},{4,5},{5,4},{6,7},{7,6},{8,9},{9,8},{10,11... | collective-permute-start | bytes 393224 | tf_op jit(solution)/shard_map/ppermute | solution.py:267
  103.9 9.1 %collective-permute-start.24 = (bf16[128,512]{1,0:T(8,128)(2,1)S(1)}, bf16[128,512]{1,0:T(8,128)(2,1)S(1)}, u32[]{:S(2)}, u32[]{:S(2)}) collective-permute-start(bf16[128,512]{1,0:T(8,128)(2,1)S(1)} %get-tuple-element.82), channel_id=1, source_target_pairs={{0,16},{1,17},{2,18},{3,19},{4,20},{5,21},{6,22},{7,23},{8,24},{9,... | collective-permute-start | bytes 393224 | tf_op jit(solution)/shard_map/ppermute | solution.py:267
  104.4 10.7 %collective-permute-start.27 = (bf16[128,512]{1,0:T(8,128)(2,1)S(1)}, bf16[128,512]{1,0:T(8,128)(2,1)S(1)}, u32[]{:S(2)}, u32[]{:S(2)}) collective-permute-start(bf16[128,512]{1,0:T(8,128)(2,1)S(1)} %get-tuple-element.85), channel_id=1, source_target_pairs={{0,17},{1,16},{2,19},{3,18},{4,21},{5,20},{6,23},{7,22},{8,25},{9,... | collective-permute-start | bytes 393224 | tf_op jit(solution)/shard_map/ppermute | solution.py:267

commit v7 on v6

--- a/solution.py
+++ b/solution.py
@@ -18,7 +18,12 @@
 QUAD = 4
 HQ = H // QUAD
 CHUNK_HEADS = (8, 8)
-PHASES = "z y0 b~ f~ q02 | z y1 k q01 | z y2 p q03 q12~ | y3 q13~ q11"
+PHASES = (
+    ("z", "y0", "b~", "f~", "q02"),
+    ("z", "y1", "k", "q01"),
+    ("z", "y2", "p", "q03", "q12~"),
+    ("y3", "q13~", "q11"),
+)
 CHUNKS = len(CHUNK_HEADS)
 FIRST_HEAD = tuple(sum(CHUNK_HEADS[:j]) for j in range(CHUNKS))
 ROW = LAT + ROPE
@@ -284,7 +289,7 @@
     give = lax.dynamic_slice_in_dim(w_up, (quarter ^ 1) * width, width, 1)
     give, lengths = lax.optimization_barrier((give, lengths))
     got = quad_swap(give, 1)
-    outer = size // 4 if size % 4 == 0 and size // 4 <= 4 else 0
+    outer = 4 if size == 16 else 0
     if outer:
         pair_rows = pl.pallas_call(
             pair_kernel,
@@ -354,9 +359,10 @@
     halves = []
     moved = [[queries[j]] + [None] * (QUAD - 1) for j in range(CHUNKS)]
     parts = {"r": tie(rows, pair_rows if outer else got)}
-    for name in PHASES.split():
+    for name in [name for phase in PHASES for name in phase + ("|",)]:
         kind, late = name[0], name[-1] == "~"
         if kind == "|":
+            phases.now.append(queries[0])
             phases.turn()
         elif kind == "z" and outer:
             line.append(phases.send(late, around, line[-1], 4))
@@ -426,13 +432,15 @@
     results = []
     for call in CALLS:
         if len(results) > 1:
-            mine_info = tie(mine_info, results[-2][2])
+            mine_info = tie(mine_info, *results[-2][1:3])
         pieces = attend(*call)
         mine_info = tie(mine_info, pieces[0])
-        results.append([pieces[0]] + [quad_swap(pieces[r], r) for r in range(1, QUAD)])
+        results.append(
+            [pieces[0]] + [quad_swap(pieces[r], r) for r in range(1, QUAD)]
+        )
     pieces = [one[r] for r in range(QUAD) for one in results]
     arrived = lax.all_to_all(
-        tie(outgoing, results[-1][0]).reshape(size, slot_count, ROW),
+        tie(outgoing, results[-1][2]).reshape(size, slot_count, ROW),
         "ctx",
         split_axis=0,
         concat_axis=0,

time: 118 us -> 121 us (1.025)
  waiting for transfers between devices: 50.3 us -> 51.9 us
    ppermute x18, starting transfers between devices: 13.7 us -> 15.5 us  [quad_swap(): return lax.ppermute(array, ('groups', 'ctx'), pairs)]
    ppermute x18, waiting for transfers between devices: 31.7 us -> 33.3 us  [quad_swap(): return lax.ppermute(array, ('groups', 'ctx'), pairs)]
  transfers between devices with their start and end apart: 29 -> 29, of which waited for: 13 -> 14; matrix products, arithmetic and copies ran while one was open for 0% -> 0% of each run, Pallas kernels for 21% -> 21%
where the time goes in v7:
time: 121 us; the launch traced here: 120 us
  waiting for transfers between devices  51.9 us (43%)
  starting transfers between devices  33.4 us (28%)
  Pallas kernels  32 us (26%)
  local copies, waits for them, and re-layouts  2.01 us (2%)
    ppermute x18, waiting for transfers between devices, quad_swap(): return lax.ppermute(array, ('groups', 'ctx'), pairs)  33.3 us
    pallas_call x3, Pallas kernels, attend(): pl.pallas_call(functools.partial(attend_kernel, outer), grid=(steps,), ou...  24 us
    ppermute x18, starting transfers between devices, quad_swap(): return lax.ppermute(array, ('groups', 'ctx'), pairs)  15.5 us
    ppermute x3, waiting for transfers between devices, around(): lax.ppermute(array, 'ctx', [(i, (i + by) % size) for i in range(size)])  12.2 us
    ppermute x5, waiting for transfers between devices, inner_swap(): return lax.ppermute(array, 'ctx', [(i, i ^ 2) for i in range(size)])  6.44 us
    ppermute x5, starting transfers between devices, inner_swap(): return lax.ppermute(array, 'ctx', [(i, i ^ 2) for i in range(size)])  5.53 us
    ppermute x3, starting transfers between devices, around(): lax.ppermute(array, 'ctx', [(i, (i + by) % size) for i in range(size)])  4.72 us
    all_to_all x1, starting transfers between devices, body(): lax.all_to_all(tie(outgoing, results[-1][2]).reshape(size, slot_count, RO...  4.63 us
  transfers between devices with their start and end apart: 29, of which 14 were waited for; matrix products, arithmetic and copies ran while one was open for 0% of the time, Pallas kernels for 21%

profile of v7, /device:TPU:0, one launch (start us, length us, event | category | flops | bytes accessed | tf_op | source)
XLA Modules:
  0.0 120.2 jit_solution(850564641490287760)
XLA Ops:
  0.6 1.0 constant_dynamic-slice_fusion
  1.6 0.5 collective-permute-start
  2.1 1.2 collective-permute-done.got
  3.3 1.0 pair.1.refs_0_
  4.3 3.0 %collective-permute-start.4 = (bf16[64,4096]{1,0:T(8,128)(2,1)S(1)}, bf16[64,4096]{1,0:T(8,128)(2,1)S(1)}, u32[]{:S(2)}, u32[]{:S(2)}) collective-permute-start(bf16[64,4096]{1,0:T(8,128)(2,1)S(1)} %pair.1.refs_0_), channel_id=1, source_target_pairs={{0,2},{1,3},{2,0},{3,1},{4,6},{5,7},{6,4},{7,5},{8,10},{9,11},{10,... | collective-permute-start | bytes 1572872 | tf_op jit(solution)/shard_map/ppermute | solution.py:278
  7.2 1.6 %collective-permute-start.3 = (bf16[64,4096]{1,0:T(8,128)(2,1)S(1)}, bf16[64,4096]{1,0:T(8,128)(2,1)S(1)}, u32[]{:S(2)}, u32[]{:S(2)}) collective-permute-start(bf16[64,4096]{1,0:T(8,128)(2,1)S(1)} %pair.1.refs_0_), channel_id=1, source_target_pairs={{0,4},{1,5},{2,6},{3,7},{4,8},{5,9},{6,10},{7,11},{8,12},{9,13},{1... | collective-permute-start | bytes 1572872 | tf_op jit(solution)/shard_map/ppermute | solution.py:275
  8.8 2.3 %rows.1 = (bf16[128,640]{1,0:T(8,128)(2,1)}, f32[128,128]{1,0:T(8,128)}, f32[128,128]{1,0:T(8,128)}, bf16[256,576]{1,0:T(8,128)(2,1)}) custom-call(s32[1]{0:T(128)} %bitcast.1.info, s32[8]{0:T(128)} %lengths, bf16[576,128]{1,0:T(8,128)(2,1)} %bitcast.8, f32[1,512]{1,0:T(1,128)} %bitcast.9, s32[1,128]{1,0:T(1,128)} %bitcast.10, f32[1,128]{1,0:T(1,128)} %constant.30.clone.freq), custom_call_target="tpu_custom_call" | custom-call | tf_op jit(solution)/shard_map/rows/pallas_call | solution.py:319
  11.1 3.4 %queries.1 = (bf16[128,1536]{1,0:T(8,128)(2,1)S(1)}, bf16[128,1536]{1,0:T(8,128)(2,1)S(1)}, bf16[128,1536]{1,0:T(8,128)(2,1)S(1)}, bf16[128,1536]{1,0:T(8,128)(2...) custom-call(s32[1]{0:T(128)} %bitcast.info, ...), custom_call_target="tpu_custom_call" | custom-call | bytes 6291456 | tf_op jit(solution)/shard_map/queries/pallas_call | solution.py:343
  14.5 1.6 %collective-permute-start.5 = (bf16[128,1536]{1,0:T(8,128)(2,1)S(1)}, bf16[128,1536]{1,0:T(8,128)(2,1)S(1)}, u32[]{:S(2)}, u32[]{:S(2)}) collective-permute-start(bf16[128,1536]{1,0:T(8,128)(2,1)S(1)} %get-tuple-element.52), channel_id=1, source_target_pairs={{0,16},{1,17},{2,18},{3,19},{4,20},{5,21},{6,22},{7,23},{8,24},{9,... | collective-permute-start | bytes 1179656 | tf_op jit(solution)/shard_map/ppermute | solution.py:272
  16.1 0.7 collective-permute-start.2
  16.7 2.4 %collective-permute-start.1 = (bf16[128,640]{1,0:T(8,128)(2,1)S(1)}, bf16[128,640]{1,0:T(8,128)(2,1)S(1)}, u32[]{:S(2)}, u32[]{:S(2)}) collective-permute-start(bf16[128,640]{1,0:T(8,128)(2,1)S(1)} %copy-done), channel_id=1, source_target_pairs={{0,2},{1,3},{2,4},{3,5},{4,6},{5,7},{6,8},{7,9},{8,10},{9,11},{10,... | collective-permute-start | bytes 491528 | tf_op jit(solution)/shard_map/ppermute | solution.py:284
  19.2 6.0 %collective-permute-done.5.refs_10_.refs_14_ = bf16[128,1536]{1,0:T(8,128)(2,1)S(1)} collective-permute-done((bf16[128,1536]{1,0:T(8,128)(2,1)S(1)}, bf16[128,1536]{1,0:T(8,128)(2,1)S(1)}, u32[]{:S(2)}, u32[]{:S(2)}) %collective-permute-start.5) | collective-permute-done | bytes 393248 | tf_op jit(solution)/shard_map/ppermute | solution.py:272
  25.2 0.0 collective-permute-done.4.refs_4_
  25.2 0.0 collective-permute-done.3.refs_1_
  25.2 0.5 collective-permute-start.8
  25.7 1.6 %collective-permute-start.7 = (bf16[64,4096]{1,0:T(8,128)(2,1)S(1)}, bf16[64,4096]{1,0:T(8,128)(2,1)S(1)}, u32[]{:S(2)}, u32[]{:S(2)}) collective-permute-start(bf16[64,4096]{1,0:T(8,128)(2,1)S(1)} %collective-permute-done.3.refs_1_), channel_id=1, source_target_pairs={{0,4},{1,5},{2,6},{3,7},{4,8},{5,9},{6,10},{7,11},{8,12},{9,13},{1... | collective-permute-start | bytes 1572872 | tf_op jit(solution)/shard_map/ppermute | solution.py:275
  27.3 0.0 collective-permute-done.1
  27.3 1.6 %collective-permute-start.6 = (bf16[384,640]{1,0:T(8,128)(2,1)S(1)}, bf16[384,640]{1,0:T(8,128)(2,1)S(1)}, u32[]{:S(2)}, u32[]{:S(2)}) collective-permute-start(bf16[384,640]{1,0:T(8,128)(2,1)S(1)} %pad_maximum_fusion), channel_id=1, source_target_pairs={{0,16},{1,17},{2,18},{3,19},{4,20},{5,21},{6,22},{7,23},{8,24},{9,... | collective-permute-start | bytes 1474568 | tf_op jit(solution)/shard_map/ppermute | solution.py:272
  28.9 1.6 %collective-permute-done.9.refs_9_.refs_13_ = bf16[128,1536]{1,0:T(8,128)(2,1)S(1)} collective-permute-done((bf16[128,1536]{1,0:T(8,128)(2,1)S(1)}, bf16[128,1536]{1,0:T(8,128)(2,1)S(1)}, u32[]{:S(2)}, u32[]{:S(2)}) %collective-permute-start.9) | collective-permute-done | bytes 393248 | tf_op jit(solution)/shard_map/ppermute | solution.py:272
  30.6 8.0 %collective-permute-done.6 = bf16[384,640]{1,0:T(8,128)(2,1)S(1)} collective-permute-done((bf16[384,640]{1,0:T(8,128)(2,1)S(1)}, bf16[384,640]{1,0:T(8,128)(2,1)S(1)}, u32[]{:S(2)}, u32[]{:S(2)}) %collective-permute-start.6) | collective-permute-done | bytes 491552 | tf_op jit(solution)/shard_map/ppermute | solution.py:272
  38.6 0.0 collective-permute-done.8.refs_5_
  38.6 1.1 collective-permute-done.7.refs_2_
  39.7 1.6 %collective-permute-start.11 = (bf16[64,4096]{1,0:T(8,128)(2,1)S(1)}, bf16[64,4096]{1,0:T(8,128)(2,1)S(1)}, u32[]{:S(2)}, u32[]{:S(2)}) collective-permute-start(bf16[64,4096]{1,0:T(8,128)(2,1)S(1)} %collective-permute-done.7.refs_2_), channel_id=1, source_target_pairs={{0,4},{1,5},{2,6},{3,7},{4,8},{5,9},{6,10},{7,11},{8,12},{9,13},{1... | collective-permute-start | bytes 1572872 | tf_op jit(solution)/shard_map/ppermute | solution.py:275
  41.3 0.1 constant_dynamic-update-slice_fusion.own
  41.3 0.1 collective-permute-start.10
  41.4 0.5 collective-permute-start.12
  41.9 1.3 %collective-permute-start.13 = (bf16[128,1536]{1,0:T(8,128)(2,1)S(1)}, bf16[128,1536]{1,0:T(8,128)(2,1)S(1)}, u32[]{:S(2)}, u32[]{:S(2)}) collective-permute-start(bf16[128,1536]{1,0:T(8,128)(2,1)S(1)} %get-tuple-element.61), channel_id=1, source_target_pairs={{0,17},{1,16},{2,19},{3,18},{4,21},{5,20},{6,23},{7,22},{8,25},{9,... | collective-permute-start | bytes 1179656 | tf_op jit(solution)/shard_map/ppermute | solution.py:272
  43.2 11.1 %collective-permute-done.11.refs_3_ = bf16[64,4096]{1,0:T(8,128)(2,1)S(1)} collective-permute-done((bf16[64,4096]{1,0:T(8,128)(2,1)S(1)}, bf16[64,4096]{1,0:T(8,128)(2,1)S(1)}, u32[]{:S(2)}, u32[]{:S(2)}) %collective-permute-start.11) | collective-permute-done | bytes 524320 | tf_op jit(solution)/shard_map/ppermute | solution.py:275
  54.3 0.0 collective-permute-done.13.refs_11_.refs_15_
  54.4 1.4 %collective-permute-done.12.refs_6_ = bf16[64,4096]{1,0:T(8,128)(2,1)S(1)} collective-permute-done((bf16[64,4096]{1,0:T(8,128)(2,1)S(1)}, bf16[64,4096]{1,0:T(8,128)(2,1)S(1)}, u32[]{:S(2)}, u32[]{:S(2)}) %collective-permute-start.12) | collective-permute-done | bytes 524320 | tf_op jit(solution)/shard_map/ppermute | solution.py:278
  55.7 0.0 collective-permute-done.10.other
  55.7 0.5 collective-permute-start.14
  56.2 1.5 %collective-permute-start.17 = (bf16[128,1536]{1,0:T(8,128)(2,1)S(1)}, bf16[128,1536]{1,0:T(8,128)(2,1)S(1)}, u32[]{:S(2)}, u32[]{:S(2)}) collective-permute-start(bf16[128,1536]{1,0:T(8,128)(2,1)S(1)} %get-tuple-element.70), channel_id=1, source_target_pairs={{0,16},{1,17},{2,18},{3,19},{4,20},{5,21},{6,22},{7,23},{8,24},{9,... | collective-permute-start | bytes 1179656 | tf_op jit(solution)/shard_map/ppermute | solution.py:272
  57.7 1.1 collective-permute-start.15
  58.8 0.0 collective-permute-start.16
  58.8 1.1 collective-permute-start.18
  59.9 5.0 %collective-permute-done.14.refs_7_ = bf16[64,2048]{1,0:T(8,128)(2,1)S(1)} collective-permute-done((bf16[64,2048]{1,0:T(8,128)(2,1)S(1)}, bf16[64,2048]{1,0:T(8,128)(2,1)S(1)}, u32[]{:S(2)}, u32[]{:S(2)}) %collective-permute-start.14) | collective-permute-done | bytes 262176 | tf_op jit(solution)/shard_map/ppermute | solution.py:278
  65.0 11.6 %attend.3 = (bf16[128,1024]{1,0:T(8,128)(2,1)S(1)}, bf16[128,1024]{1,0:T(8,128)(2,1)S(1)}, bf16[128,1024]{1,0:T(8,128)(2,1)S(1)}, bf16[128,1024]{1,0:T(8,128)(2,1)S(1)}) custom-call(s32[1]{0:T(128)} %bitcast.1.info, bf16[768,640]{1,0:T(8,128)(2,1)S(1)} %constant_dynamic-update-slice_fusion.own, bf16[768,640]{1,0:T(8,128)(2,1)S(1)} %collective-permute-done.10.other, ...), custom_call_target="tpu_custom_call" | custom-call | flops 4362076160 | bytes 8388608 | tf_op jit(solution)/shard_map/attend/pallas_call | solution.py:404
  76.6 0.1 collective-permute-start.19
  76.7 0.0 collective-permute-done.17.refs_10_.refs_14_
  76.7 1.1 collective-permute-start.20
  77.8 0.0 collective-permute-done.15.refs_7_
  77.8 0.0 collective-permute-done.16.refs_9_.refs_13_
  77.8 0.0 collective-permute-done.18.refs_11_.refs_15_
  77.8 6.2 %attend.4 = (bf16[128,512]{1,0:T(8,128)(2,1)S(1)}, bf16[128,512]{1,0:T(8,128)(2,1)S(1)}, bf16[128,512]{1,0:T(8,128)(2,1)S(1)}, bf16[128,512]{1,0:T(8,128)(2,1)S(1)}) custom-call(s32[1]{0:T(128)} %bitcast.1.info, bf16[768,640]{1,0:T(8,128)(2,1)S(1)} %constant_dynamic-update-slice_fusion.own, bf16[768,640]{1,0:T(8,128)(2,1)S(1)} %collective-permute-done.10.other, ...), custom_call_target="tpu_custom_call" | custom-call | flops 2181038080 | bytes 4194304 | tf_op jit(solution)/shard_map/attend/pallas_call | solution.py:404
  84.0 0.0 collective-permute-done.19.refs_3_
  84.0 1.4 %collective-permute-done.20.refs_6_ = bf16[128,1024]{1,0:T(8,128)(2,1)S(1)} collective-permute-done((bf16[128,1024]{1,0:T(8,128)(2,1)S(1)}, bf16[128,1024]{1,0:T(8,128)(2,1)S(1)}, u32[]{:S(2)}, u32[]{:S(2)}) %collective-permute-start.20) | collective-permute-done | bytes 262176 | tf_op jit(solution)/shard_map/ppermute | solution.py:272
  85.4 6.1 %attend.5 = (bf16[128,512]{1,0:T(8,128)(2,1)S(1)}, bf16[128,512]{1,0:T(8,128)(2,1)S(1)}, bf16[128,512]{1,0:T(8,128)(2,1)S(1)}, bf16[128,512]{1,0:T(8,128)(2,1)S(1)}) custom-call(s32[1]{0:T(128)} %bitcast.1.info, bf16[768,640]{1,0:T(8,128)(2,1)S(1)} %constant_dynamic-update-slice_fusion.own, bf16[768,640]{1,0:T(8,128)(2,1)S(1)} %collective-permute-done.10.other, ...), custom_call_target="tpu_custom_call" | custom-call | flops 2181038080 | bytes 4194304 | tf_op jit(solution)/shard_map/attend/pallas_call | solution.py:404
  91.6 1.1 collective-permute-start.24
  92.6 4.0 %collective-permute-done.24.refs_8_ = bf16[128,512]{1,0:T(8,128)(2,1)S(1)} collective-permute-done((bf16[128,512]{1,0:T(8,128)(2,1)S(1)}, bf16[128,512]{1,0:T(8,128)(2,1)S(1)}, u32[]{:S(2)}, u32[]{:S(2)}) %collective-permute-start.24) | collective-permute-done | bytes 131104 | tf_op jit(solution)/shard_map/ppermute | solution.py:272
  96.7 4.6 %all-to-all-start = ((bf16[16,16,576]{2,1,0:T(8,128)(2,1)}), bf16[16,16,576]{2,1,0:T(8,128)(2,1)S(1)}, u32[]{:S(2)}, u32[]{:S(2)}) async-start(bf16[16,16,576]{2,1,0:T(8,128)(2,1)} %bitcast.5), calls=%async_computation | async-start | bytes 655360 | tf_op jit(solution)/shard_map/all_to_all | solution.py:442
  101.3 1.5 %collective-permute-start.25 = (bf16[128,1024]{1,0:T(8,128)(2,1)S(1)}, bf16[128,1024]{1,0:T(8,128)(2,1)S(1)}, u32[]{:S(2)}, u32[]{:S(2)}) collective-permute-start(bf16[128,1024]{1,0:T(8,128)(2,1)S(1)} %get-tuple-element.83), channel_id=1, source_target_pairs={{0,17},{1,16},{2,19},{3,18},{4,21},{5,20},{6,23},{7,22},{8,25},{9,... | collective-permute-start | bytes 786440 | tf_op jit(solution)/shard_map/ppermute | solution.py:272
  102.8 0.2 collective-permute-start.21
  103.0 0.5 collective-permute-start.23
  103.5 1.2 collective-permute-start.26
  104.7 0.4 collective-permute-start.22
  105.1 4.4 %collective-permute-done.25.refs_9_ = bf16[128,1024]{1,0:T(8,128)(2,1)S(1)} collective-permute-done((bf16[128,1024]{1,0:T(8,128)(2,1)S(1)}, bf16[128,1024]{1,0:T(8,128)(2,1)S(1)}, u32[]{:S(2)}, u32[]{:S(2)}) %collective-permute-start.25) | collective-permute-done | bytes 262176 | tf_op jit(solution)/shard_map/ppermute | solution.py:272
  109.5 1.8 %collective-permute-start.27 = (bf16[128,512]{1,0:T(8,128)(2,1)S(1)}, bf16[128,512]{1,0:T(8,128)(2,1)S(1)}, u32[]{:S(2)}, u32[]{:S(2)}) collective-permute-start(bf16[128,512]{1,0:T(8,128)(2,1)S(1)} %get-tuple-element.85), channel_id=1, source_target_pairs={{0,17},{1,16},{2,19},{3,18},{4,21},{5,20},{6,23},{7,22},{8,25},{9,... | collective-permute-start | bytes 393224 | tf_op jit(solution)/shard_map/ppermute | solution.py:272
  111.3 1.9 %collective-permute-done.23.refs_7_ = bf16[128,512]{1,0:T(8,128)(2,1)S(1)} collective-permute-done((bf16[128,512]{1,0:T(8,128)(2,1)S(1)}, bf16[128,512]{1,0:T(8,128)(2,1)S(1)}, u32[]{:S(2)}, u32[]{:S(2)}) %collective-permute-start.23) | collective-permute-done | bytes 131104 | tf_op jit(solution)/shard_map/ppermute | solution.py:272
  113.2 1.9 %collective-permute-done.26.refs_10_ = bf16[128,512]{1,0:T(8,128)(2,1)S(1)} collective-permute-done((bf16[128,512]{1,0:T(8,128)(2,1)S(1)}, bf16[128,512]{1,0:T(8,128)(2,1)S(1)}, u32[]{:S(2)}, u32[]{:S(2)}) %collective-permute-start.26) | collective-permute-done | bytes 131104 | tf_op jit(solution)/shard_map/ppermute | solution.py:272
  115.1 2.8 %collective-permute-done.27.refs_11_ = bf16[128,512]{1,0:T(8,128)(2,1)S(1)} collective-permute-done((bf16[128,512]{1,0:T(8,128)(2,1)S(1)}, bf16[128,512]{1,0:T(8,128)(2,1)S(1)}, u32[]{:S(2)}, u32[]{:S(2)}) %collective-permute-start.27) | collective-permute-done | bytes 131104 | tf_op jit(solution)/shard_map/ppermute | solution.py:272
  117.9 1.4 %place.1 = bf16[128,8192]{1,0:T(8,128)(2,1)} custom-call(s32[1]{0:T(128)} %bitcast.info, bf16[128,1024]{1,0:T(8,128)(2,1)S(1)} %get-tuple-element.63.refs_0_, bf16[128,512]{1,0:T(8,128)(2,1)S(1)} %get-tuple-element.73.refs_1_, bf16[128,512]{1,0:T(8,128)(2,1)S(1)} %get-tuple-element.78.refs_2_, bf16[128,1024]{1,0:T(8,128)(2,1)S(1)} %collective-permute-done.19.refs_3_, ...), custom_call_target="tpu_custom_call" | custom-call | tf_op jit(solution)/shard_map/place/pallas_call | solution.py:450
  119.4 0.0 all-to-all-done
  119.4 0.9 copy.10
  (11 shorter events, 0.2 us)
Async XLA Ops:
  1.6 1.7 %collective-permute-start = (bf16[32,4096]{1,0:T(8,128)(2,1)S(1)}, bf16[32,4096]{1,0:T(8,128)(2,1)S(1)}, u32[]{:S(2)}, u32[]{:S(2)}) collective-permute-start(bf16[32,4096]{1,0:T(8,128)(2,1)S(1)} %constant_dynamic-slice_fusion), channel_id=1, source_target_pairs={{0,1},{1,0},{2,3},{3,2},{4,5},{5,4},{6,7},{7,6},{8,9},{9,8},{10,11... | collective-permute-start | bytes 786440 | tf_op jit(solution)/shard_map/ppermute | solution.py:272
  4.3 20.9 %collective-permute-start.4 = (bf16[64,4096]{1,0:T(8,128)(2,1)S(1)}, bf16[64,4096]{1,0:T(8,128)(2,1)S(1)}, u32[]{:S(2)}, u32[]{:S(2)}) collective-permute-start(bf16[64,4096]{1,0:T(8,128)(2,1)S(1)} %pair.1.refs_0_), channel_id=1, source_target_pairs={{0,2},{1,3},{2,0},{3,1},{4,6},{5,7},{6,4},{7,5},{8,10},{9,11},{10,... | collective-permute-start | bytes 1572872 | tf_op jit(solution)/shard_map/ppermute | solution.py:278
  7.2 17.9 %collective-permute-start.3 = (bf16[64,4096]{1,0:T(8,128)(2,1)S(1)}, bf16[64,4096]{1,0:T(8,128)(2,1)S(1)}, u32[]{:S(2)}, u32[]{:S(2)}) collective-permute-start(bf16[64,4096]{1,0:T(8,128)(2,1)S(1)} %pair.1.refs_0_), channel_id=1, source_target_pairs={{0,4},{1,5},{2,6},{3,7},{4,8},{5,9},{6,10},{7,11},{8,12},{9,13},{1... | collective-permute-start | bytes 1572872 | tf_op jit(solution)/shard_map/ppermute | solution.py:275
  11.1 4.9 %copy-start = (bf16[128,640]{1,0:T(8,128)(2,1)S(1)}, bf16[128,640]{1,0:T(8,128)(2,1)}, u32[]{:S(2)}) copy-start(bf16[128,640]{1,0:T(8,128)(2,1)} %get-tuple-element.48) | copy-start | bytes 491524
  14.5 10.7 %collective-permute-start.5 = (bf16[128,1536]{1,0:T(8,128)(2,1)S(1)}, bf16[128,1536]{1,0:T(8,128)(2,1)S(1)}, u32[]{:S(2)}, u32[]{:S(2)}) collective-permute-start(bf16[128,1536]{1,0:T(8,128)(2,1)S(1)} %get-tuple-element.52), channel_id=1, source_target_pairs={{0,16},{1,17},{2,18},{3,19},{4,20},{5,21},{6,22},{7,23},{8,24},{9,... | collective-permute-start | bytes 1179656 | tf_op jit(solution)/shard_map/ppermute | solution.py:272
  16.1 11.2 %collective-permute-start.2 = (bf16[128,640]{1,0:T(8,128)(2,1)S(1)}, bf16[128,640]{1,0:T(8,128)(2,1)S(1)}, u32[]{:S(2)}, u32[]{:S(2)}) collective-permute-start(bf16[128,640]{1,0:T(8,128)(2,1)S(1)} %copy-done), channel_id=1, source_target_pairs={{1,5},{3,7},{5,9},{7,11},{9,13},{11,15},{17,21},{19,23},{21,25},{2... | collective-permute-start | bytes 491528 | tf_op jit(solution)/shard_map/ppermute | solution.py:284
  16.7 10.5 %collective-permute-start.1 = (bf16[128,640]{1,0:T(8,128)(2,1)S(1)}, bf16[128,640]{1,0:T(8,128)(2,1)S(1)}, u32[]{:S(2)}, u32[]{:S(2)}) collective-permute-start(bf16[128,640]{1,0:T(8,128)(2,1)S(1)} %copy-done), channel_id=1, source_target_pairs={{0,2},{1,3},{2,4},{3,5},{4,6},{5,7},{6,8},{7,9},{8,10},{9,11},{10,... | collective-permute-start | bytes 491528 | tf_op jit(solution)/shard_map/ppermute | solution.py:284
  25.2 13.4 %collective-permute-start.8 = (bf16[64,4096]{1,0:T(8,128)(2,1)S(1)}, bf16[64,4096]{1,0:T(8,128)(2,1)S(1)}, u32[]{:S(2)}, u32[]{:S(2)}) collective-permute-start(bf16[64,4096]{1,0:T(8,128)(2,1)S(1)} %collective-permute-done.3.refs_1_), channel_id=1, source_target_pairs={{0,2},{1,3},{2,0},{3,1},{4,6},{5,7},{6,4},{7,5},{8,10},{9,11},{10,... | collective-permute-start | bytes 1572872 | tf_op jit(solution)/shard_map/ppermute | solution.py:278
  25.7 14.0 %collective-permute-start.7 = (bf16[64,4096]{1,0:T(8,128)(2,1)S(1)}, bf16[64,4096]{1,0:T(8,128)(2,1)S(1)}, u32[]{:S(2)}, u32[]{:S(2)}) collective-permute-start(bf16[64,4096]{1,0:T(8,128)(2,1)S(1)} %collective-permute-done.3.refs_1_), channel_id=1, source_target_pairs={{0,4},{1,5},{2,6},{3,7},{4,8},{5,9},{6,10},{7,11},{8,12},{9,13},{1... | collective-permute-start | bytes 1572872 | tf_op jit(solution)/shard_map/ppermute | solution.py:275
  27.3 11.3 %collective-permute-start.6 = (bf16[384,640]{1,0:T(8,128)(2,1)S(1)}, bf16[384,640]{1,0:T(8,128)(2,1)S(1)}, u32[]{:S(2)}, u32[]{:S(2)}) collective-permute-start(bf16[384,640]{1,0:T(8,128)(2,1)S(1)} %pad_maximum_fusion), channel_id=1, source_target_pairs={{0,16},{1,17},{2,18},{3,19},{4,20},{5,21},{6,22},{7,23},{8,24},{9,... | collective-permute-start | bytes 1474568 | tf_op jit(solution)/shard_map/ppermute | solution.py:272
  28.9 1.7 %collective-permute-start.9 = (bf16[128,1536]{1,0:T(8,128)(2,1)S(1)}, bf16[128,1536]{1,0:T(8,128)(2,1)S(1)}, u32[]{:S(2)}, u32[]{:S(2)}) collective-permute-start(bf16[128,1536]{1,0:T(8,128)(2,1)S(1)} %get-tuple-element.57), channel_id=1, source_target_pairs={{0,1},{1,0},{2,3},{3,2},{4,5},{5,4},{6,7},{7,6},{8,9},{9,8},{10,11... | collective-permute-start | bytes 1179656 | tf_op jit(solution)/shard_map/ppermute | solution.py:272
  39.7 14.6 %collective-permute-start.11 = (bf16[64,4096]{1,0:T(8,128)(2,1)S(1)}, bf16[64,4096]{1,0:T(8,128)(2,1)S(1)}, u32[]{:S(2)}, u32[]{:S(2)}) collective-permute-start(bf16[64,4096]{1,0:T(8,128)(2,1)S(1)} %collective-permute-done.7.refs_2_), channel_id=1, source_target_pairs={{0,4},{1,5},{2,6},{3,7},{4,8},{5,9},{6,10},{7,11},{8,12},{9,13},{1... | collective-permute-start | bytes 1572872 | tf_op jit(solution)/shard_map/ppermute | solution.py:275
  41.3 14.4 %collective-permute-start.10 = (bf16[768,640]{1,0:T(8,128)(2,1)S(1)}, bf16[768,640]{1,0:T(8,128)(2,1)S(1)}, u32[]{:S(2)}, u32[]{:S(2)}) collective-permute-start(bf16[768,640]{1,0:T(8,128)(2,1)S(1)} %constant_dynamic-update-slice_fusion.own), channel_id=1, source_target_pairs={{0,1},{1,0},{2,3},{3,2},{4,5},{5,4},{6,7},{7,6},{8,9},{9,8},{10,11... | collective-permute-start | bytes 2949128 | tf_op jit(solution)/shard_map/ppermute | solution.py:272
  41.4 14.3 %collective-permute-start.12 = (bf16[64,4096]{1,0:T(8,128)(2,1)S(1)}, bf16[64,4096]{1,0:T(8,128)(2,1)S(1)}, u32[]{:S(2)}, u32[]{:S(2)}) collective-permute-start(bf16[64,4096]{1,0:T(8,128)(2,1)S(1)} %collective-permute-done.7.refs_2_), channel_id=1, source_target_pairs={{0,2},{1,3},{2,0},{3,1},{4,6},{5,7},{6,4},{7,5},{8,10},{9,11},{10,... | collective-permute-start | bytes 1572872 | tf_op jit(solution)/shard_map/ppermute | solution.py:278
  41.9 12.4 %collective-permute-start.13 = (bf16[128,1536]{1,0:T(8,128)(2,1)S(1)}, bf16[128,1536]{1,0:T(8,128)(2,1)S(1)}, u32[]{:S(2)}, u32[]{:S(2)}) collective-permute-start(bf16[128,1536]{1,0:T(8,128)(2,1)S(1)} %get-tuple-element.61), channel_id=1, source_target_pairs={{0,17},{1,16},{2,19},{3,18},{4,21},{5,20},{6,23},{7,22},{8,25},{9,... | collective-permute-start | bytes 1179656 | tf_op jit(solution)/shard_map/ppermute | solution.py:272
  55.7 9.2 %collective-permute-start.14 = (bf16[64,2048]{1,0:T(8,128)(2,1)S(1)}, bf16[64,2048]{1,0:T(8,128)(2,1)S(1)}, u32[]{:S(2)}, u32[]{:S(2)}) collective-permute-start(bf16[64,2048]{1,0:T(8,128)(2,1)S(1)} %get-tuple-element.62), channel_id=1, source_target_pairs={{0,2},{1,3},{2,0},{3,1},{4,6},{5,7},{6,4},{7,5},{8,10},{9,11},{10,... | collective-permute-start | bytes 786440 | tf_op jit(solution)/shard_map/ppermute | solution.py:278
  56.2 20.5 %collective-permute-start.17 = (bf16[128,1536]{1,0:T(8,128)(2,1)S(1)}, bf16[128,1536]{1,0:T(8,128)(2,1)S(1)}, u32[]{:S(2)}, u32[]{:S(2)}) collective-permute-start(bf16[128,1536]{1,0:T(8,128)(2,1)S(1)} %get-tuple-element.70), channel_id=1, source_target_pairs={{0,16},{1,17},{2,18},{3,19},{4,20},{5,21},{6,22},{7,23},{8,24},{9,... | collective-permute-start | bytes 1179656 | tf_op jit(solution)/shard_map/ppermute | solution.py:272
  57.7 20.1 %collective-permute-start.15 = (bf16[64,2048]{1,0:T(8,128)(2,1)S(1)}, bf16[64,2048]{1,0:T(8,128)(2,1)S(1)}, u32[]{:S(2)}, u32[]{:S(2)}) collective-permute-start(bf16[64,2048]{1,0:T(8,128)(2,1)S(1)} %get-tuple-element.65), channel_id=1, source_target_pairs={{0,2},{1,3},{2,0},{3,1},{4,6},{5,7},{6,4},{7,5},{8,10},{9,11},{10,... | collective-permute-start | bytes 786440 | tf_op jit(solution)/shard_map/ppermute | solution.py:278
  58.8 19.0 %collective-permute-start.16 = (bf16[128,1536]{1,0:T(8,128)(2,1)S(1)}, bf16[128,1536]{1,0:T(8,128)(2,1)S(1)}, u32[]{:S(2)}, u32[]{:S(2)}) collective-permute-start(bf16[128,1536]{1,0:T(8,128)(2,1)S(1)} %get-tuple-element.68), channel_id=1, source_target_pairs={{0,1},{1,0},{2,3},{3,2},{4,5},{5,4},{6,7},{7,6},{8,9},{9,8},{10,11... | collective-permute-start | bytes 1179656 | tf_op jit(solution)/shard_map/ppermute | solution.py:272
  58.8 19.0 %collective-permute-start.18 = (bf16[128,1536]{1,0:T(8,128)(2,1)S(1)}, bf16[128,1536]{1,0:T(8,128)(2,1)S(1)}, u32[]{:S(2)}, u32[]{:S(2)}) collective-permute-start(bf16[128,1536]{1,0:T(8,128)(2,1)S(1)} %get-tuple-element.72), channel_id=1, source_target_pairs={{0,17},{1,16},{2,19},{3,18},{4,21},{5,20},{6,23},{7,22},{8,25},{9,... | collective-permute-start | bytes 1179656 | tf_op jit(solution)/shard_map/ppermute | solution.py:272
  76.6 7.4 %collective-permute-start.19 = (bf16[128,1024]{1,0:T(8,128)(2,1)S(1)}, bf16[128,1024]{1,0:T(8,128)(2,1)S(1)}, u32[]{:S(2)}, u32[]{:S(2)}) collective-permute-start(bf16[128,1024]{1,0:T(8,128)(2,1)S(1)} %get-tuple-element.75), channel_id=1, source_target_pairs={{0,1},{1,0},{2,3},{3,2},{4,5},{5,4},{6,7},{7,6},{8,9},{9,8},{10,11... | collective-permute-start | bytes 786440 | tf_op jit(solution)/shard_map/ppermute | solution.py:272
  76.7 8.7 %collective-permute-start.20 = (bf16[128,1024]{1,0:T(8,128)(2,1)S(1)}, bf16[128,1024]{1,0:T(8,128)(2,1)S(1)}, u32[]{:S(2)}, u32[]{:S(2)}) collective-permute-start(bf16[128,1024]{1,0:T(8,128)(2,1)S(1)} %get-tuple-element.76), channel_id=1, source_target_pairs={{0,16},{1,17},{2,18},{3,19},{4,20},{5,21},{6,22},{7,23},{8,24},{9,... | collective-permute-start | bytes 786440 | tf_op jit(solution)/shard_map/ppermute | solution.py:272
  91.6 5.1 %collective-permute-start.24 = (bf16[128,512]{1,0:T(8,128)(2,1)S(1)}, bf16[128,512]{1,0:T(8,128)(2,1)S(1)}, u32[]{:S(2)}, u32[]{:S(2)}) collective-permute-start(bf16[128,512]{1,0:T(8,128)(2,1)S(1)} %get-tuple-element.82), channel_id=1, source_target_pairs={{0,16},{1,17},{2,18},{3,19},{4,20},{5,21},{6,22},{7,23},{8,24},{9,... | collective-permute-start | bytes 393224 | tf_op jit(solution)/shard_map/ppermute | solution.py:272
  96.7 22.7 %all-to-all-start = ((bf16[16,16,576]{2,1,0:T(8,128)(2,1)}), bf16[16,16,576]{2,1,0:T(8,128)(2,1)S(1)}, u32[]{:S(2)}, u32[]{:S(2)}) async-start(bf16[16,16,576]{2,1,0:T(8,128)(2,1)} %bitcast.5), calls=%async_computation | async-start | bytes 655360 | tf_op jit(solution)/shard_map/all_to_all | solution.py:442
  101.3 8.2 %collective-permute-start.25 = (bf16[128,1024]{1,0:T(8,128)(2,1)S(1)}, bf16[128,1024]{1,0:T(8,128)(2,1)S(1)}, u32[]{:S(2)}, u32[]{:S(2)}) collective-permute-start(bf16[128,1024]{1,0:T(8,128)(2,1)S(1)} %get-tuple-element.83), channel_id=1, source_target_pairs={{0,17},{1,16},{2,19},{3,18},{4,21},{5,20},{6,23},{7,22},{8,25},{9,... | collective-permute-start | bytes 786440 | tf_op jit(solution)/shard_map/ppermute | solution.py:272
  102.8 8.5 %collective-permute-start.21 = (bf16[128,512]{1,0:T(8,128)(2,1)S(1)}, bf16[128,512]{1,0:T(8,128)(2,1)S(1)}, u32[]{:S(2)}, u32[]{:S(2)}) collective-permute-start(bf16[128,512]{1,0:T(8,128)(2,1)S(1)} %get-tuple-element.79), channel_id=1, source_target_pairs={{0,1},{1,0},{2,3},{3,2},{4,5},{5,4},{6,7},{7,6},{8,9},{9,8},{10,11... | collective-permute-start | bytes 393224 | tf_op jit(solution)/shard_map/ppermute | solution.py:272
  103.0 10.3 %collective-permute-start.23 = (bf16[128,512]{1,0:T(8,128)(2,1)S(1)}, bf16[128,512]{1,0:T(8,128)(2,1)S(1)}, u32[]{:S(2)}, u32[]{:S(2)}) collective-permute-start(bf16[128,512]{1,0:T(8,128)(2,1)S(1)} %get-tuple-element.81), channel_id=1, source_target_pairs={{0,16},{1,17},{2,18},{3,19},{4,20},{5,21},{6,22},{7,23},{8,24},{9,... | collective-permute-start | bytes 393224 | tf_op jit(solution)/shard_map/ppermute | solution.py:272
  103.5 11.6 %collective-permute-start.26 = (bf16[128,512]{1,0:T(8,128)(2,1)S(1)}, bf16[128,512]{1,0:T(8,128)(2,1)S(1)}, u32[]{:S(2)}, u32[]{:S(2)}) collective-permute-start(bf16[128,512]{1,0:T(8,128)(2,1)S(1)} %get-tuple-element.84), channel_id=1, source_target_pairs={{0,17},{1,16},{2,19},{3,18},{4,21},{5,20},{6,23},{7,22},{8,25},{9,... | collective-permute-start | bytes 393224 | tf_op jit(solution)/shard_map/ppermute | solution.py:272
  104.7 10.5 %collective-permute-start.22 = (bf16[128,512]{1,0:T(8,128)(2,1)S(1)}, bf16[128,512]{1,0:T(8,128)(2,1)S(1)}, u32[]{:S(2)}, u32[]{:S(2)}) collective-permute-start(bf16[128,512]{1,0:T(8,128)(2,1)S(1)} %get-tuple-element.80), channel_id=1, source_target_pairs={{0,1},{1,0},{2,3},{3,2},{4,5},{5,4},{6,7},{7,6},{8,9},{9,8},{10,11... | collective-permute-start | bytes 393224 | tf_op jit(solution)/shard_map/ppermute | solution.py:272
  109.5 8.4 %collective-permute-start.27 = (bf16[128,512]{1,0:T(8,128)(2,1)S(1)}, bf16[128,512]{1,0:T(8,128)(2,1)S(1)}, u32[]{:S(2)}, u32[]{:S(2)}) collective-permute-start(bf16[128,512]{1,0:T(8,128)(2,1)S(1)} %get-tuple-element.85), channel_id=1, source_target_pairs={{0,17},{1,16},{2,19},{3,18},{4,21},{5,20},{6,23},{7,22},{8,25},{9,... | collective-permute-start | bytes 393224 | tf_op jit(solution)/shard_map/ppermute | solution.py:272

commit v8 on v7

--- a/solution.py
+++ b/solution.py
@@ -22,7 +22,7 @@
     ("z", "y0", "b~", "f~", "q02"),
     ("z", "y1", "k", "q01"),
     ("z", "y2", "p", "q03", "q12~"),
-    ("y3", "q13~", "q11"),
+    ("y3", "w", "q13~", "q11"),
 )
 CHUNKS = len(CHUNK_HEADS)
 FIRST_HEAD = tuple(sum(CHUNK_HEADS[:j]) for j in range(CHUNKS))
@@ -122,57 +122,58 @@
         copy.wait()
 
 
-def attend_kernel(outer, info, own, other, *refs):
+def keys_kernel(info, own, other, latent, rope_even, rope_odd, bias):
+    tok = own.shape[0] // 6
+    mine = info[0]
+    partner = mine ^ 1
+    has_last = (mine & 1) == 1
+    starts = [mine, partner, mine - 2, partner - 2, (mine >> 1) * 2 - 3]
+    blank = jnp.zeros((tok, ROPE), jnp.bfloat16)
+    lane = lax.broadcasted_iota(jnp.int32, (tok, tok), 1)
+    row = lax.broadcasted_iota(jnp.int32, (tok, tok), 0)
+    for g in range(2):
+        mine_of, other_of = [
+            [ref[(3 * g + n) * tok : (3 * g + n + 1) * tok] for n in range(3)]
+            for ref in (own, other)
+        ]
+        pieces = [
+            mine_of[0],
+            other_of[0],
+            mine_of[1],
+            other_of[1],
+            jnp.where(has_last, mine_of[2], other_of[2]),
+        ]
+        for b, piece in enumerate(pieces):
+            here = slice(b * tok, (b + 1) * tok)
+            latent[g, here] = piece[:, :LAT]
+            turned = piece[:, LAT : LAT + ROPE]
+            rope_even[g, here] = jnp.concatenate([turned, blank], axis=1)
+            rope_odd[g, here] = jnp.concatenate([blank, turned], axis=1)
+        for half in range(2):
+            meta = pieces[half][:, LAT:].astype(jnp.float32)
+            offset = (meta[:, ROPE : ROPE + 1] * 256.0 + meta[:, ROPE + 1 : ROPE + 2]).astype(
+                jnp.int32
+            )
+            spots = starts[half] * tok + row
+            lowest = jnp.maximum(spots - offset, (starts[half] - REACH) * tok)
+            for b in range(REACH + 2):
+                keys = starts[b] * tok + lane
+                allowed = (keys >= lowest) & (keys <= spots)
+                bias[g, half * tok : (half + 1) * tok, b * tok : (b + 1) * tok] = jnp.where(
+                    allowed, 0.0, -1e30
+                )
+
+
+def attend_kernel(outer, info, latent, rope_even, rope_odd, bias, *refs):
     pieces_count = 2 * outer if outer else 1
     pieces_of_weight, refs = refs[:pieces_count], refs[pieces_count:]
     nope = refs[0:QUAD]
     rope = refs[QUAD : 2 * QUAD]
     outs = refs[2 * QUAD : 3 * QUAD]
-    latent, rope_even, rope_odd, bias, held = refs[3 * QUAD :]
+    held = refs[3 * QUAD]
     tok = nope[0].shape[0]
-    blocks = REACH + 2
     mine = info[0]
-    partner = mine ^ 1
     scale = (NOPE + ROPE) ** (-0.5) * math.log2(math.e)
-
-    @pl.when(pl.program_id(0) == 0)
-    def _():
-        has_last = (mine & 1) == 1
-        starts = [mine, partner, mine - 2, partner - 2, (mine >> 1) * 2 - 3]
-        blank = jnp.zeros((tok, ROPE), jnp.bfloat16)
-        lane = lax.broadcasted_iota(jnp.int32, (tok, tok), 1)
-        row = lax.broadcasted_iota(jnp.int32, (tok, tok), 0)
-        for g in range(2):
-            mine_of, other_of = [
-                [ref[(3 * g + n) * tok : (3 * g + n + 1) * tok] for n in range(3)]
-                for ref in (own, other)
-            ]
-            pieces = [
-                mine_of[0],
-                other_of[0],
-                mine_of[1],
-                other_of[1],
-                jnp.where(has_last, mine_of[2], other_of[2]),
-            ]
-            for b, piece in enumerate(pieces):
-                here = slice(b * tok, (b + 1) * tok)
-                latent[g, here] = piece[:, :LAT]
-                turned = piece[:, LAT : LAT + ROPE]
-                rope_even[g, here] = jnp.concatenate([turned, blank], axis=1)
-                rope_odd[g, here] = jnp.concatenate([blank, turned], axis=1)
-            for half in range(2):
-                meta = pieces[half][:, LAT:].astype(jnp.float32)
-                offset = (meta[:, ROPE : ROPE + 1] * 256.0 + meta[:, ROPE + 1 : ROPE + 2]).astype(
-                    jnp.int32
-                )
-                spots = starts[half] * tok + row
-                lowest = jnp.maximum(spots - offset, (starts[half] - REACH) * tok)
-                for b in range(blocks):
-                    keys = starts[b] * tok + lane
-                    allowed = (keys >= lowest) & (keys <= spots)
-                    bias[g, half * tok : (half + 1) * tok, b * tok : (b + 1) * tok] = jnp.where(
-                        allowed, 0.0, -1e30
-                    )
 
     if outer:
         weight = held
@@ -186,29 +187,53 @@
     else:
         weight = pieces_of_weight[0]
 
-    for g in range(2):
-        expanded = jnp.dot(latent[g], weight[...], preferred_element_type=jnp.float32).astype(
-            jnp.bfloat16
+    def expand(g):
+        wide = jnp.dot(latent[g], weight[...], preferred_element_type=jnp.float32)
+        return wide.astype(jnp.bfloat16)
+
+    def score(g, b, expanded):
+        at = slice(b * 128, (b + 1) * 128)
+        key_rope = (rope_even, rope_odd)[b][g]
+        key = jnp.concatenate([expanded[:, b * 256 : b * 256 + 128], key_rope], axis=1)
+        query = jnp.concatenate(
+            [
+                jnp.concatenate([nope[2 * g][:, at], rope[2 * g][...]], axis=1),
+                jnp.concatenate([nope[2 * g + 1][:, at], rope[2 * g + 1][...]], axis=1),
+            ],
+            axis=0,
         )
-        query_rope = jnp.concatenate([rope[2 * g][...], rope[2 * g + 1][...]], axis=0)
-        for b in range(2):
-            at = slice(b * 128, (b + 1) * 128)
-            key_rope = (rope_even, rope_odd)[b][g]
-            key = jnp.concatenate([expanded[:, b * 256 : b * 256 + 128], key_rope], axis=1)
-            value = expanded[:, b * 256 + 128 : b * 256 + 256]
-            query = jnp.concatenate([nope[2 * g][:, at], nope[2 * g + 1][:, at]], axis=0)
-            query = jnp.concatenate([query, query_rope], axis=1)
-            scores = lax.dot_general(
-                query, key, (((1,), (1,)), ((), ())), preferred_element_type=jnp.float32
-            )
-            scores = scores * scale + bias[g]
-            largest = jnp.max(scores, axis=1, keepdims=True)
-            expo = jnp.exp2(scores - largest)
-            total = jnp.sum(expo, axis=1, keepdims=True)
-            mixed = jnp.dot(expo.astype(jnp.bfloat16), value, preferred_element_type=jnp.float32)
-            mixed = (mixed / total).astype(jnp.bfloat16)
-            outs[2 * g][:, at] = mixed[:tok]
-            outs[2 * g + 1][:, at] = mixed[tok:]
+        return lax.dot_general(
+            query, key, (((1,), (1,)), ((), ())), preferred_element_type=jnp.float32
+        )
+
+    def weigh(g, scores):
+        scores = scores * scale + bias[g]
+        largest = jnp.max(scores, axis=1, keepdims=True)
+        expo = jnp.exp2(scores - largest)
+        return expo.astype(jnp.bfloat16), jnp.sum(expo, axis=1, keepdims=True)
+
+    def mix(g, b, expanded, weights, total):
+        at = slice(b * 128, (b + 1) * 128)
+        value = expanded[:, b * 256 + 128 : b * 256 + 256]
+        mixed = jnp.dot(weights, value, preferred_element_type=jnp.float32)
+        mixed = (mixed / total).astype(jnp.bfloat16)
+        outs[2 * g][:, at] = mixed[:tok]
+        outs[2 * g + 1][:, at] = mixed[tok:]
+
+    first = expand(0)
+    scores = score(0, 0, first)
+    second = expand(1)
+    weighed = weigh(0, scores)
+    scores = score(0, 1, first)
+    mix(0, 0, first, *weighed)
+    weighed = weigh(0, scores)
+    scores = score(1, 0, second)
+    mix(0, 1, first, *weighed)
+    weighed = weigh(1, scores)
+    scores = score(1, 1, second)
+    mix(1, 0, second, *weighed)
+    weighed = weigh(1, scores)
+    mix(1, 1, second, *weighed)
 
 
 def gather_kernel(info, *refs):
@@ -356,6 +381,7 @@
     phases = Phases()
     line = [pair_rows] if outer else []
     side = []
+    half = width // CHUNKS
     halves = []
     moved = [[queries[j]] + [None] * (QUAD - 1) for j in range(CHUNKS)]
     parts = {"r": tie(rows, pair_rows if outer else got)}
@@ -371,11 +397,9 @@
             if step < outer - 1:
                 side.append(phases.send(late, inner_swap, line[step]))
             else:
-                half = line[step].shape[1] // CHUNKS
-                halves = [
-                    phases.send(late, inner_swap, line[step][:, j * half : (j + 1) * half])
-                    for j in range(CHUNKS)
-                ]
+                halves.append(phases.send(late, inner_swap, line[step][:, :half]))
+        elif kind == "w" and outer:
+            halves.append(phases.send(late, around, side[-1][:, half:], 4))
         elif kind == "b":
             parts["b"] = phases.send(late, from_behind, parts["r"], 2, False)
         elif kind == "f":
@@ -396,6 +420,21 @@
         return [(piece, FIRST_HEAD[j] // 2) for piece in line + side] + [(halves[j], 0)]
 
     window = (REACH + 2) * tok
+    resident = pl.BlockSpec(memory_space=VMEM)
+    keys = pl.pallas_call(
+        keys_kernel,
+        out_shape=(
+            shape((2, window, LAT)),
+            shape((2, window, 128)),
+            shape((2, window, 128)),
+            shape((2, 2 * tok, window), jnp.float32),
+        ),
+        in_specs=[smem, resident, resident],
+        out_specs=[resident] * 4,
+        compiler_params=params,
+        cost_estimate=pl.CostEstimate(flops=0, bytes_accessed=8 << 20, transcendentals=0),
+        name="keys",
+    )(mine_info, own_rows, other_rows)
 
     def attend(j, first, steps):
         heads = 2 * steps
@@ -405,7 +444,7 @@
             functools.partial(attend_kernel, outer),
             grid=(steps,),
             out_shape=[shape((tok, heads * VDIM))] * QUAD,
-            in_specs=[smem, block(6 * tok, EXT), block(6 * tok, EXT)]
+            in_specs=[smem] + [resident] * 4
             + [
                 pl.BlockSpec((piece.shape[0], 512), lambda i, begin=begin: (0, begin + first + i))
                 for piece, begin in weights_for(j)
@@ -413,13 +452,7 @@
             + [pl.BlockSpec((tok, 256), lambda i: (0, first + i))] * QUAD
             + [pl.BlockSpec((tok, 128), lambda i: (0, CHUNK_HEADS[j] + first + i))] * QUAD,
             out_specs=[pl.BlockSpec((tok, 256), lambda i: (0, i))] * QUAD,
-            scratch_shapes=[
-                VMEM((2, window, LAT), jnp.bfloat16),
-                VMEM((2, window, 128), jnp.bfloat16),
-                VMEM((2, window, 128), jnp.bfloat16),
-                VMEM((2, 2 * tok, window), jnp.float32),
-                VMEM((LAT, 512), jnp.bfloat16),
-            ],
+            scratch_shapes=[VMEM((LAT, 512), jnp.bfloat16)],
             compiler_params=params,
             cost_estimate=pl.CostEstimate(
                 flops=flops,
@@ -427,20 +460,23 @@
                 transcendentals=heads * 4 * tok * window,
             ),
             name="attend",
-        )(mine_info, own_rows, other_rows, *pieces_of_weight, *moved[j], *moved[j])
+        )(mine_info, *keys, *pieces_of_weight, *moved[j], *moved[j])
 
     results = []
     for call in CALLS:
-        if len(results) > 1:
-            mine_info = tie(mine_info, *results[-2][1:3])
+        sent = [piece for one in results for piece in one[1:]]
+        last = len(results) + 1 == len(CALLS)
+        mine_info = tie(mine_info, *(results[0][2:3] if last else []))
         pieces = attend(*call)
         mine_info = tie(mine_info, pieces[0])
+        before = sent[:-1] if last else []
         results.append(
-            [pieces[0]] + [quad_swap(pieces[r], r) for r in range(1, QUAD)]
+            [pieces[0]] + [quad_swap(tie(pieces[r], *before), r) for r in range(1, QUAD)]
         )
     pieces = [one[r] for r in range(QUAD) for one in results]
+    sent = [piece for one in results for piece in one[1:]]
     arrived = lax.all_to_all(
-        tie(outgoing, results[-1][2]).reshape(size, slot_count, ROW),
+        tie(outgoing, *sent).reshape(size, slot_count, ROW),
         "ctx",
         split_axis=0,
         concat_axis=0,

time: 121 us -> 119 us (0.983)
  waiting for transfers between devices: 51.9 us -> 60.2 us
  Pallas kernels: 32 us -> 26.6 us
  starting transfers between devices: 33.4 us -> 29.4 us
    all_to_all x1, waiting for transfers between devices: 0.01 us -> 9.64 us  [body(): lax.all_to_all(tie(outgoing, *sent).reshape(size, slot_count, ROW), 'ctx'...]
    ppermute x18, waiting for transfers between devices: 33.3 us -> 23.7 us  [quad_swap(): return lax.ppermute(array, ('groups', 'ctx'), pairs)]
    pallas_call x3, Pallas kernels: 24 us -> 17.9 us  [attend(): pl.pallas_call(functools.partial(attend_kernel, outer), grid=(steps,), ou...]
    ppermute x3 -> x4, waiting for transfers between devices: 12.2 us -> 17.7 us  [around(): lax.ppermute(array, 'ctx', [(i, (i + by) % size) for i in range(size)])]
    ppermute x2, waiting for transfers between devices: 0.01 us -> 3.71 us  [from_behind(): return lax.ppermute(array, 'ctx', pairs)]
    ppermute x18, starting transfers between devices: 15.5 us -> 12.4 us  [quad_swap(): return lax.ppermute(array, ('groups', 'ctx'), pairs)]
    ppermute x5 -> x4, starting transfers between devices: 5.53 us -> 7.03 us  [inner_swap(): return lax.ppermute(array, 'ctx', [(i, i ^ 2) for i in range(size)])]
    ppermute x3 -> x4, starting transfers between devices: 4.72 us -> 3.37 us  [around(): lax.ppermute(array, 'ctx', [(i, (i + by) % size) for i in range(size)])]
where the time goes in v8:
time: 119 us
  waiting for transfers between devices  60.2 us (51%)
  starting transfers between devices  29.4 us (25%)
  Pallas kernels  26.6 us (22%)
  local copies, waits for them, and re-layouts  2.01 us (2%)
    ppermute x18, waiting for transfers between devices, quad_swap(): return lax.ppermute(array, ('groups', 'ctx'), pairs)  23.7 us
    pallas_call x3, Pallas kernels, attend(): pl.pallas_call(functools.partial(attend_kernel, outer), grid=(steps,), ou...  17.9 us
    ppermute x4, waiting for transfers between devices, around(): lax.ppermute(array, 'ctx', [(i, (i + by) % size) for i in range(size)])  17.7 us
    ppermute x18, starting transfers between devices, quad_swap(): return lax.ppermute(array, ('groups', 'ctx'), pairs)  12.4 us
    all_to_all x1, waiting for transfers between devices, body(): lax.all_to_all(tie(outgoing, *sent).reshape(size, slot_count, ROW), 'ctx'...  9.64 us
    ppermute x4, starting transfers between devices, inner_swap(): return lax.ppermute(array, 'ctx', [(i, i ^ 2) for i in range(size)])  7.03 us
    ppermute x4, waiting for transfers between devices, inner_swap(): return lax.ppermute(array, 'ctx', [(i, i ^ 2) for i in range(size)])  5.46 us
    ppermute x2, waiting for transfers between devices, from_behind(): return lax.ppermute(array, 'ctx', pairs)  3.71 us
  transfers between devices with their start and end apart: 29, of which 14 were waited for; matrix products, arithmetic and copies ran while one was open for 0% of the time, Pallas kernels for 21%

profile of v8, /device:TPU:0, one launch (start us, length us, event | category | flops | bytes accessed | tf_op | source)
XLA Modules:
  0.0 119.2 jit_solution(15966297568535784328)
XLA Ops:
  0.6 1.0 constant_dynamic-slice_fusion
  1.6 0.5 collective-permute-start
  2.1 1.2 collective-permute-done.got
  3.3 1.0 pair.1.refs_0_
  4.3 3.0 %collective-permute-start.4 = (bf16[64,4096]{1,0:T(8,128)(2,1)S(1)}, bf16[64,4096]{1,0:T(8,128)(2,1)S(1)}, u32[]{:S(2)}, u32[]{:S(2)}) collective-permute-start(bf16[64,4096]{1,0:T(8,128)(2,1)S(1)} %pair.1.refs_0_), channel_id=1, source_target_pairs={{0,2},{1,3},{2,0},{3,1},{4,6},{5,7},{6,4},{7,5},{8,10},{9,11},{10,... | collective-permute-start | bytes 1572872 | tf_op jit(solution)/shard_map/ppermute | solution.py:303
  7.2 1.6 %collective-permute-start.3 = (bf16[64,4096]{1,0:T(8,128)(2,1)S(1)}, bf16[64,4096]{1,0:T(8,128)(2,1)S(1)}, u32[]{:S(2)}, u32[]{:S(2)}) collective-permute-start(bf16[64,4096]{1,0:T(8,128)(2,1)S(1)} %pair.1.refs_0_), channel_id=1, source_target_pairs={{0,4},{1,5},{2,6},{3,7},{4,8},{5,9},{6,10},{7,11},{8,12},{9,13},{1... | collective-permute-start | bytes 1572872 | tf_op jit(solution)/shard_map/ppermute | solution.py:300
  8.8 2.3 %rows.1 = (bf16[128,640]{1,0:T(8,128)(2,1)}, f32[128,128]{1,0:T(8,128)}, f32[128,128]{1,0:T(8,128)}, bf16[256,576]{1,0:T(8,128)(2,1)}) custom-call(s32[1]{0:T(128)} %bitcast.1.info, s32[8]{0:T(128)} %lengths, bf16[576,128]{1,0:T(8,128)(2,1)} %bitcast.8, f32[1,512]{1,0:T(1,128)} %bitcast.9, s32[1,128]{1,0:T(1,128)} %bitcast.10, f32[1,128]{1,0:T(1,128)} %constant.30.clone.freq), custom_call_target="tpu_custom_call" | custom-call | tf_op jit(solution)/shard_map/rows/pallas_call | solution.py:344
  11.1 3.4 %queries.1 = (bf16[128,1536]{1,0:T(8,128)(2,1)S(1)}, bf16[128,1536]{1,0:T(8,128)(2,1)S(1)}, bf16[128,1536]{1,0:T(8,128)(2,1)S(1)}, bf16[128,1536]{1,0:T(8,128)(2...) custom-call(s32[1]{0:T(128)} %bitcast.info, ...), custom_call_target="tpu_custom_call" | custom-call | bytes 6291456 | tf_op jit(solution)/shard_map/queries/pallas_call | solution.py:368
  14.5 1.6 %collective-permute-start.5 = (bf16[128,1536]{1,0:T(8,128)(2,1)S(1)}, bf16[128,1536]{1,0:T(8,128)(2,1)S(1)}, u32[]{:S(2)}, u32[]{:S(2)}) collective-permute-start(bf16[128,1536]{1,0:T(8,128)(2,1)S(1)} %get-tuple-element.59), channel_id=1, source_target_pairs={{0,16},{1,17},{2,18},{3,19},{4,20},{5,21},{6,22},{7,23},{8,24},{9,... | collective-permute-start | bytes 1179656 | tf_op jit(solution)/shard_map/ppermute | solution.py:297
  16.1 0.7 collective-permute-start.2
  16.7 2.4 %collective-permute-start.1 = (bf16[128,640]{1,0:T(8,128)(2,1)S(1)}, bf16[128,640]{1,0:T(8,128)(2,1)S(1)}, u32[]{:S(2)}, u32[]{:S(2)}) collective-permute-start(bf16[128,640]{1,0:T(8,128)(2,1)S(1)} %copy-done), channel_id=1, source_target_pairs={{0,2},{1,3},{2,4},{3,5},{4,6},{5,7},{6,8},{7,9},{8,10},{9,11},{10,... | collective-permute-start | bytes 491528 | tf_op jit(solution)/shard_map/ppermute | solution.py:309
  19.2 0.0 collective-permute-done.2
  19.2 3.7 %collective-permute-done.1 = bf16[128,640]{1,0:T(8,128)(2,1)S(1)} collective-permute-done((bf16[128,640]{1,0:T(8,128)(2,1)S(1)}, bf16[128,640]{1,0:T(8,128)(2,1)S(1)}, u32[]{:S(2)}, u32[]{:S(2)}) %collective-permute-start.1) | collective-permute-done | bytes 163872 | tf_op jit(solution)/shard_map/ppermute | solution.py:309
  22.9 2.2 %collective-permute-done.5.refs_10_.refs_14_ = bf16[128,1536]{1,0:T(8,128)(2,1)S(1)} collective-permute-done((bf16[128,1536]{1,0:T(8,128)(2,1)S(1)}, bf16[128,1536]{1,0:T(8,128)(2,1)S(1)}, u32[]{:S(2)}, u32[]{:S(2)}) %collective-permute-start.5) | collective-permute-done | bytes 393248 | tf_op jit(solution)/shard_map/ppermute | solution.py:297
  25.2 0.0 collective-permute-done.4.refs_4_
  25.2 0.0 collective-permute-done.3.refs_1_
  25.2 1.5 %collective-permute-start.6 = (bf16[384,640]{1,0:T(8,128)(2,1)S(1)}, bf16[384,640]{1,0:T(8,128)(2,1)S(1)}, u32[]{:S(2)}, u32[]{:S(2)}) collective-permute-start(bf16[384,640]{1,0:T(8,128)(2,1)S(1)} %pad_maximum_fusion), channel_id=1, source_target_pairs={{0,16},{1,17},{2,18},{3,19},{4,20},{5,21},{6,22},{7,23},{8,24},{9,... | collective-permute-start | bytes 1474568 | tf_op jit(solution)/shard_map/ppermute | solution.py:297
  26.7 0.5 collective-permute-start.8
  27.2 1.7 %collective-permute-start.7 = (bf16[64,4096]{1,0:T(8,128)(2,1)S(1)}, bf16[64,4096]{1,0:T(8,128)(2,1)S(1)}, u32[]{:S(2)}, u32[]{:S(2)}) collective-permute-start(bf16[64,4096]{1,0:T(8,128)(2,1)S(1)} %collective-permute-done.3.refs_1_), channel_id=1, source_target_pairs={{0,4},{1,5},{2,6},{3,7},{4,8},{5,9},{6,10},{7,11},{8,12},{9,13},{1... | collective-permute-start | bytes 1572872 | tf_op jit(solution)/shard_map/ppermute | solution.py:300
  28.9 0.0 collective-permute-start.9
  29.0 8.1 %collective-permute-done.6 = bf16[384,640]{1,0:T(8,128)(2,1)S(1)} collective-permute-done((bf16[384,640]{1,0:T(8,128)(2,1)S(1)}, bf16[384,640]{1,0:T(8,128)(2,1)S(1)}, u32[]{:S(2)}, u32[]{:S(2)}) %collective-permute-start.6) | collective-permute-done | bytes 491552 | tf_op jit(solution)/shard_map/ppermute | solution.py:297
  37.1 0.1 constant_dynamic-update-slice_fusion.own
  37.2 0.0 collective-permute-done.9.refs_9_.refs_13_
  37.2 2.2 %collective-permute-done.8.refs_5_ = bf16[64,4096]{1,0:T(8,128)(2,1)S(1)} collective-permute-done((bf16[64,4096]{1,0:T(8,128)(2,1)S(1)}, bf16[64,4096]{1,0:T(8,128)(2,1)S(1)}, u32[]{:S(2)}, u32[]{:S(2)}) %collective-permute-start.8) | collective-permute-done | bytes 524320 | tf_op jit(solution)/shard_map/ppermute | solution.py:303
  39.3 3.7 %collective-permute-done.7.refs_2_ = bf16[64,4096]{1,0:T(8,128)(2,1)S(1)} collective-permute-done((bf16[64,4096]{1,0:T(8,128)(2,1)S(1)}, bf16[64,4096]{1,0:T(8,128)(2,1)S(1)}, u32[]{:S(2)}, u32[]{:S(2)}) %collective-permute-start.7) | collective-permute-done | bytes 524320 | tf_op jit(solution)/shard_map/ppermute | solution.py:300
  43.0 0.0 collective-permute-start.10
  43.0 0.0 collective-permute-start.11
  43.0 1.7 %collective-permute-start.12 = (bf16[64,4096]{1,0:T(8,128)(2,1)S(1)}, bf16[64,4096]{1,0:T(8,128)(2,1)S(1)}, u32[]{:S(2)}, u32[]{:S(2)}) collective-permute-start(bf16[64,4096]{1,0:T(8,128)(2,1)S(1)} %collective-permute-done.7.refs_2_), channel_id=1, source_target_pairs={{0,2},{1,3},{2,0},{3,1},{4,6},{5,7},{6,4},{7,5},{8,10},{9,11},{10,... | collective-permute-start | bytes 1572872 | tf_op jit(solution)/shard_map/ppermute | solution.py:303
  44.7 0.4 collective-permute-start.13
  45.1 14.0 %collective-permute-done.11.refs_3_ = bf16[64,4096]{1,0:T(8,128)(2,1)S(1)} collective-permute-done((bf16[64,4096]{1,0:T(8,128)(2,1)S(1)}, bf16[64,4096]{1,0:T(8,128)(2,1)S(1)}, u32[]{:S(2)}, u32[]{:S(2)}) %collective-permute-start.11) | collective-permute-done | bytes 524320 | tf_op jit(solution)/shard_map/ppermute | solution.py:300
  59.2 0.0 collective-permute-done.12.refs_6_
  59.2 0.0 collective-permute-done.10.other
  59.2 1.8 %collective-permute-start.14 = (bf16[64,2048]{1,0:T(8,128)(2,1)S(1)}, bf16[64,2048]{1,0:T(8,128)(2,1)S(1)}, u32[]{:S(2)}, u32[]{:S(2)}) collective-permute-start(bf16[64,2048]{1,0:T(8,128)(2,1)S(1)} %slice.8), channel_id=1, source_target_pairs={{0,2},{1,3},{2,0},{3,1},{4,6},{5,7},{6,4},{7,5},{8,10},{9,11},{10,... | collective-permute-start | bytes 786440 | tf_op jit(solution)/shard_map/ppermute | solution.py:303
  61.0 0.5 collective-permute-start.17
  61.6 0.1 collective-permute-start.15
  61.6 0.1 collective-permute-start.16
  61.7 1.6 %collective-permute-start.18 = (bf16[128,1536]{1,0:T(8,128)(2,1)S(1)}, bf16[128,1536]{1,0:T(8,128)(2,1)S(1)}, u32[]{:S(2)}, u32[]{:S(2)}) collective-permute-start(bf16[128,1536]{1,0:T(8,128)(2,1)S(1)} %get-tuple-element.83), channel_id=1, source_target_pairs={{0,17},{1,16},{2,19},{3,18},{4,21},{5,20},{6,23},{7,22},{8,25},{9,... | collective-permute-start | bytes 1179656 | tf_op jit(solution)/shard_map/ppermute | solution.py:297
  63.3 0.6 keys.1
  63.9 3.3 %collective-permute-done.14.refs_7_ = bf16[64,2048]{1,0:T(8,128)(2,1)S(1)} collective-permute-done((bf16[64,2048]{1,0:T(8,128)(2,1)S(1)}, bf16[64,2048]{1,0:T(8,128)(2,1)S(1)}, u32[]{:S(2)}, u32[]{:S(2)}) %collective-permute-start.14) | collective-permute-done | bytes 262176 | tf_op jit(solution)/shard_map/ppermute | solution.py:303
  67.2 8.9 %attend.3 = (bf16[128,1024]{1,0:T(8,128)(2,1)S(1)}, bf16[128,1024]{1,0:T(8,128)(2,1)S(1)}, bf16[128,1024]{1,0:T(8,128)(2,1)S(1)}, bf16[128,1024]{1,0:T(8,128)(2,1)S(1)}) custom-call(s32[1]{0:T(128)} %bitcast.1.info, bf16[2,640,512]{2,1,0:T(8,128)(2,1)S(1)} %get-tuple-element.66.latent, bf16[2,640,128]{2,1,0:T(8,128)(2,1)S(1)} %get-tuple-element.67.rope_even, ...), custom_call_target="tpu_custom_call" | custom-call | flops 4362076160 | bytes 8388608 | tf_op jit(solution)/shard_map/attend/pallas_call | solution.py:443
  76.1 0.7 collective-permute-start.19
  76.8 0.0 collective-permute-start.20
  76.8 0.0 collective-permute-done.15.refs_7_
  76.8 1.5 %collective-permute-start.22 = (bf16[128,1024]{1,0:T(8,128)(2,1)S(1)}, bf16[128,1024]{1,0:T(8,128)(2,1)S(1)}, u32[]{:S(2)}, u32[]{:S(2)}) collective-permute-start(bf16[128,1024]{1,0:T(8,128)(2,1)S(1)} %get-tuple-element.92), channel_id=1, source_target_pairs={{0,17},{1,16},{2,19},{3,18},{4,21},{5,20},{6,23},{7,22},{8,25},{9,... | collective-permute-start | bytes 786440 | tf_op jit(solution)/shard_map/ppermute | solution.py:297
  78.4 0.0 collective-permute-done.16.refs_9_.refs_13_
  78.4 1.2 collective-permute-done.18.refs_11_.refs_15_
  79.5 4.5 %attend.4 = (bf16[128,512]{1,0:T(8,128)(2,1)S(1)}, bf16[128,512]{1,0:T(8,128)(2,1)S(1)}, bf16[128,512]{1,0:T(8,128)(2,1)S(1)}, bf16[128,512]{1,0:T(8,128)(2,1)S(1)}) custom-call(s32[1]{0:T(128)} %bitcast.1.info, bf16[2,640,512]{2,1,0:T(8,128)(2,1)S(1)} %get-tuple-element.66.latent, bf16[2,640,128]{2,1,0:T(8,128)(2,1)S(1)} %get-tuple-element.67.rope_even, ...), custom_call_target="tpu_custom_call" | custom-call | flops 2181038080 | bytes 4194304 | tf_op jit(solution)/shard_map/attend/pallas_call | solution.py:443
  84.0 1.6 %collective-permute-start.23 = (bf16[128,512]{1,0:T(8,128)(2,1)S(1)}, bf16[128,512]{1,0:T(8,128)(2,1)S(1)}, u32[]{:S(2)}, u32[]{:S(2)}) collective-permute-start(bf16[128,512]{1,0:T(8,128)(2,1)S(1)} %get-tuple-element.93), channel_id=1, source_target_pairs={{0,16},{1,17},{2,18},{3,19},{4,20},{5,21},{6,22},{7,23},{8,24},{9,... | collective-permute-start | bytes 393224 | tf_op jit(solution)/shard_map/ppermute | solution.py:297
  85.6 0.5 collective-permute-start.21
  86.1 1.0 collective-permute-done.19.refs_6_
  87.1 0.1 collective-permute-start.26
  87.2 4.5 %attend.5 = (bf16[128,512]{1,0:T(8,128)(2,1)S(1)}, bf16[128,512]{1,0:T(8,128)(2,1)S(1)}, bf16[128,512]{1,0:T(8,128)(2,1)S(1)}, bf16[128,512]{1,0:T(8,128)(2,1)S(1)}) custom-call(s32[1]{0:T(128)} %bitcast.1.info, bf16[2,640,512]{2,1,0:T(8,128)(2,1)S(1)} %get-tuple-element.66.latent, bf16[2,640,128]{2,1,0:T(8,128)(2,1)S(1)} %get-tuple-element.67.rope_even, ...), custom_call_target="tpu_custom_call" | custom-call | flops 2181038080 | bytes 4194304 | tf_op jit(solution)/shard_map/attend/pallas_call | solution.py:443
  91.7 0.0 collective-permute-done.22.refs_9_
  91.7 3.6 %collective-permute-done.23.refs_7_ = bf16[128,512]{1,0:T(8,128)(2,1)S(1)} collective-permute-done((bf16[128,512]{1,0:T(8,128)(2,1)S(1)}, bf16[128,512]{1,0:T(8,128)(2,1)S(1)}, u32[]{:S(2)}, u32[]{:S(2)}) %collective-permute-start.23) | collective-permute-done | bytes 131104 | tf_op jit(solution)/shard_map/ppermute | solution.py:297
  95.3 0.5 collective-permute-start.25
  95.9 1.3 %collective-permute-start.27 = (bf16[128,512]{1,0:T(8,128)(2,1)S(1)}, bf16[128,512]{1,0:T(8,128)(2,1)S(1)}, u32[]{:S(2)}, u32[]{:S(2)}) collective-permute-start(bf16[128,512]{1,0:T(8,128)(2,1)S(1)} %get-tuple-element.99), channel_id=1, source_target_pairs={{0,17},{1,16},{2,19},{3,18},{4,21},{5,20},{6,23},{7,22},{8,25},{9,... | collective-permute-start | bytes 393224 | tf_op jit(solution)/shard_map/ppermute | solution.py:297
  97.2 0.0 collective-permute-done.26.refs_10_
  97.2 0.0 collective-permute-done.24.refs_5_
  97.2 4.4 %collective-permute-done.25.refs_8_ = bf16[128,512]{1,0:T(8,128)(2,1)S(1)} collective-permute-done((bf16[128,512]{1,0:T(8,128)(2,1)S(1)}, bf16[128,512]{1,0:T(8,128)(2,1)S(1)}, u32[]{:S(2)}, u32[]{:S(2)}) %collective-permute-start.25) | collective-permute-done | bytes 131104 | tf_op jit(solution)/shard_map/ppermute | solution.py:297
  101.6 2.0 %collective-permute-done.27.refs_11_ = bf16[128,512]{1,0:T(8,128)(2,1)S(1)} collective-permute-done((bf16[128,512]{1,0:T(8,128)(2,1)S(1)}, bf16[128,512]{1,0:T(8,128)(2,1)S(1)}, u32[]{:S(2)}, u32[]{:S(2)}) %collective-permute-start.27) | collective-permute-done | bytes 131104 | tf_op jit(solution)/shard_map/ppermute | solution.py:297
  103.7 3.5 %all-to-all-start = ((bf16[16,16,576]{2,1,0:T(8,128)(2,1)}), bf16[16,16,576]{2,1,0:T(8,128)(2,1)S(1)}, u32[]{:S(2)}, u32[]{:S(2)}) async-start(bf16[16,16,576]{2,1,0:T(8,128)(2,1)} %bitcast.5), calls=%async_computation | async-start | bytes 655360 | tf_op jit(solution)/shard_map/all_to_all | solution.py:478
  107.2 1.4 %place.1 = bf16[128,8192]{1,0:T(8,128)(2,1)} custom-call(s32[1]{0:T(128)} %bitcast.info, bf16[128,1024]{1,0:T(8,128)(2,1)S(1)} %get-tuple-element.74.refs_0_, bf16[128,512]{1,0:T(8,128)(2,1)S(1)} %get-tuple-element.84.refs_1_, bf16[128,512]{1,0:T(8,128)(2,1)S(1)} %get-tuple-element.88.refs_2_, bf16[128,1024]{1,0:T(8,128)(2,1)S(1)} %collective-permute-done.20.refs_3_, ...), custom_call_target="tpu_custom_call" | custom-call | tf_op jit(solution)/shard_map/place/pallas_call | solution.py:486
  108.6 9.6 %all-to-all-done = bf16[16,16,576]{2,1,0:T(8,128)(2,1)S(1)} async-done(((bf16[16,16,576]{2,1,0:T(8,128)(2,1)}), bf16[16,16,576]{2,1,0:T(8,128)(2,1)S(1)}, u32[]{:S(2)}, u32[]{:S(2)}) %all-to-all-start) | async-done | bytes 294944 | tf_op jit(solution)/shard_map/all_to_all | solution.py:478
  118.3 0.9 copy.10
  (13 shorter events, 0.2 us)
Async XLA Ops:
  1.6 1.7 %collective-permute-start = (bf16[32,4096]{1,0:T(8,128)(2,1)S(1)}, bf16[32,4096]{1,0:T(8,128)(2,1)S(1)}, u32[]{:S(2)}, u32[]{:S(2)}) collective-permute-start(bf16[32,4096]{1,0:T(8,128)(2,1)S(1)} %constant_dynamic-slice_fusion), channel_id=1, source_target_pairs={{0,1},{1,0},{2,3},{3,2},{4,5},{5,4},{6,7},{7,6},{8,9},{9,8},{10,11... | collective-permute-start | bytes 786440 | tf_op jit(solution)/shard_map/ppermute | solution.py:297
  4.3 20.9 %collective-permute-start.4 = (bf16[64,4096]{1,0:T(8,128)(2,1)S(1)}, bf16[64,4096]{1,0:T(8,128)(2,1)S(1)}, u32[]{:S(2)}, u32[]{:S(2)}) collective-permute-start(bf16[64,4096]{1,0:T(8,128)(2,1)S(1)} %pair.1.refs_0_), channel_id=1, source_target_pairs={{0,2},{1,3},{2,0},{3,1},{4,6},{5,7},{6,4},{7,5},{8,10},{9,11},{10,... | collective-permute-start | bytes 1572872 | tf_op jit(solution)/shard_map/ppermute | solution.py:303
  7.2 17.9 %collective-permute-start.3 = (bf16[64,4096]{1,0:T(8,128)(2,1)S(1)}, bf16[64,4096]{1,0:T(8,128)(2,1)S(1)}, u32[]{:S(2)}, u32[]{:S(2)}) collective-permute-start(bf16[64,4096]{1,0:T(8,128)(2,1)S(1)} %pair.1.refs_0_), channel_id=1, source_target_pairs={{0,4},{1,5},{2,6},{3,7},{4,8},{5,9},{6,10},{7,11},{8,12},{9,13},{1... | collective-permute-start | bytes 1572872 | tf_op jit(solution)/shard_map/ppermute | solution.py:300
  11.1 4.9 %copy-start = (bf16[128,640]{1,0:T(8,128)(2,1)S(1)}, bf16[128,640]{1,0:T(8,128)(2,1)}, u32[]{:S(2)}) copy-start(bf16[128,640]{1,0:T(8,128)(2,1)} %get-tuple-element.55) | copy-start | bytes 491524
  14.5 10.7 %collective-permute-start.5 = (bf16[128,1536]{1,0:T(8,128)(2,1)S(1)}, bf16[128,1536]{1,0:T(8,128)(2,1)S(1)}, u32[]{:S(2)}, u32[]{:S(2)}) collective-permute-start(bf16[128,1536]{1,0:T(8,128)(2,1)S(1)} %get-tuple-element.59), channel_id=1, source_target_pairs={{0,16},{1,17},{2,18},{3,19},{4,20},{5,21},{6,22},{7,23},{8,24},{9,... | collective-permute-start | bytes 1179656 | tf_op jit(solution)/shard_map/ppermute | solution.py:297
  16.1 3.1 %collective-permute-start.2 = (bf16[128,640]{1,0:T(8,128)(2,1)S(1)}, bf16[128,640]{1,0:T(8,128)(2,1)S(1)}, u32[]{:S(2)}, u32[]{:S(2)}) collective-permute-start(bf16[128,640]{1,0:T(8,128)(2,1)S(1)} %copy-done), channel_id=1, source_target_pairs={{1,5},{3,7},{5,9},{7,11},{9,13},{11,15},{17,21},{19,23},{21,25},{2... | collective-permute-start | bytes 491528 | tf_op jit(solution)/shard_map/ppermute | solution.py:309
  16.7 6.1 %collective-permute-start.1 = (bf16[128,640]{1,0:T(8,128)(2,1)S(1)}, bf16[128,640]{1,0:T(8,128)(2,1)S(1)}, u32[]{:S(2)}, u32[]{:S(2)}) collective-permute-start(bf16[128,640]{1,0:T(8,128)(2,1)S(1)} %copy-done), channel_id=1, source_target_pairs={{0,2},{1,3},{2,4},{3,5},{4,6},{5,7},{6,8},{7,9},{8,10},{9,11},{10,... | collective-permute-start | bytes 491528 | tf_op jit(solution)/shard_map/ppermute | solution.py:309
  25.2 11.9 %collective-permute-start.6 = (bf16[384,640]{1,0:T(8,128)(2,1)S(1)}, bf16[384,640]{1,0:T(8,128)(2,1)S(1)}, u32[]{:S(2)}, u32[]{:S(2)}) collective-permute-start(bf16[384,640]{1,0:T(8,128)(2,1)S(1)} %pad_maximum_fusion), channel_id=1, source_target_pairs={{0,16},{1,17},{2,18},{3,19},{4,20},{5,21},{6,22},{7,23},{8,24},{9,... | collective-permute-start | bytes 1474568 | tf_op jit(solution)/shard_map/ppermute | solution.py:297
  26.7 12.7 %collective-permute-start.8 = (bf16[64,4096]{1,0:T(8,128)(2,1)S(1)}, bf16[64,4096]{1,0:T(8,128)(2,1)S(1)}, u32[]{:S(2)}, u32[]{:S(2)}) collective-permute-start(bf16[64,4096]{1,0:T(8,128)(2,1)S(1)} %collective-permute-done.3.refs_1_), channel_id=1, source_target_pairs={{0,2},{1,3},{2,0},{3,1},{4,6},{5,7},{6,4},{7,5},{8,10},{9,11},{10,... | collective-permute-start | bytes 1572872 | tf_op jit(solution)/shard_map/ppermute | solution.py:303
  27.2 15.8 %collective-permute-start.7 = (bf16[64,4096]{1,0:T(8,128)(2,1)S(1)}, bf16[64,4096]{1,0:T(8,128)(2,1)S(1)}, u32[]{:S(2)}, u32[]{:S(2)}) collective-permute-start(bf16[64,4096]{1,0:T(8,128)(2,1)S(1)} %collective-permute-done.3.refs_1_), channel_id=1, source_target_pairs={{0,4},{1,5},{2,6},{3,7},{4,8},{5,9},{6,10},{7,11},{8,12},{9,13},{1... | collective-permute-start | bytes 1572872 | tf_op jit(solution)/shard_map/ppermute | solution.py:300
  28.9 8.3 %collective-permute-start.9 = (bf16[128,1536]{1,0:T(8,128)(2,1)S(1)}, bf16[128,1536]{1,0:T(8,128)(2,1)S(1)}, u32[]{:S(2)}, u32[]{:S(2)}) collective-permute-start(bf16[128,1536]{1,0:T(8,128)(2,1)S(1)} %get-tuple-element.64), channel_id=1, source_target_pairs={{0,1},{1,0},{2,3},{3,2},{4,5},{5,4},{6,7},{7,6},{8,9},{9,8},{10,11... | collective-permute-start | bytes 1179656 | tf_op jit(solution)/shard_map/ppermute | solution.py:297
  43.0 16.2 %collective-permute-start.10 = (bf16[768,640]{1,0:T(8,128)(2,1)S(1)}, bf16[768,640]{1,0:T(8,128)(2,1)S(1)}, u32[]{:S(2)}, u32[]{:S(2)}) collective-permute-start(bf16[768,640]{1,0:T(8,128)(2,1)S(1)} %constant_dynamic-update-slice_fusion.own), channel_id=1, source_target_pairs={{0,1},{1,0},{2,3},{3,2},{4,5},{5,4},{6,7},{7,6},{8,9},{9,8},{10,11... | collective-permute-start | bytes 2949128 | tf_op jit(solution)/shard_map/ppermute | solution.py:297
  43.0 16.1 %collective-permute-start.11 = (bf16[64,4096]{1,0:T(8,128)(2,1)S(1)}, bf16[64,4096]{1,0:T(8,128)(2,1)S(1)}, u32[]{:S(2)}, u32[]{:S(2)}) collective-permute-start(bf16[64,4096]{1,0:T(8,128)(2,1)S(1)} %collective-permute-done.7.refs_2_), channel_id=1, source_target_pairs={{0,4},{1,5},{2,6},{3,7},{4,8},{5,9},{6,10},{7,11},{8,12},{9,13},{1... | collective-permute-start | bytes 1572872 | tf_op jit(solution)/shard_map/ppermute | solution.py:300
  43.0 16.2 %collective-permute-start.12 = (bf16[64,4096]{1,0:T(8,128)(2,1)S(1)}, bf16[64,4096]{1,0:T(8,128)(2,1)S(1)}, u32[]{:S(2)}, u32[]{:S(2)}) collective-permute-start(bf16[64,4096]{1,0:T(8,128)(2,1)S(1)} %collective-permute-done.7.refs_2_), channel_id=1, source_target_pairs={{0,2},{1,3},{2,0},{3,1},{4,6},{5,7},{6,4},{7,5},{8,10},{9,11},{10,... | collective-permute-start | bytes 1572872 | tf_op jit(solution)/shard_map/ppermute | solution.py:303
  44.7 14.4 %collective-permute-start.13 = (bf16[128,1536]{1,0:T(8,128)(2,1)S(1)}, bf16[128,1536]{1,0:T(8,128)(2,1)S(1)}, u32[]{:S(2)}, u32[]{:S(2)}) collective-permute-start(bf16[128,1536]{1,0:T(8,128)(2,1)S(1)} %get-tuple-element.72), channel_id=1, source_target_pairs={{0,17},{1,16},{2,19},{3,18},{4,21},{5,20},{6,23},{7,22},{8,25},{9,... | collective-permute-start | bytes 1179656 | tf_op jit(solution)/shard_map/ppermute | solution.py:297
  59.2 8.0 %collective-permute-start.14 = (bf16[64,2048]{1,0:T(8,128)(2,1)S(1)}, bf16[64,2048]{1,0:T(8,128)(2,1)S(1)}, u32[]{:S(2)}, u32[]{:S(2)}) collective-permute-start(bf16[64,2048]{1,0:T(8,128)(2,1)S(1)} %slice.8), channel_id=1, source_target_pairs={{0,2},{1,3},{2,0},{3,1},{4,6},{5,7},{6,4},{7,5},{8,10},{9,11},{10,... | collective-permute-start | bytes 786440 | tf_op jit(solution)/shard_map/ppermute | solution.py:303
  61.0 15.8 %collective-permute-start.17 = (bf16[128,1536]{1,0:T(8,128)(2,1)S(1)}, bf16[128,1536]{1,0:T(8,128)(2,1)S(1)}, u32[]{:S(2)}, u32[]{:S(2)}) collective-permute-start(bf16[128,1536]{1,0:T(8,128)(2,1)S(1)} %get-tuple-element.81), channel_id=1, source_target_pairs={{0,16},{1,17},{2,18},{3,19},{4,20},{5,21},{6,22},{7,23},{8,24},{9,... | collective-permute-start | bytes 1179656 | tf_op jit(solution)/shard_map/ppermute | solution.py:297
  61.6 15.3 %collective-permute-start.15 = (bf16[64,2048]{1,0:T(8,128)(2,1)S(1)}, bf16[64,2048]{1,0:T(8,128)(2,1)S(1)}, u32[]{:S(2)}, u32[]{:S(2)}) collective-permute-start(bf16[64,2048]{1,0:T(8,128)(2,1)S(1)} %slice.9), channel_id=1, source_target_pairs={{0,4},{1,5},{2,6},{3,7},{4,8},{5,9},{6,10},{7,11},{8,12},{9,13},{1... | collective-permute-start | bytes 786440 | tf_op jit(solution)/shard_map/ppermute | solution.py:300
  61.6 16.7 %collective-permute-start.16 = (bf16[128,1536]{1,0:T(8,128)(2,1)S(1)}, bf16[128,1536]{1,0:T(8,128)(2,1)S(1)}, u32[]{:S(2)}, u32[]{:S(2)}) collective-permute-start(bf16[128,1536]{1,0:T(8,128)(2,1)S(1)} %get-tuple-element.79), channel_id=1, source_target_pairs={{0,1},{1,0},{2,3},{3,2},{4,5},{5,4},{6,7},{7,6},{8,9},{9,8},{10,11... | collective-permute-start | bytes 1179656 | tf_op jit(solution)/shard_map/ppermute | solution.py:297
  61.7 17.8 %collective-permute-start.18 = (bf16[128,1536]{1,0:T(8,128)(2,1)S(1)}, bf16[128,1536]{1,0:T(8,128)(2,1)S(1)}, u32[]{:S(2)}, u32[]{:S(2)}) collective-permute-start(bf16[128,1536]{1,0:T(8,128)(2,1)S(1)} %get-tuple-element.83), channel_id=1, source_target_pairs={{0,17},{1,16},{2,19},{3,18},{4,21},{5,20},{6,23},{7,22},{8,25},{9,... | collective-permute-start | bytes 1179656 | tf_op jit(solution)/shard_map/ppermute | solution.py:297
  76.1 10.9 %collective-permute-start.19 = (bf16[128,1024]{1,0:T(8,128)(2,1)S(1)}, bf16[128,1024]{1,0:T(8,128)(2,1)S(1)}, u32[]{:S(2)}, u32[]{:S(2)}) collective-permute-start(bf16[128,1024]{1,0:T(8,128)(2,1)S(1)} %get-tuple-element.86), channel_id=1, source_target_pairs={{0,16},{1,17},{2,18},{3,19},{4,20},{5,21},{6,22},{7,23},{8,24},{9,... | collective-permute-start | bytes 786440 | tf_op jit(solution)/shard_map/ppermute | solution.py:297
  76.8 14.9 %collective-permute-start.20 = (bf16[128,1024]{1,0:T(8,128)(2,1)S(1)}, bf16[128,1024]{1,0:T(8,128)(2,1)S(1)}, u32[]{:S(2)}, u32[]{:S(2)}) collective-permute-start(bf16[128,1024]{1,0:T(8,128)(2,1)S(1)} %get-tuple-element.89), channel_id=1, source_target_pairs={{0,1},{1,0},{2,3},{3,2},{4,5},{5,4},{6,7},{7,6},{8,9},{9,8},{10,11... | collective-permute-start | bytes 786440 | tf_op jit(solution)/shard_map/ppermute | solution.py:297
  76.8 14.9 %collective-permute-start.22 = (bf16[128,1024]{1,0:T(8,128)(2,1)S(1)}, bf16[128,1024]{1,0:T(8,128)(2,1)S(1)}, u32[]{:S(2)}, u32[]{:S(2)}) collective-permute-start(bf16[128,1024]{1,0:T(8,128)(2,1)S(1)} %get-tuple-element.92), channel_id=1, source_target_pairs={{0,17},{1,16},{2,19},{3,18},{4,21},{5,20},{6,23},{7,22},{8,25},{9,... | collective-permute-start | bytes 786440 | tf_op jit(solution)/shard_map/ppermute | solution.py:297
  84.0 11.3 %collective-permute-start.23 = (bf16[128,512]{1,0:T(8,128)(2,1)S(1)}, bf16[128,512]{1,0:T(8,128)(2,1)S(1)}, u32[]{:S(2)}, u32[]{:S(2)}) collective-permute-start(bf16[128,512]{1,0:T(8,128)(2,1)S(1)} %get-tuple-element.93), channel_id=1, source_target_pairs={{0,16},{1,17},{2,18},{3,19},{4,20},{5,21},{6,22},{7,23},{8,24},{9,... | collective-permute-start | bytes 393224 | tf_op jit(solution)/shard_map/ppermute | solution.py:297
  85.6 9.8 %collective-permute-start.21 = (bf16[128,512]{1,0:T(8,128)(2,1)S(1)}, bf16[128,512]{1,0:T(8,128)(2,1)S(1)}, u32[]{:S(2)}, u32[]{:S(2)}) collective-permute-start(bf16[128,512]{1,0:T(8,128)(2,1)S(1)} %get-tuple-element.90), channel_id=1, source_target_pairs={{0,1},{1,0},{2,3},{3,2},{4,5},{5,4},{6,7},{7,6},{8,9},{9,8},{10,11... | collective-permute-start | bytes 393224 | tf_op jit(solution)/shard_map/ppermute | solution.py:297
  87.1 10.1 %collective-permute-start.26 = (bf16[128,512]{1,0:T(8,128)(2,1)S(1)}, bf16[128,512]{1,0:T(8,128)(2,1)S(1)}, u32[]{:S(2)}, u32[]{:S(2)}) collective-permute-start(bf16[128,512]{1,0:T(8,128)(2,1)S(1)} %get-tuple-element.97), channel_id=1, source_target_pairs={{0,17},{1,16},{2,19},{3,18},{4,21},{5,20},{6,23},{7,22},{8,25},{9,... | collective-permute-start | bytes 393224 | tf_op jit(solution)/shard_map/ppermute | solution.py:297
  95.3 1.9 %collective-permute-start.24 = (bf16[128,512]{1,0:T(8,128)(2,1)S(1)}, bf16[128,512]{1,0:T(8,128)(2,1)S(1)}, u32[]{:S(2)}, u32[]{:S(2)}) collective-permute-start(bf16[128,512]{1,0:T(8,128)(2,1)S(1)} %get-tuple-element.94), channel_id=1, source_target_pairs={{0,1},{1,0},{2,3},{3,2},{4,5},{5,4},{6,7},{7,6},{8,9},{9,8},{10,11... | collective-permute-start | bytes 393224 | tf_op jit(solution)/shard_map/ppermute | solution.py:297
  95.3 6.3 %collective-permute-start.25 = (bf16[128,512]{1,0:T(8,128)(2,1)S(1)}, bf16[128,512]{1,0:T(8,128)(2,1)S(1)}, u32[]{:S(2)}, u32[]{:S(2)}) collective-permute-start(bf16[128,512]{1,0:T(8,128)(2,1)S(1)} %get-tuple-element.96), channel_id=1, source_target_pairs={{0,16},{1,17},{2,18},{3,19},{4,20},{5,21},{6,22},{7,23},{8,24},{9,... | collective-permute-start | bytes 393224 | tf_op jit(solution)/shard_map/ppermute | solution.py:297
  95.9 7.8 %collective-permute-start.27 = (bf16[128,512]{1,0:T(8,128)(2,1)S(1)}, bf16[128,512]{1,0:T(8,128)(2,1)S(1)}, u32[]{:S(2)}, u32[]{:S(2)}) collective-permute-start(bf16[128,512]{1,0:T(8,128)(2,1)S(1)} %get-tuple-element.99), channel_id=1, source_target_pairs={{0,17},{1,16},{2,19},{3,18},{4,21},{5,20},{6,23},{7,22},{8,25},{9,... | collective-permute-start | bytes 393224 | tf_op jit(solution)/shard_map/ppermute | solution.py:297
  103.7 14.6 %all-to-all-start = ((bf16[16,16,576]{2,1,0:T(8,128)(2,1)}), bf16[16,16,576]{2,1,0:T(8,128)(2,1)S(1)}, u32[]{:S(2)}, u32[]{:S(2)}) async-start(bf16[16,16,576]{2,1,0:T(8,128)(2,1)} %bitcast.5), calls=%async_computation | async-start | bytes 655360 | tf_op jit(solution)/shard_map/all_to_all | solution.py:478

commit v9 on v8

--- a/solution.py
+++ b/solution.py
@@ -19,17 +19,17 @@
 HQ = H // QUAD
 CHUNK_HEADS = (8, 8)
 PHASES = (
-    ("z", "y0", "b~", "f~", "q02"),
+    ("z", "y0", "b~", "f~", "q02", "d~"),
     ("z", "y1", "k", "q01"),
-    ("z", "y2", "p", "q03", "q12~"),
-    ("y3", "w", "q13~", "q11"),
+    ("z", "y2", "p", "q03"),
+    ("y3", "w", "q12~", "q13~", "q11"),
 )
 CHUNKS = len(CHUNK_HEADS)
 FIRST_HEAD = tuple(sum(CHUNK_HEADS[:j]) for j in range(CHUNKS))
 ROW = LAT + ROPE
 EXT = 640
 VMEM_LIMIT = 20 * 1024 * 1024
-CALLS = ((0, 0, 4), (1, 0, 2), (1, 2, 2))
+CALLS = ((0, 0, 2), (0, 2, 2), (1, 0, 2), (1, 2, 2))
 SMEM = pltpu.SMEM
 VMEM = pltpu.VMEM
 
@@ -378,6 +378,10 @@
         name="queries",
     )(quarter_info, *in_hbm(q_heads, tie(cosine, pair_rows if outer else got), sine))
 
+    def to_decode(array):
+        array = array.reshape(size, slot_count, ROW)
+        return lax.all_to_all(array, "ctx", split_axis=0, concat_axis=0, tiled=True)
+
     phases = Phases()
     line = [pair_rows] if outer else []
     side = []
@@ -400,6 +404,8 @@
                 halves.append(phases.send(late, inner_swap, line[step][:, :half]))
         elif kind == "w" and outer:
             halves.append(phases.send(late, around, side[-1][:, half:], 4))
+        elif kind == "d":
+            decode_cache = phases.send(late, to_decode, tie(outgoing, queries[0]))
         elif kind == "b":
             parts["b"] = phases.send(late, from_behind, parts["r"], 2, False)
         elif kind == "f":
@@ -464,25 +470,14 @@
 
     results = []
     for call in CALLS:
-        sent = [piece for one in results for piece in one[1:]]
-        last = len(results) + 1 == len(CALLS)
-        mine_info = tie(mine_info, *(results[0][2:3] if last else []))
+        mine_info = tie(mine_info, *[piece for one in results[-2:-1] for piece in one[2:]])
         pieces = attend(*call)
         mine_info = tie(mine_info, pieces[0])
-        before = sent[:-1] if last else []
+        before = results[-1][2:3] if len(results) + 1 == len(CALLS) else []
         results.append(
             [pieces[0]] + [quad_swap(tie(pieces[r], *before), r) for r in range(1, QUAD)]
         )
     pieces = [one[r] for r in range(QUAD) for one in results]
-    sent = [piece for one in results for piece in one[1:]]
-    arrived = lax.all_to_all(
-        tie(outgoing, *sent).reshape(size, slot_count, ROW),
-        "ctx",
-        split_axis=0,
-        concat_axis=0,
-        tiled=True,
-    )
-    decode_cache = arrived.reshape(size * slot_count, ROW)
     attn_out = pl.pallas_call(
         gather_kernel,
         out_shape=shape((tok, H * VDIM)),
@@ -492,7 +487,7 @@
         compiler_params=params,
         name="place",
     )(quarter_info, *pieces)
-    return (attn_out, decode_cache)
+    return (attn_out, decode_cache.reshape(size * slot_count, ROW))
 
 
 def solution(mesh):

time: 119 us -> 144 us (1.21)
  local copies, waits for them, and re-layouts: 2.01 us -> 21.3 us
  waiting for transfers between devices: 60.2 us -> 47.8 us
  Pallas kernels: 26.6 us -> 37.3 us
  starting transfers between devices: 29.4 us -> 34.4 us
    unnamed x6 -> x64, local copies, waits for them, and re-layouts: 0.94 us -> 18.5 us
    all_to_all x1, waiting for transfers between devices: 9.64 us -> 1.64 us  [to_decode(): return lax.all_to_all(array, 'ctx', split_axis=0, concat_axis=0, tiled=True)]
    pallas_call x1, Pallas kernels: 1.41 us -> 9.19 us  [body(): pl.pallas_call(gather_kernel, out_shape=shape((tok, H * VDIM)), in_specs=...]
    ppermute x18 -> x21, waiting for transfers between devices: 23.7 us -> 18.3 us  [quad_swap(): return lax.ppermute(array, ('groups', 'ctx'), pairs)]
    ppermute x4, waiting for transfers between devices: 17.7 us -> 22.9 us  [around(): lax.ppermute(array, 'ctx', [(i, (i + by) % size) for i in range(size)])]
    ppermute x18 -> x21, starting transfers between devices: 12.4 us -> 15.5 us  [quad_swap(): return lax.ppermute(array, ('groups', 'ctx'), pairs)]
    ppermute x4, starting transfers between devices: 3.37 us -> 6.31 us  [around(): lax.ppermute(array, 'ctx', [(i, (i + by) % size) for i in range(size)])]
    ppermute x4, waiting for transfers between devices: 5.46 us -> 2.82 us  [inner_swap(): return lax.ppermute(array, 'ctx', [(i, i ^ 2) for i in range(size)])]
  transfers between devices with their start and end apart: 29 -> 32, of which waited for: 14 -> 12; matrix products, arithmetic and copies ran while one was open for 0% -> 7% of each run, Pallas kernels for 21% -> 19%
where the time goes in v9:
time: 144 us; the launch traced here: 143 us
  waiting for transfers between devices  47.8 us (33%)
  Pallas kernels  37.3 us (26%)
  starting transfers between devices  34.4 us (24%)
  local copies, waits for them, and re-layouts  21.3 us (15%)
    ppermute x4, waiting for transfers between devices, around(): lax.ppermute(array, 'ctx', [(i, (i + by) % size) for i in range(size)])  22.9 us
    pallas_call x4, Pallas kernels, attend(): pl.pallas_call(functools.partial(attend_kernel, outer), grid=(steps,), ou...  19.7 us
    unnamed x64, local copies, waits for them, and re-layouts  18.5 us
    ppermute x21, waiting for transfers between devices, quad_swap(): return lax.ppermute(array, ('groups', 'ctx'), pairs)  18.3 us
    ppermute x21, starting transfers between devices, quad_swap(): return lax.ppermute(array, ('groups', 'ctx'), pairs)  15.5 us
    pallas_call x1, Pallas kernels, body(): pl.pallas_call(gather_kernel, out_shape=shape((tok, H * VDIM)), in_specs=...  9.19 us
    ppermute x4, starting transfers between devices, around(): lax.ppermute(array, 'ctx', [(i, (i + by) % size) for i in range(size)])  6.31 us
    ppermute x4, starting transfers between devices, inner_swap(): return lax.ppermute(array, 'ctx', [(i, i ^ 2) for i in range(size)])  4.83 us
  transfers between devices with their start and end apart: 32, of which 12 were waited for; matrix products, arithmetic and copies ran while one was open for 7% of the time, Pallas kernels for 19%

profile of v9, /device:TPU:0, one launch (start us, length us, event | category | flops | bytes accessed | tf_op | source)
XLA Modules:
  0.0 142.8 jit_solution(7348150190012475538)
XLA Ops:
  0.6 1.0 constant_dynamic-slice_fusion
  2.1 1.2 collective-permute-done.got
  3.3 1.0 pair.1.refs_0_
  4.3 3.0 %collective-permute-start.3 = (bf16[64,4096]{1,0:T(8,128)(2,1)S(1)}, bf16[64,4096]{1,0:T(8,128)(2,1)S(1)}, u32[]{:S(2)}, u32[]{:S(2)}) collective-permute-start(bf16[64,4096]{1,0:T(8,128)(2,1)S(1)} %pair.1.refs_0_), channel_id=1, source_target_pairs={{0,4},{1,5},{2,6},{3,7},{4,8},{5,9},{6,10},{7,11},{8,12},{9,13},{1... | collective-permute-start | bytes 1572872 | tf_op jit(solution)/shard_map/ppermute | solution.py:300
  7.3 1.5 %collective-permute-start.4 = (bf16[64,4096]{1,0:T(8,128)(2,1)S(1)}, bf16[64,4096]{1,0:T(8,128)(2,1)S(1)}, u32[]{:S(2)}, u32[]{:S(2)}) collective-permute-start(bf16[64,4096]{1,0:T(8,128)(2,1)S(1)} %pair.1.refs_0_), channel_id=1, source_target_pairs={{0,2},{1,3},{2,0},{3,1},{4,6},{5,7},{6,4},{7,5},{8,10},{9,11},{10,... | collective-permute-start | bytes 1572872 | tf_op jit(solution)/shard_map/ppermute | solution.py:303
  8.8 2.3 %rows.1 = (bf16[128,640]{1,0:T(8,128)(2,1)}, f32[128,128]{1,0:T(8,128)}, f32[128,128]{1,0:T(8,128)}, bf16[256,576]{1,0:T(8,128)(2,1)}) custom-call(s32[1]{0:T(128)} %bitcast.1.info, s32[8]{0:T(128)} %lengths, bf16[576,128]{1,0:T(8,128)(2,1)} %bitcast.8, f32[1,512]{1,0:T(1,128)} %bitcast.9, s32[1,128]{1,0:T(1,128)} %bitcast.10, f32[1,128]{1,0:T(1,128)} %constant.30.clone.freq), custom_call_target="tpu_custom_call" | custom-call | tf_op jit(solution)/shard_map/rows/pallas_call | solution.py:344
  11.1 3.4 %queries.1 = (bf16[128,1536]{1,0:T(8,128)(2,1)S(1)}, bf16[128,1536]{1,0:T(8,128)(2,1)S(1)}, bf16[128,1536]{1,0:T(8,128)(2,1)S(1)}, bf16[128,1536]{1,0:T(8,128)(2...) custom-call(s32[1]{0:T(128)} %bitcast.info, ...), custom_call_target="tpu_custom_call" | custom-call | bytes 6291456 | tf_op jit(solution)/shard_map/queries/pallas_call | solution.py:368
  14.5 0.7 copy-done.24
  15.3 0.7 copy-done.25
  16.0 0.7 copy-done.26
  16.7 1.5 %collective-permute-start.5 = (bf16[128,1536]{1,0:T(8,128)(2,1)S(1)}, bf16[128,1536]{1,0:T(8,128)(2,1)S(1)}, u32[]{:S(2)}, u32[]{:S(2)}) collective-permute-start(bf16[128,1536]{1,0:T(8,128)(2,1)S(1)} %get-tuple-element.65), channel_id=1, source_target_pairs={{0,16},{1,17},{2,18},{3,19},{4,20},{5,21},{6,22},{7,23},{8,24},{9,... | collective-permute-start | bytes 1179656 | tf_op jit(solution)/shard_map/ppermute | solution.py:297
  18.2 2.4 %collective-permute-start.1 = (bf16[128,640]{1,0:T(8,128)(2,1)S(1)}, bf16[128,640]{1,0:T(8,128)(2,1)S(1)}, u32[]{:S(2)}, u32[]{:S(2)}) collective-permute-start(bf16[128,640]{1,0:T(8,128)(2,1)S(1)} %copy-done.27), channel_id=1, source_target_pairs={{0,2},{1,3},{2,4},{3,5},{4,6},{5,7},{6,8},{7,9},{8,10},{9,11},{10,... | collective-permute-start | bytes 491528 | tf_op jit(solution)/shard_map/ppermute | solution.py:309
  20.7 0.7 collective-permute-start.2
  21.3 2.2 %collective-permute-done.1 = bf16[128,640]{1,0:T(8,128)(2,1)S(1)} collective-permute-done((bf16[128,640]{1,0:T(8,128)(2,1)S(1)}, bf16[128,640]{1,0:T(8,128)(2,1)S(1)}, u32[]{:S(2)}, u32[]{:S(2)}) %collective-permute-start.1) | collective-permute-done | bytes 163872 | tf_op jit(solution)/shard_map/ppermute | solution.py:309
  23.6 0.9 pad_maximum_fusion
  24.4 2.9 %collective-permute-done.5.refs_10_.refs_14_ = bf16[128,1536]{1,0:T(8,128)(2,1)S(1)} collective-permute-done((bf16[128,1536]{1,0:T(8,128)(2,1)S(1)}, bf16[128,1536]{1,0:T(8,128)(2,1)S(1)}, u32[]{:S(2)}, u32[]{:S(2)}) %collective-permute-start.5) | collective-permute-done | bytes 393248 | tf_op jit(solution)/shard_map/ppermute | solution.py:297
  27.4 1.6 %collective-permute-start.6 = (bf16[384,640]{1,0:T(8,128)(2,1)}, bf16[384,640]{1,0:T(8,128)(2,1)}, u32[]{:S(2)}, u32[]{:S(2)}) collective-permute-start(bf16[384,640]{1,0:T(8,128)(2,1)} %pad_maximum_fusion), channel_id=1, source_target_pairs={{0,16},{1,17},{2,18},{3,19},{4,20},{5,21},{6,22},{7,23},{8,24},{9,... | collective-permute-start | bytes 1474568 | tf_op jit(solution)/shard_map/ppermute | solution.py:297
  28.9 4.7 %all-to-all-start = ((bf16[16,16,576]{2,1,0:T(8,128)(2,1)}), bf16[16,16,576]{2,1,0:T(8,128)(2,1)}, u32[]{:S(2)}, u32[]{:S(2)}) async-start(bf16[16,16,576]{2,1,0:T(8,128)(2,1)} %bitcast.7), calls=%async_computation | async-start | bytes 655360 | tf_op jit(solution)/shard_map/all_to_all | solution.py:383
  33.6 1.9 %collective-permute-start.7 = (bf16[64,4096]{1,0:T(8,128)(2,1)S(1)}, bf16[64,4096]{1,0:T(8,128)(2,1)S(1)}, u32[]{:S(2)}, u32[]{:S(2)}) collective-permute-start(bf16[64,4096]{1,0:T(8,128)(2,1)S(1)} %collective-permute-done.3.refs_1_), channel_id=1, source_target_pairs={{0,4},{1,5},{2,6},{3,7},{4,8},{5,9},{6,10},{7,11},{8,12},{9,13},{1... | collective-permute-start | bytes 1572872 | tf_op jit(solution)/shard_map/ppermute | solution.py:300
  35.5 1.5 %collective-permute-start.8 = (bf16[64,4096]{1,0:T(8,128)(2,1)S(1)}, bf16[64,4096]{1,0:T(8,128)(2,1)S(1)}, u32[]{:S(2)}, u32[]{:S(2)}) collective-permute-start(bf16[64,4096]{1,0:T(8,128)(2,1)S(1)} %collective-permute-done.3.refs_1_), channel_id=1, source_target_pairs={{0,2},{1,3},{2,0},{3,1},{4,6},{5,7},{6,4},{7,5},{8,10},{9,11},{10,... | collective-permute-start | bytes 1572872 | tf_op jit(solution)/shard_map/ppermute | solution.py:303
  36.9 1.6 %constant_dynamic-update-slice_fusion.3 = bf16[768,640]{1,0:T(8,128)(2,1)} fusion(bf16[128,640]{1,0:T(8,128)(2,1)} %get-tuple-element.61), kind=kLoop, calls=%fused_computation.4 | loop fusion | bytes 327680
  38.5 1.6 %constant_dynamic-update-slice_fusion.2 = bf16[768,640]{1,0:T(8,128)(2,1)} fusion(bf16[768,640]{1,0:T(8,128)(2,1)} %constant_dynamic-update-slice_fusion.3, bf16[128,640]{1,0:T(8,128)(2,1)} %copy-done.28), kind=kLoop, calls=%fused_computation.3 | loop fusion | bytes 327680
  40.1 1.6 %constant_dynamic-update-slice_fusion.1 = bf16[768,640]{1,0:T(8,128)(2,1)} fusion(bf16[768,640]{1,0:T(8,128)(2,1)} %constant_dynamic-update-slice_fusion.2, bf16[128,640]{1,0:T(8,128)(2,1)} %copy-done.29), kind=kLoop, calls=%fused_computation.2 | loop fusion | bytes 327680
  41.7 1.9 %constant_dynamic-update-slice_fusion.own = bf16[768,640]{1,0:T(8,128)(2,1)} fusion(bf16[768,640]{1,0:T(8,128)(2,1)} %constant_dynamic-update-slice_fusion.1, bf16[384,640]{1,0:T(8,128)(2,1)} %collective-permute-done.6), kind=kLoop, calls=%fused_computation.1 | loop fusion | bytes 983040 | tf_op jit(solution)/shard_map/concatenate | solution.py:417
  43.6 1.6 %all-to-all-done = bf16[16,16,576]{2,1,0:T(8,128)(2,1)} async-done(((bf16[16,16,576]{2,1,0:T(8,128)(2,1)}), bf16[16,16,576]{2,1,0:T(8,128)(2,1)}, u32[]{:S(2)}, u32[]{:S(2)}) %all-to-all-start) | async-done | bytes 294944 | tf_op jit(solution)/shard_map/all_to_all | solution.py:383
  45.2 9.8 %collective-permute-done.7.refs_2_ = bf16[64,4096]{1,0:T(8,128)(2,1)S(1)} collective-permute-done((bf16[64,4096]{1,0:T(8,128)(2,1)S(1)}, bf16[64,4096]{1,0:T(8,128)(2,1)S(1)}, u32[]{:S(2)}, u32[]{:S(2)}) %collective-permute-start.7) | collective-permute-done | bytes 524320 | tf_op jit(solution)/shard_map/ppermute | solution.py:300
  55.0 0.9 collective-permute-start.10
  55.9 1.2 collective-permute-start.11
  57.1 0.8 collective-permute-start.12
  57.9 0.7 collective-permute-start.13
  58.5 13.1 %collective-permute-done.11.refs_3_ = bf16[64,4096]{1,0:T(8,128)(2,1)S(1)} collective-permute-done((bf16[64,4096]{1,0:T(8,128)(2,1)S(1)}, bf16[64,4096]{1,0:T(8,128)(2,1)S(1)}, u32[]{:S(2)}, u32[]{:S(2)}) %collective-permute-start.11) | collective-permute-done | bytes 524320 | tf_op jit(solution)/shard_map/ppermute | solution.py:300
  71.6 1.1 collective-permute-start.14
  72.7 1.4 collective-permute-start.19
  74.6 1.8 %keys.1 = (bf16[2,640,512]{2,1,0:T(8,128)(2,1)S(1)}, bf16[2,640,128]{2,1,0:T(8,128)(2,1)S(1)}, bf16[2,640,128]{2,1,0:T(8,128)(2,1)S(1)}, f32[2,256,640]{2,1,0:T(8,128)S(1)}) custom-call(s32[1]{0:T(128)} %bitcast.1.info, bf16[768,640]{1,0:T(8,128)(2,1)} %constant_dynamic-update-slice_fusion.own, bf16[768,640]{1,0:T(8,128)(2,1)S(1)} %collective-permute-done.10.other), custom_call_target="tpu_custom_call" | custom-call | bytes 8388608 | tf_op jit(solution)/shard_map/keys/pallas_call | solution.py:430
  76.3 2.8 %collective-permute-done.14.refs_7_ = bf16[64,2048]{1,0:T(8,128)(2,1)S(1)} collective-permute-done((bf16[64,2048]{1,0:T(8,128)(2,1)S(1)}, bf16[64,2048]{1,0:T(8,128)(2,1)S(1)}, u32[]{:S(2)}, u32[]{:S(2)}) %collective-permute-start.14) | collective-permute-done | bytes 262176 | tf_op jit(solution)/shard_map/ppermute | solution.py:303
  79.2 4.9 %attend.4 = (bf16[128,512]{1,0:T(8,128)(2,1)S(1)}, bf16[128,512]{1,0:T(8,128)(2,1)S(1)}, bf16[128,512]{1,0:T(8,128)(2,1)S(1)}, bf16[128,512]{1,0:T(8,128)(2,1)S(1)}) custom-call(s32[1]{0:T(128)} %bitcast.1.info, bf16[2,640,512]{2,1,0:T(8,128)(2,1)S(1)} %get-tuple-element.74.latent, bf16[2,640,128]{2,1,0:T(8,128)(2,1)S(1)} %get-tuple-element.75.rope_even, ...), custom_call_target="tpu_custom_call" | custom-call | flops 2181038080 | bytes 4194304 | tf_op jit(solution)/shard_map/attend/pallas_call | solution.py:449
  84.1 1.5 %collective-permute-start.15 = (bf16[128,512]{1,0:T(8,128)(2,1)S(1)}, bf16[128,512]{1,0:T(8,128)(2,1)S(1)}, u32[]{:S(2)}, u32[]{:S(2)}) collective-permute-start(bf16[128,512]{1,0:T(8,128)(2,1)S(1)} %get-tuple-element.86), channel_id=1, source_target_pairs={{0,16},{1,17},{2,18},{3,19},{4,20},{5,21},{6,22},{7,23},{8,24},{9,... | collective-permute-start | bytes 393224 | tf_op jit(solution)/shard_map/ppermute | solution.py:297
  85.8 9.9 %collective-permute-done.15.refs_8_ = bf16[128,512]{1,0:T(8,128)(2,1)S(1)} collective-permute-done((bf16[128,512]{1,0:T(8,128)(2,1)S(1)}, bf16[128,512]{1,0:T(8,128)(2,1)S(1)}, u32[]{:S(2)}, u32[]{:S(2)}) %collective-permute-start.15) | collective-permute-done | bytes 131104 | tf_op jit(solution)/shard_map/ppermute | solution.py:297
  95.7 0.7 collective-permute-start.16
  96.4 4.9 %attend.5 = (bf16[128,512]{1,0:T(8,128)(2,1)S(1)}, bf16[128,512]{1,0:T(8,128)(2,1)S(1)}, bf16[128,512]{1,0:T(8,128)(2,1)S(1)}, bf16[128,512]{1,0:T(8,128)(2,1)S(1)}) custom-call(s32[1]{0:T(128)} %bitcast.1.info, bf16[2,640,512]{2,1,0:T(8,128)(2,1)S(1)} %get-tuple-element.74.latent, bf16[2,640,128]{2,1,0:T(8,128)(2,1)S(1)} %get-tuple-element.75.rope_even, ...), custom_call_target="tpu_custom_call" | custom-call | flops 2181038080 | bytes 4194304 | tf_op jit(solution)/shard_map/attend/pallas_call | solution.py:449
  101.4 1.4 collective-permute-start.21
  102.8 0.8 collective-permute-start.22
  104.1 4.9 %attend.6 = (bf16[128,512]{1,0:T(8,128)(2,1)S(1)}, bf16[128,512]{1,0:T(8,128)(2,1)}, bf16[128,512]{1,0:T(8,128)(2,1)S(1)}, bf16[128,512]{1,0:T(8,128)(2,1)}) custom-call(s32[1]{0:T(128)} %bitcast.1.info, bf16[2,640,512]{2,1,0:T(8,128)(2,1)S(1)} %get-tuple-element.74.latent, bf16[2,640,128]{2,1,0:T(8,128)(2,1)S(1)} %get-tuple-element.75.rope_even, ...), custom_call_target="tpu_custom_call" | custom-call | flops 2181038080 | bytes 4194304 | tf_op jit(solution)/shard_map/attend/pallas_call | solution.py:449
  109.0 0.6 copy-done.16
  110.4 0.8 collective-permute-start.26
  111.1 1.0 collective-permute-start.29
  112.1 5.0 %attend.7 = (bf16[128,512]{1,0:T(8,128)(2,1)S(1)}, bf16[128,512]{1,0:T(8,128)(2,1)}, bf16[128,512]{1,0:T(8,128)(2,1)}, bf16[128,512]{1,0:T(8,128)(2,1)}) custom-call(s32[1]{0:T(128)} %bitcast.1.info, bf16[2,640,512]{2,1,0:T(8,128)(2,1)S(1)} %get-tuple-element.74.latent, bf16[2,640,128]{2,1,0:T(8,128)(2,1)S(1)} %get-tuple-element.75.rope_even, ...), custom_call_target="tpu_custom_call" | custom-call | flops 2181038080 | bytes 4194304 | tf_op jit(solution)/shard_map/attend/pallas_call | solution.py:449
  117.1 0.6 copy-done.20
  117.7 0.6 copy-done.18
  118.8 0.6 copy-done.12
  119.4 0.7 collective-permute-start.28
  120.2 0.6 copy-done.14
  120.8 0.7 collective-permute-start.30
  121.5 1.8 %copy.10 = bf16[256,576]{0,1:T(8,128)(2,1)} copy(bf16[256,576]{1,0:T(8,128)(2,1)} %bitcast.6) | data formatting | bytes 589824
  123.4 2.6 %collective-permute-done.28.refs_11_ = bf16[128,512]{1,0:T(8,128)(2,1)S(1)} collective-permute-done((bf16[128,512]{1,0:T(8,128)(2,1)}, bf16[128,512]{1,0:T(8,128)(2,1)S(1)}, u32[]{:S(2)}, u32[]{:S(2)}) %collective-permute-start.28) | collective-permute-done | bytes 131104 | tf_op jit(solution)/shard_map/ppermute | solution.py:297
  126.0 1.1 collective-permute-done.30.refs_15_
  127.1 0.9 copy-done.9
  128.0 0.9 copy-done.11
  128.9 0.9 copy-done.13
  129.8 0.9 copy-done.15
  130.7 0.9 copy-done.17
  131.6 0.9 copy-done.19
  132.5 0.9 copy-done.21
  133.4 9.2 %place.1 = bf16[128,8192]{1,0:T(8,128)(2,1)} custom-call(s32[1]{0:T(128)} %bitcast.info, bf16[128,512]{1,0:T(8,128)(2,1)S(1)} %get-tuple-element.82.refs_0_, bf16[128,512]{1,0:T(8,128)(2,1)S(1)} %copy-done.7, bf16[128,512]{1,0:T(8,128)(2,1)S(1)} %copy-done.17, bf16[128,512]{1,0:T(8,128)(2,1)S(1)} %copy-done.21, bf16[128,512]{1,0:T(8,128)(2,1)S(1)} %copy-done.13, ...), custom_call_target="tpu_custom_call" | custom-call | tf_op jit(solution)/shard_map/place/pallas_call | solution.py:481
  (78 shorter events, 3.1 us)
Async XLA Ops:
  1.6 1.7 %collective-permute-start = (bf16[32,4096]{1,0:T(8,128)(2,1)S(1)}, bf16[32,4096]{1,0:T(8,128)(2,1)S(1)}, u32[]{:S(2)}, u32[]{:S(2)}) collective-permute-start(bf16[32,4096]{1,0:T(8,128)(2,1)S(1)} %constant_dynamic-slice_fusion), channel_id=1, source_target_pairs={{0,1},{1,0},{2,3},{3,2},{4,5},{5,4},{6,7},{7,6},{8,9},{9,8},{10,11... | collective-permute-start | bytes 786440 | tf_op jit(solution)/shard_map/ppermute | solution.py:297
  4.3 23.1 %collective-permute-start.3 = (bf16[64,4096]{1,0:T(8,128)(2,1)S(1)}, bf16[64,4096]{1,0:T(8,128)(2,1)S(1)}, u32[]{:S(2)}, u32[]{:S(2)}) collective-permute-start(bf16[64,4096]{1,0:T(8,128)(2,1)S(1)} %pair.1.refs_0_), channel_id=1, source_target_pairs={{0,4},{1,5},{2,6},{3,7},{4,8},{5,9},{6,10},{7,11},{8,12},{9,13},{1... | collective-permute-start | bytes 1572872 | tf_op jit(solution)/shard_map/ppermute | solution.py:300
  7.3 20.1 %collective-permute-start.4 = (bf16[64,4096]{1,0:T(8,128)(2,1)S(1)}, bf16[64,4096]{1,0:T(8,128)(2,1)S(1)}, u32[]{:S(2)}, u32[]{:S(2)}) collective-permute-start(bf16[64,4096]{1,0:T(8,128)(2,1)S(1)} %pair.1.refs_0_), channel_id=1, source_target_pairs={{0,2},{1,3},{2,0},{3,1},{4,6},{5,7},{6,4},{7,5},{8,10},{9,11},{10,... | collective-permute-start | bytes 1572872 | tf_op jit(solution)/shard_map/ppermute | solution.py:303
  11.1 7.1 %copy-start.27 = (bf16[128,640]{1,0:T(8,128)(2,1)S(1)}, bf16[128,640]{1,0:T(8,128)(2,1)}, u32[]{:S(2)}) copy-start(bf16[128,640]{1,0:T(8,128)(2,1)} %get-tuple-element.61) | copy-start | bytes 491524
  14.5 0.8 copy-start.24
  15.3 0.7 copy-start.25
  16.0 0.7 copy-start.26
  16.7 10.6 %copy-start.22 = (bf16[128,1536]{1,0:T(8,128)(2,1)}, bf16[128,1536]{1,0:T(8,128)(2,1)S(1)}, u32[]{:S(2)}) copy-start(bf16[128,1536]{1,0:T(8,128)(2,1)S(1)} %get-tuple-element.96) | copy-start | bytes 1179652
  16.7 10.6 %copy-start.23 = (bf16[128,1536]{1,0:T(8,128)(2,1)}, bf16[128,1536]{1,0:T(8,128)(2,1)S(1)}, u32[]{:S(2)}) copy-start(bf16[128,1536]{1,0:T(8,128)(2,1)S(1)} %get-tuple-element.94) | copy-start | bytes 1179652
  16.7 10.6 %collective-permute-start.5 = (bf16[128,1536]{1,0:T(8,128)(2,1)S(1)}, bf16[128,1536]{1,0:T(8,128)(2,1)S(1)}, u32[]{:S(2)}, u32[]{:S(2)}) collective-permute-start(bf16[128,1536]{1,0:T(8,128)(2,1)S(1)} %get-tuple-element.65), channel_id=1, source_target_pairs={{0,16},{1,17},{2,18},{3,19},{4,20},{5,21},{6,22},{7,23},{8,24},{9,... | collective-permute-start | bytes 1179656 | tf_op jit(solution)/shard_map/ppermute | solution.py:297
  18.2 5.3 %collective-permute-start.1 = (bf16[128,640]{1,0:T(8,128)(2,1)S(1)}, bf16[128,640]{1,0:T(8,128)(2,1)S(1)}, u32[]{:S(2)}, u32[]{:S(2)}) collective-permute-start(bf16[128,640]{1,0:T(8,128)(2,1)S(1)} %copy-done.27), channel_id=1, source_target_pairs={{0,2},{1,3},{2,4},{3,5},{4,6},{5,7},{6,8},{7,9},{8,10},{9,11},{10,... | collective-permute-start | bytes 491528 | tf_op jit(solution)/shard_map/ppermute | solution.py:309
  20.7 2.9 %collective-permute-start.2 = (bf16[128,640]{1,0:T(8,128)(2,1)S(1)}, bf16[128,640]{1,0:T(8,128)(2,1)S(1)}, u32[]{:S(2)}, u32[]{:S(2)}) collective-permute-start(bf16[128,640]{1,0:T(8,128)(2,1)S(1)} %copy-done.27), channel_id=1, source_target_pairs={{1,5},{3,7},{5,9},{7,11},{9,13},{11,15},{17,21},{19,23},{21,25},{2... | collective-permute-start | bytes 491528 | tf_op jit(solution)/shard_map/ppermute | solution.py:309
  23.5 5.4 %copy-start.28 = (bf16[128,640]{1,0:T(8,128)(2,1)}, bf16[128,640]{1,0:T(8,128)(2,1)S(1)}, u32[]{:S(2)}) copy-start(bf16[128,640]{1,0:T(8,128)(2,1)S(1)} %collective-permute-done.1) | copy-start | bytes 491524
  23.5 5.4 %copy-start.29 = (bf16[128,640]{1,0:T(8,128)(2,1)}, bf16[128,640]{1,0:T(8,128)(2,1)S(1)}, u32[]{:S(2)}) copy-start(bf16[128,640]{1,0:T(8,128)(2,1)S(1)} %collective-permute-done.2) | copy-start | bytes 491524
  27.3 1.6 %copy-start = (bf16[128,1536]{1,0:T(8,128)(2,1)}, bf16[128,1536]{1,0:T(8,128)(2,1)S(1)}, u32[]{:S(2)}) copy-start(bf16[128,1536]{1,0:T(8,128)(2,1)S(1)} %collective-permute-done.5.refs_10_.refs_14_) | copy-start | bytes 1179652
  27.4 14.4 %collective-permute-start.6 = (bf16[384,640]{1,0:T(8,128)(2,1)}, bf16[384,640]{1,0:T(8,128)(2,1)}, u32[]{:S(2)}, u32[]{:S(2)}) collective-permute-start(bf16[384,640]{1,0:T(8,128)(2,1)} %pad_maximum_fusion), channel_id=1, source_target_pairs={{0,16},{1,17},{2,18},{3,19},{4,20},{5,21},{6,22},{7,23},{8,24},{9,... | collective-permute-start | bytes 1474568 | tf_op jit(solution)/shard_map/ppermute | solution.py:297
  28.9 16.3 %all-to-all-start = ((bf16[16,16,576]{2,1,0:T(8,128)(2,1)}), bf16[16,16,576]{2,1,0:T(8,128)(2,1)}, u32[]{:S(2)}, u32[]{:S(2)}) async-start(bf16[16,16,576]{2,1,0:T(8,128)(2,1)} %bitcast.7), calls=%async_computation | async-start | bytes 655360 | tf_op jit(solution)/shard_map/all_to_all | solution.py:383
  33.6 21.4 %collective-permute-start.7 = (bf16[64,4096]{1,0:T(8,128)(2,1)S(1)}, bf16[64,4096]{1,0:T(8,128)(2,1)S(1)}, u32[]{:S(2)}, u32[]{:S(2)}) collective-permute-start(bf16[64,4096]{1,0:T(8,128)(2,1)S(1)} %collective-permute-done.3.refs_1_), channel_id=1, source_target_pairs={{0,4},{1,5},{2,6},{3,7},{4,8},{5,9},{6,10},{7,11},{8,12},{9,13},{1... | collective-permute-start | bytes 1572872 | tf_op jit(solution)/shard_map/ppermute | solution.py:300
  35.5 19.6 %collective-permute-start.8 = (bf16[64,4096]{1,0:T(8,128)(2,1)S(1)}, bf16[64,4096]{1,0:T(8,128)(2,1)S(1)}, u32[]{:S(2)}, u32[]{:S(2)}) collective-permute-start(bf16[64,4096]{1,0:T(8,128)(2,1)S(1)} %collective-permute-done.3.refs_1_), channel_id=1, source_target_pairs={{0,2},{1,3},{2,0},{3,1},{4,6},{5,7},{6,4},{7,5},{8,10},{9,11},{10,... | collective-permute-start | bytes 1572872 | tf_op jit(solution)/shard_map/ppermute | solution.py:303
  36.9 8.3 %collective-permute-start.9 = (bf16[128,1536]{1,0:T(8,128)(2,1)}, bf16[128,1536]{1,0:T(8,128)(2,1)}, u32[]{:S(2)}, u32[]{:S(2)}) collective-permute-start(bf16[128,1536]{1,0:T(8,128)(2,1)} %copy-done.26), channel_id=1, source_target_pairs={{0,1},{1,0},{2,3},{3,2},{4,5},{5,4},{6,7},{7,6},{8,9},{9,8},{10,11... | collective-permute-start | bytes 1179656 | tf_op jit(solution)/shard_map/ppermute | solution.py:297
  45.2 33.9 %copy-start.1 = (bf16[128,1536]{1,0:T(8,128)(2,1)S(1)}, bf16[128,1536]{1,0:T(8,128)(2,1)}, u32[]{:S(2)}) copy-start(bf16[128,1536]{1,0:T(8,128)(2,1)} %copy-done) | copy-start | bytes 1179652
  55.0 16.6 %collective-permute-start.10 = (bf16[768,640]{1,0:T(8,128)(2,1)}, bf16[768,640]{1,0:T(8,128)(2,1)S(1)}, u32[]{:S(2)}, u32[]{:S(2)}) collective-permute-start(bf16[768,640]{1,0:T(8,128)(2,1)} %constant_dynamic-update-slice_fusion.own), channel_id=1, source_target_pairs={{0,1},{1,0},{2,3},{3,2},{4,5},{5,4},{6,7},{7,6},{8,9},{9,8},{10,11... | collective-permute-start | bytes 2949128 | tf_op jit(solution)/shard_map/ppermute | solution.py:297
  55.9 15.7 %collective-permute-start.11 = (bf16[64,4096]{1,0:T(8,128)(2,1)S(1)}, bf16[64,4096]{1,0:T(8,128)(2,1)S(1)}, u32[]{:S(2)}, u32[]{:S(2)}) collective-permute-start(bf16[64,4096]{1,0:T(8,128)(2,1)S(1)} %collective-permute-done.7.refs_2_), channel_id=1, source_target_pairs={{0,4},{1,5},{2,6},{3,7},{4,8},{5,9},{6,10},{7,11},{8,12},{9,13},{1... | collective-permute-start | bytes 1572872 | tf_op jit(solution)/shard_map/ppermute | solution.py:300
  57.1 14.5 %collective-permute-start.12 = (bf16[64,4096]{1,0:T(8,128)(2,1)S(1)}, bf16[64,4096]{1,0:T(8,128)(2,1)S(1)}, u32[]{:S(2)}, u32[]{:S(2)}) collective-permute-start(bf16[64,4096]{1,0:T(8,128)(2,1)S(1)} %collective-permute-done.7.refs_2_), channel_id=1, source_target_pairs={{0,2},{1,3},{2,0},{3,1},{4,6},{5,7},{6,4},{7,5},{8,10},{9,11},{10,... | collective-permute-start | bytes 1572872 | tf_op jit(solution)/shard_map/ppermute | solution.py:303
  57.9 13.7 %collective-permute-start.13 = (bf16[128,1536]{1,0:T(8,128)(2,1)}, bf16[128,1536]{1,0:T(8,128)(2,1)S(1)}, u32[]{:S(2)}, u32[]{:S(2)}) collective-permute-start(bf16[128,1536]{1,0:T(8,128)(2,1)} %copy-done.25), channel_id=1, source_target_pairs={{0,17},{1,16},{2,19},{3,18},{4,21},{5,20},{6,23},{7,22},{8,25},{9,... | collective-permute-start | bytes 1179656 | tf_op jit(solution)/shard_map/ppermute | solution.py:297
  71.6 7.5 %collective-permute-start.14 = (bf16[64,2048]{1,0:T(8,128)(2,1)S(1)}, bf16[64,2048]{1,0:T(8,128)(2,1)S(1)}, u32[]{:S(2)}, u32[]{:S(2)}) collective-permute-start(bf16[64,2048]{1,0:T(8,128)(2,1)S(1)} %slice.8), channel_id=1, source_target_pairs={{0,2},{1,3},{2,0},{3,1},{4,6},{5,7},{6,4},{7,5},{8,10},{9,11},{10,... | collective-permute-start | bytes 786440 | tf_op jit(solution)/shard_map/ppermute | solution.py:303
  72.7 30.9 %collective-permute-start.18 = (bf16[128,1536]{1,0:T(8,128)(2,1)}, bf16[128,1536]{1,0:T(8,128)(2,1)S(1)}, u32[]{:S(2)}, u32[]{:S(2)}) collective-permute-start(bf16[128,1536]{1,0:T(8,128)(2,1)} %copy-done.24), channel_id=1, source_target_pairs={{0,1},{1,0},{2,3},{3,2},{4,5},{5,4},{6,7},{7,6},{8,9},{9,8},{10,11... | collective-permute-start | bytes 1179656 | tf_op jit(solution)/shard_map/ppermute | solution.py:297
  72.7 30.9 %collective-permute-start.19 = (bf16[128,1536]{1,0:T(8,128)(2,1)}, bf16[128,1536]{1,0:T(8,128)(2,1)S(1)}, u32[]{:S(2)}, u32[]{:S(2)}) collective-permute-start(bf16[128,1536]{1,0:T(8,128)(2,1)} %copy-done.23), channel_id=1, source_target_pairs={{0,16},{1,17},{2,18},{3,19},{4,20},{5,21},{6,22},{7,23},{8,24},{9,... | collective-permute-start | bytes 1179656 | tf_op jit(solution)/shard_map/ppermute | solution.py:297
  74.1 30.0 %collective-permute-start.20 = (bf16[128,1536]{1,0:T(8,128)(2,1)}, bf16[128,1536]{1,0:T(8,128)(2,1)S(1)}, u32[]{:S(2)}, u32[]{:S(2)}) collective-permute-start(bf16[128,1536]{1,0:T(8,128)(2,1)} %copy-done.22), channel_id=1, source_target_pairs={{0,17},{1,16},{2,19},{3,18},{4,21},{5,20},{6,23},{7,22},{8,25},{9,... | collective-permute-start | bytes 1179656 | tf_op jit(solution)/shard_map/ppermute | solution.py:297
  84.1 11.6 %collective-permute-start.15 = (bf16[128,512]{1,0:T(8,128)(2,1)S(1)}, bf16[128,512]{1,0:T(8,128)(2,1)S(1)}, u32[]{:S(2)}, u32[]{:S(2)}) collective-permute-start(bf16[128,512]{1,0:T(8,128)(2,1)S(1)} %get-tuple-element.86), channel_id=1, source_target_pairs={{0,16},{1,17},{2,18},{3,19},{4,20},{5,21},{6,22},{7,23},{8,24},{9,... | collective-permute-start | bytes 393224 | tf_op jit(solution)/shard_map/ppermute | solution.py:297
  85.6 17.2 %collective-permute-start.17 = (bf16[64,2048]{1,0:T(8,128)(2,1)S(1)}, bf16[64,2048]{1,0:T(8,128)(2,1)S(1)}, u32[]{:S(2)}, u32[]{:S(2)}) collective-permute-start(bf16[64,2048]{1,0:T(8,128)(2,1)S(1)} %slice.9), channel_id=1, source_target_pairs={{0,4},{1,5},{2,6},{3,7},{4,8},{5,9},{6,10},{7,11},{8,12},{9,13},{1... | collective-permute-start | bytes 786440 | tf_op jit(solution)/shard_map/ppermute | solution.py:300
  95.7 5.7 %copy-start.2 = (bf16[128,512]{1,0:T(8,128)(2,1)}, bf16[128,512]{1,0:T(8,128)(2,1)S(1)}, u32[]{:S(2)}) copy-start(bf16[128,512]{1,0:T(8,128)(2,1)S(1)} %collective-permute-done.15.refs_8_) | copy-start | bytes 393220
  95.7 5.8 %collective-permute-start.16 = (bf16[128,512]{1,0:T(8,128)(2,1)S(1)}, bf16[128,512]{1,0:T(8,128)(2,1)S(1)}, u32[]{:S(2)}, u32[]{:S(2)}) collective-permute-start(bf16[128,512]{1,0:T(8,128)(2,1)S(1)} %get-tuple-element.87), channel_id=1, source_target_pairs={{0,17},{1,16},{2,19},{3,18},{4,21},{5,20},{6,23},{7,22},{8,25},{9,... | collective-permute-start | bytes 393224 | tf_op jit(solution)/shard_map/ppermute | solution.py:297
  101.4 7.7 %copy-start.6 = (bf16[128,512]{1,0:T(8,128)(2,1)}, bf16[128,512]{1,0:T(8,128)(2,1)S(1)}, u32[]{:S(2)}) copy-start(bf16[128,512]{1,0:T(8,128)(2,1)S(1)} %get-tuple-element.84.refs_1_) | copy-start | bytes 393220
  101.4 7.6 %copy-start.4 = (bf16[128,512]{1,0:T(8,128)(2,1)}, bf16[128,512]{1,0:T(8,128)(2,1)S(1)}, u32[]{:S(2)}) copy-start(bf16[128,512]{1,0:T(8,128)(2,1)S(1)} %collective-permute-done.16.refs_12_) | copy-start | bytes 393220
  101.4 8.2 %collective-permute-start.21 = (bf16[128,512]{1,0:T(8,128)(2,1)S(1)}, bf16[128,512]{1,0:T(8,128)(2,1)S(1)}, u32[]{:S(2)}, u32[]{:S(2)}) collective-permute-start(bf16[128,512]{1,0:T(8,128)(2,1)S(1)} %get-tuple-element.99), channel_id=1, source_target_pairs={{0,16},{1,17},{2,18},{3,19},{4,20},{5,21},{6,22},{7,23},{8,24},{9,... | collective-permute-start | bytes 393224 | tf_op jit(solution)/shard_map/ppermute | solution.py:297
  102.8 7.4 %collective-permute-start.22 = (bf16[128,512]{1,0:T(8,128)(2,1)S(1)}, bf16[128,512]{1,0:T(8,128)(2,1)S(1)}, u32[]{:S(2)}, u32[]{:S(2)}) collective-permute-start(bf16[128,512]{1,0:T(8,128)(2,1)S(1)} %get-tuple-element.100), channel_id=1, source_target_pairs={{0,17},{1,16},{2,19},{3,18},{4,21},{5,20},{6,23},{7,22},{8,25},{9,... | collective-permute-start | bytes 393224 | tf_op jit(solution)/shard_map/ppermute | solution.py:297
  103.6 15.2 %collective-permute-start.23 = (bf16[128,512]{1,0:T(8,128)(2,1)S(1)}, bf16[128,512]{1,0:T(8,128)(2,1)S(1)}, u32[]{:S(2)}, u32[]{:S(2)}) collective-permute-start(bf16[128,512]{1,0:T(8,128)(2,1)S(1)} %get-tuple-element.103), channel_id=1, source_target_pairs={{0,1},{1,0},{2,3},{3,2},{4,5},{5,4},{6,7},{7,6},{8,9},{9,8},{10,11... | collective-permute-start | bytes 393224 | tf_op jit(solution)/shard_map/ppermute | solution.py:297
  103.6 16.6 %collective-permute-start.24 = (bf16[128,512]{1,0:T(8,128)(2,1)S(1)}, bf16[128,512]{1,0:T(8,128)(2,1)S(1)}, u32[]{:S(2)}, u32[]{:S(2)}) collective-permute-start(bf16[128,512]{1,0:T(8,128)(2,1)S(1)} %get-tuple-element.104), channel_id=1, source_target_pairs={{0,1},{1,0},{2,3},{3,2},{4,5},{5,4},{6,7},{7,6},{8,9},{9,8},{10,11... | collective-permute-start | bytes 393224 | tf_op jit(solution)/shard_map/ppermute | solution.py:297
  109.0 0.6 copy-start.16
  109.7 7.4 %copy-start.8 = (bf16[128,512]{1,0:T(8,128)(2,1)}, bf16[128,512]{1,0:T(8,128)(2,1)S(1)}, u32[]{:S(2)}) copy-start(bf16[128,512]{1,0:T(8,128)(2,1)S(1)} %collective-permute-done.21.refs_9_) | copy-start | bytes 393220
  110.2 6.8 %copy-start.10 = (bf16[128,512]{1,0:T(8,128)(2,1)}, bf16[128,512]{1,0:T(8,128)(2,1)S(1)}, u32[]{:S(2)}) copy-start(bf16[128,512]{1,0:T(8,128)(2,1)S(1)} %collective-permute-done.22.refs_13_) | copy-start | bytes 393220
  110.2 13.1 %collective-permute-start.25 = (bf16[128,512]{1,0:T(8,128)(2,1)}, bf16[128,512]{1,0:T(8,128)(2,1)}, u32[]{:S(2)}, u32[]{:S(2)}) collective-permute-start(bf16[128,512]{1,0:T(8,128)(2,1)} %get-tuple-element.105), channel_id=1, source_target_pairs={{0,1},{1,0},{2,3},{3,2},{4,5},{5,4},{6,7},{7,6},{8,9},{9,8},{10,11... | collective-permute-start | bytes 393224 | tf_op jit(solution)/shard_map/ppermute | solution.py:297
  110.4 7.4 %collective-permute-start.26 = (bf16[128,512]{1,0:T(8,128)(2,1)S(1)}, bf16[128,512]{1,0:T(8,128)(2,1)S(1)}, u32[]{:S(2)}, u32[]{:S(2)}) collective-permute-start(bf16[128,512]{1,0:T(8,128)(2,1)S(1)} %get-tuple-element.107), channel_id=1, source_target_pairs={{0,16},{1,17},{2,18},{3,19},{4,20},{5,21},{6,22},{7,23},{8,24},{9,... | collective-permute-start | bytes 393224 | tf_op jit(solution)/shard_map/ppermute | solution.py:297
  111.1 15.9 %copy-start.3 = (bf16[128,512]{1,0:T(8,128)(2,1)S(1)}, bf16[128,512]{1,0:T(8,128)(2,1)}, u32[]{:S(2)}) copy-start(bf16[128,512]{1,0:T(8,128)(2,1)} %copy-done.2) | copy-start | bytes 393220
  111.1 15.9 %copy-start.5 = (bf16[128,512]{1,0:T(8,128)(2,1)S(1)}, bf16[128,512]{1,0:T(8,128)(2,1)}, u32[]{:S(2)}) copy-start(bf16[128,512]{1,0:T(8,128)(2,1)} %copy-done.4) | copy-start | bytes 393220
  111.1 15.9 %copy-start.7 = (bf16[128,512]{1,0:T(8,128)(2,1)S(1)}, bf16[128,512]{1,0:T(8,128)(2,1)}, u32[]{:S(2)}) copy-start(bf16[128,512]{1,0:T(8,128)(2,1)} %copy-done.6) | copy-start | bytes 393220
  111.1 12.2 %collective-permute-start.29 = (bf16[128,512]{1,0:T(8,128)(2,1)}, bf16[128,512]{1,0:T(8,128)(2,1)}, u32[]{:S(2)}, u32[]{:S(2)}) collective-permute-start(bf16[128,512]{1,0:T(8,128)(2,1)} %get-tuple-element.111), channel_id=1, source_target_pairs={{0,17},{1,16},{2,19},{3,18},{4,21},{5,20},{6,23},{7,22},{8,25},{9,... | collective-permute-start | bytes 393224 | tf_op jit(solution)/shard_map/ppermute | solution.py:297
  117.1 0.7 copy-start.20
  117.7 0.6 copy-start.18
  118.4 5.0 %collective-permute-start.27 = (bf16[128,512]{1,0:T(8,128)(2,1)}, bf16[128,512]{1,0:T(8,128)(2,1)S(1)}, u32[]{:S(2)}, u32[]{:S(2)}) collective-permute-start(bf16[128,512]{1,0:T(8,128)(2,1)} %get-tuple-element.108), channel_id=1, source_target_pairs={{0,1},{1,0},{2,3},{3,2},{4,5},{5,4},{6,7},{7,6},{8,9},{9,8},{10,11... | collective-permute-start | bytes 393224 | tf_op jit(solution)/shard_map/ppermute | solution.py:297
  118.8 0.6 copy-start.12
  119.4 6.6 %collective-permute-start.28 = (bf16[128,512]{1,0:T(8,128)(2,1)}, bf16[128,512]{1,0:T(8,128)(2,1)S(1)}, u32[]{:S(2)}, u32[]{:S(2)}) collective-permute-start(bf16[128,512]{1,0:T(8,128)(2,1)} %get-tuple-element.110), channel_id=1, source_target_pairs={{0,16},{1,17},{2,18},{3,19},{4,20},{5,21},{6,22},{7,23},{8,24},{9,... | collective-permute-start | bytes 393224 | tf_op jit(solution)/shard_map/ppermute | solution.py:297
  120.2 0.7 copy-start.14
  120.8 6.2 %collective-permute-start.30 = (bf16[128,512]{1,0:T(8,128)(2,1)}, bf16[128,512]{1,0:T(8,128)(2,1)S(1)}, u32[]{:S(2)}, u32[]{:S(2)}) collective-permute-start(bf16[128,512]{1,0:T(8,128)(2,1)} %get-tuple-element.113), channel_id=1, source_target_pairs={{0,17},{1,16},{2,19},{3,18},{4,21},{5,20},{6,23},{7,22},{8,25},{9,... | collective-permute-start | bytes 393224 | tf_op jit(solution)/shard_map/ppermute | solution.py:297
  127.1 0.9 copy-start.9
  128.0 0.9 copy-start.11
  128.9 0.9 copy-start.13
  129.8 0.9 copy-start.15
  130.7 0.9 copy-start.17
  131.6 0.9 copy-start.19
  132.5 0.9 copy-start.21

commit v10 on v8

--- a/solution.py
+++ b/solution.py
@@ -21,8 +21,8 @@
 PHASES = (
     ("z", "y0", "b~", "f~", "q02"),
     ("z", "y1", "k", "q01"),
-    ("z", "y2", "p", "q03", "q12~"),
-    ("y3", "w", "q13~", "q11"),
+    ("z", "y2", "p", "q03"),
+    ("y3", "w", "q12~", "q13~", "q11"),
 )
 CHUNKS = len(CHUNK_HEADS)
 FIRST_HEAD = tuple(sum(CHUNK_HEADS[:j]) for j in range(CHUNKS))
@@ -464,19 +464,17 @@
 
     results = []
     for call in CALLS:
-        sent = [piece for one in results for piece in one[1:]]
         last = len(results) + 1 == len(CALLS)
         mine_info = tie(mine_info, *(results[0][2:3] if last else []))
         pieces = attend(*call)
         mine_info = tie(mine_info, pieces[0])
-        before = sent[:-1] if last else []
+        before = [piece for one in results for piece in one[1:]] if last else []
         results.append(
             [pieces[0]] + [quad_swap(tie(pieces[r], *before), r) for r in range(1, QUAD)]
         )
     pieces = [one[r] for r in range(QUAD) for one in results]
-    sent = [piece for one in results for piece in one[1:]]
     arrived = lax.all_to_all(
-        tie(outgoing, *sent).reshape(size, slot_count, ROW),
+        tie(outgoing, results[-1][0], *before).reshape(size, slot_count, ROW),
         "ctx",
         split_axis=0,
         concat_axis=0,

time: 119 us -> 114 us (0.958)
  waiting for transfers between devices: 60.2 us -> 51.6 us
  starting transfers between devices: 29.4 us -> 32.2 us
    all_to_all x1, waiting for transfers between devices: 9.64 us -> 1.68 us  [body(): lax.all_to_all(tie(outgoing, results[-1][0], *before).reshape(size, slot_...]
    ppermute x4, starting transfers between devices: 3.37 us -> 6.65 us  [around(): lax.ppermute(array, 'ctx', [(i, (i + by) % size) for i in range(size)])]
    ppermute x18, waiting for transfers between devices: 23.7 us -> 25.6 us  [quad_swap(): return lax.ppermute(array, ('groups', 'ctx'), pairs)]
    ppermute x4, waiting for transfers between devices: 5.46 us -> 3.67 us  [inner_swap(): return lax.ppermute(array, 'ctx', [(i, i ^ 2) for i in range(size)])]
    ppermute x4, waiting for transfers between devices: 17.7 us -> 16.3 us  [around(): lax.ppermute(array, 'ctx', [(i, (i + by) % size) for i in range(size)])]
    ppermute x18, starting transfers between devices: 12.4 us -> 11.1 us  [quad_swap(): return lax.ppermute(array, ('groups', 'ctx'), pairs)]
    all_to_all x1, starting transfers between devices: 3.54 us -> 4.81 us  [body(): lax.all_to_all(tie(outgoing, results[-1][0], *before).reshape(size, slot_...]
  transfers between devices with their start and end apart: 29 -> 29, of which waited for: 14 -> 16; matrix products, arithmetic and copies ran while one was open for 0% -> 0% of each run, Pallas kernels for 21% -> 23%
where the time goes in v10:
time: 114 us; the launch traced here: 113 us
  waiting for transfers between devices  51.6 us (45%)
  starting transfers between devices  32.2 us (28%)
  Pallas kernels  26.6 us (23%)
  local copies, waits for them, and re-layouts  2.01 us (2%)
    ppermute x18, waiting for transfers between devices, quad_swap(): return lax.ppermute(array, ('groups', 'ctx'), pairs)  25.6 us
    pallas_call x3, Pallas kernels, attend(): pl.pallas_call(functools.partial(attend_kernel, outer), grid=(steps,), ou...  17.9 us
    ppermute x4, waiting for transfers between devices, around(): lax.ppermute(array, 'ctx', [(i, (i + by) % size) for i in range(size)])  16.3 us
    ppermute x18, starting transfers between devices, quad_swap(): return lax.ppermute(array, ('groups', 'ctx'), pairs)  11.1 us
    ppermute x4, starting transfers between devices, around(): lax.ppermute(array, 'ctx', [(i, (i + by) % size) for i in range(size)])  6.65 us
    ppermute x4, starting transfers between devices, inner_swap(): return lax.ppermute(array, 'ctx', [(i, i ^ 2) for i in range(size)])  6.53 us
    all_to_all x1, starting transfers between devices, body(): lax.all_to_all(tie(outgoing, results[-1][0], *before).reshape(size, slot_...  4.81 us
    ppermute x2, waiting for transfers between devices, from_behind(): return lax.ppermute(array, 'ctx', pairs)  4.38 us
  transfers between devices with their start and end apart: 29, of which 16 were waited for; matrix products, arithmetic and copies ran while one was open for 0% of the time, Pallas kernels for 23%

profile of v10, /device:TPU:0, one launch (start us, length us, event | category | flops | bytes accessed | tf_op | source)
XLA Modules:
  0.0 113.3 jit_solution(17393203239644193320)
XLA Ops:
  0.6 1.0 constant_dynamic-slice_fusion
  1.6 0.5 collective-permute-start
  2.1 1.2 %collective-permute-done.got = bf16[32,4096]{1,0:T(8,128)(2,1)S(1)} collective-permute-done((bf16[32,4096]{1,0:T(8,128)(2,1)S(1)}, bf16[32,4096]{1,0:T(8,128)(2,1)S(1)}, u32[]{:S(2)}, u32[]{:S(2)}) %collective-permute-start) | collective-permute-done | bytes 262176 | tf_op jit(solution)/shard_map/ppermute | solution.py:297
  3.3 1.0 pair.1.refs_0_
  4.3 3.0 %collective-permute-start.3 = (bf16[64,4096]{1,0:T(8,128)(2,1)S(1)}, bf16[64,4096]{1,0:T(8,128)(2,1)S(1)}, u32[]{:S(2)}, u32[]{:S(2)}) collective-permute-start(bf16[64,4096]{1,0:T(8,128)(2,1)S(1)} %pair.1.refs_0_), channel_id=1, source_target_pairs={{0,4},{1,5},{2,6},{3,7},{4,8},{5,9},{6,10},{7,11},{8,12},{9,13},{1... | collective-permute-start | bytes 1572872 | tf_op jit(solution)/shard_map/ppermute | solution.py:300
  7.3 1.5 %collective-permute-start.4 = (bf16[64,4096]{1,0:T(8,128)(2,1)S(1)}, bf16[64,4096]{1,0:T(8,128)(2,1)S(1)}, u32[]{:S(2)}, u32[]{:S(2)}) collective-permute-start(bf16[64,4096]{1,0:T(8,128)(2,1)S(1)} %pair.1.refs_0_), channel_id=1, source_target_pairs={{0,2},{1,3},{2,0},{3,1},{4,6},{5,7},{6,4},{7,5},{8,10},{9,11},{10,... | collective-permute-start | bytes 1572872 | tf_op jit(solution)/shard_map/ppermute | solution.py:303
  8.8 2.3 %rows.1 = (bf16[128,640]{1,0:T(8,128)(2,1)}, f32[128,128]{1,0:T(8,128)}, f32[128,128]{1,0:T(8,128)}, bf16[256,576]{1,0:T(8,128)(2,1)}) custom-call(s32[1]{0:T(128)} %bitcast.1.info, s32[8]{0:T(128)} %lengths, bf16[576,128]{1,0:T(8,128)(2,1)} %bitcast.8, f32[1,512]{1,0:T(1,128)} %bitcast.9, s32[1,128]{1,0:T(1,128)} %bitcast.10, f32[1,128]{1,0:T(1,128)} %constant.30.clone.freq), custom_call_target="tpu_custom_call" | custom-call | tf_op jit(solution)/shard_map/rows/pallas_call | solution.py:344
  11.1 3.4 %queries.1 = (bf16[128,1536]{1,0:T(8,128)(2,1)S(1)}, bf16[128,1536]{1,0:T(8,128)(2,1)S(1)}, bf16[128,1536]{1,0:T(8,128)(2,1)S(1)}, bf16[128,1536]{1,0:T(8,128)(2...) custom-call(s32[1]{0:T(128)} %bitcast.info, ...), custom_call_target="tpu_custom_call" | custom-call | bytes 6291456 | tf_op jit(solution)/shard_map/queries/pallas_call | solution.py:368
  14.5 1.6 %collective-permute-start.5 = (bf16[128,1536]{1,0:T(8,128)(2,1)S(1)}, bf16[128,1536]{1,0:T(8,128)(2,1)S(1)}, u32[]{:S(2)}, u32[]{:S(2)}) collective-permute-start(bf16[128,1536]{1,0:T(8,128)(2,1)S(1)} %get-tuple-element.59), channel_id=1, source_target_pairs={{0,16},{1,17},{2,18},{3,19},{4,20},{5,21},{6,22},{7,23},{8,24},{9,... | collective-permute-start | bytes 1179656 | tf_op jit(solution)/shard_map/ppermute | solution.py:297
  16.0 2.4 %collective-permute-start.1 = (bf16[128,640]{1,0:T(8,128)(2,1)S(1)}, bf16[128,640]{1,0:T(8,128)(2,1)S(1)}, u32[]{:S(2)}, u32[]{:S(2)}) collective-permute-start(bf16[128,640]{1,0:T(8,128)(2,1)S(1)} %copy-done), channel_id=1, source_target_pairs={{0,2},{1,3},{2,4},{3,5},{4,6},{5,7},{6,8},{7,9},{8,10},{9,11},{10,... | collective-permute-start | bytes 491528 | tf_op jit(solution)/shard_map/ppermute | solution.py:309
  18.5 0.7 collective-permute-start.2
  19.1 4.4 %collective-permute-done.1 = bf16[128,640]{1,0:T(8,128)(2,1)S(1)} collective-permute-done((bf16[128,640]{1,0:T(8,128)(2,1)S(1)}, bf16[128,640]{1,0:T(8,128)(2,1)S(1)}, u32[]{:S(2)}, u32[]{:S(2)}) %collective-permute-start.1) | collective-permute-done | bytes 163872 | tf_op jit(solution)/shard_map/ppermute | solution.py:309
  23.6 1.6 %collective-permute-done.5.refs_10_.refs_14_ = bf16[128,1536]{1,0:T(8,128)(2,1)S(1)} collective-permute-done((bf16[128,1536]{1,0:T(8,128)(2,1)S(1)}, bf16[128,1536]{1,0:T(8,128)(2,1)S(1)}, u32[]{:S(2)}, u32[]{:S(2)}) %collective-permute-start.5) | collective-permute-done | bytes 393248 | tf_op jit(solution)/shard_map/ppermute | solution.py:297
  25.1 0.0 collective-permute-done.3.refs_1_
  25.1 0.0 collective-permute-done.4.refs_4_
  25.2 1.5 %collective-permute-start.6 = (bf16[384,640]{1,0:T(8,128)(2,1)S(1)}, bf16[384,640]{1,0:T(8,128)(2,1)S(1)}, u32[]{:S(2)}, u32[]{:S(2)}) collective-permute-start(bf16[384,640]{1,0:T(8,128)(2,1)S(1)} %pad_maximum_fusion), channel_id=1, source_target_pairs={{0,16},{1,17},{2,18},{3,19},{4,20},{5,21},{6,22},{7,23},{8,24},{9,... | collective-permute-start | bytes 1474568 | tf_op jit(solution)/shard_map/ppermute | solution.py:297
  26.6 1.6 %collective-permute-start.7 = (bf16[64,4096]{1,0:T(8,128)(2,1)S(1)}, bf16[64,4096]{1,0:T(8,128)(2,1)S(1)}, u32[]{:S(2)}, u32[]{:S(2)}) collective-permute-start(bf16[64,4096]{1,0:T(8,128)(2,1)S(1)} %collective-permute-done.3.refs_1_), channel_id=1, source_target_pairs={{0,4},{1,5},{2,6},{3,7},{4,8},{5,9},{6,10},{7,11},{8,12},{9,13},{1... | collective-permute-start | bytes 1572872 | tf_op jit(solution)/shard_map/ppermute | solution.py:300
  28.3 0.9 collective-permute-start.8
  29.2 0.0 collective-permute-start.9
  29.3 7.7 %collective-permute-done.6 = bf16[384,640]{1,0:T(8,128)(2,1)S(1)} collective-permute-done((bf16[384,640]{1,0:T(8,128)(2,1)S(1)}, bf16[384,640]{1,0:T(8,128)(2,1)S(1)}, u32[]{:S(2)}, u32[]{:S(2)}) %collective-permute-start.6) | collective-permute-done | bytes 491552 | tf_op jit(solution)/shard_map/ppermute | solution.py:297
  36.9 0.1 constant_dynamic-update-slice_fusion.own
  37.0 3.6 %collective-permute-done.7.refs_2_ = bf16[64,4096]{1,0:T(8,128)(2,1)S(1)} collective-permute-done((bf16[64,4096]{1,0:T(8,128)(2,1)S(1)}, bf16[64,4096]{1,0:T(8,128)(2,1)S(1)}, u32[]{:S(2)}, u32[]{:S(2)}) %collective-permute-start.7) | collective-permute-done | bytes 524320 | tf_op jit(solution)/shard_map/ppermute | solution.py:300
  40.7 0.4 collective-permute-done.8.refs_5_
  41.1 1.6 %collective-permute-start.11 = (bf16[64,4096]{1,0:T(8,128)(2,1)S(1)}, bf16[64,4096]{1,0:T(8,128)(2,1)S(1)}, u32[]{:S(2)}, u32[]{:S(2)}) collective-permute-start(bf16[64,4096]{1,0:T(8,128)(2,1)S(1)} %collective-permute-done.7.refs_2_), channel_id=1, source_target_pairs={{0,4},{1,5},{2,6},{3,7},{4,8},{5,9},{6,10},{7,11},{8,12},{9,13},{1... | collective-permute-start | bytes 1572872 | tf_op jit(solution)/shard_map/ppermute | solution.py:300
  42.6 1.7 %collective-permute-start.12 = (bf16[64,4096]{1,0:T(8,128)(2,1)S(1)}, bf16[64,4096]{1,0:T(8,128)(2,1)S(1)}, u32[]{:S(2)}, u32[]{:S(2)}) collective-permute-start(bf16[64,4096]{1,0:T(8,128)(2,1)S(1)} %collective-permute-done.7.refs_2_), channel_id=1, source_target_pairs={{0,2},{1,3},{2,0},{3,1},{4,6},{5,7},{6,4},{7,5},{8,10},{9,11},{10,... | collective-permute-start | bytes 1572872 | tf_op jit(solution)/shard_map/ppermute | solution.py:303
  44.4 0.2 collective-permute-start.13
  44.6 12.6 %collective-permute-done.11.refs_3_ = bf16[64,4096]{1,0:T(8,128)(2,1)S(1)} collective-permute-done((bf16[64,4096]{1,0:T(8,128)(2,1)S(1)}, bf16[64,4096]{1,0:T(8,128)(2,1)S(1)}, u32[]{:S(2)}, u32[]{:S(2)}) %collective-permute-start.11) | collective-permute-done | bytes 524320 | tf_op jit(solution)/shard_map/ppermute | solution.py:300
  57.2 0.0 collective-permute-done.13.refs_11_.refs_15_
  57.2 0.0 collective-permute-done.10.other
  57.2 2.3 %collective-permute-start.14 = (bf16[64,2048]{1,0:T(8,128)(2,1)S(1)}, bf16[64,2048]{1,0:T(8,128)(2,1)S(1)}, u32[]{:S(2)}, u32[]{:S(2)}) collective-permute-start(bf16[64,2048]{1,0:T(8,128)(2,1)S(1)} %slice.8), channel_id=1, source_target_pairs={{0,2},{1,3},{2,0},{3,1},{4,6},{5,7},{6,4},{7,5},{8,10},{9,11},{10,... | collective-permute-start | bytes 786440 | tf_op jit(solution)/shard_map/ppermute | solution.py:303
  59.6 0.4 collective-permute-start.15
  60.1 0.5 collective-permute-start.17
  60.6 1.3 %collective-permute-start.18 = (bf16[128,1536]{1,0:T(8,128)(2,1)S(1)}, bf16[128,1536]{1,0:T(8,128)(2,1)S(1)}, u32[]{:S(2)}, u32[]{:S(2)}) collective-permute-start(bf16[128,1536]{1,0:T(8,128)(2,1)S(1)} %get-tuple-element.83), channel_id=1, source_target_pairs={{0,17},{1,16},{2,19},{3,18},{4,21},{5,20},{6,23},{7,22},{8,25},{9,... | collective-permute-start | bytes 1179656 | tf_op jit(solution)/shard_map/ppermute | solution.py:297
  61.9 0.6 keys.1
  62.5 3.3 %collective-permute-done.14.refs_7_ = bf16[64,2048]{1,0:T(8,128)(2,1)S(1)} collective-permute-done((bf16[64,2048]{1,0:T(8,128)(2,1)S(1)}, bf16[64,2048]{1,0:T(8,128)(2,1)S(1)}, u32[]{:S(2)}, u32[]{:S(2)}) %collective-permute-start.14) | collective-permute-done | bytes 262176 | tf_op jit(solution)/shard_map/ppermute | solution.py:303
  65.8 9.0 %attend.3 = (bf16[128,1024]{1,0:T(8,128)(2,1)S(1)}, bf16[128,1024]{1,0:T(8,128)(2,1)S(1)}, bf16[128,1024]{1,0:T(8,128)(2,1)S(1)}, bf16[128,1024]{1,0:T(8,128)(2,1)S(1)}) custom-call(s32[1]{0:T(128)} %bitcast.1.info, bf16[2,640,512]{2,1,0:T(8,128)(2,1)S(1)} %get-tuple-element.66.latent, bf16[2,640,128]{2,1,0:T(8,128)(2,1)S(1)} %get-tuple-element.67.rope_even, ...), custom_call_target="tpu_custom_call" | custom-call | flops 4362076160 | bytes 8388608 | tf_op jit(solution)/shard_map/attend/pallas_call | solution.py:443
  74.7 0.6 collective-permute-start.19
  75.3 0.0 collective-permute-done.15.refs_7_
  75.3 0.0 collective-permute-start.20
  75.3 0.0 collective-permute-done.16.refs_9_.refs_13_
  75.3 1.6 %collective-permute-start.22 = (bf16[128,1024]{1,0:T(8,128)(2,1)S(1)}, bf16[128,1024]{1,0:T(8,128)(2,1)S(1)}, u32[]{:S(2)}, u32[]{:S(2)}) collective-permute-start(bf16[128,1024]{1,0:T(8,128)(2,1)S(1)} %get-tuple-element.92), channel_id=1, source_target_pairs={{0,17},{1,16},{2,19},{3,18},{4,21},{5,20},{6,23},{7,22},{8,25},{9,... | collective-permute-start | bytes 786440 | tf_op jit(solution)/shard_map/ppermute | solution.py:297
  76.9 0.0 collective-permute-done.17.refs_10_.refs_14_
  77.0 2.7 %collective-permute-done.18.refs_11_.refs_15_ = bf16[128,1536]{1,0:T(8,128)(2,1)S(1)} collective-permute-done((bf16[128,1536]{1,0:T(8,128)(2,1)S(1)}, bf16[128,1536]{1,0:T(8,128)(2,1)S(1)}, u32[]{:S(2)}, u32[]{:S(2)}) %collective-permute-start.18) | collective-permute-done | bytes 393248 | tf_op jit(solution)/shard_map/ppermute | solution.py:297
  79.6 4.5 %attend.4 = (bf16[128,512]{1,0:T(8,128)(2,1)S(1)}, bf16[128,512]{1,0:T(8,128)(2,1)S(1)}, bf16[128,512]{1,0:T(8,128)(2,1)S(1)}, bf16[128,512]{1,0:T(8,128)(2,1)S(1)}) custom-call(s32[1]{0:T(128)} %bitcast.1.info, bf16[2,640,512]{2,1,0:T(8,128)(2,1)S(1)} %get-tuple-element.66.latent, bf16[2,640,128]{2,1,0:T(8,128)(2,1)S(1)} %get-tuple-element.67.rope_even, ...), custom_call_target="tpu_custom_call" | custom-call | flops 2181038080 | bytes 4194304 | tf_op jit(solution)/shard_map/attend/pallas_call | solution.py:443
  84.1 0.7 collective-permute-start.21
  84.8 0.5 collective-permute-start.23
  85.3 0.7 collective-permute-done.19.refs_6_
  86.0 0.2 collective-permute-start.24
  86.2 4.5 %attend.5 = (bf16[128,512]{1,0:T(8,128)(2,1)S(1)}, bf16[128,512]{1,0:T(8,128)(2,1)S(1)}, bf16[128,512]{1,0:T(8,128)(2,1)S(1)}, bf16[128,512]{1,0:T(8,128)(2,1)S(1)}) custom-call(s32[1]{0:T(128)} %bitcast.1.info, bf16[2,640,512]{2,1,0:T(8,128)(2,1)S(1)} %get-tuple-element.66.latent, bf16[2,640,128]{2,1,0:T(8,128)(2,1)S(1)} %get-tuple-element.67.rope_even, ...), custom_call_target="tpu_custom_call" | custom-call | flops 2181038080 | bytes 4194304 | tf_op jit(solution)/shard_map/attend/pallas_call | solution.py:443
  90.7 0.0 collective-permute-done.20.refs_3_
  90.7 0.1 collective-permute-done.22.refs_9_
  90.9 0.0 collective-permute-done.21.refs_4_
  90.9 3.6 %collective-permute-done.23.refs_7_ = bf16[128,512]{1,0:T(8,128)(2,1)S(1)} collective-permute-done((bf16[128,512]{1,0:T(8,128)(2,1)S(1)}, bf16[128,512]{1,0:T(8,128)(2,1)S(1)}, u32[]{:S(2)}, u32[]{:S(2)}) %collective-permute-start.23) | collective-permute-done | bytes 131104 | tf_op jit(solution)/shard_map/ppermute | solution.py:297
  94.4 2.0 %collective-permute-done.24.refs_10_ = bf16[128,512]{1,0:T(8,128)(2,1)S(1)} collective-permute-done((bf16[128,512]{1,0:T(8,128)(2,1)S(1)}, bf16[128,512]{1,0:T(8,128)(2,1)S(1)}, u32[]{:S(2)}, u32[]{:S(2)}) %collective-permute-start.24) | collective-permute-done | bytes 131104 | tf_op jit(solution)/shard_map/ppermute | solution.py:297
  96.5 4.8 %all-to-all-start = ((bf16[16,16,576]{2,1,0:T(8,128)(2,1)}), bf16[16,16,576]{2,1,0:T(8,128)(2,1)S(1)}, u32[]{:S(2)}, u32[]{:S(2)}) async-start(bf16[16,16,576]{2,1,0:T(8,128)(2,1)} %bitcast.5), calls=%async_computation | async-start | bytes 655360 | tf_op jit(solution)/shard_map/all_to_all | solution.py:476
  101.3 0.4 collective-permute-start.25
  101.7 0.5 collective-permute-start.26
  102.2 1.0 collective-permute-start.27
  103.2 0.0 collective-permute-done.25.refs_5_
  103.2 4.8 %collective-permute-done.26.refs_8_ = bf16[128,512]{1,0:T(8,128)(2,1)S(1)} collective-permute-done((bf16[128,512]{1,0:T(8,128)(2,1)S(1)}, bf16[128,512]{1,0:T(8,128)(2,1)S(1)}, u32[]{:S(2)}, u32[]{:S(2)}) %collective-permute-start.26) | collective-permute-done | bytes 131104 | tf_op jit(solution)/shard_map/ppermute | solution.py:297
  108.0 1.3 %collective-permute-done.27.refs_11_ = bf16[128,512]{1,0:T(8,128)(2,1)S(1)} collective-permute-done((bf16[128,512]{1,0:T(8,128)(2,1)S(1)}, bf16[128,512]{1,0:T(8,128)(2,1)S(1)}, u32[]{:S(2)}, u32[]{:S(2)}) %collective-permute-start.27) | collective-permute-done | bytes 131104 | tf_op jit(solution)/shard_map/ppermute | solution.py:297
  109.3 1.4 %place.1 = bf16[128,8192]{1,0:T(8,128)(2,1)} custom-call(s32[1]{0:T(128)} %bitcast.info, bf16[128,1024]{1,0:T(8,128)(2,1)S(1)} %get-tuple-element.74.refs_0_, bf16[128,512]{1,0:T(8,128)(2,1)S(1)} %get-tuple-element.84.refs_1_, bf16[128,512]{1,0:T(8,128)(2,1)S(1)} %get-tuple-element.88.refs_2_, bf16[128,1024]{1,0:T(8,128)(2,1)S(1)} %collective-permute-done.20.refs_3_, ...), custom_call_target="tpu_custom_call" | custom-call | tf_op jit(solution)/shard_map/place/pallas_call | solution.py:484
  110.7 1.7 %all-to-all-done = bf16[16,16,576]{2,1,0:T(8,128)(2,1)S(1)} async-done(((bf16[16,16,576]{2,1,0:T(8,128)(2,1)}), bf16[16,16,576]{2,1,0:T(8,128)(2,1)S(1)}, u32[]{:S(2)}, u32[]{:S(2)}) %all-to-all-start) | async-done | bytes 294944 | tf_op jit(solution)/shard_map/all_to_all | solution.py:476
  112.4 0.9 copy.10
  (13 shorter events, 0.2 us)
Async XLA Ops:
  1.6 1.7 %collective-permute-start = (bf16[32,4096]{1,0:T(8,128)(2,1)S(1)}, bf16[32,4096]{1,0:T(8,128)(2,1)S(1)}, u32[]{:S(2)}, u32[]{:S(2)}) collective-permute-start(bf16[32,4096]{1,0:T(8,128)(2,1)S(1)} %constant_dynamic-slice_fusion), channel_id=1, source_target_pairs={{0,1},{1,0},{2,3},{3,2},{4,5},{5,4},{6,7},{7,6},{8,9},{9,8},{10,11... | collective-permute-start | bytes 786440 | tf_op jit(solution)/shard_map/ppermute | solution.py:297
  4.3 20.9 %collective-permute-start.3 = (bf16[64,4096]{1,0:T(8,128)(2,1)S(1)}, bf16[64,4096]{1,0:T(8,128)(2,1)S(1)}, u32[]{:S(2)}, u32[]{:S(2)}) collective-permute-start(bf16[64,4096]{1,0:T(8,128)(2,1)S(1)} %pair.1.refs_0_), channel_id=1, source_target_pairs={{0,4},{1,5},{2,6},{3,7},{4,8},{5,9},{6,10},{7,11},{8,12},{9,13},{1... | collective-permute-start | bytes 1572872 | tf_op jit(solution)/shard_map/ppermute | solution.py:300
  7.3 17.9 %collective-permute-start.4 = (bf16[64,4096]{1,0:T(8,128)(2,1)S(1)}, bf16[64,4096]{1,0:T(8,128)(2,1)S(1)}, u32[]{:S(2)}, u32[]{:S(2)}) collective-permute-start(bf16[64,4096]{1,0:T(8,128)(2,1)S(1)} %pair.1.refs_0_), channel_id=1, source_target_pairs={{0,2},{1,3},{2,0},{3,1},{4,6},{5,7},{6,4},{7,5},{8,10},{9,11},{10,... | collective-permute-start | bytes 1572872 | tf_op jit(solution)/shard_map/ppermute | solution.py:303
  11.1 4.9 %copy-start = (bf16[128,640]{1,0:T(8,128)(2,1)S(1)}, bf16[128,640]{1,0:T(8,128)(2,1)}, u32[]{:S(2)}) copy-start(bf16[128,640]{1,0:T(8,128)(2,1)} %get-tuple-element.55) | copy-start | bytes 491524
  14.5 10.7 %collective-permute-start.5 = (bf16[128,1536]{1,0:T(8,128)(2,1)S(1)}, bf16[128,1536]{1,0:T(8,128)(2,1)S(1)}, u32[]{:S(2)}, u32[]{:S(2)}) collective-permute-start(bf16[128,1536]{1,0:T(8,128)(2,1)S(1)} %get-tuple-element.59), channel_id=1, source_target_pairs={{0,16},{1,17},{2,18},{3,19},{4,20},{5,21},{6,22},{7,23},{8,24},{9,... | collective-permute-start | bytes 1179656 | tf_op jit(solution)/shard_map/ppermute | solution.py:297
  16.0 7.5 %collective-permute-start.1 = (bf16[128,640]{1,0:T(8,128)(2,1)S(1)}, bf16[128,640]{1,0:T(8,128)(2,1)S(1)}, u32[]{:S(2)}, u32[]{:S(2)}) collective-permute-start(bf16[128,640]{1,0:T(8,128)(2,1)S(1)} %copy-done), channel_id=1, source_target_pairs={{0,2},{1,3},{2,4},{3,5},{4,6},{5,7},{6,8},{7,9},{8,10},{9,11},{10,... | collective-permute-start | bytes 491528 | tf_op jit(solution)/shard_map/ppermute | solution.py:309
  18.5 5.1 %collective-permute-start.2 = (bf16[128,640]{1,0:T(8,128)(2,1)S(1)}, bf16[128,640]{1,0:T(8,128)(2,1)S(1)}, u32[]{:S(2)}, u32[]{:S(2)}) collective-permute-start(bf16[128,640]{1,0:T(8,128)(2,1)S(1)} %copy-done), channel_id=1, source_target_pairs={{1,5},{3,7},{5,9},{7,11},{9,13},{11,15},{17,21},{19,23},{21,25},{2... | collective-permute-start | bytes 491528 | tf_op jit(solution)/shard_map/ppermute | solution.py:309
  25.2 11.8 %collective-permute-start.6 = (bf16[384,640]{1,0:T(8,128)(2,1)S(1)}, bf16[384,640]{1,0:T(8,128)(2,1)S(1)}, u32[]{:S(2)}, u32[]{:S(2)}) collective-permute-start(bf16[384,640]{1,0:T(8,128)(2,1)S(1)} %pad_maximum_fusion), channel_id=1, source_target_pairs={{0,16},{1,17},{2,18},{3,19},{4,20},{5,21},{6,22},{7,23},{8,24},{9,... | collective-permute-start | bytes 1474568 | tf_op jit(solution)/shard_map/ppermute | solution.py:297
  26.6 14.0 %collective-permute-start.7 = (bf16[64,4096]{1,0:T(8,128)(2,1)S(1)}, bf16[64,4096]{1,0:T(8,128)(2,1)S(1)}, u32[]{:S(2)}, u32[]{:S(2)}) collective-permute-start(bf16[64,4096]{1,0:T(8,128)(2,1)S(1)} %collective-permute-done.3.refs_1_), channel_id=1, source_target_pairs={{0,4},{1,5},{2,6},{3,7},{4,8},{5,9},{6,10},{7,11},{8,12},{9,13},{1... | collective-permute-start | bytes 1572872 | tf_op jit(solution)/shard_map/ppermute | solution.py:300
  28.3 12.8 %collective-permute-start.8 = (bf16[64,4096]{1,0:T(8,128)(2,1)S(1)}, bf16[64,4096]{1,0:T(8,128)(2,1)S(1)}, u32[]{:S(2)}, u32[]{:S(2)}) collective-permute-start(bf16[64,4096]{1,0:T(8,128)(2,1)S(1)} %collective-permute-done.3.refs_1_), channel_id=1, source_target_pairs={{0,2},{1,3},{2,0},{3,1},{4,6},{5,7},{6,4},{7,5},{8,10},{9,11},{10,... | collective-permute-start | bytes 1572872 | tf_op jit(solution)/shard_map/ppermute | solution.py:303
  29.2 7.8 %collective-permute-start.9 = (bf16[128,1536]{1,0:T(8,128)(2,1)S(1)}, bf16[128,1536]{1,0:T(8,128)(2,1)S(1)}, u32[]{:S(2)}, u32[]{:S(2)}) collective-permute-start(bf16[128,1536]{1,0:T(8,128)(2,1)S(1)} %get-tuple-element.64), channel_id=1, source_target_pairs={{0,1},{1,0},{2,3},{3,2},{4,5},{5,4},{6,7},{7,6},{8,9},{9,8},{10,11... | collective-permute-start | bytes 1179656 | tf_op jit(solution)/shard_map/ppermute | solution.py:297
  41.1 16.2 %collective-permute-start.10 = (bf16[768,640]{1,0:T(8,128)(2,1)S(1)}, bf16[768,640]{1,0:T(8,128)(2,1)S(1)}, u32[]{:S(2)}, u32[]{:S(2)}) collective-permute-start(bf16[768,640]{1,0:T(8,128)(2,1)S(1)} %constant_dynamic-update-slice_fusion.own), channel_id=1, source_target_pairs={{0,1},{1,0},{2,3},{3,2},{4,5},{5,4},{6,7},{7,6},{8,9},{9,8},{10,11... | collective-permute-start | bytes 2949128 | tf_op jit(solution)/shard_map/ppermute | solution.py:297
  41.1 16.1 %collective-permute-start.11 = (bf16[64,4096]{1,0:T(8,128)(2,1)S(1)}, bf16[64,4096]{1,0:T(8,128)(2,1)S(1)}, u32[]{:S(2)}, u32[]{:S(2)}) collective-permute-start(bf16[64,4096]{1,0:T(8,128)(2,1)S(1)} %collective-permute-done.7.refs_2_), channel_id=1, source_target_pairs={{0,4},{1,5},{2,6},{3,7},{4,8},{5,9},{6,10},{7,11},{8,12},{9,13},{1... | collective-permute-start | bytes 1572872 | tf_op jit(solution)/shard_map/ppermute | solution.py:300
  42.6 14.6 %collective-permute-start.12 = (bf16[64,4096]{1,0:T(8,128)(2,1)S(1)}, bf16[64,4096]{1,0:T(8,128)(2,1)S(1)}, u32[]{:S(2)}, u32[]{:S(2)}) collective-permute-start(bf16[64,4096]{1,0:T(8,128)(2,1)S(1)} %collective-permute-done.7.refs_2_), channel_id=1, source_target_pairs={{0,2},{1,3},{2,0},{3,1},{4,6},{5,7},{6,4},{7,5},{8,10},{9,11},{10,... | collective-permute-start | bytes 1572872 | tf_op jit(solution)/shard_map/ppermute | solution.py:303
  44.4 12.8 %collective-permute-start.13 = (bf16[128,1536]{1,0:T(8,128)(2,1)S(1)}, bf16[128,1536]{1,0:T(8,128)(2,1)S(1)}, u32[]{:S(2)}, u32[]{:S(2)}) collective-permute-start(bf16[128,1536]{1,0:T(8,128)(2,1)S(1)} %get-tuple-element.72), channel_id=1, source_target_pairs={{0,17},{1,16},{2,19},{3,18},{4,21},{5,20},{6,23},{7,22},{8,25},{9,... | collective-permute-start | bytes 1179656 | tf_op jit(solution)/shard_map/ppermute | solution.py:297
  57.2 8.5 %collective-permute-start.14 = (bf16[64,2048]{1,0:T(8,128)(2,1)S(1)}, bf16[64,2048]{1,0:T(8,128)(2,1)S(1)}, u32[]{:S(2)}, u32[]{:S(2)}) collective-permute-start(bf16[64,2048]{1,0:T(8,128)(2,1)S(1)} %slice.8), channel_id=1, source_target_pairs={{0,2},{1,3},{2,0},{3,1},{4,6},{5,7},{6,4},{7,5},{8,10},{9,11},{10,... | collective-permute-start | bytes 786440 | tf_op jit(solution)/shard_map/ppermute | solution.py:303
  59.6 15.7 %collective-permute-start.15 = (bf16[64,2048]{1,0:T(8,128)(2,1)S(1)}, bf16[64,2048]{1,0:T(8,128)(2,1)S(1)}, u32[]{:S(2)}, u32[]{:S(2)}) collective-permute-start(bf16[64,2048]{1,0:T(8,128)(2,1)S(1)} %slice.9), channel_id=1, source_target_pairs={{0,4},{1,5},{2,6},{3,7},{4,8},{5,9},{6,10},{7,11},{8,12},{9,13},{1... | collective-permute-start | bytes 786440 | tf_op jit(solution)/shard_map/ppermute | solution.py:300
  60.0 15.3 %collective-permute-start.16 = (bf16[128,1536]{1,0:T(8,128)(2,1)S(1)}, bf16[128,1536]{1,0:T(8,128)(2,1)S(1)}, u32[]{:S(2)}, u32[]{:S(2)}) collective-permute-start(bf16[128,1536]{1,0:T(8,128)(2,1)S(1)} %get-tuple-element.79), channel_id=1, source_target_pairs={{0,1},{1,0},{2,3},{3,2},{4,5},{5,4},{6,7},{7,6},{8,9},{9,8},{10,11... | collective-permute-start | bytes 1179656 | tf_op jit(solution)/shard_map/ppermute | solution.py:297
  60.1 16.9 %collective-permute-start.17 = (bf16[128,1536]{1,0:T(8,128)(2,1)S(1)}, bf16[128,1536]{1,0:T(8,128)(2,1)S(1)}, u32[]{:S(2)}, u32[]{:S(2)}) collective-permute-start(bf16[128,1536]{1,0:T(8,128)(2,1)S(1)} %get-tuple-element.81), channel_id=1, source_target_pairs={{0,16},{1,17},{2,18},{3,19},{4,20},{5,21},{6,22},{7,23},{8,24},{9,... | collective-permute-start | bytes 1179656 | tf_op jit(solution)/shard_map/ppermute | solution.py:297
  60.6 19.0 %collective-permute-start.18 = (bf16[128,1536]{1,0:T(8,128)(2,1)S(1)}, bf16[128,1536]{1,0:T(8,128)(2,1)S(1)}, u32[]{:S(2)}, u32[]{:S(2)}) collective-permute-start(bf16[128,1536]{1,0:T(8,128)(2,1)S(1)} %get-tuple-element.83), channel_id=1, source_target_pairs={{0,17},{1,16},{2,19},{3,18},{4,21},{5,20},{6,23},{7,22},{8,25},{9,... | collective-permute-start | bytes 1179656 | tf_op jit(solution)/shard_map/ppermute | solution.py:297
  74.7 11.3 %collective-permute-start.19 = (bf16[128,1024]{1,0:T(8,128)(2,1)S(1)}, bf16[128,1024]{1,0:T(8,128)(2,1)S(1)}, u32[]{:S(2)}, u32[]{:S(2)}) collective-permute-start(bf16[128,1024]{1,0:T(8,128)(2,1)S(1)} %get-tuple-element.86), channel_id=1, source_target_pairs={{0,16},{1,17},{2,18},{3,19},{4,20},{5,21},{6,22},{7,23},{8,24},{9,... | collective-permute-start | bytes 786440 | tf_op jit(solution)/shard_map/ppermute | solution.py:297
  75.3 15.4 %collective-permute-start.20 = (bf16[128,1024]{1,0:T(8,128)(2,1)S(1)}, bf16[128,1024]{1,0:T(8,128)(2,1)S(1)}, u32[]{:S(2)}, u32[]{:S(2)}) collective-permute-start(bf16[128,1024]{1,0:T(8,128)(2,1)S(1)} %get-tuple-element.89), channel_id=1, source_target_pairs={{0,1},{1,0},{2,3},{3,2},{4,5},{5,4},{6,7},{7,6},{8,9},{9,8},{10,11... | collective-permute-start | bytes 786440 | tf_op jit(solution)/shard_map/ppermute | solution.py:297
  75.3 15.5 %collective-permute-start.22 = (bf16[128,1024]{1,0:T(8,128)(2,1)S(1)}, bf16[128,1024]{1,0:T(8,128)(2,1)S(1)}, u32[]{:S(2)}, u32[]{:S(2)}) collective-permute-start(bf16[128,1024]{1,0:T(8,128)(2,1)S(1)} %get-tuple-element.92), channel_id=1, source_target_pairs={{0,17},{1,16},{2,19},{3,18},{4,21},{5,20},{6,23},{7,22},{8,25},{9,... | collective-permute-start | bytes 786440 | tf_op jit(solution)/shard_map/ppermute | solution.py:297
  84.1 6.7 %collective-permute-start.21 = (bf16[128,512]{1,0:T(8,128)(2,1)S(1)}, bf16[128,512]{1,0:T(8,128)(2,1)S(1)}, u32[]{:S(2)}, u32[]{:S(2)}) collective-permute-start(bf16[128,512]{1,0:T(8,128)(2,1)S(1)} %get-tuple-element.90), channel_id=1, source_target_pairs={{0,1},{1,0},{2,3},{3,2},{4,5},{5,4},{6,7},{7,6},{8,9},{9,8},{10,11... | collective-permute-start | bytes 393224 | tf_op jit(solution)/shard_map/ppermute | solution.py:297
  84.8 9.7 %collective-permute-start.23 = (bf16[128,512]{1,0:T(8,128)(2,1)S(1)}, bf16[128,512]{1,0:T(8,128)(2,1)S(1)}, u32[]{:S(2)}, u32[]{:S(2)}) collective-permute-start(bf16[128,512]{1,0:T(8,128)(2,1)S(1)} %get-tuple-element.93), channel_id=1, source_target_pairs={{0,16},{1,17},{2,18},{3,19},{4,20},{5,21},{6,22},{7,23},{8,24},{9,... | collective-permute-start | bytes 393224 | tf_op jit(solution)/shard_map/ppermute | solution.py:297
  86.0 10.5 %collective-permute-start.24 = (bf16[128,512]{1,0:T(8,128)(2,1)S(1)}, bf16[128,512]{1,0:T(8,128)(2,1)S(1)}, u32[]{:S(2)}, u32[]{:S(2)}) collective-permute-start(bf16[128,512]{1,0:T(8,128)(2,1)S(1)} %get-tuple-element.94), channel_id=1, source_target_pairs={{0,17},{1,16},{2,19},{3,18},{4,21},{5,20},{6,23},{7,22},{8,25},{9,... | collective-permute-start | bytes 393224 | tf_op jit(solution)/shard_map/ppermute | solution.py:297
  96.5 15.9 %all-to-all-start = ((bf16[16,16,576]{2,1,0:T(8,128)(2,1)}), bf16[16,16,576]{2,1,0:T(8,128)(2,1)S(1)}, u32[]{:S(2)}, u32[]{:S(2)}) async-start(bf16[16,16,576]{2,1,0:T(8,128)(2,1)} %bitcast.5), calls=%async_computation | async-start | bytes 655360 | tf_op jit(solution)/shard_map/all_to_all | solution.py:476
  101.3 1.9 %collective-permute-start.25 = (bf16[128,512]{1,0:T(8,128)(2,1)S(1)}, bf16[128,512]{1,0:T(8,128)(2,1)S(1)}, u32[]{:S(2)}, u32[]{:S(2)}) collective-permute-start(bf16[128,512]{1,0:T(8,128)(2,1)S(1)} %get-tuple-element.95), channel_id=1, source_target_pairs={{0,1},{1,0},{2,3},{3,2},{4,5},{5,4},{6,7},{7,6},{8,9},{9,8},{10,11... | collective-permute-start | bytes 393224 | tf_op jit(solution)/shard_map/ppermute | solution.py:297
  101.7 6.3 %collective-permute-start.26 = (bf16[128,512]{1,0:T(8,128)(2,1)S(1)}, bf16[128,512]{1,0:T(8,128)(2,1)S(1)}, u32[]{:S(2)}, u32[]{:S(2)}) collective-permute-start(bf16[128,512]{1,0:T(8,128)(2,1)S(1)} %get-tuple-element.97), channel_id=1, source_target_pairs={{0,16},{1,17},{2,18},{3,19},{4,20},{5,21},{6,22},{7,23},{8,24},{9,... | collective-permute-start | bytes 393224 | tf_op jit(solution)/shard_map/ppermute | solution.py:297
  102.2 7.1 %collective-permute-start.27 = (bf16[128,512]{1,0:T(8,128)(2,1)S(1)}, bf16[128,512]{1,0:T(8,128)(2,1)S(1)}, u32[]{:S(2)}, u32[]{:S(2)}) collective-permute-start(bf16[128,512]{1,0:T(8,128)(2,1)S(1)} %get-tuple-element.99), channel_id=1, source_target_pairs={{0,17},{1,16},{2,19},{3,18},{4,21},{5,20},{6,23},{7,22},{8,25},{9,... | collective-permute-start | bytes 393224 | tf_op jit(solution)/shard_map/ppermute | solution.py:297

commit v11 on v10

--- a/solution.py
+++ b/solution.py
@@ -19,10 +19,10 @@
 HQ = H // QUAD
 CHUNK_HEADS = (8, 8)
 PHASES = (
-    ("z", "y0", "b~", "f~", "q02"),
-    ("z", "y1", "k", "q01"),
-    ("z", "y2", "p", "q03"),
-    ("y3", "w", "q12~", "q13~", "q11"),
+    ("z", "y0", "k", "q02", "b~", "f~"),
+    ("z", "y1", "q03", "q01"),
+    ("z", "y2", "p", "q12"),
+    ("y3", "w", "q13~", "q11"),
 )
 CHUNKS = len(CHUNK_HEADS)
 FIRST_HEAD = tuple(sum(CHUNK_HEADS[:j]) for j in range(CHUNKS))
@@ -133,7 +133,7 @@
     row = lax.broadcasted_iota(jnp.int32, (tok, tok), 0)
     for g in range(2):
         mine_of, other_of = [
-            [ref[(3 * g + n) * tok : (3 * g + n + 1) * tok] for n in range(3)]
+            [ref[(2 * n + g) * tok : (2 * n + g + 1) * tok] for n in range(3)]
             for ref in (own, other)
         ]
         pieces = [
@@ -266,7 +266,8 @@
 
     def send(self, late, permute, array, *args):
         arrived = permute(tie(array, *self.before) if self.before else array, *args)
-        (self.late if late else self.now).append(arrived)
+        if late != "-":
+            (self.late if late == "~" else self.now).append(arrived)
         return arrived
 
 
@@ -386,7 +387,7 @@
     moved = [[queries[j]] + [None] * (QUAD - 1) for j in range(CHUNKS)]
     parts = {"r": tie(rows, pair_rows if outer else got)}
     for name in [name for phase in PHASES for name in phase + ("|",)]:
-        kind, late = name[0], name[-1] == "~"
+        kind, late = name[0], name[-1]
         if kind == "|":
             phases.now.append(queries[0])
             phases.turn()
@@ -400,15 +401,15 @@
                 halves.append(phases.send(late, inner_swap, line[step][:, :half]))
         elif kind == "w" and outer:
             halves.append(phases.send(late, around, side[-1][:, half:], 4))
+        elif kind == "k":
+            swapped = phases.send(late, quad_swap, parts["r"], 2)
+            both_groups = jnp.concatenate([parts["r"], swapped], axis=0)
         elif kind == "b":
-            parts["b"] = phases.send(late, from_behind, parts["r"], 2, False)
+            behind = phases.send(late, from_behind, both_groups, 2, False)
         elif kind == "f":
-            parts["f"] = phases.send(late, from_behind, parts["r"], 4, True)
-        elif kind == "k":
-            have = jnp.concatenate([parts["r"], parts["b"], parts["f"]], axis=0)
-            swapped = phases.send(late, quad_swap, have, 2)
+            far_behind = phases.send(late, from_behind, both_groups, 4, True)
         elif kind == "p":
-            own_rows = jnp.concatenate([have, swapped], axis=0)
+            own_rows = jnp.concatenate([both_groups, behind, far_behind], axis=0)
             other_rows = phases.send(late, quad_swap, own_rows, 1)
         elif kind == "q":
             j, r = int(name[1]), int(name[2])
@@ -468,10 +469,8 @@
         mine_info = tie(mine_info, *(results[0][2:3] if last else []))
         pieces = attend(*call)
         mine_info = tie(mine_info, pieces[0])
-        before = [piece for one in results for piece in one[1:]] if last else []
-        results.append(
-            [pieces[0]] + [quad_swap(tie(pieces[r], *before), r) for r in range(1, QUAD)]
-        )
+        before = [piece for one in results for piece in one[1:]]
+        results.append([pieces[0]] + [quad_swap(pieces[r], r) for r in range(1, QUAD)])
     pieces = [one[r] for r in range(QUAD) for one in results]
     arrived = lax.all_to_all(
         tie(outgoing, results[-1][0], *before).reshape(size, slot_count, ROW),

time: 114 us -> 107 us (0.939)
  waiting for transfers between devices: 51.6 us -> 44 us
  starting transfers between devices: 32.2 us -> 33.6 us
    ppermute x4, waiting for transfers between devices: 16.3 us -> 10.9 us  [around(): lax.ppermute(array, 'ctx', [(i, (i + by) % size) for i in range(size)])]
    ppermute x2, waiting for transfers between devices: 4.38 us -> 0.01 us  [from_behind(): return lax.ppermute(array, 'ctx', pairs)]
    ppermute x18, waiting for transfers between devices: 25.6 us -> 29 us  [quad_swap(): return lax.ppermute(array, ('groups', 'ctx'), pairs)]
    ppermute x18, starting transfers between devices: 11.1 us -> 13.4 us  [quad_swap(): return lax.ppermute(array, ('groups', 'ctx'), pairs)]
    ppermute x4, starting transfers between devices: 6.65 us -> 8.17 us  [around(): lax.ppermute(array, 'ctx', [(i, (i + by) % size) for i in range(size)])]
    ppermute x4, starting transfers between devices: 6.53 us -> 5.01 us  [inner_swap(): return lax.ppermute(array, 'ctx', [(i, i ^ 2) for i in range(size)])]
    ppermute x4, waiting for transfers between devices: 3.67 us -> 2.38 us  [inner_swap(): return lax.ppermute(array, 'ctx', [(i, i ^ 2) for i in range(size)])]
  transfers between devices with their start and end apart: 29 -> 29, of which waited for: 16 -> 15; matrix products, arithmetic and copies ran while one was open for 0% -> 0% of each run, Pallas kernels for 23% -> 24%
where the time goes in v11:
time: 107 us
  waiting for transfers between devices  44 us (41%)
  starting transfers between devices  33.6 us (31%)
  Pallas kernels  26.5 us (25%)
  local copies, waits for them, and re-layouts  2.04 us (2%)
    ppermute x18, waiting for transfers between devices, quad_swap(): return lax.ppermute(array, ('groups', 'ctx'), pairs)  29 us
    pallas_call x3, Pallas kernels, attend(): pl.pallas_call(functools.partial(attend_kernel, outer), grid=(steps,), ou...  17.9 us
    ppermute x18, starting transfers between devices, quad_swap(): return lax.ppermute(array, ('groups', 'ctx'), pairs)  13.4 us
    ppermute x4, waiting for transfers between devices, around(): lax.ppermute(array, 'ctx', [(i, (i + by) % size) for i in range(size)])  10.9 us
    ppermute x4, starting transfers between devices, around(): lax.ppermute(array, 'ctx', [(i, (i + by) % size) for i in range(size)])  8.17 us
    ppermute x4, starting transfers between devices, inner_swap(): return lax.ppermute(array, 'ctx', [(i, i ^ 2) for i in range(size)])  5.01 us
    all_to_all x1, starting transfers between devices, body(): lax.all_to_all(tie(outgoing, results[-1][0], *before).reshape(size, slot_...  4 us
    pallas_call x1, Pallas kernels, body(): pl.pallas_call(query_kernel, out_shape=[shape((tok, h * (NOPE + ROPE))) f...  3.33 us
  transfers between devices with their start and end apart: 29, of which 15 were waited for; matrix products, arithmetic and copies ran while one was open for 0% of the time, Pallas kernels for 24%

profile of v11, /device:TPU:0, one launch (start us, length us, event | category | flops | bytes accessed | tf_op | source)
XLA Modules:
  0.0 107.0 jit_solution(3057636121774492009)
XLA Ops:
  0.6 1.0 constant_dynamic-slice_fusion
  1.6 0.5 collective-permute-start
  2.1 1.2 %collective-permute-done.got = bf16[32,4096]{1,0:T(8,128)(2,1)S(1)} collective-permute-done((bf16[32,4096]{1,0:T(8,128)(2,1)S(1)}, bf16[32,4096]{1,0:T(8,128)(2,1)S(1)}, u32[]{:S(2)}, u32[]{:S(2)}) %collective-permute-start) | collective-permute-done | bytes 262176 | tf_op jit(solution)/shard_map/ppermute | solution.py:298
  3.3 1.0 pair.1.refs_0_
  4.3 3.0 %collective-permute-start.4 = (bf16[64,4096]{1,0:T(8,128)(2,1)S(1)}, bf16[64,4096]{1,0:T(8,128)(2,1)S(1)}, u32[]{:S(2)}, u32[]{:S(2)}) collective-permute-start(bf16[64,4096]{1,0:T(8,128)(2,1)S(1)} %pair.1.refs_0_), channel_id=1, source_target_pairs={{0,4},{1,5},{2,6},{3,7},{4,8},{5,9},{6,10},{7,11},{8,12},{9,13},{1... | collective-permute-start | bytes 1572872 | tf_op jit(solution)/shard_map/ppermute | solution.py:301
  7.3 1.5 %collective-permute-start.5 = (bf16[64,4096]{1,0:T(8,128)(2,1)S(1)}, bf16[64,4096]{1,0:T(8,128)(2,1)S(1)}, u32[]{:S(2)}, u32[]{:S(2)}) collective-permute-start(bf16[64,4096]{1,0:T(8,128)(2,1)S(1)} %pair.1.refs_0_), channel_id=1, source_target_pairs={{0,2},{1,3},{2,0},{3,1},{4,6},{5,7},{6,4},{7,5},{8,10},{9,11},{10,... | collective-permute-start | bytes 1572872 | tf_op jit(solution)/shard_map/ppermute | solution.py:304
  8.8 2.3 %rows.1 = (bf16[128,640]{1,0:T(8,128)(2,1)}, f32[128,128]{1,0:T(8,128)}, f32[128,128]{1,0:T(8,128)}, bf16[256,576]{1,0:T(8,128)(2,1)}) custom-call(s32[1]{0:T(128)} %bitcast.1.info, s32[8]{0:T(128)} %lengths, bf16[576,128]{1,0:T(8,128)(2,1)} %bitcast.8, f32[1,512]{1,0:T(1,128)} %bitcast.9, s32[1,128]{1,0:T(1,128)} %bitcast.10, f32[1,128]{1,0:T(1,128)} %constant.30.clone.freq), custom_call_target="tpu_custom_call" | custom-call | tf_op jit(solution)/shard_map/rows/pallas_call | solution.py:345
  11.1 1.5 %collective-permute-start.1 = (bf16[128,640]{1,0:T(8,128)(2,1)}, bf16[128,640]{1,0:T(8,128)(2,1)S(1)}, u32[]{:S(2)}, u32[]{:S(2)}) collective-permute-start(bf16[128,640]{1,0:T(8,128)(2,1)} %get-tuple-element.51), channel_id=1, source_target_pairs={{0,16},{1,17},{2,18},{3,19},{4,20},{5,21},{6,22},{7,23},{8,24},{9,... | collective-permute-start | bytes 491528 | tf_op jit(solution)/shard_map/ppermute | solution.py:298
  12.6 3.3 %queries.1 = (bf16[128,1536]{1,0:T(8,128)(2,1)S(1)}, bf16[128,1536]{1,0:T(8,128)(2,1)S(1)}, bf16[128,1536]{1,0:T(8,128)(2,1)S(1)}, bf16[128,1536]{1,0:T(8,128)(2...) custom-call(s32[1]{0:T(128)} %bitcast.info, ...), custom_call_target="tpu_custom_call" | custom-call | bytes 6291456 | tf_op jit(solution)/shard_map/queries/pallas_call | solution.py:369
  15.9 0.6 collective-permute-start.6
  16.6 0.4 collective-permute-done.1
  17.0 2.4 %collective-permute-start.2 = (bf16[256,640]{1,0:T(8,128)(2,1)S(1)}, bf16[256,640]{1,0:T(8,128)(2,1)S(1)}, u32[]{:S(2)}, u32[]{:S(2)}) collective-permute-start(bf16[256,640]{1,0:T(8,128)(2,1)S(1)} %get-tuple-element.96), channel_id=1, source_target_pairs={{0,2},{1,3},{2,4},{3,5},{4,6},{5,7},{6,8},{7,9},{8,10},{9,11},{10,... | collective-permute-start | bytes 983048 | tf_op jit(solution)/shard_map/ppermute | solution.py:310
  19.5 6.8 %collective-permute-done.6.refs_10_.refs_14_ = bf16[128,1536]{1,0:T(8,128)(2,1)S(1)} collective-permute-done((bf16[128,1536]{1,0:T(8,128)(2,1)S(1)}, bf16[128,1536]{1,0:T(8,128)(2,1)S(1)}, u32[]{:S(2)}, u32[]{:S(2)}) %collective-permute-start.6) | collective-permute-done | bytes 393248 | tf_op jit(solution)/shard_map/ppermute | solution.py:298
  26.3 0.0 collective-permute-done.4.refs_1_
  26.3 0.0 collective-permute-done.5.refs_4_
  26.3 1.6 %collective-permute-start.7 = (bf16[64,4096]{1,0:T(8,128)(2,1)S(1)}, bf16[64,4096]{1,0:T(8,128)(2,1)S(1)}, u32[]{:S(2)}, u32[]{:S(2)}) collective-permute-start(bf16[64,4096]{1,0:T(8,128)(2,1)S(1)} %collective-permute-done.4.refs_1_), channel_id=1, source_target_pairs={{0,4},{1,5},{2,6},{3,7},{4,8},{5,9},{6,10},{7,11},{8,12},{9,13},{1... | collective-permute-start | bytes 1572872 | tf_op jit(solution)/shard_map/ppermute | solution.py:301
  27.9 0.5 collective-permute-start.8
  28.4 0.7 collective-permute-start.3
  29.1 0.7 collective-permute-start.9
  29.8 0.0 collective-permute-done.2
  29.8 0.1 collective-permute-start.10
  29.9 0.0 collective-permute-done.3
  30.0 10.1 %collective-permute-done.9.refs_11_.refs_15_ = bf16[128,1536]{1,0:T(8,128)(2,1)S(1)} collective-permute-done((bf16[128,1536]{1,0:T(8,128)(2,1)S(1)}, bf16[128,1536]{1,0:T(8,128)(2,1)S(1)}, u32[]{:S(2)}, u32[]{:S(2)}) %collective-permute-start.9) | collective-permute-done | bytes 393248 | tf_op jit(solution)/shard_map/ppermute | solution.py:298
  40.1 0.0 collective-permute-done.10.refs_9_.refs_13_
  40.1 0.2 collective-permute-done.7.refs_2_
  40.3 0.0 collective-permute-done.8.refs_5_
  40.3 1.1 %collective-permute-start.11 = (bf16[768,640]{1,0:T(8,128)(2,1)S(1)}, bf16[768,640]{1,0:T(8,128)(2,1)S(1)}, u32[]{:S(2)}, u32[]{:S(2)}) collective-permute-start(bf16[768,640]{1,0:T(8,128)(2,1)S(1)} %constant_dynamic-update-slice_fusion.2.own), channel_id=1, source_target_pairs={{0,1},{1,0},{2,3},{3,2},{4,5},{5,4},{6,7},{7,6},{8,9},{9,8},{10,11... | collective-permute-start | bytes 2949128 | tf_op jit(solution)/shard_map/ppermute | solution.py:298
  41.4 2.2 %collective-permute-start.12 = (bf16[64,4096]{1,0:T(8,128)(2,1)S(1)}, bf16[64,4096]{1,0:T(8,128)(2,1)S(1)}, u32[]{:S(2)}, u32[]{:S(2)}) collective-permute-start(bf16[64,4096]{1,0:T(8,128)(2,1)S(1)} %collective-permute-done.7.refs_2_), channel_id=1, source_target_pairs={{0,4},{1,5},{2,6},{3,7},{4,8},{5,9},{6,10},{7,11},{8,12},{9,13},{1... | collective-permute-start | bytes 1572872 | tf_op jit(solution)/shard_map/ppermute | solution.py:301
  43.6 1.4 %collective-permute-start.13 = (bf16[64,4096]{1,0:T(8,128)(2,1)S(1)}, bf16[64,4096]{1,0:T(8,128)(2,1)S(1)}, u32[]{:S(2)}, u32[]{:S(2)}) collective-permute-start(bf16[64,4096]{1,0:T(8,128)(2,1)S(1)} %collective-permute-done.7.refs_2_), channel_id=1, source_target_pairs={{0,2},{1,3},{2,0},{3,1},{4,6},{5,7},{6,4},{7,5},{8,10},{9,11},{10,... | collective-permute-start | bytes 1572872 | tf_op jit(solution)/shard_map/ppermute | solution.py:304
  45.0 1.5 %collective-permute-start.14 = (bf16[128,1536]{1,0:T(8,128)(2,1)S(1)}, bf16[128,1536]{1,0:T(8,128)(2,1)S(1)}, u32[]{:S(2)}, u32[]{:S(2)}) collective-permute-start(bf16[128,1536]{1,0:T(8,128)(2,1)S(1)} %get-tuple-element.69), channel_id=1, source_target_pairs={{0,16},{1,17},{2,18},{3,19},{4,20},{5,21},{6,22},{7,23},{8,24},{9,... | collective-permute-start | bytes 1179656 | tf_op jit(solution)/shard_map/ppermute | solution.py:298
  46.5 10.6 %collective-permute-done.12.refs_3_ = bf16[64,4096]{1,0:T(8,128)(2,1)S(1)} collective-permute-done((bf16[64,4096]{1,0:T(8,128)(2,1)S(1)}, bf16[64,4096]{1,0:T(8,128)(2,1)S(1)}, u32[]{:S(2)}, u32[]{:S(2)}) %collective-permute-start.12) | collective-permute-done | bytes 524320 | tf_op jit(solution)/shard_map/ppermute | solution.py:301
  57.1 0.0 collective-permute-done.14.refs_10_.refs_14_
  57.1 0.1 collective-permute-done.13.refs_6_
  57.2 0.0 collective-permute-done.11.other
  57.2 1.6 %collective-permute-start.15 = (bf16[64,2048]{1,0:T(8,128)(2,1)S(1)}, bf16[64,2048]{1,0:T(8,128)(2,1)S(1)}, u32[]{:S(2)}, u32[]{:S(2)}) collective-permute-start(bf16[64,2048]{1,0:T(8,128)(2,1)S(1)} %slice.8), channel_id=1, source_target_pairs={{0,2},{1,3},{2,0},{3,1},{4,6},{5,7},{6,4},{7,5},{8,10},{9,11},{10,... | collective-permute-start | bytes 786440 | tf_op jit(solution)/shard_map/ppermute | solution.py:304
  58.8 1.4 %collective-permute-start.16 = (bf16[64,2048]{1,0:T(8,128)(2,1)S(1)}, bf16[64,2048]{1,0:T(8,128)(2,1)S(1)}, u32[]{:S(2)}, u32[]{:S(2)}) collective-permute-start(bf16[64,2048]{1,0:T(8,128)(2,1)S(1)} %slice.9), channel_id=1, source_target_pairs={{0,4},{1,5},{2,6},{3,7},{4,8},{5,9},{6,10},{7,11},{8,12},{9,13},{1... | collective-permute-start | bytes 786440 | tf_op jit(solution)/shard_map/ppermute | solution.py:301
  60.2 1.6 %collective-permute-start.18 = (bf16[128,1536]{1,0:T(8,128)(2,1)S(1)}, bf16[128,1536]{1,0:T(8,128)(2,1)S(1)}, u32[]{:S(2)}, u32[]{:S(2)}) collective-permute-start(bf16[128,1536]{1,0:T(8,128)(2,1)S(1)} %get-tuple-element.78), channel_id=1, source_target_pairs={{0,17},{1,16},{2,19},{3,18},{4,21},{5,20},{6,23},{7,22},{8,25},{9,... | collective-permute-start | bytes 1179656 | tf_op jit(solution)/shard_map/ppermute | solution.py:298
  61.8 0.6 keys.1
  62.4 2.3 %collective-permute-done.15.refs_7_ = bf16[64,2048]{1,0:T(8,128)(2,1)S(1)} collective-permute-done((bf16[64,2048]{1,0:T(8,128)(2,1)S(1)}, bf16[64,2048]{1,0:T(8,128)(2,1)S(1)}, u32[]{:S(2)}, u32[]{:S(2)}) %collective-permute-start.15) | collective-permute-done | bytes 262176 | tf_op jit(solution)/shard_map/ppermute | solution.py:304
  64.7 8.9 %attend.3 = (bf16[128,1024]{1,0:T(8,128)(2,1)S(1)}, bf16[128,1024]{1,0:T(8,128)(2,1)S(1)}, bf16[128,1024]{1,0:T(8,128)(2,1)S(1)}, bf16[128,1024]{1,0:T(8,128)(2,1)S(1)}) custom-call(s32[1]{0:T(128)} %bitcast.1.info, bf16[2,640,512]{2,1,0:T(8,128)(2,1)S(1)} %get-tuple-element.63.latent, bf16[2,640,128]{2,1,0:T(8,128)(2,1)S(1)} %get-tuple-element.64.rope_even, ...), custom_call_target="tpu_custom_call" | custom-call | flops 4362076160 | bytes 8388608 | tf_op jit(solution)/shard_map/attend/pallas_call | solution.py:444
  73.7 1.6 %collective-permute-start.19 = (bf16[128,1024]{1,0:T(8,128)(2,1)S(1)}, bf16[128,1024]{1,0:T(8,128)(2,1)S(1)}, u32[]{:S(2)}, u32[]{:S(2)}) collective-permute-start(bf16[128,1024]{1,0:T(8,128)(2,1)S(1)} %get-tuple-element.81), channel_id=1, source_target_pairs={{0,16},{1,17},{2,18},{3,19},{4,20},{5,21},{6,22},{7,23},{8,24},{9,... | collective-permute-start | bytes 786440 | tf_op jit(solution)/shard_map/ppermute | solution.py:298
  75.3 0.0 collective-permute-start.20
  75.3 0.0 collective-permute-done.16.refs_7_
  75.3 0.6 collective-permute-start.25
  75.9 0.0 collective-permute-done.17.refs_9_.refs_13_
  75.9 0.0 collective-permute-done.18.refs_11_.refs_15_
  75.9 4.5 %attend.4 = (bf16[128,512]{1,0:T(8,128)(2,1)S(1)}, bf16[128,512]{1,0:T(8,128)(2,1)S(1)}, bf16[128,512]{1,0:T(8,128)(2,1)S(1)}, bf16[128,512]{1,0:T(8,128)(2,1)S(1)}) custom-call(s32[1]{0:T(128)} %bitcast.1.info, bf16[2,640,512]{2,1,0:T(8,128)(2,1)S(1)} %get-tuple-element.63.latent, bf16[2,640,128]{2,1,0:T(8,128)(2,1)S(1)} %get-tuple-element.64.rope_even, ...), custom_call_target="tpu_custom_call" | custom-call | flops 2181038080 | bytes 4194304 | tf_op jit(solution)/shard_map/attend/pallas_call | solution.py:444
  80.4 0.1 collective-permute-start.21
  80.5 1.6 %collective-permute-start.23 = (bf16[128,512]{1,0:T(8,128)(2,1)S(1)}, bf16[128,512]{1,0:T(8,128)(2,1)S(1)}, u32[]{:S(2)}, u32[]{:S(2)}) collective-permute-start(bf16[128,512]{1,0:T(8,128)(2,1)S(1)} %get-tuple-element.87), channel_id=1, source_target_pairs={{0,16},{1,17},{2,18},{3,19},{4,20},{5,21},{6,22},{7,23},{8,24},{9,... | collective-permute-start | bytes 393224 | tf_op jit(solution)/shard_map/ppermute | solution.py:298
  82.0 0.7 collective-permute-done.19.refs_6_
  82.8 4.5 %attend.5 = (bf16[128,512]{1,0:T(8,128)(2,1)S(1)}, bf16[128,512]{1,0:T(8,128)(2,1)S(1)}, bf16[128,512]{1,0:T(8,128)(2,1)S(1)}, bf16[128,512]{1,0:T(8,128)(2,1)S(1)}) custom-call(s32[1]{0:T(128)} %bitcast.1.info, bf16[2,640,512]{2,1,0:T(8,128)(2,1)S(1)} %get-tuple-element.63.latent, bf16[2,640,128]{2,1,0:T(8,128)(2,1)S(1)} %get-tuple-element.64.rope_even, ...), custom_call_target="tpu_custom_call" | custom-call | flops 2181038080 | bytes 4194304 | tf_op jit(solution)/shard_map/attend/pallas_call | solution.py:444
  87.3 0.3 collective-permute-done.25.refs_9_
  87.6 2.7 %collective-permute-done.23.refs_7_ = bf16[128,512]{1,0:T(8,128)(2,1)S(1)} collective-permute-done((bf16[128,512]{1,0:T(8,128)(2,1)S(1)}, bf16[128,512]{1,0:T(8,128)(2,1)S(1)}, u32[]{:S(2)}, u32[]{:S(2)}) %collective-permute-start.23) | collective-permute-done | bytes 131104 | tf_op jit(solution)/shard_map/ppermute | solution.py:298
  90.3 0.7 collective-permute-done.26.refs_10_
  91.0 4.0 %all-to-all-start = ((bf16[16,16,576]{2,1,0:T(8,128)(2,1)}), bf16[16,16,576]{2,1,0:T(8,128)(2,1)S(1)}, u32[]{:S(2)}, u32[]{:S(2)}) async-start(bf16[16,16,576]{2,1,0:T(8,128)(2,1)} %bitcast.5), calls=%async_computation | async-start | bytes 655360 | tf_op jit(solution)/shard_map/all_to_all | solution.py:475
  95.0 0.4 collective-permute-start.22
  95.4 1.5 %collective-permute-start.24 = (bf16[128,512]{1,0:T(8,128)(2,1)S(1)}, bf16[128,512]{1,0:T(8,128)(2,1)S(1)}, u32[]{:S(2)}, u32[]{:S(2)}) collective-permute-start(bf16[128,512]{1,0:T(8,128)(2,1)S(1)} %get-tuple-element.88), channel_id=1, source_target_pairs={{0,16},{1,17},{2,18},{3,19},{4,20},{5,21},{6,22},{7,23},{8,24},{9,... | collective-permute-start | bytes 393224 | tf_op jit(solution)/shard_map/ppermute | solution.py:298
  96.9 0.0 collective-permute-start.27
  97.0 0.0 collective-permute-done.22.refs_5_
  97.0 4.8 %collective-permute-done.24.refs_8_ = bf16[128,512]{1,0:T(8,128)(2,1)S(1)} collective-permute-done((bf16[128,512]{1,0:T(8,128)(2,1)S(1)}, bf16[128,512]{1,0:T(8,128)(2,1)S(1)}, u32[]{:S(2)}, u32[]{:S(2)}) %collective-permute-start.24) | collective-permute-done | bytes 131104 | tf_op jit(solution)/shard_map/ppermute | solution.py:298
  101.8 1.3 %collective-permute-done.27.refs_11_ = bf16[128,512]{1,0:T(8,128)(2,1)S(1)} collective-permute-done((bf16[128,512]{1,0:T(8,128)(2,1)S(1)}, bf16[128,512]{1,0:T(8,128)(2,1)S(1)}, u32[]{:S(2)}, u32[]{:S(2)}) %collective-permute-start.27) | collective-permute-done | bytes 131104 | tf_op jit(solution)/shard_map/ppermute | solution.py:298
  103.0 1.4 %place.1 = bf16[128,8192]{1,0:T(8,128)(2,1)} custom-call(s32[1]{0:T(128)} %bitcast.info, bf16[128,1024]{1,0:T(8,128)(2,1)S(1)} %get-tuple-element.71.refs_0_, bf16[128,512]{1,0:T(8,128)(2,1)S(1)} %get-tuple-element.79.refs_1_, bf16[128,512]{1,0:T(8,128)(2,1)S(1)} %get-tuple-element.83.refs_2_, bf16[128,1024]{1,0:T(8,128)(2,1)S(1)} %collective-permute-done.20.refs_3_, ...), custom_call_target="tpu_custom_call" | custom-call | tf_op jit(solution)/shard_map/place/pallas_call | solution.py:483
  104.4 1.7 %all-to-all-done = bf16[16,16,576]{2,1,0:T(8,128)(2,1)S(1)} async-done(((bf16[16,16,576]{2,1,0:T(8,128)(2,1)}), bf16[16,16,576]{2,1,0:T(8,128)(2,1)S(1)}, u32[]{:S(2)}, u32[]{:S(2)}) %all-to-all-start) | async-done | bytes 294944 | tf_op jit(solution)/shard_map/all_to_all | solution.py:475
  106.1 0.9 copy.10
  (12 shorter events, 0.2 us)
Async XLA Ops:
  1.6 1.7 %collective-permute-start = (bf16[32,4096]{1,0:T(8,128)(2,1)S(1)}, bf16[32,4096]{1,0:T(8,128)(2,1)S(1)}, u32[]{:S(2)}, u32[]{:S(2)}) collective-permute-start(bf16[32,4096]{1,0:T(8,128)(2,1)S(1)} %constant_dynamic-slice_fusion), channel_id=1, source_target_pairs={{0,1},{1,0},{2,3},{3,2},{4,5},{5,4},{6,7},{7,6},{8,9},{9,8},{10,11... | collective-permute-start | bytes 786440 | tf_op jit(solution)/shard_map/ppermute | solution.py:298
  4.3 22.0 %collective-permute-start.4 = (bf16[64,4096]{1,0:T(8,128)(2,1)S(1)}, bf16[64,4096]{1,0:T(8,128)(2,1)S(1)}, u32[]{:S(2)}, u32[]{:S(2)}) collective-permute-start(bf16[64,4096]{1,0:T(8,128)(2,1)S(1)} %pair.1.refs_0_), channel_id=1, source_target_pairs={{0,4},{1,5},{2,6},{3,7},{4,8},{5,9},{6,10},{7,11},{8,12},{9,13},{1... | collective-permute-start | bytes 1572872 | tf_op jit(solution)/shard_map/ppermute | solution.py:301
  7.3 19.0 %collective-permute-start.5 = (bf16[64,4096]{1,0:T(8,128)(2,1)S(1)}, bf16[64,4096]{1,0:T(8,128)(2,1)S(1)}, u32[]{:S(2)}, u32[]{:S(2)}) collective-permute-start(bf16[64,4096]{1,0:T(8,128)(2,1)S(1)} %pair.1.refs_0_), channel_id=1, source_target_pairs={{0,2},{1,3},{2,0},{3,1},{4,6},{5,7},{6,4},{7,5},{8,10},{9,11},{10,... | collective-permute-start | bytes 1572872 | tf_op jit(solution)/shard_map/ppermute | solution.py:304
  11.1 5.4 %copy-start = (bf16[128,640]{1,0:T(8,128)(2,1)S(1)}, bf16[128,640]{1,0:T(8,128)(2,1)}, u32[]{:S(2)}) copy-start(bf16[128,640]{1,0:T(8,128)(2,1)} %get-tuple-element.51) | copy-start | bytes 491524
  11.1 5.9 %collective-permute-start.1 = (bf16[128,640]{1,0:T(8,128)(2,1)}, bf16[128,640]{1,0:T(8,128)(2,1)S(1)}, u32[]{:S(2)}, u32[]{:S(2)}) collective-permute-start(bf16[128,640]{1,0:T(8,128)(2,1)} %get-tuple-element.51), channel_id=1, source_target_pairs={{0,16},{1,17},{2,18},{3,19},{4,20},{5,21},{6,22},{7,23},{8,24},{9,... | collective-permute-start | bytes 491528 | tf_op jit(solution)/shard_map/ppermute | solution.py:298
  15.9 10.4 %collective-permute-start.6 = (bf16[128,1536]{1,0:T(8,128)(2,1)S(1)}, bf16[128,1536]{1,0:T(8,128)(2,1)S(1)}, u32[]{:S(2)}, u32[]{:S(2)}) collective-permute-start(bf16[128,1536]{1,0:T(8,128)(2,1)S(1)} %get-tuple-element.55), channel_id=1, source_target_pairs={{0,16},{1,17},{2,18},{3,19},{4,20},{5,21},{6,22},{7,23},{8,24},{9,... | collective-permute-start | bytes 1179656 | tf_op jit(solution)/shard_map/ppermute | solution.py:298
  17.0 12.7 %collective-permute-start.2 = (bf16[256,640]{1,0:T(8,128)(2,1)S(1)}, bf16[256,640]{1,0:T(8,128)(2,1)S(1)}, u32[]{:S(2)}, u32[]{:S(2)}) collective-permute-start(bf16[256,640]{1,0:T(8,128)(2,1)S(1)} %get-tuple-element.96), channel_id=1, source_target_pairs={{0,2},{1,3},{2,4},{3,5},{4,6},{5,7},{6,8},{7,9},{8,10},{9,11},{10,... | collective-permute-start | bytes 983048 | tf_op jit(solution)/shard_map/ppermute | solution.py:310
  26.3 14.0 %collective-permute-start.7 = (bf16[64,4096]{1,0:T(8,128)(2,1)S(1)}, bf16[64,4096]{1,0:T(8,128)(2,1)S(1)}, u32[]{:S(2)}, u32[]{:S(2)}) collective-permute-start(bf16[64,4096]{1,0:T(8,128)(2,1)S(1)} %collective-permute-done.4.refs_1_), channel_id=1, source_target_pairs={{0,4},{1,5},{2,6},{3,7},{4,8},{5,9},{6,10},{7,11},{8,12},{9,13},{1... | collective-permute-start | bytes 1572872 | tf_op jit(solution)/shard_map/ppermute | solution.py:301
  27.9 12.4 %collective-permute-start.8 = (bf16[64,4096]{1,0:T(8,128)(2,1)S(1)}, bf16[64,4096]{1,0:T(8,128)(2,1)S(1)}, u32[]{:S(2)}, u32[]{:S(2)}) collective-permute-start(bf16[64,4096]{1,0:T(8,128)(2,1)S(1)} %collective-permute-done.4.refs_1_), channel_id=1, source_target_pairs={{0,2},{1,3},{2,0},{3,1},{4,6},{5,7},{6,4},{7,5},{8,10},{9,11},{10,... | collective-permute-start | bytes 1572872 | tf_op jit(solution)/shard_map/ppermute | solution.py:304
  28.4 1.5 %collective-permute-start.3 = (bf16[256,640]{1,0:T(8,128)(2,1)S(1)}, bf16[256,640]{1,0:T(8,128)(2,1)S(1)}, u32[]{:S(2)}, u32[]{:S(2)}) collective-permute-start(bf16[256,640]{1,0:T(8,128)(2,1)S(1)} %get-tuple-element.96), channel_id=1, source_target_pairs={{1,5},{3,7},{5,9},{7,11},{9,13},{11,15},{17,21},{19,23},{21,25},{2... | collective-permute-start | bytes 983048 | tf_op jit(solution)/shard_map/ppermute | solution.py:310
  29.1 11.0 %collective-permute-start.9 = (bf16[128,1536]{1,0:T(8,128)(2,1)S(1)}, bf16[128,1536]{1,0:T(8,128)(2,1)S(1)}, u32[]{:S(2)}, u32[]{:S(2)}) collective-permute-start(bf16[128,1536]{1,0:T(8,128)(2,1)S(1)} %get-tuple-element.59), channel_id=1, source_target_pairs={{0,17},{1,16},{2,19},{3,18},{4,21},{5,20},{6,23},{7,22},{8,25},{9,... | collective-permute-start | bytes 1179656 | tf_op jit(solution)/shard_map/ppermute | solution.py:298
  29.8 10.3 %collective-permute-start.10 = (bf16[128,1536]{1,0:T(8,128)(2,1)S(1)}, bf16[128,1536]{1,0:T(8,128)(2,1)S(1)}, u32[]{:S(2)}, u32[]{:S(2)}) collective-permute-start(bf16[128,1536]{1,0:T(8,128)(2,1)S(1)} %get-tuple-element.61), channel_id=1, source_target_pairs={{0,1},{1,0},{2,3},{3,2},{4,5},{5,4},{6,7},{7,6},{8,9},{9,8},{10,11... | collective-permute-start | bytes 1179656 | tf_op jit(solution)/shard_map/ppermute | solution.py:298
  40.3 16.9 %collective-permute-start.11 = (bf16[768,640]{1,0:T(8,128)(2,1)S(1)}, bf16[768,640]{1,0:T(8,128)(2,1)S(1)}, u32[]{:S(2)}, u32[]{:S(2)}) collective-permute-start(bf16[768,640]{1,0:T(8,128)(2,1)S(1)} %constant_dynamic-update-slice_fusion.2.own), channel_id=1, source_target_pairs={{0,1},{1,0},{2,3},{3,2},{4,5},{5,4},{6,7},{7,6},{8,9},{9,8},{10,11... | collective-permute-start | bytes 2949128 | tf_op jit(solution)/shard_map/ppermute | solution.py:298
  41.4 15.7 %collective-permute-start.12 = (bf16[64,4096]{1,0:T(8,128)(2,1)S(1)}, bf16[64,4096]{1,0:T(8,128)(2,1)S(1)}, u32[]{:S(2)}, u32[]{:S(2)}) collective-permute-start(bf16[64,4096]{1,0:T(8,128)(2,1)S(1)} %collective-permute-done.7.refs_2_), channel_id=1, source_target_pairs={{0,4},{1,5},{2,6},{3,7},{4,8},{5,9},{6,10},{7,11},{8,12},{9,13},{1... | collective-permute-start | bytes 1572872 | tf_op jit(solution)/shard_map/ppermute | solution.py:301
  43.6 13.6 %collective-permute-start.13 = (bf16[64,4096]{1,0:T(8,128)(2,1)S(1)}, bf16[64,4096]{1,0:T(8,128)(2,1)S(1)}, u32[]{:S(2)}, u32[]{:S(2)}) collective-permute-start(bf16[64,4096]{1,0:T(8,128)(2,1)S(1)} %collective-permute-done.7.refs_2_), channel_id=1, source_target_pairs={{0,2},{1,3},{2,0},{3,1},{4,6},{5,7},{6,4},{7,5},{8,10},{9,11},{10,... | collective-permute-start | bytes 1572872 | tf_op jit(solution)/shard_map/ppermute | solution.py:304
  45.0 12.1 %collective-permute-start.14 = (bf16[128,1536]{1,0:T(8,128)(2,1)S(1)}, bf16[128,1536]{1,0:T(8,128)(2,1)S(1)}, u32[]{:S(2)}, u32[]{:S(2)}) collective-permute-start(bf16[128,1536]{1,0:T(8,128)(2,1)S(1)} %get-tuple-element.69), channel_id=1, source_target_pairs={{0,16},{1,17},{2,18},{3,19},{4,20},{5,21},{6,22},{7,23},{8,24},{9,... | collective-permute-start | bytes 1179656 | tf_op jit(solution)/shard_map/ppermute | solution.py:298
  57.2 7.5 %collective-permute-start.15 = (bf16[64,2048]{1,0:T(8,128)(2,1)S(1)}, bf16[64,2048]{1,0:T(8,128)(2,1)S(1)}, u32[]{:S(2)}, u32[]{:S(2)}) collective-permute-start(bf16[64,2048]{1,0:T(8,128)(2,1)S(1)} %slice.8), channel_id=1, source_target_pairs={{0,2},{1,3},{2,0},{3,1},{4,6},{5,7},{6,4},{7,5},{8,10},{9,11},{10,... | collective-permute-start | bytes 786440 | tf_op jit(solution)/shard_map/ppermute | solution.py:304
  58.8 16.4 %collective-permute-start.16 = (bf16[64,2048]{1,0:T(8,128)(2,1)S(1)}, bf16[64,2048]{1,0:T(8,128)(2,1)S(1)}, u32[]{:S(2)}, u32[]{:S(2)}) collective-permute-start(bf16[64,2048]{1,0:T(8,128)(2,1)S(1)} %slice.9), channel_id=1, source_target_pairs={{0,4},{1,5},{2,6},{3,7},{4,8},{5,9},{6,10},{7,11},{8,12},{9,13},{1... | collective-permute-start | bytes 786440 | tf_op jit(solution)/shard_map/ppermute | solution.py:301
  60.2 15.7 %collective-permute-start.17 = (bf16[128,1536]{1,0:T(8,128)(2,1)S(1)}, bf16[128,1536]{1,0:T(8,128)(2,1)S(1)}, u32[]{:S(2)}, u32[]{:S(2)}) collective-permute-start(bf16[128,1536]{1,0:T(8,128)(2,1)S(1)} %get-tuple-element.76), channel_id=1, source_target_pairs={{0,1},{1,0},{2,3},{3,2},{4,5},{5,4},{6,7},{7,6},{8,9},{9,8},{10,11... | collective-permute-start | bytes 1179656 | tf_op jit(solution)/shard_map/ppermute | solution.py:298
  60.2 15.7 %collective-permute-start.18 = (bf16[128,1536]{1,0:T(8,128)(2,1)S(1)}, bf16[128,1536]{1,0:T(8,128)(2,1)S(1)}, u32[]{:S(2)}, u32[]{:S(2)}) collective-permute-start(bf16[128,1536]{1,0:T(8,128)(2,1)S(1)} %get-tuple-element.78), channel_id=1, source_target_pairs={{0,17},{1,16},{2,19},{3,18},{4,21},{5,20},{6,23},{7,22},{8,25},{9,... | collective-permute-start | bytes 1179656 | tf_op jit(solution)/shard_map/ppermute | solution.py:298
  73.7 9.1 %collective-permute-start.19 = (bf16[128,1024]{1,0:T(8,128)(2,1)S(1)}, bf16[128,1024]{1,0:T(8,128)(2,1)S(1)}, u32[]{:S(2)}, u32[]{:S(2)}) collective-permute-start(bf16[128,1024]{1,0:T(8,128)(2,1)S(1)} %get-tuple-element.81), channel_id=1, source_target_pairs={{0,16},{1,17},{2,18},{3,19},{4,20},{5,21},{6,22},{7,23},{8,24},{9,... | collective-permute-start | bytes 786440 | tf_op jit(solution)/shard_map/ppermute | solution.py:298
  75.3 12.0 %collective-permute-start.20 = (bf16[128,1024]{1,0:T(8,128)(2,1)S(1)}, bf16[128,1024]{1,0:T(8,128)(2,1)S(1)}, u32[]{:S(2)}, u32[]{:S(2)}) collective-permute-start(bf16[128,1024]{1,0:T(8,128)(2,1)S(1)} %get-tuple-element.84), channel_id=1, source_target_pairs={{0,1},{1,0},{2,3},{3,2},{4,5},{5,4},{6,7},{7,6},{8,9},{9,8},{10,11... | collective-permute-start | bytes 786440 | tf_op jit(solution)/shard_map/ppermute | solution.py:298
  75.3 12.4 %collective-permute-start.25 = (bf16[128,1024]{1,0:T(8,128)(2,1)S(1)}, bf16[128,1024]{1,0:T(8,128)(2,1)S(1)}, u32[]{:S(2)}, u32[]{:S(2)}) collective-permute-start(bf16[128,1024]{1,0:T(8,128)(2,1)S(1)} %get-tuple-element.89), channel_id=1, source_target_pairs={{0,17},{1,16},{2,19},{3,18},{4,21},{5,20},{6,23},{7,22},{8,25},{9,... | collective-permute-start | bytes 786440 | tf_op jit(solution)/shard_map/ppermute | solution.py:298
  80.4 7.2 %collective-permute-start.21 = (bf16[128,512]{1,0:T(8,128)(2,1)S(1)}, bf16[128,512]{1,0:T(8,128)(2,1)S(1)}, u32[]{:S(2)}, u32[]{:S(2)}) collective-permute-start(bf16[128,512]{1,0:T(8,128)(2,1)S(1)} %get-tuple-element.85), channel_id=1, source_target_pairs={{0,1},{1,0},{2,3},{3,2},{4,5},{5,4},{6,7},{7,6},{8,9},{9,8},{10,11... | collective-permute-start | bytes 393224 | tf_op jit(solution)/shard_map/ppermute | solution.py:298
  80.5 9.9 %collective-permute-start.23 = (bf16[128,512]{1,0:T(8,128)(2,1)S(1)}, bf16[128,512]{1,0:T(8,128)(2,1)S(1)}, u32[]{:S(2)}, u32[]{:S(2)}) collective-permute-start(bf16[128,512]{1,0:T(8,128)(2,1)S(1)} %get-tuple-element.87), channel_id=1, source_target_pairs={{0,16},{1,17},{2,18},{3,19},{4,20},{5,21},{6,22},{7,23},{8,24},{9,... | collective-permute-start | bytes 393224 | tf_op jit(solution)/shard_map/ppermute | solution.py:298
  82.8 8.2 %collective-permute-start.26 = (bf16[128,512]{1,0:T(8,128)(2,1)S(1)}, bf16[128,512]{1,0:T(8,128)(2,1)S(1)}, u32[]{:S(2)}, u32[]{:S(2)}) collective-permute-start(bf16[128,512]{1,0:T(8,128)(2,1)S(1)} %get-tuple-element.90), channel_id=1, source_target_pairs={{0,17},{1,16},{2,19},{3,18},{4,21},{5,20},{6,23},{7,22},{8,25},{9,... | collective-permute-start | bytes 393224 | tf_op jit(solution)/shard_map/ppermute | solution.py:298
  91.0 15.1 %all-to-all-start = ((bf16[16,16,576]{2,1,0:T(8,128)(2,1)}), bf16[16,16,576]{2,1,0:T(8,128)(2,1)S(1)}, u32[]{:S(2)}, u32[]{:S(2)}) async-start(bf16[16,16,576]{2,1,0:T(8,128)(2,1)} %bitcast.5), calls=%async_computation | async-start | bytes 655360 | tf_op jit(solution)/shard_map/all_to_all | solution.py:475
  95.0 2.0 %collective-permute-start.22 = (bf16[128,512]{1,0:T(8,128)(2,1)S(1)}, bf16[128,512]{1,0:T(8,128)(2,1)S(1)}, u32[]{:S(2)}, u32[]{:S(2)}) collective-permute-start(bf16[128,512]{1,0:T(8,128)(2,1)S(1)} %get-tuple-element.86), channel_id=1, source_target_pairs={{0,1},{1,0},{2,3},{3,2},{4,5},{5,4},{6,7},{7,6},{8,9},{9,8},{10,11... | collective-permute-start | bytes 393224 | tf_op jit(solution)/shard_map/ppermute | solution.py:298
  95.4 6.3 %collective-permute-start.24 = (bf16[128,512]{1,0:T(8,128)(2,1)S(1)}, bf16[128,512]{1,0:T(8,128)(2,1)S(1)}, u32[]{:S(2)}, u32[]{:S(2)}) collective-permute-start(bf16[128,512]{1,0:T(8,128)(2,1)S(1)} %get-tuple-element.88), channel_id=1, source_target_pairs={{0,16},{1,17},{2,18},{3,19},{4,20},{5,21},{6,22},{7,23},{8,24},{9,... | collective-permute-start | bytes 393224 | tf_op jit(solution)/shard_map/ppermute | solution.py:298
  96.9 6.1 %collective-permute-start.27 = (bf16[128,512]{1,0:T(8,128)(2,1)S(1)}, bf16[128,512]{1,0:T(8,128)(2,1)S(1)}, u32[]{:S(2)}, u32[]{:S(2)}) collective-permute-start(bf16[128,512]{1,0:T(8,128)(2,1)S(1)} %get-tuple-element.91), channel_id=1, source_target_pairs={{0,17},{1,16},{2,19},{3,18},{4,21},{5,20},{6,23},{7,22},{8,25},{9,... | collective-permute-start | bytes 393224 | tf_op jit(solution)/shard_map/ppermute | solution.py:298

commit v12 on v11

--- a/solution.py
+++ b/solution.py
@@ -19,10 +19,10 @@
 HQ = H // QUAD
 CHUNK_HEADS = (8, 8)
 PHASES = (
-    ("z", "y0", "k", "q02", "b~", "f~"),
-    ("z", "y1", "q03", "q01"),
-    ("z", "y2", "p", "q12"),
-    ("y3", "w", "q13~", "q11"),
+    ("z", "y0", "k", "b~", "f~"),
+    ("z", "y1", "q02", "q01"),
+    ("z", "y2", "p", "q03"),
+    ("y3", "w", "q12~", "q13~", "q11"),
 )
 CHUNKS = len(CHUNK_HEADS)
 FIRST_HEAD = tuple(sum(CHUNK_HEADS[:j]) for j in range(CHUNKS))

time: 107 us -> 113 us (1.056)
  starting transfers between devices: 33.6 us -> 38.2 us
    ppermute x4, starting transfers between devices: 5.01 us -> 10.1 us  [inner_swap(): return lax.ppermute(array, 'ctx', [(i, i ^ 2) for i in range(size)])]
    ppermute x4, waiting for transfers between devices: 10.9 us -> 9.52 us  [around(): lax.ppermute(array, 'ctx', [(i, (i + by) % size) for i in range(size)])]
  transfers between devices with their start and end apart: 29 -> 29, of which waited for: 15 -> 14; matrix products, arithmetic and copies ran while one was open for 0% -> 1% of each run, Pallas kernels for 24% -> 23%
where the time goes in v12:
time: 113 us; the launch traced here: 112 us
  waiting for transfers between devices  43.9 us (39%)
  starting transfers between devices  38.2 us (34%)
  Pallas kernels  26.5 us (23%)
  local copies, waits for them, and re-layouts  2.98 us (3%)
    ppermute x18, waiting for transfers between devices, quad_swap(): return lax.ppermute(array, ('groups', 'ctx'), pairs)  30 us
    pallas_call x3, Pallas kernels, attend(): pl.pallas_call(functools.partial(attend_kernel, outer), grid=(steps,), ou...  17.9 us
    ppermute x18, starting transfers between devices, quad_swap(): return lax.ppermute(array, ('groups', 'ctx'), pairs)  12.5 us
    ppermute x4, starting transfers between devices, inner_swap(): return lax.ppermute(array, 'ctx', [(i, i ^ 2) for i in range(size)])  10.1 us
    ppermute x4, waiting for transfers between devices, around(): lax.ppermute(array, 'ctx', [(i, (i + by) % size) for i in range(size)])  9.52 us
    ppermute x4, starting transfers between devices, around(): lax.ppermute(array, 'ctx', [(i, (i + by) % size) for i in range(size)])  8.68 us
    all_to_all x1, starting transfers between devices, body(): lax.all_to_all(tie(outgoing, results[-1][0], *before).reshape(size, slot_...  3.85 us
    pallas_call x1, Pallas kernels, body(): pl.pallas_call(query_kernel, out_shape=[shape((tok, h * (NOPE + ROPE))) f...  3.33 us
  transfers between devices with their start and end apart: 29, of which 14 were waited for; matrix products, arithmetic and copies ran while one was open for 1% of the time, Pallas kernels for 23%

profile of v12, /device:TPU:0, one launch (start us, length us, event | category | flops | bytes accessed | tf_op | source)
XLA Modules:
  0.0 112.5 jit_solution(16428745866447924107)
XLA Ops:
  0.6 1.0 constant_dynamic-slice_fusion
  1.6 0.5 collective-permute-start
  2.1 1.2 %collective-permute-done.got = bf16[32,4096]{1,0:T(8,128)(2,1)S(1)} collective-permute-done((bf16[32,4096]{1,0:T(8,128)(2,1)S(1)}, bf16[32,4096]{1,0:T(8,128)(2,1)S(1)}, u32[]{:S(2)}, u32[]{:S(2)}) %collective-permute-start) | collective-permute-done | bytes 262176 | tf_op jit(solution)/shard_map/ppermute | solution.py:298
  3.3 1.0 pair.1.refs_0_
  4.3 3.0 %collective-permute-start.4 = (bf16[64,4096]{1,0:T(8,128)(2,1)S(1)}, bf16[64,4096]{1,0:T(8,128)(2,1)S(1)}, u32[]{:S(2)}, u32[]{:S(2)}) collective-permute-start(bf16[64,4096]{1,0:T(8,128)(2,1)S(1)} %pair.1.refs_0_), channel_id=1, source_target_pairs={{0,4},{1,5},{2,6},{3,7},{4,8},{5,9},{6,10},{7,11},{8,12},{9,13},{1... | collective-permute-start | bytes 1572872 | tf_op jit(solution)/shard_map/ppermute | solution.py:301
  7.3 1.5 %collective-permute-start.5 = (bf16[64,4096]{1,0:T(8,128)(2,1)S(1)}, bf16[64,4096]{1,0:T(8,128)(2,1)S(1)}, u32[]{:S(2)}, u32[]{:S(2)}) collective-permute-start(bf16[64,4096]{1,0:T(8,128)(2,1)S(1)} %pair.1.refs_0_), channel_id=1, source_target_pairs={{0,2},{1,3},{2,0},{3,1},{4,6},{5,7},{6,4},{7,5},{8,10},{9,11},{10,... | collective-permute-start | bytes 1572872 | tf_op jit(solution)/shard_map/ppermute | solution.py:304
  8.8 2.3 %rows.1 = (bf16[128,640]{1,0:T(8,128)(2,1)}, f32[128,128]{1,0:T(8,128)}, f32[128,128]{1,0:T(8,128)}, bf16[256,576]{1,0:T(8,128)(2,1)}) custom-call(s32[1]{0:T(128)} %bitcast.1.info, s32[8]{0:T(128)} %lengths, bf16[576,128]{1,0:T(8,128)(2,1)} %bitcast.8, f32[1,512]{1,0:T(1,128)} %bitcast.9, s32[1,128]{1,0:T(1,128)} %bitcast.10, f32[1,128]{1,0:T(1,128)} %constant.30.clone.freq), custom_call_target="tpu_custom_call" | custom-call | tf_op jit(solution)/shard_map/rows/pallas_call | solution.py:345
  11.1 1.5 %collective-permute-start.1 = (bf16[128,640]{1,0:T(8,128)(2,1)}, bf16[128,640]{1,0:T(8,128)(2,1)S(1)}, u32[]{:S(2)}, u32[]{:S(2)}) collective-permute-start(bf16[128,640]{1,0:T(8,128)(2,1)} %get-tuple-element.52), channel_id=1, source_target_pairs={{0,16},{1,17},{2,18},{3,19},{4,20},{5,21},{6,22},{7,23},{8,24},{9,... | collective-permute-start | bytes 491528 | tf_op jit(solution)/shard_map/ppermute | solution.py:298
  12.6 1.0 constant_dynamic-update-slice_fusion.1
  13.6 3.4 %collective-permute-done.1 = bf16[128,640]{1,0:T(8,128)(2,1)S(1)} collective-permute-done((bf16[128,640]{1,0:T(8,128)(2,1)}, bf16[128,640]{1,0:T(8,128)(2,1)S(1)}, u32[]{:S(2)}, u32[]{:S(2)}) %collective-permute-start.1) | collective-permute-done | bytes 163872 | tf_op jit(solution)/shard_map/ppermute | solution.py:298
  17.0 2.4 %collective-permute-start.2 = (bf16[256,640]{1,0:T(8,128)(2,1)S(1)}, bf16[256,640]{1,0:T(8,128)(2,1)S(1)}, u32[]{:S(2)}, u32[]{:S(2)}) collective-permute-start(bf16[256,640]{1,0:T(8,128)(2,1)S(1)} %get-tuple-element.98), channel_id=1, source_target_pairs={{0,2},{1,3},{2,4},{3,5},{4,6},{5,7},{6,8},{7,9},{8,10},{9,11},{10,... | collective-permute-start | bytes 983048 | tf_op jit(solution)/shard_map/ppermute | solution.py:310
  19.5 3.3 %queries.1 = (bf16[128,1536]{1,0:T(8,128)(2,1)S(1)}, bf16[128,1536]{1,0:T(8,128)(2,1)S(1)}, bf16[128,1536]{1,0:T(8,128)(2,1)S(1)}, bf16[128,1536]{1,0:T(8,128)(2...) custom-call(s32[1]{0:T(128)} %bitcast.info, ...), custom_call_target="tpu_custom_call" | custom-call | bytes 6291456 | tf_op jit(solution)/shard_map/queries/pallas_call | solution.py:369
  22.8 0.0 collective-permute-done.4.refs_1_
  22.8 0.0 collective-permute-done.5.refs_4_
  22.8 1.6 %collective-permute-start.6 = (bf16[64,4096]{1,0:T(8,128)(2,1)S(1)}, bf16[64,4096]{1,0:T(8,128)(2,1)S(1)}, u32[]{:S(2)}, u32[]{:S(2)}) collective-permute-start(bf16[64,4096]{1,0:T(8,128)(2,1)S(1)} %collective-permute-done.4.refs_1_), channel_id=1, source_target_pairs={{0,4},{1,5},{2,6},{3,7},{4,8},{5,9},{6,10},{7,11},{8,12},{9,13},{1... | collective-permute-start | bytes 1572872 | tf_op jit(solution)/shard_map/ppermute | solution.py:301
  24.5 2.5 %collective-permute-start.7 = (bf16[64,4096]{1,0:T(8,128)(2,1)S(1)}, bf16[64,4096]{1,0:T(8,128)(2,1)S(1)}, u32[]{:S(2)}, u32[]{:S(2)}) collective-permute-start(bf16[64,4096]{1,0:T(8,128)(2,1)S(1)} %collective-permute-done.4.refs_1_), channel_id=1, source_target_pairs={{0,2},{1,3},{2,0},{3,1},{4,6},{5,7},{6,4},{7,5},{8,10},{9,11},{10,... | collective-permute-start | bytes 1572872 | tf_op jit(solution)/shard_map/ppermute | solution.py:304
  27.0 0.7 collective-permute-start.3
  27.7 1.6 %collective-permute-start.8 = (bf16[128,1536]{1,0:T(8,128)(2,1)S(1)}, bf16[128,1536]{1,0:T(8,128)(2,1)S(1)}, u32[]{:S(2)}, u32[]{:S(2)}) collective-permute-start(bf16[128,1536]{1,0:T(8,128)(2,1)S(1)} %get-tuple-element.59), channel_id=1, source_target_pairs={{0,16},{1,17},{2,18},{3,19},{4,20},{5,21},{6,22},{7,23},{8,24},{9,... | collective-permute-start | bytes 1179656 | tf_op jit(solution)/shard_map/ppermute | solution.py:298
  29.2 0.0 collective-permute-done.2
  29.2 0.0 collective-permute-start.9
  29.3 0.0 collective-permute-done.3
  29.3 8.7 %collective-permute-done.8.refs_10_.refs_14_ = bf16[128,1536]{1,0:T(8,128)(2,1)S(1)} collective-permute-done((bf16[128,1536]{1,0:T(8,128)(2,1)S(1)}, bf16[128,1536]{1,0:T(8,128)(2,1)S(1)}, u32[]{:S(2)}, u32[]{:S(2)}) %collective-permute-start.8) | collective-permute-done | bytes 393248 | tf_op jit(solution)/shard_map/ppermute | solution.py:298
  38.0 0.0 collective-permute-done.9.refs_9_.refs_13_
  38.1 0.0 collective-permute-done.6.refs_2_
  38.1 0.2 collective-permute-done.7.refs_5_
  38.3 0.0 collective-permute-start.10
  38.3 2.7 %collective-permute-start.11 = (bf16[64,4096]{1,0:T(8,128)(2,1)S(1)}, bf16[64,4096]{1,0:T(8,128)(2,1)S(1)}, u32[]{:S(2)}, u32[]{:S(2)}) collective-permute-start(bf16[64,4096]{1,0:T(8,128)(2,1)S(1)} %collective-permute-done.6.refs_2_), channel_id=1, source_target_pairs={{0,4},{1,5},{2,6},{3,7},{4,8},{5,9},{6,10},{7,11},{8,12},{9,13},{1... | collective-permute-start | bytes 1572872 | tf_op jit(solution)/shard_map/ppermute | solution.py:301
  40.9 4.0 %collective-permute-start.12 = (bf16[64,4096]{1,0:T(8,128)(2,1)S(1)}, bf16[64,4096]{1,0:T(8,128)(2,1)S(1)}, u32[]{:S(2)}, u32[]{:S(2)}) collective-permute-start(bf16[64,4096]{1,0:T(8,128)(2,1)S(1)} %collective-permute-done.6.refs_2_), channel_id=1, source_target_pairs={{0,2},{1,3},{2,0},{3,1},{4,6},{5,7},{6,4},{7,5},{8,10},{9,11},{10,... | collective-permute-start | bytes 1572872 | tf_op jit(solution)/shard_map/ppermute | solution.py:304
  45.0 0.6 collective-permute-start.13
  45.6 9.5 %collective-permute-done.11.refs_3_ = bf16[64,4096]{1,0:T(8,128)(2,1)S(1)} collective-permute-done((bf16[64,4096]{1,0:T(8,128)(2,1)S(1)}, bf16[64,4096]{1,0:T(8,128)(2,1)S(1)}, u32[]{:S(2)}, u32[]{:S(2)}) %collective-permute-start.11) | collective-permute-done | bytes 524320 | tf_op jit(solution)/shard_map/ppermute | solution.py:301
  55.1 1.2 %collective-permute-done.13.refs_11_.refs_15_ = bf16[128,1536]{1,0:T(8,128)(2,1)S(1)} collective-permute-done((bf16[128,1536]{1,0:T(8,128)(2,1)S(1)}, bf16[128,1536]{1,0:T(8,128)(2,1)S(1)}, u32[]{:S(2)}, u32[]{:S(2)}) %collective-permute-start.13) | collective-permute-done | bytes 393248 | tf_op jit(solution)/shard_map/ppermute | solution.py:298
  56.3 0.5 collective-permute-done.12.refs_6_
  56.8 0.0 collective-permute-done.10.other
  56.8 2.0 %collective-permute-start.14 = (bf16[64,2048]{1,0:T(8,128)(2,1)S(1)}, bf16[64,2048]{1,0:T(8,128)(2,1)S(1)}, u32[]{:S(2)}, u32[]{:S(2)}) collective-permute-start(bf16[64,2048]{1,0:T(8,128)(2,1)S(1)} %slice.8), channel_id=1, source_target_pairs={{0,2},{1,3},{2,0},{3,1},{4,6},{5,7},{6,4},{7,5},{8,10},{9,11},{10,... | collective-permute-start | bytes 786440 | tf_op jit(solution)/shard_map/ppermute | solution.py:304
  58.8 1.4 %collective-permute-start.15 = (bf16[64,2048]{1,0:T(8,128)(2,1)S(1)}, bf16[64,2048]{1,0:T(8,128)(2,1)S(1)}, u32[]{:S(2)}, u32[]{:S(2)}) collective-permute-start(bf16[64,2048]{1,0:T(8,128)(2,1)S(1)} %slice.9), channel_id=1, source_target_pairs={{0,4},{1,5},{2,6},{3,7},{4,8},{5,9},{6,10},{7,11},{8,12},{9,13},{1... | collective-permute-start | bytes 786440 | tf_op jit(solution)/shard_map/ppermute | solution.py:301
  60.2 0.0 collective-permute-start.16
  60.2 1.5 %collective-permute-start.17 = (bf16[128,1536]{1,0:T(8,128)(2,1)S(1)}, bf16[128,1536]{1,0:T(8,128)(2,1)S(1)}, u32[]{:S(2)}, u32[]{:S(2)}) collective-permute-start(bf16[128,1536]{1,0:T(8,128)(2,1)S(1)} %get-tuple-element.78), channel_id=1, source_target_pairs={{0,16},{1,17},{2,18},{3,19},{4,20},{5,21},{6,22},{7,23},{8,24},{9,... | collective-permute-start | bytes 1179656 | tf_op jit(solution)/shard_map/ppermute | solution.py:298
  61.7 0.4 collective-permute-start.18
  62.1 0.6 keys.1
  62.7 2.0 %collective-permute-done.14.refs_7_ = bf16[64,2048]{1,0:T(8,128)(2,1)S(1)} collective-permute-done((bf16[64,2048]{1,0:T(8,128)(2,1)S(1)}, bf16[64,2048]{1,0:T(8,128)(2,1)S(1)}, u32[]{:S(2)}, u32[]{:S(2)}) %collective-permute-start.14) | collective-permute-done | bytes 262176 | tf_op jit(solution)/shard_map/ppermute | solution.py:304
  64.7 8.9 %attend.3 = (bf16[128,1024]{1,0:T(8,128)(2,1)S(1)}, bf16[128,1024]{1,0:T(8,128)(2,1)S(1)}, bf16[128,1024]{1,0:T(8,128)(2,1)S(1)}, bf16[128,1024]{1,0:T(8,128)(2,1)S(1)}) custom-call(s32[1]{0:T(128)} %bitcast.1.info, bf16[2,640,512]{2,1,0:T(8,128)(2,1)S(1)} %get-tuple-element.63.latent, bf16[2,640,128]{2,1,0:T(8,128)(2,1)S(1)} %get-tuple-element.64.rope_even, ...), custom_call_target="tpu_custom_call" | custom-call | flops 4362076160 | bytes 8388608 | tf_op jit(solution)/shard_map/attend/pallas_call | solution.py:444
  73.7 1.6 %collective-permute-start.19 = (bf16[128,1024]{1,0:T(8,128)(2,1)S(1)}, bf16[128,1024]{1,0:T(8,128)(2,1)S(1)}, u32[]{:S(2)}, u32[]{:S(2)}) collective-permute-start(bf16[128,1024]{1,0:T(8,128)(2,1)S(1)} %get-tuple-element.83), channel_id=1, source_target_pairs={{0,16},{1,17},{2,18},{3,19},{4,20},{5,21},{6,22},{7,23},{8,24},{9,... | collective-permute-start | bytes 786440 | tf_op jit(solution)/shard_map/ppermute | solution.py:298
  75.3 0.0 collective-permute-done.15.refs_7_
  75.3 0.0 collective-permute-done.16.refs_9_.refs_13_
  75.3 0.6 collective-permute-start.25
  75.9 3.9 %collective-permute-done.18.refs_11_.refs_15_ = bf16[128,1536]{1,0:T(8,128)(2,1)S(1)} collective-permute-done((bf16[128,1536]{1,0:T(8,128)(2,1)S(1)}, bf16[128,1536]{1,0:T(8,128)(2,1)S(1)}, u32[]{:S(2)}, u32[]{:S(2)}) %collective-permute-start.18) | collective-permute-done | bytes 393248 | tf_op jit(solution)/shard_map/ppermute | solution.py:298
  79.8 4.5 %attend.4 = (bf16[128,512]{1,0:T(8,128)(2,1)S(1)}, bf16[128,512]{1,0:T(8,128)(2,1)S(1)}, bf16[128,512]{1,0:T(8,128)(2,1)S(1)}, bf16[128,512]{1,0:T(8,128)(2,1)S(1)}) custom-call(s32[1]{0:T(128)} %bitcast.1.info, bf16[2,640,512]{2,1,0:T(8,128)(2,1)S(1)} %get-tuple-element.63.latent, bf16[2,640,128]{2,1,0:T(8,128)(2,1)S(1)} %get-tuple-element.64.rope_even, ...), custom_call_target="tpu_custom_call" | custom-call | flops 2181038080 | bytes 4194304 | tf_op jit(solution)/shard_map/attend/pallas_call | solution.py:444
  84.3 0.7 collective-permute-start.21
  85.0 1.5 %collective-permute-start.23 = (bf16[128,512]{1,0:T(8,128)(2,1)S(1)}, bf16[128,512]{1,0:T(8,128)(2,1)S(1)}, u32[]{:S(2)}, u32[]{:S(2)}) collective-permute-start(bf16[128,512]{1,0:T(8,128)(2,1)S(1)} %get-tuple-element.89), channel_id=1, source_target_pairs={{0,16},{1,17},{2,18},{3,19},{4,20},{5,21},{6,22},{7,23},{8,24},{9,... | collective-permute-start | bytes 393224 | tf_op jit(solution)/shard_map/ppermute | solution.py:298
  86.5 0.2 collective-permute-start.26
  86.6 4.5 %attend.5 = (bf16[128,512]{1,0:T(8,128)(2,1)S(1)}, bf16[128,512]{1,0:T(8,128)(2,1)S(1)}, bf16[128,512]{1,0:T(8,128)(2,1)S(1)}, bf16[128,512]{1,0:T(8,128)(2,1)S(1)}) custom-call(s32[1]{0:T(128)} %bitcast.1.info, bf16[2,640,512]{2,1,0:T(8,128)(2,1)S(1)} %get-tuple-element.63.latent, bf16[2,640,128]{2,1,0:T(8,128)(2,1)S(1)} %get-tuple-element.64.rope_even, ...), custom_call_target="tpu_custom_call" | custom-call | flops 2181038080 | bytes 4194304 | tf_op jit(solution)/shard_map/attend/pallas_call | solution.py:444
  91.2 0.0 collective-permute-done.20.refs_3_
  91.2 0.0 collective-permute-done.25.refs_9_
  91.2 3.4 %collective-permute-done.23.refs_7_ = bf16[128,512]{1,0:T(8,128)(2,1)S(1)} collective-permute-done((bf16[128,512]{1,0:T(8,128)(2,1)S(1)}, bf16[128,512]{1,0:T(8,128)(2,1)S(1)}, u32[]{:S(2)}, u32[]{:S(2)}) %collective-permute-start.23) | collective-permute-done | bytes 131104 | tf_op jit(solution)/shard_map/ppermute | solution.py:298
  94.6 2.0 %collective-permute-done.26.refs_10_ = bf16[128,512]{1,0:T(8,128)(2,1)S(1)} collective-permute-done((bf16[128,512]{1,0:T(8,128)(2,1)S(1)}, bf16[128,512]{1,0:T(8,128)(2,1)S(1)}, u32[]{:S(2)}, u32[]{:S(2)}) %collective-permute-start.26) | collective-permute-done | bytes 131104 | tf_op jit(solution)/shard_map/ppermute | solution.py:298
  96.7 3.8 %all-to-all-start = ((bf16[16,16,576]{2,1,0:T(8,128)(2,1)}), bf16[16,16,576]{2,1,0:T(8,128)(2,1)S(1)}, u32[]{:S(2)}, u32[]{:S(2)}) async-start(bf16[16,16,576]{2,1,0:T(8,128)(2,1)} %bitcast.5), calls=%async_computation | async-start | bytes 655360 | tf_op jit(solution)/shard_map/all_to_all | solution.py:475
  100.5 0.4 collective-permute-start.22
  100.9 1.5 %collective-permute-start.24 = (bf16[128,512]{1,0:T(8,128)(2,1)S(1)}, bf16[128,512]{1,0:T(8,128)(2,1)S(1)}, u32[]{:S(2)}, u32[]{:S(2)}) collective-permute-start(bf16[128,512]{1,0:T(8,128)(2,1)S(1)} %get-tuple-element.90), channel_id=1, source_target_pairs={{0,16},{1,17},{2,18},{3,19},{4,20},{5,21},{6,22},{7,23},{8,24},{9,... | collective-permute-start | bytes 393224 | tf_op jit(solution)/shard_map/ppermute | solution.py:298
  102.4 0.0 collective-permute-start.27
  102.5 4.8 %collective-permute-done.24.refs_8_ = bf16[128,512]{1,0:T(8,128)(2,1)S(1)} collective-permute-done((bf16[128,512]{1,0:T(8,128)(2,1)S(1)}, bf16[128,512]{1,0:T(8,128)(2,1)S(1)}, u32[]{:S(2)}, u32[]{:S(2)}) %collective-permute-start.24) | collective-permute-done | bytes 131104 | tf_op jit(solution)/shard_map/ppermute | solution.py:298
  107.3 1.3 %collective-permute-done.27.refs_11_ = bf16[128,512]{1,0:T(8,128)(2,1)S(1)} collective-permute-done((bf16[128,512]{1,0:T(8,128)(2,1)S(1)}, bf16[128,512]{1,0:T(8,128)(2,1)S(1)}, u32[]{:S(2)}, u32[]{:S(2)}) %collective-permute-start.27) | collective-permute-done | bytes 131104 | tf_op jit(solution)/shard_map/ppermute | solution.py:298
  108.5 1.4 %place.1 = bf16[128,8192]{1,0:T(8,128)(2,1)} custom-call(s32[1]{0:T(128)} %bitcast.info, bf16[128,1024]{1,0:T(8,128)(2,1)S(1)} %get-tuple-element.71.refs_0_, bf16[128,512]{1,0:T(8,128)(2,1)S(1)} %get-tuple-element.81.refs_1_, bf16[128,512]{1,0:T(8,128)(2,1)S(1)} %get-tuple-element.85.refs_2_, bf16[128,1024]{1,0:T(8,128)(2,1)S(1)} %collective-permute-done.20.refs_3_, ...), custom_call_target="tpu_custom_call" | custom-call | tf_op jit(solution)/shard_map/place/pallas_call | solution.py:483
  109.9 1.7 %all-to-all-done = bf16[16,16,576]{2,1,0:T(8,128)(2,1)S(1)} async-done(((bf16[16,16,576]{2,1,0:T(8,128)(2,1)}), bf16[16,16,576]{2,1,0:T(8,128)(2,1)S(1)}, u32[]{:S(2)}, u32[]{:S(2)}) %all-to-all-start) | async-done | bytes 294944 | tf_op jit(solution)/shard_map/all_to_all | solution.py:475
  111.6 0.9 copy.10
  (10 shorter events, 0.2 us)
Async XLA Ops:
  1.6 1.7 %collective-permute-start = (bf16[32,4096]{1,0:T(8,128)(2,1)S(1)}, bf16[32,4096]{1,0:T(8,128)(2,1)S(1)}, u32[]{:S(2)}, u32[]{:S(2)}) collective-permute-start(bf16[32,4096]{1,0:T(8,128)(2,1)S(1)} %constant_dynamic-slice_fusion), channel_id=1, source_target_pairs={{0,1},{1,0},{2,3},{3,2},{4,5},{5,4},{6,7},{7,6},{8,9},{9,8},{10,11... | collective-permute-start | bytes 786440 | tf_op jit(solution)/shard_map/ppermute | solution.py:298
  4.3 18.5 %collective-permute-start.4 = (bf16[64,4096]{1,0:T(8,128)(2,1)S(1)}, bf16[64,4096]{1,0:T(8,128)(2,1)S(1)}, u32[]{:S(2)}, u32[]{:S(2)}) collective-permute-start(bf16[64,4096]{1,0:T(8,128)(2,1)S(1)} %pair.1.refs_0_), channel_id=1, source_target_pairs={{0,4},{1,5},{2,6},{3,7},{4,8},{5,9},{6,10},{7,11},{8,12},{9,13},{1... | collective-permute-start | bytes 1572872 | tf_op jit(solution)/shard_map/ppermute | solution.py:301
  7.3 15.6 %collective-permute-start.5 = (bf16[64,4096]{1,0:T(8,128)(2,1)S(1)}, bf16[64,4096]{1,0:T(8,128)(2,1)S(1)}, u32[]{:S(2)}, u32[]{:S(2)}) collective-permute-start(bf16[64,4096]{1,0:T(8,128)(2,1)S(1)} %pair.1.refs_0_), channel_id=1, source_target_pairs={{0,2},{1,3},{2,0},{3,1},{4,6},{5,7},{6,4},{7,5},{8,10},{9,11},{10,... | collective-permute-start | bytes 1572872 | tf_op jit(solution)/shard_map/ppermute | solution.py:304
  11.1 5.9 %collective-permute-start.1 = (bf16[128,640]{1,0:T(8,128)(2,1)}, bf16[128,640]{1,0:T(8,128)(2,1)S(1)}, u32[]{:S(2)}, u32[]{:S(2)}) collective-permute-start(bf16[128,640]{1,0:T(8,128)(2,1)} %get-tuple-element.52), channel_id=1, source_target_pairs={{0,16},{1,17},{2,18},{3,19},{4,20},{5,21},{6,22},{7,23},{8,24},{9,... | collective-permute-start | bytes 491528 | tf_op jit(solution)/shard_map/ppermute | solution.py:298
  17.0 12.2 %collective-permute-start.2 = (bf16[256,640]{1,0:T(8,128)(2,1)S(1)}, bf16[256,640]{1,0:T(8,128)(2,1)S(1)}, u32[]{:S(2)}, u32[]{:S(2)}) collective-permute-start(bf16[256,640]{1,0:T(8,128)(2,1)S(1)} %get-tuple-element.98), channel_id=1, source_target_pairs={{0,2},{1,3},{2,4},{3,5},{4,6},{5,7},{6,8},{7,9},{8,10},{9,11},{10,... | collective-permute-start | bytes 983048 | tf_op jit(solution)/shard_map/ppermute | solution.py:310
  22.8 15.2 %collective-permute-start.6 = (bf16[64,4096]{1,0:T(8,128)(2,1)S(1)}, bf16[64,4096]{1,0:T(8,128)(2,1)S(1)}, u32[]{:S(2)}, u32[]{:S(2)}) collective-permute-start(bf16[64,4096]{1,0:T(8,128)(2,1)S(1)} %collective-permute-done.4.refs_1_), channel_id=1, source_target_pairs={{0,4},{1,5},{2,6},{3,7},{4,8},{5,9},{6,10},{7,11},{8,12},{9,13},{1... | collective-permute-start | bytes 1572872 | tf_op jit(solution)/shard_map/ppermute | solution.py:301
  24.5 13.8 %collective-permute-start.7 = (bf16[64,4096]{1,0:T(8,128)(2,1)S(1)}, bf16[64,4096]{1,0:T(8,128)(2,1)S(1)}, u32[]{:S(2)}, u32[]{:S(2)}) collective-permute-start(bf16[64,4096]{1,0:T(8,128)(2,1)S(1)} %collective-permute-done.4.refs_1_), channel_id=1, source_target_pairs={{0,2},{1,3},{2,0},{3,1},{4,6},{5,7},{6,4},{7,5},{8,10},{9,11},{10,... | collective-permute-start | bytes 1572872 | tf_op jit(solution)/shard_map/ppermute | solution.py:304
  27.0 2.3 %collective-permute-start.3 = (bf16[256,640]{1,0:T(8,128)(2,1)S(1)}, bf16[256,640]{1,0:T(8,128)(2,1)S(1)}, u32[]{:S(2)}, u32[]{:S(2)}) collective-permute-start(bf16[256,640]{1,0:T(8,128)(2,1)S(1)} %get-tuple-element.98), channel_id=1, source_target_pairs={{1,5},{3,7},{5,9},{7,11},{9,13},{11,15},{17,21},{19,23},{21,25},{2... | collective-permute-start | bytes 983048 | tf_op jit(solution)/shard_map/ppermute | solution.py:310
  27.7 10.4 %collective-permute-start.8 = (bf16[128,1536]{1,0:T(8,128)(2,1)S(1)}, bf16[128,1536]{1,0:T(8,128)(2,1)S(1)}, u32[]{:S(2)}, u32[]{:S(2)}) collective-permute-start(bf16[128,1536]{1,0:T(8,128)(2,1)S(1)} %get-tuple-element.59), channel_id=1, source_target_pairs={{0,16},{1,17},{2,18},{3,19},{4,20},{5,21},{6,22},{7,23},{8,24},{9,... | collective-permute-start | bytes 1179656 | tf_op jit(solution)/shard_map/ppermute | solution.py:298
  29.2 8.8 %collective-permute-start.9 = (bf16[128,1536]{1,0:T(8,128)(2,1)S(1)}, bf16[128,1536]{1,0:T(8,128)(2,1)S(1)}, u32[]{:S(2)}, u32[]{:S(2)}) collective-permute-start(bf16[128,1536]{1,0:T(8,128)(2,1)S(1)} %get-tuple-element.61), channel_id=1, source_target_pairs={{0,1},{1,0},{2,3},{3,2},{4,5},{5,4},{6,7},{7,6},{8,9},{9,8},{10,11... | collective-permute-start | bytes 1179656 | tf_op jit(solution)/shard_map/ppermute | solution.py:298
  38.3 18.6 %collective-permute-start.10 = (bf16[768,640]{1,0:T(8,128)(2,1)S(1)}, bf16[768,640]{1,0:T(8,128)(2,1)S(1)}, u32[]{:S(2)}, u32[]{:S(2)}) collective-permute-start(bf16[768,640]{1,0:T(8,128)(2,1)S(1)} %constant_dynamic-update-slice_fusion.2.own), channel_id=1, source_target_pairs={{0,1},{1,0},{2,3},{3,2},{4,5},{5,4},{6,7},{7,6},{8,9},{9,8},{10,11... | collective-permute-start | bytes 2949128 | tf_op jit(solution)/shard_map/ppermute | solution.py:298
  38.3 16.8 %collective-permute-start.11 = (bf16[64,4096]{1,0:T(8,128)(2,1)S(1)}, bf16[64,4096]{1,0:T(8,128)(2,1)S(1)}, u32[]{:S(2)}, u32[]{:S(2)}) collective-permute-start(bf16[64,4096]{1,0:T(8,128)(2,1)S(1)} %collective-permute-done.6.refs_2_), channel_id=1, source_target_pairs={{0,4},{1,5},{2,6},{3,7},{4,8},{5,9},{6,10},{7,11},{8,12},{9,13},{1... | collective-permute-start | bytes 1572872 | tf_op jit(solution)/shard_map/ppermute | solution.py:301
  40.9 15.9 %collective-permute-start.12 = (bf16[64,4096]{1,0:T(8,128)(2,1)S(1)}, bf16[64,4096]{1,0:T(8,128)(2,1)S(1)}, u32[]{:S(2)}, u32[]{:S(2)}) collective-permute-start(bf16[64,4096]{1,0:T(8,128)(2,1)S(1)} %collective-permute-done.6.refs_2_), channel_id=1, source_target_pairs={{0,2},{1,3},{2,0},{3,1},{4,6},{5,7},{6,4},{7,5},{8,10},{9,11},{10,... | collective-permute-start | bytes 1572872 | tf_op jit(solution)/shard_map/ppermute | solution.py:304
  45.0 11.4 %collective-permute-start.13 = (bf16[128,1536]{1,0:T(8,128)(2,1)S(1)}, bf16[128,1536]{1,0:T(8,128)(2,1)S(1)}, u32[]{:S(2)}, u32[]{:S(2)}) collective-permute-start(bf16[128,1536]{1,0:T(8,128)(2,1)S(1)} %get-tuple-element.69), channel_id=1, source_target_pairs={{0,17},{1,16},{2,19},{3,18},{4,21},{5,20},{6,23},{7,22},{8,25},{9,... | collective-permute-start | bytes 1179656 | tf_op jit(solution)/shard_map/ppermute | solution.py:298
  56.8 7.9 %collective-permute-start.14 = (bf16[64,2048]{1,0:T(8,128)(2,1)S(1)}, bf16[64,2048]{1,0:T(8,128)(2,1)S(1)}, u32[]{:S(2)}, u32[]{:S(2)}) collective-permute-start(bf16[64,2048]{1,0:T(8,128)(2,1)S(1)} %slice.8), channel_id=1, source_target_pairs={{0,2},{1,3},{2,0},{3,1},{4,6},{5,7},{6,4},{7,5},{8,10},{9,11},{10,... | collective-permute-start | bytes 786440 | tf_op jit(solution)/shard_map/ppermute | solution.py:304
  58.8 16.4 %collective-permute-start.15 = (bf16[64,2048]{1,0:T(8,128)(2,1)S(1)}, bf16[64,2048]{1,0:T(8,128)(2,1)S(1)}, u32[]{:S(2)}, u32[]{:S(2)}) collective-permute-start(bf16[64,2048]{1,0:T(8,128)(2,1)S(1)} %slice.9), channel_id=1, source_target_pairs={{0,4},{1,5},{2,6},{3,7},{4,8},{5,9},{6,10},{7,11},{8,12},{9,13},{1... | collective-permute-start | bytes 786440 | tf_op jit(solution)/shard_map/ppermute | solution.py:301
  60.2 15.0 %collective-permute-start.16 = (bf16[128,1536]{1,0:T(8,128)(2,1)S(1)}, bf16[128,1536]{1,0:T(8,128)(2,1)S(1)}, u32[]{:S(2)}, u32[]{:S(2)}) collective-permute-start(bf16[128,1536]{1,0:T(8,128)(2,1)S(1)} %get-tuple-element.76), channel_id=1, source_target_pairs={{0,1},{1,0},{2,3},{3,2},{4,5},{5,4},{6,7},{7,6},{8,9},{9,8},{10,11... | collective-permute-start | bytes 1179656 | tf_op jit(solution)/shard_map/ppermute | solution.py:298
  60.2 15.7 %collective-permute-start.17 = (bf16[128,1536]{1,0:T(8,128)(2,1)S(1)}, bf16[128,1536]{1,0:T(8,128)(2,1)S(1)}, u32[]{:S(2)}, u32[]{:S(2)}) collective-permute-start(bf16[128,1536]{1,0:T(8,128)(2,1)S(1)} %get-tuple-element.78), channel_id=1, source_target_pairs={{0,16},{1,17},{2,18},{3,19},{4,20},{5,21},{6,22},{7,23},{8,24},{9,... | collective-permute-start | bytes 1179656 | tf_op jit(solution)/shard_map/ppermute | solution.py:298
  61.7 18.1 %collective-permute-start.18 = (bf16[128,1536]{1,0:T(8,128)(2,1)S(1)}, bf16[128,1536]{1,0:T(8,128)(2,1)S(1)}, u32[]{:S(2)}, u32[]{:S(2)}) collective-permute-start(bf16[128,1536]{1,0:T(8,128)(2,1)S(1)} %get-tuple-element.80), channel_id=1, source_target_pairs={{0,17},{1,16},{2,19},{3,18},{4,21},{5,20},{6,23},{7,22},{8,25},{9,... | collective-permute-start | bytes 1179656 | tf_op jit(solution)/shard_map/ppermute | solution.py:298
  73.7 12.8 %collective-permute-start.19 = (bf16[128,1024]{1,0:T(8,128)(2,1)S(1)}, bf16[128,1024]{1,0:T(8,128)(2,1)S(1)}, u32[]{:S(2)}, u32[]{:S(2)}) collective-permute-start(bf16[128,1024]{1,0:T(8,128)(2,1)S(1)} %get-tuple-element.83), channel_id=1, source_target_pairs={{0,16},{1,17},{2,18},{3,19},{4,20},{5,21},{6,22},{7,23},{8,24},{9,... | collective-permute-start | bytes 786440 | tf_op jit(solution)/shard_map/ppermute | solution.py:298
  75.3 15.9 %collective-permute-start.20 = (bf16[128,1024]{1,0:T(8,128)(2,1)S(1)}, bf16[128,1024]{1,0:T(8,128)(2,1)S(1)}, u32[]{:S(2)}, u32[]{:S(2)}) collective-permute-start(bf16[128,1024]{1,0:T(8,128)(2,1)S(1)} %get-tuple-element.86), channel_id=1, source_target_pairs={{0,1},{1,0},{2,3},{3,2},{4,5},{5,4},{6,7},{7,6},{8,9},{9,8},{10,11... | collective-permute-start | bytes 786440 | tf_op jit(solution)/shard_map/ppermute | solution.py:298
  75.3 15.9 %collective-permute-start.25 = (bf16[128,1024]{1,0:T(8,128)(2,1)S(1)}, bf16[128,1024]{1,0:T(8,128)(2,1)S(1)}, u32[]{:S(2)}, u32[]{:S(2)}) collective-permute-start(bf16[128,1024]{1,0:T(8,128)(2,1)S(1)} %get-tuple-element.91), channel_id=1, source_target_pairs={{0,17},{1,16},{2,19},{3,18},{4,21},{5,20},{6,23},{7,22},{8,25},{9,... | collective-permute-start | bytes 786440 | tf_op jit(solution)/shard_map/ppermute | solution.py:298
  84.3 6.9 %collective-permute-start.21 = (bf16[128,512]{1,0:T(8,128)(2,1)S(1)}, bf16[128,512]{1,0:T(8,128)(2,1)S(1)}, u32[]{:S(2)}, u32[]{:S(2)}) collective-permute-start(bf16[128,512]{1,0:T(8,128)(2,1)S(1)} %get-tuple-element.87), channel_id=1, source_target_pairs={{0,1},{1,0},{2,3},{3,2},{4,5},{5,4},{6,7},{7,6},{8,9},{9,8},{10,11... | collective-permute-start | bytes 393224 | tf_op jit(solution)/shard_map/ppermute | solution.py:298
  85.0 9.7 %collective-permute-start.23 = (bf16[128,512]{1,0:T(8,128)(2,1)S(1)}, bf16[128,512]{1,0:T(8,128)(2,1)S(1)}, u32[]{:S(2)}, u32[]{:S(2)}) collective-permute-start(bf16[128,512]{1,0:T(8,128)(2,1)S(1)} %get-tuple-element.89), channel_id=1, source_target_pairs={{0,16},{1,17},{2,18},{3,19},{4,20},{5,21},{6,22},{7,23},{8,24},{9,... | collective-permute-start | bytes 393224 | tf_op jit(solution)/shard_map/ppermute | solution.py:298
  86.5 10.2 %collective-permute-start.26 = (bf16[128,512]{1,0:T(8,128)(2,1)S(1)}, bf16[128,512]{1,0:T(8,128)(2,1)S(1)}, u32[]{:S(2)}, u32[]{:S(2)}) collective-permute-start(bf16[128,512]{1,0:T(8,128)(2,1)S(1)} %get-tuple-element.92), channel_id=1, source_target_pairs={{0,17},{1,16},{2,19},{3,18},{4,21},{5,20},{6,23},{7,22},{8,25},{9,... | collective-permute-start | bytes 393224 | tf_op jit(solution)/shard_map/ppermute | solution.py:298
  96.7 15.0 %all-to-all-start = ((bf16[16,16,576]{2,1,0:T(8,128)(2,1)}), bf16[16,16,576]{2,1,0:T(8,128)(2,1)S(1)}, u32[]{:S(2)}, u32[]{:S(2)}) async-start(bf16[16,16,576]{2,1,0:T(8,128)(2,1)} %bitcast.5), calls=%async_computation | async-start | bytes 655360 | tf_op jit(solution)/shard_map/all_to_all | solution.py:475
  100.5 1.9 %collective-permute-start.22 = (bf16[128,512]{1,0:T(8,128)(2,1)S(1)}, bf16[128,512]{1,0:T(8,128)(2,1)S(1)}, u32[]{:S(2)}, u32[]{:S(2)}) collective-permute-start(bf16[128,512]{1,0:T(8,128)(2,1)S(1)} %get-tuple-element.88), channel_id=1, source_target_pairs={{0,1},{1,0},{2,3},{3,2},{4,5},{5,4},{6,7},{7,6},{8,9},{9,8},{10,11... | collective-permute-start | bytes 393224 | tf_op jit(solution)/shard_map/ppermute | solution.py:298
  100.9 6.3 %collective-permute-start.24 = (bf16[128,512]{1,0:T(8,128)(2,1)S(1)}, bf16[128,512]{1,0:T(8,128)(2,1)S(1)}, u32[]{:S(2)}, u32[]{:S(2)}) collective-permute-start(bf16[128,512]{1,0:T(8,128)(2,1)S(1)} %get-tuple-element.90), channel_id=1, source_target_pairs={{0,16},{1,17},{2,18},{3,19},{4,20},{5,21},{6,22},{7,23},{8,24},{9,... | collective-permute-start | bytes 393224 | tf_op jit(solution)/shard_map/ppermute | solution.py:298
  102.4 6.1 %collective-permute-start.27 = (bf16[128,512]{1,0:T(8,128)(2,1)S(1)}, bf16[128,512]{1,0:T(8,128)(2,1)S(1)}, u32[]{:S(2)}, u32[]{:S(2)}) collective-permute-start(bf16[128,512]{1,0:T(8,128)(2,1)S(1)} %get-tuple-element.93), channel_id=1, source_target_pairs={{0,17},{1,16},{2,19},{3,18},{4,21},{5,20},{6,23},{7,22},{8,25},{9,... | collective-permute-start | bytes 393224 | tf_op jit(solution)/shard_map/ppermute | solution.py:298

commit v13 on v11

--- a/solution.py
+++ b/solution.py
@@ -20,9 +20,9 @@
 CHUNK_HEADS = (8, 8)
 PHASES = (
     ("z", "y0", "k", "q02", "b~", "f~"),
-    ("z", "y1", "q03", "q01"),
-    ("z", "y2", "p", "q12"),
-    ("y3", "w", "q13~", "q11"),
+    ("z", "y1", "q03", "q01", "e"),
+    ("z", "y2", "p", "q12", "e"),
+    ("y3", "w", "q13~", "q11", "e-", "e-"),
 )
 CHUNKS = len(CHUNK_HEADS)
 FIRST_HEAD = tuple(sum(CHUNK_HEADS[:j]) for j in range(CHUNKS))
@@ -35,7 +35,18 @@
 
 
 def rows_kernel(
-    slot_count, info, lengths, kv, gain, ranks, freq, rows_out, cos_out, sin_out, outgoing_out
+    slot_count,
+    relative,
+    info,
+    lengths,
+    kv,
+    gain,
+    ranks,
+    freq,
+    rows_out,
+    cos_out,
+    sin_out,
+    outgoing_out,
 ):
     tok = kv.shape[1]
     base = info[0] * tok
@@ -66,7 +77,11 @@
     rows_out[:, :LAT] = latent.astype(jnp.bfloat16)
     rows_out[:, LAT:] = tail.astype(jnp.bfloat16)
 
-    rank_row = jnp.broadcast_to(ranks[...], (tok, tok)).astype(jnp.float32)
+    block = ranks[...]
+    if relative:
+        away = block ^ info[0]
+        block = ((away & 1) << 3) | ((away & 2) << 1) | ((away & 4) >> 1) | (away >> 3)
+    rank_row = jnp.broadcast_to(block, (tok, tok)).astype(jnp.float32)
     rank_col = rank_row.T
     earlier = lax.broadcasted_iota(jnp.int32, (tok, tok), 0) < lax.broadcasted_iota(
         jnp.int32, (tok, tok), 1
@@ -236,6 +251,20 @@
     mix(1, 1, second, *weighed)
 
 
+def sort_kernel(info, relative, out, sem):
+    rows = relative.shape[1]
+    copies = []
+    for d in range(relative.shape[0]):
+        begin = pl.multiple_of((info[0] ^ d) * rows, rows)
+        copies.append(
+            pltpu.make_async_copy(relative.at[d], out.at[pl.ds(begin, rows)], sem.at[d])
+        )
+    for copy in copies:
+        copy.start()
+    for copy in copies:
+        copy.wait()
+
+
 def gather_kernel(info, *refs):
     pieces, out, sems = refs[:-2], refs[-2], refs[-1]
     copies = []
@@ -302,6 +331,9 @@
 
     def inner_swap(array):
         return lax.ppermute(array, "ctx", [(i, i ^ 2) for i in range(size)])
+
+    def pair_swap(array, distance):
+        return lax.ppermute(array, "ctx", [(i, i ^ distance) for i in range(size)])
 
     def from_behind(array, by, odd_only):
         first = 1 if odd_only else 0
@@ -343,7 +375,7 @@
         return pl.BlockSpec(dims, lambda i: (0,) * len(dims))
 
     rows, cosine, sine, outgoing = pl.pallas_call(
-        functools.partial(rows_kernel, slot_count),
+        functools.partial(rows_kernel, slot_count, outer > 0),
         grid=(1,),
         out_shape=(
             shape((tok, EXT)),
@@ -385,6 +417,8 @@
     half = width // CHUNKS
     halves = []
     moved = [[queries[j]] + [None] * (QUAD - 1) for j in range(CHUNKS)]
+    held = outgoing.reshape(1, size, slot_count, ROW)
+    exchanged = []
     parts = {"r": tie(rows, pair_rows if outer else got)}
     for name in [name for phase in PHASES for name in phase + ("|",)]:
         kind, late = name[0], name[-1]
@@ -411,6 +445,11 @@
         elif kind == "p":
             own_rows = jnp.concatenate([both_groups, behind, far_behind], axis=0)
             other_rows = phases.send(late, quad_swap, own_rows, 1)
+        elif kind == "e" and outer:
+            half_of = held.shape[1] // 2
+            distance = 1 << len(exchanged)
+            exchanged.append(phases.send(late, pair_swap, held[:, half_of:], distance))
+            held = jnp.concatenate([held[:, :half_of], exchanged[-1]], axis=0)
         elif kind == "q":
             j, r = int(name[1]), int(name[2])
             moved[j][r] = phases.send(late, quad_swap, queries[r * CHUNKS + j], r)
@@ -466,20 +505,29 @@
     results = []
     for call in CALLS:
         last = len(results) + 1 == len(CALLS)
-        mine_info = tie(mine_info, *(results[0][2:3] if last else []))
+        mine_info = tie(mine_info, *(results[0][2:3] + exchanged[3:] if last else exchanged[2:3]))
         pieces = attend(*call)
         mine_info = tie(mine_info, pieces[0])
-        before = [piece for one in results for piece in one[1:]]
-        results.append([pieces[0]] + [quad_swap(pieces[r], r) for r in range(1, QUAD)])
+        before = results[-1][2:] if last else []
+        results.append(
+            [pieces[0], quad_swap(tie(pieces[1], *before), 1)]
+            + [quad_swap(pieces[r], r) for r in (2, 3)]
+        )
     pieces = [one[r] for r in range(QUAD) for one in results]
-    arrived = lax.all_to_all(
-        tie(outgoing, results[-1][0], *before).reshape(size, slot_count, ROW),
-        "ctx",
-        split_axis=0,
-        concat_axis=0,
-        tiled=True,
-    )
-    decode_cache = arrived.reshape(size * slot_count, ROW)
+    if outer:
+        decode_cache = pl.pallas_call(
+            sort_kernel,
+            out_shape=shape((size * slot_count, ROW)),
+            in_specs=[smem, anywhere],
+            out_specs=anywhere,
+            scratch_shapes=[pltpu.SemaphoreType.DMA((size,))],
+            compiler_params=params,
+            name="sort",
+        )(mine_info, held.reshape(size, slot_count, ROW))
+    else:
+        outgoing = tie(outgoing, results[-1][0]).reshape(size, slot_count, ROW)
+        arrived = lax.all_to_all(outgoing, "ctx", split_axis=0, concat_axis=0, tiled=True)
+        decode_cache = arrived.reshape(size * slot_count, ROW)
     attn_out = pl.pallas_call(
         gather_kernel,
         out_shape=shape((tok, H * VDIM)),

time: 107 us -> 105 us (0.981)
  waiting for transfers between devices: 44 us -> 38.6 us
  starting transfers between devices: 33.6 us -> 35.8 us
    ppermute x0 -> x4, waiting for transfers between devices: none -> 16.2 us  [pair_swap(): return lax.ppermute(array, 'ctx', [(i, i ^ distance) for i in range(size)])]
    ppermute x4, waiting for transfers between devices: 10.9 us -> 0.01 us  [around(): lax.ppermute(array, 'ctx', [(i, (i + by) % size) for i in range(size)])]
    ppermute x18, waiting for transfers between devices: 29 us -> 19.9 us  [quad_swap(): return lax.ppermute(array, ('groups', 'ctx'), pairs)]
    ppermute x0 -> x4, starting transfers between devices: none -> 4.14 us  [pair_swap(): return lax.ppermute(array, 'ctx', [(i, i ^ distance) for i in range(size)])]
    all_to_all x1 -> x0, starting transfers between devices: 4 us -> none  [body(): lax.all_to_all(tie(outgoing, results[-1][0], *before).reshape(size, slot_...]
    ppermute x4, starting transfers between devices: 8.17 us -> 10.5 us  [around(): lax.ppermute(array, 'ctx', [(i, (i + by) % size) for i in range(size)])]
    all_to_all x1 -> x0, waiting for transfers between devices: 1.68 us -> none  [body(): lax.all_to_all(tie(outgoing, results[-1][0], *before).reshape(size, slot_...]
    ppermute x18, starting transfers between devices: 13.4 us -> 12 us  [quad_swap(): return lax.ppermute(array, ('groups', 'ctx'), pairs)]
  transfers between devices with their start and end apart: 29 -> 32, of which waited for: 15 -> 11; matrix products, arithmetic and copies ran while one was open for 0% -> 1% of each run, Pallas kernels for 24% -> 24%
where the time goes in v13:
time: 105 us
  waiting for transfers between devices  38.6 us (37%)
  starting transfers between devices  35.8 us (34%)
  Pallas kernels  27.2 us (26%)
  local copies, waits for them, and re-layouts  2.11 us (2%)
    ppermute x18, waiting for transfers between devices, quad_swap(): return lax.ppermute(array, ('groups', 'ctx'), pairs)  19.9 us
    pallas_call x3, Pallas kernels, attend(): pl.pallas_call(functools.partial(attend_kernel, outer), grid=(steps,), ou...  17.9 us
    ppermute x4, waiting for transfers between devices, pair_swap(): return lax.ppermute(array, 'ctx', [(i, i ^ distance) for i in range(size)])  16.2 us
    ppermute x18, starting transfers between devices, quad_swap(): return lax.ppermute(array, ('groups', 'ctx'), pairs)  12 us
    ppermute x4, starting transfers between devices, around(): lax.ppermute(array, 'ctx', [(i, (i + by) % size) for i in range(size)])  10.5 us
    ppermute x4, starting transfers between devices, inner_swap(): return lax.ppermute(array, 'ctx', [(i, i ^ 2) for i in range(size)])  6.02 us
    ppermute x4, starting transfers between devices, pair_swap(): return lax.ppermute(array, 'ctx', [(i, i ^ distance) for i in range(size)])  4.14 us
    pallas_call x1, Pallas kernels, body(): pl.pallas_call(query_kernel, out_shape=[shape((tok, h * (NOPE + ROPE))) f...  3.38 us
  transfers between devices with their start and end apart: 32, of which 11 were waited for; matrix products, arithmetic and copies ran while one was open for 1% of the time, Pallas kernels for 24%

profile of v13, /device:TPU:0, one launch (start us, length us, event | category | flops | bytes accessed | tf_op | source)
XLA Modules:
  0.0 104.9 jit_solution(13179254803694735569)
XLA Ops:
  0.6 1.0 constant_dynamic-slice_fusion
  1.6 0.5 collective-permute-start
  2.1 2.3 %rows.1 = (bf16[128,640]{1,0:T(8,128)(2,1)}, f32[128,128]{1,0:T(8,128)}, f32[128,128]{1,0:T(8,128)}, bf16[256,576]{1,0:T(8,128)(2,1)}) custom-call(s32[1]{0:T(128)} %bitcast.1.info, s32[8]{0:T(128)} %lengths, bf16[576,128]{1,0:T(8,128)(2,1)} %bitcast.9, f32[1,512]{1,0:T(1,128)} %bitcast.10, s32[1,128]{1,0:T(1,128)} %bitcast.11, f32[1,128]{1,0:T(1,128)} %constant.30.clone.freq), custom_call_target="tpu_custom_call" | custom-call | tf_op jit(solution)/shard_map/rows/pallas_call | solution.py:377
  4.4 0.0 collective-permute-done.got
  4.5 1.0 pair.1.refs_0_
  5.4 0.0 copy-start.1
  5.4 2.6 %collective-permute-start.3 = (bf16[128,640]{1,0:T(8,128)(2,1)}, bf16[128,640]{1,0:T(8,128)(2,1)S(1)}, u32[]{:S(2)}, u32[]{:S(2)}) collective-permute-start(bf16[128,640]{1,0:T(8,128)(2,1)} %get-tuple-element.59), channel_id=1, source_target_pairs={{0,16},{1,17},{2,18},{3,19},{4,20},{5,21},{6,22},{7,23},{8,24},{9,... | collective-permute-start | bytes 491528 | tf_op jit(solution)/shard_map/ppermute | solution.py:327
  8.0 1.6 %collective-permute-start.1 = (bf16[64,4096]{1,0:T(8,128)(2,1)S(1)}, bf16[64,4096]{1,0:T(8,128)(2,1)S(1)}, u32[]{:S(2)}, u32[]{:S(2)}) collective-permute-start(bf16[64,4096]{1,0:T(8,128)(2,1)S(1)} %pair.1.refs_0_), channel_id=1, source_target_pairs={{0,4},{1,5},{2,6},{3,7},{4,8},{5,9},{6,10},{7,11},{8,12},{9,13},{1... | collective-permute-start | bytes 1572872 | tf_op jit(solution)/shard_map/ppermute | solution.py:330
  9.6 1.5 %collective-permute-start.2 = (bf16[64,4096]{1,0:T(8,128)(2,1)S(1)}, bf16[64,4096]{1,0:T(8,128)(2,1)S(1)}, u32[]{:S(2)}, u32[]{:S(2)}) collective-permute-start(bf16[64,4096]{1,0:T(8,128)(2,1)S(1)} %pair.1.refs_0_), channel_id=1, source_target_pairs={{0,2},{1,3},{2,0},{3,1},{4,6},{5,7},{6,4},{7,5},{8,10},{9,11},{10,... | collective-permute-start | bytes 1572872 | tf_op jit(solution)/shard_map/ppermute | solution.py:333
  11.1 3.4 %queries.1 = (bf16[128,1536]{1,0:T(8,128)(2,1)S(1)}, bf16[128,1536]{1,0:T(8,128)(2,1)S(1)}, bf16[128,1536]{1,0:T(8,128)(2,1)S(1)}, bf16[128,1536]{1,0:T(8,128)(2...) custom-call(s32[1]{0:T(128)} %bitcast.info, ...), custom_call_target="tpu_custom_call" | custom-call | bytes 6291456 | tf_op jit(solution)/shard_map/queries/pallas_call | solution.py:401
  14.5 0.6 collective-permute-start.4
  15.1 0.0 collective-permute-done.3
  15.2 2.4 %collective-permute-start.10 = (bf16[256,640]{1,0:T(8,128)(2,1)S(1)}, bf16[256,640]{1,0:T(8,128)(2,1)S(1)}, u32[]{:S(2)}, u32[]{:S(2)}) collective-permute-start(bf16[256,640]{1,0:T(8,128)(2,1)S(1)} %get-tuple-element.117), channel_id=1, source_target_pairs={{0,2},{1,3},{2,4},{3,5},{4,6},{5,7},{6,8},{7,9},{8,10},{9,11},{10,... | collective-permute-start | bytes 983048 | tf_op jit(solution)/shard_map/ppermute | solution.py:342
  17.6 0.7 collective-permute-start.11
  18.3 6.9 %collective-permute-done.4.refs_10_.refs_14_ = bf16[128,1536]{1,0:T(8,128)(2,1)S(1)} collective-permute-done((bf16[128,1536]{1,0:T(8,128)(2,1)S(1)}, bf16[128,1536]{1,0:T(8,128)(2,1)S(1)}, u32[]{:S(2)}, u32[]{:S(2)}) %collective-permute-start.4) | collective-permute-done | bytes 393248 | tf_op jit(solution)/shard_map/ppermute | solution.py:327
  25.2 6.6 %collective-permute-start.6 = (bf16[64,4096]{1,0:T(8,128)(2,1)S(1)}, bf16[64,4096]{1,0:T(8,128)(2,1)S(1)}, u32[]{:S(2)}, u32[]{:S(2)}) collective-permute-start(bf16[64,4096]{1,0:T(8,128)(2,1)S(1)} %collective-permute-done.1.refs_1_), channel_id=1, source_target_pairs={{0,4},{1,5},{2,6},{3,7},{4,8},{5,9},{6,10},{7,11},{8,12},{9,13},{1... | collective-permute-start | bytes 1572872 | tf_op jit(solution)/shard_map/ppermute | solution.py:330
  31.9 0.0 collective-permute-start.7
  31.9 0.0 collective-permute-start.8
  31.9 0.0 collective-permute-done.10
  31.9 0.6 collective-permute-start.9
  32.6 0.0 collective-permute-done.11
  32.6 0.1 collective-permute-start.5
  32.8 1.4 %collective-permute-done.5 = bf16[1,8,16,576]{3,2,0,1:T(8,128)(2,1)S(1)} collective-permute-done((bf16[1,8,16,576]{3,2,0,1:T(8,128)(2,1)S(1)}, bf16[1,8,16,576]{3,2,0,1:T(8,128)(2,1)S(1)}, u32[]{:S(2)}, u32[]{:S(2)}) %collective-permute-start.5) | collective-permute-done | bytes 147488 | tf_op jit(solution)/shard_map/ppermute | solution.py:336
  34.1 8.3 %collective-permute-done.8.refs_11_.refs_15_ = bf16[128,1536]{1,0:T(8,128)(2,1)S(1)} collective-permute-done((bf16[128,1536]{1,0:T(8,128)(2,1)S(1)}, bf16[128,1536]{1,0:T(8,128)(2,1)S(1)}, u32[]{:S(2)}, u32[]{:S(2)}) %collective-permute-start.8) | collective-permute-done | bytes 393248 | tf_op jit(solution)/shard_map/ppermute | solution.py:327
  42.4 0.0 collective-permute-done.7.refs_5_
  42.4 0.1 collective-permute-start.15
  42.5 1.6 %collective-permute-start.13 = (bf16[64,4096]{1,0:T(8,128)(2,1)S(1)}, bf16[64,4096]{1,0:T(8,128)(2,1)S(1)}, u32[]{:S(2)}, u32[]{:S(2)}) collective-permute-start(bf16[64,4096]{1,0:T(8,128)(2,1)S(1)} %collective-permute-done.6.refs_2_), channel_id=1, source_target_pairs={{0,4},{1,5},{2,6},{3,7},{4,8},{5,9},{6,10},{7,11},{8,12},{9,13},{1... | collective-permute-start | bytes 1572872 | tf_op jit(solution)/shard_map/ppermute | solution.py:330
  44.1 2.7 %collective-permute-start.14 = (bf16[64,4096]{1,0:T(8,128)(2,1)S(1)}, bf16[64,4096]{1,0:T(8,128)(2,1)S(1)}, u32[]{:S(2)}, u32[]{:S(2)}) collective-permute-start(bf16[64,4096]{1,0:T(8,128)(2,1)S(1)} %collective-permute-done.6.refs_2_), channel_id=1, source_target_pairs={{0,2},{1,3},{2,0},{3,1},{4,6},{5,7},{6,4},{7,5},{8,10},{9,11},{10,... | collective-permute-start | bytes 1572872 | tf_op jit(solution)/shard_map/ppermute | solution.py:333
  46.8 0.8 collective-permute-start.16
  47.7 0.1 collective-permute-start.12
  47.7 14.4 %collective-permute-done.12 = bf16[2,4,16,576]{3,2,0,1:T(8,128)(2,1)S(1)} collective-permute-done((bf16[2,4,16,576]{3,2,0,1:T(8,128)(2,1)S(1)}, bf16[2,4,16,576]{3,2,0,1:T(8,128)(2,1)S(1)}, u32[]{:S(2)}, u32[]{:S(2)}) %collective-permute-start.12) | collective-permute-done | bytes 147488 | tf_op jit(solution)/shard_map/ppermute | solution.py:336
  62.1 0.0 collective-permute-done.16.refs_10_.refs_14_
  62.1 0.0 collective-permute-done.13.refs_3_
  62.2 0.0 collective-permute-done.15.other
  62.2 1.6 %collective-permute-start.17 = (bf16[4,2,16,576]{3,2,0,1:T(8,128)(2,1)S(1)}, bf16[4,2,16,576]{3,2,0,1:T(8,128)(2,1)S(1)}, u32[]{:S(2)}, u32[]{:S(2)}) collective-permute-start(bf16[4,2,16,576]{3,2,0,1:T(8,128)(2,1)S(1)} %fusion.1), channel_id=1, source_target_pairs={{0,4},{1,5},{2,6},{3,7},{4,0},{5,1},{6,2},{7,3},{8,12},{9,13},{10,... | collective-permute-start | bytes 442376 | tf_op jit(solution)/shard_map/ppermute | solution.py:336
  63.8 1.8 %collective-permute-start.18 = (bf16[64,2048]{1,0:T(8,128)(2,1)S(1)}, bf16[64,2048]{1,0:T(8,128)(2,1)S(1)}, u32[]{:S(2)}, u32[]{:S(2)}) collective-permute-start(bf16[64,2048]{1,0:T(8,128)(2,1)S(1)} %slice.46), channel_id=1, source_target_pairs={{0,2},{1,3},{2,0},{3,1},{4,6},{5,7},{6,4},{7,5},{8,10},{9,11},{10,... | collective-permute-start | bytes 786440 | tf_op jit(solution)/shard_map/ppermute | solution.py:333
  65.7 0.7 collective-permute-start.19
  66.4 0.0 collective-permute-start.20
  66.4 1.3 %collective-permute-start.21 = (bf16[128,1536]{1,0:T(8,128)(2,1)S(1)}, bf16[128,1536]{1,0:T(8,128)(2,1)S(1)}, u32[]{:S(2)}, u32[]{:S(2)}) collective-permute-start(bf16[128,1536]{1,0:T(8,128)(2,1)S(1)} %get-tuple-element.91), channel_id=1, source_target_pairs={{0,17},{1,16},{2,19},{3,18},{4,21},{5,20},{6,23},{7,22},{8,25},{9,... | collective-permute-start | bytes 1179656 | tf_op jit(solution)/shard_map/ppermute | solution.py:327
  67.7 0.6 keys.1
  68.2 0.2 collective-permute-done.17
  68.5 0.1 fusion
  68.5 2.5 %collective-permute-done.18.refs_7_ = bf16[64,2048]{1,0:T(8,128)(2,1)S(1)} collective-permute-done((bf16[64,2048]{1,0:T(8,128)(2,1)S(1)}, bf16[64,2048]{1,0:T(8,128)(2,1)S(1)}, u32[]{:S(2)}, u32[]{:S(2)}) %collective-permute-start.18) | collective-permute-done | bytes 262176 | tf_op jit(solution)/shard_map/ppermute | solution.py:333
  71.0 8.9 %attend.3 = (bf16[128,1024]{1,0:T(8,128)(2,1)S(1)}, bf16[128,1024]{1,0:T(8,128)(2,1)S(1)}, bf16[128,1024]{1,0:T(8,128)(2,1)S(1)}, bf16[128,1024]{1,0:T(8,128)(2,1)S(1)}) custom-call(s32[1]{0:T(128)} %bitcast.1.info, bf16[2,640,512]{2,1,0:T(8,128)(2,1)S(1)} %get-tuple-element.78.latent, bf16[2,640,128]{2,1,0:T(8,128)(2,1)S(1)} %get-tuple-element.79.rope_even, ...), custom_call_target="tpu_custom_call" | custom-call | flops 4362076160 | bytes 8388608 | tf_op jit(solution)/shard_map/attend/pallas_call | solution.py:483
  79.9 0.6 collective-permute-start.22
  80.6 2.4 %collective-permute-start.23 = (bf16[8,1,16,576]{3,2,0,1:T(8,128)(2,1)S(1)}, bf16[8,1,16,576]{3,2,0,1:T(8,128)(2,1)S(1)}, u32[]{:S(2)}, u32[]{:S(2)}) collective-permute-start(bf16[8,1,16,576]{3,2,0,1:T(8,128)(2,1)S(1)} %get-tuple-element.95), channel_id=1, source_target_pairs={{0,8},{1,9},{2,10},{3,11},{4,12},{5,13},{6,14},{7,15},{8,0},{9,1},... | collective-permute-start | bytes 442376 | tf_op jit(solution)/shard_map/ppermute | solution.py:336
  82.9 0.0 collective-permute-done.19.refs_7_
  82.9 0.0 collective-permute-start.24
  82.9 1.1 %collective-permute-start.30 = (bf16[128,1024]{1,0:T(8,128)(2,1)S(1)}, bf16[128,1024]{1,0:T(8,128)(2,1)S(1)}, u32[]{:S(2)}, u32[]{:S(2)}) collective-permute-start(bf16[128,1024]{1,0:T(8,128)(2,1)S(1)} %get-tuple-element.105), channel_id=1, source_target_pairs={{0,17},{1,16},{2,19},{3,18},{4,21},{5,20},{6,23},{7,22},{8,25},{9,... | collective-permute-start | bytes 786440 | tf_op jit(solution)/shard_map/ppermute | solution.py:327
  84.0 4.5 %attend.4 = (bf16[128,512]{1,0:T(8,128)(2,1)S(1)}, bf16[128,512]{1,0:T(8,128)(2,1)S(1)}, bf16[128,512]{1,0:T(8,128)(2,1)S(1)}, bf16[128,512]{1,0:T(8,128)(2,1)S(1)}) custom-call(s32[1]{0:T(128)} %bitcast.1.info, bf16[2,640,512]{2,1,0:T(8,128)(2,1)S(1)} %get-tuple-element.78.latent, bf16[2,640,128]{2,1,0:T(8,128)(2,1)S(1)} %get-tuple-element.79.rope_even, ...), custom_call_target="tpu_custom_call" | custom-call | flops 2181038080 | bytes 4194304 | tf_op jit(solution)/shard_map/attend/pallas_call | solution.py:483
  88.5 0.1 collective-permute-start.25
  88.7 0.2 collective-permute-done.23
  88.9 1.4 %collective-permute-start.26 = (bf16[128,512]{1,0:T(8,128)(2,1)S(1)}, bf16[128,512]{1,0:T(8,128)(2,1)S(1)}, u32[]{:S(2)}, u32[]{:S(2)}) collective-permute-start(bf16[128,512]{1,0:T(8,128)(2,1)S(1)} %get-tuple-element.101), channel_id=1, source_target_pairs={{0,16},{1,17},{2,18},{3,19},{4,20},{5,21},{6,22},{7,23},{8,24},{9,... | collective-permute-start | bytes 393224 | tf_op jit(solution)/shard_map/ppermute | solution.py:327
  90.3 0.1 collective-permute-start.27
  90.5 4.5 %attend.5 = (bf16[128,512]{1,0:T(8,128)(2,1)S(1)}, bf16[128,512]{1,0:T(8,128)(2,1)S(1)}, bf16[128,512]{1,0:T(8,128)(2,1)S(1)}, bf16[128,512]{1,0:T(8,128)(2,1)S(1)}) custom-call(s32[1]{0:T(128)} %bitcast.1.info, bf16[2,640,512]{2,1,0:T(8,128)(2,1)S(1)} %get-tuple-element.78.latent, bf16[2,640,128]{2,1,0:T(8,128)(2,1)S(1)} %get-tuple-element.79.rope_even, ...), custom_call_target="tpu_custom_call" | custom-call | flops 2181038080 | bytes 4194304 | tf_op jit(solution)/shard_map/attend/pallas_call | solution.py:483
  95.0 0.2 collective-permute-done.26.refs_7_
  95.2 1.5 %collective-permute-start.29 = (bf16[128,512]{1,0:T(8,128)(2,1)S(1)}, bf16[128,512]{1,0:T(8,128)(2,1)S(1)}, u32[]{:S(2)}, u32[]{:S(2)}) collective-permute-start(bf16[128,512]{1,0:T(8,128)(2,1)S(1)} %get-tuple-element.104), channel_id=1, source_target_pairs={{0,16},{1,17},{2,18},{3,19},{4,20},{5,21},{6,22},{7,23},{8,24},{9,... | collective-permute-start | bytes 393224 | tf_op jit(solution)/shard_map/ppermute | solution.py:327
  96.7 0.5 collective-permute-done.27.refs_10_
  97.2 0.6 collective-permute-start.31
  97.9 0.6 sort.1
  98.5 0.9 copy.9
  99.4 2.1 %collective-permute-done.29.refs_8_ = bf16[128,512]{1,0:T(8,128)(2,1)S(1)} collective-permute-done((bf16[128,512]{1,0:T(8,128)(2,1)S(1)}, bf16[128,512]{1,0:T(8,128)(2,1)S(1)}, u32[]{:S(2)}, u32[]{:S(2)}) %collective-permute-start.29) | collective-permute-done | bytes 131104 | tf_op jit(solution)/shard_map/ppermute | solution.py:327
  101.5 1.9 %collective-permute-done.31.refs_11_ = bf16[128,512]{1,0:T(8,128)(2,1)S(1)} collective-permute-done((bf16[128,512]{1,0:T(8,128)(2,1)S(1)}, bf16[128,512]{1,0:T(8,128)(2,1)S(1)}, u32[]{:S(2)}, u32[]{:S(2)}) %collective-permute-start.31) | collective-permute-done | bytes 131104 | tf_op jit(solution)/shard_map/ppermute | solution.py:327
  103.4 1.4 %place.1 = bf16[128,8192]{1,0:T(8,128)(2,1)} custom-call(s32[1]{0:T(128)} %bitcast.info, bf16[128,1024]{1,0:T(8,128)(2,1)S(1)} %get-tuple-element.83.refs_0_, bf16[128,512]{1,0:T(8,128)(2,1)S(1)} %get-tuple-element.92.refs_1_, bf16[128,512]{1,0:T(8,128)(2,1)S(1)} %get-tuple-element.97.refs_2_, bf16[128,1024]{1,0:T(8,128)(2,1)S(1)} %collective-permute-done.24.refs_3_, ...), custom_call_target="tpu_custom_call" | custom-call | tf_op jit(solution)/shard_map/place/pallas_call | solution.py:531
  (27 shorter events, 0.4 us)
Async XLA Ops:
  1.6 2.8 %collective-permute-start = (bf16[32,4096]{1,0:T(8,128)(2,1)S(1)}, bf16[32,4096]{1,0:T(8,128)(2,1)S(1)}, u32[]{:S(2)}, u32[]{:S(2)}) collective-permute-start(bf16[32,4096]{1,0:T(8,128)(2,1)S(1)} %constant_dynamic-slice_fusion), channel_id=1, source_target_pairs={{0,1},{1,0},{2,3},{3,2},{4,5},{5,4},{6,7},{7,6},{8,9},{9,8},{10,11... | collective-permute-start | bytes 786440 | tf_op jit(solution)/shard_map/ppermute | solution.py:327
  5.4 9.7 %copy-start.1 = (bf16[128,640]{1,0:T(8,128)(2,1)S(1)}, bf16[128,640]{1,0:T(8,128)(2,1)}, u32[]{:S(2)}) copy-start(bf16[128,640]{1,0:T(8,128)(2,1)} %get-tuple-element.59) | copy-start | bytes 491524
  5.4 9.7 %collective-permute-start.3 = (bf16[128,640]{1,0:T(8,128)(2,1)}, bf16[128,640]{1,0:T(8,128)(2,1)S(1)}, u32[]{:S(2)}, u32[]{:S(2)}) collective-permute-start(bf16[128,640]{1,0:T(8,128)(2,1)} %get-tuple-element.59), channel_id=1, source_target_pairs={{0,16},{1,17},{2,18},{3,19},{4,20},{5,21},{6,22},{7,23},{8,24},{9,... | collective-permute-start | bytes 491528 | tf_op jit(solution)/shard_map/ppermute | solution.py:327
  8.0 17.2 %collective-permute-start.1 = (bf16[64,4096]{1,0:T(8,128)(2,1)S(1)}, bf16[64,4096]{1,0:T(8,128)(2,1)S(1)}, u32[]{:S(2)}, u32[]{:S(2)}) collective-permute-start(bf16[64,4096]{1,0:T(8,128)(2,1)S(1)} %pair.1.refs_0_), channel_id=1, source_target_pairs={{0,4},{1,5},{2,6},{3,7},{4,8},{5,9},{6,10},{7,11},{8,12},{9,13},{1... | collective-permute-start | bytes 1572872 | tf_op jit(solution)/shard_map/ppermute | solution.py:330
  9.6 15.7 %collective-permute-start.2 = (bf16[64,4096]{1,0:T(8,128)(2,1)S(1)}, bf16[64,4096]{1,0:T(8,128)(2,1)S(1)}, u32[]{:S(2)}, u32[]{:S(2)}) collective-permute-start(bf16[64,4096]{1,0:T(8,128)(2,1)S(1)} %pair.1.refs_0_), channel_id=1, source_target_pairs={{0,2},{1,3},{2,0},{3,1},{4,6},{5,7},{6,4},{7,5},{8,10},{9,11},{10,... | collective-permute-start | bytes 1572872 | tf_op jit(solution)/shard_map/ppermute | solution.py:333
  11.1 21.4 %copy-start = (bf16[256,576]{1,0:T(8,128)(2,1)S(1)}, bf16[256,576]{1,0:T(8,128)(2,1)}, u32[]{:S(2)}) copy-start(bf16[256,576]{1,0:T(8,128)(2,1)} %get-tuple-element.56) | copy-start | bytes 884740
  14.5 10.7 %collective-permute-start.4 = (bf16[128,1536]{1,0:T(8,128)(2,1)S(1)}, bf16[128,1536]{1,0:T(8,128)(2,1)S(1)}, u32[]{:S(2)}, u32[]{:S(2)}) collective-permute-start(bf16[128,1536]{1,0:T(8,128)(2,1)S(1)} %get-tuple-element.63), channel_id=1, source_target_pairs={{0,16},{1,17},{2,18},{3,19},{4,20},{5,21},{6,22},{7,23},{8,24},{9,... | collective-permute-start | bytes 1179656 | tf_op jit(solution)/shard_map/ppermute | solution.py:327
  15.2 16.7 %collective-permute-start.10 = (bf16[256,640]{1,0:T(8,128)(2,1)S(1)}, bf16[256,640]{1,0:T(8,128)(2,1)S(1)}, u32[]{:S(2)}, u32[]{:S(2)}) collective-permute-start(bf16[256,640]{1,0:T(8,128)(2,1)S(1)} %get-tuple-element.117), channel_id=1, source_target_pairs={{0,2},{1,3},{2,4},{3,5},{4,6},{5,7},{6,8},{7,9},{8,10},{9,11},{10,... | collective-permute-start | bytes 983048 | tf_op jit(solution)/shard_map/ppermute | solution.py:342
  17.6 14.9 %collective-permute-start.11 = (bf16[256,640]{1,0:T(8,128)(2,1)S(1)}, bf16[256,640]{1,0:T(8,128)(2,1)S(1)}, u32[]{:S(2)}, u32[]{:S(2)}) collective-permute-start(bf16[256,640]{1,0:T(8,128)(2,1)S(1)} %get-tuple-element.117), channel_id=1, source_target_pairs={{1,5},{3,7},{5,9},{7,11},{9,13},{11,15},{17,21},{19,23},{21,25},{2... | collective-permute-start | bytes 983048 | tf_op jit(solution)/shard_map/ppermute | solution.py:342
  25.2 17.1 %collective-permute-start.6 = (bf16[64,4096]{1,0:T(8,128)(2,1)S(1)}, bf16[64,4096]{1,0:T(8,128)(2,1)S(1)}, u32[]{:S(2)}, u32[]{:S(2)}) collective-permute-start(bf16[64,4096]{1,0:T(8,128)(2,1)S(1)} %collective-permute-done.1.refs_1_), channel_id=1, source_target_pairs={{0,4},{1,5},{2,6},{3,7},{4,8},{5,9},{6,10},{7,11},{8,12},{9,13},{1... | collective-permute-start | bytes 1572872 | tf_op jit(solution)/shard_map/ppermute | solution.py:330
  31.9 10.5 %collective-permute-start.7 = (bf16[64,4096]{1,0:T(8,128)(2,1)S(1)}, bf16[64,4096]{1,0:T(8,128)(2,1)S(1)}, u32[]{:S(2)}, u32[]{:S(2)}) collective-permute-start(bf16[64,4096]{1,0:T(8,128)(2,1)S(1)} %collective-permute-done.1.refs_1_), channel_id=1, source_target_pairs={{0,2},{1,3},{2,0},{3,1},{4,6},{5,7},{6,4},{7,5},{8,10},{9,11},{10,... | collective-permute-start | bytes 1572872 | tf_op jit(solution)/shard_map/ppermute | solution.py:333
  31.9 10.5 %collective-permute-start.8 = (bf16[128,1536]{1,0:T(8,128)(2,1)S(1)}, bf16[128,1536]{1,0:T(8,128)(2,1)S(1)}, u32[]{:S(2)}, u32[]{:S(2)}) collective-permute-start(bf16[128,1536]{1,0:T(8,128)(2,1)S(1)} %get-tuple-element.68), channel_id=1, source_target_pairs={{0,17},{1,16},{2,19},{3,18},{4,21},{5,20},{6,23},{7,22},{8,25},{9,... | collective-permute-start | bytes 1179656 | tf_op jit(solution)/shard_map/ppermute | solution.py:327
  31.9 10.5 %collective-permute-start.9 = (bf16[128,1536]{1,0:T(8,128)(2,1)S(1)}, bf16[128,1536]{1,0:T(8,128)(2,1)S(1)}, u32[]{:S(2)}, u32[]{:S(2)}) collective-permute-start(bf16[128,1536]{1,0:T(8,128)(2,1)S(1)} %get-tuple-element.70), channel_id=1, source_target_pairs={{0,1},{1,0},{2,3},{3,2},{4,5},{5,4},{6,7},{7,6},{8,9},{9,8},{10,11... | collective-permute-start | bytes 1179656 | tf_op jit(solution)/shard_map/ppermute | solution.py:327
  32.6 1.5 %collective-permute-start.5 = (bf16[1,8,16,576]{3,2,0,1:T(8,128)(2,1)S(1)}, bf16[1,8,16,576]{3,2,0,1:T(8,128)(2,1)S(1)}, u32[]{:S(2)}, u32[]{:S(2)}) collective-permute-start(bf16[1,8,16,576]{3,2,0,1:T(8,128)(2,1)S(1)} %get-tuple-element.65), channel_id=1, source_target_pairs={{0,1},{1,0},{2,3},{3,2},{4,5},{5,4},{6,7},{7,6},{8,9},{9,8},{10,11... | collective-permute-start | bytes 442376 | tf_op jit(solution)/shard_map/ppermute | solution.py:336
  42.4 19.8 %collective-permute-start.15 = (bf16[768,640]{1,0:T(8,128)(2,1)S(1)}, bf16[768,640]{1,0:T(8,128)(2,1)S(1)}, u32[]{:S(2)}, u32[]{:S(2)}) collective-permute-start(bf16[768,640]{1,0:T(8,128)(2,1)S(1)} %constant_dynamic-update-slice_fusion.2.own), channel_id=1, source_target_pairs={{0,1},{1,0},{2,3},{3,2},{4,5},{5,4},{6,7},{7,6},{8,9},{9,8},{10,11... | collective-permute-start | bytes 2949128 | tf_op jit(solution)/shard_map/ppermute | solution.py:327
  42.5 19.7 %collective-permute-start.13 = (bf16[64,4096]{1,0:T(8,128)(2,1)S(1)}, bf16[64,4096]{1,0:T(8,128)(2,1)S(1)}, u32[]{:S(2)}, u32[]{:S(2)}) collective-permute-start(bf16[64,4096]{1,0:T(8,128)(2,1)S(1)} %collective-permute-done.6.refs_2_), channel_id=1, source_target_pairs={{0,4},{1,5},{2,6},{3,7},{4,8},{5,9},{6,10},{7,11},{8,12},{9,13},{1... | collective-permute-start | bytes 1572872 | tf_op jit(solution)/shard_map/ppermute | solution.py:330
  44.1 18.1 %collective-permute-start.14 = (bf16[64,4096]{1,0:T(8,128)(2,1)S(1)}, bf16[64,4096]{1,0:T(8,128)(2,1)S(1)}, u32[]{:S(2)}, u32[]{:S(2)}) collective-permute-start(bf16[64,4096]{1,0:T(8,128)(2,1)S(1)} %collective-permute-done.6.refs_2_), channel_id=1, source_target_pairs={{0,2},{1,3},{2,0},{3,1},{4,6},{5,7},{6,4},{7,5},{8,10},{9,11},{10,... | collective-permute-start | bytes 1572872 | tf_op jit(solution)/shard_map/ppermute | solution.py:333
  46.8 15.4 %collective-permute-start.16 = (bf16[128,1536]{1,0:T(8,128)(2,1)S(1)}, bf16[128,1536]{1,0:T(8,128)(2,1)S(1)}, u32[]{:S(2)}, u32[]{:S(2)}) collective-permute-start(bf16[128,1536]{1,0:T(8,128)(2,1)S(1)} %get-tuple-element.75), channel_id=1, source_target_pairs={{0,16},{1,17},{2,18},{3,19},{4,20},{5,21},{6,22},{7,23},{8,24},{9,... | collective-permute-start | bytes 1179656 | tf_op jit(solution)/shard_map/ppermute | solution.py:327
  47.7 14.4 %collective-permute-start.12 = (bf16[2,4,16,576]{3,2,0,1:T(8,128)(2,1)S(1)}, bf16[2,4,16,576]{3,2,0,1:T(8,128)(2,1)S(1)}, u32[]{:S(2)}, u32[]{:S(2)}) collective-permute-start(bf16[2,4,16,576]{3,2,0,1:T(8,128)(2,1)S(1)} %get-tuple-element.71), channel_id=1, source_target_pairs={{0,2},{1,3},{2,0},{3,1},{4,6},{5,7},{6,4},{7,5},{8,10},{9,11},{10,... | collective-permute-start | bytes 442376 | tf_op jit(solution)/shard_map/ppermute | solution.py:336
  62.2 6.3 %collective-permute-start.17 = (bf16[4,2,16,576]{3,2,0,1:T(8,128)(2,1)S(1)}, bf16[4,2,16,576]{3,2,0,1:T(8,128)(2,1)S(1)}, u32[]{:S(2)}, u32[]{:S(2)}) collective-permute-start(bf16[4,2,16,576]{3,2,0,1:T(8,128)(2,1)S(1)} %fusion.1), channel_id=1, source_target_pairs={{0,4},{1,5},{2,6},{3,7},{4,0},{5,1},{6,2},{7,3},{8,12},{9,13},{10,... | collective-permute-start | bytes 442376 | tf_op jit(solution)/shard_map/ppermute | solution.py:336
  63.8 7.1 %collective-permute-start.18 = (bf16[64,2048]{1,0:T(8,128)(2,1)S(1)}, bf16[64,2048]{1,0:T(8,128)(2,1)S(1)}, u32[]{:S(2)}, u32[]{:S(2)}) collective-permute-start(bf16[64,2048]{1,0:T(8,128)(2,1)S(1)} %slice.46), channel_id=1, source_target_pairs={{0,2},{1,3},{2,0},{3,1},{4,6},{5,7},{6,4},{7,5},{8,10},{9,11},{10,... | collective-permute-start | bytes 786440 | tf_op jit(solution)/shard_map/ppermute | solution.py:333
  65.7 17.3 %collective-permute-start.19 = (bf16[64,2048]{1,0:T(8,128)(2,1)S(1)}, bf16[64,2048]{1,0:T(8,128)(2,1)S(1)}, u32[]{:S(2)}, u32[]{:S(2)}) collective-permute-start(bf16[64,2048]{1,0:T(8,128)(2,1)S(1)} %slice.47), channel_id=1, source_target_pairs={{0,4},{1,5},{2,6},{3,7},{4,8},{5,9},{6,10},{7,11},{8,12},{9,13},{1... | collective-permute-start | bytes 786440 | tf_op jit(solution)/shard_map/ppermute | solution.py:330
  66.4 16.6 %collective-permute-start.20 = (bf16[128,1536]{1,0:T(8,128)(2,1)S(1)}, bf16[128,1536]{1,0:T(8,128)(2,1)S(1)}, u32[]{:S(2)}, u32[]{:S(2)}) collective-permute-start(bf16[128,1536]{1,0:T(8,128)(2,1)S(1)} %get-tuple-element.89), channel_id=1, source_target_pairs={{0,1},{1,0},{2,3},{3,2},{4,5},{5,4},{6,7},{7,6},{8,9},{9,8},{10,11... | collective-permute-start | bytes 1179656 | tf_op jit(solution)/shard_map/ppermute | solution.py:327
  66.4 17.7 %collective-permute-start.21 = (bf16[128,1536]{1,0:T(8,128)(2,1)S(1)}, bf16[128,1536]{1,0:T(8,128)(2,1)S(1)}, u32[]{:S(2)}, u32[]{:S(2)}) collective-permute-start(bf16[128,1536]{1,0:T(8,128)(2,1)S(1)} %get-tuple-element.91), channel_id=1, source_target_pairs={{0,17},{1,16},{2,19},{3,18},{4,21},{5,20},{6,23},{7,22},{8,25},{9,... | collective-permute-start | bytes 1179656 | tf_op jit(solution)/shard_map/ppermute | solution.py:327
  79.9 10.4 %collective-permute-start.22 = (bf16[128,1024]{1,0:T(8,128)(2,1)S(1)}, bf16[128,1024]{1,0:T(8,128)(2,1)S(1)}, u32[]{:S(2)}, u32[]{:S(2)}) collective-permute-start(bf16[128,1024]{1,0:T(8,128)(2,1)S(1)} %get-tuple-element.94), channel_id=1, source_target_pairs={{0,16},{1,17},{2,18},{3,19},{4,20},{5,21},{6,22},{7,23},{8,24},{9,... | collective-permute-start | bytes 786440 | tf_op jit(solution)/shard_map/ppermute | solution.py:327
  80.6 8.3 %collective-permute-start.23 = (bf16[8,1,16,576]{3,2,0,1:T(8,128)(2,1)S(1)}, bf16[8,1,16,576]{3,2,0,1:T(8,128)(2,1)S(1)}, u32[]{:S(2)}, u32[]{:S(2)}) collective-permute-start(bf16[8,1,16,576]{3,2,0,1:T(8,128)(2,1)S(1)} %get-tuple-element.95), channel_id=1, source_target_pairs={{0,8},{1,9},{2,10},{3,11},{4,12},{5,13},{6,14},{7,15},{8,0},{9,1},... | collective-permute-start | bytes 442376 | tf_op jit(solution)/shard_map/ppermute | solution.py:336
  82.9 14.9 %collective-permute-start.24 = (bf16[128,1024]{1,0:T(8,128)(2,1)S(1)}, bf16[128,1024]{1,0:T(8,128)(2,1)S(1)}, u32[]{:S(2)}, u32[]{:S(2)}) collective-permute-start(bf16[128,1024]{1,0:T(8,128)(2,1)S(1)} %get-tuple-element.98), channel_id=1, source_target_pairs={{0,1},{1,0},{2,3},{3,2},{4,5},{5,4},{6,7},{7,6},{8,9},{9,8},{10,11... | collective-permute-start | bytes 786440 | tf_op jit(solution)/shard_map/ppermute | solution.py:327
  82.9 16.4 %collective-permute-start.30 = (bf16[128,1024]{1,0:T(8,128)(2,1)S(1)}, bf16[128,1024]{1,0:T(8,128)(2,1)S(1)}, u32[]{:S(2)}, u32[]{:S(2)}) collective-permute-start(bf16[128,1024]{1,0:T(8,128)(2,1)S(1)} %get-tuple-element.105), channel_id=1, source_target_pairs={{0,17},{1,16},{2,19},{3,18},{4,21},{5,20},{6,23},{7,22},{8,25},{9,... | collective-permute-start | bytes 786440 | tf_op jit(solution)/shard_map/ppermute | solution.py:327
  88.5 10.9 %collective-permute-start.25 = (bf16[128,512]{1,0:T(8,128)(2,1)S(1)}, bf16[128,512]{1,0:T(8,128)(2,1)S(1)}, u32[]{:S(2)}, u32[]{:S(2)}) collective-permute-start(bf16[128,512]{1,0:T(8,128)(2,1)S(1)} %get-tuple-element.99), channel_id=1, source_target_pairs={{0,1},{1,0},{2,3},{3,2},{4,5},{5,4},{6,7},{7,6},{8,9},{9,8},{10,11... | collective-permute-start | bytes 393224 | tf_op jit(solution)/shard_map/ppermute | solution.py:327
  88.9 6.3 %collective-permute-start.26 = (bf16[128,512]{1,0:T(8,128)(2,1)S(1)}, bf16[128,512]{1,0:T(8,128)(2,1)S(1)}, u32[]{:S(2)}, u32[]{:S(2)}) collective-permute-start(bf16[128,512]{1,0:T(8,128)(2,1)S(1)} %get-tuple-element.101), channel_id=1, source_target_pairs={{0,16},{1,17},{2,18},{3,19},{4,20},{5,21},{6,22},{7,23},{8,24},{9,... | collective-permute-start | bytes 393224 | tf_op jit(solution)/shard_map/ppermute | solution.py:327
  90.3 6.9 %collective-permute-start.27 = (bf16[128,512]{1,0:T(8,128)(2,1)S(1)}, bf16[128,512]{1,0:T(8,128)(2,1)S(1)}, u32[]{:S(2)}, u32[]{:S(2)}) collective-permute-start(bf16[128,512]{1,0:T(8,128)(2,1)S(1)} %get-tuple-element.102), channel_id=1, source_target_pairs={{0,17},{1,16},{2,19},{3,18},{4,21},{5,20},{6,23},{7,22},{8,25},{9,... | collective-permute-start | bytes 393224 | tf_op jit(solution)/shard_map/ppermute | solution.py:327
  95.2 6.3 %collective-permute-start.29 = (bf16[128,512]{1,0:T(8,128)(2,1)S(1)}, bf16[128,512]{1,0:T(8,128)(2,1)S(1)}, u32[]{:S(2)}, u32[]{:S(2)}) collective-permute-start(bf16[128,512]{1,0:T(8,128)(2,1)S(1)} %get-tuple-element.104), channel_id=1, source_target_pairs={{0,16},{1,17},{2,18},{3,19},{4,20},{5,21},{6,22},{7,23},{8,24},{9,... | collective-permute-start | bytes 393224 | tf_op jit(solution)/shard_map/ppermute | solution.py:327
  97.2 6.2 %collective-permute-start.31 = (bf16[128,512]{1,0:T(8,128)(2,1)S(1)}, bf16[128,512]{1,0:T(8,128)(2,1)S(1)}, u32[]{:S(2)}, u32[]{:S(2)}) collective-permute-start(bf16[128,512]{1,0:T(8,128)(2,1)S(1)} %get-tuple-element.106), channel_id=1, source_target_pairs={{0,17},{1,16},{2,19},{3,18},{4,21},{5,20},{6,23},{7,22},{8,25},{9,... | collective-permute-start | bytes 393224 | tf_op jit(solution)/shard_map/ppermute | solution.py:327
  97.8 5.6 %collective-permute-start.28 = (bf16[128,512]{1,0:T(8,128)(2,1)S(1)}, bf16[128,512]{1,0:T(8,128)(2,1)S(1)}, u32[]{:S(2)}, u32[]{:S(2)}) collective-permute-start(bf16[128,512]{1,0:T(8,128)(2,1)S(1)} %get-tuple-element.103), channel_id=1, source_target_pairs={{0,1},{1,0},{2,3},{3,2},{4,5},{5,4},{6,7},{7,6},{8,9},{9,8},{10,11... | collective-permute-start | bytes 393224 | tf_op jit(solution)/shard_map/ppermute | solution.py:327

commit v14 on v13

--- a/solution.py
+++ b/solution.py
@@ -20,9 +20,9 @@
 CHUNK_HEADS = (8, 8)
 PHASES = (
     ("z", "y0", "k", "q02", "b~", "f~"),
-    ("z", "y1", "q03", "q01", "e"),
-    ("z", "y2", "p", "q12", "e"),
-    ("y3", "w", "q13~", "q11", "e-", "e-"),
+    ("z", "y1", "q03", "q01", "e-"),
+    ("z", "y2", "p", "q12"),
+    ("y3", "w", "q13~", "q11", "e-", "e-", "e-"),
 )
 CHUNKS = len(CHUNK_HEADS)
 FIRST_HEAD = tuple(sum(CHUNK_HEADS[:j]) for j in range(CHUNKS))
@@ -505,7 +505,8 @@
     results = []
     for call in CALLS:
         last = len(results) + 1 == len(CALLS)
-        mine_info = tie(mine_info, *(results[0][2:3] + exchanged[3:] if last else exchanged[2:3]))
+        mine_info = tie(mine_info, *exchanged[len(results) : len(results) + 1])
+        mine_info = tie(mine_info, *(results[0][2:3] if last else []))
         pieces = attend(*call)
         mine_info = tie(mine_info, pieces[0])
         before = results[-1][2:] if last else []

time: 105 us -> 104 us (level)
  starting transfers between devices: 35.8 us -> 33.5 us
  waiting for transfers between devices: 38.6 us -> 40.3 us
    ppermute x18, waiting for transfers between devices: 19.9 us -> 33.3 us  [quad_swap(): return lax.ppermute(array, ('groups', 'ctx'), pairs)]
    ppermute x4, waiting for transfers between devices: 16.2 us -> 3.01 us  [pair_swap(): return lax.ppermute(array, 'ctx', [(i, i ^ distance) for i in range(size)])]
    ppermute x4, starting transfers between devices: 10.5 us -> 8.34 us  [around(): lax.ppermute(array, 'ctx', [(i, (i + by) % size) for i in range(size)])]
    ppermute x4, starting transfers between devices: 6.02 us -> 4.01 us  [inner_swap(): return lax.ppermute(array, 'ctx', [(i, i ^ 2) for i in range(size)])]
    ppermute x4, waiting for transfers between devices: 0.01 us -> 1.87 us  [around(): lax.ppermute(array, 'ctx', [(i, (i + by) % size) for i in range(size)])]
    ppermute x18, starting transfers between devices: 12 us -> 13.2 us  [quad_swap(): return lax.ppermute(array, ('groups', 'ctx'), pairs)]
  transfers between devices with their start and end apart: 32 -> 32, of which waited for: 11 -> 15; matrix products, arithmetic and copies ran while one was open for 1% -> 1% of each run, Pallas kernels for 24% -> 24%
where the time goes in v14:
time: 104 us
  waiting for transfers between devices  40.3 us (39%)
  starting transfers between devices  33.5 us (32%)
  Pallas kernels  27.2 us (26%)
  local copies, waits for them, and re-layouts  2.1 us (2%)
    ppermute x18, waiting for transfers between devices, quad_swap(): return lax.ppermute(array, ('groups', 'ctx'), pairs)  33.3 us
    pallas_call x3, Pallas kernels, attend(): pl.pallas_call(functools.partial(attend_kernel, outer), grid=(steps,), ou...  17.9 us
    ppermute x18, starting transfers between devices, quad_swap(): return lax.ppermute(array, ('groups', 'ctx'), pairs)  13.2 us
    ppermute x4, starting transfers between devices, around(): lax.ppermute(array, 'ctx', [(i, (i + by) % size) for i in range(size)])  8.34 us
    ppermute x4, starting transfers between devices, pair_swap(): return lax.ppermute(array, 'ctx', [(i, i ^ distance) for i in range(size)])  4.84 us
    ppermute x4, starting transfers between devices, inner_swap(): return lax.ppermute(array, 'ctx', [(i, i ^ 2) for i in range(size)])  4.01 us
    pallas_call x1, Pallas kernels, body(): pl.pallas_call(query_kernel, out_shape=[shape((tok, h * (NOPE + ROPE))) f...  3.38 us
    ppermute x2, starting transfers between devices, from_behind(): return lax.ppermute(array, 'ctx', pairs)  3.1 us
  transfers between devices with their start and end apart: 32, of which 15 were waited for; matrix products, arithmetic and copies ran while one was open for 1% of the time, Pallas kernels for 24%

profile of v14, /device:TPU:0, one launch (start us, length us, event | category | flops | bytes accessed | tf_op | source)
XLA Modules:
  0.0 104.3 jit_solution(17939266513144167724)
XLA Ops:
  0.6 1.0 constant_dynamic-slice_fusion
  1.6 0.5 collective-permute-start
  2.1 1.2 %collective-permute-done.got = bf16[32,4096]{1,0:T(8,128)(2,1)S(1)} collective-permute-done((bf16[32,4096]{1,0:T(8,128)(2,1)S(1)}, bf16[32,4096]{1,0:T(8,128)(2,1)S(1)}, u32[]{:S(2)}, u32[]{:S(2)}) %collective-permute-start) | collective-permute-done | bytes 262176 | tf_op jit(solution)/shard_map/ppermute | solution.py:327
  3.3 1.0 pair.1.refs_0_
  4.3 3.0 %collective-permute-start.1 = (bf16[64,4096]{1,0:T(8,128)(2,1)S(1)}, bf16[64,4096]{1,0:T(8,128)(2,1)S(1)}, u32[]{:S(2)}, u32[]{:S(2)}) collective-permute-start(bf16[64,4096]{1,0:T(8,128)(2,1)S(1)} %pair.1.refs_0_), channel_id=1, source_target_pairs={{0,4},{1,5},{2,6},{3,7},{4,8},{5,9},{6,10},{7,11},{8,12},{9,13},{1... | collective-permute-start | bytes 1572872 | tf_op jit(solution)/shard_map/ppermute | solution.py:330
  7.3 1.5 %collective-permute-start.2 = (bf16[64,4096]{1,0:T(8,128)(2,1)S(1)}, bf16[64,4096]{1,0:T(8,128)(2,1)S(1)}, u32[]{:S(2)}, u32[]{:S(2)}) collective-permute-start(bf16[64,4096]{1,0:T(8,128)(2,1)S(1)} %pair.1.refs_0_), channel_id=1, source_target_pairs={{0,2},{1,3},{2,0},{3,1},{4,6},{5,7},{6,4},{7,5},{8,10},{9,11},{10,... | collective-permute-start | bytes 1572872 | tf_op jit(solution)/shard_map/ppermute | solution.py:333
  8.8 2.3 %rows.1 = (bf16[128,640]{1,0:T(8,128)(2,1)}, f32[128,128]{1,0:T(8,128)}, f32[128,128]{1,0:T(8,128)}, bf16[256,576]{1,0:T(8,128)(2,1)}) custom-call(s32[1]{0:T(128)} %bitcast.1.info, s32[8]{0:T(128)} %lengths, bf16[576,128]{1,0:T(8,128)(2,1)} %bitcast.9, f32[1,512]{1,0:T(1,128)} %bitcast.10, s32[1,128]{1,0:T(1,128)} %bitcast.11, f32[1,128]{1,0:T(1,128)} %constant.30.clone.freq), custom_call_target="tpu_custom_call" | custom-call | tf_op jit(solution)/shard_map/rows/pallas_call | solution.py:377
  11.1 1.5 %collective-permute-start.3 = (bf16[128,640]{1,0:T(8,128)(2,1)}, bf16[128,640]{1,0:T(8,128)(2,1)S(1)}, u32[]{:S(2)}, u32[]{:S(2)}) collective-permute-start(bf16[128,640]{1,0:T(8,128)(2,1)} %get-tuple-element.60), channel_id=1, source_target_pairs={{0,16},{1,17},{2,18},{3,19},{4,20},{5,21},{6,22},{7,23},{8,24},{9,... | collective-permute-start | bytes 491528 | tf_op jit(solution)/shard_map/ppermute | solution.py:327
  12.6 3.4 %queries.1 = (bf16[128,1536]{1,0:T(8,128)(2,1)S(1)}, bf16[128,1536]{1,0:T(8,128)(2,1)S(1)}, bf16[128,1536]{1,0:T(8,128)(2,1)S(1)}, bf16[128,1536]{1,0:T(8,128)(2...) custom-call(s32[1]{0:T(128)} %bitcast.info, ...), custom_call_target="tpu_custom_call" | custom-call | bytes 6291456 | tf_op jit(solution)/shard_map/queries/pallas_call | solution.py:401
  16.0 0.6 collective-permute-start.4
  16.6 0.4 collective-permute-done.3
  17.0 2.4 %collective-permute-start.6 = (bf16[256,640]{1,0:T(8,128)(2,1)S(1)}, bf16[256,640]{1,0:T(8,128)(2,1)S(1)}, u32[]{:S(2)}, u32[]{:S(2)}) collective-permute-start(bf16[256,640]{1,0:T(8,128)(2,1)S(1)} %get-tuple-element.118), channel_id=1, source_target_pairs={{0,2},{1,3},{2,4},{3,5},{4,6},{5,7},{6,8},{7,9},{8,10},{9,11},{10,... | collective-permute-start | bytes 983048 | tf_op jit(solution)/shard_map/ppermute | solution.py:342
  19.5 6.9 %collective-permute-done.4.refs_10_.refs_14_ = bf16[128,1536]{1,0:T(8,128)(2,1)S(1)} collective-permute-done((bf16[128,1536]{1,0:T(8,128)(2,1)S(1)}, bf16[128,1536]{1,0:T(8,128)(2,1)S(1)}, u32[]{:S(2)}, u32[]{:S(2)}) %collective-permute-start.4) | collective-permute-done | bytes 393248 | tf_op jit(solution)/shard_map/ppermute | solution.py:327
  26.4 0.0 collective-permute-done.2.refs_4_
  26.4 1.6 %collective-permute-start.8 = (bf16[64,4096]{1,0:T(8,128)(2,1)S(1)}, bf16[64,4096]{1,0:T(8,128)(2,1)S(1)}, u32[]{:S(2)}, u32[]{:S(2)}) collective-permute-start(bf16[64,4096]{1,0:T(8,128)(2,1)S(1)} %collective-permute-done.1.refs_1_), channel_id=1, source_target_pairs={{0,4},{1,5},{2,6},{3,7},{4,8},{5,9},{6,10},{7,11},{8,12},{9,13},{1... | collective-permute-start | bytes 1572872 | tf_op jit(solution)/shard_map/ppermute | solution.py:330
  28.0 0.5 collective-permute-start.9
  28.5 0.7 collective-permute-start.7
  29.1 0.6 collective-permute-start.10
  29.7 0.2 collective-permute-start.11
  29.9 0.0 collective-permute-done.7
  30.0 10.2 %collective-permute-done.10.refs_11_.refs_15_ = bf16[128,1536]{1,0:T(8,128)(2,1)S(1)} collective-permute-done((bf16[128,1536]{1,0:T(8,128)(2,1)S(1)}, bf16[128,1536]{1,0:T(8,128)(2,1)S(1)}, u32[]{:S(2)}, u32[]{:S(2)}) %collective-permute-start.10) | collective-permute-done | bytes 393248 | tf_op jit(solution)/shard_map/ppermute | solution.py:327
  40.2 0.0 collective-permute-done.11.refs_9_.refs_13_
  40.2 0.2 collective-permute-done.8.refs_2_
  40.4 0.0 collective-permute-done.9.refs_5_
  40.4 1.1 %collective-permute-start.12 = (bf16[768,640]{1,0:T(8,128)(2,1)S(1)}, bf16[768,640]{1,0:T(8,128)(2,1)S(1)}, u32[]{:S(2)}, u32[]{:S(2)}) collective-permute-start(bf16[768,640]{1,0:T(8,128)(2,1)S(1)} %constant_dynamic-update-slice_fusion.2.own), channel_id=1, source_target_pairs={{0,1},{1,0},{2,3},{3,2},{4,5},{5,4},{6,7},{7,6},{8,9},{9,8},{10,11... | collective-permute-start | bytes 2949128 | tf_op jit(solution)/shard_map/ppermute | solution.py:327
  41.4 2.2 %collective-permute-start.13 = (bf16[64,4096]{1,0:T(8,128)(2,1)S(1)}, bf16[64,4096]{1,0:T(8,128)(2,1)S(1)}, u32[]{:S(2)}, u32[]{:S(2)}) collective-permute-start(bf16[64,4096]{1,0:T(8,128)(2,1)S(1)} %collective-permute-done.8.refs_2_), channel_id=1, source_target_pairs={{0,4},{1,5},{2,6},{3,7},{4,8},{5,9},{6,10},{7,11},{8,12},{9,13},{1... | collective-permute-start | bytes 1572872 | tf_op jit(solution)/shard_map/ppermute | solution.py:330
  43.6 1.3 %collective-permute-start.14 = (bf16[64,4096]{1,0:T(8,128)(2,1)S(1)}, bf16[64,4096]{1,0:T(8,128)(2,1)S(1)}, u32[]{:S(2)}, u32[]{:S(2)}) collective-permute-start(bf16[64,4096]{1,0:T(8,128)(2,1)S(1)} %collective-permute-done.8.refs_2_), channel_id=1, source_target_pairs={{0,2},{1,3},{2,0},{3,1},{4,6},{5,7},{6,4},{7,5},{8,10},{9,11},{10,... | collective-permute-start | bytes 1572872 | tf_op jit(solution)/shard_map/ppermute | solution.py:333
  45.0 1.5 %collective-permute-start.15 = (bf16[128,1536]{1,0:T(8,128)(2,1)S(1)}, bf16[128,1536]{1,0:T(8,128)(2,1)S(1)}, u32[]{:S(2)}, u32[]{:S(2)}) collective-permute-start(bf16[128,1536]{1,0:T(8,128)(2,1)S(1)} %get-tuple-element.80), channel_id=1, source_target_pairs={{0,16},{1,17},{2,18},{3,19},{4,20},{5,21},{6,22},{7,23},{8,24},{9,... | collective-permute-start | bytes 1179656 | tf_op jit(solution)/shard_map/ppermute | solution.py:327
  46.5 0.1 collective-permute-start.5
  46.6 1.4 %collective-permute-done.5 = bf16[1,8,16,576]{3,2,0,1:T(8,128)(2,1)S(1)} collective-permute-done((bf16[1,8,16,576]{3,2,0,1:T(8,128)(2,1)S(1)}, bf16[1,8,16,576]{3,2,0,1:T(8,128)(2,1)S(1)}, u32[]{:S(2)}, u32[]{:S(2)}) %collective-permute-start.5) | collective-permute-done | bytes 147488 | tf_op jit(solution)/shard_map/ppermute | solution.py:336
  48.0 7.5 %collective-permute-done.15.refs_10_.refs_14_ = bf16[128,1536]{1,0:T(8,128)(2,1)S(1)} collective-permute-done((bf16[128,1536]{1,0:T(8,128)(2,1)S(1)}, bf16[128,1536]{1,0:T(8,128)(2,1)S(1)}, u32[]{:S(2)}, u32[]{:S(2)}) %collective-permute-start.15) | collective-permute-done | bytes 393248 | tf_op jit(solution)/shard_map/ppermute | solution.py:327
  55.5 1.6 %collective-permute-done.13.refs_3_ = bf16[64,4096]{1,0:T(8,128)(2,1)S(1)} collective-permute-done((bf16[64,4096]{1,0:T(8,128)(2,1)S(1)}, bf16[64,4096]{1,0:T(8,128)(2,1)S(1)}, u32[]{:S(2)}, u32[]{:S(2)}) %collective-permute-start.13) | collective-permute-done | bytes 524320 | tf_op jit(solution)/shard_map/ppermute | solution.py:330
  57.1 0.1 collective-permute-done.14.refs_6_
  57.3 1.4 %collective-permute-start.17 = (bf16[2,4,16,576]{3,2,0,1:T(8,128)(2,1)S(1)}, bf16[2,4,16,576]{3,2,0,1:T(8,128)(2,1)S(1)}, u32[]{:S(2)}, u32[]{:S(2)}) collective-permute-start(bf16[2,4,16,576]{3,2,0,1:T(8,128)(2,1)S(1)} %fusion.2), channel_id=1, source_target_pairs={{0,2},{1,3},{2,0},{3,1},{4,6},{5,7},{6,4},{7,5},{8,10},{9,11},{10,... | collective-permute-start | bytes 442376 | tf_op jit(solution)/shard_map/ppermute | solution.py:336
  58.7 0.7 collective-permute-start.16
  59.4 1.6 %collective-permute-start.18 = (bf16[64,2048]{1,0:T(8,128)(2,1)S(1)}, bf16[64,2048]{1,0:T(8,128)(2,1)S(1)}, u32[]{:S(2)}, u32[]{:S(2)}) collective-permute-start(bf16[64,2048]{1,0:T(8,128)(2,1)S(1)} %slice.45), channel_id=1, source_target_pairs={{0,4},{1,5},{2,6},{3,7},{4,8},{5,9},{6,10},{7,11},{8,12},{9,13},{1... | collective-permute-start | bytes 786440 | tf_op jit(solution)/shard_map/ppermute | solution.py:330
  61.0 1.2 %collective-permute-start.20 = (bf16[128,1536]{1,0:T(8,128)(2,1)S(1)}, bf16[128,1536]{1,0:T(8,128)(2,1)S(1)}, u32[]{:S(2)}, u32[]{:S(2)}) collective-permute-start(bf16[128,1536]{1,0:T(8,128)(2,1)S(1)} %get-tuple-element.91), channel_id=1, source_target_pairs={{0,17},{1,16},{2,19},{3,18},{4,21},{5,20},{6,23},{7,22},{8,25},{9,... | collective-permute-start | bytes 1179656 | tf_op jit(solution)/shard_map/ppermute | solution.py:327
  62.2 0.6 keys.1
  62.8 1.6 %collective-permute-done.17 = bf16[2,4,16,576]{3,2,0,1:T(8,128)(2,1)S(1)} collective-permute-done((bf16[2,4,16,576]{3,2,0,1:T(8,128)(2,1)S(1)}, bf16[2,4,16,576]{3,2,0,1:T(8,128)(2,1)S(1)}, u32[]{:S(2)}, u32[]{:S(2)}) %collective-permute-start.17) | collective-permute-done | bytes 147488 | tf_op jit(solution)/shard_map/ppermute | solution.py:336
  64.4 0.1 fusion
  64.5 1.6 %collective-permute-start.21 = (bf16[4,2,16,576]{3,2,0,1:T(8,128)(2,1)S(1)}, bf16[4,2,16,576]{3,2,0,1:T(8,128)(2,1)S(1)}, u32[]{:S(2)}, u32[]{:S(2)}) collective-permute-start(bf16[4,2,16,576]{3,2,0,1:T(8,128)(2,1)S(1)} %get-tuple-element.94), channel_id=1, source_target_pairs={{0,4},{1,5},{2,6},{3,7},{4,0},{5,1},{6,2},{7,3},{8,12},{9,13},{10,... | collective-permute-start | bytes 442376 | tf_op jit(solution)/shard_map/ppermute | solution.py:336
  66.1 2.0 %collective-permute-done.16.refs_7_ = bf16[64,2048]{1,0:T(8,128)(2,1)S(1)} collective-permute-done((bf16[64,2048]{1,0:T(8,128)(2,1)S(1)}, bf16[64,2048]{1,0:T(8,128)(2,1)S(1)}, u32[]{:S(2)}, u32[]{:S(2)}) %collective-permute-start.16) | collective-permute-done | bytes 262176 | tf_op jit(solution)/shard_map/ppermute | solution.py:333
  68.1 9.0 %attend.3 = (bf16[128,1024]{1,0:T(8,128)(2,1)S(1)}, bf16[128,1024]{1,0:T(8,128)(2,1)S(1)}, bf16[128,1024]{1,0:T(8,128)(2,1)S(1)}, bf16[128,1024]{1,0:T(8,128)(2,1)S(1)}) custom-call(s32[1]{0:T(128)} %bitcast.1.info, bf16[2,640,512]{2,1,0:T(8,128)(2,1)S(1)} %get-tuple-element.74.latent, bf16[2,640,128]{2,1,0:T(8,128)(2,1)S(1)} %get-tuple-element.75.rope_even, ...), custom_call_target="tpu_custom_call" | custom-call | flops 4362076160 | bytes 8388608 | tf_op jit(solution)/shard_map/attend/pallas_call | solution.py:483
  77.1 1.5 %collective-permute-start.22 = (bf16[128,1024]{1,0:T(8,128)(2,1)S(1)}, bf16[128,1024]{1,0:T(8,128)(2,1)S(1)}, u32[]{:S(2)}, u32[]{:S(2)}) collective-permute-start(bf16[128,1024]{1,0:T(8,128)(2,1)S(1)} %get-tuple-element.96), channel_id=1, source_target_pairs={{0,16},{1,17},{2,18},{3,19},{4,20},{5,21},{6,22},{7,23},{8,24},{9,... | collective-permute-start | bytes 786440 | tf_op jit(solution)/shard_map/ppermute | solution.py:327
  78.6 0.1 fusion.1
  78.7 0.7 collective-permute-start.29
  79.4 0.0 collective-permute-done.19.refs_9_.refs_13_
  79.4 1.7 %collective-permute-start.31 = (bf16[8,1,16,576]{3,2,0,1:T(8,128)(2,1)S(1)}, bf16[8,1,16,576]{3,2,0,1:T(8,128)(2,1)S(1)}, u32[]{:S(2)}, u32[]{:S(2)}) collective-permute-start(bf16[8,1,16,576]{3,2,0,1:T(8,128)(2,1)S(1)} %get-tuple-element.109), channel_id=1, source_target_pairs={{0,8},{1,9},{2,10},{3,11},{4,12},{5,13},{6,14},{7,15},{8,0},{9,1},... | collective-permute-start | bytes 442376 | tf_op jit(solution)/shard_map/ppermute | solution.py:336
  81.1 4.5 %attend.4 = (bf16[128,512]{1,0:T(8,128)(2,1)S(1)}, bf16[128,512]{1,0:T(8,128)(2,1)S(1)}, bf16[128,512]{1,0:T(8,128)(2,1)S(1)}, bf16[128,512]{1,0:T(8,128)(2,1)S(1)}) custom-call(s32[1]{0:T(128)} %bitcast.1.info, bf16[2,640,512]{2,1,0:T(8,128)(2,1)S(1)} %get-tuple-element.74.latent, bf16[2,640,128]{2,1,0:T(8,128)(2,1)S(1)} %get-tuple-element.75.rope_even, ...), custom_call_target="tpu_custom_call" | custom-call | flops 2181038080 | bytes 4194304 | tf_op jit(solution)/shard_map/attend/pallas_call | solution.py:483
  85.6 1.7 %collective-permute-start.25 = (bf16[128,512]{1,0:T(8,128)(2,1)S(1)}, bf16[128,512]{1,0:T(8,128)(2,1)S(1)}, u32[]{:S(2)}, u32[]{:S(2)}) collective-permute-start(bf16[128,512]{1,0:T(8,128)(2,1)S(1)} %get-tuple-element.102), channel_id=1, source_target_pairs={{0,16},{1,17},{2,18},{3,19},{4,20},{5,21},{6,22},{7,23},{8,24},{9,... | collective-permute-start | bytes 393224 | tf_op jit(solution)/shard_map/ppermute | solution.py:327
  87.3 0.0 collective-permute-start.26
  87.3 4.5 %attend.5 = (bf16[128,512]{1,0:T(8,128)(2,1)S(1)}, bf16[128,512]{1,0:T(8,128)(2,1)S(1)}, bf16[128,512]{1,0:T(8,128)(2,1)S(1)}, bf16[128,512]{1,0:T(8,128)(2,1)S(1)}) custom-call(s32[1]{0:T(128)} %bitcast.1.info, bf16[2,640,512]{2,1,0:T(8,128)(2,1)S(1)} %get-tuple-element.74.latent, bf16[2,640,128]{2,1,0:T(8,128)(2,1)S(1)} %get-tuple-element.75.rope_even, ...), custom_call_target="tpu_custom_call" | custom-call | flops 2181038080 | bytes 4194304 | tf_op jit(solution)/shard_map/attend/pallas_call | solution.py:483
  91.8 1.7 %collective-permute-done.25.refs_7_ = bf16[128,512]{1,0:T(8,128)(2,1)S(1)} collective-permute-done((bf16[128,512]{1,0:T(8,128)(2,1)S(1)}, bf16[128,512]{1,0:T(8,128)(2,1)S(1)}, u32[]{:S(2)}, u32[]{:S(2)}) %collective-permute-start.25) | collective-permute-done | bytes 131104 | tf_op jit(solution)/shard_map/ppermute | solution.py:327
  93.5 0.0 collective-permute-start.24
  93.5 0.8 collective-permute-done.26.refs_10_
  94.3 1.1 %collective-permute-start.28 = (bf16[128,512]{1,0:T(8,128)(2,1)S(1)}, bf16[128,512]{1,0:T(8,128)(2,1)S(1)}, u32[]{:S(2)}, u32[]{:S(2)}) collective-permute-start(bf16[128,512]{1,0:T(8,128)(2,1)S(1)} %get-tuple-element.105), channel_id=1, source_target_pairs={{0,16},{1,17},{2,18},{3,19},{4,20},{5,21},{6,22},{7,23},{8,24},{9,... | collective-permute-start | bytes 393224 | tf_op jit(solution)/shard_map/ppermute | solution.py:327
  95.3 0.9 collective-permute-start.30
  96.2 0.2 collective-permute-start.27
  96.5 0.6 sort.1
  97.1 0.9 copy.9
  98.0 0.0 collective-permute-done.29.refs_9_
  98.0 2.6 %collective-permute-done.28.refs_8_ = bf16[128,512]{1,0:T(8,128)(2,1)S(1)} collective-permute-done((bf16[128,512]{1,0:T(8,128)(2,1)S(1)}, bf16[128,512]{1,0:T(8,128)(2,1)S(1)}, u32[]{:S(2)}, u32[]{:S(2)}) %collective-permute-start.28) | collective-permute-done | bytes 131104 | tf_op jit(solution)/shard_map/ppermute | solution.py:327
  100.5 2.2 %collective-permute-done.30.refs_11_ = bf16[128,512]{1,0:T(8,128)(2,1)S(1)} collective-permute-done((bf16[128,512]{1,0:T(8,128)(2,1)S(1)}, bf16[128,512]{1,0:T(8,128)(2,1)S(1)}, u32[]{:S(2)}, u32[]{:S(2)}) %collective-permute-start.30) | collective-permute-done | bytes 131104 | tf_op jit(solution)/shard_map/ppermute | solution.py:327
  102.7 1.4 %place.1 = bf16[128,8192]{1,0:T(8,128)(2,1)} custom-call(s32[1]{0:T(128)} %bitcast.info, bf16[128,1024]{1,0:T(8,128)(2,1)S(1)} %get-tuple-element.82.refs_0_, bf16[128,512]{1,0:T(8,128)(2,1)S(1)} %get-tuple-element.92.refs_1_, bf16[128,512]{1,0:T(8,128)(2,1)S(1)} %get-tuple-element.98.refs_2_, bf16[128,1024]{1,0:T(8,128)(2,1)S(1)} %collective-permute-done.23.refs_3_, ...), custom_call_target="tpu_custom_call" | custom-call | tf_op jit(solution)/shard_map/place/pallas_call | solution.py:532
  (27 shorter events, 0.4 us)
Async XLA Ops:
  1.6 1.7 %collective-permute-start = (bf16[32,4096]{1,0:T(8,128)(2,1)S(1)}, bf16[32,4096]{1,0:T(8,128)(2,1)S(1)}, u32[]{:S(2)}, u32[]{:S(2)}) collective-permute-start(bf16[32,4096]{1,0:T(8,128)(2,1)S(1)} %constant_dynamic-slice_fusion), channel_id=1, source_target_pairs={{0,1},{1,0},{2,3},{3,2},{4,5},{5,4},{6,7},{7,6},{8,9},{9,8},{10,11... | collective-permute-start | bytes 786440 | tf_op jit(solution)/shard_map/ppermute | solution.py:327
  4.3 22.1 %collective-permute-start.1 = (bf16[64,4096]{1,0:T(8,128)(2,1)S(1)}, bf16[64,4096]{1,0:T(8,128)(2,1)S(1)}, u32[]{:S(2)}, u32[]{:S(2)}) collective-permute-start(bf16[64,4096]{1,0:T(8,128)(2,1)S(1)} %pair.1.refs_0_), channel_id=1, source_target_pairs={{0,4},{1,5},{2,6},{3,7},{4,8},{5,9},{6,10},{7,11},{8,12},{9,13},{1... | collective-permute-start | bytes 1572872 | tf_op jit(solution)/shard_map/ppermute | solution.py:330
  7.3 19.1 %collective-permute-start.2 = (bf16[64,4096]{1,0:T(8,128)(2,1)S(1)}, bf16[64,4096]{1,0:T(8,128)(2,1)S(1)}, u32[]{:S(2)}, u32[]{:S(2)}) collective-permute-start(bf16[64,4096]{1,0:T(8,128)(2,1)S(1)} %pair.1.refs_0_), channel_id=1, source_target_pairs={{0,2},{1,3},{2,0},{3,1},{4,6},{5,7},{6,4},{7,5},{8,10},{9,11},{10,... | collective-permute-start | bytes 1572872 | tf_op jit(solution)/shard_map/ppermute | solution.py:333
  11.1 5.5 %copy-start.1 = (bf16[128,640]{1,0:T(8,128)(2,1)S(1)}, bf16[128,640]{1,0:T(8,128)(2,1)}, u32[]{:S(2)}) copy-start(bf16[128,640]{1,0:T(8,128)(2,1)} %get-tuple-element.60) | copy-start | bytes 491524
  11.1 5.9 %collective-permute-start.3 = (bf16[128,640]{1,0:T(8,128)(2,1)}, bf16[128,640]{1,0:T(8,128)(2,1)S(1)}, u32[]{:S(2)}, u32[]{:S(2)}) collective-permute-start(bf16[128,640]{1,0:T(8,128)(2,1)} %get-tuple-element.60), channel_id=1, source_target_pairs={{0,16},{1,17},{2,18},{3,19},{4,20},{5,21},{6,22},{7,23},{8,24},{9,... | collective-permute-start | bytes 491528 | tf_op jit(solution)/shard_map/ppermute | solution.py:327
  12.6 33.9 %copy-start = (bf16[256,576]{1,0:T(8,128)(2,1)S(1)}, bf16[256,576]{1,0:T(8,128)(2,1)}, u32[]{:S(2)}) copy-start(bf16[256,576]{1,0:T(8,128)(2,1)} %get-tuple-element.57) | copy-start | bytes 884740
  16.0 10.4 %collective-permute-start.4 = (bf16[128,1536]{1,0:T(8,128)(2,1)S(1)}, bf16[128,1536]{1,0:T(8,128)(2,1)S(1)}, u32[]{:S(2)}, u32[]{:S(2)}) collective-permute-start(bf16[128,1536]{1,0:T(8,128)(2,1)S(1)} %get-tuple-element.64), channel_id=1, source_target_pairs={{0,16},{1,17},{2,18},{3,19},{4,20},{5,21},{6,22},{7,23},{8,24},{9,... | collective-permute-start | bytes 1179656 | tf_op jit(solution)/shard_map/ppermute | solution.py:327
  17.0 12.7 %collective-permute-start.6 = (bf16[256,640]{1,0:T(8,128)(2,1)S(1)}, bf16[256,640]{1,0:T(8,128)(2,1)S(1)}, u32[]{:S(2)}, u32[]{:S(2)}) collective-permute-start(bf16[256,640]{1,0:T(8,128)(2,1)S(1)} %get-tuple-element.118), channel_id=1, source_target_pairs={{0,2},{1,3},{2,4},{3,5},{4,6},{5,7},{6,8},{7,9},{8,10},{9,11},{10,... | collective-permute-start | bytes 983048 | tf_op jit(solution)/shard_map/ppermute | solution.py:342
  26.4 14.0 %collective-permute-start.8 = (bf16[64,4096]{1,0:T(8,128)(2,1)S(1)}, bf16[64,4096]{1,0:T(8,128)(2,1)S(1)}, u32[]{:S(2)}, u32[]{:S(2)}) collective-permute-start(bf16[64,4096]{1,0:T(8,128)(2,1)S(1)} %collective-permute-done.1.refs_1_), channel_id=1, source_target_pairs={{0,4},{1,5},{2,6},{3,7},{4,8},{5,9},{6,10},{7,11},{8,12},{9,13},{1... | collective-permute-start | bytes 1572872 | tf_op jit(solution)/shard_map/ppermute | solution.py:330
  28.0 12.4 %collective-permute-start.9 = (bf16[64,4096]{1,0:T(8,128)(2,1)S(1)}, bf16[64,4096]{1,0:T(8,128)(2,1)S(1)}, u32[]{:S(2)}, u32[]{:S(2)}) collective-permute-start(bf16[64,4096]{1,0:T(8,128)(2,1)S(1)} %collective-permute-done.1.refs_1_), channel_id=1, source_target_pairs={{0,2},{1,3},{2,0},{3,1},{4,6},{5,7},{6,4},{7,5},{8,10},{9,11},{10,... | collective-permute-start | bytes 1572872 | tf_op jit(solution)/shard_map/ppermute | solution.py:333
  28.5 1.5 %collective-permute-start.7 = (bf16[256,640]{1,0:T(8,128)(2,1)S(1)}, bf16[256,640]{1,0:T(8,128)(2,1)S(1)}, u32[]{:S(2)}, u32[]{:S(2)}) collective-permute-start(bf16[256,640]{1,0:T(8,128)(2,1)S(1)} %get-tuple-element.118), channel_id=1, source_target_pairs={{1,5},{3,7},{5,9},{7,11},{9,13},{11,15},{17,21},{19,23},{21,25},{2... | collective-permute-start | bytes 983048 | tf_op jit(solution)/shard_map/ppermute | solution.py:342
  29.1 11.0 %collective-permute-start.10 = (bf16[128,1536]{1,0:T(8,128)(2,1)S(1)}, bf16[128,1536]{1,0:T(8,128)(2,1)S(1)}, u32[]{:S(2)}, u32[]{:S(2)}) collective-permute-start(bf16[128,1536]{1,0:T(8,128)(2,1)S(1)} %get-tuple-element.70), channel_id=1, source_target_pairs={{0,17},{1,16},{2,19},{3,18},{4,21},{5,20},{6,23},{7,22},{8,25},{9,... | collective-permute-start | bytes 1179656 | tf_op jit(solution)/shard_map/ppermute | solution.py:327
  29.7 10.4 %collective-permute-start.11 = (bf16[128,1536]{1,0:T(8,128)(2,1)S(1)}, bf16[128,1536]{1,0:T(8,128)(2,1)S(1)}, u32[]{:S(2)}, u32[]{:S(2)}) collective-permute-start(bf16[128,1536]{1,0:T(8,128)(2,1)S(1)} %get-tuple-element.72), channel_id=1, source_target_pairs={{0,1},{1,0},{2,3},{3,2},{4,5},{5,4},{6,7},{7,6},{8,9},{9,8},{10,11... | collective-permute-start | bytes 1179656 | tf_op jit(solution)/shard_map/ppermute | solution.py:327
  40.4 16.9 %collective-permute-start.12 = (bf16[768,640]{1,0:T(8,128)(2,1)S(1)}, bf16[768,640]{1,0:T(8,128)(2,1)S(1)}, u32[]{:S(2)}, u32[]{:S(2)}) collective-permute-start(bf16[768,640]{1,0:T(8,128)(2,1)S(1)} %constant_dynamic-update-slice_fusion.2.own), channel_id=1, source_target_pairs={{0,1},{1,0},{2,3},{3,2},{4,5},{5,4},{6,7},{7,6},{8,9},{9,8},{10,11... | collective-permute-start | bytes 2949128 | tf_op jit(solution)/shard_map/ppermute | solution.py:327
  41.4 15.7 %collective-permute-start.13 = (bf16[64,4096]{1,0:T(8,128)(2,1)S(1)}, bf16[64,4096]{1,0:T(8,128)(2,1)S(1)}, u32[]{:S(2)}, u32[]{:S(2)}) collective-permute-start(bf16[64,4096]{1,0:T(8,128)(2,1)S(1)} %collective-permute-done.8.refs_2_), channel_id=1, source_target_pairs={{0,4},{1,5},{2,6},{3,7},{4,8},{5,9},{6,10},{7,11},{8,12},{9,13},{1... | collective-permute-start | bytes 1572872 | tf_op jit(solution)/shard_map/ppermute | solution.py:330
  43.6 13.6 %collective-permute-start.14 = (bf16[64,4096]{1,0:T(8,128)(2,1)S(1)}, bf16[64,4096]{1,0:T(8,128)(2,1)S(1)}, u32[]{:S(2)}, u32[]{:S(2)}) collective-permute-start(bf16[64,4096]{1,0:T(8,128)(2,1)S(1)} %collective-permute-done.8.refs_2_), channel_id=1, source_target_pairs={{0,2},{1,3},{2,0},{3,1},{4,6},{5,7},{6,4},{7,5},{8,10},{9,11},{10,... | collective-permute-start | bytes 1572872 | tf_op jit(solution)/shard_map/ppermute | solution.py:333
  45.0 10.5 %collective-permute-start.15 = (bf16[128,1536]{1,0:T(8,128)(2,1)S(1)}, bf16[128,1536]{1,0:T(8,128)(2,1)S(1)}, u32[]{:S(2)}, u32[]{:S(2)}) collective-permute-start(bf16[128,1536]{1,0:T(8,128)(2,1)S(1)} %get-tuple-element.80), channel_id=1, source_target_pairs={{0,16},{1,17},{2,18},{3,19},{4,20},{5,21},{6,22},{7,23},{8,24},{9,... | collective-permute-start | bytes 1179656 | tf_op jit(solution)/shard_map/ppermute | solution.py:327
  46.5 1.5 %collective-permute-start.5 = (bf16[1,8,16,576]{3,2,0,1:T(8,128)(2,1)S(1)}, bf16[1,8,16,576]{3,2,0,1:T(8,128)(2,1)S(1)}, u32[]{:S(2)}, u32[]{:S(2)}) collective-permute-start(bf16[1,8,16,576]{3,2,0,1:T(8,128)(2,1)S(1)} %get-tuple-element.66), channel_id=1, source_target_pairs={{0,1},{1,0},{2,3},{3,2},{4,5},{5,4},{6,7},{7,6},{8,9},{9,8},{10,11... | collective-permute-start | bytes 442376 | tf_op jit(solution)/shard_map/ppermute | solution.py:336
  57.3 7.1 %collective-permute-start.17 = (bf16[2,4,16,576]{3,2,0,1:T(8,128)(2,1)S(1)}, bf16[2,4,16,576]{3,2,0,1:T(8,128)(2,1)S(1)}, u32[]{:S(2)}, u32[]{:S(2)}) collective-permute-start(bf16[2,4,16,576]{3,2,0,1:T(8,128)(2,1)S(1)} %fusion.2), channel_id=1, source_target_pairs={{0,2},{1,3},{2,0},{3,1},{4,6},{5,7},{6,4},{7,5},{8,10},{9,11},{10,... | collective-permute-start | bytes 442376 | tf_op jit(solution)/shard_map/ppermute | solution.py:336
  58.7 9.4 %collective-permute-start.16 = (bf16[64,2048]{1,0:T(8,128)(2,1)S(1)}, bf16[64,2048]{1,0:T(8,128)(2,1)S(1)}, u32[]{:S(2)}, u32[]{:S(2)}) collective-permute-start(bf16[64,2048]{1,0:T(8,128)(2,1)S(1)} %slice.41), channel_id=1, source_target_pairs={{0,2},{1,3},{2,0},{3,1},{4,6},{5,7},{6,4},{7,5},{8,10},{9,11},{10,... | collective-permute-start | bytes 786440 | tf_op jit(solution)/shard_map/ppermute | solution.py:333
  59.4 19.3 %collective-permute-start.18 = (bf16[64,2048]{1,0:T(8,128)(2,1)S(1)}, bf16[64,2048]{1,0:T(8,128)(2,1)S(1)}, u32[]{:S(2)}, u32[]{:S(2)}) collective-permute-start(bf16[64,2048]{1,0:T(8,128)(2,1)S(1)} %slice.45), channel_id=1, source_target_pairs={{0,4},{1,5},{2,6},{3,7},{4,8},{5,9},{6,10},{7,11},{8,12},{9,13},{1... | collective-permute-start | bytes 786440 | tf_op jit(solution)/shard_map/ppermute | solution.py:330
  61.0 18.5 %collective-permute-start.19 = (bf16[128,1536]{1,0:T(8,128)(2,1)S(1)}, bf16[128,1536]{1,0:T(8,128)(2,1)S(1)}, u32[]{:S(2)}, u32[]{:S(2)}) collective-permute-start(bf16[128,1536]{1,0:T(8,128)(2,1)S(1)} %get-tuple-element.89), channel_id=1, source_target_pairs={{0,1},{1,0},{2,3},{3,2},{4,5},{5,4},{6,7},{7,6},{8,9},{9,8},{10,11... | collective-permute-start | bytes 1179656 | tf_op jit(solution)/shard_map/ppermute | solution.py:327
  61.0 20.2 %collective-permute-start.20 = (bf16[128,1536]{1,0:T(8,128)(2,1)S(1)}, bf16[128,1536]{1,0:T(8,128)(2,1)S(1)}, u32[]{:S(2)}, u32[]{:S(2)}) collective-permute-start(bf16[128,1536]{1,0:T(8,128)(2,1)S(1)} %get-tuple-element.91), channel_id=1, source_target_pairs={{0,17},{1,16},{2,19},{3,18},{4,21},{5,20},{6,23},{7,22},{8,25},{9,... | collective-permute-start | bytes 1179656 | tf_op jit(solution)/shard_map/ppermute | solution.py:327
  64.5 14.1 %collective-permute-start.21 = (bf16[4,2,16,576]{3,2,0,1:T(8,128)(2,1)S(1)}, bf16[4,2,16,576]{3,2,0,1:T(8,128)(2,1)S(1)}, u32[]{:S(2)}, u32[]{:S(2)}) collective-permute-start(bf16[4,2,16,576]{3,2,0,1:T(8,128)(2,1)S(1)} %get-tuple-element.94), channel_id=1, source_target_pairs={{0,4},{1,5},{2,6},{3,7},{4,0},{5,1},{6,2},{7,3},{8,12},{9,13},{10,... | collective-permute-start | bytes 442376 | tf_op jit(solution)/shard_map/ppermute | solution.py:336
  77.1 10.2 %collective-permute-start.22 = (bf16[128,1024]{1,0:T(8,128)(2,1)S(1)}, bf16[128,1024]{1,0:T(8,128)(2,1)S(1)}, u32[]{:S(2)}, u32[]{:S(2)}) collective-permute-start(bf16[128,1024]{1,0:T(8,128)(2,1)S(1)} %get-tuple-element.96), channel_id=1, source_target_pairs={{0,16},{1,17},{2,18},{3,19},{4,20},{5,21},{6,22},{7,23},{8,24},{9,... | collective-permute-start | bytes 786440 | tf_op jit(solution)/shard_map/ppermute | solution.py:327
  78.6 17.6 %collective-permute-start.23 = (bf16[128,1024]{1,0:T(8,128)(2,1)S(1)}, bf16[128,1024]{1,0:T(8,128)(2,1)S(1)}, u32[]{:S(2)}, u32[]{:S(2)}) collective-permute-start(bf16[128,1024]{1,0:T(8,128)(2,1)S(1)} %get-tuple-element.99), channel_id=1, source_target_pairs={{0,1},{1,0},{2,3},{3,2},{4,5},{5,4},{6,7},{7,6},{8,9},{9,8},{10,11... | collective-permute-start | bytes 786440 | tf_op jit(solution)/shard_map/ppermute | solution.py:327
  78.7 19.3 %collective-permute-start.29 = (bf16[128,1024]{1,0:T(8,128)(2,1)S(1)}, bf16[128,1024]{1,0:T(8,128)(2,1)S(1)}, u32[]{:S(2)}, u32[]{:S(2)}) collective-permute-start(bf16[128,1024]{1,0:T(8,128)(2,1)S(1)} %get-tuple-element.106), channel_id=1, source_target_pairs={{0,17},{1,16},{2,19},{3,18},{4,21},{5,20},{6,23},{7,22},{8,25},{9,... | collective-permute-start | bytes 786440 | tf_op jit(solution)/shard_map/ppermute | solution.py:327
  79.4 15.9 %collective-permute-start.31 = (bf16[8,1,16,576]{3,2,0,1:T(8,128)(2,1)S(1)}, bf16[8,1,16,576]{3,2,0,1:T(8,128)(2,1)S(1)}, u32[]{:S(2)}, u32[]{:S(2)}) collective-permute-start(bf16[8,1,16,576]{3,2,0,1:T(8,128)(2,1)S(1)} %get-tuple-element.109), channel_id=1, source_target_pairs={{0,8},{1,9},{2,10},{3,11},{4,12},{5,13},{6,14},{7,15},{8,0},{9,1},... | collective-permute-start | bytes 442376 | tf_op jit(solution)/shard_map/ppermute | solution.py:336
  85.6 7.8 %collective-permute-start.25 = (bf16[128,512]{1,0:T(8,128)(2,1)S(1)}, bf16[128,512]{1,0:T(8,128)(2,1)S(1)}, u32[]{:S(2)}, u32[]{:S(2)}) collective-permute-start(bf16[128,512]{1,0:T(8,128)(2,1)S(1)} %get-tuple-element.102), channel_id=1, source_target_pairs={{0,16},{1,17},{2,18},{3,19},{4,20},{5,21},{6,22},{7,23},{8,24},{9,... | collective-permute-start | bytes 393224 | tf_op jit(solution)/shard_map/ppermute | solution.py:327
  87.3 7.0 %collective-permute-start.26 = (bf16[128,512]{1,0:T(8,128)(2,1)S(1)}, bf16[128,512]{1,0:T(8,128)(2,1)S(1)}, u32[]{:S(2)}, u32[]{:S(2)}) collective-permute-start(bf16[128,512]{1,0:T(8,128)(2,1)S(1)} %get-tuple-element.103), channel_id=1, source_target_pairs={{0,17},{1,16},{2,19},{3,18},{4,21},{5,20},{6,23},{7,22},{8,25},{9,... | collective-permute-start | bytes 393224 | tf_op jit(solution)/shard_map/ppermute | solution.py:327
  93.5 4.5 %collective-permute-start.24 = (bf16[128,512]{1,0:T(8,128)(2,1)S(1)}, bf16[128,512]{1,0:T(8,128)(2,1)S(1)}, u32[]{:S(2)}, u32[]{:S(2)}) collective-permute-start(bf16[128,512]{1,0:T(8,128)(2,1)S(1)} %get-tuple-element.100), channel_id=1, source_target_pairs={{0,1},{1,0},{2,3},{3,2},{4,5},{5,4},{6,7},{7,6},{8,9},{9,8},{10,11... | collective-permute-start | bytes 393224 | tf_op jit(solution)/shard_map/ppermute | solution.py:327
  94.3 6.3 %collective-permute-start.28 = (bf16[128,512]{1,0:T(8,128)(2,1)S(1)}, bf16[128,512]{1,0:T(8,128)(2,1)S(1)}, u32[]{:S(2)}, u32[]{:S(2)}) collective-permute-start(bf16[128,512]{1,0:T(8,128)(2,1)S(1)} %get-tuple-element.105), channel_id=1, source_target_pairs={{0,16},{1,17},{2,18},{3,19},{4,20},{5,21},{6,22},{7,23},{8,24},{9,... | collective-permute-start | bytes 393224 | tf_op jit(solution)/shard_map/ppermute | solution.py:327
  95.3 7.4 %collective-permute-start.30 = (bf16[128,512]{1,0:T(8,128)(2,1)S(1)}, bf16[128,512]{1,0:T(8,128)(2,1)S(1)}, u32[]{:S(2)}, u32[]{:S(2)}) collective-permute-start(bf16[128,512]{1,0:T(8,128)(2,1)S(1)} %get-tuple-element.107), channel_id=1, source_target_pairs={{0,17},{1,16},{2,19},{3,18},{4,21},{5,20},{6,23},{7,22},{8,25},{9,... | collective-permute-start | bytes 393224 | tf_op jit(solution)/shard_map/ppermute | solution.py:327
  96.2 6.5 %collective-permute-start.27 = (bf16[128,512]{1,0:T(8,128)(2,1)S(1)}, bf16[128,512]{1,0:T(8,128)(2,1)S(1)}, u32[]{:S(2)}, u32[]{:S(2)}) collective-permute-start(bf16[128,512]{1,0:T(8,128)(2,1)S(1)} %get-tuple-element.104), channel_id=1, source_target_pairs={{0,1},{1,0},{2,3},{3,2},{4,5},{5,4},{6,7},{7,6},{8,9},{9,8},{10,11... | collective-permute-start | bytes 393224 | tf_op jit(solution)/shard_map/ppermute | solution.py:327

commit v15 on v14

--- a/solution.py
+++ b/solution.py
@@ -20,16 +20,16 @@
 CHUNK_HEADS = (8, 8)
 PHASES = (
     ("z", "y0", "k", "q02", "b~", "f~"),
-    ("z", "y1", "q03", "q01", "e-"),
+    ("z", "y1", "q03", "q01"),
     ("z", "y2", "p", "q12"),
-    ("y3", "w", "q13~", "q11", "e-", "e-", "e-"),
+    ("y3", "w", "q13~", "q11"),
 )
 CHUNKS = len(CHUNK_HEADS)
 FIRST_HEAD = tuple(sum(CHUNK_HEADS[:j]) for j in range(CHUNKS))
 ROW = LAT + ROPE
 EXT = 640
 VMEM_LIMIT = 20 * 1024 * 1024
-CALLS = ((0, 0, 4), (1, 0, 2), (1, 2, 2))
+CALLS = ((0, 0, 2), (0, 2, 2), (1, 0, 2), (1, 2, 2))
 SMEM = pltpu.SMEM
 VMEM = pltpu.VMEM
 
@@ -417,8 +417,6 @@
     half = width // CHUNKS
     halves = []
     moved = [[queries[j]] + [None] * (QUAD - 1) for j in range(CHUNKS)]
-    held = outgoing.reshape(1, size, slot_count, ROW)
-    exchanged = []
     parts = {"r": tie(rows, pair_rows if outer else got)}
     for name in [name for phase in PHASES for name in phase + ("|",)]:
         kind, late = name[0], name[-1]
@@ -445,11 +443,6 @@
         elif kind == "p":
             own_rows = jnp.concatenate([both_groups, behind, far_behind], axis=0)
             other_rows = phases.send(late, quad_swap, own_rows, 1)
-        elif kind == "e" and outer:
-            half_of = held.shape[1] // 2
-            distance = 1 << len(exchanged)
-            exchanged.append(phases.send(late, pair_swap, held[:, half_of:], distance))
-            held = jnp.concatenate([held[:, :half_of], exchanged[-1]], axis=0)
         elif kind == "q":
             j, r = int(name[1]), int(name[2])
             moved[j][r] = phases.send(late, quad_swap, queries[r * CHUNKS + j], r)
@@ -502,14 +495,28 @@
             name="attend",
         )(mine_info, *keys, *pieces_of_weight, *moved[j], *moved[j])
 
+    held = outgoing.reshape(1, size, slot_count, ROW)
+    exchanged = []
+
+    def exchange(*others):
+        half_of = held.shape[1] // 2
+        moving = tie(held[:, half_of:], *others)
+        exchanged.append(pair_swap(moving, 1 << len(exchanged)))
+        return jnp.concatenate([held[:, :half_of], exchanged[-1]], axis=0)
+
+    if outer:
+        held = exchange(*line[outer - 1 :])
     results = []
     for call in CALLS:
         last = len(results) + 1 == len(CALLS)
-        mine_info = tie(mine_info, *exchanged[len(results) : len(results) + 1])
-        mine_info = tie(mine_info, *(results[0][2:3] if last else []))
+        if results:
+            mine_info = tie(mine_info, *halves[1:], *exchanged[len(results) - 1 : len(results)])
+        mine_info = tie(mine_info, *[piece for one in results[-2:-1] for piece in one[2:]])
         pieces = attend(*call)
         mine_info = tie(mine_info, pieces[0])
         before = results[-1][2:] if last else []
+        if outer and not last:
+            held = exchange(pieces[0])
         results.append(
             [pieces[0], quad_swap(tie(pieces[1], *before), 1)]
             + [quad_swap(pieces[r], r) for r in (2, 3)]

time: 104 us -> 106 us (1.019)
  starting transfers between devices: 33.5 us -> 34.9 us
    ppermute x4, waiting for transfers between devices: 1.87 us -> 10.9 us  [around(): lax.ppermute(array, 'ctx', [(i, (i + by) % size) for i in range(size)])]
    ppermute x18 -> x21, waiting for transfers between devices: 33.3 us -> 24.9 us  [quad_swap(): return lax.ppermute(array, ('groups', 'ctx'), pairs)]
    ppermute x18 -> x21, starting transfers between devices: 13.2 us -> 15.5 us  [quad_swap(): return lax.ppermute(array, ('groups', 'ctx'), pairs)]
    ppermute x4, starting transfers between devices: 4.84 us -> 3.05 us  [pair_swap(): return lax.ppermute(array, 'ctx', [(i, i ^ distance) for i in range(size)])]
    ppermute x4, waiting for transfers between devices: 3.01 us -> 1.6 us  [pair_swap(): return lax.ppermute(array, 'ctx', [(i, i ^ distance) for i in range(size)])]
    ppermute x4, waiting for transfers between devices: 2.11 us -> 3.32 us  [inner_swap(): return lax.ppermute(array, 'ctx', [(i, i ^ 2) for i in range(size)])]
    pallas_call x3 -> x4, Pallas kernels: 17.9 us -> 18 us  [attend(): pl.pallas_call(functools.partial(attend_kernel, outer), grid=(steps,), ou...]
  transfers between devices with their start and end apart: 32 -> 35, of which waited for: 15 -> 11; matrix products, arithmetic and copies ran while one was open for 1% -> 0% of each run, Pallas kernels for 24% -> 24%
where the time goes in v15:
time: 106 us
  waiting for transfers between devices  40.7 us (38%)
  starting transfers between devices  34.9 us (33%)
  Pallas kernels  27.3 us (26%)
  local copies, waits for them, and re-layouts  2.1 us (2%)
    ppermute x21, waiting for transfers between devices, quad_swap(): return lax.ppermute(array, ('groups', 'ctx'), pairs)  24.9 us
    pallas_call x4, Pallas kernels, attend(): pl.pallas_call(functools.partial(attend_kernel, outer), grid=(steps,), ou...  18 us
    ppermute x21, starting transfers between devices, quad_swap(): return lax.ppermute(array, ('groups', 'ctx'), pairs)  15.5 us
    ppermute x4, waiting for transfers between devices, around(): lax.ppermute(array, 'ctx', [(i, (i + by) % size) for i in range(size)])  10.9 us
    ppermute x4, starting transfers between devices, around(): lax.ppermute(array, 'ctx', [(i, (i + by) % size) for i in range(size)])  8.36 us
    ppermute x4, starting transfers between devices, inner_swap(): return lax.ppermute(array, 'ctx', [(i, i ^ 2) for i in range(size)])  4.91 us
    pallas_call x1, Pallas kernels, body(): pl.pallas_call(query_kernel, out_shape=[shape((tok, h * (NOPE + ROPE))) f...  3.38 us
    ppermute x4, waiting for transfers between devices, inner_swap(): return lax.ppermute(array, 'ctx', [(i, i ^ 2) for i in range(size)])  3.32 us
  transfers between devices with their start and end apart: 35, of which 11 were waited for; matrix products, arithmetic and copies ran while one was open for 0% of the time, Pallas kernels for 24%

profile of v15, /device:TPU:0, one launch (start us, length us, event | category | flops | bytes accessed | tf_op | source)
XLA Modules:
  0.0 106.1 jit_solution(15791726539398328618)
XLA Ops:
  0.6 1.0 constant_dynamic-slice_fusion
  1.6 0.5 collective-permute-start
  2.1 1.2 %collective-permute-done.got = bf16[32,4096]{1,0:T(8,128)(2,1)S(1)} collective-permute-done((bf16[32,4096]{1,0:T(8,128)(2,1)S(1)}, bf16[32,4096]{1,0:T(8,128)(2,1)S(1)}, u32[]{:S(2)}, u32[]{:S(2)}) %collective-permute-start) | collective-permute-done | bytes 262176 | tf_op jit(solution)/shard_map/ppermute | solution.py:327
  3.3 1.0 pair.1.refs_0_
  4.3 3.0 %collective-permute-start.4 = (bf16[64,4096]{1,0:T(8,128)(2,1)S(1)}, bf16[64,4096]{1,0:T(8,128)(2,1)S(1)}, u32[]{:S(2)}, u32[]{:S(2)}) collective-permute-start(bf16[64,4096]{1,0:T(8,128)(2,1)S(1)} %pair.1.refs_0_), channel_id=1, source_target_pairs={{0,4},{1,5},{2,6},{3,7},{4,8},{5,9},{6,10},{7,11},{8,12},{9,13},{1... | collective-permute-start | bytes 1572872 | tf_op jit(solution)/shard_map/ppermute | solution.py:330
  7.3 1.5 %collective-permute-start.5 = (bf16[64,4096]{1,0:T(8,128)(2,1)S(1)}, bf16[64,4096]{1,0:T(8,128)(2,1)S(1)}, u32[]{:S(2)}, u32[]{:S(2)}) collective-permute-start(bf16[64,4096]{1,0:T(8,128)(2,1)S(1)} %pair.1.refs_0_), channel_id=1, source_target_pairs={{0,2},{1,3},{2,0},{3,1},{4,6},{5,7},{6,4},{7,5},{8,10},{9,11},{10,... | collective-permute-start | bytes 1572872 | tf_op jit(solution)/shard_map/ppermute | solution.py:333
  8.8 2.3 %rows.1 = (bf16[128,640]{1,0:T(8,128)(2,1)}, f32[128,128]{1,0:T(8,128)}, f32[128,128]{1,0:T(8,128)}, bf16[256,576]{1,0:T(8,128)(2,1)}) custom-call(s32[1]{0:T(128)} %bitcast.1.info, s32[8]{0:T(128)} %lengths, bf16[576,128]{1,0:T(8,128)(2,1)} %bitcast.9, f32[1,512]{1,0:T(1,128)} %bitcast.10, s32[1,128]{1,0:T(1,128)} %bitcast.11, f32[1,128]{1,0:T(1,128)} %constant.30.clone.freq), custom_call_target="tpu_custom_call" | custom-call | tf_op jit(solution)/shard_map/rows/pallas_call | solution.py:377
  11.1 1.5 %collective-permute-start.1 = (bf16[128,640]{1,0:T(8,128)(2,1)}, bf16[128,640]{1,0:T(8,128)(2,1)S(1)}, u32[]{:S(2)}, u32[]{:S(2)}) collective-permute-start(bf16[128,640]{1,0:T(8,128)(2,1)} %get-tuple-element.65), channel_id=1, source_target_pairs={{0,16},{1,17},{2,18},{3,19},{4,20},{5,21},{6,22},{7,23},{8,24},{9,... | collective-permute-start | bytes 491528 | tf_op jit(solution)/shard_map/ppermute | solution.py:327
  12.6 3.4 %queries.1 = (bf16[128,1536]{1,0:T(8,128)(2,1)S(1)}, bf16[128,1536]{1,0:T(8,128)(2,1)S(1)}, bf16[128,1536]{1,0:T(8,128)(2,1)S(1)}, bf16[128,1536]{1,0:T(8,128)(2...) custom-call(s32[1]{0:T(128)} %bitcast.info, ...), custom_call_target="tpu_custom_call" | custom-call | bytes 6291456 | tf_op jit(solution)/shard_map/queries/pallas_call | solution.py:401
  16.0 0.6 collective-permute-start.6
  16.6 0.4 collective-permute-done.1
  17.0 2.4 %collective-permute-start.2 = (bf16[256,640]{1,0:T(8,128)(2,1)S(1)}, bf16[256,640]{1,0:T(8,128)(2,1)S(1)}, u32[]{:S(2)}, u32[]{:S(2)}) collective-permute-start(bf16[256,640]{1,0:T(8,128)(2,1)S(1)} %get-tuple-element.130), channel_id=1, source_target_pairs={{0,2},{1,3},{2,4},{3,5},{4,6},{5,7},{6,8},{7,9},{8,10},{9,11},{10,... | collective-permute-start | bytes 983048 | tf_op jit(solution)/shard_map/ppermute | solution.py:342
  19.5 6.9 %collective-permute-done.6.refs_10_.refs_14_ = bf16[128,1536]{1,0:T(8,128)(2,1)S(1)} collective-permute-done((bf16[128,1536]{1,0:T(8,128)(2,1)S(1)}, bf16[128,1536]{1,0:T(8,128)(2,1)S(1)}, u32[]{:S(2)}, u32[]{:S(2)}) %collective-permute-start.6) | collective-permute-done | bytes 393248 | tf_op jit(solution)/shard_map/ppermute | solution.py:327
  26.4 1.6 %collective-permute-start.7 = (bf16[64,4096]{1,0:T(8,128)(2,1)S(1)}, bf16[64,4096]{1,0:T(8,128)(2,1)S(1)}, u32[]{:S(2)}, u32[]{:S(2)}) collective-permute-start(bf16[64,4096]{1,0:T(8,128)(2,1)S(1)} %collective-permute-done.4.refs_1_), channel_id=1, source_target_pairs={{0,4},{1,5},{2,6},{3,7},{4,8},{5,9},{6,10},{7,11},{8,12},{9,13},{1... | collective-permute-start | bytes 1572872 | tf_op jit(solution)/shard_map/ppermute | solution.py:330
  28.0 0.5 collective-permute-start.8
  28.5 0.7 collective-permute-start.3
  29.1 0.6 collective-permute-start.9
  29.7 0.0 collective-permute-done.2
  29.7 0.2 collective-permute-start.10
  29.9 0.0 collective-permute-done.3
  30.0 10.2 %collective-permute-done.9.refs_11_.refs_15_ = bf16[128,1536]{1,0:T(8,128)(2,1)S(1)} collective-permute-done((bf16[128,1536]{1,0:T(8,128)(2,1)S(1)}, bf16[128,1536]{1,0:T(8,128)(2,1)S(1)}, u32[]{:S(2)}, u32[]{:S(2)}) %collective-permute-start.9) | collective-permute-done | bytes 393248 | tf_op jit(solution)/shard_map/ppermute | solution.py:327
  40.2 0.0 collective-permute-done.10.refs_9_.refs_13_
  40.2 0.2 collective-permute-done.7.refs_2_
  40.4 1.1 %collective-permute-start.11 = (bf16[768,640]{1,0:T(8,128)(2,1)S(1)}, bf16[768,640]{1,0:T(8,128)(2,1)S(1)}, u32[]{:S(2)}, u32[]{:S(2)}) collective-permute-start(bf16[768,640]{1,0:T(8,128)(2,1)S(1)} %constant_dynamic-update-slice_fusion.2.own), channel_id=1, source_target_pairs={{0,1},{1,0},{2,3},{3,2},{4,5},{5,4},{6,7},{7,6},{8,9},{9,8},{10,11... | collective-permute-start | bytes 2949128 | tf_op jit(solution)/shard_map/ppermute | solution.py:327
  41.4 2.2 %collective-permute-start.12 = (bf16[64,4096]{1,0:T(8,128)(2,1)S(1)}, bf16[64,4096]{1,0:T(8,128)(2,1)S(1)}, u32[]{:S(2)}, u32[]{:S(2)}) collective-permute-start(bf16[64,4096]{1,0:T(8,128)(2,1)S(1)} %collective-permute-done.7.refs_2_), channel_id=1, source_target_pairs={{0,4},{1,5},{2,6},{3,7},{4,8},{5,9},{6,10},{7,11},{8,12},{9,13},{1... | collective-permute-start | bytes 1572872 | tf_op jit(solution)/shard_map/ppermute | solution.py:330
  43.6 1.3 %collective-permute-start.13 = (bf16[64,4096]{1,0:T(8,128)(2,1)S(1)}, bf16[64,4096]{1,0:T(8,128)(2,1)S(1)}, u32[]{:S(2)}, u32[]{:S(2)}) collective-permute-start(bf16[64,4096]{1,0:T(8,128)(2,1)S(1)} %collective-permute-done.7.refs_2_), channel_id=1, source_target_pairs={{0,2},{1,3},{2,0},{3,1},{4,6},{5,7},{6,4},{7,5},{8,10},{9,11},{10,... | collective-permute-start | bytes 1572872 | tf_op jit(solution)/shard_map/ppermute | solution.py:333
  45.0 1.5 %collective-permute-start.14 = (bf16[128,1536]{1,0:T(8,128)(2,1)S(1)}, bf16[128,1536]{1,0:T(8,128)(2,1)S(1)}, u32[]{:S(2)}, u32[]{:S(2)}) collective-permute-start(bf16[128,1536]{1,0:T(8,128)(2,1)S(1)} %get-tuple-element.83), channel_id=1, source_target_pairs={{0,16},{1,17},{2,18},{3,19},{4,20},{5,21},{6,22},{7,23},{8,24},{9,... | collective-permute-start | bytes 1179656 | tf_op jit(solution)/shard_map/ppermute | solution.py:327
  46.5 10.6 %collective-permute-done.12.refs_3_ = bf16[64,4096]{1,0:T(8,128)(2,1)S(1)} collective-permute-done((bf16[64,4096]{1,0:T(8,128)(2,1)S(1)}, bf16[64,4096]{1,0:T(8,128)(2,1)S(1)}, u32[]{:S(2)}, u32[]{:S(2)}) %collective-permute-start.12) | collective-permute-done | bytes 524320 | tf_op jit(solution)/shard_map/ppermute | solution.py:330
  57.1 0.0 collective-permute-start.17
  57.2 0.0 collective-permute-done.14.refs_10_.refs_14_
  57.2 0.1 collective-permute-done.13.refs_6_
  57.2 0.0 collective-permute-done.11.other
  57.3 1.6 %collective-permute-start.15 = (bf16[64,2048]{1,0:T(8,128)(2,1)S(1)}, bf16[64,2048]{1,0:T(8,128)(2,1)S(1)}, u32[]{:S(2)}, u32[]{:S(2)}) collective-permute-start(bf16[64,2048]{1,0:T(8,128)(2,1)S(1)} %slice.40), channel_id=1, source_target_pairs={{0,2},{1,3},{2,0},{3,1},{4,6},{5,7},{6,4},{7,5},{8,10},{9,11},{10,... | collective-permute-start | bytes 786440 | tf_op jit(solution)/shard_map/ppermute | solution.py:333
  58.8 1.6 %collective-permute-start.16 = (bf16[64,2048]{1,0:T(8,128)(2,1)S(1)}, bf16[64,2048]{1,0:T(8,128)(2,1)S(1)}, u32[]{:S(2)}, u32[]{:S(2)}) collective-permute-start(bf16[64,2048]{1,0:T(8,128)(2,1)S(1)} %slice.41), channel_id=1, source_target_pairs={{0,4},{1,5},{2,6},{3,7},{4,8},{5,9},{6,10},{7,11},{8,12},{9,13},{1... | collective-permute-start | bytes 786440 | tf_op jit(solution)/shard_map/ppermute | solution.py:330
  60.5 0.1 collective-permute-start.21
  60.5 1.6 %collective-permute-start.22 = (bf16[128,1536]{1,0:T(8,128)(2,1)S(1)}, bf16[128,1536]{1,0:T(8,128)(2,1)S(1)}, u32[]{:S(2)}, u32[]{:S(2)}) collective-permute-start(bf16[128,1536]{1,0:T(8,128)(2,1)S(1)} %get-tuple-element.102), channel_id=1, source_target_pairs={{0,17},{1,16},{2,19},{3,18},{4,21},{5,20},{6,23},{7,22},{8,25},{9,... | collective-permute-start | bytes 1179656 | tf_op jit(solution)/shard_map/ppermute | solution.py:327
  62.1 0.6 keys.1
  62.7 3.2 %collective-permute-done.15.refs_7_ = bf16[64,2048]{1,0:T(8,128)(2,1)S(1)} collective-permute-done((bf16[64,2048]{1,0:T(8,128)(2,1)S(1)}, bf16[64,2048]{1,0:T(8,128)(2,1)S(1)}, u32[]{:S(2)}, u32[]{:S(2)}) %collective-permute-start.15) | collective-permute-done | bytes 262176 | tf_op jit(solution)/shard_map/ppermute | solution.py:333
  66.0 4.5 %attend.4 = (bf16[128,512]{1,0:T(8,128)(2,1)S(1)}, bf16[128,512]{1,0:T(8,128)(2,1)S(1)}, bf16[128,512]{1,0:T(8,128)(2,1)S(1)}, bf16[128,512]{1,0:T(8,128)(2,1)S(1)}) custom-call(s32[1]{0:T(128)} %bitcast.1.info, bf16[2,640,512]{2,1,0:T(8,128)(2,1)S(1)} %get-tuple-element.77.latent, bf16[2,640,128]{2,1,0:T(8,128)(2,1)S(1)} %get-tuple-element.78.rope_even, ...), custom_call_target="tpu_custom_call" | custom-call | flops 2181038080 | bytes 4194304 | tf_op jit(solution)/shard_map/attend/pallas_call | solution.py:476
  70.5 1.6 %collective-permute-start.18 = (bf16[2,4,16,576]{3,2,0,1:T(8,128)(2,1)S(1)}, bf16[2,4,16,576]{3,2,0,1:T(8,128)(2,1)S(1)}, u32[]{:S(2)}, u32[]{:S(2)}) collective-permute-start(bf16[2,4,16,576]{3,2,0,1:T(8,128)(2,1)S(1)} %fusion.2), channel_id=1, source_target_pairs={{0,2},{1,3},{2,0},{3,1},{4,6},{5,7},{6,4},{7,5},{8,10},{9,11},{10,... | collective-permute-start | bytes 442376 | tf_op jit(solution)/shard_map/ppermute | solution.py:336
  72.1 1.5 %collective-permute-start.19 = (bf16[128,512]{1,0:T(8,128)(2,1)S(1)}, bf16[128,512]{1,0:T(8,128)(2,1)S(1)}, u32[]{:S(2)}, u32[]{:S(2)}) collective-permute-start(bf16[128,512]{1,0:T(8,128)(2,1)S(1)} %get-tuple-element.95), channel_id=1, source_target_pairs={{0,16},{1,17},{2,18},{3,19},{4,20},{5,21},{6,22},{7,23},{8,24},{9,... | collective-permute-start | bytes 393224 | tf_op jit(solution)/shard_map/ppermute | solution.py:327
  73.6 4.5 %attend.5 = (bf16[128,512]{1,0:T(8,128)(2,1)S(1)}, bf16[128,512]{1,0:T(8,128)(2,1)S(1)}, bf16[128,512]{1,0:T(8,128)(2,1)S(1)}, bf16[128,512]{1,0:T(8,128)(2,1)S(1)}) custom-call(s32[1]{0:T(128)} %bitcast.1.info, bf16[2,640,512]{2,1,0:T(8,128)(2,1)S(1)} %get-tuple-element.77.latent, bf16[2,640,128]{2,1,0:T(8,128)(2,1)S(1)} %get-tuple-element.78.rope_even, ...), custom_call_target="tpu_custom_call" | custom-call | flops 2181038080 | bytes 4194304 | tf_op jit(solution)/shard_map/attend/pallas_call | solution.py:476
  78.1 0.9 collective-permute-start.24
  78.9 1.2 %collective-permute-start.25 = (bf16[128,512]{1,0:T(8,128)(2,1)S(1)}, bf16[128,512]{1,0:T(8,128)(2,1)S(1)}, u32[]{:S(2)}, u32[]{:S(2)}) collective-permute-start(bf16[128,512]{1,0:T(8,128)(2,1)S(1)} %get-tuple-element.108), channel_id=1, source_target_pairs={{0,17},{1,16},{2,19},{3,18},{4,21},{5,20},{6,23},{7,22},{8,25},{9,... | collective-permute-start | bytes 393224 | tf_op jit(solution)/shard_map/ppermute | solution.py:327
  80.2 0.2 collective-permute-start.26
  80.3 0.1 fusion
  80.4 0.4 collective-permute-start.27
  80.8 0.2 collective-permute-start.23
  81.0 4.5 %attend.6 = (bf16[128,512]{1,0:T(8,128)(2,1)S(1)}, bf16[128,512]{1,0:T(8,128)(2,1)S(1)}, bf16[128,512]{1,0:T(8,128)(2,1)S(1)}, bf16[128,512]{1,0:T(8,128)(2,1)S(1)}) custom-call(s32[1]{0:T(128)} %bitcast.1.info, bf16[2,640,512]{2,1,0:T(8,128)(2,1)S(1)} %get-tuple-element.77.latent, bf16[2,640,128]{2,1,0:T(8,128)(2,1)S(1)} %get-tuple-element.78.rope_even, ...), custom_call_target="tpu_custom_call" | custom-call | flops 2181038080 | bytes 4194304 | tf_op jit(solution)/shard_map/attend/pallas_call | solution.py:476
  85.5 1.6 %collective-permute-done.23 = bf16[4,2,16,576]{3,2,0,1:T(8,128)(2,1)S(1)} collective-permute-done((bf16[4,2,16,576]{3,2,0,1:T(8,128)(2,1)S(1)}, bf16[4,2,16,576]{3,2,0,1:T(8,128)(2,1)S(1)}, u32[]{:S(2)}, u32[]{:S(2)}) %collective-permute-start.23) | collective-permute-done | bytes 147488 | tf_op jit(solution)/shard_map/ppermute | solution.py:336
  87.1 1.4 %collective-permute-start.29 = (bf16[128,512]{1,0:T(8,128)(2,1)S(1)}, bf16[128,512]{1,0:T(8,128)(2,1)S(1)}, u32[]{:S(2)}, u32[]{:S(2)}) collective-permute-start(bf16[128,512]{1,0:T(8,128)(2,1)S(1)} %get-tuple-element.115), channel_id=1, source_target_pairs={{0,16},{1,17},{2,18},{3,19},{4,20},{5,21},{6,22},{7,23},{8,24},{9,... | collective-permute-start | bytes 393224 | tf_op jit(solution)/shard_map/ppermute | solution.py:327
  88.5 0.1 fusion.1
  88.6 1.3 %collective-permute-start.34 = (bf16[8,1,16,576]{3,2,0,1:T(8,128)(2,1)S(1)}, bf16[8,1,16,576]{3,2,0,1:T(8,128)(2,1)S(1)}, u32[]{:S(2)}, u32[]{:S(2)}) collective-permute-start(bf16[8,1,16,576]{3,2,0,1:T(8,128)(2,1)S(1)} %get-tuple-element.121), channel_id=1, source_target_pairs={{0,8},{1,9},{2,10},{3,11},{4,12},{5,13},{6,14},{7,15},{8,0},{9,1},... | collective-permute-start | bytes 442376 | tf_op jit(solution)/shard_map/ppermute | solution.py:336
  89.9 4.5 %attend.7 = (bf16[128,512]{1,0:T(8,128)(2,1)S(1)}, bf16[128,512]{1,0:T(8,128)(2,1)S(1)}, bf16[128,512]{1,0:T(8,128)(2,1)S(1)}, bf16[128,512]{1,0:T(8,128)(2,1)S(1)}) custom-call(s32[1]{0:T(128)} %bitcast.1.info, bf16[2,640,512]{2,1,0:T(8,128)(2,1)S(1)} %get-tuple-element.77.latent, bf16[2,640,128]{2,1,0:T(8,128)(2,1)S(1)} %get-tuple-element.78.rope_even, ...), custom_call_target="tpu_custom_call" | custom-call | flops 2181038080 | bytes 4194304 | tf_op jit(solution)/shard_map/attend/pallas_call | solution.py:476
  94.4 0.5 collective-permute-start.28
  94.9 0.1 collective-permute-start.31
  95.0 1.4 %collective-permute-start.32 = (bf16[128,512]{1,0:T(8,128)(2,1)S(1)}, bf16[128,512]{1,0:T(8,128)(2,1)S(1)}, u32[]{:S(2)}, u32[]{:S(2)}) collective-permute-start(bf16[128,512]{1,0:T(8,128)(2,1)S(1)} %get-tuple-element.118), channel_id=1, source_target_pairs={{0,16},{1,17},{2,18},{3,19},{4,20},{5,21},{6,22},{7,23},{8,24},{9,... | collective-permute-start | bytes 393224 | tf_op jit(solution)/shard_map/ppermute | solution.py:327
  96.4 0.3 collective-permute-start.33
  96.8 4.6 %collective-permute-done.32.refs_11_ = bf16[128,512]{1,0:T(8,128)(2,1)S(1)} collective-permute-done((bf16[128,512]{1,0:T(8,128)(2,1)S(1)}, bf16[128,512]{1,0:T(8,128)(2,1)S(1)}, u32[]{:S(2)}, u32[]{:S(2)}) %collective-permute-start.32) | collective-permute-done | bytes 131104 | tf_op jit(solution)/shard_map/ppermute | solution.py:327
  101.4 1.7 %collective-permute-done.33.refs_15_ = bf16[128,512]{1,0:T(8,128)(2,1)S(1)} collective-permute-done((bf16[128,512]{1,0:T(8,128)(2,1)S(1)}, bf16[128,512]{1,0:T(8,128)(2,1)S(1)}, u32[]{:S(2)}, u32[]{:S(2)}) %collective-permute-start.33) | collective-permute-done | bytes 131104 | tf_op jit(solution)/shard_map/ppermute | solution.py:327
  103.1 1.4 %place.1 = bf16[128,8192]{1,0:T(8,128)(2,1)} custom-call(s32[1]{0:T(128)} %bitcast.info, bf16[128,512]{1,0:T(8,128)(2,1)S(1)} %get-tuple-element.85.refs_0_, bf16[128,512]{1,0:T(8,128)(2,1)S(1)} %get-tuple-element.91.refs_1_, bf16[128,512]{1,0:T(8,128)(2,1)S(1)} %get-tuple-element.103.refs_2_, bf16[128,512]{1,0:T(8,128)(2,1)S(1)} %get-tuple-element.110.refs_3_, ...), custom_call_target="tpu_custom_call" | custom-call | tf_op jit(solution)/shard_map/place/pallas_call | solution.py:539
  104.5 0.1 maximum_bitcast_fusion.relative
  104.6 0.6 sort.1
  105.2 0.9 copy.9
  (34 shorter events, 0.3 us)
Async XLA Ops:
  1.6 1.7 %collective-permute-start = (bf16[32,4096]{1,0:T(8,128)(2,1)S(1)}, bf16[32,4096]{1,0:T(8,128)(2,1)S(1)}, u32[]{:S(2)}, u32[]{:S(2)}) collective-permute-start(bf16[32,4096]{1,0:T(8,128)(2,1)S(1)} %constant_dynamic-slice_fusion), channel_id=1, source_target_pairs={{0,1},{1,0},{2,3},{3,2},{4,5},{5,4},{6,7},{7,6},{8,9},{9,8},{10,11... | collective-permute-start | bytes 786440 | tf_op jit(solution)/shard_map/ppermute | solution.py:327
  4.3 22.1 %collective-permute-start.4 = (bf16[64,4096]{1,0:T(8,128)(2,1)S(1)}, bf16[64,4096]{1,0:T(8,128)(2,1)S(1)}, u32[]{:S(2)}, u32[]{:S(2)}) collective-permute-start(bf16[64,4096]{1,0:T(8,128)(2,1)S(1)} %pair.1.refs_0_), channel_id=1, source_target_pairs={{0,4},{1,5},{2,6},{3,7},{4,8},{5,9},{6,10},{7,11},{8,12},{9,13},{1... | collective-permute-start | bytes 1572872 | tf_op jit(solution)/shard_map/ppermute | solution.py:330
  7.3 19.1 %collective-permute-start.5 = (bf16[64,4096]{1,0:T(8,128)(2,1)S(1)}, bf16[64,4096]{1,0:T(8,128)(2,1)S(1)}, u32[]{:S(2)}, u32[]{:S(2)}) collective-permute-start(bf16[64,4096]{1,0:T(8,128)(2,1)S(1)} %pair.1.refs_0_), channel_id=1, source_target_pairs={{0,2},{1,3},{2,0},{3,1},{4,6},{5,7},{6,4},{7,5},{8,10},{9,11},{10,... | collective-permute-start | bytes 1572872 | tf_op jit(solution)/shard_map/ppermute | solution.py:333
  11.1 5.5 %copy-start.1 = (bf16[128,640]{1,0:T(8,128)(2,1)S(1)}, bf16[128,640]{1,0:T(8,128)(2,1)}, u32[]{:S(2)}) copy-start(bf16[128,640]{1,0:T(8,128)(2,1)} %get-tuple-element.65) | copy-start | bytes 491524
  11.1 5.9 %collective-permute-start.1 = (bf16[128,640]{1,0:T(8,128)(2,1)}, bf16[128,640]{1,0:T(8,128)(2,1)S(1)}, u32[]{:S(2)}, u32[]{:S(2)}) collective-permute-start(bf16[128,640]{1,0:T(8,128)(2,1)} %get-tuple-element.65), channel_id=1, source_target_pairs={{0,16},{1,17},{2,18},{3,19},{4,20},{5,21},{6,22},{7,23},{8,24},{9,... | collective-permute-start | bytes 491528 | tf_op jit(solution)/shard_map/ppermute | solution.py:327
  12.6 33.9 %copy-start = (bf16[256,576]{1,0:T(8,128)(2,1)S(1)}, bf16[256,576]{1,0:T(8,128)(2,1)}, u32[]{:S(2)}) copy-start(bf16[256,576]{1,0:T(8,128)(2,1)} %get-tuple-element.88) | copy-start | bytes 884740
  16.0 10.4 %collective-permute-start.6 = (bf16[128,1536]{1,0:T(8,128)(2,1)S(1)}, bf16[128,1536]{1,0:T(8,128)(2,1)S(1)}, u32[]{:S(2)}, u32[]{:S(2)}) collective-permute-start(bf16[128,1536]{1,0:T(8,128)(2,1)S(1)} %get-tuple-element.69), channel_id=1, source_target_pairs={{0,16},{1,17},{2,18},{3,19},{4,20},{5,21},{6,22},{7,23},{8,24},{9,... | collective-permute-start | bytes 1179656 | tf_op jit(solution)/shard_map/ppermute | solution.py:327
  17.0 12.7 %collective-permute-start.2 = (bf16[256,640]{1,0:T(8,128)(2,1)S(1)}, bf16[256,640]{1,0:T(8,128)(2,1)S(1)}, u32[]{:S(2)}, u32[]{:S(2)}) collective-permute-start(bf16[256,640]{1,0:T(8,128)(2,1)S(1)} %get-tuple-element.130), channel_id=1, source_target_pairs={{0,2},{1,3},{2,4},{3,5},{4,6},{5,7},{6,8},{7,9},{8,10},{9,11},{10,... | collective-permute-start | bytes 983048 | tf_op jit(solution)/shard_map/ppermute | solution.py:342
  26.4 14.0 %collective-permute-start.7 = (bf16[64,4096]{1,0:T(8,128)(2,1)S(1)}, bf16[64,4096]{1,0:T(8,128)(2,1)S(1)}, u32[]{:S(2)}, u32[]{:S(2)}) collective-permute-start(bf16[64,4096]{1,0:T(8,128)(2,1)S(1)} %collective-permute-done.4.refs_1_), channel_id=1, source_target_pairs={{0,4},{1,5},{2,6},{3,7},{4,8},{5,9},{6,10},{7,11},{8,12},{9,13},{1... | collective-permute-start | bytes 1572872 | tf_op jit(solution)/shard_map/ppermute | solution.py:330
  28.0 12.4 %collective-permute-start.8 = (bf16[64,4096]{1,0:T(8,128)(2,1)S(1)}, bf16[64,4096]{1,0:T(8,128)(2,1)S(1)}, u32[]{:S(2)}, u32[]{:S(2)}) collective-permute-start(bf16[64,4096]{1,0:T(8,128)(2,1)S(1)} %collective-permute-done.4.refs_1_), channel_id=1, source_target_pairs={{0,2},{1,3},{2,0},{3,1},{4,6},{5,7},{6,4},{7,5},{8,10},{9,11},{10,... | collective-permute-start | bytes 1572872 | tf_op jit(solution)/shard_map/ppermute | solution.py:333
  28.5 1.5 %collective-permute-start.3 = (bf16[256,640]{1,0:T(8,128)(2,1)S(1)}, bf16[256,640]{1,0:T(8,128)(2,1)S(1)}, u32[]{:S(2)}, u32[]{:S(2)}) collective-permute-start(bf16[256,640]{1,0:T(8,128)(2,1)S(1)} %get-tuple-element.130), channel_id=1, source_target_pairs={{1,5},{3,7},{5,9},{7,11},{9,13},{11,15},{17,21},{19,23},{21,25},{2... | collective-permute-start | bytes 983048 | tf_op jit(solution)/shard_map/ppermute | solution.py:342
  29.1 11.0 %collective-permute-start.9 = (bf16[128,1536]{1,0:T(8,128)(2,1)S(1)}, bf16[128,1536]{1,0:T(8,128)(2,1)S(1)}, u32[]{:S(2)}, u32[]{:S(2)}) collective-permute-start(bf16[128,1536]{1,0:T(8,128)(2,1)S(1)} %get-tuple-element.73), channel_id=1, source_target_pairs={{0,17},{1,16},{2,19},{3,18},{4,21},{5,20},{6,23},{7,22},{8,25},{9,... | collective-permute-start | bytes 1179656 | tf_op jit(solution)/shard_map/ppermute | solution.py:327
  29.7 10.4 %collective-permute-start.10 = (bf16[128,1536]{1,0:T(8,128)(2,1)S(1)}, bf16[128,1536]{1,0:T(8,128)(2,1)S(1)}, u32[]{:S(2)}, u32[]{:S(2)}) collective-permute-start(bf16[128,1536]{1,0:T(8,128)(2,1)S(1)} %get-tuple-element.75), channel_id=1, source_target_pairs={{0,1},{1,0},{2,3},{3,2},{4,5},{5,4},{6,7},{7,6},{8,9},{9,8},{10,11... | collective-permute-start | bytes 1179656 | tf_op jit(solution)/shard_map/ppermute | solution.py:327
  40.4 16.9 %collective-permute-start.11 = (bf16[768,640]{1,0:T(8,128)(2,1)S(1)}, bf16[768,640]{1,0:T(8,128)(2,1)S(1)}, u32[]{:S(2)}, u32[]{:S(2)}) collective-permute-start(bf16[768,640]{1,0:T(8,128)(2,1)S(1)} %constant_dynamic-update-slice_fusion.2.own), channel_id=1, source_target_pairs={{0,1},{1,0},{2,3},{3,2},{4,5},{5,4},{6,7},{7,6},{8,9},{9,8},{10,11... | collective-permute-start | bytes 2949128 | tf_op jit(solution)/shard_map/ppermute | solution.py:327
  41.4 15.7 %collective-permute-start.12 = (bf16[64,4096]{1,0:T(8,128)(2,1)S(1)}, bf16[64,4096]{1,0:T(8,128)(2,1)S(1)}, u32[]{:S(2)}, u32[]{:S(2)}) collective-permute-start(bf16[64,4096]{1,0:T(8,128)(2,1)S(1)} %collective-permute-done.7.refs_2_), channel_id=1, source_target_pairs={{0,4},{1,5},{2,6},{3,7},{4,8},{5,9},{6,10},{7,11},{8,12},{9,13},{1... | collective-permute-start | bytes 1572872 | tf_op jit(solution)/shard_map/ppermute | solution.py:330
  43.6 13.6 %collective-permute-start.13 = (bf16[64,4096]{1,0:T(8,128)(2,1)S(1)}, bf16[64,4096]{1,0:T(8,128)(2,1)S(1)}, u32[]{:S(2)}, u32[]{:S(2)}) collective-permute-start(bf16[64,4096]{1,0:T(8,128)(2,1)S(1)} %collective-permute-done.7.refs_2_), channel_id=1, source_target_pairs={{0,2},{1,3},{2,0},{3,1},{4,6},{5,7},{6,4},{7,5},{8,10},{9,11},{10,... | collective-permute-start | bytes 1572872 | tf_op jit(solution)/shard_map/ppermute | solution.py:333
  45.0 12.2 %collective-permute-start.14 = (bf16[128,1536]{1,0:T(8,128)(2,1)S(1)}, bf16[128,1536]{1,0:T(8,128)(2,1)S(1)}, u32[]{:S(2)}, u32[]{:S(2)}) collective-permute-start(bf16[128,1536]{1,0:T(8,128)(2,1)S(1)} %get-tuple-element.83), channel_id=1, source_target_pairs={{0,16},{1,17},{2,18},{3,19},{4,20},{5,21},{6,22},{7,23},{8,24},{9,... | collective-permute-start | bytes 1179656 | tf_op jit(solution)/shard_map/ppermute | solution.py:327
  57.1 3.3 %collective-permute-start.17 = (bf16[1,8,16,576]{3,2,0,1:T(8,128)(2,1)S(1)}, bf16[1,8,16,576]{3,2,0,1:T(8,128)(2,1)S(1)}, u32[]{:S(2)}, u32[]{:S(2)}) collective-permute-start(bf16[1,8,16,576]{3,2,0,1:T(8,128)(2,1)S(1)} %get-tuple-element.89), channel_id=1, source_target_pairs={{0,1},{1,0},{2,3},{3,2},{4,5},{5,4},{6,7},{7,6},{8,9},{9,8},{10,11... | collective-permute-start | bytes 442376 | tf_op jit(solution)/shard_map/ppermute | solution.py:336
  57.3 8.7 %collective-permute-start.15 = (bf16[64,2048]{1,0:T(8,128)(2,1)S(1)}, bf16[64,2048]{1,0:T(8,128)(2,1)S(1)}, u32[]{:S(2)}, u32[]{:S(2)}) collective-permute-start(bf16[64,2048]{1,0:T(8,128)(2,1)S(1)} %slice.40), channel_id=1, source_target_pairs={{0,2},{1,3},{2,0},{3,1},{4,6},{5,7},{6,4},{7,5},{8,10},{9,11},{10,... | collective-permute-start | bytes 786440 | tf_op jit(solution)/shard_map/ppermute | solution.py:333
  58.8 11.6 %collective-permute-start.16 = (bf16[64,2048]{1,0:T(8,128)(2,1)S(1)}, bf16[64,2048]{1,0:T(8,128)(2,1)S(1)}, u32[]{:S(2)}, u32[]{:S(2)}) collective-permute-start(bf16[64,2048]{1,0:T(8,128)(2,1)S(1)} %slice.41), channel_id=1, source_target_pairs={{0,4},{1,5},{2,6},{3,7},{4,8},{5,9},{6,10},{7,11},{8,12},{9,13},{1... | collective-permute-start | bytes 786440 | tf_op jit(solution)/shard_map/ppermute | solution.py:330
  60.5 20.0 %collective-permute-start.21 = (bf16[128,1536]{1,0:T(8,128)(2,1)S(1)}, bf16[128,1536]{1,0:T(8,128)(2,1)S(1)}, u32[]{:S(2)}, u32[]{:S(2)}) collective-permute-start(bf16[128,1536]{1,0:T(8,128)(2,1)S(1)} %get-tuple-element.100), channel_id=1, source_target_pairs={{0,1},{1,0},{2,3},{3,2},{4,5},{5,4},{6,7},{7,6},{8,9},{9,8},{10,11... | collective-permute-start | bytes 1179656 | tf_op jit(solution)/shard_map/ppermute | solution.py:327
  60.5 20.3 %collective-permute-start.22 = (bf16[128,1536]{1,0:T(8,128)(2,1)S(1)}, bf16[128,1536]{1,0:T(8,128)(2,1)S(1)}, u32[]{:S(2)}, u32[]{:S(2)}) collective-permute-start(bf16[128,1536]{1,0:T(8,128)(2,1)S(1)} %get-tuple-element.102), channel_id=1, source_target_pairs={{0,17},{1,16},{2,19},{3,18},{4,21},{5,20},{6,23},{7,22},{8,25},{9,... | collective-permute-start | bytes 1179656 | tf_op jit(solution)/shard_map/ppermute | solution.py:327
  70.5 7.6 %collective-permute-start.18 = (bf16[2,4,16,576]{3,2,0,1:T(8,128)(2,1)S(1)}, bf16[2,4,16,576]{3,2,0,1:T(8,128)(2,1)S(1)}, u32[]{:S(2)}, u32[]{:S(2)}) collective-permute-start(bf16[2,4,16,576]{3,2,0,1:T(8,128)(2,1)S(1)} %fusion.2), channel_id=1, source_target_pairs={{0,2},{1,3},{2,0},{3,1},{4,6},{5,7},{6,4},{7,5},{8,10},{9,11},{10,... | collective-permute-start | bytes 442376 | tf_op jit(solution)/shard_map/ppermute | solution.py:336
  72.1 6.9 %collective-permute-start.19 = (bf16[128,512]{1,0:T(8,128)(2,1)S(1)}, bf16[128,512]{1,0:T(8,128)(2,1)S(1)}, u32[]{:S(2)}, u32[]{:S(2)}) collective-permute-start(bf16[128,512]{1,0:T(8,128)(2,1)S(1)} %get-tuple-element.95), channel_id=1, source_target_pairs={{0,16},{1,17},{2,18},{3,19},{4,20},{5,21},{6,22},{7,23},{8,24},{9,... | collective-permute-start | bytes 393224 | tf_op jit(solution)/shard_map/ppermute | solution.py:327
  73.6 6.6 %collective-permute-start.20 = (bf16[128,512]{1,0:T(8,128)(2,1)S(1)}, bf16[128,512]{1,0:T(8,128)(2,1)S(1)}, u32[]{:S(2)}, u32[]{:S(2)}) collective-permute-start(bf16[128,512]{1,0:T(8,128)(2,1)S(1)} %get-tuple-element.96), channel_id=1, source_target_pairs={{0,17},{1,16},{2,19},{3,18},{4,21},{5,20},{6,23},{7,22},{8,25},{9,... | collective-permute-start | bytes 393224 | tf_op jit(solution)/shard_map/ppermute | solution.py:327
  78.1 10.4 %collective-permute-start.24 = (bf16[128,512]{1,0:T(8,128)(2,1)S(1)}, bf16[128,512]{1,0:T(8,128)(2,1)S(1)}, u32[]{:S(2)}, u32[]{:S(2)}) collective-permute-start(bf16[128,512]{1,0:T(8,128)(2,1)S(1)} %get-tuple-element.107), channel_id=1, source_target_pairs={{0,16},{1,17},{2,18},{3,19},{4,20},{5,21},{6,22},{7,23},{8,24},{9,... | collective-permute-start | bytes 393224 | tf_op jit(solution)/shard_map/ppermute | solution.py:327
  78.9 9.6 %collective-permute-start.25 = (bf16[128,512]{1,0:T(8,128)(2,1)S(1)}, bf16[128,512]{1,0:T(8,128)(2,1)S(1)}, u32[]{:S(2)}, u32[]{:S(2)}) collective-permute-start(bf16[128,512]{1,0:T(8,128)(2,1)S(1)} %get-tuple-element.108), channel_id=1, source_target_pairs={{0,17},{1,16},{2,19},{3,18},{4,21},{5,20},{6,23},{7,22},{8,25},{9,... | collective-permute-start | bytes 393224 | tf_op jit(solution)/shard_map/ppermute | solution.py:327
  80.2 14.9 %collective-permute-start.26 = (bf16[128,512]{1,0:T(8,128)(2,1)S(1)}, bf16[128,512]{1,0:T(8,128)(2,1)S(1)}, u32[]{:S(2)}, u32[]{:S(2)}) collective-permute-start(bf16[128,512]{1,0:T(8,128)(2,1)S(1)} %get-tuple-element.111), channel_id=1, source_target_pairs={{0,1},{1,0},{2,3},{3,2},{4,5},{5,4},{6,7},{7,6},{8,9},{9,8},{10,11... | collective-permute-start | bytes 393224 | tf_op jit(solution)/shard_map/ppermute | solution.py:327
  80.4 16.0 %collective-permute-start.27 = (bf16[128,512]{1,0:T(8,128)(2,1)S(1)}, bf16[128,512]{1,0:T(8,128)(2,1)S(1)}, u32[]{:S(2)}, u32[]{:S(2)}) collective-permute-start(bf16[128,512]{1,0:T(8,128)(2,1)S(1)} %get-tuple-element.112), channel_id=1, source_target_pairs={{0,1},{1,0},{2,3},{3,2},{4,5},{5,4},{6,7},{7,6},{8,9},{9,8},{10,11... | collective-permute-start | bytes 393224 | tf_op jit(solution)/shard_map/ppermute | solution.py:327
  80.8 6.3 %collective-permute-start.23 = (bf16[4,2,16,576]{3,2,0,1:T(8,128)(2,1)S(1)}, bf16[4,2,16,576]{3,2,0,1:T(8,128)(2,1)S(1)}, u32[]{:S(2)}, u32[]{:S(2)}) collective-permute-start(bf16[4,2,16,576]{3,2,0,1:T(8,128)(2,1)S(1)} %get-tuple-element.105), channel_id=1, source_target_pairs={{0,4},{1,5},{2,6},{3,7},{4,0},{5,1},{6,2},{7,3},{8,12},{9,13},{10,... | collective-permute-start | bytes 442376 | tf_op jit(solution)/shard_map/ppermute | solution.py:336
  87.1 7.3 %collective-permute-start.29 = (bf16[128,512]{1,0:T(8,128)(2,1)S(1)}, bf16[128,512]{1,0:T(8,128)(2,1)S(1)}, u32[]{:S(2)}, u32[]{:S(2)}) collective-permute-start(bf16[128,512]{1,0:T(8,128)(2,1)S(1)} %get-tuple-element.115), channel_id=1, source_target_pairs={{0,16},{1,17},{2,18},{3,19},{4,20},{5,21},{6,22},{7,23},{8,24},{9,... | collective-permute-start | bytes 393224 | tf_op jit(solution)/shard_map/ppermute | solution.py:327
  88.5 6.4 %collective-permute-start.30 = (bf16[128,512]{1,0:T(8,128)(2,1)S(1)}, bf16[128,512]{1,0:T(8,128)(2,1)S(1)}, u32[]{:S(2)}, u32[]{:S(2)}) collective-permute-start(bf16[128,512]{1,0:T(8,128)(2,1)S(1)} %get-tuple-element.116), channel_id=1, source_target_pairs={{0,17},{1,16},{2,19},{3,18},{4,21},{5,20},{6,23},{7,22},{8,25},{9,... | collective-permute-start | bytes 393224 | tf_op jit(solution)/shard_map/ppermute | solution.py:327
  88.6 15.9 %collective-permute-start.34 = (bf16[8,1,16,576]{3,2,0,1:T(8,128)(2,1)S(1)}, bf16[8,1,16,576]{3,2,0,1:T(8,128)(2,1)S(1)}, u32[]{:S(2)}, u32[]{:S(2)}) collective-permute-start(bf16[8,1,16,576]{3,2,0,1:T(8,128)(2,1)S(1)} %get-tuple-element.121), channel_id=1, source_target_pairs={{0,8},{1,9},{2,10},{3,11},{4,12},{5,13},{6,14},{7,15},{8,0},{9,1},... | collective-permute-start | bytes 442376 | tf_op jit(solution)/shard_map/ppermute | solution.py:336
  94.4 2.4 %collective-permute-start.28 = (bf16[128,512]{1,0:T(8,128)(2,1)S(1)}, bf16[128,512]{1,0:T(8,128)(2,1)S(1)}, u32[]{:S(2)}, u32[]{:S(2)}) collective-permute-start(bf16[128,512]{1,0:T(8,128)(2,1)S(1)} %get-tuple-element.113), channel_id=1, source_target_pairs={{0,1},{1,0},{2,3},{3,2},{4,5},{5,4},{6,7},{7,6},{8,9},{9,8},{10,11... | collective-permute-start | bytes 393224 | tf_op jit(solution)/shard_map/ppermute | solution.py:327
  94.9 1.9 %collective-permute-start.31 = (bf16[128,512]{1,0:T(8,128)(2,1)S(1)}, bf16[128,512]{1,0:T(8,128)(2,1)S(1)}, u32[]{:S(2)}, u32[]{:S(2)}) collective-permute-start(bf16[128,512]{1,0:T(8,128)(2,1)S(1)} %get-tuple-element.117), channel_id=1, source_target_pairs={{0,1},{1,0},{2,3},{3,2},{4,5},{5,4},{6,7},{7,6},{8,9},{9,8},{10,11... | collective-permute-start | bytes 393224 | tf_op jit(solution)/shard_map/ppermute | solution.py:327
  95.0 6.3 %collective-permute-start.32 = (bf16[128,512]{1,0:T(8,128)(2,1)S(1)}, bf16[128,512]{1,0:T(8,128)(2,1)S(1)}, u32[]{:S(2)}, u32[]{:S(2)}) collective-permute-start(bf16[128,512]{1,0:T(8,128)(2,1)S(1)} %get-tuple-element.118), channel_id=1, source_target_pairs={{0,16},{1,17},{2,18},{3,19},{4,20},{5,21},{6,22},{7,23},{8,24},{9,... | collective-permute-start | bytes 393224 | tf_op jit(solution)/shard_map/ppermute | solution.py:327
  96.4 6.6 %collective-permute-start.33 = (bf16[128,512]{1,0:T(8,128)(2,1)S(1)}, bf16[128,512]{1,0:T(8,128)(2,1)S(1)}, u32[]{:S(2)}, u32[]{:S(2)}) collective-permute-start(bf16[128,512]{1,0:T(8,128)(2,1)S(1)} %get-tuple-element.119), channel_id=1, source_target_pairs={{0,17},{1,16},{2,19},{3,18},{4,21},{5,20},{6,23},{7,22},{8,25},{9,... | collective-permute-start | bytes 393224 | tf_op jit(solution)/shard_map/ppermute | solution.py:327

commit v16 on v15

--- a/solution.py
+++ b/solution.py
@@ -29,7 +29,7 @@
 ROW = LAT + ROPE
 EXT = 640
 VMEM_LIMIT = 20 * 1024 * 1024
-CALLS = ((0, 0, 2), (0, 2, 2), (1, 0, 2), (1, 2, 2))
+CALLS = ((0, 0, 4), (1, 0, 2), (1, 2, 2))
 SMEM = pltpu.SMEM
 VMEM = pltpu.VMEM
 
@@ -506,12 +506,13 @@
 
     if outer:
         held = exchange(*line[outer - 1 :])
+        held = exchange(halves[0])
     results = []
     for call in CALLS:
         last = len(results) + 1 == len(CALLS)
         if results:
-            mine_info = tie(mine_info, *halves[1:], *exchanged[len(results) - 1 : len(results)])
-        mine_info = tie(mine_info, *[piece for one in results[-2:-1] for piece in one[2:]])
+            mine_info = tie(mine_info, *halves[1:], *exchanged[len(results) : len(results) + 1])
+        mine_info = tie(mine_info, *(results[0][2:3] if last else []))
         pieces = attend(*call)
         mine_info = tie(mine_info, pieces[0])
         before = results[-1][2:] if last else []
@@ -544,7 +545,7 @@
         scratch_shapes=[pltpu.SemaphoreType.DMA((len(pieces),))],
         compiler_params=params,
         name="place",
-    )(quarter_info, *pieces)
+    )(tie(quarter_info, decode_cache), *pieces)
     return (attn_out, decode_cache)
 
 

time: 106 us -> 105 us (level)
    ppermute x4, waiting for transfers between devices: 1.6 us -> 0.21 us  [pair_swap(): return lax.ppermute(array, 'ctx', [(i, i ^ distance) for i in range(size)])]
    ppermute x21 -> x18, starting transfers between devices: 15.5 us -> 14.1 us  [quad_swap(): return lax.ppermute(array, ('groups', 'ctx'), pairs)]
    ppermute x21 -> x18, waiting for transfers between devices: 24.9 us -> 25.8 us  [quad_swap(): return lax.ppermute(array, ('groups', 'ctx'), pairs)]
    pallas_call x4 -> x3, Pallas kernels: 18 us -> 17.9 us  [attend(): pl.pallas_call(functools.partial(attend_kernel, outer), grid=(steps,), ou...]
  transfers between devices with their start and end apart: 35 -> 32, of which waited for: 11 -> 14; matrix products, arithmetic and copies ran while one was open for 0% -> 1% of each run, Pallas kernels for 24% -> 24%
where the time goes in v16:
time: 105 us
  waiting for transfers between devices  40.2 us (38%)
  starting transfers between devices  33.9 us (32%)
  Pallas kernels  27.2 us (26%)
  local copies, waits for them, and re-layouts  2.1 us (2%)
    ppermute x18, waiting for transfers between devices, quad_swap(): return lax.ppermute(array, ('groups', 'ctx'), pairs)  25.8 us
    pallas_call x3, Pallas kernels, attend(): pl.pallas_call(functools.partial(attend_kernel, outer), grid=(steps,), ou...  17.9 us
    ppermute x18, starting transfers between devices, quad_swap(): return lax.ppermute(array, ('groups', 'ctx'), pairs)  14.1 us
    ppermute x4, waiting for transfers between devices, around(): lax.ppermute(array, 'ctx', [(i, (i + by) % size) for i in range(size)])  10.9 us
    ppermute x4, starting transfers between devices, around(): lax.ppermute(array, 'ctx', [(i, (i + by) % size) for i in range(size)])  8.36 us
    ppermute x4, starting transfers between devices, inner_swap(): return lax.ppermute(array, 'ctx', [(i, i ^ 2) for i in range(size)])  4.91 us
    ppermute x4, waiting for transfers between devices, inner_swap(): return lax.ppermute(array, 'ctx', [(i, i ^ 2) for i in range(size)])  3.39 us
    pallas_call x1, Pallas kernels, body(): pl.pallas_call(query_kernel, out_shape=[shape((tok, h * (NOPE + ROPE))) f...  3.38 us
  transfers between devices with their start and end apart: 32, of which 14 were waited for; matrix products, arithmetic and copies ran while one was open for 1% of the time, Pallas kernels for 24%

profile of v16, /device:TPU:0, one launch (start us, length us, event | category | flops | bytes accessed | tf_op | source)
XLA Modules:
  0.0 104.6 jit_solution(14989957089662921532)
XLA Ops:
  0.6 1.0 constant_dynamic-slice_fusion
  1.6 0.5 collective-permute-start
  2.1 1.2 %collective-permute-done.got = bf16[32,4096]{1,0:T(8,128)(2,1)S(1)} collective-permute-done((bf16[32,4096]{1,0:T(8,128)(2,1)S(1)}, bf16[32,4096]{1,0:T(8,128)(2,1)S(1)}, u32[]{:S(2)}, u32[]{:S(2)}) %collective-permute-start) | collective-permute-done | bytes 262176 | tf_op jit(solution)/shard_map/ppermute | solution.py:327
  3.3 1.0 pair.1.refs_0_
  4.3 3.0 %collective-permute-start.4 = (bf16[64,4096]{1,0:T(8,128)(2,1)S(1)}, bf16[64,4096]{1,0:T(8,128)(2,1)S(1)}, u32[]{:S(2)}, u32[]{:S(2)}) collective-permute-start(bf16[64,4096]{1,0:T(8,128)(2,1)S(1)} %pair.1.refs_0_), channel_id=1, source_target_pairs={{0,4},{1,5},{2,6},{3,7},{4,8},{5,9},{6,10},{7,11},{8,12},{9,13},{1... | collective-permute-start | bytes 1572872 | tf_op jit(solution)/shard_map/ppermute | solution.py:330
  7.3 1.5 %collective-permute-start.5 = (bf16[64,4096]{1,0:T(8,128)(2,1)S(1)}, bf16[64,4096]{1,0:T(8,128)(2,1)S(1)}, u32[]{:S(2)}, u32[]{:S(2)}) collective-permute-start(bf16[64,4096]{1,0:T(8,128)(2,1)S(1)} %pair.1.refs_0_), channel_id=1, source_target_pairs={{0,2},{1,3},{2,0},{3,1},{4,6},{5,7},{6,4},{7,5},{8,10},{9,11},{10,... | collective-permute-start | bytes 1572872 | tf_op jit(solution)/shard_map/ppermute | solution.py:333
  8.8 2.3 %rows.1 = (bf16[128,640]{1,0:T(8,128)(2,1)}, f32[128,128]{1,0:T(8,128)}, f32[128,128]{1,0:T(8,128)}, bf16[256,576]{1,0:T(8,128)(2,1)}) custom-call(s32[1]{0:T(128)} %bitcast.1.info, s32[8]{0:T(128)} %lengths, bf16[576,128]{1,0:T(8,128)(2,1)} %bitcast.9, f32[1,512]{1,0:T(1,128)} %bitcast.10, s32[1,128]{1,0:T(1,128)} %bitcast.11, f32[1,128]{1,0:T(1,128)} %constant.30.clone.freq), custom_call_target="tpu_custom_call" | custom-call | tf_op jit(solution)/shard_map/rows/pallas_call | solution.py:377
  11.1 1.5 %collective-permute-start.1 = (bf16[128,640]{1,0:T(8,128)(2,1)}, bf16[128,640]{1,0:T(8,128)(2,1)S(1)}, u32[]{:S(2)}, u32[]{:S(2)}) collective-permute-start(bf16[128,640]{1,0:T(8,128)(2,1)} %get-tuple-element.59), channel_id=1, source_target_pairs={{0,16},{1,17},{2,18},{3,19},{4,20},{5,21},{6,22},{7,23},{8,24},{9,... | collective-permute-start | bytes 491528 | tf_op jit(solution)/shard_map/ppermute | solution.py:327
  12.6 3.4 %queries.1 = (bf16[128,1536]{1,0:T(8,128)(2,1)S(1)}, bf16[128,1536]{1,0:T(8,128)(2,1)S(1)}, bf16[128,1536]{1,0:T(8,128)(2,1)S(1)}, bf16[128,1536]{1,0:T(8,128)(2...) custom-call(s32[1]{0:T(128)} %bitcast.info, ...), custom_call_target="tpu_custom_call" | custom-call | bytes 6291456 | tf_op jit(solution)/shard_map/queries/pallas_call | solution.py:401
  16.0 0.6 collective-permute-start.6
  16.6 0.4 collective-permute-done.1
  17.0 2.4 %collective-permute-start.2 = (bf16[256,640]{1,0:T(8,128)(2,1)S(1)}, bf16[256,640]{1,0:T(8,128)(2,1)S(1)}, u32[]{:S(2)}, u32[]{:S(2)}) collective-permute-start(bf16[256,640]{1,0:T(8,128)(2,1)S(1)} %get-tuple-element.118), channel_id=1, source_target_pairs={{0,2},{1,3},{2,4},{3,5},{4,6},{5,7},{6,8},{7,9},{8,10},{9,11},{10,... | collective-permute-start | bytes 983048 | tf_op jit(solution)/shard_map/ppermute | solution.py:342
  19.5 6.9 %collective-permute-done.6.refs_10_.refs_14_ = bf16[128,1536]{1,0:T(8,128)(2,1)S(1)} collective-permute-done((bf16[128,1536]{1,0:T(8,128)(2,1)S(1)}, bf16[128,1536]{1,0:T(8,128)(2,1)S(1)}, u32[]{:S(2)}, u32[]{:S(2)}) %collective-permute-start.6) | collective-permute-done | bytes 393248 | tf_op jit(solution)/shard_map/ppermute | solution.py:327
  26.4 0.0 collective-permute-done.4.refs_1_
  26.4 0.0 collective-permute-done.5.refs_4_
  26.4 1.6 %collective-permute-start.7 = (bf16[64,4096]{1,0:T(8,128)(2,1)S(1)}, bf16[64,4096]{1,0:T(8,128)(2,1)S(1)}, u32[]{:S(2)}, u32[]{:S(2)}) collective-permute-start(bf16[64,4096]{1,0:T(8,128)(2,1)S(1)} %collective-permute-done.4.refs_1_), channel_id=1, source_target_pairs={{0,4},{1,5},{2,6},{3,7},{4,8},{5,9},{6,10},{7,11},{8,12},{9,13},{1... | collective-permute-start | bytes 1572872 | tf_op jit(solution)/shard_map/ppermute | solution.py:330
  28.0 0.5 collective-permute-start.8
  28.5 0.7 collective-permute-start.3
  29.1 0.6 collective-permute-start.9
  29.7 0.2 collective-permute-start.10
  29.9 0.0 collective-permute-done.3
  30.0 10.2 %collective-permute-done.9.refs_11_.refs_15_ = bf16[128,1536]{1,0:T(8,128)(2,1)S(1)} collective-permute-done((bf16[128,1536]{1,0:T(8,128)(2,1)S(1)}, bf16[128,1536]{1,0:T(8,128)(2,1)S(1)}, u32[]{:S(2)}, u32[]{:S(2)}) %collective-permute-start.9) | collective-permute-done | bytes 393248 | tf_op jit(solution)/shard_map/ppermute | solution.py:327
  40.2 0.0 collective-permute-done.10.refs_9_.refs_13_
  40.2 0.2 collective-permute-done.7.refs_2_
  40.4 0.0 collective-permute-done.8.refs_5_
  40.4 1.1 %collective-permute-start.11 = (bf16[768,640]{1,0:T(8,128)(2,1)S(1)}, bf16[768,640]{1,0:T(8,128)(2,1)S(1)}, u32[]{:S(2)}, u32[]{:S(2)}) collective-permute-start(bf16[768,640]{1,0:T(8,128)(2,1)S(1)} %constant_dynamic-update-slice_fusion.2.own), channel_id=1, source_target_pairs={{0,1},{1,0},{2,3},{3,2},{4,5},{5,4},{6,7},{7,6},{8,9},{9,8},{10,11... | collective-permute-start | bytes 2949128 | tf_op jit(solution)/shard_map/ppermute | solution.py:327
  41.4 2.2 %collective-permute-start.12 = (bf16[64,4096]{1,0:T(8,128)(2,1)S(1)}, bf16[64,4096]{1,0:T(8,128)(2,1)S(1)}, u32[]{:S(2)}, u32[]{:S(2)}) collective-permute-start(bf16[64,4096]{1,0:T(8,128)(2,1)S(1)} %collective-permute-done.7.refs_2_), channel_id=1, source_target_pairs={{0,4},{1,5},{2,6},{3,7},{4,8},{5,9},{6,10},{7,11},{8,12},{9,13},{1... | collective-permute-start | bytes 1572872 | tf_op jit(solution)/shard_map/ppermute | solution.py:330
  43.6 1.3 %collective-permute-start.13 = (bf16[64,4096]{1,0:T(8,128)(2,1)S(1)}, bf16[64,4096]{1,0:T(8,128)(2,1)S(1)}, u32[]{:S(2)}, u32[]{:S(2)}) collective-permute-start(bf16[64,4096]{1,0:T(8,128)(2,1)S(1)} %collective-permute-done.7.refs_2_), channel_id=1, source_target_pairs={{0,2},{1,3},{2,0},{3,1},{4,6},{5,7},{6,4},{7,5},{8,10},{9,11},{10,... | collective-permute-start | bytes 1572872 | tf_op jit(solution)/shard_map/ppermute | solution.py:333
  45.0 1.5 %collective-permute-start.14 = (bf16[128,1536]{1,0:T(8,128)(2,1)S(1)}, bf16[128,1536]{1,0:T(8,128)(2,1)S(1)}, u32[]{:S(2)}, u32[]{:S(2)}) collective-permute-start(bf16[128,1536]{1,0:T(8,128)(2,1)S(1)} %get-tuple-element.77), channel_id=1, source_target_pairs={{0,16},{1,17},{2,18},{3,19},{4,20},{5,21},{6,22},{7,23},{8,24},{9,... | collective-permute-start | bytes 1179656 | tf_op jit(solution)/shard_map/ppermute | solution.py:327
  46.5 10.6 %collective-permute-done.12.refs_3_ = bf16[64,4096]{1,0:T(8,128)(2,1)S(1)} collective-permute-done((bf16[64,4096]{1,0:T(8,128)(2,1)S(1)}, bf16[64,4096]{1,0:T(8,128)(2,1)S(1)}, u32[]{:S(2)}, u32[]{:S(2)}) %collective-permute-start.12) | collective-permute-done | bytes 524320 | tf_op jit(solution)/shard_map/ppermute | solution.py:330
  57.2 0.1 collective-permute-done.13.refs_6_
  57.3 1.6 %collective-permute-start.15 = (bf16[64,2048]{1,0:T(8,128)(2,1)S(1)}, bf16[64,2048]{1,0:T(8,128)(2,1)S(1)}, u32[]{:S(2)}, u32[]{:S(2)}) collective-permute-start(bf16[64,2048]{1,0:T(8,128)(2,1)S(1)} %slice.40), channel_id=1, source_target_pairs={{0,2},{1,3},{2,0},{3,1},{4,6},{5,7},{6,4},{7,5},{8,10},{9,11},{10,... | collective-permute-start | bytes 786440 | tf_op jit(solution)/shard_map/ppermute | solution.py:333
  58.8 0.0 collective-permute-done.17
  58.9 1.6 %collective-permute-start.16 = (bf16[64,2048]{1,0:T(8,128)(2,1)S(1)}, bf16[64,2048]{1,0:T(8,128)(2,1)S(1)}, u32[]{:S(2)}, u32[]{:S(2)}) collective-permute-start(bf16[64,2048]{1,0:T(8,128)(2,1)S(1)} %slice.41), channel_id=1, source_target_pairs={{0,4},{1,5},{2,6},{3,7},{4,8},{5,9},{6,10},{7,11},{8,12},{9,13},{1... | collective-permute-start | bytes 786440 | tf_op jit(solution)/shard_map/ppermute | solution.py:330
  60.5 1.6 %collective-permute-start.20 = (bf16[128,1536]{1,0:T(8,128)(2,1)S(1)}, bf16[128,1536]{1,0:T(8,128)(2,1)S(1)}, u32[]{:S(2)}, u32[]{:S(2)}) collective-permute-start(bf16[128,1536]{1,0:T(8,128)(2,1)S(1)} %get-tuple-element.90), channel_id=1, source_target_pairs={{0,17},{1,16},{2,19},{3,18},{4,21},{5,20},{6,23},{7,22},{8,25},{9,... | collective-permute-start | bytes 1179656 | tf_op jit(solution)/shard_map/ppermute | solution.py:327
  62.1 0.6 keys.1
  62.7 3.3 %collective-permute-done.15.refs_7_ = bf16[64,2048]{1,0:T(8,128)(2,1)S(1)} collective-permute-done((bf16[64,2048]{1,0:T(8,128)(2,1)S(1)}, bf16[64,2048]{1,0:T(8,128)(2,1)S(1)}, u32[]{:S(2)}, u32[]{:S(2)}) %collective-permute-start.15) | collective-permute-done | bytes 262176 | tf_op jit(solution)/shard_map/ppermute | solution.py:333
  66.0 1.5 %collective-permute-start.18 = (bf16[2,4,16,576]{3,2,0,1:T(8,128)(2,1)S(1)}, bf16[2,4,16,576]{3,2,0,1:T(8,128)(2,1)S(1)}, u32[]{:S(2)}, u32[]{:S(2)}) collective-permute-start(bf16[2,4,16,576]{3,2,0,1:T(8,128)(2,1)S(1)} %fusion.2), channel_id=1, source_target_pairs={{0,2},{1,3},{2,0},{3,1},{4,6},{5,7},{6,4},{7,5},{8,10},{9,11},{10,... | collective-permute-start | bytes 442376 | tf_op jit(solution)/shard_map/ppermute | solution.py:336
  67.5 8.9 %attend.3 = (bf16[128,1024]{1,0:T(8,128)(2,1)S(1)}, bf16[128,1024]{1,0:T(8,128)(2,1)S(1)}, bf16[128,1024]{1,0:T(8,128)(2,1)S(1)}, bf16[128,1024]{1,0:T(8,128)(2,1)S(1)}) custom-call(s32[1]{0:T(128)} %bitcast.1.info, bf16[2,640,512]{2,1,0:T(8,128)(2,1)S(1)} %get-tuple-element.71.latent, bf16[2,640,128]{2,1,0:T(8,128)(2,1)S(1)} %get-tuple-element.72.rope_even, ...), custom_call_target="tpu_custom_call" | custom-call | flops 4362076160 | bytes 8388608 | tf_op jit(solution)/shard_map/attend/pallas_call | solution.py:476
  76.5 1.6 %collective-permute-start.22 = (bf16[128,1024]{1,0:T(8,128)(2,1)S(1)}, bf16[128,1024]{1,0:T(8,128)(2,1)S(1)}, u32[]{:S(2)}, u32[]{:S(2)}) collective-permute-start(bf16[128,1024]{1,0:T(8,128)(2,1)S(1)} %get-tuple-element.95), channel_id=1, source_target_pairs={{0,16},{1,17},{2,18},{3,19},{4,20},{5,21},{6,22},{7,23},{8,24},{9,... | collective-permute-start | bytes 786440 | tf_op jit(solution)/shard_map/ppermute | solution.py:327
  78.0 0.0 collective-permute-done.16.refs_7_
  78.0 0.0 collective-permute-start.24
  78.0 0.6 collective-permute-start.30
  78.7 0.1 fusion
  78.8 0.0 collective-permute-done.19.refs_9_.refs_13_
  78.8 0.2 collective-permute-start.21
  79.0 4.5 %attend.4 = (bf16[128,512]{1,0:T(8,128)(2,1)S(1)}, bf16[128,512]{1,0:T(8,128)(2,1)S(1)}, bf16[128,512]{1,0:T(8,128)(2,1)S(1)}, bf16[128,512]{1,0:T(8,128)(2,1)S(1)}) custom-call(s32[1]{0:T(128)} %bitcast.1.info, bf16[2,640,512]{2,1,0:T(8,128)(2,1)S(1)} %get-tuple-element.71.latent, bf16[2,640,128]{2,1,0:T(8,128)(2,1)S(1)} %get-tuple-element.72.rope_even, ...), custom_call_target="tpu_custom_call" | custom-call | flops 2181038080 | bytes 4194304 | tf_op jit(solution)/shard_map/attend/pallas_call | solution.py:476
  83.5 1.6 %collective-permute-start.26 = (bf16[128,512]{1,0:T(8,128)(2,1)S(1)}, bf16[128,512]{1,0:T(8,128)(2,1)S(1)}, u32[]{:S(2)}, u32[]{:S(2)}) collective-permute-start(bf16[128,512]{1,0:T(8,128)(2,1)S(1)} %get-tuple-element.104), channel_id=1, source_target_pairs={{0,16},{1,17},{2,18},{3,19},{4,20},{5,21},{6,22},{7,23},{8,24},{9,... | collective-permute-start | bytes 393224 | tf_op jit(solution)/shard_map/ppermute | solution.py:327
  85.1 0.0 collective-permute-done.21
  85.1 0.3 collective-permute-start.27
  85.4 0.1 fusion.1
  85.4 0.4 collective-permute-done.22.refs_6_
  85.8 1.6 %collective-permute-start.23 = (bf16[8,1,16,576]{3,2,0,1:T(8,128)(2,1)S(1)}, bf16[8,1,16,576]{3,2,0,1:T(8,128)(2,1)S(1)}, u32[]{:S(2)}, u32[]{:S(2)}) collective-permute-start(bf16[8,1,16,576]{3,2,0,1:T(8,128)(2,1)S(1)} %get-tuple-element.99), channel_id=1, source_target_pairs={{0,8},{1,9},{2,10},{3,11},{4,12},{5,13},{6,14},{7,15},{8,0},{9,1},... | collective-permute-start | bytes 442376 | tf_op jit(solution)/shard_map/ppermute | solution.py:336
  87.4 4.5 %attend.5 = (bf16[128,512]{1,0:T(8,128)(2,1)S(1)}, bf16[128,512]{1,0:T(8,128)(2,1)S(1)}, bf16[128,512]{1,0:T(8,128)(2,1)S(1)}, bf16[128,512]{1,0:T(8,128)(2,1)S(1)}) custom-call(s32[1]{0:T(128)} %bitcast.1.info, bf16[2,640,512]{2,1,0:T(8,128)(2,1)S(1)} %get-tuple-element.71.latent, bf16[2,640,128]{2,1,0:T(8,128)(2,1)S(1)} %get-tuple-element.72.rope_even, ...), custom_call_target="tpu_custom_call" | custom-call | flops 2181038080 | bytes 4194304 | tf_op jit(solution)/shard_map/attend/pallas_call | solution.py:476
  91.9 2.1 %collective-permute-done.26.refs_7_ = bf16[128,512]{1,0:T(8,128)(2,1)S(1)} collective-permute-done((bf16[128,512]{1,0:T(8,128)(2,1)S(1)}, bf16[128,512]{1,0:T(8,128)(2,1)S(1)}, u32[]{:S(2)}, u32[]{:S(2)}) %collective-permute-start.26) | collective-permute-done | bytes 131104 | tf_op jit(solution)/shard_map/ppermute | solution.py:327
  94.0 0.4 collective-permute-done.27.refs_10_
  94.5 1.1 %collective-permute-start.28 = (bf16[128,512]{1,0:T(8,128)(2,1)S(1)}, bf16[128,512]{1,0:T(8,128)(2,1)S(1)}, u32[]{:S(2)}, u32[]{:S(2)}) collective-permute-start(bf16[128,512]{1,0:T(8,128)(2,1)S(1)} %get-tuple-element.106), channel_id=1, source_target_pairs={{0,1},{1,0},{2,3},{3,2},{4,5},{5,4},{6,7},{7,6},{8,9},{9,8},{10,11... | collective-permute-start | bytes 393224 | tf_op jit(solution)/shard_map/ppermute | solution.py:327
  95.6 1.5 %collective-permute-start.29 = (bf16[128,512]{1,0:T(8,128)(2,1)S(1)}, bf16[128,512]{1,0:T(8,128)(2,1)S(1)}, u32[]{:S(2)}, u32[]{:S(2)}) collective-permute-start(bf16[128,512]{1,0:T(8,128)(2,1)S(1)} %get-tuple-element.107), channel_id=1, source_target_pairs={{0,16},{1,17},{2,18},{3,19},{4,20},{5,21},{6,22},{7,23},{8,24},{9,... | collective-permute-start | bytes 393224 | tf_op jit(solution)/shard_map/ppermute | solution.py:327
  97.1 0.2 collective-permute-done.23
  97.3 0.6 sort.1
  98.0 0.9 copy.9
  98.8 2.8 %collective-permute-done.29.refs_8_ = bf16[128,512]{1,0:T(8,128)(2,1)S(1)} collective-permute-done((bf16[128,512]{1,0:T(8,128)(2,1)S(1)}, bf16[128,512]{1,0:T(8,128)(2,1)S(1)}, u32[]{:S(2)}, u32[]{:S(2)}) %collective-permute-start.29) | collective-permute-done | bytes 131104 | tf_op jit(solution)/shard_map/ppermute | solution.py:327
  101.7 1.4 %collective-permute-done.31.refs_11_ = bf16[128,512]{1,0:T(8,128)(2,1)S(1)} collective-permute-done((bf16[128,512]{1,0:T(8,128)(2,1)S(1)}, bf16[128,512]{1,0:T(8,128)(2,1)S(1)}, u32[]{:S(2)}, u32[]{:S(2)}) %collective-permute-start.31) | collective-permute-done | bytes 131104 | tf_op jit(solution)/shard_map/ppermute | solution.py:327
  103.1 1.4 %place.1 = bf16[128,8192]{1,0:T(8,128)(2,1)} custom-call(s32[1]{0:T(128)} %bitcast.info, bf16[128,1024]{1,0:T(8,128)(2,1)S(1)} %get-tuple-element.79.refs_0_, bf16[128,512]{1,0:T(8,128)(2,1)S(1)} %get-tuple-element.91.refs_1_, bf16[128,512]{1,0:T(8,128)(2,1)S(1)} %get-tuple-element.97.refs_2_, bf16[128,1024]{1,0:T(8,128)(2,1)S(1)} %collective-permute-done.24.refs_3_, ...), custom_call_target="tpu_custom_call" | custom-call | tf_op jit(solution)/shard_map/place/pallas_call | solution.py:540
  (27 shorter events, 0.4 us)
Async XLA Ops:
  1.6 1.7 %collective-permute-start = (bf16[32,4096]{1,0:T(8,128)(2,1)S(1)}, bf16[32,4096]{1,0:T(8,128)(2,1)S(1)}, u32[]{:S(2)}, u32[]{:S(2)}) collective-permute-start(bf16[32,4096]{1,0:T(8,128)(2,1)S(1)} %constant_dynamic-slice_fusion), channel_id=1, source_target_pairs={{0,1},{1,0},{2,3},{3,2},{4,5},{5,4},{6,7},{7,6},{8,9},{9,8},{10,11... | collective-permute-start | bytes 786440 | tf_op jit(solution)/shard_map/ppermute | solution.py:327
  4.3 22.1 %collective-permute-start.4 = (bf16[64,4096]{1,0:T(8,128)(2,1)S(1)}, bf16[64,4096]{1,0:T(8,128)(2,1)S(1)}, u32[]{:S(2)}, u32[]{:S(2)}) collective-permute-start(bf16[64,4096]{1,0:T(8,128)(2,1)S(1)} %pair.1.refs_0_), channel_id=1, source_target_pairs={{0,4},{1,5},{2,6},{3,7},{4,8},{5,9},{6,10},{7,11},{8,12},{9,13},{1... | collective-permute-start | bytes 1572872 | tf_op jit(solution)/shard_map/ppermute | solution.py:330
  7.3 19.1 %collective-permute-start.5 = (bf16[64,4096]{1,0:T(8,128)(2,1)S(1)}, bf16[64,4096]{1,0:T(8,128)(2,1)S(1)}, u32[]{:S(2)}, u32[]{:S(2)}) collective-permute-start(bf16[64,4096]{1,0:T(8,128)(2,1)S(1)} %pair.1.refs_0_), channel_id=1, source_target_pairs={{0,2},{1,3},{2,0},{3,1},{4,6},{5,7},{6,4},{7,5},{8,10},{9,11},{10,... | collective-permute-start | bytes 1572872 | tf_op jit(solution)/shard_map/ppermute | solution.py:333
  11.1 5.5 %copy-start.1 = (bf16[128,640]{1,0:T(8,128)(2,1)S(1)}, bf16[128,640]{1,0:T(8,128)(2,1)}, u32[]{:S(2)}) copy-start(bf16[128,640]{1,0:T(8,128)(2,1)} %get-tuple-element.59) | copy-start | bytes 491524
  11.1 5.9 %collective-permute-start.1 = (bf16[128,640]{1,0:T(8,128)(2,1)}, bf16[128,640]{1,0:T(8,128)(2,1)S(1)}, u32[]{:S(2)}, u32[]{:S(2)}) collective-permute-start(bf16[128,640]{1,0:T(8,128)(2,1)} %get-tuple-element.59), channel_id=1, source_target_pairs={{0,16},{1,17},{2,18},{3,19},{4,20},{5,21},{6,22},{7,23},{8,24},{9,... | collective-permute-start | bytes 491528 | tf_op jit(solution)/shard_map/ppermute | solution.py:327
  12.6 33.9 %copy-start = (bf16[256,576]{1,0:T(8,128)(2,1)S(1)}, bf16[256,576]{1,0:T(8,128)(2,1)}, u32[]{:S(2)}) copy-start(bf16[256,576]{1,0:T(8,128)(2,1)} %get-tuple-element.82) | copy-start | bytes 884740
  16.0 10.4 %collective-permute-start.6 = (bf16[128,1536]{1,0:T(8,128)(2,1)S(1)}, bf16[128,1536]{1,0:T(8,128)(2,1)S(1)}, u32[]{:S(2)}, u32[]{:S(2)}) collective-permute-start(bf16[128,1536]{1,0:T(8,128)(2,1)S(1)} %get-tuple-element.63), channel_id=1, source_target_pairs={{0,16},{1,17},{2,18},{3,19},{4,20},{5,21},{6,22},{7,23},{8,24},{9,... | collective-permute-start | bytes 1179656 | tf_op jit(solution)/shard_map/ppermute | solution.py:327
  17.0 12.7 %collective-permute-start.2 = (bf16[256,640]{1,0:T(8,128)(2,1)S(1)}, bf16[256,640]{1,0:T(8,128)(2,1)S(1)}, u32[]{:S(2)}, u32[]{:S(2)}) collective-permute-start(bf16[256,640]{1,0:T(8,128)(2,1)S(1)} %get-tuple-element.118), channel_id=1, source_target_pairs={{0,2},{1,3},{2,4},{3,5},{4,6},{5,7},{6,8},{7,9},{8,10},{9,11},{10,... | collective-permute-start | bytes 983048 | tf_op jit(solution)/shard_map/ppermute | solution.py:342
  26.4 14.0 %collective-permute-start.7 = (bf16[64,4096]{1,0:T(8,128)(2,1)S(1)}, bf16[64,4096]{1,0:T(8,128)(2,1)S(1)}, u32[]{:S(2)}, u32[]{:S(2)}) collective-permute-start(bf16[64,4096]{1,0:T(8,128)(2,1)S(1)} %collective-permute-done.4.refs_1_), channel_id=1, source_target_pairs={{0,4},{1,5},{2,6},{3,7},{4,8},{5,9},{6,10},{7,11},{8,12},{9,13},{1... | collective-permute-start | bytes 1572872 | tf_op jit(solution)/shard_map/ppermute | solution.py:330
  28.0 12.4 %collective-permute-start.8 = (bf16[64,4096]{1,0:T(8,128)(2,1)S(1)}, bf16[64,4096]{1,0:T(8,128)(2,1)S(1)}, u32[]{:S(2)}, u32[]{:S(2)}) collective-permute-start(bf16[64,4096]{1,0:T(8,128)(2,1)S(1)} %collective-permute-done.4.refs_1_), channel_id=1, source_target_pairs={{0,2},{1,3},{2,0},{3,1},{4,6},{5,7},{6,4},{7,5},{8,10},{9,11},{10,... | collective-permute-start | bytes 1572872 | tf_op jit(solution)/shard_map/ppermute | solution.py:333
  28.5 1.5 %collective-permute-start.3 = (bf16[256,640]{1,0:T(8,128)(2,1)S(1)}, bf16[256,640]{1,0:T(8,128)(2,1)S(1)}, u32[]{:S(2)}, u32[]{:S(2)}) collective-permute-start(bf16[256,640]{1,0:T(8,128)(2,1)S(1)} %get-tuple-element.118), channel_id=1, source_target_pairs={{1,5},{3,7},{5,9},{7,11},{9,13},{11,15},{17,21},{19,23},{21,25},{2... | collective-permute-start | bytes 983048 | tf_op jit(solution)/shard_map/ppermute | solution.py:342
  29.1 11.0 %collective-permute-start.9 = (bf16[128,1536]{1,0:T(8,128)(2,1)S(1)}, bf16[128,1536]{1,0:T(8,128)(2,1)S(1)}, u32[]{:S(2)}, u32[]{:S(2)}) collective-permute-start(bf16[128,1536]{1,0:T(8,128)(2,1)S(1)} %get-tuple-element.67), channel_id=1, source_target_pairs={{0,17},{1,16},{2,19},{3,18},{4,21},{5,20},{6,23},{7,22},{8,25},{9,... | collective-permute-start | bytes 1179656 | tf_op jit(solution)/shard_map/ppermute | solution.py:327
  29.7 10.4 %collective-permute-start.10 = (bf16[128,1536]{1,0:T(8,128)(2,1)S(1)}, bf16[128,1536]{1,0:T(8,128)(2,1)S(1)}, u32[]{:S(2)}, u32[]{:S(2)}) collective-permute-start(bf16[128,1536]{1,0:T(8,128)(2,1)S(1)} %get-tuple-element.69), channel_id=1, source_target_pairs={{0,1},{1,0},{2,3},{3,2},{4,5},{5,4},{6,7},{7,6},{8,9},{9,8},{10,11... | collective-permute-start | bytes 1179656 | tf_op jit(solution)/shard_map/ppermute | solution.py:327
  40.4 16.9 %collective-permute-start.11 = (bf16[768,640]{1,0:T(8,128)(2,1)S(1)}, bf16[768,640]{1,0:T(8,128)(2,1)S(1)}, u32[]{:S(2)}, u32[]{:S(2)}) collective-permute-start(bf16[768,640]{1,0:T(8,128)(2,1)S(1)} %constant_dynamic-update-slice_fusion.2.own), channel_id=1, source_target_pairs={{0,1},{1,0},{2,3},{3,2},{4,5},{5,4},{6,7},{7,6},{8,9},{9,8},{10,11... | collective-permute-start | bytes 2949128 | tf_op jit(solution)/shard_map/ppermute | solution.py:327
  41.4 15.7 %collective-permute-start.12 = (bf16[64,4096]{1,0:T(8,128)(2,1)S(1)}, bf16[64,4096]{1,0:T(8,128)(2,1)S(1)}, u32[]{:S(2)}, u32[]{:S(2)}) collective-permute-start(bf16[64,4096]{1,0:T(8,128)(2,1)S(1)} %collective-permute-done.7.refs_2_), channel_id=1, source_target_pairs={{0,4},{1,5},{2,6},{3,7},{4,8},{5,9},{6,10},{7,11},{8,12},{9,13},{1... | collective-permute-start | bytes 1572872 | tf_op jit(solution)/shard_map/ppermute | solution.py:330
  43.6 13.6 %collective-permute-start.13 = (bf16[64,4096]{1,0:T(8,128)(2,1)S(1)}, bf16[64,4096]{1,0:T(8,128)(2,1)S(1)}, u32[]{:S(2)}, u32[]{:S(2)}) collective-permute-start(bf16[64,4096]{1,0:T(8,128)(2,1)S(1)} %collective-permute-done.7.refs_2_), channel_id=1, source_target_pairs={{0,2},{1,3},{2,0},{3,1},{4,6},{5,7},{6,4},{7,5},{8,10},{9,11},{10,... | collective-permute-start | bytes 1572872 | tf_op jit(solution)/shard_map/ppermute | solution.py:333
  45.0 12.2 %collective-permute-start.14 = (bf16[128,1536]{1,0:T(8,128)(2,1)S(1)}, bf16[128,1536]{1,0:T(8,128)(2,1)S(1)}, u32[]{:S(2)}, u32[]{:S(2)}) collective-permute-start(bf16[128,1536]{1,0:T(8,128)(2,1)S(1)} %get-tuple-element.77), channel_id=1, source_target_pairs={{0,16},{1,17},{2,18},{3,19},{4,20},{5,21},{6,22},{7,23},{8,24},{9,... | collective-permute-start | bytes 1179656 | tf_op jit(solution)/shard_map/ppermute | solution.py:327
  57.1 1.7 %collective-permute-start.17 = (bf16[1,8,16,576]{3,2,0,1:T(8,128)(2,1)S(1)}, bf16[1,8,16,576]{3,2,0,1:T(8,128)(2,1)S(1)}, u32[]{:S(2)}, u32[]{:S(2)}) collective-permute-start(bf16[1,8,16,576]{3,2,0,1:T(8,128)(2,1)S(1)} %get-tuple-element.83), channel_id=1, source_target_pairs={{0,1},{1,0},{2,3},{3,2},{4,5},{5,4},{6,7},{7,6},{8,9},{9,8},{10,11... | collective-permute-start | bytes 442376 | tf_op jit(solution)/shard_map/ppermute | solution.py:336
  57.3 8.7 %collective-permute-start.15 = (bf16[64,2048]{1,0:T(8,128)(2,1)S(1)}, bf16[64,2048]{1,0:T(8,128)(2,1)S(1)}, u32[]{:S(2)}, u32[]{:S(2)}) collective-permute-start(bf16[64,2048]{1,0:T(8,128)(2,1)S(1)} %slice.40), channel_id=1, source_target_pairs={{0,2},{1,3},{2,0},{3,1},{4,6},{5,7},{6,4},{7,5},{8,10},{9,11},{10,... | collective-permute-start | bytes 786440 | tf_op jit(solution)/shard_map/ppermute | solution.py:333
  58.9 19.2 %collective-permute-start.16 = (bf16[64,2048]{1,0:T(8,128)(2,1)S(1)}, bf16[64,2048]{1,0:T(8,128)(2,1)S(1)}, u32[]{:S(2)}, u32[]{:S(2)}) collective-permute-start(bf16[64,2048]{1,0:T(8,128)(2,1)S(1)} %slice.41), channel_id=1, source_target_pairs={{0,4},{1,5},{2,6},{3,7},{4,8},{5,9},{6,10},{7,11},{8,12},{9,13},{1... | collective-permute-start | bytes 786440 | tf_op jit(solution)/shard_map/ppermute | solution.py:330
  60.5 18.3 %collective-permute-start.19 = (bf16[128,1536]{1,0:T(8,128)(2,1)S(1)}, bf16[128,1536]{1,0:T(8,128)(2,1)S(1)}, u32[]{:S(2)}, u32[]{:S(2)}) collective-permute-start(bf16[128,1536]{1,0:T(8,128)(2,1)S(1)} %get-tuple-element.88), channel_id=1, source_target_pairs={{0,1},{1,0},{2,3},{3,2},{4,5},{5,4},{6,7},{7,6},{8,9},{9,8},{10,11... | collective-permute-start | bytes 1179656 | tf_op jit(solution)/shard_map/ppermute | solution.py:327
  60.5 18.6 %collective-permute-start.20 = (bf16[128,1536]{1,0:T(8,128)(2,1)S(1)}, bf16[128,1536]{1,0:T(8,128)(2,1)S(1)}, u32[]{:S(2)}, u32[]{:S(2)}) collective-permute-start(bf16[128,1536]{1,0:T(8,128)(2,1)S(1)} %get-tuple-element.90), channel_id=1, source_target_pairs={{0,17},{1,16},{2,19},{3,18},{4,21},{5,20},{6,23},{7,22},{8,25},{9,... | collective-permute-start | bytes 1179656 | tf_op jit(solution)/shard_map/ppermute | solution.py:327
  66.0 12.1 %collective-permute-start.18 = (bf16[2,4,16,576]{3,2,0,1:T(8,128)(2,1)S(1)}, bf16[2,4,16,576]{3,2,0,1:T(8,128)(2,1)S(1)}, u32[]{:S(2)}, u32[]{:S(2)}) collective-permute-start(bf16[2,4,16,576]{3,2,0,1:T(8,128)(2,1)S(1)} %fusion.2), channel_id=1, source_target_pairs={{0,2},{1,3},{2,0},{3,1},{4,6},{5,7},{6,4},{7,5},{8,10},{9,11},{10,... | collective-permute-start | bytes 442376 | tf_op jit(solution)/shard_map/ppermute | solution.py:336
  76.5 9.3 %collective-permute-start.22 = (bf16[128,1024]{1,0:T(8,128)(2,1)S(1)}, bf16[128,1024]{1,0:T(8,128)(2,1)S(1)}, u32[]{:S(2)}, u32[]{:S(2)}) collective-permute-start(bf16[128,1024]{1,0:T(8,128)(2,1)S(1)} %get-tuple-element.95), channel_id=1, source_target_pairs={{0,16},{1,17},{2,18},{3,19},{4,20},{5,21},{6,22},{7,23},{8,24},{9,... | collective-permute-start | bytes 786440 | tf_op jit(solution)/shard_map/ppermute | solution.py:327
  78.0 17.5 %collective-permute-start.24 = (bf16[128,1024]{1,0:T(8,128)(2,1)S(1)}, bf16[128,1024]{1,0:T(8,128)(2,1)S(1)}, u32[]{:S(2)}, u32[]{:S(2)}) collective-permute-start(bf16[128,1024]{1,0:T(8,128)(2,1)S(1)} %get-tuple-element.101), channel_id=1, source_target_pairs={{0,1},{1,0},{2,3},{3,2},{4,5},{5,4},{6,7},{7,6},{8,9},{9,8},{10,11... | collective-permute-start | bytes 786440 | tf_op jit(solution)/shard_map/ppermute | solution.py:327
  78.0 20.8 %collective-permute-start.30 = (bf16[128,1024]{1,0:T(8,128)(2,1)S(1)}, bf16[128,1024]{1,0:T(8,128)(2,1)S(1)}, u32[]{:S(2)}, u32[]{:S(2)}) collective-permute-start(bf16[128,1024]{1,0:T(8,128)(2,1)S(1)} %get-tuple-element.108), channel_id=1, source_target_pairs={{0,17},{1,16},{2,19},{3,18},{4,21},{5,20},{6,23},{7,22},{8,25},{9,... | collective-permute-start | bytes 786440 | tf_op jit(solution)/shard_map/ppermute | solution.py:327
  78.8 6.3 %collective-permute-start.21 = (bf16[4,2,16,576]{3,2,0,1:T(8,128)(2,1)S(1)}, bf16[4,2,16,576]{3,2,0,1:T(8,128)(2,1)S(1)}, u32[]{:S(2)}, u32[]{:S(2)}) collective-permute-start(bf16[4,2,16,576]{3,2,0,1:T(8,128)(2,1)S(1)} %get-tuple-element.93), channel_id=1, source_target_pairs={{0,4},{1,5},{2,6},{3,7},{4,0},{5,1},{6,2},{7,3},{8,12},{9,13},{10,... | collective-permute-start | bytes 442376 | tf_op jit(solution)/shard_map/ppermute | solution.py:336
  83.5 10.5 %collective-permute-start.26 = (bf16[128,512]{1,0:T(8,128)(2,1)S(1)}, bf16[128,512]{1,0:T(8,128)(2,1)S(1)}, u32[]{:S(2)}, u32[]{:S(2)}) collective-permute-start(bf16[128,512]{1,0:T(8,128)(2,1)S(1)} %get-tuple-element.104), channel_id=1, source_target_pairs={{0,16},{1,17},{2,18},{3,19},{4,20},{5,21},{6,22},{7,23},{8,24},{9,... | collective-permute-start | bytes 393224 | tf_op jit(solution)/shard_map/ppermute | solution.py:327
  85.1 9.3 %collective-permute-start.27 = (bf16[128,512]{1,0:T(8,128)(2,1)S(1)}, bf16[128,512]{1,0:T(8,128)(2,1)S(1)}, u32[]{:S(2)}, u32[]{:S(2)}) collective-permute-start(bf16[128,512]{1,0:T(8,128)(2,1)S(1)} %get-tuple-element.105), channel_id=1, source_target_pairs={{0,17},{1,16},{2,19},{3,18},{4,21},{5,20},{6,23},{7,22},{8,25},{9,... | collective-permute-start | bytes 393224 | tf_op jit(solution)/shard_map/ppermute | solution.py:327
  85.8 11.5 %collective-permute-start.23 = (bf16[8,1,16,576]{3,2,0,1:T(8,128)(2,1)S(1)}, bf16[8,1,16,576]{3,2,0,1:T(8,128)(2,1)S(1)}, u32[]{:S(2)}, u32[]{:S(2)}) collective-permute-start(bf16[8,1,16,576]{3,2,0,1:T(8,128)(2,1)S(1)} %get-tuple-element.99), channel_id=1, source_target_pairs={{0,8},{1,9},{2,10},{3,11},{4,12},{5,13},{6,14},{7,15},{8,0},{9,1},... | collective-permute-start | bytes 442376 | tf_op jit(solution)/shard_map/ppermute | solution.py:336
  94.0 4.8 %collective-permute-start.25 = (bf16[128,512]{1,0:T(8,128)(2,1)S(1)}, bf16[128,512]{1,0:T(8,128)(2,1)S(1)}, u32[]{:S(2)}, u32[]{:S(2)}) collective-permute-start(bf16[128,512]{1,0:T(8,128)(2,1)S(1)} %get-tuple-element.102), channel_id=1, source_target_pairs={{0,1},{1,0},{2,3},{3,2},{4,5},{5,4},{6,7},{7,6},{8,9},{9,8},{10,11... | collective-permute-start | bytes 393224 | tf_op jit(solution)/shard_map/ppermute | solution.py:327
  94.5 4.4 %collective-permute-start.28 = (bf16[128,512]{1,0:T(8,128)(2,1)S(1)}, bf16[128,512]{1,0:T(8,128)(2,1)S(1)}, u32[]{:S(2)}, u32[]{:S(2)}) collective-permute-start(bf16[128,512]{1,0:T(8,128)(2,1)S(1)} %get-tuple-element.106), channel_id=1, source_target_pairs={{0,1},{1,0},{2,3},{3,2},{4,5},{5,4},{6,7},{7,6},{8,9},{9,8},{10,11... | collective-permute-start | bytes 393224 | tf_op jit(solution)/shard_map/ppermute | solution.py:327
  95.6 6.1 %collective-permute-start.29 = (bf16[128,512]{1,0:T(8,128)(2,1)S(1)}, bf16[128,512]{1,0:T(8,128)(2,1)S(1)}, u32[]{:S(2)}, u32[]{:S(2)}) collective-permute-start(bf16[128,512]{1,0:T(8,128)(2,1)S(1)} %get-tuple-element.107), channel_id=1, source_target_pairs={{0,16},{1,17},{2,18},{3,19},{4,20},{5,21},{6,22},{7,23},{8,24},{9,... | collective-permute-start | bytes 393224 | tf_op jit(solution)/shard_map/ppermute | solution.py:327
  97.3 5.8 %collective-permute-start.31 = (bf16[128,512]{1,0:T(8,128)(2,1)S(1)}, bf16[128,512]{1,0:T(8,128)(2,1)S(1)}, u32[]{:S(2)}, u32[]{:S(2)}) collective-permute-start(bf16[128,512]{1,0:T(8,128)(2,1)S(1)} %get-tuple-element.109), channel_id=1, source_target_pairs={{0,17},{1,16},{2,19},{3,18},{4,21},{5,20},{6,23},{7,22},{8,25},{9,... | collective-permute-start | bytes 393224 | tf_op jit(solution)/shard_map/ppermute | solution.py:327

commit v17 on v16

--- a/solution.py
+++ b/solution.py
@@ -512,16 +512,16 @@
         last = len(results) + 1 == len(CALLS)
         if results:
             mine_info = tie(mine_info, *halves[1:], *exchanged[len(results) : len(results) + 1])
-        mine_info = tie(mine_info, *(results[0][2:3] if last else []))
+        mine_info = tie(mine_info, *(results[0][2:] if last else []))
         pieces = attend(*call)
         mine_info = tie(mine_info, pieces[0])
-        before = results[-1][2:] if last else []
         if outer and not last:
             held = exchange(pieces[0])
-        results.append(
-            [pieces[0], quad_swap(tie(pieces[1], *before), 1)]
-            + [quad_swap(pieces[r], r) for r in (2, 3)]
-        )
+        sent = list(pieces)
+        for r in (2, 3, 1):
+            before = ([sent[2]] if r == 1 else [results[-1][r]]) if last else []
+            sent[r] = quad_swap(tie(pieces[r], *before), r)
+        results.append(sent)
     pieces = [one[r] for r in range(QUAD) for one in results]
     if outer:
         decode_cache = pl.pallas_call(

time: 105 us -> 107 us (1.019)
  waiting for transfers between devices: 40.2 us -> 43.1 us
    ppermute x18, waiting for transfers between devices: 25.8 us -> 28.7 us  [quad_swap(): return lax.ppermute(array, ('groups', 'ctx'), pairs)]
  transfers between devices with their start and end apart: 32 -> 32, of which waited for: 14 -> 13; matrix products, arithmetic and copies ran while one was open for 1% -> 1% of each run, Pallas kernels for 24% -> 23%
where the time goes in v17:
time: 107 us
  waiting for transfers between devices  43.1 us (40%)
  starting transfers between devices  32.9 us (31%)
  Pallas kernels  27.2 us (25%)
  local copies, waits for them, and re-layouts  2.1 us (2%)
    ppermute x18, waiting for transfers between devices, quad_swap(): return lax.ppermute(array, ('groups', 'ctx'), pairs)  28.7 us
    pallas_call x3, Pallas kernels, attend(): pl.pallas_call(functools.partial(attend_kernel, outer), grid=(steps,), ou...  17.9 us
    ppermute x18, starting transfers between devices, quad_swap(): return lax.ppermute(array, ('groups', 'ctx'), pairs)  13.8 us
    ppermute x4, waiting for transfers between devices, around(): lax.ppermute(array, 'ctx', [(i, (i + by) % size) for i in range(size)])  10.9 us
    ppermute x4, starting transfers between devices, around(): lax.ppermute(array, 'ctx', [(i, (i + by) % size) for i in range(size)])  8.36 us
    ppermute x4, starting transfers between devices, inner_swap(): return lax.ppermute(array, 'ctx', [(i, i ^ 2) for i in range(size)])  4.91 us
    ppermute x4, waiting for transfers between devices, inner_swap(): return lax.ppermute(array, 'ctx', [(i, i ^ 2) for i in range(size)])  3.39 us
    pallas_call x1, Pallas kernels, body(): pl.pallas_call(query_kernel, out_shape=[shape((tok, h * (NOPE + ROPE))) f...  3.38 us
  transfers between devices with their start and end apart: 32, of which 13 were waited for; matrix products, arithmetic and copies ran while one was open for 1% of the time, Pallas kernels for 23%

profile of v17, /device:TPU:0, one launch (start us, length us, event | category | flops | bytes accessed | tf_op | source)
XLA Modules:
  0.0 106.5 jit_solution(2195306096675249512)
XLA Ops:
  0.6 1.0 constant_dynamic-slice_fusion
  1.6 0.5 collective-permute-start
  2.1 1.2 %collective-permute-done.got = bf16[32,4096]{1,0:T(8,128)(2,1)S(1)} collective-permute-done((bf16[32,4096]{1,0:T(8,128)(2,1)S(1)}, bf16[32,4096]{1,0:T(8,128)(2,1)S(1)}, u32[]{:S(2)}, u32[]{:S(2)}) %collective-permute-start) | collective-permute-done | bytes 262176 | tf_op jit(solution)/shard_map/ppermute | solution.py:327
  3.3 1.0 pair.1.refs_0_
  4.3 3.0 %collective-permute-start.4 = (bf16[64,4096]{1,0:T(8,128)(2,1)S(1)}, bf16[64,4096]{1,0:T(8,128)(2,1)S(1)}, u32[]{:S(2)}, u32[]{:S(2)}) collective-permute-start(bf16[64,4096]{1,0:T(8,128)(2,1)S(1)} %pair.1.refs_0_), channel_id=1, source_target_pairs={{0,4},{1,5},{2,6},{3,7},{4,8},{5,9},{6,10},{7,11},{8,12},{9,13},{1... | collective-permute-start | bytes 1572872 | tf_op jit(solution)/shard_map/ppermute | solution.py:330
  7.3 1.5 %collective-permute-start.5 = (bf16[64,4096]{1,0:T(8,128)(2,1)S(1)}, bf16[64,4096]{1,0:T(8,128)(2,1)S(1)}, u32[]{:S(2)}, u32[]{:S(2)}) collective-permute-start(bf16[64,4096]{1,0:T(8,128)(2,1)S(1)} %pair.1.refs_0_), channel_id=1, source_target_pairs={{0,2},{1,3},{2,0},{3,1},{4,6},{5,7},{6,4},{7,5},{8,10},{9,11},{10,... | collective-permute-start | bytes 1572872 | tf_op jit(solution)/shard_map/ppermute | solution.py:333
  8.8 2.3 %rows.1 = (bf16[128,640]{1,0:T(8,128)(2,1)}, f32[128,128]{1,0:T(8,128)}, f32[128,128]{1,0:T(8,128)}, bf16[256,576]{1,0:T(8,128)(2,1)}) custom-call(s32[1]{0:T(128)} %bitcast.1.info, s32[8]{0:T(128)} %lengths, bf16[576,128]{1,0:T(8,128)(2,1)} %bitcast.9, f32[1,512]{1,0:T(1,128)} %bitcast.10, s32[1,128]{1,0:T(1,128)} %bitcast.11, f32[1,128]{1,0:T(1,128)} %constant.30.clone.freq), custom_call_target="tpu_custom_call" | custom-call | tf_op jit(solution)/shard_map/rows/pallas_call | solution.py:377
  11.1 1.5 %collective-permute-start.1 = (bf16[128,640]{1,0:T(8,128)(2,1)}, bf16[128,640]{1,0:T(8,128)(2,1)S(1)}, u32[]{:S(2)}, u32[]{:S(2)}) collective-permute-start(bf16[128,640]{1,0:T(8,128)(2,1)} %get-tuple-element.61), channel_id=1, source_target_pairs={{0,16},{1,17},{2,18},{3,19},{4,20},{5,21},{6,22},{7,23},{8,24},{9,... | collective-permute-start | bytes 491528 | tf_op jit(solution)/shard_map/ppermute | solution.py:327
  12.6 3.4 %queries.1 = (bf16[128,1536]{1,0:T(8,128)(2,1)S(1)}, bf16[128,1536]{1,0:T(8,128)(2,1)S(1)}, bf16[128,1536]{1,0:T(8,128)(2,1)S(1)}, bf16[128,1536]{1,0:T(8,128)(2...) custom-call(s32[1]{0:T(128)} %bitcast.info, ...), custom_call_target="tpu_custom_call" | custom-call | bytes 6291456 | tf_op jit(solution)/shard_map/queries/pallas_call | solution.py:401
  16.0 0.6 collective-permute-start.6
  16.6 0.4 collective-permute-done.1
  17.0 2.4 %collective-permute-start.2 = (bf16[256,640]{1,0:T(8,128)(2,1)S(1)}, bf16[256,640]{1,0:T(8,128)(2,1)S(1)}, u32[]{:S(2)}, u32[]{:S(2)}) collective-permute-start(bf16[256,640]{1,0:T(8,128)(2,1)S(1)} %get-tuple-element.122), channel_id=1, source_target_pairs={{0,2},{1,3},{2,4},{3,5},{4,6},{5,7},{6,8},{7,9},{8,10},{9,11},{10,... | collective-permute-start | bytes 983048 | tf_op jit(solution)/shard_map/ppermute | solution.py:342
  19.5 6.9 %collective-permute-done.6.refs_10_.refs_14_ = bf16[128,1536]{1,0:T(8,128)(2,1)S(1)} collective-permute-done((bf16[128,1536]{1,0:T(8,128)(2,1)S(1)}, bf16[128,1536]{1,0:T(8,128)(2,1)S(1)}, u32[]{:S(2)}, u32[]{:S(2)}) %collective-permute-start.6) | collective-permute-done | bytes 393248 | tf_op jit(solution)/shard_map/ppermute | solution.py:327
  26.4 0.0 collective-permute-done.4.refs_1_
  26.4 0.0 collective-permute-done.5.refs_4_
  26.4 1.6 %collective-permute-start.7 = (bf16[64,4096]{1,0:T(8,128)(2,1)S(1)}, bf16[64,4096]{1,0:T(8,128)(2,1)S(1)}, u32[]{:S(2)}, u32[]{:S(2)}) collective-permute-start(bf16[64,4096]{1,0:T(8,128)(2,1)S(1)} %collective-permute-done.4.refs_1_), channel_id=1, source_target_pairs={{0,4},{1,5},{2,6},{3,7},{4,8},{5,9},{6,10},{7,11},{8,12},{9,13},{1... | collective-permute-start | bytes 1572872 | tf_op jit(solution)/shard_map/ppermute | solution.py:330
  28.0 0.5 collective-permute-start.8
  28.5 0.7 collective-permute-start.3
  29.1 0.6 collective-permute-start.9
  29.7 0.0 collective-permute-done.2
  29.7 0.2 collective-permute-start.10
  30.0 10.2 %collective-permute-done.9.refs_11_.refs_15_ = bf16[128,1536]{1,0:T(8,128)(2,1)S(1)} collective-permute-done((bf16[128,1536]{1,0:T(8,128)(2,1)S(1)}, bf16[128,1536]{1,0:T(8,128)(2,1)S(1)}, u32[]{:S(2)}, u32[]{:S(2)}) %collective-permute-start.9) | collective-permute-done | bytes 393248 | tf_op jit(solution)/shard_map/ppermute | solution.py:327
  40.2 0.2 collective-permute-done.7.refs_2_
  40.4 0.0 collective-permute-done.8.refs_5_
  40.4 1.1 %collective-permute-start.11 = (bf16[768,640]{1,0:T(8,128)(2,1)S(1)}, bf16[768,640]{1,0:T(8,128)(2,1)S(1)}, u32[]{:S(2)}, u32[]{:S(2)}) collective-permute-start(bf16[768,640]{1,0:T(8,128)(2,1)S(1)} %constant_dynamic-update-slice_fusion.2.own), channel_id=1, source_target_pairs={{0,1},{1,0},{2,3},{3,2},{4,5},{5,4},{6,7},{7,6},{8,9},{9,8},{10,11... | collective-permute-start | bytes 2949128 | tf_op jit(solution)/shard_map/ppermute | solution.py:327
  41.4 2.2 %collective-permute-start.12 = (bf16[64,4096]{1,0:T(8,128)(2,1)S(1)}, bf16[64,4096]{1,0:T(8,128)(2,1)S(1)}, u32[]{:S(2)}, u32[]{:S(2)}) collective-permute-start(bf16[64,4096]{1,0:T(8,128)(2,1)S(1)} %collective-permute-done.7.refs_2_), channel_id=1, source_target_pairs={{0,4},{1,5},{2,6},{3,7},{4,8},{5,9},{6,10},{7,11},{8,12},{9,13},{1... | collective-permute-start | bytes 1572872 | tf_op jit(solution)/shard_map/ppermute | solution.py:330
  43.6 1.3 %collective-permute-start.13 = (bf16[64,4096]{1,0:T(8,128)(2,1)S(1)}, bf16[64,4096]{1,0:T(8,128)(2,1)S(1)}, u32[]{:S(2)}, u32[]{:S(2)}) collective-permute-start(bf16[64,4096]{1,0:T(8,128)(2,1)S(1)} %collective-permute-done.7.refs_2_), channel_id=1, source_target_pairs={{0,2},{1,3},{2,0},{3,1},{4,6},{5,7},{6,4},{7,5},{8,10},{9,11},{10,... | collective-permute-start | bytes 1572872 | tf_op jit(solution)/shard_map/ppermute | solution.py:333
  45.0 1.5 %collective-permute-start.14 = (bf16[128,1536]{1,0:T(8,128)(2,1)S(1)}, bf16[128,1536]{1,0:T(8,128)(2,1)S(1)}, u32[]{:S(2)}, u32[]{:S(2)}) collective-permute-start(bf16[128,1536]{1,0:T(8,128)(2,1)S(1)} %get-tuple-element.79), channel_id=1, source_target_pairs={{0,16},{1,17},{2,18},{3,19},{4,20},{5,21},{6,22},{7,23},{8,24},{9,... | collective-permute-start | bytes 1179656 | tf_op jit(solution)/shard_map/ppermute | solution.py:327
  46.5 10.6 %collective-permute-done.12.refs_3_ = bf16[64,4096]{1,0:T(8,128)(2,1)S(1)} collective-permute-done((bf16[64,4096]{1,0:T(8,128)(2,1)S(1)}, bf16[64,4096]{1,0:T(8,128)(2,1)S(1)}, u32[]{:S(2)}, u32[]{:S(2)}) %collective-permute-start.12) | collective-permute-done | bytes 524320 | tf_op jit(solution)/shard_map/ppermute | solution.py:330
  57.1 0.0 collective-permute-start.17
  57.2 0.1 collective-permute-done.13.refs_6_
  57.2 0.0 collective-permute-done.11.other
  57.3 1.6 %collective-permute-start.15 = (bf16[64,2048]{1,0:T(8,128)(2,1)S(1)}, bf16[64,2048]{1,0:T(8,128)(2,1)S(1)}, u32[]{:S(2)}, u32[]{:S(2)}) collective-permute-start(bf16[64,2048]{1,0:T(8,128)(2,1)S(1)} %slice.40), channel_id=1, source_target_pairs={{0,2},{1,3},{2,0},{3,1},{4,6},{5,7},{6,4},{7,5},{8,10},{9,11},{10,... | collective-permute-start | bytes 786440 | tf_op jit(solution)/shard_map/ppermute | solution.py:333
  58.8 0.0 collective-permute-done.17
  58.9 1.6 %collective-permute-start.16 = (bf16[64,2048]{1,0:T(8,128)(2,1)S(1)}, bf16[64,2048]{1,0:T(8,128)(2,1)S(1)}, u32[]{:S(2)}, u32[]{:S(2)}) collective-permute-start(bf16[64,2048]{1,0:T(8,128)(2,1)S(1)} %slice.41), channel_id=1, source_target_pairs={{0,4},{1,5},{2,6},{3,7},{4,8},{5,9},{6,10},{7,11},{8,12},{9,13},{1... | collective-permute-start | bytes 786440 | tf_op jit(solution)/shard_map/ppermute | solution.py:330
  60.5 0.0 collective-permute-start.19
  60.5 1.6 %collective-permute-start.20 = (bf16[128,1536]{1,0:T(8,128)(2,1)S(1)}, bf16[128,1536]{1,0:T(8,128)(2,1)S(1)}, u32[]{:S(2)}, u32[]{:S(2)}) collective-permute-start(bf16[128,1536]{1,0:T(8,128)(2,1)S(1)} %get-tuple-element.92), channel_id=1, source_target_pairs={{0,17},{1,16},{2,19},{3,18},{4,21},{5,20},{6,23},{7,22},{8,25},{9,... | collective-permute-start | bytes 1179656 | tf_op jit(solution)/shard_map/ppermute | solution.py:327
  62.1 0.6 keys.1
  62.7 3.3 %collective-permute-done.15.refs_7_ = bf16[64,2048]{1,0:T(8,128)(2,1)S(1)} collective-permute-done((bf16[64,2048]{1,0:T(8,128)(2,1)S(1)}, bf16[64,2048]{1,0:T(8,128)(2,1)S(1)}, u32[]{:S(2)}, u32[]{:S(2)}) %collective-permute-start.15) | collective-permute-done | bytes 262176 | tf_op jit(solution)/shard_map/ppermute | solution.py:333
  66.0 1.5 %collective-permute-start.18 = (bf16[2,4,16,576]{3,2,0,1:T(8,128)(2,1)S(1)}, bf16[2,4,16,576]{3,2,0,1:T(8,128)(2,1)S(1)}, u32[]{:S(2)}, u32[]{:S(2)}) collective-permute-start(bf16[2,4,16,576]{3,2,0,1:T(8,128)(2,1)S(1)} %fusion.2), channel_id=1, source_target_pairs={{0,2},{1,3},{2,0},{3,1},{4,6},{5,7},{6,4},{7,5},{8,10},{9,11},{10,... | collective-permute-start | bytes 442376 | tf_op jit(solution)/shard_map/ppermute | solution.py:336
  67.5 8.9 %attend.3 = (bf16[128,1024]{1,0:T(8,128)(2,1)S(1)}, bf16[128,1024]{1,0:T(8,128)(2,1)S(1)}, bf16[128,1024]{1,0:T(8,128)(2,1)S(1)}, bf16[128,1024]{1,0:T(8,128)(2,1)S(1)}) custom-call(s32[1]{0:T(128)} %bitcast.1.info, bf16[2,640,512]{2,1,0:T(8,128)(2,1)S(1)} %get-tuple-element.73.latent, bf16[2,640,128]{2,1,0:T(8,128)(2,1)S(1)} %get-tuple-element.74.rope_even, ...), custom_call_target="tpu_custom_call" | custom-call | flops 4362076160 | bytes 8388608 | tf_op jit(solution)/shard_map/attend/pallas_call | solution.py:476
  76.5 1.6 %collective-permute-start.22 = (bf16[128,1024]{1,0:T(8,128)(2,1)S(1)}, bf16[128,1024]{1,0:T(8,128)(2,1)S(1)}, u32[]{:S(2)}, u32[]{:S(2)}) collective-permute-start(bf16[128,1024]{1,0:T(8,128)(2,1)S(1)} %get-tuple-element.97), channel_id=1, source_target_pairs={{0,16},{1,17},{2,18},{3,19},{4,20},{5,21},{6,22},{7,23},{8,24},{9,... | collective-permute-start | bytes 786440 | tf_op jit(solution)/shard_map/ppermute | solution.py:327
  78.0 0.0 collective-permute-start.23
  78.0 0.1 fusion
  78.1 0.0 collective-permute-done.16.refs_7_
  78.1 0.3 collective-permute-start.21
  78.4 0.0 collective-permute-done.20.refs_11_.refs_15_
  78.4 4.5 %attend.4 = (bf16[128,512]{1,0:T(8,128)(2,1)S(1)}, bf16[128,512]{1,0:T(8,128)(2,1)S(1)}, bf16[128,512]{1,0:T(8,128)(2,1)S(1)}, bf16[128,512]{1,0:T(8,128)(2,1)S(1)}) custom-call(s32[1]{0:T(128)} %bitcast.1.info, bf16[2,640,512]{2,1,0:T(8,128)(2,1)S(1)} %get-tuple-element.73.latent, bf16[2,640,128]{2,1,0:T(8,128)(2,1)S(1)} %get-tuple-element.74.rope_even, ...), custom_call_target="tpu_custom_call" | custom-call | flops 2181038080 | bytes 4194304 | tf_op jit(solution)/shard_map/attend/pallas_call | solution.py:476
  82.9 0.8 collective-permute-start.27
  83.7 1.2 %collective-permute-start.30 = (bf16[128,512]{1,0:T(8,128)(2,1)S(1)}, bf16[128,512]{1,0:T(8,128)(2,1)S(1)}, u32[]{:S(2)}, u32[]{:S(2)}) collective-permute-start(bf16[128,512]{1,0:T(8,128)(2,1)S(1)} %get-tuple-element.111), channel_id=1, source_target_pairs={{0,17},{1,16},{2,19},{3,18},{4,21},{5,20},{6,23},{7,22},{8,25},{9,... | collective-permute-start | bytes 393224 | tf_op jit(solution)/shard_map/ppermute | solution.py:327
  84.8 0.1 collective-permute-done.21
  85.0 0.8 collective-permute-done.22.refs_6_
  85.8 4.6 %collective-permute-done.23.refs_9_ = bf16[128,1024]{1,0:T(8,128)(2,1)S(1)} collective-permute-done((bf16[128,1024]{1,0:T(8,128)(2,1)S(1)}, bf16[128,1024]{1,0:T(8,128)(2,1)S(1)}, u32[]{:S(2)}, u32[]{:S(2)}) %collective-permute-start.23) | collective-permute-done | bytes 262176 | tf_op jit(solution)/shard_map/ppermute | solution.py:327
  90.4 0.1 fusion.1
  90.5 0.9 collective-permute-start.24
  91.4 4.5 %attend.5 = (bf16[128,512]{1,0:T(8,128)(2,1)S(1)}, bf16[128,512]{1,0:T(8,128)(2,1)S(1)}, bf16[128,512]{1,0:T(8,128)(2,1)S(1)}, bf16[128,512]{1,0:T(8,128)(2,1)S(1)}) custom-call(s32[1]{0:T(128)} %bitcast.1.info, bf16[2,640,512]{2,1,0:T(8,128)(2,1)S(1)} %get-tuple-element.73.latent, bf16[2,640,128]{2,1,0:T(8,128)(2,1)S(1)} %get-tuple-element.74.rope_even, ...), custom_call_target="tpu_custom_call" | custom-call | flops 2181038080 | bytes 4194304 | tf_op jit(solution)/shard_map/attend/pallas_call | solution.py:476
  95.9 0.6 collective-permute-start.28
  96.6 1.5 %collective-permute-start.25 = (bf16[128,1024]{1,0:T(8,128)(2,1)S(1)}, bf16[128,1024]{1,0:T(8,128)(2,1)S(1)}, u32[]{:S(2)}, u32[]{:S(2)}) collective-permute-start(bf16[128,1024]{1,0:T(8,128)(2,1)S(1)} %get-tuple-element.104), channel_id=1, source_target_pairs={{0,1},{1,0},{2,3},{3,2},{4,5},{5,4},{6,7},{7,6},{8,9},{9,8},{10,11... | collective-permute-start | bytes 786440 | tf_op jit(solution)/shard_map/ppermute | solution.py:327
  98.0 0.7 collective-permute-start.31
  98.7 3.7 %collective-permute-done.28.refs_8_ = bf16[128,512]{1,0:T(8,128)(2,1)S(1)} collective-permute-done((bf16[128,512]{1,0:T(8,128)(2,1)S(1)}, bf16[128,512]{1,0:T(8,128)(2,1)S(1)}, u32[]{:S(2)}, u32[]{:S(2)}) %collective-permute-start.28) | collective-permute-done | bytes 131104 | tf_op jit(solution)/shard_map/ppermute | solution.py:327
  102.4 0.6 sort.1
  103.1 0.9 copy.9
  104.0 1.0 collective-permute-done.31.refs_11_
  104.9 1.4 %place.1 = bf16[128,8192]{1,0:T(8,128)(2,1)} custom-call(s32[1]{0:T(128)} %bitcast.info, bf16[128,1024]{1,0:T(8,128)(2,1)S(1)} %get-tuple-element.81.refs_0_, bf16[128,512]{1,0:T(8,128)(2,1)S(1)} %get-tuple-element.93.refs_1_, bf16[128,512]{1,0:T(8,128)(2,1)S(1)} %get-tuple-element.100.refs_2_, bf16[128,1024]{1,0:T(8,128)(2,1)S(1)} %collective-permute-done.25.refs_3_, ...), custom_call_target="tpu_custom_call" | custom-call | tf_op jit(solution)/shard_map/place/pallas_call | solution.py:540
  (27 shorter events, 0.4 us)
Async XLA Ops:
  1.6 1.7 %collective-permute-start = (bf16[32,4096]{1,0:T(8,128)(2,1)S(1)}, bf16[32,4096]{1,0:T(8,128)(2,1)S(1)}, u32[]{:S(2)}, u32[]{:S(2)}) collective-permute-start(bf16[32,4096]{1,0:T(8,128)(2,1)S(1)} %constant_dynamic-slice_fusion), channel_id=1, source_target_pairs={{0,1},{1,0},{2,3},{3,2},{4,5},{5,4},{6,7},{7,6},{8,9},{9,8},{10,11... | collective-permute-start | bytes 786440 | tf_op jit(solution)/shard_map/ppermute | solution.py:327
  4.3 22.1 %collective-permute-start.4 = (bf16[64,4096]{1,0:T(8,128)(2,1)S(1)}, bf16[64,4096]{1,0:T(8,128)(2,1)S(1)}, u32[]{:S(2)}, u32[]{:S(2)}) collective-permute-start(bf16[64,4096]{1,0:T(8,128)(2,1)S(1)} %pair.1.refs_0_), channel_id=1, source_target_pairs={{0,4},{1,5},{2,6},{3,7},{4,8},{5,9},{6,10},{7,11},{8,12},{9,13},{1... | collective-permute-start | bytes 1572872 | tf_op jit(solution)/shard_map/ppermute | solution.py:330
  7.3 19.1 %collective-permute-start.5 = (bf16[64,4096]{1,0:T(8,128)(2,1)S(1)}, bf16[64,4096]{1,0:T(8,128)(2,1)S(1)}, u32[]{:S(2)}, u32[]{:S(2)}) collective-permute-start(bf16[64,4096]{1,0:T(8,128)(2,1)S(1)} %pair.1.refs_0_), channel_id=1, source_target_pairs={{0,2},{1,3},{2,0},{3,1},{4,6},{5,7},{6,4},{7,5},{8,10},{9,11},{10,... | collective-permute-start | bytes 1572872 | tf_op jit(solution)/shard_map/ppermute | solution.py:333
  11.1 5.5 %copy-start.1 = (bf16[128,640]{1,0:T(8,128)(2,1)S(1)}, bf16[128,640]{1,0:T(8,128)(2,1)}, u32[]{:S(2)}) copy-start(bf16[128,640]{1,0:T(8,128)(2,1)} %get-tuple-element.61) | copy-start | bytes 491524
  11.1 5.9 %collective-permute-start.1 = (bf16[128,640]{1,0:T(8,128)(2,1)}, bf16[128,640]{1,0:T(8,128)(2,1)S(1)}, u32[]{:S(2)}, u32[]{:S(2)}) collective-permute-start(bf16[128,640]{1,0:T(8,128)(2,1)} %get-tuple-element.61), channel_id=1, source_target_pairs={{0,16},{1,17},{2,18},{3,19},{4,20},{5,21},{6,22},{7,23},{8,24},{9,... | collective-permute-start | bytes 491528 | tf_op jit(solution)/shard_map/ppermute | solution.py:327
  12.6 33.9 %copy-start = (bf16[256,576]{1,0:T(8,128)(2,1)S(1)}, bf16[256,576]{1,0:T(8,128)(2,1)}, u32[]{:S(2)}) copy-start(bf16[256,576]{1,0:T(8,128)(2,1)} %get-tuple-element.84) | copy-start | bytes 884740
  16.0 10.4 %collective-permute-start.6 = (bf16[128,1536]{1,0:T(8,128)(2,1)S(1)}, bf16[128,1536]{1,0:T(8,128)(2,1)S(1)}, u32[]{:S(2)}, u32[]{:S(2)}) collective-permute-start(bf16[128,1536]{1,0:T(8,128)(2,1)S(1)} %get-tuple-element.65), channel_id=1, source_target_pairs={{0,16},{1,17},{2,18},{3,19},{4,20},{5,21},{6,22},{7,23},{8,24},{9,... | collective-permute-start | bytes 1179656 | tf_op jit(solution)/shard_map/ppermute | solution.py:327
  17.0 12.7 %collective-permute-start.2 = (bf16[256,640]{1,0:T(8,128)(2,1)S(1)}, bf16[256,640]{1,0:T(8,128)(2,1)S(1)}, u32[]{:S(2)}, u32[]{:S(2)}) collective-permute-start(bf16[256,640]{1,0:T(8,128)(2,1)S(1)} %get-tuple-element.122), channel_id=1, source_target_pairs={{0,2},{1,3},{2,4},{3,5},{4,6},{5,7},{6,8},{7,9},{8,10},{9,11},{10,... | collective-permute-start | bytes 983048 | tf_op jit(solution)/shard_map/ppermute | solution.py:342
  26.4 14.0 %collective-permute-start.7 = (bf16[64,4096]{1,0:T(8,128)(2,1)S(1)}, bf16[64,4096]{1,0:T(8,128)(2,1)S(1)}, u32[]{:S(2)}, u32[]{:S(2)}) collective-permute-start(bf16[64,4096]{1,0:T(8,128)(2,1)S(1)} %collective-permute-done.4.refs_1_), channel_id=1, source_target_pairs={{0,4},{1,5},{2,6},{3,7},{4,8},{5,9},{6,10},{7,11},{8,12},{9,13},{1... | collective-permute-start | bytes 1572872 | tf_op jit(solution)/shard_map/ppermute | solution.py:330
  28.0 12.4 %collective-permute-start.8 = (bf16[64,4096]{1,0:T(8,128)(2,1)S(1)}, bf16[64,4096]{1,0:T(8,128)(2,1)S(1)}, u32[]{:S(2)}, u32[]{:S(2)}) collective-permute-start(bf16[64,4096]{1,0:T(8,128)(2,1)S(1)} %collective-permute-done.4.refs_1_), channel_id=1, source_target_pairs={{0,2},{1,3},{2,0},{3,1},{4,6},{5,7},{6,4},{7,5},{8,10},{9,11},{10,... | collective-permute-start | bytes 1572872 | tf_op jit(solution)/shard_map/ppermute | solution.py:333
  28.5 1.5 %collective-permute-start.3 = (bf16[256,640]{1,0:T(8,128)(2,1)S(1)}, bf16[256,640]{1,0:T(8,128)(2,1)S(1)}, u32[]{:S(2)}, u32[]{:S(2)}) collective-permute-start(bf16[256,640]{1,0:T(8,128)(2,1)S(1)} %get-tuple-element.122), channel_id=1, source_target_pairs={{1,5},{3,7},{5,9},{7,11},{9,13},{11,15},{17,21},{19,23},{21,25},{2... | collective-permute-start | bytes 983048 | tf_op jit(solution)/shard_map/ppermute | solution.py:342
  29.1 11.0 %collective-permute-start.9 = (bf16[128,1536]{1,0:T(8,128)(2,1)S(1)}, bf16[128,1536]{1,0:T(8,128)(2,1)S(1)}, u32[]{:S(2)}, u32[]{:S(2)}) collective-permute-start(bf16[128,1536]{1,0:T(8,128)(2,1)S(1)} %get-tuple-element.69), channel_id=1, source_target_pairs={{0,17},{1,16},{2,19},{3,18},{4,21},{5,20},{6,23},{7,22},{8,25},{9,... | collective-permute-start | bytes 1179656 | tf_op jit(solution)/shard_map/ppermute | solution.py:327
  29.7 10.4 %collective-permute-start.10 = (bf16[128,1536]{1,0:T(8,128)(2,1)S(1)}, bf16[128,1536]{1,0:T(8,128)(2,1)S(1)}, u32[]{:S(2)}, u32[]{:S(2)}) collective-permute-start(bf16[128,1536]{1,0:T(8,128)(2,1)S(1)} %get-tuple-element.71), channel_id=1, source_target_pairs={{0,1},{1,0},{2,3},{3,2},{4,5},{5,4},{6,7},{7,6},{8,9},{9,8},{10,11... | collective-permute-start | bytes 1179656 | tf_op jit(solution)/shard_map/ppermute | solution.py:327
  40.4 16.9 %collective-permute-start.11 = (bf16[768,640]{1,0:T(8,128)(2,1)S(1)}, bf16[768,640]{1,0:T(8,128)(2,1)S(1)}, u32[]{:S(2)}, u32[]{:S(2)}) collective-permute-start(bf16[768,640]{1,0:T(8,128)(2,1)S(1)} %constant_dynamic-update-slice_fusion.2.own), channel_id=1, source_target_pairs={{0,1},{1,0},{2,3},{3,2},{4,5},{5,4},{6,7},{7,6},{8,9},{9,8},{10,11... | collective-permute-start | bytes 2949128 | tf_op jit(solution)/shard_map/ppermute | solution.py:327
  41.4 15.7 %collective-permute-start.12 = (bf16[64,4096]{1,0:T(8,128)(2,1)S(1)}, bf16[64,4096]{1,0:T(8,128)(2,1)S(1)}, u32[]{:S(2)}, u32[]{:S(2)}) collective-permute-start(bf16[64,4096]{1,0:T(8,128)(2,1)S(1)} %collective-permute-done.7.refs_2_), channel_id=1, source_target_pairs={{0,4},{1,5},{2,6},{3,7},{4,8},{5,9},{6,10},{7,11},{8,12},{9,13},{1... | collective-permute-start | bytes 1572872 | tf_op jit(solution)/shard_map/ppermute | solution.py:330
  43.6 13.6 %collective-permute-start.13 = (bf16[64,4096]{1,0:T(8,128)(2,1)S(1)}, bf16[64,4096]{1,0:T(8,128)(2,1)S(1)}, u32[]{:S(2)}, u32[]{:S(2)}) collective-permute-start(bf16[64,4096]{1,0:T(8,128)(2,1)S(1)} %collective-permute-done.7.refs_2_), channel_id=1, source_target_pairs={{0,2},{1,3},{2,0},{3,1},{4,6},{5,7},{6,4},{7,5},{8,10},{9,11},{10,... | collective-permute-start | bytes 1572872 | tf_op jit(solution)/shard_map/ppermute | solution.py:333
  45.0 12.2 %collective-permute-start.14 = (bf16[128,1536]{1,0:T(8,128)(2,1)S(1)}, bf16[128,1536]{1,0:T(8,128)(2,1)S(1)}, u32[]{:S(2)}, u32[]{:S(2)}) collective-permute-start(bf16[128,1536]{1,0:T(8,128)(2,1)S(1)} %get-tuple-element.79), channel_id=1, source_target_pairs={{0,16},{1,17},{2,18},{3,19},{4,20},{5,21},{6,22},{7,23},{8,24},{9,... | collective-permute-start | bytes 1179656 | tf_op jit(solution)/shard_map/ppermute | solution.py:327
  57.1 1.7 %collective-permute-start.17 = (bf16[1,8,16,576]{3,2,0,1:T(8,128)(2,1)S(1)}, bf16[1,8,16,576]{3,2,0,1:T(8,128)(2,1)S(1)}, u32[]{:S(2)}, u32[]{:S(2)}) collective-permute-start(bf16[1,8,16,576]{3,2,0,1:T(8,128)(2,1)S(1)} %get-tuple-element.85), channel_id=1, source_target_pairs={{0,1},{1,0},{2,3},{3,2},{4,5},{5,4},{6,7},{7,6},{8,9},{9,8},{10,11... | collective-permute-start | bytes 442376 | tf_op jit(solution)/shard_map/ppermute | solution.py:336
  57.3 8.7 %collective-permute-start.15 = (bf16[64,2048]{1,0:T(8,128)(2,1)S(1)}, bf16[64,2048]{1,0:T(8,128)(2,1)S(1)}, u32[]{:S(2)}, u32[]{:S(2)}) collective-permute-start(bf16[64,2048]{1,0:T(8,128)(2,1)S(1)} %slice.40), channel_id=1, source_target_pairs={{0,2},{1,3},{2,0},{3,1},{4,6},{5,7},{6,4},{7,5},{8,10},{9,11},{10,... | collective-permute-start | bytes 786440 | tf_op jit(solution)/shard_map/ppermute | solution.py:333
  58.9 19.3 %collective-permute-start.16 = (bf16[64,2048]{1,0:T(8,128)(2,1)S(1)}, bf16[64,2048]{1,0:T(8,128)(2,1)S(1)}, u32[]{:S(2)}, u32[]{:S(2)}) collective-permute-start(bf16[64,2048]{1,0:T(8,128)(2,1)S(1)} %slice.41), channel_id=1, source_target_pairs={{0,4},{1,5},{2,6},{3,7},{4,8},{5,9},{6,10},{7,11},{8,12},{9,13},{1... | collective-permute-start | bytes 786440 | tf_op jit(solution)/shard_map/ppermute | solution.py:330
  60.5 17.9 %collective-permute-start.19 = (bf16[128,1536]{1,0:T(8,128)(2,1)S(1)}, bf16[128,1536]{1,0:T(8,128)(2,1)S(1)}, u32[]{:S(2)}, u32[]{:S(2)}) collective-permute-start(bf16[128,1536]{1,0:T(8,128)(2,1)S(1)} %get-tuple-element.90), channel_id=1, source_target_pairs={{0,1},{1,0},{2,3},{3,2},{4,5},{5,4},{6,7},{7,6},{8,9},{9,8},{10,11... | collective-permute-start | bytes 1179656 | tf_op jit(solution)/shard_map/ppermute | solution.py:327
  60.5 17.9 %collective-permute-start.20 = (bf16[128,1536]{1,0:T(8,128)(2,1)S(1)}, bf16[128,1536]{1,0:T(8,128)(2,1)S(1)}, u32[]{:S(2)}, u32[]{:S(2)}) collective-permute-start(bf16[128,1536]{1,0:T(8,128)(2,1)S(1)} %get-tuple-element.92), channel_id=1, source_target_pairs={{0,17},{1,16},{2,19},{3,18},{4,21},{5,20},{6,23},{7,22},{8,25},{9,... | collective-permute-start | bytes 1179656 | tf_op jit(solution)/shard_map/ppermute | solution.py:327
  66.0 12.0 %collective-permute-start.18 = (bf16[2,4,16,576]{3,2,0,1:T(8,128)(2,1)S(1)}, bf16[2,4,16,576]{3,2,0,1:T(8,128)(2,1)S(1)}, u32[]{:S(2)}, u32[]{:S(2)}) collective-permute-start(bf16[2,4,16,576]{3,2,0,1:T(8,128)(2,1)S(1)} %fusion.2), channel_id=1, source_target_pairs={{0,2},{1,3},{2,0},{3,1},{4,6},{5,7},{6,4},{7,5},{8,10},{9,11},{10,... | collective-permute-start | bytes 442376 | tf_op jit(solution)/shard_map/ppermute | solution.py:336
  76.5 9.3 %collective-permute-start.22 = (bf16[128,1024]{1,0:T(8,128)(2,1)S(1)}, bf16[128,1024]{1,0:T(8,128)(2,1)S(1)}, u32[]{:S(2)}, u32[]{:S(2)}) collective-permute-start(bf16[128,1024]{1,0:T(8,128)(2,1)S(1)} %get-tuple-element.97), channel_id=1, source_target_pairs={{0,16},{1,17},{2,18},{3,19},{4,20},{5,21},{6,22},{7,23},{8,24},{9,... | collective-permute-start | bytes 786440 | tf_op jit(solution)/shard_map/ppermute | solution.py:327
  78.0 12.4 %collective-permute-start.23 = (bf16[128,1024]{1,0:T(8,128)(2,1)S(1)}, bf16[128,1024]{1,0:T(8,128)(2,1)S(1)}, u32[]{:S(2)}, u32[]{:S(2)}) collective-permute-start(bf16[128,1024]{1,0:T(8,128)(2,1)S(1)} %get-tuple-element.98), channel_id=1, source_target_pairs={{0,17},{1,16},{2,19},{3,18},{4,21},{5,20},{6,23},{7,22},{8,25},{9,... | collective-permute-start | bytes 786440 | tf_op jit(solution)/shard_map/ppermute | solution.py:327
  78.1 6.8 %collective-permute-start.21 = (bf16[4,2,16,576]{3,2,0,1:T(8,128)(2,1)S(1)}, bf16[4,2,16,576]{3,2,0,1:T(8,128)(2,1)S(1)}, u32[]{:S(2)}, u32[]{:S(2)}) collective-permute-start(bf16[4,2,16,576]{3,2,0,1:T(8,128)(2,1)S(1)} %get-tuple-element.95), channel_id=1, source_target_pairs={{0,4},{1,5},{2,6},{3,7},{4,0},{5,1},{6,2},{7,3},{8,12},{9,13},{10,... | collective-permute-start | bytes 442376 | tf_op jit(solution)/shard_map/ppermute | solution.py:336
  82.9 13.0 %collective-permute-start.27 = (bf16[128,512]{1,0:T(8,128)(2,1)S(1)}, bf16[128,512]{1,0:T(8,128)(2,1)S(1)}, u32[]{:S(2)}, u32[]{:S(2)}) collective-permute-start(bf16[128,512]{1,0:T(8,128)(2,1)S(1)} %get-tuple-element.108), channel_id=1, source_target_pairs={{0,16},{1,17},{2,18},{3,19},{4,20},{5,21},{6,22},{7,23},{8,24},{9,... | collective-permute-start | bytes 393224 | tf_op jit(solution)/shard_map/ppermute | solution.py:327
  83.7 14.4 %collective-permute-start.30 = (bf16[128,512]{1,0:T(8,128)(2,1)S(1)}, bf16[128,512]{1,0:T(8,128)(2,1)S(1)}, u32[]{:S(2)}, u32[]{:S(2)}) collective-permute-start(bf16[128,512]{1,0:T(8,128)(2,1)S(1)} %get-tuple-element.111), channel_id=1, source_target_pairs={{0,17},{1,16},{2,19},{3,18},{4,21},{5,20},{6,23},{7,22},{8,25},{9,... | collective-permute-start | bytes 393224 | tf_op jit(solution)/shard_map/ppermute | solution.py:327
  90.5 11.9 %collective-permute-start.24 = (bf16[8,1,16,576]{3,2,0,1:T(8,128)(2,1)S(1)}, bf16[8,1,16,576]{3,2,0,1:T(8,128)(2,1)S(1)}, u32[]{:S(2)}, u32[]{:S(2)}) collective-permute-start(bf16[8,1,16,576]{3,2,0,1:T(8,128)(2,1)S(1)} %get-tuple-element.102), channel_id=1, source_target_pairs={{0,8},{1,9},{2,10},{3,11},{4,12},{5,13},{6,14},{7,15},{8,0},{9,1},... | collective-permute-start | bytes 442376 | tf_op jit(solution)/shard_map/ppermute | solution.py:336
  95.9 6.4 %collective-permute-start.28 = (bf16[128,512]{1,0:T(8,128)(2,1)S(1)}, bf16[128,512]{1,0:T(8,128)(2,1)S(1)}, u32[]{:S(2)}, u32[]{:S(2)}) collective-permute-start(bf16[128,512]{1,0:T(8,128)(2,1)S(1)} %get-tuple-element.109), channel_id=1, source_target_pairs={{0,16},{1,17},{2,18},{3,19},{4,20},{5,21},{6,22},{7,23},{8,24},{9,... | collective-permute-start | bytes 393224 | tf_op jit(solution)/shard_map/ppermute | solution.py:327
  96.6 7.4 %collective-permute-start.25 = (bf16[128,1024]{1,0:T(8,128)(2,1)S(1)}, bf16[128,1024]{1,0:T(8,128)(2,1)S(1)}, u32[]{:S(2)}, u32[]{:S(2)}) collective-permute-start(bf16[128,1024]{1,0:T(8,128)(2,1)S(1)} %get-tuple-element.104), channel_id=1, source_target_pairs={{0,1},{1,0},{2,3},{3,2},{4,5},{5,4},{6,7},{7,6},{8,9},{9,8},{10,11... | collective-permute-start | bytes 786440 | tf_op jit(solution)/shard_map/ppermute | solution.py:327
  98.0 5.9 %collective-permute-start.26 = (bf16[128,512]{1,0:T(8,128)(2,1)S(1)}, bf16[128,512]{1,0:T(8,128)(2,1)S(1)}, u32[]{:S(2)}, u32[]{:S(2)}) collective-permute-start(bf16[128,512]{1,0:T(8,128)(2,1)S(1)} %get-tuple-element.105), channel_id=1, source_target_pairs={{0,1},{1,0},{2,3},{3,2},{4,5},{5,4},{6,7},{7,6},{8,9},{9,8},{10,11... | collective-permute-start | bytes 393224 | tf_op jit(solution)/shard_map/ppermute | solution.py:327
  98.0 6.9 %collective-permute-start.31 = (bf16[128,512]{1,0:T(8,128)(2,1)S(1)}, bf16[128,512]{1,0:T(8,128)(2,1)S(1)}, u32[]{:S(2)}, u32[]{:S(2)}) collective-permute-start(bf16[128,512]{1,0:T(8,128)(2,1)S(1)} %get-tuple-element.113), channel_id=1, source_target_pairs={{0,17},{1,16},{2,19},{3,18},{4,21},{5,20},{6,23},{7,22},{8,25},{9,... | collective-permute-start | bytes 393224 | tf_op jit(solution)/shard_map/ppermute | solution.py:327
  102.4 2.6 %collective-permute-start.29 = (bf16[128,512]{1,0:T(8,128)(2,1)S(1)}, bf16[128,512]{1,0:T(8,128)(2,1)S(1)}, u32[]{:S(2)}, u32[]{:S(2)}) collective-permute-start(bf16[128,512]{1,0:T(8,128)(2,1)S(1)} %get-tuple-element.110), channel_id=1, source_target_pairs={{0,1},{1,0},{2,3},{3,2},{4,5},{5,4},{6,7},{7,6},{8,9},{9,8},{10,11... | collective-permute-start | bytes 393224 | tf_op jit(solution)/shard_map/ppermute | solution.py:327

commit v18 on v16

--- a/solution.py
+++ b/solution.py
@@ -411,6 +411,15 @@
         name="queries",
     )(quarter_info, *in_hbm(q_heads, tie(cosine, pair_rows if outer else got), sine))
 
+    held = outgoing.reshape(1, size, slot_count, ROW)
+    exchanged = []
+
+    def exchange(*others):
+        half_of = held.shape[1] // 2
+        moving = tie(held[:, half_of:], *others)
+        exchanged.append(pair_swap(moving, 1 << len(exchanged)))
+        return jnp.concatenate([held[:, :half_of], exchanged[-1]], axis=0)
+
     phases = Phases()
     line = [pair_rows] if outer else []
     side = []
@@ -441,11 +450,18 @@
         elif kind == "f":
             far_behind = phases.send(late, from_behind, both_groups, 4, True)
         elif kind == "p":
+            if outer:
+                held = exchange(line[1])
+                both_groups = tie(both_groups, exchanged[0])
             own_rows = jnp.concatenate([both_groups, behind, far_behind], axis=0)
             other_rows = phases.send(late, quad_swap, own_rows, 1)
         elif kind == "q":
             j, r = int(name[1]), int(name[2])
-            moved[j][r] = phases.send(late, quad_swap, queries[r * CHUNKS + j], r)
+            if outer and name[1:3] == "13":
+                held = exchange(line[2])
+            moved[j][r] = phases.send(
+                late, quad_swap, tie(queries[r * CHUNKS + j], *exchanged[1:]), r
+            )
 
     def weights_for(j):
         if not outer:
@@ -495,18 +511,6 @@
             name="attend",
         )(mine_info, *keys, *pieces_of_weight, *moved[j], *moved[j])
 
-    held = outgoing.reshape(1, size, slot_count, ROW)
-    exchanged = []
-
-    def exchange(*others):
-        half_of = held.shape[1] // 2
-        moving = tie(held[:, half_of:], *others)
-        exchanged.append(pair_swap(moving, 1 << len(exchanged)))
-        return jnp.concatenate([held[:, :half_of], exchanged[-1]], axis=0)
-
-    if outer:
-        held = exchange(*line[outer - 1 :])
-        held = exchange(halves[0])
     results = []
     for call in CALLS:
         last = len(results) + 1 == len(CALLS)

time: 105 us -> 110 us (1.048)
  waiting for transfers between devices: 40.2 us -> 43.5 us
  starting transfers between devices: 33.9 us -> 35.7 us
    ppermute x4, starting transfers between devices: 8.36 us -> 13.8 us  [around(): lax.ppermute(array, 'ctx', [(i, (i + by) % size) for i in range(size)])]
    ppermute x4, waiting for transfers between devices: 10.9 us -> 14.4 us  [around(): lax.ppermute(array, 'ctx', [(i, (i + by) % size) for i in range(size)])]
    ppermute x4, starting transfers between devices: 4.91 us -> 1.53 us  [inner_swap(): return lax.ppermute(array, 'ctx', [(i, i ^ 2) for i in range(size)])]
    ppermute x4, waiting for transfers between devices: 0.21 us -> 3.51 us  [pair_swap(): return lax.ppermute(array, 'ctx', [(i, i ^ distance) for i in range(size)])]
    ppermute x18, waiting for transfers between devices: 25.8 us -> 23.1 us  [quad_swap(): return lax.ppermute(array, ('groups', 'ctx'), pairs)]
    ppermute x18, starting transfers between devices: 14.1 us -> 12.8 us  [quad_swap(): return lax.ppermute(array, ('groups', 'ctx'), pairs)]
  transfers between devices with their start and end apart: 32 -> 32, of which waited for: 14 -> 13; matrix products, arithmetic and copies ran while one was open for 1% -> 1% of each run, Pallas kernels for 24% -> 23%
where the time goes in v18:
time: 110 us
  waiting for transfers between devices  43.5 us (40%)
  starting transfers between devices  35.7 us (32%)
  Pallas kernels  27.2 us (25%)
  local copies, waits for them, and re-layouts  2.11 us (2%)
    ppermute x18, waiting for transfers between devices, quad_swap(): return lax.ppermute(array, ('groups', 'ctx'), pairs)  23.1 us
    pallas_call x3, Pallas kernels, attend(): pl.pallas_call(functools.partial(attend_kernel, outer), grid=(steps,), ou...  17.9 us
    ppermute x4, waiting for transfers between devices, around(): lax.ppermute(array, 'ctx', [(i, (i + by) % size) for i in range(size)])  14.4 us
    ppermute x4, starting transfers between devices, around(): lax.ppermute(array, 'ctx', [(i, (i + by) % size) for i in range(size)])  13.8 us
    ppermute x18, starting transfers between devices, quad_swap(): return lax.ppermute(array, ('groups', 'ctx'), pairs)  12.8 us
    ppermute x4, starting transfers between devices, pair_swap(): return lax.ppermute(array, 'ctx', [(i, i ^ distance) for i in range(size)])  4.36 us
    ppermute x4, waiting for transfers between devices, pair_swap(): return lax.ppermute(array, 'ctx', [(i, i ^ distance) for i in range(size)])  3.51 us
    pallas_call x1, Pallas kernels, body(): pl.pallas_call(query_kernel, out_shape=[shape((tok, h * (NOPE + ROPE))) f...  3.33 us
  transfers between devices with their start and end apart: 32, of which 13 were waited for; matrix products, arithmetic and copies ran while one was open for 1% of the time, Pallas kernels for 23%

profile of v18, /device:TPU:0, one launch (start us, length us, event | category | flops | bytes accessed | tf_op | source)
XLA Modules:
  0.0 109.7 jit_solution(2008962468715105097)
XLA Ops:
  0.6 1.0 constant_dynamic-slice_fusion
  1.6 0.5 collective-permute-start
  2.1 1.2 %collective-permute-done.got = bf16[32,4096]{1,0:T(8,128)(2,1)S(1)} collective-permute-done((bf16[32,4096]{1,0:T(8,128)(2,1)S(1)}, bf16[32,4096]{1,0:T(8,128)(2,1)S(1)}, u32[]{:S(2)}, u32[]{:S(2)}) %collective-permute-start) | collective-permute-done | bytes 262176 | tf_op jit(solution)/shard_map/ppermute | solution.py:327
  3.3 1.0 pair.1.refs_0_
  4.3 3.0 %collective-permute-start.2 = (bf16[64,4096]{1,0:T(8,128)(2,1)S(1)}, bf16[64,4096]{1,0:T(8,128)(2,1)S(1)}, u32[]{:S(2)}, u32[]{:S(2)}) collective-permute-start(bf16[64,4096]{1,0:T(8,128)(2,1)S(1)} %pair.1.refs_0_), channel_id=1, source_target_pairs={{0,4},{1,5},{2,6},{3,7},{4,8},{5,9},{6,10},{7,11},{8,12},{9,13},{1... | collective-permute-start | bytes 1572872 | tf_op jit(solution)/shard_map/ppermute | solution.py:330
  7.3 2.3 %rows.1 = (bf16[128,640]{1,0:T(8,128)(2,1)}, f32[128,128]{1,0:T(8,128)}, f32[128,128]{1,0:T(8,128)}, bf16[256,576]{1,0:T(8,128)(2,1)}) custom-call(s32[1]{0:T(128)} %bitcast.1.info, s32[8]{0:T(128)} %lengths, bf16[576,128]{1,0:T(8,128)(2,1)} %bitcast.9, f32[1,512]{1,0:T(1,128)} %bitcast.10, s32[1,128]{1,0:T(1,128)} %bitcast.11, f32[1,128]{1,0:T(1,128)} %constant.30.clone.freq), custom_call_target="tpu_custom_call" | custom-call | tf_op jit(solution)/shard_map/rows/pallas_call | solution.py:377
  9.6 1.5 %collective-permute-start.1 = (bf16[128,640]{1,0:T(8,128)(2,1)}, bf16[128,640]{1,0:T(8,128)(2,1)S(1)}, u32[]{:S(2)}, u32[]{:S(2)}) collective-permute-start(bf16[128,640]{1,0:T(8,128)(2,1)} %get-tuple-element.62), channel_id=1, source_target_pairs={{0,16},{1,17},{2,18},{3,19},{4,20},{5,21},{6,22},{7,23},{8,24},{9,... | collective-permute-start | bytes 491528 | tf_op jit(solution)/shard_map/ppermute | solution.py:327
  11.1 1.5 %collective-permute-start.6 = (bf16[64,4096]{1,0:T(8,128)(2,1)S(1)}, bf16[64,4096]{1,0:T(8,128)(2,1)S(1)}, u32[]{:S(2)}, u32[]{:S(2)}) collective-permute-start(bf16[64,4096]{1,0:T(8,128)(2,1)S(1)} %pair.1.refs_0_), channel_id=1, source_target_pairs={{0,2},{1,3},{2,0},{3,1},{4,6},{5,7},{6,4},{7,5},{8,10},{9,11},{10,... | collective-permute-start | bytes 1572872 | tf_op jit(solution)/shard_map/ppermute | solution.py:333
  12.6 3.3 %queries.1 = (bf16[128,1536]{1,0:T(8,128)(2,1)S(1)}, bf16[128,1536]{1,0:T(8,128)(2,1)S(1)}, bf16[128,1536]{1,0:T(8,128)(2,1)S(1)}, bf16[128,1536]{1,0:T(8,128)(2...) custom-call(s32[1]{0:T(128)} %bitcast.info, ...), custom_call_target="tpu_custom_call" | custom-call | bytes 6291456 | tf_op jit(solution)/shard_map/queries/pallas_call | solution.py:401
  15.9 0.6 collective-permute-start.7
  16.6 0.0 collective-permute-done.1
  16.6 2.6 %collective-permute-start.4 = (bf16[256,640]{1,0:T(8,128)(2,1)S(1)}, bf16[256,640]{1,0:T(8,128)(2,1)S(1)}, u32[]{:S(2)}, u32[]{:S(2)}) collective-permute-start(bf16[256,640]{1,0:T(8,128)(2,1)S(1)} %constant_dynamic-update-slice_fusion), channel_id=1, source_target_pairs={{0,2},{1,3},{2,4},{3,5},{4,6},{5,7},{6,8},{7,9},{8,10},{9,11},{10,... | collective-permute-start | bytes 983048 | tf_op jit(solution)/shard_map/ppermute | solution.py:342
  19.3 2.2 %collective-permute-done.2.refs_1_ = bf16[64,4096]{1,0:T(8,128)(2,1)S(1)} collective-permute-done((bf16[64,4096]{1,0:T(8,128)(2,1)S(1)}, bf16[64,4096]{1,0:T(8,128)(2,1)S(1)}, u32[]{:S(2)}, u32[]{:S(2)}) %collective-permute-start.2) | collective-permute-done | bytes 524320 | tf_op jit(solution)/shard_map/ppermute | solution.py:330
  21.5 0.0 collective-permute-start.3
  21.5 4.8 %collective-permute-done.7.refs_10_.refs_14_ = bf16[128,1536]{1,0:T(8,128)(2,1)S(1)} collective-permute-done((bf16[128,1536]{1,0:T(8,128)(2,1)S(1)}, bf16[128,1536]{1,0:T(8,128)(2,1)S(1)}, u32[]{:S(2)}, u32[]{:S(2)}) %collective-permute-start.7) | collective-permute-done | bytes 393248 | tf_op jit(solution)/shard_map/ppermute | solution.py:327
  26.3 0.0 collective-permute-done.6.refs_4_
  26.3 6.8 %collective-permute-start.8 = (bf16[64,4096]{1,0:T(8,128)(2,1)S(1)}, bf16[64,4096]{1,0:T(8,128)(2,1)S(1)}, u32[]{:S(2)}, u32[]{:S(2)}) collective-permute-start(bf16[64,4096]{1,0:T(8,128)(2,1)S(1)} %collective-permute-done.2.refs_1_), channel_id=1, source_target_pairs={{0,4},{1,5},{2,6},{3,7},{4,8},{5,9},{6,10},{7,11},{8,12},{9,13},{1... | collective-permute-start | bytes 1572872 | tf_op jit(solution)/shard_map/ppermute | solution.py:330
  33.1 0.0 collective-permute-start.9
  33.1 0.7 collective-permute-start.5
  33.8 1.1 %collective-permute-start.10 = (bf16[128,1536]{1,0:T(8,128)(2,1)S(1)}, bf16[128,1536]{1,0:T(8,128)(2,1)S(1)}, u32[]{:S(2)}, u32[]{:S(2)}) collective-permute-start(bf16[128,1536]{1,0:T(8,128)(2,1)S(1)} %get-tuple-element.73), channel_id=1, source_target_pairs={{0,17},{1,16},{2,19},{3,18},{4,21},{5,20},{6,23},{7,22},{8,25},{9,... | collective-permute-start | bytes 1179656 | tf_op jit(solution)/shard_map/ppermute | solution.py:327
  34.9 0.0 collective-permute-start.11
  35.0 0.0 collective-permute-done.5
  35.1 9.1 %collective-permute-done.10.refs_11_.refs_15_ = bf16[128,1536]{1,0:T(8,128)(2,1)S(1)} collective-permute-done((bf16[128,1536]{1,0:T(8,128)(2,1)S(1)}, bf16[128,1536]{1,0:T(8,128)(2,1)S(1)}, u32[]{:S(2)}, u32[]{:S(2)}) %collective-permute-start.10) | collective-permute-done | bytes 393248 | tf_op jit(solution)/shard_map/ppermute | solution.py:327
  44.2 0.0 collective-permute-done.11.refs_9_.refs_13_
  44.2 1.3 %collective-permute-done.8.refs_2_ = bf16[64,4096]{1,0:T(8,128)(2,1)S(1)} collective-permute-done((bf16[64,4096]{1,0:T(8,128)(2,1)S(1)}, bf16[64,4096]{1,0:T(8,128)(2,1)S(1)}, u32[]{:S(2)}, u32[]{:S(2)}) %collective-permute-start.8) | collective-permute-done | bytes 524320 | tf_op jit(solution)/shard_map/ppermute | solution.py:330
  45.5 1.4 %collective-permute-start.12 = (bf16[768,640]{1,0:T(8,128)(2,1)S(1)}, bf16[768,640]{1,0:T(8,128)(2,1)S(1)}, u32[]{:S(2)}, u32[]{:S(2)}) collective-permute-start(bf16[768,640]{1,0:T(8,128)(2,1)S(1)} %constant_dynamic-update-slice_fusion.2.own), channel_id=1, source_target_pairs={{0,1},{1,0},{2,3},{3,2},{4,5},{5,4},{6,7},{7,6},{8,9},{9,8},{10,11... | collective-permute-start | bytes 2949128 | tf_op jit(solution)/shard_map/ppermute | solution.py:327
  46.9 2.2 %collective-permute-start.13 = (bf16[64,4096]{1,0:T(8,128)(2,1)S(1)}, bf16[64,4096]{1,0:T(8,128)(2,1)S(1)}, u32[]{:S(2)}, u32[]{:S(2)}) collective-permute-start(bf16[64,4096]{1,0:T(8,128)(2,1)S(1)} %collective-permute-done.8.refs_2_), channel_id=1, source_target_pairs={{0,4},{1,5},{2,6},{3,7},{4,8},{5,9},{6,10},{7,11},{8,12},{9,13},{1... | collective-permute-start | bytes 1572872 | tf_op jit(solution)/shard_map/ppermute | solution.py:330
  49.1 0.5 collective-permute-start.15
  49.6 2.1 %collective-permute-start.18 = (bf16[2,4,16,576]{3,2,0,1:T(8,128)(2,1)S(1)}, bf16[2,4,16,576]{3,2,0,1:T(8,128)(2,1)S(1)}, u32[]{:S(2)}, u32[]{:S(2)}) collective-permute-start(bf16[2,4,16,576]{3,2,0,1:T(8,128)(2,1)S(1)} %fusion.2), channel_id=1, source_target_pairs={{0,2},{1,3},{2,0},{3,1},{4,6},{5,7},{6,4},{7,5},{8,10},{9,11},{10,... | collective-permute-start | bytes 442376 | tf_op jit(solution)/shard_map/ppermute | solution.py:336
  51.7 10.8 %collective-permute-done.13.refs_3_ = bf16[64,4096]{1,0:T(8,128)(2,1)S(1)} collective-permute-done((bf16[64,4096]{1,0:T(8,128)(2,1)S(1)}, bf16[64,4096]{1,0:T(8,128)(2,1)S(1)}, u32[]{:S(2)}, u32[]{:S(2)}) %collective-permute-start.13) | collective-permute-done | bytes 524320 | tf_op jit(solution)/shard_map/ppermute | solution.py:330
  62.6 1.3 %collective-permute-done.14.refs_6_ = bf16[64,4096]{1,0:T(8,128)(2,1)S(1)} collective-permute-done((bf16[64,4096]{1,0:T(8,128)(2,1)S(1)}, bf16[64,4096]{1,0:T(8,128)(2,1)S(1)}, u32[]{:S(2)}, u32[]{:S(2)}) %collective-permute-start.14) | collective-permute-done | bytes 524320 | tf_op jit(solution)/shard_map/ppermute | solution.py:333
  63.9 0.0 collective-permute-done.12.other
  63.9 0.0 collective-permute-start.16
  63.9 3.5 %collective-permute-done.18 = bf16[2,4,16,576]{3,2,0,1:T(8,128)(2,1)S(1)} collective-permute-done((bf16[2,4,16,576]{3,2,0,1:T(8,128)(2,1)S(1)}, bf16[2,4,16,576]{3,2,0,1:T(8,128)(2,1)S(1)}, u32[]{:S(2)}, u32[]{:S(2)}) %collective-permute-start.18) | collective-permute-done | bytes 147488 | tf_op jit(solution)/shard_map/ppermute | solution.py:336
  67.4 0.1 fusion
  67.5 1.8 %collective-permute-start.17 = (bf16[64,2048]{1,0:T(8,128)(2,1)S(1)}, bf16[64,2048]{1,0:T(8,128)(2,1)S(1)}, u32[]{:S(2)}, u32[]{:S(2)}) collective-permute-start(bf16[64,2048]{1,0:T(8,128)(2,1)S(1)} %slice.42), channel_id=1, source_target_pairs={{0,4},{1,5},{2,6},{3,7},{4,8},{5,9},{6,10},{7,11},{8,12},{9,13},{1... | collective-permute-start | bytes 786440 | tf_op jit(solution)/shard_map/ppermute | solution.py:330
  69.3 0.0 collective-permute-start.19
  69.3 0.6 collective-permute-start.20
  70.0 0.6 keys.1
  70.6 1.2 %collective-permute-done.16.refs_7_ = bf16[64,2048]{1,0:T(8,128)(2,1)S(1)} collective-permute-done((bf16[64,2048]{1,0:T(8,128)(2,1)S(1)}, bf16[64,2048]{1,0:T(8,128)(2,1)S(1)}, u32[]{:S(2)}, u32[]{:S(2)}) %collective-permute-start.16) | collective-permute-done | bytes 262176 | tf_op jit(solution)/shard_map/ppermute | solution.py:333
  71.8 8.9 %attend.3 = (bf16[128,1024]{1,0:T(8,128)(2,1)S(1)}, bf16[128,1024]{1,0:T(8,128)(2,1)S(1)}, bf16[128,1024]{1,0:T(8,128)(2,1)S(1)}, bf16[128,1024]{1,0:T(8,128)(2,1)S(1)}) custom-call(s32[1]{0:T(128)} %bitcast.1.info, bf16[2,640,512]{2,1,0:T(8,128)(2,1)S(1)} %get-tuple-element.77.latent, bf16[2,640,128]{2,1,0:T(8,128)(2,1)S(1)} %get-tuple-element.78.rope_even, ...), custom_call_target="tpu_custom_call" | custom-call | flops 4362076160 | bytes 8388608 | tf_op jit(solution)/shard_map/attend/pallas_call | solution.py:492
  80.8 0.0 collective-permute-done.17.refs_7_
  80.8 1.6 %collective-permute-start.21 = (bf16[4,2,16,576]{3,2,0,1:T(8,128)(2,1)S(1)}, bf16[4,2,16,576]{3,2,0,1:T(8,128)(2,1)S(1)}, u32[]{:S(2)}, u32[]{:S(2)}) collective-permute-start(bf16[4,2,16,576]{3,2,0,1:T(8,128)(2,1)S(1)} %get-tuple-element.99), channel_id=1, source_target_pairs={{0,4},{1,5},{2,6},{3,7},{4,0},{5,1},{6,2},{7,3},{8,12},{9,13},{10,... | collective-permute-start | bytes 442376 | tf_op jit(solution)/shard_map/ppermute | solution.py:336
  82.4 0.5 collective-permute-start.22
  83.0 0.0 collective-permute-start.24
  83.0 1.6 %collective-permute-start.30 = (bf16[128,1024]{1,0:T(8,128)(2,1)S(1)}, bf16[128,1024]{1,0:T(8,128)(2,1)S(1)}, u32[]{:S(2)}, u32[]{:S(2)}) collective-permute-start(bf16[128,1024]{1,0:T(8,128)(2,1)S(1)} %get-tuple-element.114), channel_id=1, source_target_pairs={{0,17},{1,16},{2,19},{3,18},{4,21},{5,20},{6,23},{7,22},{8,25},{9,... | collective-permute-start | bytes 786440 | tf_op jit(solution)/shard_map/ppermute | solution.py:327
  84.6 4.5 %attend.4 = (bf16[128,512]{1,0:T(8,128)(2,1)S(1)}, bf16[128,512]{1,0:T(8,128)(2,1)S(1)}, bf16[128,512]{1,0:T(8,128)(2,1)S(1)}, bf16[128,512]{1,0:T(8,128)(2,1)S(1)}) custom-call(s32[1]{0:T(128)} %bitcast.1.info, bf16[2,640,512]{2,1,0:T(8,128)(2,1)S(1)} %get-tuple-element.77.latent, bf16[2,640,128]{2,1,0:T(8,128)(2,1)S(1)} %get-tuple-element.78.rope_even, ...), custom_call_target="tpu_custom_call" | custom-call | flops 2181038080 | bytes 4194304 | tf_op jit(solution)/shard_map/attend/pallas_call | solution.py:492
  89.1 0.6 collective-permute-start.26
  89.7 0.0 collective-permute-done.21
  89.7 0.8 collective-permute-start.27
  90.5 0.1 fusion.1
  90.5 1.1 %collective-permute-done.22.refs_6_ = bf16[128,1024]{1,0:T(8,128)(2,1)S(1)} collective-permute-done((bf16[128,1024]{1,0:T(8,128)(2,1)S(1)}, bf16[128,1024]{1,0:T(8,128)(2,1)S(1)}, u32[]{:S(2)}, u32[]{:S(2)}) %collective-permute-start.22) | collective-permute-done | bytes 262176 | tf_op jit(solution)/shard_map/ppermute | solution.py:327
  91.7 0.6 collective-permute-start.23
  92.3 4.5 %attend.5 = (bf16[128,512]{1,0:T(8,128)(2,1)S(1)}, bf16[128,512]{1,0:T(8,128)(2,1)S(1)}, bf16[128,512]{1,0:T(8,128)(2,1)S(1)}, bf16[128,512]{1,0:T(8,128)(2,1)S(1)}) custom-call(s32[1]{0:T(128)} %bitcast.1.info, bf16[2,640,512]{2,1,0:T(8,128)(2,1)S(1)} %get-tuple-element.77.latent, bf16[2,640,128]{2,1,0:T(8,128)(2,1)S(1)} %get-tuple-element.78.rope_even, ...), custom_call_target="tpu_custom_call" | custom-call | flops 2181038080 | bytes 4194304 | tf_op jit(solution)/shard_map/attend/pallas_call | solution.py:492
  96.8 2.2 %collective-permute-done.26.refs_7_ = bf16[128,512]{1,0:T(8,128)(2,1)S(1)} collective-permute-done((bf16[128,512]{1,0:T(8,128)(2,1)S(1)}, bf16[128,512]{1,0:T(8,128)(2,1)S(1)}, u32[]{:S(2)}, u32[]{:S(2)}) %collective-permute-start.26) | collective-permute-done | bytes 131104 | tf_op jit(solution)/shard_map/ppermute | solution.py:327
  99.0 0.0 collective-permute-start.25
  99.0 0.0 collective-permute-done.27.refs_10_
  99.0 0.9 collective-permute-start.29
  99.9 1.9 %collective-permute-start.31 = (bf16[128,512]{1,0:T(8,128)(2,1)S(1)}, bf16[128,512]{1,0:T(8,128)(2,1)S(1)}, u32[]{:S(2)}, u32[]{:S(2)}) collective-permute-start(bf16[128,512]{1,0:T(8,128)(2,1)S(1)} %get-tuple-element.115), channel_id=1, source_target_pairs={{0,17},{1,16},{2,19},{3,18},{4,21},{5,20},{6,23},{7,22},{8,25},{9,... | collective-permute-start | bytes 393224 | tf_op jit(solution)/shard_map/ppermute | solution.py:327
  101.9 0.6 sort.1
  102.6 0.9 copy.9
  103.4 1.4 %collective-permute-done.29.refs_8_ = bf16[128,512]{1,0:T(8,128)(2,1)S(1)} collective-permute-done((bf16[128,512]{1,0:T(8,128)(2,1)S(1)}, bf16[128,512]{1,0:T(8,128)(2,1)S(1)}, u32[]{:S(2)}, u32[]{:S(2)}) %collective-permute-start.29) | collective-permute-done | bytes 131104 | tf_op jit(solution)/shard_map/ppermute | solution.py:327
  104.9 3.3 %collective-permute-done.31.refs_11_ = bf16[128,512]{1,0:T(8,128)(2,1)S(1)} collective-permute-done((bf16[128,512]{1,0:T(8,128)(2,1)S(1)}, bf16[128,512]{1,0:T(8,128)(2,1)S(1)}, u32[]{:S(2)}, u32[]{:S(2)}) %collective-permute-start.31) | collective-permute-done | bytes 131104 | tf_op jit(solution)/shard_map/ppermute | solution.py:327
  108.2 1.4 %place.1 = bf16[128,8192]{1,0:T(8,128)(2,1)} custom-call(s32[1]{0:T(128)} %bitcast.info, bf16[128,1024]{1,0:T(8,128)(2,1)S(1)} %get-tuple-element.85.refs_0_, bf16[128,512]{1,0:T(8,128)(2,1)S(1)} %get-tuple-element.97.refs_1_, bf16[128,512]{1,0:T(8,128)(2,1)S(1)} %get-tuple-element.103.refs_2_, bf16[128,1024]{1,0:T(8,128)(2,1)S(1)} %collective-permute-done.24.refs_3_, ...), custom_call_target="tpu_custom_call" | custom-call | tf_op jit(solution)/shard_map/place/pallas_call | solution.py:544
  (28 shorter events, 0.4 us)
Async XLA Ops:
  1.6 1.7 %collective-permute-start = (bf16[32,4096]{1,0:T(8,128)(2,1)S(1)}, bf16[32,4096]{1,0:T(8,128)(2,1)S(1)}, u32[]{:S(2)}, u32[]{:S(2)}) collective-permute-start(bf16[32,4096]{1,0:T(8,128)(2,1)S(1)} %constant_dynamic-slice_fusion), channel_id=1, source_target_pairs={{0,1},{1,0},{2,3},{3,2},{4,5},{5,4},{6,7},{7,6},{8,9},{9,8},{10,11... | collective-permute-start | bytes 786440 | tf_op jit(solution)/shard_map/ppermute | solution.py:327
  4.3 17.2 %collective-permute-start.2 = (bf16[64,4096]{1,0:T(8,128)(2,1)S(1)}, bf16[64,4096]{1,0:T(8,128)(2,1)S(1)}, u32[]{:S(2)}, u32[]{:S(2)}) collective-permute-start(bf16[64,4096]{1,0:T(8,128)(2,1)S(1)} %pair.1.refs_0_), channel_id=1, source_target_pairs={{0,4},{1,5},{2,6},{3,7},{4,8},{5,9},{6,10},{7,11},{8,12},{9,13},{1... | collective-permute-start | bytes 1572872 | tf_op jit(solution)/shard_map/ppermute | solution.py:330
  9.6 7.0 %copy-start.1 = (bf16[128,640]{1,0:T(8,128)(2,1)S(1)}, bf16[128,640]{1,0:T(8,128)(2,1)}, u32[]{:S(2)}) copy-start(bf16[128,640]{1,0:T(8,128)(2,1)} %get-tuple-element.62) | copy-start | bytes 491524
  9.6 9.7 %copy-start = (bf16[256,576]{1,0:T(8,128)(2,1)S(1)}, bf16[256,576]{1,0:T(8,128)(2,1)}, u32[]{:S(2)}) copy-start(bf16[256,576]{1,0:T(8,128)(2,1)} %get-tuple-element.63) | copy-start | bytes 884740
  9.6 7.0 %collective-permute-start.1 = (bf16[128,640]{1,0:T(8,128)(2,1)}, bf16[128,640]{1,0:T(8,128)(2,1)S(1)}, u32[]{:S(2)}, u32[]{:S(2)}) collective-permute-start(bf16[128,640]{1,0:T(8,128)(2,1)} %get-tuple-element.62), channel_id=1, source_target_pairs={{0,16},{1,17},{2,18},{3,19},{4,20},{5,21},{6,22},{7,23},{8,24},{9,... | collective-permute-start | bytes 491528 | tf_op jit(solution)/shard_map/ppermute | solution.py:327
  11.1 15.2 %collective-permute-start.6 = (bf16[64,4096]{1,0:T(8,128)(2,1)S(1)}, bf16[64,4096]{1,0:T(8,128)(2,1)S(1)}, u32[]{:S(2)}, u32[]{:S(2)}) collective-permute-start(bf16[64,4096]{1,0:T(8,128)(2,1)S(1)} %pair.1.refs_0_), channel_id=1, source_target_pairs={{0,2},{1,3},{2,0},{3,1},{4,6},{5,7},{6,4},{7,5},{8,10},{9,11},{10,... | collective-permute-start | bytes 1572872 | tf_op jit(solution)/shard_map/ppermute | solution.py:333
  15.9 10.4 %collective-permute-start.7 = (bf16[128,1536]{1,0:T(8,128)(2,1)S(1)}, bf16[128,1536]{1,0:T(8,128)(2,1)S(1)}, u32[]{:S(2)}, u32[]{:S(2)}) collective-permute-start(bf16[128,1536]{1,0:T(8,128)(2,1)S(1)} %get-tuple-element.69), channel_id=1, source_target_pairs={{0,16},{1,17},{2,18},{3,19},{4,20},{5,21},{6,22},{7,23},{8,24},{9,... | collective-permute-start | bytes 1179656 | tf_op jit(solution)/shard_map/ppermute | solution.py:327
  16.6 17.2 %collective-permute-start.4 = (bf16[256,640]{1,0:T(8,128)(2,1)S(1)}, bf16[256,640]{1,0:T(8,128)(2,1)S(1)}, u32[]{:S(2)}, u32[]{:S(2)}) collective-permute-start(bf16[256,640]{1,0:T(8,128)(2,1)S(1)} %constant_dynamic-update-slice_fusion), channel_id=1, source_target_pairs={{0,2},{1,3},{2,4},{3,5},{4,6},{5,7},{6,8},{7,9},{8,10},{9,11},{10,... | collective-permute-start | bytes 983048 | tf_op jit(solution)/shard_map/ppermute | solution.py:342
  21.5 13.4 %collective-permute-start.3 = (bf16[1,8,16,576]{3,2,0,1:T(8,128)(2,1)S(1)}, bf16[1,8,16,576]{3,2,0,1:T(8,128)(2,1)S(1)}, u32[]{:S(2)}, u32[]{:S(2)}) collective-permute-start(bf16[1,8,16,576]{3,2,0,1:T(8,128)(2,1)S(1)} %get-tuple-element.64), channel_id=1, source_target_pairs={{0,1},{1,0},{2,3},{3,2},{4,5},{5,4},{6,7},{7,6},{8,9},{9,8},{10,11... | collective-permute-start | bytes 442376 | tf_op jit(solution)/shard_map/ppermute | solution.py:336
  26.3 19.1 %collective-permute-start.8 = (bf16[64,4096]{1,0:T(8,128)(2,1)S(1)}, bf16[64,4096]{1,0:T(8,128)(2,1)S(1)}, u32[]{:S(2)}, u32[]{:S(2)}) collective-permute-start(bf16[64,4096]{1,0:T(8,128)(2,1)S(1)} %collective-permute-done.2.refs_1_), channel_id=1, source_target_pairs={{0,4},{1,5},{2,6},{3,7},{4,8},{5,9},{6,10},{7,11},{8,12},{9,13},{1... | collective-permute-start | bytes 1572872 | tf_op jit(solution)/shard_map/ppermute | solution.py:330
  33.1 12.4 %collective-permute-start.9 = (bf16[64,4096]{1,0:T(8,128)(2,1)S(1)}, bf16[64,4096]{1,0:T(8,128)(2,1)S(1)}, u32[]{:S(2)}, u32[]{:S(2)}) collective-permute-start(bf16[64,4096]{1,0:T(8,128)(2,1)S(1)} %collective-permute-done.2.refs_1_), channel_id=1, source_target_pairs={{0,2},{1,3},{2,0},{3,1},{4,6},{5,7},{6,4},{7,5},{8,10},{9,11},{10,... | collective-permute-start | bytes 1572872 | tf_op jit(solution)/shard_map/ppermute | solution.py:333
  33.1 1.9 %collective-permute-start.5 = (bf16[256,640]{1,0:T(8,128)(2,1)S(1)}, bf16[256,640]{1,0:T(8,128)(2,1)S(1)}, u32[]{:S(2)}, u32[]{:S(2)}) collective-permute-start(bf16[256,640]{1,0:T(8,128)(2,1)S(1)} %constant_dynamic-update-slice_fusion), channel_id=1, source_target_pairs={{1,5},{3,7},{5,9},{7,11},{9,13},{11,15},{17,21},{19,23},{21,25},{2... | collective-permute-start | bytes 983048 | tf_op jit(solution)/shard_map/ppermute | solution.py:342
  33.8 10.4 %collective-permute-start.10 = (bf16[128,1536]{1,0:T(8,128)(2,1)S(1)}, bf16[128,1536]{1,0:T(8,128)(2,1)S(1)}, u32[]{:S(2)}, u32[]{:S(2)}) collective-permute-start(bf16[128,1536]{1,0:T(8,128)(2,1)S(1)} %get-tuple-element.73), channel_id=1, source_target_pairs={{0,17},{1,16},{2,19},{3,18},{4,21},{5,20},{6,23},{7,22},{8,25},{9,... | collective-permute-start | bytes 1179656 | tf_op jit(solution)/shard_map/ppermute | solution.py:327
  34.9 9.2 %collective-permute-start.11 = (bf16[128,1536]{1,0:T(8,128)(2,1)S(1)}, bf16[128,1536]{1,0:T(8,128)(2,1)S(1)}, u32[]{:S(2)}, u32[]{:S(2)}) collective-permute-start(bf16[128,1536]{1,0:T(8,128)(2,1)S(1)} %get-tuple-element.75), channel_id=1, source_target_pairs={{0,1},{1,0},{2,3},{3,2},{4,5},{5,4},{6,7},{7,6},{8,9},{9,8},{10,11... | collective-permute-start | bytes 1179656 | tf_op jit(solution)/shard_map/ppermute | solution.py:327
  45.5 18.4 %collective-permute-start.12 = (bf16[768,640]{1,0:T(8,128)(2,1)S(1)}, bf16[768,640]{1,0:T(8,128)(2,1)S(1)}, u32[]{:S(2)}, u32[]{:S(2)}) collective-permute-start(bf16[768,640]{1,0:T(8,128)(2,1)S(1)} %constant_dynamic-update-slice_fusion.2.own), channel_id=1, source_target_pairs={{0,1},{1,0},{2,3},{3,2},{4,5},{5,4},{6,7},{7,6},{8,9},{9,8},{10,11... | collective-permute-start | bytes 2949128 | tf_op jit(solution)/shard_map/ppermute | solution.py:327
  46.9 15.7 %collective-permute-start.13 = (bf16[64,4096]{1,0:T(8,128)(2,1)S(1)}, bf16[64,4096]{1,0:T(8,128)(2,1)S(1)}, u32[]{:S(2)}, u32[]{:S(2)}) collective-permute-start(bf16[64,4096]{1,0:T(8,128)(2,1)S(1)} %collective-permute-done.8.refs_2_), channel_id=1, source_target_pairs={{0,4},{1,5},{2,6},{3,7},{4,8},{5,9},{6,10},{7,11},{8,12},{9,13},{1... | collective-permute-start | bytes 1572872 | tf_op jit(solution)/shard_map/ppermute | solution.py:330
  49.1 14.8 %collective-permute-start.14 = (bf16[64,4096]{1,0:T(8,128)(2,1)S(1)}, bf16[64,4096]{1,0:T(8,128)(2,1)S(1)}, u32[]{:S(2)}, u32[]{:S(2)}) collective-permute-start(bf16[64,4096]{1,0:T(8,128)(2,1)S(1)} %collective-permute-done.8.refs_2_), channel_id=1, source_target_pairs={{0,2},{1,3},{2,0},{3,1},{4,6},{5,7},{6,4},{7,5},{8,10},{9,11},{10,... | collective-permute-start | bytes 1572872 | tf_op jit(solution)/shard_map/ppermute | solution.py:333
  49.1 13.5 %collective-permute-start.15 = (bf16[128,1536]{1,0:T(8,128)(2,1)S(1)}, bf16[128,1536]{1,0:T(8,128)(2,1)S(1)}, u32[]{:S(2)}, u32[]{:S(2)}) collective-permute-start(bf16[128,1536]{1,0:T(8,128)(2,1)S(1)} %get-tuple-element.83), channel_id=1, source_target_pairs={{0,16},{1,17},{2,18},{3,19},{4,20},{5,21},{6,22},{7,23},{8,24},{9,... | collective-permute-start | bytes 1179656 | tf_op jit(solution)/shard_map/ppermute | solution.py:327
  49.6 17.8 %collective-permute-start.18 = (bf16[2,4,16,576]{3,2,0,1:T(8,128)(2,1)S(1)}, bf16[2,4,16,576]{3,2,0,1:T(8,128)(2,1)S(1)}, u32[]{:S(2)}, u32[]{:S(2)}) collective-permute-start(bf16[2,4,16,576]{3,2,0,1:T(8,128)(2,1)S(1)} %fusion.2), channel_id=1, source_target_pairs={{0,2},{1,3},{2,0},{3,1},{4,6},{5,7},{6,4},{7,5},{8,10},{9,11},{10,... | collective-permute-start | bytes 442376 | tf_op jit(solution)/shard_map/ppermute | solution.py:336
  63.9 7.9 %collective-permute-start.16 = (bf16[64,2048]{1,0:T(8,128)(2,1)S(1)}, bf16[64,2048]{1,0:T(8,128)(2,1)S(1)}, u32[]{:S(2)}, u32[]{:S(2)}) collective-permute-start(bf16[64,2048]{1,0:T(8,128)(2,1)S(1)} %slice.41), channel_id=1, source_target_pairs={{0,2},{1,3},{2,0},{3,1},{4,6},{5,7},{6,4},{7,5},{8,10},{9,11},{10,... | collective-permute-start | bytes 786440 | tf_op jit(solution)/shard_map/ppermute | solution.py:333
  67.5 13.3 %collective-permute-start.17 = (bf16[64,2048]{1,0:T(8,128)(2,1)S(1)}, bf16[64,2048]{1,0:T(8,128)(2,1)S(1)}, u32[]{:S(2)}, u32[]{:S(2)}) collective-permute-start(bf16[64,2048]{1,0:T(8,128)(2,1)S(1)} %slice.42), channel_id=1, source_target_pairs={{0,4},{1,5},{2,6},{3,7},{4,8},{5,9},{6,10},{7,11},{8,12},{9,13},{1... | collective-permute-start | bytes 786440 | tf_op jit(solution)/shard_map/ppermute | solution.py:330
  69.3 13.6 %collective-permute-start.19 = (bf16[128,1536]{1,0:T(8,128)(2,1)S(1)}, bf16[128,1536]{1,0:T(8,128)(2,1)S(1)}, u32[]{:S(2)}, u32[]{:S(2)}) collective-permute-start(bf16[128,1536]{1,0:T(8,128)(2,1)S(1)} %get-tuple-element.93), channel_id=1, source_target_pairs={{0,1},{1,0},{2,3},{3,2},{4,5},{5,4},{6,7},{7,6},{8,9},{9,8},{10,11... | collective-permute-start | bytes 1179656 | tf_op jit(solution)/shard_map/ppermute | solution.py:327
  69.3 15.2 %collective-permute-start.20 = (bf16[128,1536]{1,0:T(8,128)(2,1)S(1)}, bf16[128,1536]{1,0:T(8,128)(2,1)S(1)}, u32[]{:S(2)}, u32[]{:S(2)}) collective-permute-start(bf16[128,1536]{1,0:T(8,128)(2,1)S(1)} %get-tuple-element.96), channel_id=1, source_target_pairs={{0,17},{1,16},{2,19},{3,18},{4,21},{5,20},{6,23},{7,22},{8,25},{9,... | collective-permute-start | bytes 1179656 | tf_op jit(solution)/shard_map/ppermute | solution.py:327
  80.8 8.9 %collective-permute-start.21 = (bf16[4,2,16,576]{3,2,0,1:T(8,128)(2,1)S(1)}, bf16[4,2,16,576]{3,2,0,1:T(8,128)(2,1)S(1)}, u32[]{:S(2)}, u32[]{:S(2)}) collective-permute-start(bf16[4,2,16,576]{3,2,0,1:T(8,128)(2,1)S(1)} %get-tuple-element.99), channel_id=1, source_target_pairs={{0,4},{1,5},{2,6},{3,7},{4,0},{5,1},{6,2},{7,3},{8,12},{9,13},{10,... | collective-permute-start | bytes 442376 | tf_op jit(solution)/shard_map/ppermute | solution.py:336
  82.4 9.2 %collective-permute-start.22 = (bf16[128,1024]{1,0:T(8,128)(2,1)S(1)}, bf16[128,1024]{1,0:T(8,128)(2,1)S(1)}, u32[]{:S(2)}, u32[]{:S(2)}) collective-permute-start(bf16[128,1024]{1,0:T(8,128)(2,1)S(1)} %get-tuple-element.101), channel_id=1, source_target_pairs={{0,16},{1,17},{2,18},{3,19},{4,20},{5,21},{6,22},{7,23},{8,24},{9,... | collective-permute-start | bytes 786440 | tf_op jit(solution)/shard_map/ppermute | solution.py:327
  83.0 17.0 %collective-permute-start.24 = (bf16[128,1024]{1,0:T(8,128)(2,1)S(1)}, bf16[128,1024]{1,0:T(8,128)(2,1)S(1)}, u32[]{:S(2)}, u32[]{:S(2)}) collective-permute-start(bf16[128,1024]{1,0:T(8,128)(2,1)S(1)} %get-tuple-element.107), channel_id=1, source_target_pairs={{0,1},{1,0},{2,3},{3,2},{4,5},{5,4},{6,7},{7,6},{8,9},{9,8},{10,11... | collective-permute-start | bytes 786440 | tf_op jit(solution)/shard_map/ppermute | solution.py:327
  83.0 20.5 %collective-permute-start.30 = (bf16[128,1024]{1,0:T(8,128)(2,1)S(1)}, bf16[128,1024]{1,0:T(8,128)(2,1)S(1)}, u32[]{:S(2)}, u32[]{:S(2)}) collective-permute-start(bf16[128,1024]{1,0:T(8,128)(2,1)S(1)} %get-tuple-element.114), channel_id=1, source_target_pairs={{0,17},{1,16},{2,19},{3,18},{4,21},{5,20},{6,23},{7,22},{8,25},{9,... | collective-permute-start | bytes 786440 | tf_op jit(solution)/shard_map/ppermute | solution.py:327
  89.1 9.9 %collective-permute-start.26 = (bf16[128,512]{1,0:T(8,128)(2,1)S(1)}, bf16[128,512]{1,0:T(8,128)(2,1)S(1)}, u32[]{:S(2)}, u32[]{:S(2)}) collective-permute-start(bf16[128,512]{1,0:T(8,128)(2,1)S(1)} %get-tuple-element.110), channel_id=1, source_target_pairs={{0,16},{1,17},{2,18},{3,19},{4,20},{5,21},{6,22},{7,23},{8,24},{9,... | collective-permute-start | bytes 393224 | tf_op jit(solution)/shard_map/ppermute | solution.py:327
  89.7 9.3 %collective-permute-start.27 = (bf16[128,512]{1,0:T(8,128)(2,1)S(1)}, bf16[128,512]{1,0:T(8,128)(2,1)S(1)}, u32[]{:S(2)}, u32[]{:S(2)}) collective-permute-start(bf16[128,512]{1,0:T(8,128)(2,1)S(1)} %get-tuple-element.111), channel_id=1, source_target_pairs={{0,17},{1,16},{2,19},{3,18},{4,21},{5,20},{6,23},{7,22},{8,25},{9,... | collective-permute-start | bytes 393224 | tf_op jit(solution)/shard_map/ppermute | solution.py:327
  91.7 10.2 %collective-permute-start.23 = (bf16[8,1,16,576]{3,2,0,1:T(8,128)(2,1)S(1)}, bf16[8,1,16,576]{3,2,0,1:T(8,128)(2,1)S(1)}, u32[]{:S(2)}, u32[]{:S(2)}) collective-permute-start(bf16[8,1,16,576]{3,2,0,1:T(8,128)(2,1)S(1)} %get-tuple-element.105), channel_id=1, source_target_pairs={{0,8},{1,9},{2,10},{3,11},{4,12},{5,13},{6,14},{7,15},{8,0},{9,1},... | collective-permute-start | bytes 442376 | tf_op jit(solution)/shard_map/ppermute | solution.py:336
  99.0 4.5 %collective-permute-start.25 = (bf16[128,512]{1,0:T(8,128)(2,1)S(1)}, bf16[128,512]{1,0:T(8,128)(2,1)S(1)}, u32[]{:S(2)}, u32[]{:S(2)}) collective-permute-start(bf16[128,512]{1,0:T(8,128)(2,1)S(1)} %get-tuple-element.108), channel_id=1, source_target_pairs={{0,1},{1,0},{2,3},{3,2},{4,5},{5,4},{6,7},{7,6},{8,9},{9,8},{10,11... | collective-permute-start | bytes 393224 | tf_op jit(solution)/shard_map/ppermute | solution.py:327
  99.0 5.9 %collective-permute-start.29 = (bf16[128,512]{1,0:T(8,128)(2,1)S(1)}, bf16[128,512]{1,0:T(8,128)(2,1)S(1)}, u32[]{:S(2)}, u32[]{:S(2)}) collective-permute-start(bf16[128,512]{1,0:T(8,128)(2,1)S(1)} %get-tuple-element.113), channel_id=1, source_target_pairs={{0,16},{1,17},{2,18},{3,19},{4,20},{5,21},{6,22},{7,23},{8,24},{9,... | collective-permute-start | bytes 393224 | tf_op jit(solution)/shard_map/ppermute | solution.py:327
  99.9 8.2 %collective-permute-start.31 = (bf16[128,512]{1,0:T(8,128)(2,1)S(1)}, bf16[128,512]{1,0:T(8,128)(2,1)S(1)}, u32[]{:S(2)}, u32[]{:S(2)}) collective-permute-start(bf16[128,512]{1,0:T(8,128)(2,1)S(1)} %get-tuple-element.115), channel_id=1, source_target_pairs={{0,17},{1,16},{2,19},{3,18},{4,21},{5,20},{6,23},{7,22},{8,25},{9,... | collective-permute-start | bytes 393224 | tf_op jit(solution)/shard_map/ppermute | solution.py:327
  101.9 6.3 %collective-permute-start.28 = (bf16[128,512]{1,0:T(8,128)(2,1)S(1)}, bf16[128,512]{1,0:T(8,128)(2,1)S(1)}, u32[]{:S(2)}, u32[]{:S(2)}) collective-permute-start(bf16[128,512]{1,0:T(8,128)(2,1)S(1)} %get-tuple-element.112), channel_id=1, source_target_pairs={{0,1},{1,0},{2,3},{3,2},{4,5},{5,4},{6,7},{7,6},{8,9},{9,8},{10,11... | collective-permute-start | bytes 393224 | tf_op jit(solution)/shard_map/ppermute | solution.py:327

commit v19 on v14

--- a/solution.py
+++ b/solution.py
@@ -29,7 +29,7 @@
 ROW = LAT + ROPE
 EXT = 640
 VMEM_LIMIT = 20 * 1024 * 1024
-CALLS = ((0, 0, 4), (1, 0, 2), (1, 2, 2))
+CALLS = ((0, 0, 4), (1, 0, 3), (1, 3, 1))
 SMEM = pltpu.SMEM
 VMEM = pltpu.VMEM
 

time: 104 us -> 105 us (level)
    ppermute x4, waiting for transfers between devices: 3.01 us -> 4.26 us  [pair_swap(): return lax.ppermute(array, 'ctx', [(i, i ^ distance) for i in range(size)])]
  transfers between devices with their start and end apart: 32 -> 32, of which waited for: 15 -> 14; matrix products, arithmetic and copies ran while one was open for 1% -> 1% of each run, Pallas kernels for 24% -> 24%
where the time goes in v19:
time: 105 us
  waiting for transfers between devices  40.6 us (39%)
  starting transfers between devices  33.7 us (32%)
  Pallas kernels  27 us (26%)
  local copies, waits for them, and re-layouts  2.1 us (2%)
    ppermute x18, waiting for transfers between devices, quad_swap(): return lax.ppermute(array, ('groups', 'ctx'), pairs)  32.4 us
    pallas_call x3, Pallas kernels, attend(): pl.pallas_call(functools.partial(attend_kernel, outer), grid=(steps,), ou...  17.8 us
    ppermute x18, starting transfers between devices, quad_swap(): return lax.ppermute(array, ('groups', 'ctx'), pairs)  13.2 us
    ppermute x4, starting transfers between devices, around(): lax.ppermute(array, 'ctx', [(i, (i + by) % size) for i in range(size)])  8.34 us
    ppermute x4, starting transfers between devices, pair_swap(): return lax.ppermute(array, 'ctx', [(i, i ^ distance) for i in range(size)])  5.01 us
    ppermute x4, waiting for transfers between devices, pair_swap(): return lax.ppermute(array, 'ctx', [(i, i ^ distance) for i in range(size)])  4.26 us
    ppermute x4, starting transfers between devices, inner_swap(): return lax.ppermute(array, 'ctx', [(i, i ^ 2) for i in range(size)])  4.01 us
    pallas_call x1, Pallas kernels, body(): pl.pallas_call(query_kernel, out_shape=[shape((tok, h * (NOPE + ROPE))) f...  3.38 us
  transfers between devices with their start and end apart: 32, of which 14 were waited for; matrix products, arithmetic and copies ran while one was open for 1% of the time, Pallas kernels for 24%

profile of v19, /device:TPU:0, one launch (start us, length us, event | category | flops | bytes accessed | tf_op | source)
XLA Modules:
  0.0 104.6 jit_solution(5395777350641359531)
XLA Ops:
  0.6 1.0 constant_dynamic-slice_fusion
  1.6 0.5 collective-permute-start
  2.1 1.2 %collective-permute-done.got = bf16[32,4096]{1,0:T(8,128)(2,1)S(1)} collective-permute-done((bf16[32,4096]{1,0:T(8,128)(2,1)S(1)}, bf16[32,4096]{1,0:T(8,128)(2,1)S(1)}, u32[]{:S(2)}, u32[]{:S(2)}) %collective-permute-start) | collective-permute-done | bytes 262176 | tf_op jit(solution)/shard_map/ppermute | solution.py:327
  3.3 1.0 pair.1.refs_0_
  4.3 3.0 %collective-permute-start.1 = (bf16[64,4096]{1,0:T(8,128)(2,1)S(1)}, bf16[64,4096]{1,0:T(8,128)(2,1)S(1)}, u32[]{:S(2)}, u32[]{:S(2)}) collective-permute-start(bf16[64,4096]{1,0:T(8,128)(2,1)S(1)} %pair.1.refs_0_), channel_id=1, source_target_pairs={{0,4},{1,5},{2,6},{3,7},{4,8},{5,9},{6,10},{7,11},{8,12},{9,13},{1... | collective-permute-start | bytes 1572872 | tf_op jit(solution)/shard_map/ppermute | solution.py:330
  7.3 1.5 %collective-permute-start.2 = (bf16[64,4096]{1,0:T(8,128)(2,1)S(1)}, bf16[64,4096]{1,0:T(8,128)(2,1)S(1)}, u32[]{:S(2)}, u32[]{:S(2)}) collective-permute-start(bf16[64,4096]{1,0:T(8,128)(2,1)S(1)} %pair.1.refs_0_), channel_id=1, source_target_pairs={{0,2},{1,3},{2,0},{3,1},{4,6},{5,7},{6,4},{7,5},{8,10},{9,11},{10,... | collective-permute-start | bytes 1572872 | tf_op jit(solution)/shard_map/ppermute | solution.py:333
  8.8 2.3 %rows.1 = (bf16[128,640]{1,0:T(8,128)(2,1)}, f32[128,128]{1,0:T(8,128)}, f32[128,128]{1,0:T(8,128)}, bf16[256,576]{1,0:T(8,128)(2,1)}) custom-call(s32[1]{0:T(128)} %bitcast.1.info, s32[8]{0:T(128)} %lengths, bf16[576,128]{1,0:T(8,128)(2,1)} %bitcast.9, f32[1,512]{1,0:T(1,128)} %bitcast.10, s32[1,128]{1,0:T(1,128)} %bitcast.11, f32[1,128]{1,0:T(1,128)} %constant.30.clone.freq), custom_call_target="tpu_custom_call" | custom-call | tf_op jit(solution)/shard_map/rows/pallas_call | solution.py:377
  11.1 1.5 %collective-permute-start.3 = (bf16[128,640]{1,0:T(8,128)(2,1)}, bf16[128,640]{1,0:T(8,128)(2,1)S(1)}, u32[]{:S(2)}, u32[]{:S(2)}) collective-permute-start(bf16[128,640]{1,0:T(8,128)(2,1)} %get-tuple-element.60), channel_id=1, source_target_pairs={{0,16},{1,17},{2,18},{3,19},{4,20},{5,21},{6,22},{7,23},{8,24},{9,... | collective-permute-start | bytes 491528 | tf_op jit(solution)/shard_map/ppermute | solution.py:327
  12.6 3.4 %queries.1 = (bf16[128,1536]{1,0:T(8,128)(2,1)S(1)}, bf16[128,1536]{1,0:T(8,128)(2,1)S(1)}, bf16[128,1536]{1,0:T(8,128)(2,1)S(1)}, bf16[128,1536]{1,0:T(8,128)(2...) custom-call(s32[1]{0:T(128)} %bitcast.info, ...), custom_call_target="tpu_custom_call" | custom-call | bytes 6291456 | tf_op jit(solution)/shard_map/queries/pallas_call | solution.py:401
  16.0 0.6 collective-permute-start.4
  16.6 0.4 collective-permute-done.3
  17.0 2.4 %collective-permute-start.6 = (bf16[256,640]{1,0:T(8,128)(2,1)S(1)}, bf16[256,640]{1,0:T(8,128)(2,1)S(1)}, u32[]{:S(2)}, u32[]{:S(2)}) collective-permute-start(bf16[256,640]{1,0:T(8,128)(2,1)S(1)} %get-tuple-element.118), channel_id=1, source_target_pairs={{0,2},{1,3},{2,4},{3,5},{4,6},{5,7},{6,8},{7,9},{8,10},{9,11},{10,... | collective-permute-start | bytes 983048 | tf_op jit(solution)/shard_map/ppermute | solution.py:342
  19.5 6.9 %collective-permute-done.4.refs_10_.refs_14_ = bf16[128,1536]{1,0:T(8,128)(2,1)S(1)} collective-permute-done((bf16[128,1536]{1,0:T(8,128)(2,1)S(1)}, bf16[128,1536]{1,0:T(8,128)(2,1)S(1)}, u32[]{:S(2)}, u32[]{:S(2)}) %collective-permute-start.4) | collective-permute-done | bytes 393248 | tf_op jit(solution)/shard_map/ppermute | solution.py:327
  26.4 0.0 collective-permute-done.1.refs_1_
  26.4 1.6 %collective-permute-start.8 = (bf16[64,4096]{1,0:T(8,128)(2,1)S(1)}, bf16[64,4096]{1,0:T(8,128)(2,1)S(1)}, u32[]{:S(2)}, u32[]{:S(2)}) collective-permute-start(bf16[64,4096]{1,0:T(8,128)(2,1)S(1)} %collective-permute-done.1.refs_1_), channel_id=1, source_target_pairs={{0,4},{1,5},{2,6},{3,7},{4,8},{5,9},{6,10},{7,11},{8,12},{9,13},{1... | collective-permute-start | bytes 1572872 | tf_op jit(solution)/shard_map/ppermute | solution.py:330
  28.0 0.5 collective-permute-start.9
  28.5 0.7 collective-permute-start.7
  29.1 0.6 collective-permute-start.10
  29.7 0.0 collective-permute-done.6
  29.7 0.2 collective-permute-start.11
  30.0 10.2 %collective-permute-done.10.refs_11_.refs_15_ = bf16[128,1536]{1,0:T(8,128)(2,1)S(1)} collective-permute-done((bf16[128,1536]{1,0:T(8,128)(2,1)S(1)}, bf16[128,1536]{1,0:T(8,128)(2,1)S(1)}, u32[]{:S(2)}, u32[]{:S(2)}) %collective-permute-start.10) | collective-permute-done | bytes 393248 | tf_op jit(solution)/shard_map/ppermute | solution.py:327
  40.2 0.0 collective-permute-done.11.refs_9_.refs_13_
  40.2 0.2 collective-permute-done.8.refs_2_
  40.4 1.1 %collective-permute-start.12 = (bf16[768,640]{1,0:T(8,128)(2,1)S(1)}, bf16[768,640]{1,0:T(8,128)(2,1)S(1)}, u32[]{:S(2)}, u32[]{:S(2)}) collective-permute-start(bf16[768,640]{1,0:T(8,128)(2,1)S(1)} %constant_dynamic-update-slice_fusion.2.own), channel_id=1, source_target_pairs={{0,1},{1,0},{2,3},{3,2},{4,5},{5,4},{6,7},{7,6},{8,9},{9,8},{10,11... | collective-permute-start | bytes 2949128 | tf_op jit(solution)/shard_map/ppermute | solution.py:327
  41.4 2.2 %collective-permute-start.13 = (bf16[64,4096]{1,0:T(8,128)(2,1)S(1)}, bf16[64,4096]{1,0:T(8,128)(2,1)S(1)}, u32[]{:S(2)}, u32[]{:S(2)}) collective-permute-start(bf16[64,4096]{1,0:T(8,128)(2,1)S(1)} %collective-permute-done.8.refs_2_), channel_id=1, source_target_pairs={{0,4},{1,5},{2,6},{3,7},{4,8},{5,9},{6,10},{7,11},{8,12},{9,13},{1... | collective-permute-start | bytes 1572872 | tf_op jit(solution)/shard_map/ppermute | solution.py:330
  43.6 1.3 %collective-permute-start.14 = (bf16[64,4096]{1,0:T(8,128)(2,1)S(1)}, bf16[64,4096]{1,0:T(8,128)(2,1)S(1)}, u32[]{:S(2)}, u32[]{:S(2)}) collective-permute-start(bf16[64,4096]{1,0:T(8,128)(2,1)S(1)} %collective-permute-done.8.refs_2_), channel_id=1, source_target_pairs={{0,2},{1,3},{2,0},{3,1},{4,6},{5,7},{6,4},{7,5},{8,10},{9,11},{10,... | collective-permute-start | bytes 1572872 | tf_op jit(solution)/shard_map/ppermute | solution.py:333
  45.0 1.5 %collective-permute-start.15 = (bf16[128,1536]{1,0:T(8,128)(2,1)S(1)}, bf16[128,1536]{1,0:T(8,128)(2,1)S(1)}, u32[]{:S(2)}, u32[]{:S(2)}) collective-permute-start(bf16[128,1536]{1,0:T(8,128)(2,1)S(1)} %get-tuple-element.80), channel_id=1, source_target_pairs={{0,16},{1,17},{2,18},{3,19},{4,20},{5,21},{6,22},{7,23},{8,24},{9,... | collective-permute-start | bytes 1179656 | tf_op jit(solution)/shard_map/ppermute | solution.py:327
  46.5 0.1 collective-permute-start.5
  46.6 1.4 %collective-permute-done.5 = bf16[1,8,16,576]{3,2,0,1:T(8,128)(2,1)S(1)} collective-permute-done((bf16[1,8,16,576]{3,2,0,1:T(8,128)(2,1)S(1)}, bf16[1,8,16,576]{3,2,0,1:T(8,128)(2,1)S(1)}, u32[]{:S(2)}, u32[]{:S(2)}) %collective-permute-start.5) | collective-permute-done | bytes 147488 | tf_op jit(solution)/shard_map/ppermute | solution.py:336
  48.0 7.5 %collective-permute-done.15.refs_10_.refs_14_ = bf16[128,1536]{1,0:T(8,128)(2,1)S(1)} collective-permute-done((bf16[128,1536]{1,0:T(8,128)(2,1)S(1)}, bf16[128,1536]{1,0:T(8,128)(2,1)S(1)}, u32[]{:S(2)}, u32[]{:S(2)}) %collective-permute-start.15) | collective-permute-done | bytes 393248 | tf_op jit(solution)/shard_map/ppermute | solution.py:327
  55.5 1.6 %collective-permute-done.13.refs_3_ = bf16[64,4096]{1,0:T(8,128)(2,1)S(1)} collective-permute-done((bf16[64,4096]{1,0:T(8,128)(2,1)S(1)}, bf16[64,4096]{1,0:T(8,128)(2,1)S(1)}, u32[]{:S(2)}, u32[]{:S(2)}) %collective-permute-start.13) | collective-permute-done | bytes 524320 | tf_op jit(solution)/shard_map/ppermute | solution.py:330
  57.1 0.1 collective-permute-done.14.refs_6_
  57.2 0.0 collective-permute-done.12.other
  57.3 1.4 %collective-permute-start.17 = (bf16[2,4,16,576]{3,2,0,1:T(8,128)(2,1)S(1)}, bf16[2,4,16,576]{3,2,0,1:T(8,128)(2,1)S(1)}, u32[]{:S(2)}, u32[]{:S(2)}) collective-permute-start(bf16[2,4,16,576]{3,2,0,1:T(8,128)(2,1)S(1)} %fusion.2), channel_id=1, source_target_pairs={{0,2},{1,3},{2,0},{3,1},{4,6},{5,7},{6,4},{7,5},{8,10},{9,11},{10,... | collective-permute-start | bytes 442376 | tf_op jit(solution)/shard_map/ppermute | solution.py:336
  58.7 0.7 collective-permute-start.16
  59.4 1.6 %collective-permute-start.18 = (bf16[64,2048]{1,0:T(8,128)(2,1)S(1)}, bf16[64,2048]{1,0:T(8,128)(2,1)S(1)}, u32[]{:S(2)}, u32[]{:S(2)}) collective-permute-start(bf16[64,2048]{1,0:T(8,128)(2,1)S(1)} %slice.45), channel_id=1, source_target_pairs={{0,4},{1,5},{2,6},{3,7},{4,8},{5,9},{6,10},{7,11},{8,12},{9,13},{1... | collective-permute-start | bytes 786440 | tf_op jit(solution)/shard_map/ppermute | solution.py:330
  61.0 0.0 collective-permute-start.19
  61.0 1.2 %collective-permute-start.20 = (bf16[128,1536]{1,0:T(8,128)(2,1)S(1)}, bf16[128,1536]{1,0:T(8,128)(2,1)S(1)}, u32[]{:S(2)}, u32[]{:S(2)}) collective-permute-start(bf16[128,1536]{1,0:T(8,128)(2,1)S(1)} %get-tuple-element.91), channel_id=1, source_target_pairs={{0,17},{1,16},{2,19},{3,18},{4,21},{5,20},{6,23},{7,22},{8,25},{9,... | collective-permute-start | bytes 1179656 | tf_op jit(solution)/shard_map/ppermute | solution.py:327
  62.2 0.6 keys.1
  62.8 1.6 %collective-permute-done.17 = bf16[2,4,16,576]{3,2,0,1:T(8,128)(2,1)S(1)} collective-permute-done((bf16[2,4,16,576]{3,2,0,1:T(8,128)(2,1)S(1)}, bf16[2,4,16,576]{3,2,0,1:T(8,128)(2,1)S(1)}, u32[]{:S(2)}, u32[]{:S(2)}) %collective-permute-start.17) | collective-permute-done | bytes 147488 | tf_op jit(solution)/shard_map/ppermute | solution.py:336
  64.4 0.1 fusion
  64.5 1.6 %collective-permute-start.21 = (bf16[4,2,16,576]{3,2,0,1:T(8,128)(2,1)S(1)}, bf16[4,2,16,576]{3,2,0,1:T(8,128)(2,1)S(1)}, u32[]{:S(2)}, u32[]{:S(2)}) collective-permute-start(bf16[4,2,16,576]{3,2,0,1:T(8,128)(2,1)S(1)} %get-tuple-element.94), channel_id=1, source_target_pairs={{0,4},{1,5},{2,6},{3,7},{4,0},{5,1},{6,2},{7,3},{8,12},{9,13},{10,... | collective-permute-start | bytes 442376 | tf_op jit(solution)/shard_map/ppermute | solution.py:336
  66.1 2.0 %collective-permute-done.16.refs_7_ = bf16[64,2048]{1,0:T(8,128)(2,1)S(1)} collective-permute-done((bf16[64,2048]{1,0:T(8,128)(2,1)S(1)}, bf16[64,2048]{1,0:T(8,128)(2,1)S(1)}, u32[]{:S(2)}, u32[]{:S(2)}) %collective-permute-start.16) | collective-permute-done | bytes 262176 | tf_op jit(solution)/shard_map/ppermute | solution.py:333
  68.1 9.0 %attend.3 = (bf16[128,1024]{1,0:T(8,128)(2,1)S(1)}, bf16[128,1024]{1,0:T(8,128)(2,1)S(1)}, bf16[128,1024]{1,0:T(8,128)(2,1)S(1)}, bf16[128,1024]{1,0:T(8,128)(2,1)S(1)}) custom-call(s32[1]{0:T(128)} %bitcast.1.info, bf16[2,640,512]{2,1,0:T(8,128)(2,1)S(1)} %get-tuple-element.74.latent, bf16[2,640,128]{2,1,0:T(8,128)(2,1)S(1)} %get-tuple-element.75.rope_even, ...), custom_call_target="tpu_custom_call" | custom-call | flops 4362076160 | bytes 8388608 | tf_op jit(solution)/shard_map/attend/pallas_call | solution.py:483
  77.1 1.5 %collective-permute-start.22 = (bf16[128,1024]{1,0:T(8,128)(2,1)S(1)}, bf16[128,1024]{1,0:T(8,128)(2,1)S(1)}, u32[]{:S(2)}, u32[]{:S(2)}) collective-permute-start(bf16[128,1024]{1,0:T(8,128)(2,1)S(1)} %get-tuple-element.96), channel_id=1, source_target_pairs={{0,16},{1,17},{2,18},{3,19},{4,20},{5,21},{6,22},{7,23},{8,24},{9,... | collective-permute-start | bytes 786440 | tf_op jit(solution)/shard_map/ppermute | solution.py:327
  78.6 0.0 collective-permute-done.18.refs_7_
  78.6 0.0 collective-permute-done.19.refs_9_.refs_13_
  78.6 0.0 collective-permute-done.20.refs_11_.refs_15_
  78.6 6.8 %attend.4 = (bf16[128,768]{1,0:T(8,128)(2,1)S(1)}, bf16[128,768]{1,0:T(8,128)(2,1)S(1)}, bf16[128,768]{1,0:T(8,128)(2,1)S(1)}, bf16[128,768]{1,0:T(8,128)(2,1)S(1)}) custom-call(s32[1]{0:T(128)} %bitcast.1.info, bf16[2,640,512]{2,1,0:T(8,128)(2,1)S(1)} %get-tuple-element.74.latent, bf16[2,640,128]{2,1,0:T(8,128)(2,1)S(1)} %get-tuple-element.75.rope_even, ...), custom_call_target="tpu_custom_call" | custom-call | flops 3271557120 | bytes 6291456 | tf_op jit(solution)/shard_map/attend/pallas_call | solution.py:483
  85.4 0.6 collective-permute-start.25
  86.0 0.0 collective-permute-start.23
  86.0 1.6 %collective-permute-start.26 = (bf16[128,768]{1,0:T(8,128)(2,1)S(1)}, bf16[128,768]{1,0:T(8,128)(2,1)S(1)}, u32[]{:S(2)}, u32[]{:S(2)}) collective-permute-start(bf16[128,768]{1,0:T(8,128)(2,1)S(1)} %get-tuple-element.103), channel_id=1, source_target_pairs={{0,17},{1,16},{2,19},{3,18},{4,21},{5,20},{6,23},{7,22},{8,25},{9,... | collective-permute-start | bytes 589832 | tf_op jit(solution)/shard_map/ppermute | solution.py:327
  87.6 0.1 fusion.1
  87.7 1.9 %collective-permute-start.31 = (bf16[8,1,16,576]{3,2,0,1:T(8,128)(2,1)S(1)}, bf16[8,1,16,576]{3,2,0,1:T(8,128)(2,1)S(1)}, u32[]{:S(2)}, u32[]{:S(2)}) collective-permute-start(bf16[8,1,16,576]{3,2,0,1:T(8,128)(2,1)S(1)} %get-tuple-element.109), channel_id=1, source_target_pairs={{0,8},{1,9},{2,10},{3,11},{4,12},{5,13},{6,14},{7,15},{8,0},{9,1},... | collective-permute-start | bytes 442376 | tf_op jit(solution)/shard_map/ppermute | solution.py:336
  89.5 0.0 collective-permute-start.29
  89.5 3.7 %collective-permute-done.25.refs_7_ = bf16[128,768]{1,0:T(8,128)(2,1)S(1)} collective-permute-done((bf16[128,768]{1,0:T(8,128)(2,1)S(1)}, bf16[128,768]{1,0:T(8,128)(2,1)S(1)}, u32[]{:S(2)}, u32[]{:S(2)}) %collective-permute-start.25) | collective-permute-done | bytes 196640 | tf_op jit(solution)/shard_map/ppermute | solution.py:327
  93.3 2.1 %attend.5 = (bf16[128,256]{1,0:T(8,128)(2,1)S(1)}, bf16[128,256]{1,0:T(8,128)(2,1)S(1)}, bf16[128,256]{1,0:T(8,128)(2,1)S(1)}, bf16[128,256]{1,0:T(8,128)(2,1)S(1)}) custom-call(s32[1]{0:T(128)} %bitcast.1.info, bf16[2,640,512]{2,1,0:T(8,128)(2,1)S(1)} %get-tuple-element.74.latent, bf16[2,640,128]{2,1,0:T(8,128)(2,1)S(1)} %get-tuple-element.75.rope_even, ...), custom_call_target="tpu_custom_call" | custom-call | flops 1090519040 | bytes 2097152 | tf_op jit(solution)/shard_map/attend/pallas_call | solution.py:483
  95.3 1.7 %collective-permute-start.28 = (bf16[128,256]{1,0:T(8,128)(2,1)S(1)}, bf16[128,256]{1,0:T(8,128)(2,1)S(1)}, u32[]{:S(2)}, u32[]{:S(2)}) collective-permute-start(bf16[128,256]{1,0:T(8,128)(2,1)S(1)} %get-tuple-element.105), channel_id=1, source_target_pairs={{0,16},{1,17},{2,18},{3,19},{4,20},{5,21},{6,22},{7,23},{8,24},{9,... | collective-permute-start | bytes 196616 | tf_op jit(solution)/shard_map/ppermute | solution.py:327
  97.0 1.3 %collective-permute-done.31 = bf16[8,1,16,576]{3,2,0,1:T(8,128)(2,1)S(1)} collective-permute-done((bf16[8,1,16,576]{3,2,0,1:T(8,128)(2,1)S(1)}, bf16[8,1,16,576]{3,2,0,1:T(8,128)(2,1)S(1)}, u32[]{:S(2)}, u32[]{:S(2)}) %collective-permute-start.31) | collective-permute-done | bytes 147488 | tf_op jit(solution)/shard_map/ppermute | solution.py:336
  98.3 0.7 collective-permute-start.30
  99.0 0.6 sort.1
  99.6 0.9 copy.9
  100.5 2.5 %collective-permute-done.28.refs_8_ = bf16[128,256]{1,0:T(8,128)(2,1)S(1)} collective-permute-done((bf16[128,256]{1,0:T(8,128)(2,1)S(1)}, bf16[128,256]{1,0:T(8,128)(2,1)S(1)}, u32[]{:S(2)}, u32[]{:S(2)}) %collective-permute-start.28) | collective-permute-done | bytes 65568 | tf_op jit(solution)/shard_map/ppermute | solution.py:327
  103.1 1.4 %place.1 = bf16[128,8192]{1,0:T(8,128)(2,1)} custom-call(s32[1]{0:T(128)} %bitcast.info, bf16[128,1024]{1,0:T(8,128)(2,1)S(1)} %get-tuple-element.82.refs_0_, bf16[128,768]{1,0:T(8,128)(2,1)S(1)} %get-tuple-element.92.refs_1_, bf16[128,256]{1,0:T(8,128)(2,1)S(1)} %get-tuple-element.98.refs_2_, bf16[128,1024]{1,0:T(8,128)(2,1)S(1)} %collective-permute-done.23.refs_3_, ...), custom_call_target="tpu_custom_call" | custom-call | tf_op jit(solution)/shard_map/place/pallas_call | solution.py:532
  (27 shorter events, 0.4 us)
Async XLA Ops:
  1.6 1.7 %collective-permute-start = (bf16[32,4096]{1,0:T(8,128)(2,1)S(1)}, bf16[32,4096]{1,0:T(8,128)(2,1)S(1)}, u32[]{:S(2)}, u32[]{:S(2)}) collective-permute-start(bf16[32,4096]{1,0:T(8,128)(2,1)S(1)} %constant_dynamic-slice_fusion), channel_id=1, source_target_pairs={{0,1},{1,0},{2,3},{3,2},{4,5},{5,4},{6,7},{7,6},{8,9},{9,8},{10,11... | collective-permute-start | bytes 786440 | tf_op jit(solution)/shard_map/ppermute | solution.py:327
  4.3 22.1 %collective-permute-start.1 = (bf16[64,4096]{1,0:T(8,128)(2,1)S(1)}, bf16[64,4096]{1,0:T(8,128)(2,1)S(1)}, u32[]{:S(2)}, u32[]{:S(2)}) collective-permute-start(bf16[64,4096]{1,0:T(8,128)(2,1)S(1)} %pair.1.refs_0_), channel_id=1, source_target_pairs={{0,4},{1,5},{2,6},{3,7},{4,8},{5,9},{6,10},{7,11},{8,12},{9,13},{1... | collective-permute-start | bytes 1572872 | tf_op jit(solution)/shard_map/ppermute | solution.py:330
  7.3 19.1 %collective-permute-start.2 = (bf16[64,4096]{1,0:T(8,128)(2,1)S(1)}, bf16[64,4096]{1,0:T(8,128)(2,1)S(1)}, u32[]{:S(2)}, u32[]{:S(2)}) collective-permute-start(bf16[64,4096]{1,0:T(8,128)(2,1)S(1)} %pair.1.refs_0_), channel_id=1, source_target_pairs={{0,2},{1,3},{2,0},{3,1},{4,6},{5,7},{6,4},{7,5},{8,10},{9,11},{10,... | collective-permute-start | bytes 1572872 | tf_op jit(solution)/shard_map/ppermute | solution.py:333
  11.1 5.5 %copy-start.1 = (bf16[128,640]{1,0:T(8,128)(2,1)S(1)}, bf16[128,640]{1,0:T(8,128)(2,1)}, u32[]{:S(2)}) copy-start(bf16[128,640]{1,0:T(8,128)(2,1)} %get-tuple-element.60) | copy-start | bytes 491524
  11.1 5.9 %collective-permute-start.3 = (bf16[128,640]{1,0:T(8,128)(2,1)}, bf16[128,640]{1,0:T(8,128)(2,1)S(1)}, u32[]{:S(2)}, u32[]{:S(2)}) collective-permute-start(bf16[128,640]{1,0:T(8,128)(2,1)} %get-tuple-element.60), channel_id=1, source_target_pairs={{0,16},{1,17},{2,18},{3,19},{4,20},{5,21},{6,22},{7,23},{8,24},{9,... | collective-permute-start | bytes 491528 | tf_op jit(solution)/shard_map/ppermute | solution.py:327
  12.6 33.9 %copy-start = (bf16[256,576]{1,0:T(8,128)(2,1)S(1)}, bf16[256,576]{1,0:T(8,128)(2,1)}, u32[]{:S(2)}) copy-start(bf16[256,576]{1,0:T(8,128)(2,1)} %get-tuple-element.57) | copy-start | bytes 884740
  16.0 10.4 %collective-permute-start.4 = (bf16[128,1536]{1,0:T(8,128)(2,1)S(1)}, bf16[128,1536]{1,0:T(8,128)(2,1)S(1)}, u32[]{:S(2)}, u32[]{:S(2)}) collective-permute-start(bf16[128,1536]{1,0:T(8,128)(2,1)S(1)} %get-tuple-element.64), channel_id=1, source_target_pairs={{0,16},{1,17},{2,18},{3,19},{4,20},{5,21},{6,22},{7,23},{8,24},{9,... | collective-permute-start | bytes 1179656 | tf_op jit(solution)/shard_map/ppermute | solution.py:327
  17.0 12.7 %collective-permute-start.6 = (bf16[256,640]{1,0:T(8,128)(2,1)S(1)}, bf16[256,640]{1,0:T(8,128)(2,1)S(1)}, u32[]{:S(2)}, u32[]{:S(2)}) collective-permute-start(bf16[256,640]{1,0:T(8,128)(2,1)S(1)} %get-tuple-element.118), channel_id=1, source_target_pairs={{0,2},{1,3},{2,4},{3,5},{4,6},{5,7},{6,8},{7,9},{8,10},{9,11},{10,... | collective-permute-start | bytes 983048 | tf_op jit(solution)/shard_map/ppermute | solution.py:342
  26.4 14.0 %collective-permute-start.8 = (bf16[64,4096]{1,0:T(8,128)(2,1)S(1)}, bf16[64,4096]{1,0:T(8,128)(2,1)S(1)}, u32[]{:S(2)}, u32[]{:S(2)}) collective-permute-start(bf16[64,4096]{1,0:T(8,128)(2,1)S(1)} %collective-permute-done.1.refs_1_), channel_id=1, source_target_pairs={{0,4},{1,5},{2,6},{3,7},{4,8},{5,9},{6,10},{7,11},{8,12},{9,13},{1... | collective-permute-start | bytes 1572872 | tf_op jit(solution)/shard_map/ppermute | solution.py:330
  28.0 12.4 %collective-permute-start.9 = (bf16[64,4096]{1,0:T(8,128)(2,1)S(1)}, bf16[64,4096]{1,0:T(8,128)(2,1)S(1)}, u32[]{:S(2)}, u32[]{:S(2)}) collective-permute-start(bf16[64,4096]{1,0:T(8,128)(2,1)S(1)} %collective-permute-done.1.refs_1_), channel_id=1, source_target_pairs={{0,2},{1,3},{2,0},{3,1},{4,6},{5,7},{6,4},{7,5},{8,10},{9,11},{10,... | collective-permute-start | bytes 1572872 | tf_op jit(solution)/shard_map/ppermute | solution.py:333
  28.5 1.5 %collective-permute-start.7 = (bf16[256,640]{1,0:T(8,128)(2,1)S(1)}, bf16[256,640]{1,0:T(8,128)(2,1)S(1)}, u32[]{:S(2)}, u32[]{:S(2)}) collective-permute-start(bf16[256,640]{1,0:T(8,128)(2,1)S(1)} %get-tuple-element.118), channel_id=1, source_target_pairs={{1,5},{3,7},{5,9},{7,11},{9,13},{11,15},{17,21},{19,23},{21,25},{2... | collective-permute-start | bytes 983048 | tf_op jit(solution)/shard_map/ppermute | solution.py:342
  29.1 11.0 %collective-permute-start.10 = (bf16[128,1536]{1,0:T(8,128)(2,1)S(1)}, bf16[128,1536]{1,0:T(8,128)(2,1)S(1)}, u32[]{:S(2)}, u32[]{:S(2)}) collective-permute-start(bf16[128,1536]{1,0:T(8,128)(2,1)S(1)} %get-tuple-element.70), channel_id=1, source_target_pairs={{0,17},{1,16},{2,19},{3,18},{4,21},{5,20},{6,23},{7,22},{8,25},{9,... | collective-permute-start | bytes 1179656 | tf_op jit(solution)/shard_map/ppermute | solution.py:327
  29.7 10.4 %collective-permute-start.11 = (bf16[128,1536]{1,0:T(8,128)(2,1)S(1)}, bf16[128,1536]{1,0:T(8,128)(2,1)S(1)}, u32[]{:S(2)}, u32[]{:S(2)}) collective-permute-start(bf16[128,1536]{1,0:T(8,128)(2,1)S(1)} %get-tuple-element.72), channel_id=1, source_target_pairs={{0,1},{1,0},{2,3},{3,2},{4,5},{5,4},{6,7},{7,6},{8,9},{9,8},{10,11... | collective-permute-start | bytes 1179656 | tf_op jit(solution)/shard_map/ppermute | solution.py:327
  40.4 16.9 %collective-permute-start.12 = (bf16[768,640]{1,0:T(8,128)(2,1)S(1)}, bf16[768,640]{1,0:T(8,128)(2,1)S(1)}, u32[]{:S(2)}, u32[]{:S(2)}) collective-permute-start(bf16[768,640]{1,0:T(8,128)(2,1)S(1)} %constant_dynamic-update-slice_fusion.2.own), channel_id=1, source_target_pairs={{0,1},{1,0},{2,3},{3,2},{4,5},{5,4},{6,7},{7,6},{8,9},{9,8},{10,11... | collective-permute-start | bytes 2949128 | tf_op jit(solution)/shard_map/ppermute | solution.py:327
  41.4 15.7 %collective-permute-start.13 = (bf16[64,4096]{1,0:T(8,128)(2,1)S(1)}, bf16[64,4096]{1,0:T(8,128)(2,1)S(1)}, u32[]{:S(2)}, u32[]{:S(2)}) collective-permute-start(bf16[64,4096]{1,0:T(8,128)(2,1)S(1)} %collective-permute-done.8.refs_2_), channel_id=1, source_target_pairs={{0,4},{1,5},{2,6},{3,7},{4,8},{5,9},{6,10},{7,11},{8,12},{9,13},{1... | collective-permute-start | bytes 1572872 | tf_op jit(solution)/shard_map/ppermute | solution.py:330
  43.6 13.6 %collective-permute-start.14 = (bf16[64,4096]{1,0:T(8,128)(2,1)S(1)}, bf16[64,4096]{1,0:T(8,128)(2,1)S(1)}, u32[]{:S(2)}, u32[]{:S(2)}) collective-permute-start(bf16[64,4096]{1,0:T(8,128)(2,1)S(1)} %collective-permute-done.8.refs_2_), channel_id=1, source_target_pairs={{0,2},{1,3},{2,0},{3,1},{4,6},{5,7},{6,4},{7,5},{8,10},{9,11},{10,... | collective-permute-start | bytes 1572872 | tf_op jit(solution)/shard_map/ppermute | solution.py:333
  45.0 10.5 %collective-permute-start.15 = (bf16[128,1536]{1,0:T(8,128)(2,1)S(1)}, bf16[128,1536]{1,0:T(8,128)(2,1)S(1)}, u32[]{:S(2)}, u32[]{:S(2)}) collective-permute-start(bf16[128,1536]{1,0:T(8,128)(2,1)S(1)} %get-tuple-element.80), channel_id=1, source_target_pairs={{0,16},{1,17},{2,18},{3,19},{4,20},{5,21},{6,22},{7,23},{8,24},{9,... | collective-permute-start | bytes 1179656 | tf_op jit(solution)/shard_map/ppermute | solution.py:327
  46.5 1.5 %collective-permute-start.5 = (bf16[1,8,16,576]{3,2,0,1:T(8,128)(2,1)S(1)}, bf16[1,8,16,576]{3,2,0,1:T(8,128)(2,1)S(1)}, u32[]{:S(2)}, u32[]{:S(2)}) collective-permute-start(bf16[1,8,16,576]{3,2,0,1:T(8,128)(2,1)S(1)} %get-tuple-element.66), channel_id=1, source_target_pairs={{0,1},{1,0},{2,3},{3,2},{4,5},{5,4},{6,7},{7,6},{8,9},{9,8},{10,11... | collective-permute-start | bytes 442376 | tf_op jit(solution)/shard_map/ppermute | solution.py:336
  57.3 7.1 %collective-permute-start.17 = (bf16[2,4,16,576]{3,2,0,1:T(8,128)(2,1)S(1)}, bf16[2,4,16,576]{3,2,0,1:T(8,128)(2,1)S(1)}, u32[]{:S(2)}, u32[]{:S(2)}) collective-permute-start(bf16[2,4,16,576]{3,2,0,1:T(8,128)(2,1)S(1)} %fusion.2), channel_id=1, source_target_pairs={{0,2},{1,3},{2,0},{3,1},{4,6},{5,7},{6,4},{7,5},{8,10},{9,11},{10,... | collective-permute-start | bytes 442376 | tf_op jit(solution)/shard_map/ppermute | solution.py:336
  58.7 9.4 %collective-permute-start.16 = (bf16[64,2048]{1,0:T(8,128)(2,1)S(1)}, bf16[64,2048]{1,0:T(8,128)(2,1)S(1)}, u32[]{:S(2)}, u32[]{:S(2)}) collective-permute-start(bf16[64,2048]{1,0:T(8,128)(2,1)S(1)} %slice.41), channel_id=1, source_target_pairs={{0,2},{1,3},{2,0},{3,1},{4,6},{5,7},{6,4},{7,5},{8,10},{9,11},{10,... | collective-permute-start | bytes 786440 | tf_op jit(solution)/shard_map/ppermute | solution.py:333
  59.4 19.2 %collective-permute-start.18 = (bf16[64,2048]{1,0:T(8,128)(2,1)S(1)}, bf16[64,2048]{1,0:T(8,128)(2,1)S(1)}, u32[]{:S(2)}, u32[]{:S(2)}) collective-permute-start(bf16[64,2048]{1,0:T(8,128)(2,1)S(1)} %slice.45), channel_id=1, source_target_pairs={{0,4},{1,5},{2,6},{3,7},{4,8},{5,9},{6,10},{7,11},{8,12},{9,13},{1... | collective-permute-start | bytes 786440 | tf_op jit(solution)/shard_map/ppermute | solution.py:330
  61.0 17.7 %collective-permute-start.19 = (bf16[128,1536]{1,0:T(8,128)(2,1)S(1)}, bf16[128,1536]{1,0:T(8,128)(2,1)S(1)}, u32[]{:S(2)}, u32[]{:S(2)}) collective-permute-start(bf16[128,1536]{1,0:T(8,128)(2,1)S(1)} %get-tuple-element.89), channel_id=1, source_target_pairs={{0,1},{1,0},{2,3},{3,2},{4,5},{5,4},{6,7},{7,6},{8,9},{9,8},{10,11... | collective-permute-start | bytes 1179656 | tf_op jit(solution)/shard_map/ppermute | solution.py:327
  61.0 17.7 %collective-permute-start.20 = (bf16[128,1536]{1,0:T(8,128)(2,1)S(1)}, bf16[128,1536]{1,0:T(8,128)(2,1)S(1)}, u32[]{:S(2)}, u32[]{:S(2)}) collective-permute-start(bf16[128,1536]{1,0:T(8,128)(2,1)S(1)} %get-tuple-element.91), channel_id=1, source_target_pairs={{0,17},{1,16},{2,19},{3,18},{4,21},{5,20},{6,23},{7,22},{8,25},{9,... | collective-permute-start | bytes 1179656 | tf_op jit(solution)/shard_map/ppermute | solution.py:327
  64.5 23.1 %collective-permute-start.21 = (bf16[4,2,16,576]{3,2,0,1:T(8,128)(2,1)S(1)}, bf16[4,2,16,576]{3,2,0,1:T(8,128)(2,1)S(1)}, u32[]{:S(2)}, u32[]{:S(2)}) collective-permute-start(bf16[4,2,16,576]{3,2,0,1:T(8,128)(2,1)S(1)} %get-tuple-element.94), channel_id=1, source_target_pairs={{0,4},{1,5},{2,6},{3,7},{4,0},{5,1},{6,2},{7,3},{8,12},{9,13},{10,... | collective-permute-start | bytes 442376 | tf_op jit(solution)/shard_map/ppermute | solution.py:336
  77.1 12.5 %collective-permute-start.22 = (bf16[128,1024]{1,0:T(8,128)(2,1)S(1)}, bf16[128,1024]{1,0:T(8,128)(2,1)S(1)}, u32[]{:S(2)}, u32[]{:S(2)}) collective-permute-start(bf16[128,1024]{1,0:T(8,128)(2,1)S(1)} %get-tuple-element.96), channel_id=1, source_target_pairs={{0,16},{1,17},{2,18},{3,19},{4,20},{5,21},{6,22},{7,23},{8,24},{9,... | collective-permute-start | bytes 786440 | tf_op jit(solution)/shard_map/ppermute | solution.py:327
  85.4 7.8 %collective-permute-start.25 = (bf16[128,768]{1,0:T(8,128)(2,1)S(1)}, bf16[128,768]{1,0:T(8,128)(2,1)S(1)}, u32[]{:S(2)}, u32[]{:S(2)}) collective-permute-start(bf16[128,768]{1,0:T(8,128)(2,1)S(1)} %get-tuple-element.102), channel_id=1, source_target_pairs={{0,16},{1,17},{2,18},{3,19},{4,20},{5,21},{6,22},{7,23},{8,24},{9,... | collective-permute-start | bytes 589832 | tf_op jit(solution)/shard_map/ppermute | solution.py:327
  86.0 12.9 %collective-permute-start.23 = (bf16[128,1024]{1,0:T(8,128)(2,1)S(1)}, bf16[128,1024]{1,0:T(8,128)(2,1)S(1)}, u32[]{:S(2)}, u32[]{:S(2)}) collective-permute-start(bf16[128,1024]{1,0:T(8,128)(2,1)S(1)} %get-tuple-element.99), channel_id=1, source_target_pairs={{0,1},{1,0},{2,3},{3,2},{4,5},{5,4},{6,7},{7,6},{8,9},{9,8},{10,11... | collective-permute-start | bytes 786440 | tf_op jit(solution)/shard_map/ppermute | solution.py:327
  86.0 9.3 %collective-permute-start.26 = (bf16[128,768]{1,0:T(8,128)(2,1)S(1)}, bf16[128,768]{1,0:T(8,128)(2,1)S(1)}, u32[]{:S(2)}, u32[]{:S(2)}) collective-permute-start(bf16[128,768]{1,0:T(8,128)(2,1)S(1)} %get-tuple-element.103), channel_id=1, source_target_pairs={{0,17},{1,16},{2,19},{3,18},{4,21},{5,20},{6,23},{7,22},{8,25},{9,... | collective-permute-start | bytes 589832 | tf_op jit(solution)/shard_map/ppermute | solution.py:327
  87.7 10.6 %collective-permute-start.31 = (bf16[8,1,16,576]{3,2,0,1:T(8,128)(2,1)S(1)}, bf16[8,1,16,576]{3,2,0,1:T(8,128)(2,1)S(1)}, u32[]{:S(2)}, u32[]{:S(2)}) collective-permute-start(bf16[8,1,16,576]{3,2,0,1:T(8,128)(2,1)S(1)} %get-tuple-element.109), channel_id=1, source_target_pairs={{0,8},{1,9},{2,10},{3,11},{4,12},{5,13},{6,14},{7,15},{8,0},{9,1},... | collective-permute-start | bytes 442376 | tf_op jit(solution)/shard_map/ppermute | solution.py:336
  89.5 11.0 %collective-permute-start.29 = (bf16[128,1024]{1,0:T(8,128)(2,1)S(1)}, bf16[128,1024]{1,0:T(8,128)(2,1)S(1)}, u32[]{:S(2)}, u32[]{:S(2)}) collective-permute-start(bf16[128,1024]{1,0:T(8,128)(2,1)S(1)} %get-tuple-element.106), channel_id=1, source_target_pairs={{0,17},{1,16},{2,19},{3,18},{4,21},{5,20},{6,23},{7,22},{8,25},{9,... | collective-permute-start | bytes 786440 | tf_op jit(solution)/shard_map/ppermute | solution.py:327
  93.2 9.8 %collective-permute-start.24 = (bf16[128,768]{1,0:T(8,128)(2,1)S(1)}, bf16[128,768]{1,0:T(8,128)(2,1)S(1)}, u32[]{:S(2)}, u32[]{:S(2)}) collective-permute-start(bf16[128,768]{1,0:T(8,128)(2,1)S(1)} %get-tuple-element.100), channel_id=1, source_target_pairs={{0,1},{1,0},{2,3},{3,2},{4,5},{5,4},{6,7},{7,6},{8,9},{9,8},{10,11... | collective-permute-start | bytes 589832 | tf_op jit(solution)/shard_map/ppermute | solution.py:327
  95.3 7.7 %collective-permute-start.28 = (bf16[128,256]{1,0:T(8,128)(2,1)S(1)}, bf16[128,256]{1,0:T(8,128)(2,1)S(1)}, u32[]{:S(2)}, u32[]{:S(2)}) collective-permute-start(bf16[128,256]{1,0:T(8,128)(2,1)S(1)} %get-tuple-element.105), channel_id=1, source_target_pairs={{0,16},{1,17},{2,18},{3,19},{4,20},{5,21},{6,22},{7,23},{8,24},{9,... | collective-permute-start | bytes 196616 | tf_op jit(solution)/shard_map/ppermute | solution.py:327
  98.3 4.8 %collective-permute-start.30 = (bf16[128,256]{1,0:T(8,128)(2,1)S(1)}, bf16[128,256]{1,0:T(8,128)(2,1)S(1)}, u32[]{:S(2)}, u32[]{:S(2)}) collective-permute-start(bf16[128,256]{1,0:T(8,128)(2,1)S(1)} %get-tuple-element.107), channel_id=1, source_target_pairs={{0,17},{1,16},{2,19},{3,18},{4,21},{5,20},{6,23},{7,22},{8,25},{9,... | collective-permute-start | bytes 196616 | tf_op jit(solution)/shard_map/ppermute | solution.py:327
  98.9 4.1 %collective-permute-start.27 = (bf16[128,256]{1,0:T(8,128)(2,1)S(1)}, bf16[128,256]{1,0:T(8,128)(2,1)S(1)}, u32[]{:S(2)}, u32[]{:S(2)}) collective-permute-start(bf16[128,256]{1,0:T(8,128)(2,1)S(1)} %get-tuple-element.104), channel_id=1, source_target_pairs={{0,1},{1,0},{2,3},{3,2},{4,5},{5,4},{6,7},{7,6},{8,9},{9,8},{10,11... | collective-permute-start | bytes 196616 | tf_op jit(solution)/shard_map/ppermute | solution.py:327
